TPU v7x, 32 devices: a whole 2x2x4 slice. The times are simulated.
32 devices in a mesh: clip: 8 (over z, y), row: 4 (over x, core).
Axes of the slice: x: 2, y: 2, z: 4, core: 2. Of those that a mesh axis runs over, the one named last changes fastest.
Arguments:
- tokens: bfloat16 [8, 12, 16, 16, 1024], P('clip', None, 'row'), may hold values from -6 to 6
- condition: bfloat16 [8, 12, 1024], P('clip'), may hold values from -6 to 6
- cotangent: bfloat16 [8, 12, 16, 16, 1024], P('clip', None, 'row'), may hold values from -6 to 6
- positions: int32 [2, 8, 12, 16, 16], P(None, 'clip', None, 'row'), may hold values from 0 to 46, as said below
- patch_mask: int32 [8, 12, 16, 16], P('clip', None, 'row'), may hold values from 0 to 1, as said below
- frame_count: int32 [8], P('clip'), may hold values from 6 to 12, as said below
- adaptive_weight: float32 [1024, 6144], P(None, ('clip', 'row')), may hold values from -0.046875 to 0.046875
- adaptive_offsets: float32 [6144], P(('clip', 'row'))
- attend_weight: float32 [1024, 3072], P(('clip', 'row')), may hold values from -0.1875 to 0.1875
- project_weight: float32 [1024, 1024], P(None, ('clip', 'row')), may hold values from -1.5 to 1.5
- widen_weight: float32 [1024, 4096], P(('clip', 'row')), may hold values from -0.1875 to 0.1875
- narrow_weight: float32 [4096, 1024], P(None, ('clip', 'row')), may hold values from -0.09375 to 0.09375
- adaptive_first: float32 [1024, 6144], P(None, ('clip', 'row')), may hold values from -0.00036621094 to 0.00036621094
- adaptive_second: float32 [1024, 6144], P(None, ('clip', 'row')), may hold values from 5.3494315e-10 to 2.1397726e-09
- offsets_first: float32 [6144], P(('clip', 'row')), may hold values from -0.0007324219 to 0.0007324219
- offsets_second: float32 [6144], P(('clip', 'row')), may hold values from 2.1185866e-09 to 8.474347e-09
- attend_first: float32 [1024, 3072], P(('clip', 'row')), may hold values from -0.00036621094 to 0.00036621094
- attend_second: float32 [1024, 3072], P(('clip', 'row')), may hold values from 5.3494315e-10 to 2.1397726e-09
- project_first: float32 [1024, 1024], P(None, ('clip', 'row')), may hold values from -0.00036621094 to 0.00036621094
- project_second: float32 [1024, 1024], P(None, ('clip', 'row')), may hold values from 5.3494315e-10 to 2.1397726e-09
- widen_first: float32 [1024, 4096], P(('clip', 'row')), may hold values from -0.00036621094 to 0.00036621094
- widen_second: float32 [1024, 4096], P(('clip', 'row')), may hold values from 5.3494315e-10 to 2.1397726e-09
- narrow_first: float32 [4096, 1024], P(None, ('clip', 'row')), may hold values from -0.00036621094 to 0.00036621094
- narrow_second: float32 [4096, 1024], P(None, ('clip', 'row')), may hold values from 5.3494315e-10 to 2.1397726e-09
Outputs:
- block_out: bfloat16 [8, 12, 16, 16, 1024], P('clip', None, 'row')
- input_gradient: float32 [8, 12, 16, 16, 1024], P('clip', None, 'row')
- gradient_norm: float32 [], replicated
- adaptive_gradient: float32 [1024, 6144], P(None, ('clip', 'row'))
- adaptive_moment: float32 [1024, 6144], P(None, ('clip', 'row'))
- adaptive_variance: float32 [1024, 6144], P(None, ('clip', 'row'))
- adaptive_master: float32 [1024, 6144], P(None, ('clip', 'row'))
- adaptive_copy: bfloat16 [1024, 6144], P(None, ('clip', 'row'))
- offsets_gradient: float32 [6144], P(('clip', 'row'))
- offsets_moment: float32 [6144], P(('clip', 'row'))
- offsets_variance: float32 [6144], P(('clip', 'row'))
- offsets_master: float32 [6144], P(('clip', 'row'))
- offsets_copy: bfloat16 [6144], P(('clip', 'row'))
- attend_gradient: float32 [1024, 3072], P(('clip', 'row'))
- attend_moment: float32 [1024, 3072], P(('clip', 'row'))
- attend_variance: float32 [1024, 3072], P(('clip', 'row'))
- attend_master: float32 [1024, 3072], P(('clip', 'row'))
- attend_copy: bfloat16 [1024, 3072], P(('clip', 'row'))
- project_gradient: float32 [1024, 1024], P(None, ('clip', 'row'))
- project_moment: float32 [1024, 1024], P(None, ('clip', 'row'))
- project_variance: float32 [1024, 1024], P(None, ('clip', 'row'))
- project_master: float32 [1024, 1024], P(None, ('clip', 'row'))
- project_copy: bfloat16 [1024, 1024], P(None, ('clip', 'row'))
- widen_gradient: float32 [1024, 4096], P(('clip', 'row'))
- widen_moment: float32 [1024, 4096], P(('clip', 'row'))
- widen_variance: float32 [1024, 4096], P(('clip', 'row'))
- widen_master: float32 [1024, 4096], P(('clip', 'row'))
- widen_copy: bfloat16 [1024, 4096], P(('clip', 'row'))
- narrow_gradient: float32 [4096, 1024], P(None, ('clip', 'row'))
- narrow_moment: float32 [4096, 1024], P(None, ('clip', 'row'))
- narrow_variance: float32 [4096, 1024], P(None, ('clip', 'row'))
- narrow_master: float32 [4096, 1024], P(None, ('clip', 'row'))
- narrow_copy: bfloat16 [4096, 1024], P(None, ('clip', 'row'))
Inputs may be any that keep to these rules, and one draw needn't show every extreme that they name: `positions`: each frame's patches carry their row and column in the frame plus an offset of that frame. `patch_mask`: the first patch of every frame is real. `frame_count`: some clip has all 12 frames.
All inputs are finite; a program needn't handle non-finite values.
Results may differ from a plain program's by a relative error of at most 0.014.
The roundings to bfloat16 on the way count: a program that leaves them out, or rounds other values in their place, can miss the bound.
Values may be sent and summed in bfloat16 or wider, within the bound.
No kernel may reach another device: no remote copies, remote signals or barrier semaphores. Data moves between devices by JAX's collectives and lax.ppermute only.
A program may use at most 640 MiB of HBM per device.

v0:
```python
import math

import jax
import jax.numpy as jnp
from jax import lax
from jax.sharding import PartitionSpec as P

HEAD_DIM = 64
STEP = 10


clip_limit = 1.0
beta_one = 0.9
beta_two = 0.99
epsilon_adam = 1e-08
matrix_rate = 0.03
output_rate = 0.15
offset_rate = 0.5
decay_rate = 0.1


def layer_norm(values):
    center = values - jnp.mean(values, axis=-1, keepdims=True)
    spread = jnp.mean(center * center, axis=-1, keepdims=True)
    inverse = lax.rsqrt(spread + 1e-06)
    return (center * inverse, inverse)


def norm_back(normed, inverse, upstream):
    average = jnp.mean(upstream, axis=-1, keepdims=True)
    along = jnp.mean(upstream * normed, axis=-1, keepdims=True)
    return inverse * (upstream - average - normed * along)


def rotary(vectors, row_place, col_place, direction):
    quarter = vectors.shape[-1] // 4
    freqs = jnp.exp(-math.log(10000.0) * jnp.arange(quarter, dtype=jnp.float32) / quarter)
    row_angle = row_place.astype(jnp.float32)[:, None] * freqs
    col_angle = col_place.astype(jnp.float32)[:, None] * freqs
    angles = jnp.concatenate([row_angle, row_angle, col_angle, col_angle], axis=-1)
    cosine = jnp.cos(angles)[:, None, :]
    sine = direction * jnp.sin(angles)[:, None, :]
    pieces = vectors.reshape(vectors.shape[:-1] + (4, quarter))
    turned = jnp.concatenate(
        [-pieces[..., 1, :], pieces[..., 0, :], -pieces[..., 3, :], pieces[..., 2, :]], axis=-1
    )
    return vectors * cosine + turned * sine


def adam_update(master, first, second, gradient, rate, decay):
    moment = beta_one * first + (1.0 - beta_one) * gradient
    variance = beta_two * second + (1.0 - beta_two) * gradient * gradient
    corrected = (
        moment
        / (1.0 - beta_one**STEP)
        / (jnp.sqrt(variance / (1.0 - beta_two**STEP)) + epsilon_adam)
    )
    updated = master - rate * (corrected + decay * master)
    return (gradient, moment, variance, updated, updated.astype(jnp.bfloat16))


def local(
    tokens,
    condition,
    cotangent,
    positions,
    patch_mask,
    frame_count,
    adaptive_weight,
    adaptive_offsets,
    attend_weight,
    project_weight,
    widen_weight,
    narrow_weight,
    adaptive_first,
    adaptive_second,
    offsets_first,
    offsets_second,
    attend_first,
    attend_second,
    project_first,
    project_second,
    widen_first,
    widen_second,
    narrow_first,
    narrow_second,
):
    frames, patch_rows, grid_cols, model_width = tokens.shape[1:]
    per_frame = patch_rows * grid_cols
    tokens_dev = frames * per_frame
    head_dim = HEAD_DIM
    head_count = model_width // head_dim
    head_group = min(2, head_count)
    scale_factor = head_dim ** (-0.5)
    attend_full, widen_full = (
        lax.all_gather(attend_weight.astype(jnp.bfloat16), ("clip", "row"), axis=0, tiled=True),
        lax.all_gather(widen_weight.astype(jnp.bfloat16), ("clip", "row"), axis=0, tiled=True),
    )
    adaptive_full, offsets_full, project_full, narrow_full = (
        lax.all_gather(adaptive_weight.astype(jnp.bfloat16), ("clip", "row"), axis=1, tiled=True),
        lax.all_gather(
            adaptive_offsets.astype(jnp.bfloat16)[None, :], ("clip", "row"), axis=1, tiled=True
        ),
        lax.all_gather(project_weight.astype(jnp.bfloat16), ("clip", "row"), axis=1, tiled=True),
        lax.all_gather(narrow_weight.astype(jnp.bfloat16), ("clip", "row"), axis=1, tiled=True),
    )
    residual_in = tokens.reshape(frames, per_frame, model_width).astype(jnp.float32)
    cond_act = jax.nn.silu(condition[0].astype(jnp.float32)).astype(jnp.bfloat16)
    modulation = jnp.dot(
        cond_act, adaptive_full, preferred_element_type=jnp.float32
    ) + offsets_full.astype(jnp.float32)
    shift_one, scale_one, gate_one, shift_two, scale_two, gate_two = [
        modulation[:, None, piece_index * model_width : (piece_index + 1) * model_width]
        for piece_index in range(6)
    ]
    normed_one, inverse_one = layer_norm(residual_in)
    hidden_one = (
        (normed_one * (1.0 + scale_one) + shift_one)
        .astype(jnp.bfloat16)
        .reshape(tokens_dev, model_width)
    )
    projected = jnp.dot(hidden_one, attend_full, preferred_element_type=jnp.float32)
    row_place = positions[0].reshape(-1)
    col_place = positions[1].reshape(-1)
    queries = rotary(
        projected[:, :model_width].reshape(tokens_dev, head_count, head_dim),
        row_place,
        col_place,
        1.0,
    ).astype(jnp.bfloat16)
    keys_local = rotary(
        projected[:, model_width : 2 * model_width].reshape(tokens_dev, head_count, head_dim),
        row_place,
        col_place,
        1.0,
    ).astype(jnp.bfloat16)
    values_local = projected[:, 2 * model_width :].astype(jnp.bfloat16)
    frame_index = lax.broadcasted_iota(jnp.int32, (frames, patch_rows, grid_cols), 0)
    valid_local = ((frame_index < frame_count[0]) & (patch_mask[0] == 1)).astype(jnp.bfloat16)
    keys_all, values_all, valid_all = (
        lax.all_gather(
            keys_local.reshape(frames, patch_rows, grid_cols, model_width),
            "row",
            axis=1,
            tiled=True,
        ),
        lax.all_gather(
            values_local.reshape(frames, patch_rows, grid_cols, model_width),
            "row",
            axis=1,
            tiled=True,
        ),
        lax.all_gather(valid_local, "row", axis=1, tiled=True),
    )
    clip_rows = keys_all.shape[1]
    clip_tokens = frames * clip_rows * grid_cols
    keys_all = keys_all.reshape(clip_tokens, head_count, head_dim)
    values_all = values_all.reshape(clip_tokens, head_count, head_dim)
    key_valid = valid_all.reshape(clip_tokens) > 0.5

    def logits_of(head_start):
        query_part = queries[:, head_start : head_start + head_group]
        key_part = keys_all[:, head_start : head_start + head_group]
        logits = (
            jnp.einsum("shd,khd->hsk", query_part, key_part, preferred_element_type=jnp.float32)
            * scale_factor
        )
        return jnp.where(key_valid[None, None, :], logits, -jnp.inf)

    starts = list(range(0, head_count, head_group))
    outputs, row_peaks, row_totals = ([], [], [])
    for head_start in starts:
        logits = logits_of(head_start)
        row_peak = jnp.max(logits, axis=-1, keepdims=True)
        shifted = jnp.exp(logits - row_peak)
        row_total = jnp.sum(shifted, axis=-1, keepdims=True)
        probs_low = (shifted / row_total).astype(jnp.bfloat16)
        outputs.append(
            jnp.einsum(
                "hsk,khd->shd",
                probs_low,
                values_all[:, head_start : head_start + head_group],
                preferred_element_type=jnp.float32,
            )
        )
        row_peaks.append(row_peak)
        row_totals.append(row_total)
    attended = (
        jnp.concatenate(outputs, axis=1).reshape(tokens_dev, model_width).astype(jnp.bfloat16)
    )
    attention_out = jnp.dot(attended, project_full, preferred_element_type=jnp.float32).reshape(
        frames, per_frame, model_width
    )
    middle = residual_in + gate_one * attention_out
    normed_two, inverse_two = layer_norm(middle)
    hidden_two = (
        (normed_two * (1.0 + scale_two) + shift_two)
        .astype(jnp.bfloat16)
        .reshape(tokens_dev, model_width)
    )
    widened = jnp.dot(hidden_two, widen_full, preferred_element_type=jnp.float32)
    activated, gelu_back = jax.vjp(lambda values: jax.nn.gelu(values, approximate=True), widened)
    activated = activated.astype(jnp.bfloat16)
    branch_out = jnp.dot(activated, narrow_full, preferred_element_type=jnp.float32).reshape(
        frames, per_frame, model_width
    )
    block_out = (middle + gate_two * branch_out).astype(jnp.bfloat16).reshape(tokens.shape)
    attend_back, widen_back, project_back, narrow_back = (
        attend_full,
        widen_full,
        project_full,
        narrow_full,
    )
    upstream = cotangent.reshape(frames, per_frame, model_width).astype(jnp.float32)
    gate_two_grad = jnp.sum(upstream * branch_out, axis=1)
    branch_grad = (gate_two * upstream).astype(jnp.bfloat16).reshape(tokens_dev, model_width)
    narrow_grad = jnp.einsum(
        "sf,sd->fd", activated, branch_grad, preferred_element_type=jnp.float32
    )
    active_grad = jnp.einsum(
        "sd,fd->sf", branch_grad, narrow_back, preferred_element_type=jnp.float32
    )
    widened_grad = gelu_back(active_grad)[0].astype(jnp.bfloat16)
    widen_grad = jnp.einsum(
        "sd,sf->df", hidden_two, widened_grad, preferred_element_type=jnp.float32
    )
    hidden_two_grad = jnp.einsum(
        "sf,df->sd", widened_grad, widen_back, preferred_element_type=jnp.float32
    ).reshape(frames, per_frame, model_width)
    shift_two_grad = jnp.sum(hidden_two_grad, axis=1)
    scale_two_grad = jnp.sum(hidden_two_grad * normed_two, axis=1)
    middle_grad = upstream + norm_back(normed_two, inverse_two, hidden_two_grad * (1.0 + scale_two))
    gate_one_grad = jnp.sum(middle_grad * attention_out, axis=1)
    attention_grad = (gate_one * middle_grad).astype(jnp.bfloat16).reshape(tokens_dev, model_width)
    project_grad = jnp.einsum(
        "sd,se->de", attended, attention_grad, preferred_element_type=jnp.float32
    )
    attended_grad = jnp.einsum(
        "se,de->sd", attention_grad, project_back, preferred_element_type=jnp.float32
    )
    attended_grad = attended_grad.astype(jnp.bfloat16).reshape(tokens_dev, head_count, head_dim)
    query_grads, key_grads, value_grads = ([], [], [])
    for group_slot, head_start in enumerate(starts):
        logits = logits_of(head_start)
        softer = jnp.exp(logits - row_peaks[group_slot]) / row_totals[group_slot]
        softer_low = softer.astype(jnp.bfloat16)
        out_part = attended_grad[:, head_start : head_start + head_group]
        value_grads.append(
            jnp.einsum("hsk,shd->khd", softer_low, out_part, preferred_element_type=jnp.float32)
        )
        prob_grad = jnp.einsum(
            "shd,khd->hsk",
            out_part,
            values_all[:, head_start : head_start + head_group],
            preferred_element_type=jnp.float32,
        )
        centered = prob_grad - jnp.sum(softer * prob_grad, axis=-1, keepdims=True)
        logit_grad = (softer * centered).astype(jnp.bfloat16)
        query_grads.append(
            scale_factor
            * jnp.einsum(
                "hsk,khd->shd",
                logit_grad,
                keys_all[:, head_start : head_start + head_group],
                preferred_element_type=jnp.float32,
            )
        )
        key_grads.append(
            scale_factor
            * jnp.einsum(
                "hsk,shd->khd",
                logit_grad,
                queries[:, head_start : head_start + head_group],
                preferred_element_type=jnp.float32,
            )
        )
    key_sum, value_sum = (
        lax.psum_scatter(
            jnp.concatenate(key_grads, axis=1)
            .reshape(frames, clip_rows, grid_cols, model_width)
            .astype(jnp.bfloat16),
            "row",
            scatter_dimension=1,
            tiled=True,
        ).astype(jnp.float32),
        lax.psum_scatter(
            jnp.concatenate(value_grads, axis=1)
            .reshape(frames, clip_rows, grid_cols, model_width)
            .astype(jnp.bfloat16),
            "row",
            scatter_dimension=1,
            tiled=True,
        ).astype(jnp.float32),
    )
    query_back = rotary(jnp.concatenate(query_grads, axis=1), row_place, col_place, -1.0)
    key_back = rotary(key_sum.reshape(tokens_dev, head_count, head_dim), row_place, col_place, -1.0)
    projected_grad = jnp.concatenate(
        [
            query_back.reshape(tokens_dev, model_width),
            key_back.reshape(tokens_dev, model_width),
            value_sum.reshape(tokens_dev, model_width),
        ],
        axis=1,
    ).astype(jnp.bfloat16)
    attend_grad = jnp.einsum(
        "sd,sf->df", hidden_one, projected_grad, preferred_element_type=jnp.float32
    )
    hidden_one_grad = jnp.einsum(
        "sf,df->sd", projected_grad, attend_back, preferred_element_type=jnp.float32
    ).reshape(frames, per_frame, model_width)
    shift_one_grad = jnp.sum(hidden_one_grad, axis=1)
    scale_one_grad = jnp.sum(hidden_one_grad * normed_one, axis=1)
    input_gradient = (
        middle_grad + norm_back(normed_one, inverse_one, hidden_one_grad * (1.0 + scale_one))
    ).reshape(tokens.shape)
    modulation_grad = jnp.concatenate(
        [
            shift_one_grad,
            scale_one_grad,
            gate_one_grad,
            shift_two_grad,
            scale_two_grad,
            gate_two_grad,
        ],
        axis=1,
    )
    attend_sum, widen_sum = (
        lax.psum_scatter(attend_grad, ("clip", "row"), scatter_dimension=0, tiled=True),
        lax.psum_scatter(widen_grad, ("clip", "row"), scatter_dimension=0, tiled=True),
    )
    adaptive_grad = jnp.dot(
        cond_act.astype(jnp.float32).T,
        modulation_grad,
        precision=lax.Precision.HIGHEST,
        preferred_element_type=jnp.float32,
    )
    offsets_grad = jnp.sum(modulation_grad, axis=0, keepdims=True)
    adaptive_sum, offsets_sum, project_sum, narrow_sum = (
        lax.psum_scatter(adaptive_grad, ("clip", "row"), scatter_dimension=1, tiled=True),
        lax.psum_scatter(offsets_grad, ("clip", "row"), scatter_dimension=1, tiled=True),
        lax.psum_scatter(project_grad, ("clip", "row"), scatter_dimension=1, tiled=True),
        lax.psum_scatter(narrow_grad, ("clip", "row"), scatter_dimension=1, tiled=True),
    )
    offsets_sum = offsets_sum.reshape(-1)
    reduced = [adaptive_sum, offsets_sum, attend_sum, project_sum, widen_sum, narrow_sum]
    squares = sum((jnp.sum(item * item) for item in reduced))
    gradient_norm = jnp.sqrt(lax.psum(squares, ("clip", "row")))
    factor = clip_limit / jnp.maximum(gradient_norm, clip_limit)
    masters = (
        adaptive_weight,
        adaptive_offsets,
        attend_weight,
        project_weight,
        widen_weight,
        narrow_weight,
    )
    firsts = (adaptive_first, offsets_first, attend_first, project_first, widen_first, narrow_first)
    seconds = (
        adaptive_second,
        offsets_second,
        attend_second,
        project_second,
        widen_second,
        narrow_second,
    )
    rates = (matrix_rate, offset_rate, matrix_rate, output_rate, matrix_rate, matrix_rate)
    decays = (decay_rate, 0.0, decay_rate, decay_rate, decay_rate, decay_rate)
    results = [block_out, input_gradient, gradient_norm]
    for master, first, second, gradient, rate, decay in zip(
        masters, firsts, seconds, reduced, rates, decays
    ):
        results.extend(adam_update(master, first, second, factor * gradient, rate, decay))
    return tuple(results)


def solution(mesh):
    placed = (
        P("clip", None, "row", None, None),
        P("clip", None, None),
        P("clip", None, "row", None, None),
        P(None, "clip", None, "row", None),
        P("clip", None, "row", None),
        P("clip"),
        P(None, ("clip", "row")),
        P(("clip", "row")),
        P(("clip", "row"), None),
        P(None, ("clip", "row")),
        P(("clip", "row"), None),
        P(None, ("clip", "row")),
        P(None, ("clip", "row")),
        P(None, ("clip", "row")),
        P(("clip", "row")),
        P(("clip", "row")),
        P(("clip", "row"), None),
        P(("clip", "row"), None),
        P(None, ("clip", "row")),
        P(None, ("clip", "row")),
        P(("clip", "row"), None),
        P(("clip", "row"), None),
        P(None, ("clip", "row")),
        P(None, ("clip", "row")),
    )
    return jax.shard_map(
        local,
        mesh=mesh,
        in_specs=placed,
        out_specs=(
            P("clip", None, "row", None, None),
            P("clip", None, "row", None, None),
            P(),
            P(None, ("clip", "row")),
            P(None, ("clip", "row")),
            P(None, ("clip", "row")),
            P(None, ("clip", "row")),
            P(None, ("clip", "row")),
            P(("clip", "row")),
            P(("clip", "row")),
            P(("clip", "row")),
            P(("clip", "row")),
            P(("clip", "row")),
            P(("clip", "row"), None),
            P(("clip", "row"), None),
            P(("clip", "row"), None),
            P(("clip", "row"), None),
            P(("clip", "row"), None),
            P(None, ("clip", "row")),
            P(None, ("clip", "row")),
            P(None, ("clip", "row")),
            P(None, ("clip", "row")),
            P(None, ("clip", "row")),
            P(("clip", "row"), None),
            P(("clip", "row"), None),
            P(("clip", "row"), None),
            P(("clip", "row"), None),
            P(("clip", "row"), None),
            P(None, ("clip", "row")),
            P(None, ("clip", "row")),
            P(None, ("clip", "row")),
            P(None, ("clip", "row")),
            P(None, ("clip", "row")),
        ),
        check_vma=False,
    )
```

profile of v0, /device:TPU:0, one launch (start us, length us, event | category | flops | bytes accessed | tf_op | source)
XLA Modules:
  0.0 2735.4 jit_solution(16501834352295476182)
XLA Ops:
  13.8 43.2 %all-reduce = bf16[6144]{0:T(1024)(128)(2,1)S(1)} all-reduce(bf16[6144]{0:T(1024)(128)(2,1)S(1)} %dynamic-update-slice), channel_id=2, replica_groups=mesh['clip'=8,'row'=4] {'clip','row'}, use_global_device_ids=true, to_apply=%add | all-reduce | flops 6144 | bytes 24576
  71.9 39.4 %all-gather.9.cloned.1.call-done = bf16[1024,6144]{0,1:T(8,128)(2,1)} async-done(((bf16[1024,192]{0,1:T(8,128)(2,1)}), bf16[1024,6144]{0,1:T(8,128)(2,1)}) %all-gather.9.cloned.1.call-update) | async-done | bytes 12582928 | tf_op jit(solution)/shard_map/all_gather | solution.py:100
  121.2 61.3 %all-gather.11.cloned.1.call-done = bf16[1024,3072]{1,0:T(8,128)(2,1)} async-done(((bf16[32,3072]{1,0:T(8,128)(2,1)}), bf16[1024,3072]{1,0:T(8,128)(2,1)}) %all-gather.11.cloned.1.call-update) | async-done | bytes 6291472 | tf_op jit(solution)/shard_map/all_gather | solution.py:96
  274.2 34.3 %all-gather.15.cloned.1.call-done = bf16[12,16,16,1024]{3,2,1,0:T(8,128)(2,1)} async-done(((bf16[12,4,16,1024]{3,2,1,0:T(8,128)(2,1)}), bf16[12,16,16,1024]{3,2,1,0:T(8,128)(2,1)}) %all-gather.15.cloned.1.call-update) | async-done | bytes 6291472 | tf_op jit(solution)/shard_map/all_gather | solution.py:141
  325.6 23.0 fusion.319
  398.8 23.2 fusion.320
  473.6 21.6 fusion.323
  495.2 21.3 fusion.324
  525.4 21.4 fusion.325
  556.0 21.3 fusion.326
  586.2 21.4 fusion.327
  616.7 21.3 fusion.328
  645.9 21.5 fusion.329
  695.7 21.7 fusion.330
  795.6 20.6 fusion.22
  1045.7 17.2 convert_element_type.277
  1110.1 20.3 multiply_convert_fusion.2
  1130.5 17.1 multiply_convert_fusion.3
  1147.7 17.1 multiply_convert_fusion.4
  1164.8 17.1 multiply_convert_fusion.5
  1181.9 17.3 multiply_convert_fusion.6
  1251.8 17.2 convert_element_type.275
  1318.3 172.6 %all-reduce.6.cloned.1.call-done = (bf16[12,16,16,1024]{3,2,1,0:T(8,128)(2,1)}, bf16[12,16,16,1024]{3,2,1,0:T(8,128)(2,1)}) async-done(((bf16[12,16,16,1024]{3,2,1,0:T(8,128)(2,1)}, bf16[12,16,16,1024]{3,2,1,0:T(8,128)(2,1)}), (bf16[12,16,16,1024]{3,2,1,0:T(8,128)(2,1)}, bf16[12,16,16,1024]{3,2,1,0:T(8,128)(2,1)})) %all-reduce.6.cloned.1.call-update) | async-done | bytes 12582928
  1498.0 19.0 reshape_reshape.11
  1519.4 44.8 %fusion.318 = (f32[768,16,1,16]{3,2,1,0:T(1,128)}, f32[768,16,1,16]{3,2,1,0:T(1,128)}, f32[768,16,1,16]{3,2,1,0:T(1,128)}, f32[768,16,1,16]{3,2,1,0:T(1,128)}) fusion(f32[768,16,4,16]{3,2,1,0:T(4,128)} %reshape_reshape.11), kind=kLoop, calls=%fused_computation.396 | loop fusion | bytes 6291456 | tf_op jit(solution)/shard_map/slice | solution.py:45
  1703.3 40.6 %reduce-scatter.25.cloned.1.call-done = f32[192,1]{1,0:T(8,128)} async-done(((f32[6144,1]{1,0:T(8,128)}), f32[192,1]{1,0:T(8,128)}) %reduce-scatter.25.cloned.1.call-update) | async-done | bytes 784
  1745.5 140.4 %reduce-scatter.19.cloned.1.call-done = f32[1024,32]{0,1:T(8,128)} async-done(((f32[1024,1024]{0,1:T(8,128)}), f32[1024,32]{0,1:T(8,128)}) %reduce-scatter.19.cloned.1.call-update) | async-done | bytes 131088 | tf_op jit(solution)/shard_map/reduce_scatter | solution.py:341
  1887.5 156.2 %reduce-scatter.17.cloned.1.call-done = f32[32,3072]{1,0:T(8,128)} async-done(((f32[1024,3072]{1,0:T(8,128)}), f32[32,3072]{1,0:T(8,128)}) %reduce-scatter.17.cloned.1.call-update) | async-done | bytes 393232 | tf_op jit(solution)/shard_map/reduce_scatter | solution.py:328
  2045.4 182.4 %reduce-scatter.21.cloned.1.call-done = f32[32,4096]{1,0:T(8,128)} async-done(((f32[1024,4096]{1,0:T(8,128)}), f32[32,4096]{1,0:T(8,128)}) %reduce-scatter.21.cloned.1.call-update) | async-done | bytes 524304 | tf_op jit(solution)/shard_map/reduce_scatter | solution.py:329
  2229.6 185.1 %reduce-scatter.23.cloned.1.call-done = f32[4096,32]{0,1:T(8,128)} async-done(((f32[4096,1024]{0,1:T(8,128)}), f32[4096,32]{0,1:T(8,128)}) %reduce-scatter.23.cloned.1.call-update) | async-done | bytes 524304 | tf_op jit(solution)/shard_map/reduce_scatter | solution.py:342
  2416.4 252.9 %reduce-scatter.15.cloned.1.call-done = f32[1024,192]{0,1:T(8,128)} async-done(((f32[1024,6144]{0,1:T(8,128)}), f32[1024,192]{0,1:T(8,128)}) %reduce-scatter.15.cloned.1.call-update) | async-done | bytes 786448 | tf_op jit(solution)/shard_map/reduce_scatter | solution.py:339
  2675.1 40.2 %psum.7 = f32[]{:T(128)} all-reduce(f32[]{:T(128)S(6)} %add.250), channel_id=1, replica_groups=mesh['clip'=8,'row'=4] {'clip','row'}, use_global_device_ids=true, to_apply=%region_53.54 | all-reduce | flops 1 | bytes 8 | tf_op jit(solution)/shard_map/psum | solution.py:347
  (491 shorter events, 938.7 us)
Async XLA Ops:
  7.2 104.0 %all-gather.9.cloned.1.call-start = ((), (), s32[]{:S(2)}) async-start(), calls=%async_computation.6 | async-start | bytes 12976128 | tf_op jit(solution)/shard_map/all_gather | solution.py:100
  9.2 173.2 %all-gather.11.cloned.1.call-start = ((), (), s32[]{:S(2)}) async-start(), calls=%async_computation.7 | async-start | bytes 6488064 | tf_op jit(solution)/shard_map/all_gather | solution.py:96
  11.0 251.0 %all-gather.21.cloned.1.call-start = ((), (), s32[]{:S(2)}) async-start(), calls=%async_computation.12 | async-start | bytes 8650752 | tf_op jit(solution)/shard_map/all_gather | solution.py:105
  12.8 295.6 %all-gather.15.cloned.1.call-start = ((), (), s32[]{:S(2)}) async-start(), calls=%async_computation.9 | async-start | bytes 7864320 | tf_op jit(solution)/shard_map/all_gather | solution.py:141
  208.5 458.8 %copy-start.3 = (bf16[768,16,64]{0,2,1:T(8,128)(2,1)}, bf16[768,16,64]{0,2,1:T(8,128)(2,1)S(1)}, u32[]{:S(2)}) copy-start(bf16[768,16,64]{0,2,1:T(8,128)(2,1)S(1)} %get-tuple-element.125) | copy-start | bytes 4718596
  238.4 143.6 %all-gather.13.cloned.1.call-start = ((), (), s32[]{:S(2)}) async-start(), calls=%async_computation.8 | async-start | bytes 7864320 | tf_op jit(solution)/shard_map/all_gather | solution.py:147
  241.9 544.1 %all-gather.17.cloned.1.call-start = ((), (), s32[]{:S(2)}) async-start(), calls=%async_computation.10 | async-start | bytes 2162688 | tf_op jit(solution)/shard_map/all_gather | solution.py:104
  242.6 553.0 %all-gather.19.cloned.1.call-start = ((), (), s32[]{:S(2)}) async-start(), calls=%async_computation.11 | async-start | bytes 8650752 | tf_op jit(solution)/shard_map/all_gather | solution.py:97
  244.5 1246.4 %all-reduce.6.cloned.1.call-start = ((), (), s32[]{:S(2)}) async-start(), calls=%async_computation.19 | async-start | bytes 25165824
  352.2 315.1 %copy-start.16 = (bf16[3072,2,64]{0,2,1:T(8,128)(2,1)}, bf16[3072,2,64]{0,2,1:T(8,128)(2,1)S(1)}, u32[]{:S(2)}) copy-start(bf16[3072,2,64]{0,2,1:T(8,128)(2,1)S(1)} %copy.377) | copy-start | bytes 2359300
  356.1 281.9 %copy-start.18 = (bf16[3072,2,64]{0,2,1:T(8,128)(2,1)}, bf16[3072,2,64]{0,2,1:T(8,128)(2,1)S(1)}, u32[]{:S(2)}) copy-start(bf16[3072,2,64]{0,2,1:T(8,128)(2,1)S(1)} %copy.375) | copy-start | bytes 2359300
  495.2 180.2 %copy-start.105 = (f32[2,768]{1,0:T(2,128)}, f32[2,768]{1,0:T(2,128)S(1)}, u32[]{:S(2)}) copy-start(f32[2,768]{1,0:T(2,128)S(1)} %get-tuple-element.133) | copy-start | bytes 18436
  516.5 169.1 %copy-start.94 = (f32[2,768]{1,0:T(2,128)}, f32[2,768]{1,0:T(2,128)S(1)}, u32[]{:S(2)}) copy-start(f32[2,768]{1,0:T(2,128)S(1)} %get-tuple-element.135) | copy-start | bytes 18436
  546.8 170.7 %copy-start.97 = (f32[2,768]{1,0:T(2,128)}, f32[2,768]{1,0:T(2,128)S(1)}, u32[]{:S(2)}) copy-start(f32[2,768]{1,0:T(2,128)S(1)} %get-tuple-element.137) | copy-start | bytes 18436
  577.2 150.5 %copy-start.100 = (f32[2,768]{1,0:T(2,128)}, f32[2,768]{1,0:T(2,128)S(1)}, u32[]{:S(2)}) copy-start(f32[2,768]{1,0:T(2,128)S(1)} %get-tuple-element.139) | copy-start | bytes 18436
  667.3 212.6 %copy-start.111 = (f32[2,768]{1,0:T(2,128)}, f32[2,768]{1,0:T(2,128)S(1)}, u32[]{:S(2)}) copy-start(f32[2,768]{1,0:T(2,128)S(1)} %get-tuple-element.145) | copy-start | bytes 18436
  1269.1 474.8 %reduce-scatter.25.cloned.1.call-start = ((), (), s32[]{:S(2)}) async-start(), calls=%async_computation.18 | async-start | bytes 3244032
  1642.0 243.9 %reduce-scatter.19.cloned.1.call-start = ((), (), s32[]{:S(2)}) async-start(), calls=%async_computation.15 | async-start | bytes 4325376 | tf_op jit(solution)/shard_map/reduce_scatter | solution.py:341
  1647.9 395.8 %reduce-scatter.17.cloned.1.call-start = ((), (), s32[]{:S(2)}) async-start(), calls=%async_computation.14 | async-start | bytes 12976128 | tf_op jit(solution)/shard_map/reduce_scatter | solution.py:328
  1659.5 568.2 %reduce-scatter.21.cloned.1.call-start = ((), (), s32[]{:S(2)}) async-start(), calls=%async_computation.16 | async-start | bytes 17301504 | tf_op jit(solution)/shard_map/reduce_scatter | solution.py:329
  1674.2 740.5 %reduce-scatter.23.cloned.1.call-start = ((), (), s32[]{:S(2)}) async-start(), calls=%async_computation.17 | async-start | bytes 17301504 | tf_op jit(solution)/shard_map/reduce_scatter | solution.py:342
  1689.1 980.2 %reduce-scatter.15.cloned.1.call-start = ((), (), s32[]{:S(2)}) async-start(), calls=%async_computation.13 | async-start | bytes 25952256 | tf_op jit(solution)/shard_map/reduce_scatter | solution.py:339
  1703.2 1012.9 %copy-start.123 = (f32[192]{0:T(256)S(1)}, f32[192]{0:T(256)}, u32[]{:S(2)}) copy-start(f32[192]{0:T(256)} %param.31) | copy-start | bytes 2308
  1703.2 1012.9 %copy-start.124 = (f32[192]{0:T(256)S(1)}, f32[192]{0:T(256)}, u32[]{:S(2)}) copy-start(f32[192]{0:T(256)} %param.39) | copy-start | bytes 2308
  1703.2 1012.9 %copy-start.125 = (f32[192]{0:T(256)S(1)}, f32[192]{0:T(256)}, u32[]{:S(2)}) copy-start(f32[192]{0:T(256)} %param.38) | copy-start | bytes 2308
  1703.2 1015.4 %copy-start.46 = (f32[32,3072]{1,0:T(8,128)S(1)}, f32[32,3072]{1,0:T(8,128)}, u32[]{:S(2)}) copy-start(f32[32,3072]{1,0:T(8,128)} %param.32) | copy-start | bytes 1179652
  1703.3 1018.1 %copy-start.37 = (f32[4096,32]{0,1:T(8,128)S(1)}, f32[4096,32]{0,1:T(8,128)}, u32[]{:S(2)}) copy-start(f32[4096,32]{0,1:T(8,128)} %param.35) | copy-start | bytes 1572868
  1703.3 1018.1 %copy-start.72 = (f32[4096,32]{0,1:T(8,128)S(1)}, f32[4096,32]{0,1:T(8,128)}, u32[]{:S(2)}) copy-start(f32[4096,32]{0,1:T(8,128)} %param.47) | copy-start | bytes 1572868
  1703.3 1018.1 %copy-start.73 = (f32[4096,32]{0,1:T(8,128)S(1)}, f32[4096,32]{0,1:T(8,128)}, u32[]{:S(2)}) copy-start(f32[4096,32]{0,1:T(8,128)} %param.46) | copy-start | bytes 1572868
  1703.3 1020.6 %copy-start.38 = (f32[32,4096]{1,0:T(8,128)S(1)}, f32[32,4096]{1,0:T(8,128)}, u32[]{:S(2)}) copy-start(f32[32,4096]{1,0:T(8,128)} %param.34) | copy-start | bytes 1572868
  1703.3 1020.6 %copy-start.74 = (f32[32,4096]{1,0:T(8,128)S(1)}, f32[32,4096]{1,0:T(8,128)}, u32[]{:S(2)}) copy-start(f32[32,4096]{1,0:T(8,128)} %param.45) | copy-start | bytes 1572868
  2227.8 496.2 %copy-start.39 = (f32[32,4096]{1,0:T(8,128)S(1)}, f32[32,4096]{1,0:T(8,128)}, u32[]{:S(2)}) copy-start(f32[32,4096]{1,0:T(8,128)} %reduce-scatter.21.cloned.1.call-done) | copy-start | bytes 1572868
  (118 other events, 2064.2 us)
Sparse Core Ops, SparseCore 0:
  11.5 99.7 all-gather.8
  114.7 67.7 all-gather.10
  185.9 75.9 all-gather.20
  263.4 45.0 all-gather.14
  310.5 46.3 all-gather.12
  360.2 56.3 all-gather.16
  420.0 76.3 all-gather.18
  1269.2 221.5 all-reduce.5
  1642.1 101.7 reduce-scatter.24
  1746.0 139.8 reduce-scatter.18
  1892.0 151.6 reduce-scatter.16
  2045.9 181.7 reduce-scatter.20
  2230.1 184.4 reduce-scatter.22
  2422.1 247.1 reduce-scatter.14
where the time goes:
time: 2750 us; the launch traced here: 2740 us
  waiting for transfers between devices  1270 us (46%)
  matrix products  557 us (20%)
  local copies, waits for them, and re-layouts  414 us (15%)
  other arithmetic  377 us (14%)
  blocking collectives  88.7 us (3%)
    reduce_scatter x1, waiting for transfers between devices, local(): lax.psum_scatter(adaptive_grad, ('clip', 'row'), scatter_dimension=1, til...  253 us
    unnamed x16, waiting for transfers between devices  213 us
    reduce_scatter x1, waiting for transfers between devices, local(): lax.psum_scatter(narrow_grad, ('clip', 'row'), scatter_dimension=1, tiled...  185 us
    reduce_scatter x1, waiting for transfers between devices, local(): lax.psum_scatter(widen_grad, ('clip', 'row'), scatter_dimension=0, tiled=...  182 us
    sub x8, other arithmetic, local(): shifted = jnp.exp(logits - row_peak)  171 us
    reduce_scatter x1, waiting for transfers between devices, local(): lax.psum_scatter(attend_grad, ('clip', 'row'), scatter_dimension=0, tiled...  156 us
    unnamed x304, local copies, waits for them, and re-layouts  141 us
    reduce_scatter x1, waiting for transfers between devices, local(): lax.psum_scatter(project_grad, ('clip', 'row'), scatter_dimension=1, tile...  140 us
  transfers between devices with their start and end apart: 14, of which 11 were waited for; matrix products, arithmetic and copies ran while one was open for 26% of the time, Pallas kernels for 0%

commit v1 on v0

v1 whole, which is shorter than its diff:
```python
import functools
import math

import jax
import jax.numpy as jnp
from jax import lax
from jax.experimental import pallas as pl
from jax.experimental.pallas import tpu as pltpu
from jax.sharding import PartitionSpec as P

HEAD_DIM = 64
STEP = 10

clip_limit = 1.0
beta_one = 0.9
beta_two = 0.99
epsilon_adam = 1e-08
matrix_rate = 0.03
output_rate = 0.15
offset_rate = 0.5
decay_rate = 0.1

bf16 = jnp.bfloat16
f32 = jnp.float32
LOG2E = 1.4426950408889634
MASKED = -1e30
NN = (((1,), (0,)), ((), ()))
NT = (((1,), (1,)), ((), ()))
TN = (((0,), (0,)), ((), ()))
MIB = 2**20
VMEM = pltpu.VMEM


def dot(left, right, dims=NN):
    return lax.dot_general(left, right, dims, preferred_element_type=f32)


def whole(memory_space=VMEM):
    return pl.BlockSpec(memory_space=memory_space)


def params(mib=60):
    return pltpu.CompilerParams(vmem_limit_bytes=mib * MIB)


def cost(flops, nbytes, trans=0):
    return pl.CostEstimate(
        flops=int(flops), bytes_accessed=int(nbytes), transcendentals=int(trans)
    )


def layer_norm(values):
    center = values - jnp.mean(values, axis=-1, keepdims=True)
    spread = jnp.mean(center * center, axis=-1, keepdims=True)
    inverse = lax.rsqrt(spread + 1e-06)
    return center * inverse, inverse


def norm_back(normed, inverse, upstream):
    average = jnp.mean(upstream, axis=-1, keepdims=True)
    along = jnp.mean(upstream * normed, axis=-1, keepdims=True)
    return inverse * (upstream - average - normed * along)


def split3(value):
    one = value.astype(bf16)
    rest = value - one.astype(f32)
    two = rest.astype(bf16)
    three = (rest - two.astype(f32)).astype(bf16)
    return one, two, three


def turn_pieces(pieces, cosine, sine):
    quarter = HEAD_DIM // 4
    out = []
    for start in range(0, HEAD_DIM, 2 * quarter):
        u = pieces[start : start + quarter]
        w = pieces[start + quarter : start + 2 * quarter]
        place = slice(start // 2, start // 2 + quarter)
        out.append(u * cosine[place] - w * sine[place])
        out.append(w * cosine[place] + u * sine[place])
    return jnp.concatenate(out, axis=0)


def qkv_kernel(half, one, two, mod, weight, cosine, sine, out):
    step = pl.program_id(0)
    values = jnp.where(step < half, one[...].astype(f32), two[...].astype(f32))
    normed, _ = layer_norm(values)
    hidden = normed * (1.0 + mod[:, 1:2, :]) + mod[:, 0:1, :]
    count = hidden.shape[0] * hidden.shape[1]
    hidden = hidden.astype(bf16).reshape(count, hidden.shape[2])
    projected = dot(weight[...], hidden, NT)
    third = projected.shape[0] // 3
    cos, sin = cosine[...], sine[...]
    for head in range(0, 2 * third, HEAD_DIM):
        out[head : head + HEAD_DIM, :] = turn_pieces(
            projected[head : head + HEAD_DIM], cos, sin
        ).astype(bf16)
    out[2 * third :, :] = projected[2 * third :].astype(bf16)


def token_specs(frames, tokens, width, chunk):
    half = frames // chunk
    return half, [
        pl.BlockSpec((chunk, tokens, width), lambda i: (jnp.minimum(i, half - 1), 0, 0)),
        pl.BlockSpec((chunk, tokens, width), lambda i: (jnp.maximum(i - half, 0), 0, 0)),
        pl.BlockSpec((chunk, 6, width), lambda i: (lax.rem(i, half), 0, 0)),
    ]


def project_qkv(one, two, mod, weight, cosine, sine):
    frames, tokens, width = one.shape
    chunk = 4
    half, specs = token_specs(frames, tokens, width, chunk)
    block, total = chunk * tokens, 2 * frames * tokens
    rows = weight.shape[0]
    angle = pl.BlockSpec((cosine.shape[0], block), lambda i: (0, i))
    return pl.pallas_call(
        functools.partial(qkv_kernel, half),
        grid=(2 * half,),
        in_specs=specs + [whole(), angle, angle],
        out_specs=pl.BlockSpec((rows, block), lambda i: (0, i)),
        out_shape=jax.ShapeDtypeStruct((rows, total), bf16),
        compiler_params=params(),
        cost_estimate=cost(2 * rows * total * width, 4 * total * width),
    )(one, two, mod, weight, cosine, sine)


def attend_kernel(heads, q_ref, k1, k2, v1, v2, bias, out, lse, k_wide, v_wide):
    total = bias.shape[1]
    block = q_ref.shape[1]

    @pl.when(pl.program_id(0) == 0)
    def _():
        for head in range(heads):
            rows = slice(head * HEAD_DIM, (head + 1) * HEAD_DIM)
            keys = jnp.concatenate([k1[rows, :], k2[rows, :]], axis=1)
            vals = jnp.concatenate([v1[rows, :], v2[rows, :]], axis=1)
            wide = jnp.concatenate([keys, keys, bias[...].astype(bf16), jnp.zeros((127, total), bf16)], axis=0)
            k_wide[head] = jnp.transpose(wide)
            v_wide[head] = jnp.concatenate([vals, jnp.ones((HEAD_DIM, total), bf16)], axis=0)

    def scores(head):
        part = q_ref[head * HEAD_DIM : (head + 1) * HEAD_DIM, :].astype(f32)
        part = part * (HEAD_DIM ** (-0.5) * LOG2E)
        high = part.astype(bf16)
        low = (part - high.astype(f32)).astype(bf16)
        wide = jnp.concatenate([high, low, jnp.ones((1, block), bf16), jnp.zeros((127, block), bf16)], axis=0)
        return dot(k_wide[head], wide)

    logits = scores(0)
    for head in range(heads):
        later = scores(head + 1) if head + 1 < heads else None
        peak = jnp.max(logits, axis=0, keepdims=True)
        probs = jnp.exp2(logits - peak).astype(bf16)
        mixed = dot(v_wide[head], probs)
        norm = mixed[HEAD_DIM : HEAD_DIM + 1]
        out[head * HEAD_DIM : (head + 1) * HEAD_DIM, :] = (mixed[:HEAD_DIM] / norm).astype(bf16)
        lse[head : head + 1, :] = peak + jnp.log2(norm)
        logits = later


def attend(queries, ours, theirs, bias):
    rows, count = queries.shape[0] // 3, queries.shape[1]
    total = bias.shape[1]
    heads = rows // HEAD_DIM
    block = 512 if count % 512 == 0 else 128

    def piece(index):
        return pl.BlockSpec((rows, count), lambda i: (index, 0))

    return pl.pallas_call(
        functools.partial(attend_kernel, heads),
        grid=(count // block,),
        in_specs=[
            pl.BlockSpec((rows, block), lambda i: (0, i)),
            piece(1),
            piece(1),
            piece(2),
            piece(2),
            pl.BlockSpec((1, total), lambda i: (0, 0)),
        ],
        out_specs=[
            pl.BlockSpec((rows, block), lambda i: (0, i)),
            pl.BlockSpec((heads, block), lambda i: (0, i)),
        ],
        out_shape=[
            jax.ShapeDtypeStruct((rows, count), bf16),
            jax.ShapeDtypeStruct((heads, count), f32),
        ],
        scratch_shapes=[
            VMEM((heads, total, 256), bf16),
            VMEM((heads, 2 * HEAD_DIM, total), bf16),
        ],
        compiler_params=params(),
        cost_estimate=cost(16 * total * count * rows, 4 * rows * total, heads * count * total),
    )(queries, ours, theirs, ours, theirs, bias)


def attend_back_kernel(
    heads, last, q_ref, k1, k2, v1, v2, bias, out_ref, grad_ref, lse, cosine, sine, cos_all, sin_all,
    *rest,
):
    if last:
        dk_in, dv_in, dq, dk, dv, k_wide, v_wide, dk_sum, dv_sum = rest
    else:
        dq, dk_sum, dv_sum, k_wide, v_wide = rest
    total = bias.shape[1]
    block = q_ref.shape[1]
    scale = HEAD_DIM ** (-0.5)
    step = pl.program_id(0)

    @pl.when(step == 0)
    def _():
        for head in range(heads):
            rows = slice(head * HEAD_DIM, (head + 1) * HEAD_DIM)
            keys = jnp.concatenate([k1[rows, :], k2[rows, :]], axis=1)
            vals = jnp.concatenate([v1[rows, :], v2[rows, :]], axis=1)
            k_wide[head] = jnp.concatenate(
                [keys, keys, bias[...].astype(bf16), jnp.ones((15, total), bf16), jnp.zeros((112, total), bf16)],
                axis=0,
            )
            v_wide[head] = jnp.concatenate([vals, jnp.ones((HEAD_DIM, total), bf16)], axis=0)
        if last:
            dk_sum[...] = dk_in[...]
            dv_sum[...] = dv_in[...]
        else:
            dk_sum[...] = jnp.zeros_like(dk_sum)
            dv_sum[...] = jnp.zeros_like(dv_sum)

    def scores(head):
        rows = slice(head * HEAD_DIM, (head + 1) * HEAD_DIM)
        part = q_ref[rows, :].astype(f32) * (scale * LOG2E)
        high = part.astype(bf16)
        low = (part - high.astype(f32)).astype(bf16)
        one, two, three = split3(-lse[head : head + 1, :])
        wide = jnp.concatenate(
            [high, low, jnp.ones((1, block), bf16), one, two, three, jnp.zeros((124, block), bf16)],
            axis=0,
        )
        grad = grad_ref[rows, :]
        mean = jnp.sum(grad.astype(f32) * out_ref[rows, :].astype(f32), axis=0, keepdims=True)
        one, two, three = split3(-mean)
        grad_wide = jnp.concatenate([grad, one, two, three, jnp.zeros((61, block), bf16)], axis=0)
        return dot(wide, k_wide[head], TN), dot(grad_wide, v_wide[head], TN)

    pad = jnp.zeros((HEAD_DIM, block), bf16)
    logits, centered = scores(0)
    for head in range(heads):
        rows = slice(head * HEAD_DIM, (head + 1) * HEAD_DIM)
        later = scores(head + 1) if head + 1 < heads else (None, None)
        probs = jnp.exp2(logits)
        low = probs.astype(bf16)
        logit_grad = (probs * centered).astype(bf16)
        grad_pad = jnp.concatenate([grad_ref[rows, :], pad], axis=0)
        q_pad = jnp.concatenate([q_ref[rows, :], pad], axis=0)
        dv_sum[rows, :] += dot(grad_pad, low)[:HEAD_DIM]
        dk_sum[rows, :] += dot(q_pad, logit_grad)[:HEAD_DIM]
        q_grad = dot(k_wide[head][: 2 * HEAD_DIM], logit_grad, NT)[:HEAD_DIM] * scale
        dq[rows, :] = turn_pieces(q_grad, cosine[...], -sine[...]).astype(bf16)
        logits, centered = later

    if last:

        @pl.when(step == pl.num_programs(0) - 1)
        def _():
            for head in range(heads):
                rows = slice(head * HEAD_DIM, (head + 1) * HEAD_DIM)
                dk[rows, :] = turn_pieces(dk_sum[rows, :] * scale, cos_all[...], -sin_all[...]).astype(bf16)
            dv[...] = dv_sum[...].astype(bf16)


def attend_back(queries, ours, theirs, bias, out, grad, lse, angles, offset, sums=None):
    rows, count = queries.shape[0] // 3, queries.shape[1]
    total = bias.shape[1]
    heads = rows // HEAD_DIM
    block = 256 if count % 256 == 0 else 128
    steps = count // block
    last = sums is not None
    cosine, sine = angles

    def piece(index):
        return pl.BlockSpec((rows, count), lambda i: (index, 0))

    moving = pl.BlockSpec((rows, block), lambda i: (0, i))
    fixed = pl.BlockSpec((rows, total), lambda i: (0, 0))
    angle = pl.BlockSpec((cosine.shape[0], block), lambda i: (0, i + offset * steps))
    in_specs = [
        moving,
        piece(1),
        piece(1),
        piece(2),
        piece(2),
        pl.BlockSpec((1, total), lambda i: (0, 0)),
        moving,
        moving,
        pl.BlockSpec((heads, block), lambda i: (0, i)),
        angle,
        angle,
        whole(),
        whole(),
    ]
    operands = [queries, ours, theirs, ours, theirs, bias, out, grad, lse, cosine, sine, cosine, sine]
    kind = f32
    scratch = [
        VMEM((heads, 256, total), bf16),
        VMEM((heads, 2 * HEAD_DIM, total), bf16),
    ]
    if last:
        in_specs += [whole(), whole()]
        operands += list(sums)
        kind = bf16
        scratch += [VMEM((rows, total), f32), VMEM((rows, total), f32)]
    return pl.pallas_call(
        functools.partial(attend_back_kernel, heads, last),
        grid=(steps,),
        in_specs=in_specs,
        out_specs=[moving, fixed, fixed],
        out_shape=[
            jax.ShapeDtypeStruct((rows, count), bf16),
            jax.ShapeDtypeStruct((rows, total), kind),
            jax.ShapeDtypeStruct((rows, total), kind),
        ],
        scratch_shapes=scratch,
        compiler_params=params(63),
        cost_estimate=cost(34 * total * count * rows, 8 * rows * total, heads * count * total),
    )(*operands)


def project_kernel(order, a0, a1, a2, a3, proj, tokens, cotangent, mod, att_out, hidden, branch):
    features = a0.shape[0]
    mixed = None
    for slot, part in enumerate((a0, a1, a2, a3)):
        rows = proj[pl.ds(pl.multiple_of(order[slot] * features, features), features), :]
        term = dot(part[...], rows, TN)
        mixed = term if mixed is None else mixed + term
    shape = tokens.shape
    mixed = mixed.reshape(shape)
    att_out[...] = mixed
    middle = tokens[...].astype(f32) + mod[:, 2:3, :] * mixed
    normed, _ = layer_norm(middle)
    hidden_two = normed * (1.0 + mod[:, 4:5, :]) + mod[:, 3:4, :]
    flat = (shape[0] * shape[1], shape[2])
    hidden[...] = hidden_two.astype(bf16).reshape(flat)
    branch[...] = (mod[:, 5:6, :] * cotangent[...].astype(f32)).astype(bf16).reshape(flat)


def project_out(order, parts, proj, tokens, cotangent, mod):
    frames, per_frame, width = tokens.shape
    chunk = 4
    block = chunk * per_frame
    features = parts[0].shape[0]
    cube = pl.BlockSpec((chunk, per_frame, width), lambda i: (i, 0, 0))
    flat = pl.BlockSpec((block, width), lambda i: (i, 0))
    return pl.pallas_call(
        project_kernel,
        grid=(frames // chunk,),
        in_specs=[whole(pltpu.SMEM)]
        + [pl.BlockSpec((features, block), lambda i: (0, i))] * 4
        + [whole(), cube, cube, pl.BlockSpec((chunk, 6, width), lambda i: (i, 0, 0))],
        out_specs=[cube, flat, flat],
        out_shape=[
            jax.ShapeDtypeStruct(tokens.shape, f32),
            jax.ShapeDtypeStruct((frames * per_frame, width), bf16),
            jax.ShapeDtypeStruct((frames * per_frame, width), bf16),
        ],
        compiler_params=params(),
        cost_estimate=cost(2 * frames * per_frame * width * width, 14 * frames * per_frame * width),
    )(order, *parts, proj, tokens, cotangent, mod)


def feed_kernel(
    order, weights, hidden, branch, tokens, cotangent, att_out, mod, a0, a1, a2, a3, proj,
    grads, block_out, middle_grad, mod_grad, d0, d1, d2, d3, proj_raw, out_sum, in_sum, att_grad,
):
    step = pl.program_id(0)
    count, width = hidden.shape
    units = weights.shape[3]
    widen = weights[:, 0].reshape(width, units)
    narrow = weights[:, 1].reshape(width, units)
    hid, bra = hidden[...], branch[...]
    wide = dot(hid, widen)
    active_grad = dot(bra, narrow)
    factor = math.sqrt(2.0 / math.pi)
    square = wide * wide
    bend = jnp.tanh(factor * wide * (1.0 + 0.044715 * square))
    active = (0.5 * wide * (1.0 + bend)).astype(bf16)
    slope = 0.5 * (1.0 + bend) + 0.5 * wide * (1.0 - bend * bend) * (
        factor * (1.0 + 3.0 * 0.044715 * square)
    )
    wide_grad = (active_grad * slope).astype(bf16)
    out_part = dot(active, narrow, NT)
    in_part = dot(wide_grad, widen, NT)

    @pl.when(step == 0)
    def _():
        out_sum[...] = out_part
        in_sum[...] = in_part

    @pl.when(step > 0)
    def _():
        out_sum[...] += out_part
        in_sum[...] += in_part

    shape = (grads.shape[0], grads.shape[2], units)
    grads[:, 0] = dot(hid, wide_grad, TN).astype(bf16).reshape(shape)
    grads[:, 1] = dot(bra, active, TN).astype(bf16).reshape(shape)

    @pl.when(step == pl.num_programs(0) - 1)
    def _():
        frames, per_frame, _ = tokens.shape
        chunk = 2
        for start in range(0, frames, chunk):
            some = slice(start, start + chunk)
            flat = slice(start * per_frame, (start + chunk) * per_frame)
            cube = (chunk, per_frame, width)
            here = mod[some]
            att = att_out[some]
            middle = tokens[some].astype(f32) + here[:, 2:3] * att
            normed, inverse = layer_norm(middle)
            upstream = cotangent[some].astype(f32)
            branch_out = out_sum[flat, :].reshape(cube)
            block_out[some] = (middle + here[:, 5:6] * branch_out).astype(bf16)
            mod_grad[some, 3:4] = jnp.sum(upstream * branch_out, axis=1, keepdims=True)
            hid_grad = in_sum[flat, :].reshape(cube)
            mod_grad[some, 1:2] = jnp.sum(hid_grad, axis=1, keepdims=True)
            mod_grad[some, 2:3] = jnp.sum(hid_grad * normed, axis=1, keepdims=True)
            mid = upstream + norm_back(normed, inverse, hid_grad * (1.0 + here[:, 4:5]))
            middle_grad[some] = mid
            mod_grad[some, 0:1] = jnp.sum(mid * att, axis=1, keepdims=True)
            att_grad[flat, :] = (here[:, 2:3] * mid).astype(bf16).reshape(chunk * per_frame, width)
        features = a0.shape[0]
        grad = att_grad[...]
        for slot, (part, out) in enumerate(((a0, d0), (a1, d1), (a2, d2), (a3, d3))):
            place = pl.ds(pl.multiple_of(order[slot] * features, features), features)
            out[...] = dot(proj[place, :], grad, NT).astype(bf16)
            proj_raw[place, :] = dot(part[...], grad).astype(bf16)


def feed_forward(order, weights, hidden, branch, tokens, cotangent, att_out, mod, parts, proj):
    count, width = hidden.shape
    groups, _, rows, units = weights.shape
    block = 512
    frames = tokens.shape[0]
    features = parts[0].shape[0]
    spec = pl.BlockSpec((groups, 2, rows, block), lambda i: (0, 0, 0, i))
    return pl.pallas_call(
        feed_kernel,
        grid=(units // block,),
        in_specs=[whole(pltpu.SMEM), spec] + [whole()] * 11,
        out_specs=[spec] + [whole()] * 8,
        out_shape=[
            jax.ShapeDtypeStruct(weights.shape, bf16),
            jax.ShapeDtypeStruct(tokens.shape, bf16),
            jax.ShapeDtypeStruct(tokens.shape, f32),
            jax.ShapeDtypeStruct((frames, 4, width), f32),
        ]
        + [jax.ShapeDtypeStruct((features, count), bf16)] * 4
        + [jax.ShapeDtypeStruct((width, width), bf16)],
        scratch_shapes=[VMEM((count, width), f32), VMEM((count, width), f32), VMEM((count, width), bf16)],
        compiler_params=params(62),
        cost_estimate=cost(12 * count * width * units, 8 * width * units),
    )(order, weights, hidden, branch, tokens, cotangent, att_out, mod, *parts, proj)


def first_back_kernel(half, last, one, two, mod, dq, dk, dv, weight, *rest):
    if last:
        raw_in, mod_in, grads, raw, mod_grad, total = rest
    else:
        grads, total, mod_grad = rest
    step = pl.program_id(0)
    chunk = mod.shape[0]

    @pl.when(step == 0)
    def _():
        total[...] = raw_in[...] if last else jnp.zeros_like(total)
        mod_grad[...] = mod_in[...] if last else jnp.zeros_like(mod_grad)

    values = jnp.where(step < half, one[...].astype(f32), two[...].astype(f32))
    normed, _ = layer_norm(values)
    hidden = normed * (1.0 + mod[:, 1:2, :]) + mod[:, 0:1, :]
    shape = hidden.shape
    hidden = hidden.astype(bf16).reshape(shape[0] * shape[1], shape[2])
    pieces = jnp.concatenate([dq[...], dk[...], dv[...]], axis=0)
    total[...] += dot(pieces, hidden)
    back = dot(pieces, weight[...], TN)
    grads[...] = back.astype(bf16).reshape(grads.shape)
    back = back.reshape(shape)
    place = pl.ds(lax.rem(step, half) * chunk, chunk)
    mod_grad[place, 0:1] += jnp.sum(back, axis=1, keepdims=True)
    mod_grad[place, 1:2] += jnp.sum(back * normed, axis=1, keepdims=True)

    if last:

        @pl.when(step == pl.num_programs(0) - 1)
        def _():
            raw[...] = jnp.transpose(total[...]).astype(bf16)


def first_back(one, two, mod, dq, dk, dv, weight, offset, sums=None):
    frames, tokens, width = one.shape
    chunk = 4
    half, specs = token_specs(frames, tokens, width, chunk)
    block, count = chunk * tokens, 2 * frames * tokens
    rows = dq.shape[0]
    last = sums is not None
    moved = pl.BlockSpec((rows, block), lambda i: (0, i + offset * 2 * half))
    in_specs = specs + [pl.BlockSpec((rows, block), lambda i: (0, i)), moved, moved, whole()]
    operands = [one, two, mod, dq, dk, dv, weight]
    grads = jax.ShapeDtypeStruct((2, frames * tokens, width), bf16)
    grads_spec = pl.BlockSpec((1, block, width), lambda i: (i // half, lax.rem(i, half), 0))
    mods = jax.ShapeDtypeStruct((frames, 2, width), f32)
    if last:
        in_specs += [whole(), whole()]
        operands += list(sums)
        out_shape = [grads, jax.ShapeDtypeStruct((width, 3 * rows), bf16), mods]
        scratch = [VMEM((3 * rows, width), f32)]
    else:
        out_shape = [grads, jax.ShapeDtypeStruct((3 * rows, width), f32), mods]
        scratch = []
    return pl.pallas_call(
        functools.partial(first_back_kernel, half, last),
        grid=(2 * half,),
        in_specs=in_specs,
        out_specs=[grads_spec, whole(), whole()],
        out_shape=out_shape,
        scratch_shapes=scratch,
        compiler_params=params(),
        cost_estimate=cost(12 * rows * count * width, 6 * count * width),
    )(*operands)


def input_kernel(tokens, mod, middle_grad, one, two, three, out):
    normed, inverse = layer_norm(tokens[...].astype(f32))
    grad = one[...].astype(f32) + two[...].astype(f32) + three[...].astype(f32)
    grad = grad.reshape(tokens.shape) * (1.0 + mod[:, 1:2, :])
    out[...] = middle_grad[...] + norm_back(normed, inverse, grad)


def input_back(tokens, mod, middle_grad, parts):
    frames, per_frame, width = tokens.shape
    chunk = 4
    cube = pl.BlockSpec((chunk, per_frame, width), lambda i: (i, 0, 0))
    flat = pl.BlockSpec((chunk * per_frame, width), lambda i: (i, 0))
    return pl.pallas_call(
        input_kernel,
        grid=(frames // chunk,),
        in_specs=[cube, pl.BlockSpec((chunk, 6, width), lambda i: (i, 0, 0)), cube, flat, flat, flat],
        out_specs=cube,
        out_shape=jax.ShapeDtypeStruct(tokens.shape, f32),
        compiler_params=params(),
        cost_estimate=cost(20 * frames * per_frame * width, 16 * frames * per_frame * width),
    )(tokens, mod, middle_grad, *parts)


def swap(value, axis, size, step):
    return lax.ppermute(value, axis, [(place, place ^ step) for place in range(size)])


def in_order(stacked, place):
    count = stacked.shape[0]
    return jnp.concatenate(
        [lax.dynamic_index_in_dim(stacked, place ^ index, 0) for index in range(count)], axis=0
    )


def gather_clip(value, clips, clip):
    pieces = [value] + [swap(value, "clip", clips, step) for step in range(1, clips)]
    return in_order(jnp.stack(pieces), clip)


def sum_clip(value, clips, clip):
    total = lax.dynamic_index_in_dim(value, clip, 0, keepdims=False).astype(f32)
    for step in range(1, clips):
        piece = lax.dynamic_index_in_dim(value, clip ^ step, 0, keepdims=False)
        total = total + swap(piece, "clip", clips, step).astype(f32)
    return total


def adam_update(master, first, second, gradient, rate, decay):
    moment = beta_one * first + (1.0 - beta_one) * gradient
    variance = beta_two * second + (1.0 - beta_two) * gradient * gradient
    corrected = (
        moment
        / (1.0 - beta_one**STEP)
        / (jnp.sqrt(variance / (1.0 - beta_two**STEP)) + epsilon_adam)
    )
    updated = master - rate * (corrected + decay * master)
    return (gradient, moment, variance, updated, updated.astype(jnp.bfloat16))


def local(
    clips,
    rows,
    tokens,
    condition,
    cotangent,
    positions,
    patch_mask,
    frame_count,
    adaptive_weight,
    adaptive_offsets,
    attend_weight,
    project_weight,
    widen_weight,
    narrow_weight,
    adaptive_first,
    adaptive_second,
    offsets_first,
    offsets_second,
    attend_first,
    attend_second,
    project_first,
    project_second,
    widen_first,
    widen_second,
    narrow_first,
    narrow_second,
):
    frames, patch_rows, grid_cols, width = tokens.shape[1:]
    per_frame = patch_rows * grid_cols
    count = frames * per_frame
    devices = clips * rows
    features = width // rows
    clip, row = lax.axis_index("clip"), lax.axis_index("row")
    both = ("clip", "row")
    order = (row ^ jnp.arange(rows)).astype(jnp.int32)

    shard = widen_weight.shape[0]
    feed_shard = jnp.concatenate(
        [widen_weight.astype(bf16), narrow_weight.T.astype(bf16)], axis=0
    )
    units = feed_shard.shape[1]
    feed_full = lax.all_gather(feed_shard, both, axis=0, tiled=True)
    feed_full = feed_full.reshape(devices, 2, shard, units)
    fused = shard % 16 == 0
    if not fused:
        feed_full = feed_full.transpose(1, 0, 2, 3).reshape(1, 2, width, units)

    own = tokens.reshape(frames, per_frame, width)
    upstream = cotangent.reshape(frames, per_frame, width)
    tok1 = swap(own, "row", rows, 1)
    tok2 = swap(own, "row", rows, 2)
    tok3 = swap(tok2, "row", rows, 1)

    attend_mine = attend_weight.astype(bf16).reshape(shard, 3, rows, features)
    attend_mine = attend_mine.transpose(2, 0, 1, 3).reshape(rows, shard, 3 * features)
    pieces = []
    for step in range(rows):
        piece = lax.dynamic_index_in_dim(attend_mine, row ^ step, 0, keepdims=False)
        pieces.append(swap(piece, "row", rows, step) if step else piece)
    attend_clip = in_order(jnp.stack(pieces), row)
    attend_full = gather_clip(attend_clip, clips, clip).reshape(width, 3 * features)
    attend_turned = attend_full.T

    cond_act = jax.nn.silu(condition[0].astype(f32)).astype(bf16)
    cond_all = lax.all_to_all(
        jnp.broadcast_to(cond_act[None], (clips, frames, width)), "clip", 0, 0, tiled=True
    ).reshape(clips * frames, width)
    mod_mine = dot(cond_all, adaptive_weight.astype(bf16)) + adaptive_offsets.astype(bf16).astype(
        f32
    )
    part = mod_mine.shape[1]
    mod_mine = jnp.broadcast_to(
        mod_mine.reshape(clips, 1, frames, part), (clips, rows, frames, part)
    )
    mod = lax.all_to_all(mod_mine.reshape(devices, frames, part), both, 0, 0, tiled=True)
    mod = mod.transpose(1, 0, 2).reshape(frames, 6, width)

    frame_index = lax.broadcasted_iota(jnp.int32, (frames, patch_rows, grid_cols), 0)
    valid = (frame_index < frame_count[0]) & (patch_mask[0] == 1)
    small = jnp.stack(
        [positions[0].reshape(-1), positions[1].reshape(-1), valid.reshape(-1)]
    ).astype(f32)
    small = jnp.concatenate(
        [small] + [swap(small, "row", rows, step) for step in range(1, rows)], axis=1
    )
    bias = jnp.where(small[2:3] > 0.5, 0.0, MASKED)
    quarter = HEAD_DIM // 4
    freqs = jnp.exp(-math.log(10000.0) * jnp.arange(quarter, dtype=f32) / quarter)
    angles = jnp.concatenate([freqs[:, None] * small[0:1], freqs[:, None] * small[1:2]], axis=0)
    cosine, sine = jnp.cos(angles), jnp.sin(angles)
    near = 2 * count

    project_clip = gather_clip(project_weight.T.astype(bf16), clips, clip)
    project_far = swap(project_clip, "row", rows, 2)
    project_full = jnp.stack(
        [
            project_clip,
            swap(project_clip, "row", rows, 1),
            project_far,
            swap(project_far, "row", rows, 1),
        ]
    )
    project_full = in_order(project_full, row).transpose(1, 0, 2, 3).reshape(width, width).T

    qkv_near = project_qkv(own, tok1, mod, attend_turned, cosine[:, :near], sine[:, :near])
    qkv_far = project_qkv(tok2, tok3, mod, attend_turned, cosine[:, near:], sine[:, near:])
    out_far, lse_far = attend(qkv_far, qkv_near, qkv_far, bias)
    out_near, lse_near = attend(qkv_near, qkv_near, qkv_far, bias)
    parts = [
        out_near[:, :count],
        swap(out_near[:, count:], "row", rows, 1),
        swap(out_far[:, :count], "row", rows, 2),
        swap(out_far[:, count:], "row", rows, 3),
    ]
    att_out, hidden_two, branch_grad = project_out(order, parts, project_full, own, upstream, mod)
    feed_raw, block_out, middle_grad, mod_late, d0, d1, d2, d3, project_raw = feed_forward(
        order, feed_full, hidden_two, branch_grad, own, upstream, att_out, mod, parts, project_full
    )
    if not fused:
        feed_raw = feed_raw.reshape(2, devices, shard, units).transpose(1, 0, 2, 3)
    feed_sum = lax.psum_scatter(
        feed_raw.reshape(devices * 2 * shard, units), both, scatter_dimension=0, tiled=True
    ).astype(f32)
    widen_sum, narrow_sum = feed_sum[:shard], feed_sum[shard:].T

    project_raw = project_raw.T.reshape(clips, rows, shard, width).transpose(1, 0, 2, 3)
    piece = [lax.dynamic_index_in_dim(project_raw, row ^ step, 0, keepdims=False) for step in range(rows)]
    here = (piece[0].astype(f32) + swap(piece[1], "row", rows, 1).astype(f32)).astype(bf16)
    there = (piece[2].astype(f32) + swap(piece[3], "row", rows, 1).astype(f32)).astype(bf16)
    here = (here.astype(f32) + swap(there, "row", rows, 2).astype(f32)).astype(bf16)
    project_sum = sum_clip(here, clips, clip).T

    grad_near = jnp.concatenate([d0, swap(d1, "row", rows, 1)], axis=1)
    grad_far = jnp.concatenate([swap(d2, "row", rows, 2), swap(d3, "row", rows, 3)], axis=1)
    turning = (cosine, sine)
    dq_near, dk, dv = attend_back(
        qkv_near, qkv_near, qkv_far, bias, out_near, grad_near, lse_near, turning, 0
    )
    dq_far, dk, dv = attend_back(
        qkv_far, qkv_near, qkv_far, bias, out_far, grad_far, lse_far, turning, 1, (dk, dv)
    )
    back_far, raw, mod_early = first_back(tok2, tok3, mod, dq_far, dk, dv, attend_turned, 1)
    back_near, attend_raw, mod_early = first_back(
        own, tok1, mod, dq_near, dk, dv, attend_turned, 0, (raw, mod_early)
    )

    attend_mine = sum_clip(attend_raw.reshape(clips, rows, shard, 3 * features), clips, clip)
    pieces = []
    for step in range(rows):
        piece = lax.dynamic_index_in_dim(attend_mine, row ^ step, 0, keepdims=False)
        pieces.append(swap(piece, "row", rows, step) if step else piece)
    attend_sum = in_order(jnp.stack(pieces), row).reshape(rows, shard, 3, features)
    attend_sum = attend_sum.transpose(1, 2, 0, 3).reshape(shard, 3 * width)

    far = (
        back_far[0].astype(f32) + swap(back_far[1], "row", rows, 1).astype(f32)
    ).astype(bf16)
    input_gradient = input_back(
        own,
        mod,
        middle_grad,
        (back_near[0], swap(back_near[1], "row", rows, 1), swap(far, "row", rows, 2)),
    )

    mod_grad = jnp.concatenate([mod_early, mod_late], axis=1)
    mod_grad = mod_grad.reshape(frames, devices, part).transpose(1, 0, 2)
    mod_grad = lax.all_to_all(mod_grad, both, 0, 0, tiled=True)
    mod_grad = jnp.sum(mod_grad.reshape(clips, rows, frames, part), axis=1)
    mod_grad = mod_grad.reshape(clips * frames, part)
    adaptive_sum = lax.dot_general(
        mod_grad,
        cond_all.astype(f32),
        TN,
        precision=lax.Precision.HIGHEST,
        preferred_element_type=f32,
    ).T
    offsets_sum = jnp.sum(mod_grad, axis=0)

    reduced = [adaptive_sum, offsets_sum, attend_sum, project_sum, widen_sum, narrow_sum]
    squares = sum((jnp.sum(item * item) for item in reduced))
    squares = lax.all_to_all(
        jnp.broadcast_to(squares, (devices, 8, 128)), both, 0, 0, tiled=True
    )
    gradient_norm = jnp.sqrt(jnp.sum(squares[:, 0, 0]))
    factor = clip_limit / jnp.maximum(gradient_norm, clip_limit)
    masters = (
        adaptive_weight,
        adaptive_offsets,
        attend_weight,
        project_weight,
        widen_weight,
        narrow_weight,
    )
    firsts = (adaptive_first, offsets_first, attend_first, project_first, widen_first, narrow_first)
    seconds = (
        adaptive_second,
        offsets_second,
        attend_second,
        project_second,
        widen_second,
        narrow_second,
    )
    rates = (matrix_rate, offset_rate, matrix_rate, output_rate, matrix_rate, matrix_rate)
    decays = (decay_rate, 0.0, decay_rate, decay_rate, decay_rate, decay_rate)
    results = [block_out.reshape(tokens.shape), input_gradient.reshape(tokens.shape), gradient_norm]
    for master, first, second, gradient, rate, decay in zip(
        masters, firsts, seconds, reduced, rates, decays
    ):
        results.extend(adam_update(master, first, second, factor * gradient, rate, decay))
    return tuple(results)


def solution(mesh):
    both = ("clip", "row")
    token = P("clip", None, "row", None, None)
    down, across, line = P(both, None), P(None, both), P(both)
    placed = (
        token,
        P("clip", None, None),
        token,
        P(None, "clip", None, "row", None),
        P("clip", None, "row", None),
        P("clip"),
        across,
        line,
        down,
        across,
        down,
        across,
        across,
        across,
        line,
        line,
        down,
        down,
        across,
        across,
        down,
        down,
        across,
        across,
    )
    outs = (token, token, P())
    for spec in (across, line, down, across, down, across):
        outs += (spec,) * 5
    return jax.shard_map(
        functools.partial(local, mesh.shape["clip"], mesh.shape["row"]),
        mesh=mesh,
        in_specs=placed,
        out_specs=outs,
        check_vma=False,
    )
```

time: 2750 us -> 661 us (0.24)
  waiting for transfers between devices: 1270 us -> 152 us
  matrix products: 557 us -> 1.49 us
  local copies, waits for them, and re-layouts: 414 us -> 44.8 us
  other arithmetic: 377 us -> 32 us
  Pallas kernels: 0 us -> 279 us
  starting transfers between devices: 0.99 us -> 123 us
  blocking collectives: 88.7 us -> 0 us
    reduce_scatter x5 -> x1, waiting for transfers between devices: 917 us -> 0.02 us  [local(): lax.psum_scatter(feed_raw.reshape(devices * 2 * shard, units), both, scat...]
    dot_general x62 -> x2, matrix products: 557 us -> 1.49 us  [the longest x1 1.23 us: local(): lax.dot_general(mod_grad, cond_all.astype(f32), TN, precision=lax.Precisi...]
    pallas_call x0 -> x11, Pallas kernels: none -> 279 us  [the longest x2 98 us: attend_back(): pl.pallas_call(functools.partial(attend_back_kernel, heads, last), grid=(...]
    unnamed x16 -> x2, waiting for transfers between devices: 213 us -> 0.03 us
    sub x8 -> x0, other arithmetic: 171 us -> none  [local(): shifted = jnp.exp(logits - row_peak)]
    convert_element_type x22 -> x11, other arithmetic: 153 us -> 7.68 us  [the longest x1 3.23 us: local(): far = (back_far[0].astype(f32) + swap(back_far[1], 'row', rows, 1).astype...]
    all_gather x7 -> x1, waiting for transfers between devices: 145 us -> 0.01 us  [local(): feed_full = lax.all_gather(feed_shard, both, axis=0, tiled=True)]
    ppermute x0 -> x55, waiting for transfers between devices: none -> 137 us  [swap(): lax.ppermute(value, axis, [(place, place ^ step) for place in range(size)])]
  transfers between devices with their start and end apart: 14 -> 61, of which waited for: 11 -> 21; matrix products, arithmetic and copies ran while one was open for 26% -> 10% of each run, Pallas kernels for 0% -> 33%
where the time goes in v1:
time: 661 us; the launch traced here: 654 us
  Pallas kernels  279 us (42%)
  waiting for transfers between devices  152 us (23%)
  starting transfers between devices  123 us (19%)
  local copies, waits for them, and re-layouts  44.8 us (7%)
  other arithmetic  32 us (5%)
  between operations  22 us (3%)
    ppermute x55, waiting for transfers between devices, swap(): lax.ppermute(value, axis, [(place, place ^ step) for place in range(size)])  137 us
    pallas_call x2, Pallas kernels, attend_back(): pl.pallas_call(functools.partial(attend_back_kernel, heads, last), grid=(...  98 us
    ppermute x55, starting transfers between devices, swap(): lax.ppermute(value, axis, [(place, place ^ step) for place in range(size)])  96.7 us
    pallas_call x1, Pallas kernels, feed_forward(): pl.pallas_call(feed_kernel, grid=(units // block,), in_specs=[whole(pltpu...  65.7 us
    pallas_call x2, Pallas kernels, attend(): pl.pallas_call(functools.partial(attend_kernel, heads), grid=(count // bl...  55.7 us
    pallas_call x2, Pallas kernels, first_back(): pl.pallas_call(functools.partial(first_back_kernel, half, last), grid=(2...  26.8 us
    pallas_call x2, Pallas kernels, project_qkv(): pl.pallas_call(functools.partial(qkv_kernel, half), grid=(2 * half,), in_...  18 us
    unnamed x108, local copies, waits for them, and re-layouts  16.7 us
  transfers between devices with their start and end apart: 61, of which 21 were waited for; matrix products, arithmetic and copies ran while one was open for 10% of the time, Pallas kernels for 33%

profile of v1, /device:TPU:0, one launch (start us, length us, event | category | flops | bytes accessed | tf_op | source)
XLA Modules:
  0.0 653.9 jit_solution(8001332162681996040)
XLA Ops:
  20.3 4.8 all-to-all-start
  37.3 4.1 collective-permute-done.19
  42.1 4.9 collective-permute-done.20
  60.9 4.9 collective-permute-done.4
  68.5 8.7 %collective-permute-done.5 = bf16[4,32,768]{2,1,0:T(8,128)(2,1)S(1)} collective-permute-done((bf16[4,32,768]{2,1,0:T(8,128)(2,1)S(1)}, bf16[4,32,768]{2,1,0:T(8,128)(2,1)S(1)}, u32[]{:S(2)}, u32[]{:S(2)}) %collective-permute-start.5) | collective-permute-done | bytes 196640 | tf_op jit(solution)/shard_map/ppermute | solution.py:557
  81.2 15.0 %collective-permute-done.6 = bf16[4,32,768]{2,1,0:T(8,128)(2,1)S(1)} collective-permute-done((bf16[4,32,768]{2,1,0:T(8,128)(2,1)S(1)}, bf16[4,32,768]{2,1,0:T(8,128)(2,1)S(1)}, u32[]{:S(2)}, u32[]{:S(2)}) %collective-permute-start.6) | collective-permute-done | bytes 196640 | tf_op jit(solution)/shard_map/ppermute | solution.py:557
  96.2 17.3 %collective-permute-done.7 = bf16[4,32,768]{2,1,0:T(8,128)(2,1)S(1)} collective-permute-done((bf16[4,32,768]{2,1,0:T(8,128)(2,1)S(1)}, bf16[4,32,768]{2,1,0:T(8,128)(2,1)S(1)}, u32[]{:S(2)}, u32[]{:S(2)}) %collective-permute-start.7) | collective-permute-done | bytes 196640 | tf_op jit(solution)/shard_map/ppermute | solution.py:557
  113.6 7.5 %collective-permute-start.10 = (bf16[4,32,768]{2,1,0:T(8,128)(2,1)S(1)}, bf16[4,32,768]{2,1,0:T(8,128)(2,1)S(1)}, u32[]{:S(2)}, u32[]{:S(2)}) collective-permute-start(bf16[4,32,768]{2,1,0:T(8,128)(2,1)S(1)} %pad_maximum_fusion.10), channel_id=1, source_target_pairs={{0,28},{4,24},{8,20},{12,16},{16,12},{20,8},{24,4},{28,0},{1,29},{... | collective-permute-start | bytes 589832 | tf_op jit(solution)/shard_map/ppermute | solution.py:557
  121.1 6.3 collective-permute-start.27
  134.1 14.4 %all-to-all-start.1 = ((f32[32,12,192]{2,1,0:T(8,128)}), f32[32,12,192]{2,1,0:T(8,128)S(1)}, u32[]{:S(2)}, u32[]{:S(2)}) async-start(f32[32,12,192]{2,1,0:T(8,128)} %bitcast.4), calls=%async_computation.1 | async-start | bytes 1048576 | tf_op jit(solution)/shard_map/all_to_all | solution.py:667
  159.6 14.5 %all-to-all-done.1 = f32[32,12,192]{2,1,0:T(8,128)S(1)} async-done(((f32[32,12,192]{2,1,0:T(8,128)}), f32[32,12,192]{2,1,0:T(8,128)S(1)}, u32[]{:S(2)}, u32[]{:S(2)}) %all-to-all-start.1) | async-done | bytes 294944 | tf_op jit(solution)/shard_map/all_to_all | solution.py:667
  175.4 9.0 %shard_map.487.q_ref.k1.v1 = bf16[768,1536]{1,0:T(8,128)(2,1)} custom-call(bf16[12,64,1024]{2,1,0:T(8,128)(2,1)} %bitcast.171, bf16[12,64,1024]{2,1,0:T(8,128)(2,1)} %collective-permute-done.two, f32[12,6,1024]{2,1,0:T(8,128)} %reshape.183.mod, bf16[768,1024]{1,0:T(8,128)(2,1)} %bitcast.184, f32[32,1536]{1,0:T(8,128)} %get-tuple-element.179.cosine, ...), custom_call_target="tpu_custom_call" | custom-call | flops 2415919104 | bytes 6291456 | tf_op jit(solution)/shard_map/pallas_call | solution.py:118
  184.4 9.0 %shard_map.488.k2.v2.q_ref = bf16[768,1536]{1,0:T(8,128)(2,1)} custom-call(bf16[12,64,1024]{2,1,0:T(8,128)(2,1)} %collective-permute-done.14.one, bf16[12,64,1024]{2,1,0:T(8,128)(2,1)} %collective-permute-done.15.two, f32[12,6,1024]{2,1,0:T(8,128)} %reshape.183.mod, bf16[768,1024]{1,0:T(8,128)(2,1)} %bitcast.185, f32[32,1536]{1,0:T(8,128)} %get-tuple-element.180.cosine, ...), custom_call_target="tpu_custom_call" | custom-call | flops 2415919104 | bytes 6291456 | tf_op jit(solution)/shard_map/pallas_call | solution.py:118
  193.4 27.7 %shard_map.490 = (bf16[256,1536]{1,0:T(8,128)(2,1)}, f32[4,1536]{1,0:T(4,128)}) custom-call(bf16[768,1536]{1,0:T(8,128)(2,1)} %shard_map.488.k2.v2.q_ref, bf16[768,1536]{1,0:T(8,128)(2,1)} %shard_map.487.q_ref.k1.v1, bf16[768,1536]{1,0:T(8,128)(2,1)} %shard_map.488.k2.v2.q_ref, bf16[768,1536]{1,0:T(8,128)(2,1)} %shard_map.487.q_ref.k1.v1, ...), custom_call_target="tpu_custom_call" | custom-call | flops 19327352832 | bytes 3145728 | tf_op jit(solution)/shard_map/pallas_call | solution.py:172
  221.1 28.0 %shard_map.489 = (bf16[256,1536]{1,0:T(8,128)(2,1)}, f32[4,1536]{1,0:T(4,128)}) custom-call(bf16[768,1536]{1,0:T(8,128)(2,1)} %shard_map.487.q_ref.k1.v1, bf16[768,1536]{1,0:T(8,128)(2,1)} %shard_map.487.q_ref.k1.v1, bf16[768,1536]{1,0:T(8,128)(2,1)} %shard_map.488.k2.v2.q_ref, bf16[768,1536]{1,0:T(8,128)(2,1)} %shard_map.487.q_ref.k1.v1, ...), custom_call_target="tpu_custom_call" | custom-call | flops 19327352832 | bytes 3145728 | tf_op jit(solution)/shard_map/pallas_call | solution.py:172
  261.5 8.6 %collective-permute-done.17.a2 = bf16[256,768]{1,0:T(8,128)(2,1)S(1)} collective-permute-done((bf16[256,768]{1,0:T(8,128)(2,1)}, bf16[256,768]{1,0:T(8,128)(2,1)S(1)}, u32[]{:S(2)}, u32[]{:S(2)}) %collective-permute-start.17) | collective-permute-done | bytes 393248 | tf_op jit(solution)/shard_map/ppermute | solution.py:557
  270.9 7.5 %shard_map.491 = (f32[12,64,1024]{2,1,0:T(8,128)}, bf16[768,1024]{1,0:T(8,128)(2,1)}, bf16[768,1024]{1,0:T(8,128)(2,1)}) custom-call(s32[4]{0:T(128)} %iota_xor_fusion.order, bf16[256,768]{1,0:T(8,128)(2,1)} %get-tuple-element.140.a0, bf16[256,768]{1,0:T(8,128)(2,1)} %copy-done.27, bf16[256,768]{1,0:T(8,128)(2,1)} %copy-done.26, ...), custom_call_target="tpu_custom_call" | custom-call | flops 1610612736 | bytes 11010048 | tf_op jit(solution)/shard_map/pallas_call | solution.py:355
  278.4 65.7 %shard_map.492 = (bf16[32,2,32,4096]{3,2,1,0:T(8,128)(2,1)}, bf16[12,64,1024]{2,1,0:T(8,128)(2,1)}, f32[12,64,1024]{2,1,0:T(8,128)}, f32[12,4,1024]{2,1,0:T(4,12...) custom-call(s32[4]{0:T(128)} %iota_xor_fusion.order, ...), custom_call_target="tpu_custom_call" | custom-call | flops 38654705664 | bytes 33554432 | tf_op jit(solution)/shard_map/pallas_call | solution.py:447
  352.5 13.0 %collective-permute-done.30 = bf16[256,768]{1,0:T(8,128)(2,1)S(1)} collective-permute-done((bf16[256,768]{1,0:T(8,128)(2,1)}, bf16[256,768]{1,0:T(8,128)(2,1)S(1)}, u32[]{:S(2)}, u32[]{:S(2)}) %collective-permute-start.30) | collective-permute-done | bytes 393248 | tf_op jit(solution)/shard_map/ppermute | solution.py:557
  365.4 15.5 %collective-permute-done.31 = bf16[256,768]{1,0:T(8,128)(2,1)} collective-permute-done((bf16[256,768]{1,0:T(8,128)(2,1)}, bf16[256,768]{1,0:T(8,128)(2,1)}, u32[]{:S(2)}, u32[]{:S(2)}) %collective-permute-start.31) | collective-permute-done | bytes 393248 | tf_op jit(solution)/shard_map/ppermute | solution.py:557
  382.9 47.7 %shard_map.493 = (bf16[256,1536]{1,0:T(8,128)(2,1)}, f32[256,3072]{1,0:T(8,128)}, f32[256,3072]{1,0:T(8,128)}) custom-call(bf16[768,1536]{1,0:T(8,128)(2,1)} %shard_map.487.q_ref.k1.v1, bf16[768,1536]{1,0:T(8,128)(2,1)} %shard_map.487.q_ref.k1.v1, bf16[768,1536]{1,0:T(8,128)(2,1)} %shard_map.488.k2.v2.q_ref, bf16[768,1536]{1,0:T(8,128)(2,1)} %shard_map.487.q_ref.k1.v1, ...), custom_call_target="tpu_custom_call" | custom-call | flops 41070624768 | bytes 6291456 | tf_op jit(solution)/shard_map/pallas_call | solution.py:314
  430.6 50.3 %shard_map.494 = (bf16[256,1536]{1,0:T(8,128)(2,1)}, bf16[256,3072]{1,0:T(8,128)(2,1)}, bf16[256,3072]{1,0:T(8,128)(2,1)}) custom-call(bf16[768,1536]{1,0:T(8,128)(2,1)} %shard_map.488.k2.v2.q_ref, bf16[768,1536]{1,0:T(8,128)(2,1)} %shard_map.487.q_ref.k1.v1, bf16[768,1536]{1,0:T(8,128)(2,1)} %shard_map.488.k2.v2.q_ref, ...), custom_call_target="tpu_custom_call" | custom-call | flops 41070624768 | bytes 6291456 | tf_op jit(solution)/shard_map/pallas_call | solution.py:314
  480.8 12.5 %shard_map.495 = (bf16[2,768,1024]{2,1,0:T(8,128)(2,1)}, f32[768,1024]{1,0:T(8,128)}, f32[12,2,1024]{2,1,0:T(2,128)}) custom-call(bf16[12,64,1024]{2,1,0:T(8,128)(2,1)} %collective-permute-done.14.one, bf16[12,64,1024]{2,1,0:T(8,128)(2,1)} %collective-permute-done.15.two, f32[12,6,1024]{2,1,0:T(8,128)} %reshape.183.mod, ...), custom_call_target="tpu_custom_call" | custom-call | flops 4831838208 | bytes 9437184 | tf_op jit(solution)/shard_map/pallas_call | solution.py:521
  495.0 14.3 %shard_map.496 = (bf16[2,768,1024]{2,1,0:T(8,128)(2,1)}, bf16[1024,768]{1,0:T(8,128)(2,1)}, f32[12,2,1024]{2,1,0:T(2,128)}) custom-call(bf16[12,64,1024]{2,1,0:T(8,128)(2,1)} %bitcast.174, bf16[12,64,1024]{2,1,0:T(8,128)(2,1)} %collective-permute-done.two, f32[12,6,1024]{2,1,0:T(8,128)} %reshape.183.mod, bf16[256,1536]{1,0:T(8,128)(2,1)} %get-tuple-element.71.dq, ...), custom_call_target="tpu_custom_call" | custom-call | flops 4831838208 | bytes 9437184 | tf_op jit(solution)/shard_map/pallas_call | solution.py:521
  528.1 10.4 %collective-permute-done.35 = bf16[4,32,768]{2,1,0:T(8,128)(2,1)S(1)} collective-permute-done((bf16[4,32,768]{2,1,0:T(8,128)(2,1)S(1)}, bf16[4,32,768]{2,1,0:T(8,128)(2,1)S(1)}, u32[]{:S(2)}, u32[]{:S(2)}) %collective-permute-start.35) | collective-permute-done | bytes 196640 | tf_op jit(solution)/shard_map/ppermute | solution.py:557
  538.5 20.1 %collective-permute-start.37 = (bf16[4,32,768]{2,1,0:T(8,128)(2,1)S(1)}, bf16[4,32,768]{2,1,0:T(8,128)(2,1)S(1)}, u32[]{:S(2)}, u32[]{:S(2)}) collective-permute-start(bf16[4,32,768]{2,1,0:T(8,128)(2,1)S(1)} %get-tuple-element.135), channel_id=1, source_target_pairs={{0,12},{4,8},{8,4},{12,0},{16,28},{20,24},{24,20},{28,16},{1,13},{... | collective-permute-start | bytes 589832 | tf_op jit(solution)/shard_map/ppermute | solution.py:557
  558.6 5.4 collective-permute-start.36
  564.3 7.8 %collective-permute-done.38 = bf16[4,32,768]{2,1,0:T(8,128)(2,1)S(1)} collective-permute-done((bf16[4,32,768]{2,1,0:T(8,128)(2,1)S(1)}, bf16[4,32,768]{2,1,0:T(8,128)(2,1)S(1)}, u32[]{:S(2)}, u32[]{:S(2)}) %collective-permute-start.38) | collective-permute-done | bytes 196640 | tf_op jit(solution)/shard_map/ppermute | solution.py:557
  572.1 5.2 collective-permute-done.36
  591.2 4.2 collective-permute-start.48
  620.1 5.8 collective-permute-done.34.three
  626.0 7.2 %shard_map.497 = f32[12,64,1024]{2,1,0:T(8,128)} custom-call(bf16[12,64,1024]{2,1,0:T(8,128)(2,1)} %bitcast.175, f32[12,6,1024]{2,1,0:T(8,128)} %reshape.183.mod, f32[12,64,1024]{2,1,0:T(8,128)} %get-tuple-element.67.middle_grad, bf16[768,1024]{1,0:T(8,128)(2,1)} %get-tuple-element.123.one, bf16[768,1024]{1,0:T(8,128)(2,1)} %collective-permute-done.32.two, ...), custom_call_target="tpu_custom_call" | custom-call | flops 15728640 | bytes 12582912 | tf_op jit(solution)/shard_map/pallas_call | solution.py:545
  (299 shorter events, 154.6 us)
Async XLA Ops:
  7.2 271.2 %all-gather.2.cloned.1.call-start = ((), (), s32[]{:S(2)}) async-start(), calls=%async_computation.5 | async-start | bytes 17301504 | tf_op jit(solution)/shard_map/all_gather | solution.py:634
  15.3 38.9 %collective-permute-start.24 = (bf16[32,1024]{1,0:T(8,128)(2,1)}, bf16[32,1024]{1,0:T(8,128)(2,1)}, u32[]{:S(2)}, u32[]{:S(2)}) collective-permute-start(bf16[32,1024]{1,0:T(8,128)(2,1)} %convert_bitcast_fusion.1), channel_id=1, source_target_pairs={{0,24},{4,28},{8,16},{12,20},{16,8},{20,12},{24,0},{28,4},{1,25},{... | collective-permute-start | bytes 196616 | tf_op jit(solution)/shard_map/ppermute | solution.py:557
  19.2 31.8 %collective-permute-start.23 = (bf16[32,1024]{1,0:T(8,128)(2,1)}, bf16[32,1024]{1,0:T(8,128)(2,1)}, u32[]{:S(2)}, u32[]{:S(2)}) collective-permute-start(bf16[32,1024]{1,0:T(8,128)(2,1)} %convert_bitcast_fusion.1), channel_id=1, source_target_pairs={{0,20},{4,16},{8,28},{12,24},{16,4},{20,0},{24,12},{28,8},{1,21},{... | collective-permute-start | bytes 196616 | tf_op jit(solution)/shard_map/ppermute | solution.py:557
  20.3 112.5 %all-to-all-start = ((bf16[8,12,1024]{2,1,0:T(8,128)(2,1)}), bf16[8,12,1024]{2,1,0:T(8,128)(2,1)S(1)}, u32[]{:S(2)}, u32[]{:S(2)}) async-start(bf16[8,12,1024]{2,1,0:T(8,128)(2,1)} %broadcast_in_dim.30), calls=%async_computation | async-start | bytes 524288 | tf_op jit(solution)/shard_map/all_to_all | solution.py:657
  31.3 19.6 %collective-permute-start.22 = (bf16[32,1024]{1,0:T(8,128)(2,1)}, bf16[32,1024]{1,0:T(8,128)(2,1)S(1)}, u32[]{:S(2)}, u32[]{:S(2)}) collective-permute-start(bf16[32,1024]{1,0:T(8,128)(2,1)} %convert_bitcast_fusion.1), channel_id=1, source_target_pairs={{0,16},{4,20},{8,24},{12,28},{16,0},{20,4},{24,8},{28,12},{1,17},{... | collective-permute-start | bytes 196616 | tf_op jit(solution)/shard_map/ppermute | solution.py:557
  49.3 78.3 %collective-permute-start.14 = (bf16[12,64,1024]{2,1,0:T(8,128)(2,1)S(1)}, bf16[12,64,1024]{2,1,0:T(8,128)(2,1)}, u32[]{:S(2)}, u32[]{:S(2)}) collective-permute-start(bf16[12,64,1024]{2,1,0:T(8,128)(2,1)S(1)} %bitcast.176), channel_id=1, source_target_pairs={{0,2},{1,3},{2,0},{3,1},{4,6},{5,7},{6,4},{7,5},{8,10},{9,11},{10,... | collective-permute-start | bytes 4718600 | tf_op jit(solution)/shard_map/ppermute | solution.py:557
  50.8 124.6 %collective-permute-start = (bf16[12,64,1024]{2,1,0:T(8,128)(2,1)S(1)}, bf16[12,64,1024]{2,1,0:T(8,128)(2,1)}, u32[]{:S(2)}, u32[]{:S(2)}) collective-permute-start(bf16[12,64,1024]{2,1,0:T(8,128)(2,1)S(1)} %bitcast.177), channel_id=1, source_target_pairs={{0,1},{1,0},{2,3},{3,2},{4,5},{5,4},{6,7},{7,6},{8,9},{9,8},{10,11... | collective-permute-start | bytes 4718600 | tf_op jit(solution)/shard_map/ppermute | solution.py:557
  51.0 76.5 %collective-permute-start.9 = (bf16[4,32,768]{2,1,0:T(8,128)(2,1)S(1)}, bf16[4,32,768]{2,1,0:T(8,128)(2,1)S(1)}, u32[]{:S(2)}, u32[]{:S(2)}) collective-permute-start(bf16[4,32,768]{2,1,0:T(8,128)(2,1)S(1)} %pad_maximum_fusion.10), channel_id=1, source_target_pairs={{0,24},{4,28},{8,16},{12,20},{16,8},{20,12},{24,0},{28,4},{1,25},{... | collective-permute-start | bytes 589832 | tf_op jit(solution)/shard_map/ppermute | solution.py:557
  54.2 66.9 %collective-permute-start.8 = (bf16[4,32,768]{2,1,0:T(8,128)(2,1)S(1)}, bf16[4,32,768]{2,1,0:T(8,128)(2,1)S(1)}, u32[]{:S(2)}, u32[]{:S(2)}) collective-permute-start(bf16[4,32,768]{2,1,0:T(8,128)(2,1)S(1)} %pad_maximum_fusion.10), channel_id=1, source_target_pairs={{0,20},{4,16},{8,28},{12,24},{16,4},{20,0},{24,12},{28,8},{1,21},{... | collective-permute-start | bytes 589832 | tf_op jit(solution)/shard_map/ppermute | solution.py:557
  77.3 18.9 %collective-permute-start.6 = (bf16[4,32,768]{2,1,0:T(8,128)(2,1)S(1)}, bf16[4,32,768]{2,1,0:T(8,128)(2,1)S(1)}, u32[]{:S(2)}, u32[]{:S(2)}) collective-permute-start(bf16[4,32,768]{2,1,0:T(8,128)(2,1)S(1)} %pad_maximum_fusion.10), channel_id=1, source_target_pairs={{0,12},{4,8},{8,4},{12,0},{16,28},{20,24},{24,20},{28,16},{1,13},{... | collective-permute-start | bytes 589832 | tf_op jit(solution)/shard_map/ppermute | solution.py:557
  121.1 38.3 %collective-permute-start.27 = (bf16[8,32,1024]{2,1,0:T(8,128)(2,1)}, bf16[8,32,1024]{2,1,0:T(8,128)(2,1)}, u32[]{:S(2)}, u32[]{:S(2)}) collective-permute-start(bf16[8,32,1024]{2,1,0:T(8,128)(2,1)} %constant_dynamic-update-slice_fusion.8), channel_id=1, source_target_pairs={{0,2},{1,3},{2,0},{3,1},{4,6},{5,7},{6,4},{7,5},{8,10},{9,11},{10,... | collective-permute-start | bytes 1572872 | tf_op jit(solution)/shard_map/ppermute | solution.py:557
  127.4 125.3 %collective-permute-start.26 = (bf16[8,32,1024]{2,1,0:T(8,128)(2,1)}, bf16[8,32,1024]{2,1,0:T(8,128)(2,1)}, u32[]{:S(2)}, u32[]{:S(2)}) collective-permute-start(bf16[8,32,1024]{2,1,0:T(8,128)(2,1)} %constant_dynamic-update-slice_fusion.8), channel_id=1, source_target_pairs={{0,1},{1,0},{2,3},{3,2},{4,5},{5,4},{6,7},{7,6},{8,9},{9,8},{10,11... | collective-permute-start | bytes 1572872 | tf_op jit(solution)/shard_map/ppermute | solution.py:557
  127.6 56.8 %collective-permute-start.15 = (bf16[12,64,1024]{2,1,0:T(8,128)(2,1)}, bf16[12,64,1024]{2,1,0:T(8,128)(2,1)}, u32[]{:S(2)}, u32[]{:S(2)}) collective-permute-start(bf16[12,64,1024]{2,1,0:T(8,128)(2,1)} %collective-permute-done.14.one), channel_id=1, source_target_pairs={{0,1},{1,0},{2,3},{3,2},{4,5},{5,4},{6,7},{7,6},{8,9},{9,8},{10,11... | collective-permute-start | bytes 4718600 | tf_op jit(solution)/shard_map/ppermute | solution.py:557
  134.1 40.1 %all-to-all-start.1 = ((f32[32,12,192]{2,1,0:T(8,128)}), f32[32,12,192]{2,1,0:T(8,128)S(1)}, u32[]{:S(2)}, u32[]{:S(2)}) async-start(f32[32,12,192]{2,1,0:T(8,128)} %bitcast.4), calls=%async_computation.1 | async-start | bytes 1048576 | tf_op jit(solution)/shard_map/all_to_all | solution.py:667
  148.5 464.9 %reduce-scatter.2.cloned.1.call-start = ((), (), s32[]{:S(2)}) async-start(), calls=%async_computation.6 | async-start | bytes 17301504 | tf_op jit(solution)/shard_map/reduce_scatter | solution.py:713
  159.4 93.4 %collective-permute-start.28 = (bf16[8,32,1024]{2,1,0:T(8,128)(2,1)}, bf16[8,32,1024]{2,1,0:T(8,128)(2,1)}, u32[]{:S(2)}, u32[]{:S(2)}) collective-permute-start(bf16[8,32,1024]{2,1,0:T(8,128)(2,1)} %collective-permute-done.27), channel_id=1, source_target_pairs={{0,1},{1,0},{2,3},{3,2},{4,5},{5,4},{6,7},{7,6},{8,9},{9,8},{10,11... | collective-permute-start | bytes 1572872 | tf_op jit(solution)/shard_map/ppermute | solution.py:557
  250.2 19.9 %collective-permute-start.17 = (bf16[256,768]{1,0:T(8,128)(2,1)}, bf16[256,768]{1,0:T(8,128)(2,1)S(1)}, u32[]{:S(2)}, u32[]{:S(2)}) collective-permute-start(bf16[256,768]{1,0:T(8,128)(2,1)} %get-tuple-element.138), channel_id=1, source_target_pairs={{0,2},{1,3},{2,0},{3,1},{4,6},{5,7},{6,4},{7,5},{8,10},{9,11},{10,... | collective-permute-start | bytes 1179656 | tf_op jit(solution)/shard_map/ppermute | solution.py:557
  344.2 21.2 %collective-permute-start.30 = (bf16[256,768]{1,0:T(8,128)(2,1)}, bf16[256,768]{1,0:T(8,128)(2,1)S(1)}, u32[]{:S(2)}, u32[]{:S(2)}) collective-permute-start(bf16[256,768]{1,0:T(8,128)(2,1)} %get-tuple-element.72), channel_id=1, source_target_pairs={{0,2},{1,3},{2,0},{3,1},{4,6},{5,7},{6,4},{7,5},{8,10},{9,11},{10,... | collective-permute-start | bytes 1179656 | tf_op jit(solution)/shard_map/ppermute | solution.py:557
  344.8 36.1 %collective-permute-start.31 = (bf16[256,768]{1,0:T(8,128)(2,1)}, bf16[256,768]{1,0:T(8,128)(2,1)}, u32[]{:S(2)}, u32[]{:S(2)}) collective-permute-start(bf16[256,768]{1,0:T(8,128)(2,1)} %get-tuple-element.73), channel_id=1, source_target_pairs={{0,3},{1,2},{2,1},{3,0},{4,7},{5,6},{6,5},{7,4},{8,11},{9,10},{10,... | collective-permute-start | bytes 1179656 | tf_op jit(solution)/shard_map/ppermute | solution.py:557
  350.2 176.0 %collective-permute-start.46 = (bf16[8,32,1024]{2,1,0:T(8,128)(2,1)}, bf16[8,32,1024]{2,1,0:T(8,128)(2,1)S(1)}, u32[]{:S(2)}, u32[]{:S(2)}) collective-permute-start(bf16[8,32,1024]{2,1,0:T(8,128)(2,1)} %get-tuple-element.125), channel_id=1, source_target_pairs={{0,1},{1,0},{2,3},{3,2},{4,5},{5,4},{6,7},{7,6},{8,9},{9,8},{10,11... | collective-permute-start | bytes 1572872 | tf_op jit(solution)/shard_map/ppermute | solution.py:557
  494.9 84.5 %collective-permute-start.33 = (bf16[768,1024]{1,0:T(8,128)(2,1)S(1)}, bf16[768,1024]{1,0:T(8,128)(2,1)}, u32[]{:S(2)}, u32[]{:S(2)}) collective-permute-start(bf16[768,1024]{1,0:T(8,128)(2,1)S(1)} %slice_bitcast_fusion), channel_id=1, source_target_pairs={{0,1},{1,0},{2,3},{3,2},{4,5},{5,4},{6,7},{7,6},{8,9},{9,8},{10,11... | collective-permute-start | bytes 4718600 | tf_op jit(solution)/shard_map/ppermute | solution.py:557
  511.5 83.9 %all-to-all-start.2 = ((f32[32,12,192]{2,1,0:T(8,128)}), f32[32,12,192]{2,1,0:T(8,128)S(1)}, u32[]{:S(2)}, u32[]{:S(2)}) async-start(f32[32,12,192]{2,1,0:T(8,128)} %bitcast.161), calls=%async_computation.2 | async-start | bytes 1048576 | tf_op jit(solution)/shard_map/all_to_all | solution.py:759
  516.9 21.6 %collective-permute-start.35 = (bf16[4,32,768]{2,1,0:T(8,128)(2,1)S(1)}, bf16[4,32,768]{2,1,0:T(8,128)(2,1)S(1)}, u32[]{:S(2)}, u32[]{:S(2)}) collective-permute-start(bf16[4,32,768]{2,1,0:T(8,128)(2,1)S(1)} %get-tuple-element.130), channel_id=1, source_target_pairs={{0,4},{4,0},{8,12},{12,8},{16,20},{20,16},{24,28},{28,24},{1,5},{5... | collective-permute-start | bytes 589832 | tf_op jit(solution)/shard_map/ppermute | solution.py:557
  518.7 19.8 %collective-permute-start.41 = (bf16[4,32,768]{2,1,0:T(8,128)(2,1)S(1)}, bf16[4,32,768]{2,1,0:T(8,128)(2,1)S(1)}, u32[]{:S(2)}, u32[]{:S(2)}) collective-permute-start(bf16[4,32,768]{2,1,0:T(8,128)(2,1)S(1)} %get-tuple-element.131), channel_id=1, source_target_pairs={{0,28},{4,24},{8,20},{12,16},{16,12},{20,8},{24,4},{28,0},{1,29},{... | collective-permute-start | bytes 589832 | tf_op jit(solution)/shard_map/ppermute | solution.py:557
  522.1 36.5 %collective-permute-start.40 = (bf16[4,32,768]{2,1,0:T(8,128)(2,1)S(1)}, bf16[4,32,768]{2,1,0:T(8,128)(2,1)S(1)}, u32[]{:S(2)}, u32[]{:S(2)}) collective-permute-start(bf16[4,32,768]{2,1,0:T(8,128)(2,1)S(1)} %get-tuple-element.132), channel_id=1, source_target_pairs={{0,24},{4,28},{8,16},{12,20},{16,8},{20,12},{24,0},{28,4},{1,25},{... | collective-permute-start | bytes 589832 | tf_op jit(solution)/shard_map/ppermute | solution.py:557
  526.2 38.0 %collective-permute-start.39 = (bf16[4,32,768]{2,1,0:T(8,128)(2,1)S(1)}, bf16[4,32,768]{2,1,0:T(8,128)(2,1)S(1)}, u32[]{:S(2)}, u32[]{:S(2)}) collective-permute-start(bf16[4,32,768]{2,1,0:T(8,128)(2,1)S(1)} %get-tuple-element.133), channel_id=1, source_target_pairs={{0,20},{4,16},{8,28},{12,24},{16,4},{20,0},{24,12},{28,8},{1,21},{... | collective-permute-start | bytes 589832 | tf_op jit(solution)/shard_map/ppermute | solution.py:557
  538.5 33.6 %collective-permute-start.38 = (bf16[4,32,768]{2,1,0:T(8,128)(2,1)S(1)}, bf16[4,32,768]{2,1,0:T(8,128)(2,1)S(1)}, u32[]{:S(2)}, u32[]{:S(2)}) collective-permute-start(bf16[4,32,768]{2,1,0:T(8,128)(2,1)S(1)} %get-tuple-element.134), channel_id=1, source_target_pairs={{0,16},{4,20},{8,24},{12,28},{16,0},{20,4},{24,8},{28,12},{1,17},{... | collective-permute-start | bytes 589832 | tf_op jit(solution)/shard_map/ppermute | solution.py:557
  538.5 33.6 %collective-permute-start.37 = (bf16[4,32,768]{2,1,0:T(8,128)(2,1)S(1)}, bf16[4,32,768]{2,1,0:T(8,128)(2,1)S(1)}, u32[]{:S(2)}, u32[]{:S(2)}) collective-permute-start(bf16[4,32,768]{2,1,0:T(8,128)(2,1)S(1)} %get-tuple-element.135), channel_id=1, source_target_pairs={{0,12},{4,8},{8,4},{12,0},{16,28},{20,24},{24,20},{28,16},{1,13},{... | collective-permute-start | bytes 589832 | tf_op jit(solution)/shard_map/ppermute | solution.py:557
  564.2 26.6 %collective-permute-start.45 = (bf16[8,32,1024]{2,1,0:T(8,128)(2,1)S(1)}, bf16[8,32,1024]{2,1,0:T(8,128)(2,1)S(1)}, u32[]{:S(2)}, u32[]{:S(2)}) collective-permute-start(bf16[8,32,1024]{2,1,0:T(8,128)(2,1)S(1)} %copy-done.24), channel_id=1, source_target_pairs={{0,1},{1,0},{2,3},{3,2},{4,5},{5,4},{6,7},{7,6},{8,9},{9,8},{10,11... | collective-permute-start | bytes 1572872 | tf_op jit(solution)/shard_map/ppermute | solution.py:557
  572.1 18.7 %collective-permute-start.47 = (bf16[8,32,1024]{2,1,0:T(8,128)(2,1)S(1)}, bf16[8,32,1024]{2,1,0:T(8,128)(2,1)S(1)}, u32[]{:S(2)}, u32[]{:S(2)}) collective-permute-start(bf16[8,32,1024]{2,1,0:T(8,128)(2,1)S(1)} %fusion.1), channel_id=1, source_target_pairs={{0,2},{1,3},{2,0},{3,1},{4,6},{5,7},{6,4},{7,5},{8,10},{9,11},{10,... | collective-permute-start | bytes 1572872 | tf_op jit(solution)/shard_map/ppermute | solution.py:557
  586.5 33.6 %collective-permute-start.32 = (bf16[768,1024]{1,0:T(8,128)(2,1)}, bf16[768,1024]{1,0:T(8,128)(2,1)}, u32[]{:S(2)}, u32[]{:S(2)}) collective-permute-start(bf16[768,1024]{1,0:T(8,128)(2,1)} %get-tuple-element.122), channel_id=1, source_target_pairs={{0,1},{1,0},{2,3},{3,2},{4,5},{5,4},{6,7},{7,6},{8,9},{9,8},{10,11... | collective-permute-start | bytes 4718600 | tf_op jit(solution)/shard_map/ppermute | solution.py:557
  589.8 36.2 %collective-permute-start.34 = (bf16[768,1024]{1,0:T(8,128)(2,1)}, bf16[768,1024]{1,0:T(8,128)(2,1)}, u32[]{:S(2)}, u32[]{:S(2)}) collective-permute-start(bf16[768,1024]{1,0:T(8,128)(2,1)} %fusion), channel_id=1, source_target_pairs={{0,2},{1,3},{2,0},{3,1},{4,6},{5,7},{6,4},{7,5},{8,10},{9,11},{10,... | collective-permute-start | bytes 4718600 | tf_op jit(solution)/shard_map/ppermute | solution.py:557
  (70 other events, 622.5 us)
Sparse Core Ops, SparseCore 0:
  11.5 165.3 all-gather.1
  344.3 206.1 reduce-scatter.1

commit v2 on v1

--- a/solution.py
+++ b/solution.py
@@ -85,10 +85,10 @@
 def qkv_kernel(half, one, two, mod, weight, cosine, sine, out):
     step = pl.program_id(0)
     values = jnp.where(step < half, one[...].astype(f32), two[...].astype(f32))
-    normed, _ = layer_norm(values)
+    count, width = values.shape
+    normed, _ = layer_norm(values.reshape(mod.shape[0], -1, width))
     hidden = normed * (1.0 + mod[:, 1:2, :]) + mod[:, 0:1, :]
-    count = hidden.shape[0] * hidden.shape[1]
-    hidden = hidden.astype(bf16).reshape(count, hidden.shape[2])
+    hidden = hidden.astype(bf16).reshape(count, width)
     projected = dot(weight[...], hidden, NT)
     third = projected.shape[0] // 3
     cos, sin = cosine[...], sine[...]
@@ -99,22 +99,22 @@
     out[2 * third :, :] = projected[2 * third :].astype(bf16)
 
 
-def token_specs(frames, tokens, width, chunk):
+def token_specs(frames, block, width, chunk):
     half = frames // chunk
     return half, [
-        pl.BlockSpec((chunk, tokens, width), lambda i: (jnp.minimum(i, half - 1), 0, 0)),
-        pl.BlockSpec((chunk, tokens, width), lambda i: (jnp.maximum(i - half, 0), 0, 0)),
+        pl.BlockSpec((block, width), lambda i: (jnp.minimum(i, half - 1), 0)),
+        pl.BlockSpec((block, width), lambda i: (jnp.maximum(i - half, 0), 0)),
         pl.BlockSpec((chunk, 6, width), lambda i: (lax.rem(i, half), 0, 0)),
     ]
 
 
-def project_qkv(one, two, mod, weight, cosine, sine):
-    frames, tokens, width = one.shape
-    chunk = 4
-    half, specs = token_specs(frames, tokens, width, chunk)
-    block, total = chunk * tokens, 2 * frames * tokens
+def project_qkv(one, two, mod, weight, cosine, sine, offset):
+    total, width = cosine.shape[1] // 2, weight.shape[1]
+    frames, chunk = mod.shape[0], 4
+    block = total // 2 // frames * chunk
+    half, specs = token_specs(frames, block, width, chunk)
     rows = weight.shape[0]
-    angle = pl.BlockSpec((cosine.shape[0], block), lambda i: (0, i))
+    angle = pl.BlockSpec((cosine.shape[0], block), lambda i: (0, i + offset * 2 * half))
     return pl.pallas_call(
         functools.partial(qkv_kernel, half),
         grid=(2 * half,),
@@ -198,7 +198,7 @@
 
 
 def attend_back_kernel(
-    heads, last, q_ref, k1, k2, v1, v2, bias, out_ref, grad_ref, lse, cosine, sine, cos_all, sin_all,
+    heads, last, q_ref, k1, k2, v1, v2, bias, out_ref, grad1, grad2, lse, cosine, sine, cos_all, sin_all,
     *rest,
 ):
     if last:
@@ -209,6 +209,8 @@
     block = q_ref.shape[1]
     scale = HEAD_DIM ** (-0.5)
     step = pl.program_id(0)
+    first_half = step < pl.num_programs(0) // 2
+    grad_all = jnp.where(first_half, grad1[...].astype(f32), grad2[...].astype(f32)).astype(bf16)
 
     @pl.when(step == 0)
     def _():
@@ -238,7 +240,7 @@
             [high, low, jnp.ones((1, block), bf16), one, two, three, jnp.zeros((124, block), bf16)],
             axis=0,
         )
-        grad = grad_ref[rows, :]
+        grad = grad_all[rows, :]
         mean = jnp.sum(grad.astype(f32) * out_ref[rows, :].astype(f32), axis=0, keepdims=True)
         one, two, three = split3(-mean)
         grad_wide = jnp.concatenate([grad, one, two, three, jnp.zeros((61, block), bf16)], axis=0)
@@ -252,7 +254,7 @@
         probs = jnp.exp2(logits)
         low = probs.astype(bf16)
         logit_grad = (probs * centered).astype(bf16)
-        grad_pad = jnp.concatenate([grad_ref[rows, :], pad], axis=0)
+        grad_pad = jnp.concatenate([grad_all[rows, :], pad], axis=0)
         q_pad = jnp.concatenate([q_ref[rows, :], pad], axis=0)
         dv_sum[rows, :] += dot(grad_pad, low)[:HEAD_DIM]
         dk_sum[rows, :] += dot(q_pad, logit_grad)[:HEAD_DIM]
@@ -270,12 +272,13 @@
             dv[...] = dv_sum[...].astype(bf16)
 
 
-def attend_back(queries, ours, theirs, bias, out, grad, lse, angles, offset, sums=None):
+def attend_back(queries, ours, theirs, bias, out, grads, lse, angles, offset, sums=None):
     rows, count = queries.shape[0] // 3, queries.shape[1]
     total = bias.shape[1]
     heads = rows // HEAD_DIM
     block = 256 if count % 256 == 0 else 128
     steps = count // block
+    half = steps // 2
     last = sums is not None
     cosine, sine = angles
 
@@ -293,14 +296,15 @@
         piece(2),
         pl.BlockSpec((1, total), lambda i: (0, 0)),
         moving,
-        moving,
+        pl.BlockSpec((rows, block), lambda i: (0, jnp.minimum(i, half - 1))),
+        pl.BlockSpec((rows, block), lambda i: (0, jnp.maximum(i - half, 0))),
         pl.BlockSpec((heads, block), lambda i: (0, i)),
         angle,
         angle,
         whole(),
         whole(),
     ]
-    operands = [queries, ours, theirs, ours, theirs, bias, out, grad, lse, cosine, sine, cosine, sine]
+    operands = [queries, ours, theirs, ours, theirs, bias, out, *grads, lse, cosine, sine, cosine, sine]
     kind = f32
     scratch = [
         VMEM((heads, 256, total), bf16),
@@ -447,7 +451,10 @@
     return pl.pallas_call(
         feed_kernel,
         grid=(units // block,),
-        in_specs=[whole(pltpu.SMEM), spec] + [whole()] * 11,
+        in_specs=[whole(pltpu.SMEM), spec]
+        + [whole()] * 6
+        + [pl.BlockSpec((features, count), lambda i: (0, 0))] * 4
+        + [whole()],
         out_specs=[spec] + [whole()] * 8,
         out_shape=[
             jax.ShapeDtypeStruct(weights.shape, bf16),
@@ -477,10 +484,11 @@
         mod_grad[...] = mod_in[...] if last else jnp.zeros_like(mod_grad)
 
     values = jnp.where(step < half, one[...].astype(f32), two[...].astype(f32))
-    normed, _ = layer_norm(values)
+    count, width = values.shape
+    shape = (chunk, count // chunk, width)
+    normed, _ = layer_norm(values.reshape(shape))
     hidden = normed * (1.0 + mod[:, 1:2, :]) + mod[:, 0:1, :]
-    shape = hidden.shape
-    hidden = hidden.astype(bf16).reshape(shape[0] * shape[1], shape[2])
+    hidden = hidden.astype(bf16).reshape(count, width)
     pieces = jnp.concatenate([dq[...], dk[...], dv[...]], axis=0)
     total[...] += dot(pieces, hidden)
     back = dot(pieces, weight[...], TN)
@@ -498,11 +506,11 @@
 
 
 def first_back(one, two, mod, dq, dk, dv, weight, offset, sums=None):
-    frames, tokens, width = one.shape
-    chunk = 4
-    half, specs = token_specs(frames, tokens, width, chunk)
-    block, count = chunk * tokens, 2 * frames * tokens
-    rows = dq.shape[0]
+    rows, count = dq.shape
+    frames, width = mod.shape[0], weight.shape[1]
+    chunk, tokens = 4, count // 2 // frames
+    block = chunk * tokens
+    half, specs = token_specs(frames, block, width, chunk)
     last = sums is not None
     moved = pl.BlockSpec((rows, block), lambda i: (0, i + offset * 2 * half))
     in_specs = specs + [pl.BlockSpec((rows, block), lambda i: (0, i)), moved, moved, whole()]
@@ -555,26 +563,6 @@
 
 def swap(value, axis, size, step):
     return lax.ppermute(value, axis, [(place, place ^ step) for place in range(size)])
-
-
-def in_order(stacked, place):
-    count = stacked.shape[0]
-    return jnp.concatenate(
-        [lax.dynamic_index_in_dim(stacked, place ^ index, 0) for index in range(count)], axis=0
-    )
-
-
-def gather_clip(value, clips, clip):
-    pieces = [value] + [swap(value, "clip", clips, step) for step in range(1, clips)]
-    return in_order(jnp.stack(pieces), clip)
-
-
-def sum_clip(value, clips, clip):
-    total = lax.dynamic_index_in_dim(value, clip, 0, keepdims=False).astype(f32)
-    for step in range(1, clips):
-        piece = lax.dynamic_index_in_dim(value, clip ^ step, 0, keepdims=False)
-        total = total + swap(piece, "clip", clips, step).astype(f32)
-    return total
 
 
 def adam_update(master, first, second, gradient, rate, decay):
@@ -622,7 +610,7 @@
     count = frames * per_frame
     devices = clips * rows
     features = width // rows
-    clip, row = lax.axis_index("clip"), lax.axis_index("row")
+    row = lax.axis_index("row")
     both = ("clip", "row")
     order = (row ^ jnp.arange(rows)).astype(jnp.int32)
 
@@ -637,73 +625,75 @@
     if not fused:
         feed_full = feed_full.transpose(1, 0, 2, 3).reshape(1, 2, width, units)
 
-    own = tokens.reshape(frames, per_frame, width)
-    upstream = cotangent.reshape(frames, per_frame, width)
-    tok1 = swap(own, "row", rows, 1)
-    tok2 = swap(own, "row", rows, 2)
-    tok3 = swap(tok2, "row", rows, 1)
-
-    attend_mine = attend_weight.astype(bf16).reshape(shard, 3, rows, features)
-    attend_mine = attend_mine.transpose(2, 0, 1, 3).reshape(rows, shard, 3 * features)
-    pieces = []
-    for step in range(rows):
-        piece = lax.dynamic_index_in_dim(attend_mine, row ^ step, 0, keepdims=False)
-        pieces.append(swap(piece, "row", rows, step) if step else piece)
-    attend_clip = in_order(jnp.stack(pieces), row)
-    attend_full = gather_clip(attend_clip, clips, clip).reshape(width, 3 * features)
-    attend_turned = attend_full.T
-
     cond_act = jax.nn.silu(condition[0].astype(f32)).astype(bf16)
     cond_all = lax.all_to_all(
         jnp.broadcast_to(cond_act[None], (clips, frames, width)), "clip", 0, 0, tiled=True
     ).reshape(clips * frames, width)
-    mod_mine = dot(cond_all, adaptive_weight.astype(bf16)) + adaptive_offsets.astype(bf16).astype(
-        f32
-    )
-    part = mod_mine.shape[1]
-    mod_mine = jnp.broadcast_to(
-        mod_mine.reshape(clips, 1, frames, part), (clips, rows, frames, part)
-    )
-    mod = lax.all_to_all(mod_mine.reshape(devices, frames, part), both, 0, 0, tiled=True)
-    mod = mod.transpose(1, 0, 2).reshape(frames, 6, width)
-
+
+    own = tokens.reshape(frames, per_frame, width)
+    upstream = cotangent.reshape(frames, per_frame, width)
     frame_index = lax.broadcasted_iota(jnp.int32, (frames, patch_rows, grid_cols), 0)
     valid = (frame_index < frame_count[0]) & (patch_mask[0] == 1)
     small = jnp.stack(
         [positions[0].reshape(-1), positions[1].reshape(-1), valid.reshape(-1)]
+    ).astype(bf16)
+    spare = -(-count // width)
+    small = jnp.pad(small, ((0, 0), (0, spare * width - count))).reshape(3 * spare, width)
+    small = jnp.pad(small, ((0, 16 - 3 * spare), (0, 0)))
+    tok0 = jnp.concatenate([own.reshape(count, width), small], axis=0)
+    tok2 = swap(tok0, "row", rows, 2)
+    tok1 = swap(tok0, "row", rows, 1)
+    tok3 = swap(tok2, "row", rows, 1)
+
+    attend_mine = attend_weight.astype(bf16).reshape(shard, 3, rows, features)
+    attend_mine = attend_mine.transpose(2, 0, 1, 3).reshape(1, rows, shard, 3 * features)
+    attend_mine = jnp.broadcast_to(attend_mine, (clips, rows, shard, 3 * features))
+    attend_full = lax.all_to_all(
+        attend_mine.reshape(devices, shard, 3 * features), both, 0, 0, tiled=True
+    )
+    attend_turned = attend_full.reshape(width, 3 * features).T
+
+    mod_mine = dot(cond_all, adaptive_weight.astype(bf16)) + adaptive_offsets.astype(bf16).astype(
+        f32
+    )
+    part = mod_mine.shape[1]
+    mod_mine = jnp.broadcast_to(
+        mod_mine.reshape(clips, 1, frames, part), (clips, rows, frames, part)
+    )
+    mod = lax.all_to_all(mod_mine.reshape(devices, frames, part), both, 0, 0, tiled=True)
+    mod = mod.transpose(1, 0, 2).reshape(frames, 6, width)
+
+    small = jnp.concatenate(
+        [
+            piece[count : count + 3 * spare].reshape(3, spare * width)[:, :count]
+            for piece in (tok0, tok1, tok2, tok3)
+        ],
+        axis=1,
     ).astype(f32)
-    small = jnp.concatenate(
-        [small] + [swap(small, "row", rows, step) for step in range(1, rows)], axis=1
-    )
     bias = jnp.where(small[2:3] > 0.5, 0.0, MASKED)
     quarter = HEAD_DIM // 4
     freqs = jnp.exp(-math.log(10000.0) * jnp.arange(quarter, dtype=f32) / quarter)
     angles = jnp.concatenate([freqs[:, None] * small[0:1], freqs[:, None] * small[1:2]], axis=0)
     cosine, sine = jnp.cos(angles), jnp.sin(angles)
-    near = 2 * count
-
-    project_clip = gather_clip(project_weight.T.astype(bf16), clips, clip)
-    project_far = swap(project_clip, "row", rows, 2)
-    project_full = jnp.stack(
-        [
-            project_clip,
-            swap(project_clip, "row", rows, 1),
-            project_far,
-            swap(project_far, "row", rows, 1),
-        ]
-    )
-    project_full = in_order(project_full, row).transpose(1, 0, 2, 3).reshape(width, width).T
-
-    qkv_near = project_qkv(own, tok1, mod, attend_turned, cosine[:, :near], sine[:, :near])
-    qkv_far = project_qkv(tok2, tok3, mod, attend_turned, cosine[:, near:], sine[:, near:])
+
+    qkv_near = project_qkv(tok0, tok1, mod, attend_turned, cosine, sine, 0)
+    qkv_far = project_qkv(tok2, tok3, mod, attend_turned, cosine, sine, 1)
+
+    project_mine, qkv_near = lax.optimization_barrier((project_weight.T.astype(bf16), qkv_near))
+    project_full = lax.all_to_all(
+        jnp.broadcast_to(project_mine[None], (clips, shard, width)), "clip", 0, 0, tiled=True
+    )
+    project_full = lax.all_to_all(
+        jnp.broadcast_to(project_full[None], (rows, clips, shard, width)), "row", 0, 0, tiled=True
+    )
+    project_full = project_full.transpose(1, 0, 2, 3).reshape(width, width).T
+
     out_far, lse_far = attend(qkv_far, qkv_near, qkv_far, bias)
+    out_far, qkv_near = lax.optimization_barrier((out_far, qkv_near))
+    part2 = swap(out_far[:, :count], "row", rows, 2)
+    part3 = swap(out_far[:, count:], "row", rows, 3)
     out_near, lse_near = attend(qkv_near, qkv_near, qkv_far, bias)
-    parts = [
-        out_near[:, :count],
-        swap(out_near[:, count:], "row", rows, 1),
-        swap(out_far[:, :count], "row", rows, 2),
-        swap(out_far[:, count:], "row", rows, 3),
-    ]
+    parts = [out_near, swap(out_near[:, count:], "row", rows, 1), part2, part3]
     att_out, hidden_two, branch_grad = project_out(order, parts, project_full, own, upstream, mod)
     feed_raw, block_out, middle_grad, mod_late, d0, d1, d2, d3, project_raw = feed_forward(
         order, feed_full, hidden_two, branch_grad, own, upstream, att_out, mod, parts, project_full
@@ -716,32 +706,32 @@
     widen_sum, narrow_sum = feed_sum[:shard], feed_sum[shard:].T
 
     project_raw = project_raw.T.reshape(clips, rows, shard, width).transpose(1, 0, 2, 3)
-    piece = [lax.dynamic_index_in_dim(project_raw, row ^ step, 0, keepdims=False) for step in range(rows)]
-    here = (piece[0].astype(f32) + swap(piece[1], "row", rows, 1).astype(f32)).astype(bf16)
-    there = (piece[2].astype(f32) + swap(piece[3], "row", rows, 1).astype(f32)).astype(bf16)
-    here = (here.astype(f32) + swap(there, "row", rows, 2).astype(f32)).astype(bf16)
-    project_sum = sum_clip(here, clips, clip).T
-
-    grad_near = jnp.concatenate([d0, swap(d1, "row", rows, 1)], axis=1)
-    grad_far = jnp.concatenate([swap(d2, "row", rows, 2), swap(d3, "row", rows, 3)], axis=1)
+    project_raw = lax.all_to_all(project_raw, "row", 0, 0, tiled=True)
+    project_raw = jnp.sum(project_raw.astype(f32), axis=0).astype(bf16)
+    project_raw = lax.all_to_all(project_raw, "clip", 0, 0, tiled=True)
+    project_sum = jnp.sum(project_raw.astype(f32), axis=0).T
+
     turning = (cosine, sine)
+    d2 = swap(d2, "row", rows, 2)
+    d3 = swap(d3, "row", rows, 3)
+    d1 = swap(d1, "row", rows, 1)
     dq_near, dk, dv = attend_back(
-        qkv_near, qkv_near, qkv_far, bias, out_near, grad_near, lse_near, turning, 0
-    )
+        qkv_near, qkv_near, qkv_far, bias, out_near, (d0, d1), lse_near, turning, 0
+    )
+    dk, d2, d3 = lax.optimization_barrier((dk, d2, d3))
     dq_far, dk, dv = attend_back(
-        qkv_far, qkv_near, qkv_far, bias, out_far, grad_far, lse_far, turning, 1, (dk, dv)
+        qkv_far, qkv_near, qkv_far, bias, out_far, (d2, d3), lse_far, turning, 1, (dk, dv)
     )
     back_far, raw, mod_early = first_back(tok2, tok3, mod, dq_far, dk, dv, attend_turned, 1)
+    back_far, dq_near = lax.optimization_barrier((back_far, dq_near))
     back_near, attend_raw, mod_early = first_back(
-        own, tok1, mod, dq_near, dk, dv, attend_turned, 0, (raw, mod_early)
-    )
-
-    attend_mine = sum_clip(attend_raw.reshape(clips, rows, shard, 3 * features), clips, clip)
-    pieces = []
-    for step in range(rows):
-        piece = lax.dynamic_index_in_dim(attend_mine, row ^ step, 0, keepdims=False)
-        pieces.append(swap(piece, "row", rows, step) if step else piece)
-    attend_sum = in_order(jnp.stack(pieces), row).reshape(rows, shard, 3, features)
+        tok0, tok1, mod, dq_near, dk, dv, attend_turned, 0, (raw, mod_early)
+    )
+
+    attend_raw = lax.all_to_all(
+        attend_raw.reshape(devices, shard, 3 * features), both, 0, 0, tiled=True
+    )
+    attend_sum = jnp.sum(attend_raw.reshape(clips, rows, shard, 3, features).astype(f32), axis=0)
     attend_sum = attend_sum.transpose(1, 2, 0, 3).reshape(shard, 3 * width)
 
     far = (

time: 661 us -> 605 us (0.915)
  starting transfers between devices: 123 us -> 67.7 us
  blocking collectives: 0 us -> 21.2 us
  waiting for transfers between devices: 152 us -> 139 us
  local copies, waits for them, and re-layouts: 44.8 us -> 36.1 us
    ppermute x55 -> x12, waiting for transfers between devices: 137 us -> 42.6 us  [swap(): lax.ppermute(value, axis, [(place, place ^ step) for place in range(size)])]
    ppermute x55 -> x12, starting transfers between devices: 96.7 us -> 8.22 us  [swap(): lax.ppermute(value, axis, [(place, place ^ step) for place in range(size)])]
    all_to_all x0 -> x5, waiting for transfers between devices: none -> 42.5 us  [the longest x1 33 us: local(): lax.all_to_all(attend_raw.reshape(devices, shard, 3 * features), both, 0,...]
    all_to_all x0 -> x5, starting transfers between devices: none -> 25.1 us  [the longest x1 8.48 us: local(): lax.all_to_all(attend_raw.reshape(devices, shard, 3 * features), both, 0,...]
    all_to_all x0 -> x1, blocking collectives: none -> 21.2 us  [local(): project_raw = lax.all_to_all(project_raw, 'clip', 0, 0, tiled=True)]
    all_to_all x1, waiting for transfers between devices: 0.01 us -> 17.7 us  [local(): mod_grad = lax.all_to_all(mod_grad, both, 0, 0, tiled=True)]
    all_to_all x1, starting transfers between devices: 2.87 us -> 16.4 us  [local(): lax.all_to_all(jnp.broadcast_to(squares, (devices, 8, 128)), both, 0, 0,...]
    unnamed x108 -> x64, local copies, waits for them, and re-layouts: 16.7 us -> 3.32 us
  transfers between devices with their start and end apart: 61 -> 23, of which waited for: 21 -> 10; matrix products, arithmetic and copies ran while one was open for 10% -> 8% of each run, Pallas kernels for 33% -> 36%
where the time goes in v2:
time: 605 us; the launch traced here: 598 us
  Pallas kernels  280 us (46%)
  waiting for transfers between devices  139 us (23%)
  starting transfers between devices  67.7 us (11%)
  local copies, waits for them, and re-layouts  36.1 us (6%)
  other arithmetic  30.8 us (5%)
  between operations  21.6 us (4%)
  blocking collectives  21.2 us (4%)
    pallas_call x2, Pallas kernels, attend_back(): pl.pallas_call(functools.partial(attend_back_kernel, heads, last), grid=(...  99 us
    pallas_call x1, Pallas kernels, feed_forward(): pl.pallas_call(feed_kernel, grid=(units // block,), in_specs=[whole(pltpu...  65.8 us
    pallas_call x2, Pallas kernels, attend(): pl.pallas_call(functools.partial(attend_kernel, heads), grid=(count // bl...  55.5 us
    ppermute x12, waiting for transfers between devices, swap(): lax.ppermute(value, axis, [(place, place ^ step) for place in range(size)])  42.6 us
    all_to_all x1, waiting for transfers between devices, local(): lax.all_to_all(attend_raw.reshape(devices, shard, 3 * features), both, 0,...  33 us
    pallas_call x2, Pallas kernels, first_back(): pl.pallas_call(functools.partial(first_back_kernel, half, last), grid=(2...  26.9 us
    all_to_all x1, blocking collectives, local(): project_raw = lax.all_to_all(project_raw, 'clip', 0, 0, tiled=True)  21.2 us
    pallas_call x2, Pallas kernels, project_qkv(): pl.pallas_call(functools.partial(qkv_kernel, half), grid=(2 * half,), in_...  18.1 us
  transfers between devices with their start and end apart: 23, of which 10 were waited for; matrix products, arithmetic and copies ran while one was open for 8% of the time, Pallas kernels for 36%

profile of v2, /device:TPU:0, one launch (start us, length us, event | category | flops | bytes accessed | tf_op | source)
XLA Modules:
  0.0 598.4 jit_solution(14867968975450202984)
XLA Ops:
  11.1 7.3 %all-to-all-start = ((bf16[8,12,1024]{2,1,0:T(8,128)(2,1)}), bf16[8,12,1024]{2,1,0:T(8,128)(2,1)S(1)}, u32[]{:S(2)}, u32[]{:S(2)}) async-start(bf16[8,12,1024]{2,1,0:T(8,128)(2,1)} %broadcast_in_dim.49), calls=%async_computation | async-start | bytes 524288 | tf_op jit(solution)/shard_map/all_to_all | solution.py:629
  19.6 8.9 %all-to-all-done = bf16[8,12,1024]{2,1,0:T(8,128)(2,1)S(1)} async-done(((bf16[8,12,1024]{2,1,0:T(8,128)(2,1)}), bf16[8,12,1024]{2,1,0:T(8,128)(2,1)S(1)}, u32[]{:S(2)}, u32[]{:S(2)}) %all-to-all-start) | async-done | bytes 196640 | tf_op jit(solution)/shard_map/all_to_all | solution.py:629
  30.4 4.5 all-to-all-start.1
  38.5 17.6 %all-to-all-done.1 = f32[32,12,192]{2,1,0:T(8,128)S(1)} async-done(((f32[32,12,192]{2,1,0:T(8,128)}), f32[32,12,192]{2,1,0:T(8,128)S(1)}, u32[]{:S(2)}, u32[]{:S(2)}) %all-to-all-start.1) | async-done | bytes 294944 | tf_op jit(solution)/shard_map/all_to_all | solution.py:663
  57.5 4.6 all-to-all-start.2
  62.4 42.0 %collective-permute-done.one = bf16[784,1024]{1,0:T(8,128)(2,1)} collective-permute-done((bf16[784,1024]{1,0:T(8,128)(2,1)}, bf16[784,1024]{1,0:T(8,128)(2,1)}, u32[]{:S(2)}, u32[]{:S(2)}) %collective-permute-start) | collective-permute-done | bytes 1605664 | tf_op jit(solution)/shard_map/ppermute | solution.py:565
  107.1 4.1 all-to-all-done.2
  115.9 9.1 %shard_map.488.k1.v1.q_ref = bf16[768,1536]{1,0:T(8,128)(2,1)} custom-call(bf16[784,1024]{1,0:T(8,128)(2,1)} %fusion.2.one, bf16[784,1024]{1,0:T(8,128)(2,1)} %collective-permute-done.2.two, f32[12,6,1024]{2,1,0:T(8,128)} %reshape.169.mod, bf16[768,1024]{1,0:T(8,128)(2,1)} %bitcast.74, f32[32,3072]{1,0:T(8,128)} %get-tuple-element.143.cosine.cos_all, ...), custom_call_target="tpu_custom_call" | custom-call | flops 2415919104 | bytes 6291456 | tf_op jit(solution)/shard_map/pallas_call | solution.py:118
  125.8 4.0 all-to-all-start.3
  129.8 9.0 %shard_map.487.q_ref.k2.v2 = bf16[768,1536]{1,0:T(8,128)(2,1)} custom-call(bf16[784,1024]{1,0:T(8,128)(2,1)} %collective-permute-done.one, bf16[784,1024]{1,0:T(8,128)(2,1)} %collective-permute-done.1.two, f32[12,6,1024]{2,1,0:T(8,128)} %reshape.169.mod, bf16[768,1024]{1,0:T(8,128)(2,1)} %bitcast.75, f32[32,3072]{1,0:T(8,128)} %get-tuple-element.143.cosine.cos_all, ...), custom_call_target="tpu_custom_call" | custom-call | flops 2415919104 | bytes 6291456 | tf_op jit(solution)/shard_map/pallas_call | solution.py:118
  139.4 27.7 %shard_map.489 = (bf16[256,1536]{1,0:T(8,128)(2,1)}, f32[4,1536]{1,0:T(4,128)}) custom-call(bf16[768,1536]{1,0:T(8,128)(2,1)} %shard_map.487.q_ref.k2.v2, bf16[768,1536]{1,0:T(8,128)(2,1)} %shard_map.488.k1.v1.q_ref, bf16[768,1536]{1,0:T(8,128)(2,1)} %shard_map.487.q_ref.k2.v2, bf16[768,1536]{1,0:T(8,128)(2,1)} %shard_map.488.k1.v1.q_ref, ...), custom_call_target="tpu_custom_call" | custom-call | flops 19327352832 | bytes 3145728 | tf_op jit(solution)/shard_map/pallas_call | solution.py:172
  171.4 3.6 all-to-all-start.4
  175.2 27.7 %shard_map.490 = (bf16[256,1536]{1,0:T(8,128)(2,1)}, f32[4,1536]{1,0:T(4,128)}) custom-call(bf16[768,1536]{1,0:T(8,128)(2,1)} %shard_map.488.k1.v1.q_ref, bf16[768,1536]{1,0:T(8,128)(2,1)} %shard_map.488.k1.v1.q_ref, bf16[768,1536]{1,0:T(8,128)(2,1)} %shard_map.487.q_ref.k2.v2, bf16[768,1536]{1,0:T(8,128)(2,1)} %shard_map.488.k1.v1.q_ref, ...), custom_call_target="tpu_custom_call" | custom-call | flops 19327352832 | bytes 3145728 | tf_op jit(solution)/shard_map/pallas_call | solution.py:172
  205.0 5.4 all-to-all-done.4
  211.9 3.9 copy.100
  215.9 7.5 %shard_map.491 = (f32[12,64,1024]{2,1,0:T(8,128)}, bf16[768,1024]{1,0:T(8,128)(2,1)}, bf16[768,1024]{1,0:T(8,128)(2,1)}) custom-call(s32[4]{0:T(128)} %iota_xor_fusion.order, bf16[256,1536]{1,0:T(8,128)(2,1)} %get-tuple-element.73.a0.out_ref, bf16[256,768]{1,0:T(8,128)(2,1)} %collective-permute-done.3.a1, bf16[256,768]{1,0:T(8,128)(2,1)} %collective-permute-done.4.a2, ...), custom_call_target="tpu_custom_call" | custom-call | flops 1610612736 | bytes 11010048 | tf_op jit(solution)/shard_map/pallas_call | solution.py:359
  223.4 65.8 %shard_map.492 = (bf16[32,2,32,4096]{3,2,1,0:T(8,128)(2,1)}, bf16[12,64,1024]{2,1,0:T(8,128)(2,1)}, f32[12,64,1024]{2,1,0:T(8,128)}, f32[12,4,1024]{2,1,0:T(4,12...) custom-call(s32[4]{0:T(128)} %iota_xor_fusion.order, ...), custom_call_target="tpu_custom_call" | custom-call | flops 38654705664 | bytes 33554432 | tf_op jit(solution)/shard_map/pallas_call | solution.py:451
  296.5 4.4 all-to-all-start.7
  301.0 48.3 %shard_map.493 = (bf16[256,1536]{1,0:T(8,128)(2,1)}, f32[256,3072]{1,0:T(8,128)}, f32[256,3072]{1,0:T(8,128)}) custom-call(bf16[768,1536]{1,0:T(8,128)(2,1)} %shard_map.488.k1.v1.q_ref, bf16[768,1536]{1,0:T(8,128)(2,1)} %shard_map.488.k1.v1.q_ref, bf16[768,1536]{1,0:T(8,128)(2,1)} %shard_map.487.q_ref.k2.v2, bf16[768,1536]{1,0:T(8,128)(2,1)} %shard_map.488.k1.v1.q_ref, ...), custom_call_target="tpu_custom_call" | custom-call | flops 41070624768 | bytes 6291456 | tf_op jit(solution)/shard_map/pallas_call | solution.py:318
  349.4 50.6 %shard_map.494 = (bf16[256,1536]{1,0:T(8,128)(2,1)}, bf16[256,3072]{1,0:T(8,128)(2,1)}, bf16[256,3072]{1,0:T(8,128)(2,1)}) custom-call(bf16[768,1536]{1,0:T(8,128)(2,1)} %shard_map.487.q_ref.k2.v2, bf16[768,1536]{1,0:T(8,128)(2,1)} %shard_map.488.k1.v1.q_ref, bf16[768,1536]{1,0:T(8,128)(2,1)} %shard_map.487.q_ref.k2.v2, ...), custom_call_target="tpu_custom_call" | custom-call | flops 41070624768 | bytes 6291456 | tf_op jit(solution)/shard_map/pallas_call | solution.py:318
  400.0 12.6 %shard_map.495 = (bf16[2,768,1024]{2,1,0:T(8,128)(2,1)}, f32[768,1024]{1,0:T(8,128)}, f32[12,2,1024]{2,1,0:T(2,128)}) custom-call(bf16[784,1024]{1,0:T(8,128)(2,1)} %collective-permute-done.one, bf16[784,1024]{1,0:T(8,128)(2,1)} %collective-permute-done.1.two, f32[12,6,1024]{2,1,0:T(8,128)} %reshape.169.mod, bf16[256,1536]{1,0:T(8,128)(2,1)} %get-tuple-element.92.dq, ...), custom_call_target="tpu_custom_call" | custom-call | flops 4831838208 | bytes 9437184 | tf_op jit(solution)/shard_map/pallas_call | solution.py:529
  412.6 14.3 %shard_map.496 = (bf16[2,768,1024]{2,1,0:T(8,128)(2,1)}, bf16[1024,768]{1,0:T(8,128)(2,1)}, f32[12,2,1024]{2,1,0:T(2,128)}) custom-call(bf16[784,1024]{1,0:T(8,128)(2,1)} %fusion.2.one, bf16[784,1024]{1,0:T(8,128)(2,1)} %collective-permute-done.2.two, f32[12,6,1024]{2,1,0:T(8,128)} %reshape.169.mod, bf16[256,1536]{1,0:T(8,128)(2,1)} %get-tuple-element.97.dq, ...), custom_call_target="tpu_custom_call" | custom-call | flops 4831838208 | bytes 9437184 | tf_op jit(solution)/shard_map/pallas_call | solution.py:529
  429.1 5.9 all-to-all-start.5
  437.1 17.7 %all-to-all-done.5 = f32[32,12,192]{2,1,0:T(8,128)S(1)} async-done(((f32[32,12,192]{2,1,0:T(8,128)}), f32[32,12,192]{2,1,0:T(8,128)S(1)}, u32[]{:S(2)}, u32[]{:S(2)}) %all-to-all-start.5) | async-done | bytes 294944 | tf_op jit(solution)/shard_map/all_to_all | solution.py:749
  454.9 21.2 %all_to_all.50 = bf16[8,32,1024]{2,1,0:T(8,128)(2,1)S(1)} all-to-all(bf16[8,32,1024]{2,1,0:T(8,128)(2,1)S(1)} %reduce_sum.117), channel_id=1, replica_groups=mesh['clip'=8,'row'=4] {'clip'}, dimensions={0} | all-to-all | bytes 1048576 | tf_op jit(solution)/shard_map/all_to_all | solution.py:711
  476.1 8.5 %all-to-all-start.6 = ((bf16[32,32,768]{2,1,0:T(8,128)(2,1)}), bf16[32,32,768]{2,1,0:T(8,128)(2,1)S(1)}, u32[]{:S(2)}, u32[]{:S(2)}) async-start(bf16[32,32,768]{2,1,0:T(8,128)(2,1)} %bitcast.78), calls=%async_computation.6 | async-start | bytes 3145728 | tf_op jit(solution)/shard_map/all_to_all | solution.py:731
  497.6 33.0 %all-to-all-done.6 = bf16[32,32,768]{2,1,0:T(8,128)(2,1)S(1)} async-done(((bf16[32,32,768]{2,1,0:T(8,128)(2,1)}), bf16[32,32,768]{2,1,0:T(8,128)(2,1)S(1)}, u32[]{:S(2)}, u32[]{:S(2)}) %all-to-all-start.6) | async-done | bytes 1572896 | tf_op jit(solution)/shard_map/all_to_all | solution.py:731
  530.6 3.2 reshape.184
  533.9 3.1 reduce_sum.115
  539.2 9.2 %reduce-scatter.2.cloned.1.call-done = bf16[64,4096]{1,0:T(8,128)(2,1)} async-done(((bf16[2048,4096]{1,0:T(8,128)(2,1)}), bf16[64,4096]{1,0:T(8,128)(2,1)}) %reduce-scatter.2.cloned.1.call-update) | async-done | bytes 524304 | tf_op jit(solution)/shard_map/reduce_scatter | solution.py:703
  552.2 16.4 %all-to-all-start.9 = ((f32[32,8,128]{2,1,0:T(8,128)}), f32[32,8,128]{2,1,0:T(8,128)S(1)}, u32[]{:S(2)}, u32[]{:S(2)}) async-start(f32[32,8,128]{2,1,0:T(8,128)} %broadcast_in_dim.58), calls=%async_computation.10 | async-start | bytes 262144 | tf_op jit(solution)/shard_map/all_to_all | solution.py:763
  568.7 7.2 %shard_map.497 = f32[12,64,1024]{2,1,0:T(8,128)} custom-call(bf16[12,64,1024]{2,1,0:T(8,128)(2,1)} %bitcast.64, f32[12,6,1024]{2,1,0:T(8,128)} %reshape.169.mod, f32[12,64,1024]{2,1,0:T(8,128)} %get-tuple-element.80.middle_grad, bf16[768,1024]{1,0:T(8,128)(2,1)} %get-tuple-element.139.one, bf16[768,1024]{1,0:T(8,128)(2,1)} %collective-permute-done.9.two, ...), custom_call_target="tpu_custom_call" | custom-call | flops 15728640 | bytes 12582912 | tf_op jit(solution)/shard_map/pallas_call | solution.py:553
  (169 shorter events, 68.1 us)
Async XLA Ops:
  7.2 216.2 %all-gather.2.cloned.1.call-start = ((), (), s32[]{:S(2)}) async-start(), calls=%async_computation.11 | async-start | bytes 17301504 | tf_op jit(solution)/shard_map/all_gather | solution.py:622
  8.3 10.9 %copy-start.24 = (s32[1,12,4,16]{3,2,1,0:T(4,128)S(1)}, s32[1,12,4,16]{3,2,1,0:T(4,128)}, u32[]{:S(2)}) copy-start(s32[1,12,4,16]{3,2,1,0:T(4,128)} %param.28) | copy-start | bytes 9220
  8.4 11.0 %copy-start.22 = (s32[2,1,12,4,16]{4,3,2,1,0:T(4,128)S(1)}, s32[2,1,12,4,16]{4,3,2,1,0:T(4,128)}, u32[]{:S(2)}) copy-start(s32[2,1,12,4,16]{4,3,2,1,0:T(4,128)} %param.27) | copy-start | bytes 18436
  8.4 11.2 %copy-start.25 = (f32[192]{0:T(256)S(1)}, f32[192]{0:T(256)}, u32[]{:S(2)}) copy-start(f32[192]{0:T(256)} %param.31) | copy-start | bytes 2308
  9.5 19.7 %copy-start.3 = (f32[1024,192]{0,1:T(8,128)S(1)}, f32[1024,192]{0,1:T(8,128)}, u32[]{:S(2)}) copy-start(f32[1024,192]{0,1:T(8,128)} %param.30) | copy-start | bytes 2359300
  11.1 17.3 %all-to-all-start = ((bf16[8,12,1024]{2,1,0:T(8,128)(2,1)}), bf16[8,12,1024]{2,1,0:T(8,128)(2,1)S(1)}, u32[]{:S(2)}, u32[]{:S(2)}) async-start(bf16[8,12,1024]{2,1,0:T(8,128)(2,1)} %broadcast_in_dim.49), calls=%async_computation | async-start | bytes 524288 | tf_op jit(solution)/shard_map/all_to_all | solution.py:629
  29.2 5.7 copy-start
  30.4 25.8 %all-to-all-start.1 = ((f32[32,12,192]{2,1,0:T(8,128)}), f32[32,12,192]{2,1,0:T(8,128)S(1)}, u32[]{:S(2)}, u32[]{:S(2)}) async-start(f32[32,12,192]{2,1,0:T(8,128)} %bitcast.5), calls=%async_computation.1 | async-start | bytes 1048576 | tf_op jit(solution)/shard_map/all_to_all | solution.py:663
  36.3 68.1 %collective-permute-start = (bf16[784,1024]{1,0:T(8,128)(2,1)}, bf16[784,1024]{1,0:T(8,128)(2,1)}, u32[]{:S(2)}, u32[]{:S(2)}) collective-permute-start(bf16[784,1024]{1,0:T(8,128)(2,1)} %fusion.2.one), channel_id=1, source_target_pairs={{0,2},{1,3},{2,0},{3,1},{4,6},{5,7},{6,4},{7,5},{8,10},{9,11},{10,... | collective-permute-start | bytes 4816904 | tf_op jit(solution)/shard_map/ppermute | solution.py:565
  57.5 46.9 %copy-start.16 = (f32[1024,32]{0,1:T(8,128)S(1)}, f32[1024,32]{0,1:T(8,128)}, u32[]{:S(2)}) copy-start(f32[1024,32]{0,1:T(8,128)} %param.33) | copy-start | bytes 393220
  57.5 53.7 %all-to-all-start.2 = ((bf16[32,32,768]{2,1,0:T(8,128)(2,1)}), bf16[32,32,768]{2,1,0:T(8,128)(2,1)S(1)}, u32[]{:S(2)}, u32[]{:S(2)}) async-start(bf16[32,32,768]{2,1,0:T(8,128)(2,1)} %bitcast.8), calls=%async_computation.2 | async-start | bytes 3145728 | tf_op jit(solution)/shard_map/all_to_all | solution.py:651
  62.0 44.3 %collective-permute-start.2 = (bf16[784,1024]{1,0:T(8,128)(2,1)}, bf16[784,1024]{1,0:T(8,128)(2,1)}, u32[]{:S(2)}, u32[]{:S(2)}) collective-permute-start(bf16[784,1024]{1,0:T(8,128)(2,1)} %fusion.2.one), channel_id=1, source_target_pairs={{0,1},{1,0},{2,3},{3,2},{4,5},{5,4},{6,7},{7,6},{8,9},{9,8},{10,11... | collective-permute-start | bytes 4816904 | tf_op jit(solution)/shard_map/ppermute | solution.py:565
  104.4 8.5 %collective-permute-start.1 = (bf16[784,1024]{1,0:T(8,128)(2,1)}, bf16[784,1024]{1,0:T(8,128)(2,1)}, u32[]{:S(2)}, u32[]{:S(2)}) collective-permute-start(bf16[784,1024]{1,0:T(8,128)(2,1)} %collective-permute-done.one), channel_id=1, source_target_pairs={{0,1},{1,0},{2,3},{3,2},{4,5},{5,4},{6,7},{7,6},{8,9},{9,8},{10,11... | collective-permute-start | bytes 4816904 | tf_op jit(solution)/shard_map/ppermute | solution.py:565
  125.8 44.0 %all-to-all-start.3 = ((bf16[8,32,1024]{2,1,0:T(8,128)(2,1)}), bf16[8,32,1024]{2,1,0:T(8,128)(2,1)S(1)}, u32[]{:S(2)}, u32[]{:S(2)}) async-start(bf16[8,32,1024]{2,1,0:T(8,128)(2,1)} %broadcast_in_dim.56), calls=%async_computation.3 | async-start | bytes 1048576 | tf_op jit(solution)/shard_map/all_to_all | solution.py:683
  168.3 47.6 %collective-permute-start.5 = (bf16[256,768]{1,0:T(8,128)(2,1)S(1)}, bf16[256,768]{1,0:T(8,128)(2,1)}, u32[]{:S(2)}, u32[]{:S(2)}) collective-permute-start(bf16[256,768]{1,0:T(8,128)(2,1)S(1)} %get-tuple-element.140), channel_id=1, source_target_pairs={{0,3},{1,2},{2,1},{3,0},{4,7},{5,6},{6,5},{7,4},{8,11},{9,10},{10,... | collective-permute-start | bytes 1179656 | tf_op jit(solution)/shard_map/ppermute | solution.py:565
  169.0 46.9 %collective-permute-start.4 = (bf16[256,768]{1,0:T(8,128)(2,1)S(1)}, bf16[256,768]{1,0:T(8,128)(2,1)}, u32[]{:S(2)}, u32[]{:S(2)}) collective-permute-start(bf16[256,768]{1,0:T(8,128)(2,1)S(1)} %get-tuple-element.141), channel_id=1, source_target_pairs={{0,2},{1,3},{2,0},{3,1},{4,6},{5,7},{6,4},{7,5},{8,10},{9,11},{10,... | collective-permute-start | bytes 1179656 | tf_op jit(solution)/shard_map/ppermute | solution.py:565
  171.4 39.1 %all-to-all-start.4 = ((bf16[4,8,32,1024]{3,2,1,0:T(8,128)(2,1)}), bf16[4,8,32,1024]{3,2,1,0:T(8,128)(2,1)S(1)}, u32[]{:S(2)}, u32[]{:S(2)}) async-start(bf16[4,8,32,1024]{3,2,1,0:T(8,128)(2,1)} %broadcast_in_dim.57), calls=%async_computation.4 | async-start | bytes 4194304 | tf_op jit(solution)/shard_map/all_to_all | solution.py:686
  175.0 373.4 %reduce-scatter.2.cloned.1.call-start = ((), (), s32[]{:S(2)}) async-start(), calls=%async_computation.12 | async-start | bytes 17301504 | tf_op jit(solution)/shard_map/reduce_scatter | solution.py:703
  204.0 11.9 %collective-permute-start.3 = (bf16[256,768]{1,0:T(8,128)(2,1)S(1)}, bf16[256,768]{1,0:T(8,128)(2,1)}, u32[]{:S(2)}, u32[]{:S(2)}) collective-permute-start(bf16[256,768]{1,0:T(8,128)(2,1)S(1)} %slice.72), channel_id=1, source_target_pairs={{0,1},{1,0},{2,3},{3,2},{4,5},{5,4},{6,7},{7,6},{8,9},{9,8},{10,11... | collective-permute-start | bytes 1179656 | tf_op jit(solution)/shard_map/ppermute | solution.py:565
  290.3 10.7 %collective-permute-start.6 = (bf16[256,768]{1,0:T(8,128)(2,1)S(1)}, bf16[256,768]{1,0:T(8,128)(2,1)}, u32[]{:S(2)}, u32[]{:S(2)}) collective-permute-start(bf16[256,768]{1,0:T(8,128)(2,1)S(1)} %copy-done.31), channel_id=1, source_target_pairs={{0,1},{1,0},{2,3},{3,2},{4,5},{5,4},{6,7},{7,6},{8,9},{9,8},{10,11... | collective-permute-start | bytes 1179656 | tf_op jit(solution)/shard_map/ppermute | solution.py:565
  290.4 59.0 %collective-permute-start.7 = (bf16[256,768]{1,0:T(8,128)(2,1)S(1)}, bf16[256,768]{1,0:T(8,128)(2,1)}, u32[]{:S(2)}, u32[]{:S(2)}) collective-permute-start(bf16[256,768]{1,0:T(8,128)(2,1)S(1)} %copy-done.30), channel_id=1, source_target_pairs={{0,2},{1,3},{2,0},{3,1},{4,6},{5,7},{6,4},{7,5},{8,10},{9,11},{10,... | collective-permute-start | bytes 1179656 | tf_op jit(solution)/shard_map/ppermute | solution.py:565
  291.8 57.5 %collective-permute-start.8 = (bf16[256,768]{1,0:T(8,128)(2,1)S(1)}, bf16[256,768]{1,0:T(8,128)(2,1)}, u32[]{:S(2)}, u32[]{:S(2)}) collective-permute-start(bf16[256,768]{1,0:T(8,128)(2,1)S(1)} %copy-done.29), channel_id=1, source_target_pairs={{0,3},{1,2},{2,1},{3,0},{4,7},{5,6},{6,5},{7,4},{8,11},{9,10},{10,... | collective-permute-start | bytes 1179656 | tf_op jit(solution)/shard_map/ppermute | solution.py:565
  296.5 132.6 %all-to-all-start.7 = ((bf16[4,8,32,1024]{3,2,1,0:T(8,128)(2,1)}), bf16[4,8,32,1024]{3,2,1,0:T(8,128)(2,1)}, u32[]{:S(2)}, u32[]{:S(2)}) async-start(bf16[4,8,32,1024]{3,2,1,0:T(8,128)(2,1)} %copy.105), calls=%async_computation.7 | async-start | bytes 4194304 | tf_op jit(solution)/shard_map/all_to_all | solution.py:709
  412.6 14.3 %copy-start.20 = (f32[12,4,1024]{2,1,0:T(4,128)S(1)}, f32[12,4,1024]{2,1,0:T(4,128)}, u32[]{:S(2)}) copy-start(f32[12,4,1024]{2,1,0:T(4,128)} %get-tuple-element.103) | copy-start | bytes 589828
  429.1 25.8 %all-to-all-start.5 = ((f32[32,12,192]{2,1,0:T(8,128)}), f32[32,12,192]{2,1,0:T(8,128)S(1)}, u32[]{:S(2)}, u32[]{:S(2)}) async-start(f32[32,12,192]{2,1,0:T(8,128)} %bitcast.58), calls=%async_computation.5 | async-start | bytes 1048576 | tf_op jit(solution)/shard_map/all_to_all | solution.py:749
  476.1 54.5 %all-to-all-start.6 = ((bf16[32,32,768]{2,1,0:T(8,128)(2,1)}), bf16[32,32,768]{2,1,0:T(8,128)(2,1)S(1)}, u32[]{:S(2)}, u32[]{:S(2)}) async-start(bf16[32,32,768]{2,1,0:T(8,128)(2,1)} %bitcast.78), calls=%async_computation.6 | async-start | bytes 3145728 | tf_op jit(solution)/shard_map/all_to_all | solution.py:731
  486.3 3.6 collective-permute-start.10
  489.1 5.3 copy-start.6
  489.1 79.6 %collective-permute-start.9 = (bf16[768,1024]{1,0:T(8,128)(2,1)}, bf16[768,1024]{1,0:T(8,128)(2,1)}, u32[]{:S(2)}, u32[]{:S(2)}) collective-permute-start(bf16[768,1024]{1,0:T(8,128)(2,1)} %get-tuple-element.138), channel_id=1, source_target_pairs={{0,1},{1,0},{2,3},{3,2},{4,5},{5,4},{6,7},{7,6},{8,9},{9,8},{10,11... | collective-permute-start | bytes 4718600 | tf_op jit(solution)/shard_map/ppermute | solution.py:565
  491.9 76.8 %collective-permute-start.11 = (bf16[768,1024]{1,0:T(8,128)(2,1)}, bf16[768,1024]{1,0:T(8,128)(2,1)}, u32[]{:S(2)}, u32[]{:S(2)}) collective-permute-start(bf16[768,1024]{1,0:T(8,128)(2,1)} %fusion.1), channel_id=1, source_target_pairs={{0,2},{1,3},{2,0},{3,1},{4,6},{5,7},{6,4},{7,5},{8,10},{9,11},{10,... | collective-permute-start | bytes 4718600 | tf_op jit(solution)/shard_map/ppermute | solution.py:565
  552.2 24.7 %all-to-all-start.9 = ((f32[32,8,128]{2,1,0:T(8,128)}), f32[32,8,128]{2,1,0:T(8,128)S(1)}, u32[]{:S(2)}, u32[]{:S(2)}) async-start(f32[32,8,128]{2,1,0:T(8,128)} %broadcast_in_dim.58), calls=%async_computation.10 | async-start | bytes 262144 | tf_op jit(solution)/shard_map/all_to_all | solution.py:763
  578.9 6.8 %copy-start.11 = (f32[32,3072]{1,0:T(8,128)}, f32[32,3072]{1,0:T(8,128)S(1)}, u32[]{:S(2)}) copy-start(f32[32,3072]{1,0:T(8,128)S(1)} %mul.354) | copy-start | bytes 1179652
  (23 other events, 54.6 us)
Sparse Core Ops, SparseCore 0:
  11.5 158.9 all-gather.1
  289.4 258.8 reduce-scatter.1

commit v3 on v2

--- a/solution.py
+++ b/solution.py
@@ -27,6 +27,7 @@
 NN = (((1,), (0,)), ((), ()))
 NT = (((1,), (1,)), ((), ()))
 TN = (((0,), (0,)), ((), ()))
+TT = (((0,), (1,)), ((), ()))
 MIB = 2**20
 VMEM = pltpu.VMEM
 
@@ -335,8 +336,8 @@
     features = a0.shape[0]
     mixed = None
     for slot, part in enumerate((a0, a1, a2, a3)):
-        rows = proj[pl.ds(pl.multiple_of(order[slot] * features, features), features), :]
-        term = dot(part[...], rows, TN)
+        columns = proj[:, pl.ds(pl.multiple_of(order[slot] * features, features), features)]
+        term = dot(part[...], columns, TT)
         mixed = term if mixed is None else mixed + term
     shape = tokens.shape
     mixed = mixed.reshape(shape)
@@ -437,7 +438,7 @@
         grad = att_grad[...]
         for slot, (part, out) in enumerate(((a0, d0), (a1, d1), (a2, d2), (a3, d3))):
             place = pl.ds(pl.multiple_of(order[slot] * features, features), features)
-            out[...] = dot(proj[place, :], grad, NT).astype(bf16)
+            out[...] = dot(proj[:, place], grad, TT).astype(bf16)
             proj_raw[place, :] = dot(part[...], grad).astype(bf16)
 
 
@@ -563,6 +564,25 @@
 
 def swap(value, axis, size, step):
     return lax.ppermute(value, axis, [(place, place ^ step) for place in range(size)])
+
+
+def relative(value, place):
+    count = value.shape[0]
+    tail = value.shape[1:]
+    step = 1
+    while step < count:
+        pairs = value.reshape((count // (2 * step), 2, step) + tail)
+        turned = jnp.concatenate([pairs[:, 1:], pairs[:, :1]], axis=1)
+        value = jnp.where((place & step) != 0, turned, pairs).reshape((count,) + tail)
+        step *= 2
+    return value
+
+
+def trade(blocks, axis, size):
+    pieces = [blocks[0]]
+    for step in range(1, size):
+        pieces.append(swap(blocks[step], axis, size, step))
+    return jnp.stack(pieces)
 
 
 def adam_update(master, first, second, gradient, rate, decay):
@@ -610,7 +630,7 @@
     count = frames * per_frame
     devices = clips * rows
     features = width // rows
-    row = lax.axis_index("row")
+    clip, row = lax.axis_index("clip"), lax.axis_index("row")
     both = ("clip", "row")
     order = (row ^ jnp.arange(rows)).astype(jnp.int32)
 
@@ -624,11 +644,6 @@
     fused = shard % 16 == 0
     if not fused:
         feed_full = feed_full.transpose(1, 0, 2, 3).reshape(1, 2, width, units)
-
-    cond_act = jax.nn.silu(condition[0].astype(f32)).astype(bf16)
-    cond_all = lax.all_to_all(
-        jnp.broadcast_to(cond_act[None], (clips, frames, width)), "clip", 0, 0, tiled=True
-    ).reshape(clips * frames, width)
 
     own = tokens.reshape(frames, per_frame, width)
     upstream = cotangent.reshape(frames, per_frame, width)
@@ -653,14 +668,18 @@
     )
     attend_turned = attend_full.reshape(width, 3 * features).T
 
+    cond_act = jax.nn.silu(condition[0].astype(f32)).astype(bf16)
+    cond_act, tok0 = lax.optimization_barrier((cond_act, tok0))
+    cond_all = trade([cond_act] * clips, "clip", clips).reshape(clips * frames, width)
     mod_mine = dot(cond_all, adaptive_weight.astype(bf16)) + adaptive_offsets.astype(bf16).astype(
         f32
     )
     part = mod_mine.shape[1]
-    mod_mine = jnp.broadcast_to(
-        mod_mine.reshape(clips, 1, frames, part), (clips, rows, frames, part)
-    )
-    mod = lax.all_to_all(mod_mine.reshape(devices, frames, part), both, 0, 0, tiled=True)
+    mod = trade(mod_mine.reshape(clips, frames, part), "clip", clips)[None]
+    for step in (1, 2):
+        mod = jnp.concatenate([mod, swap(mod, "row", rows, step)], axis=0)
+    mod = relative(mod, row).reshape(rows, clips, frames * part).swapaxes(0, 1)
+    mod = relative(mod, clip).reshape(devices, frames, part)
     mod = mod.transpose(1, 0, 2).reshape(frames, 6, width)
 
     small = jnp.concatenate(
@@ -686,7 +705,7 @@
     project_full = lax.all_to_all(
         jnp.broadcast_to(project_full[None], (rows, clips, shard, width)), "row", 0, 0, tiled=True
     )
-    project_full = project_full.transpose(1, 0, 2, 3).reshape(width, width).T
+    project_full = project_full.transpose(1, 0, 2, 3).reshape(width, width)
 
     out_far, lse_far = attend(qkv_far, qkv_near, qkv_far, bias)
     out_far, qkv_near = lax.optimization_barrier((out_far, qkv_near))
@@ -745,9 +764,13 @@
     )
 
     mod_grad = jnp.concatenate([mod_early, mod_late], axis=1)
-    mod_grad = mod_grad.reshape(frames, devices, part).transpose(1, 0, 2)
-    mod_grad = lax.all_to_all(mod_grad, both, 0, 0, tiled=True)
-    mod_grad = jnp.sum(mod_grad.reshape(clips, rows, frames, part), axis=1)
+    mod_grad = mod_grad.reshape(frames, clips, rows, part).transpose(1, 2, 0, 3)
+    mod_grad = relative(mod_grad.reshape(clips, rows * frames, part), clip)
+    mod_grad = mod_grad.reshape(clips, rows, frames * part).swapaxes(0, 1)
+    mod_grad = relative(mod_grad, row)
+    mod_grad = mod_grad[:2] + swap(mod_grad[2:], "row", rows, 2)
+    mod_grad = mod_grad[0] + swap(mod_grad[1], "row", rows, 1)
+    mod_grad = trade(mod_grad.reshape(clips, frames, part), "clip", clips)
     mod_grad = mod_grad.reshape(clips * frames, part)
     adaptive_sum = lax.dot_general(
         mod_grad,
@@ -760,6 +783,7 @@
 
     reduced = [adaptive_sum, offsets_sum, attend_sum, project_sum, widen_sum, narrow_sum]
     squares = sum((jnp.sum(item * item) for item in reduced))
+    squares, input_gradient = lax.optimization_barrier((squares, input_gradient))
     squares = lax.all_to_all(
         jnp.broadcast_to(squares, (devices, 8, 128)), both, 0, 0, tiled=True
     )

time: 605 us -> 665 us (1.099)
  waiting for transfers between devices: 139 us -> 173 us
  starting transfers between devices: 67.7 us -> 92.1 us
  blocking collectives: 21.2 us -> 12 us
  other arithmetic: 30.8 us -> 37.9 us
    ppermute x12 -> x37, waiting for transfers between devices: 42.6 us -> 155 us  [swap(): lax.ppermute(value, axis, [(place, place ^ step) for place in range(size)])]
    ppermute x12 -> x37, starting transfers between devices: 8.22 us -> 54 us  [swap(): lax.ppermute(value, axis, [(place, place ^ step) for place in range(size)])]
    all_to_all x1, waiting for transfers between devices: 33 us -> 0.01 us  [local(): lax.all_to_all(attend_raw.reshape(devices, shard, 3 * features), both, 0,...]
    all_to_all x4 -> x1, waiting for transfers between devices: 45.1 us -> 12.5 us  [local(): project_raw = lax.all_to_all(project_raw, 'clip', 0, 0, tiled=True)]
    all_to_all x4 -> x1, starting transfers between devices: 34.2 us -> 6.46 us  [local(): project_raw = lax.all_to_all(project_raw, 'clip', 0, 0, tiled=True)]
    all_to_all x1, blocking collectives: 21.2 us -> 12 us  [local(): lax.all_to_all(jnp.broadcast_to(squares, (devices, 8, 128)), both, 0, 0,...]
    reduce_scatter x1, waiting for transfers between devices: 9.24 us -> 0.01 us  [local(): lax.psum_scatter(feed_raw.reshape(devices * 2 * shard, units), both, scat...]
  transfers between devices with their start and end apart: 23 -> 45, of which waited for: 10 -> 11; matrix products, arithmetic and copies ran while one was open for 8% -> 9% of each run, Pallas kernels for 36% -> 33%
where the time goes in v3:
time: 665 us; the launch traced here: 657 us
  Pallas kernels  280 us (42%)
  waiting for transfers between devices  173 us (26%)
  starting transfers between devices  92.1 us (14%)
  local copies, waits for them, and re-layouts  38.4 us (6%)
  other arithmetic  37.9 us (6%)
  between operations  22.2 us (3%)
  blocking collectives  12 us (2%)
    ppermute x37, waiting for transfers between devices, swap(): lax.ppermute(value, axis, [(place, place ^ step) for place in range(size)])  155 us
    pallas_call x2, Pallas kernels, attend_back(): pl.pallas_call(functools.partial(attend_back_kernel, heads, last), grid=(...  98.9 us
    pallas_call x1, Pallas kernels, feed_forward(): pl.pallas_call(feed_kernel, grid=(units // block,), in_specs=[whole(pltpu...  65.9 us
    pallas_call x2, Pallas kernels, attend(): pl.pallas_call(functools.partial(attend_kernel, heads), grid=(count // bl...  55.4 us
    ppermute x37, starting transfers between devices, swap(): lax.ppermute(value, axis, [(place, place ^ step) for place in range(size)])  54 us
    pallas_call x2, Pallas kernels, first_back(): pl.pallas_call(functools.partial(first_back_kernel, half, last), grid=(2...  26.9 us
    pallas_call x2, Pallas kernels, project_qkv(): pl.pallas_call(functools.partial(qkv_kernel, half), grid=(2 * half,), in_...  18.3 us
  transfers between devices with their start and end apart: 45, of which 11 were waited for; matrix products, arithmetic and copies ran while one was open for 9% of the time, Pallas kernels for 33%

profile of v3, /device:TPU:0, one launch (start us, length us, event | category | flops | bytes accessed | tf_op | source)
XLA Modules:
  0.0 657.3 jit_solution(11513094192666647353)
XLA Ops:
  13.0 6.1 collective-permute-start.8
  32.8 3.9 collective-permute-done.4
  38.8 5.0 collective-permute-start.15
  53.1 3.5 collective-permute-done.11
  60.4 5.3 all-to-all-start
  69.9 73.5 %collective-permute-done.17 = f32[2,8,12,192]{3,2,1,0:T(8,128)S(1)} collective-permute-done((f32[2,8,12,192]{3,2,1,0:T(8,128)S(1)}, f32[2,8,12,192]{3,2,1,0:T(8,128)S(1)}, u32[]{:S(2)}, u32[]{:S(2)}) %collective-permute-start.17) | collective-permute-done | bytes 147488 | tf_op jit(solution)/shard_map/ppermute | solution.py:566
  156.4 9.2 %shard_map.488.k1.v1.q_ref = bf16[768,1536]{1,0:T(8,128)(2,1)} custom-call(bf16[784,1024]{1,0:T(8,128)(2,1)} %fusion.2.one, bf16[784,1024]{1,0:T(8,128)(2,1)} %collective-permute-done.18.two, f32[12,6,1024]{2,1,0:T(8,128)} %reshape.525.mod, bf16[768,1024]{1,0:T(8,128)(2,1)} %bitcast.212, f32[32,3072]{1,0:T(8,128)} %get-tuple-element.175.cosine.cos_all, ...), custom_call_target="tpu_custom_call" | custom-call | flops 2415919104 | bytes 6291456 | tf_op jit(solution)/shard_map/pallas_call | solution.py:119
  166.5 7.1 %all-to-all-start.1 = ((bf16[8,32,1024]{2,1,0:T(8,128)(2,1)}), bf16[8,32,1024]{2,1,0:T(8,128)(2,1)S(1)}, u32[]{:S(2)}, u32[]{:S(2)}) async-start(bf16[8,32,1024]{2,1,0:T(8,128)(2,1)} %broadcast_in_dim.41), calls=%async_computation.1 | async-start | bytes 1048576 | tf_op jit(solution)/shard_map/all_to_all | solution.py:702
  173.7 9.0 %shard_map.487.q_ref.k2.v2 = bf16[768,1536]{1,0:T(8,128)(2,1)} custom-call(bf16[784,1024]{1,0:T(8,128)(2,1)} %collective-permute-done.one, bf16[784,1024]{1,0:T(8,128)(2,1)} %collective-permute-done.1.two, f32[12,6,1024]{2,1,0:T(8,128)} %reshape.525.mod, bf16[768,1024]{1,0:T(8,128)(2,1)} %bitcast.213, f32[32,3072]{1,0:T(8,128)} %get-tuple-element.175.cosine.cos_all, ...), custom_call_target="tpu_custom_call" | custom-call | flops 2415919104 | bytes 6291456 | tf_op jit(solution)/shard_map/pallas_call | solution.py:119
  183.3 27.7 %shard_map.489 = (bf16[256,1536]{1,0:T(8,128)(2,1)}, f32[4,1536]{1,0:T(4,128)}) custom-call(bf16[768,1536]{1,0:T(8,128)(2,1)} %shard_map.487.q_ref.k2.v2, bf16[768,1536]{1,0:T(8,128)(2,1)} %shard_map.488.k1.v1.q_ref, bf16[768,1536]{1,0:T(8,128)(2,1)} %shard_map.487.q_ref.k2.v2, bf16[768,1536]{1,0:T(8,128)(2,1)} %shard_map.488.k1.v1.q_ref, ...), custom_call_target="tpu_custom_call" | custom-call | flops 19327352832 | bytes 3145728 | tf_op jit(solution)/shard_map/pallas_call | solution.py:173
  215.7 3.6 all-to-all-start.2
  219.5 27.7 %shard_map.490 = (bf16[256,1536]{1,0:T(8,128)(2,1)}, f32[4,1536]{1,0:T(4,128)}) custom-call(bf16[768,1536]{1,0:T(8,128)(2,1)} %shard_map.488.k1.v1.q_ref, bf16[768,1536]{1,0:T(8,128)(2,1)} %shard_map.488.k1.v1.q_ref, bf16[768,1536]{1,0:T(8,128)(2,1)} %shard_map.487.q_ref.k2.v2, bf16[768,1536]{1,0:T(8,128)(2,1)} %shard_map.488.k1.v1.q_ref, ...), custom_call_target="tpu_custom_call" | custom-call | flops 19327352832 | bytes 3145728 | tf_op jit(solution)/shard_map/pallas_call | solution.py:173
  249.3 5.3 all-to-all-done.2
  256.1 7.6 %shard_map.491 = (f32[12,64,1024]{2,1,0:T(8,128)}, bf16[768,1024]{1,0:T(8,128)(2,1)}, bf16[768,1024]{1,0:T(8,128)(2,1)}) custom-call(s32[4]{0:T(128)} %iota_xor_fusion.order, bf16[256,1536]{1,0:T(8,128)(2,1)} %get-tuple-element.79.a0.out_ref, bf16[256,768]{1,0:T(8,128)(2,1)} %collective-permute-done.19.a1, bf16[256,768]{1,0:T(8,128)(2,1)} %collective-permute-done.20.a2, ...), custom_call_target="tpu_custom_call" | custom-call | flops 1610612736 | bytes 11010048 | tf_op jit(solution)/shard_map/pallas_call | solution.py:360
  263.7 65.9 %shard_map.492 = (bf16[32,2,32,4096]{3,2,1,0:T(8,128)(2,1)}, bf16[12,64,1024]{2,1,0:T(8,128)(2,1)}, f32[12,64,1024]{2,1,0:T(8,128)}, f32[12,4,1024]{2,1,0:T(4,12...) custom-call(s32[4]{0:T(128)} %iota_xor_fusion.order, ...), custom_call_target="tpu_custom_call" | custom-call | flops 38654705664 | bytes 33554432 | tf_op jit(solution)/shard_map/pallas_call | solution.py:452
  336.9 4.4 all-to-all-start.4
  341.4 48.3 %shard_map.493 = (bf16[256,1536]{1,0:T(8,128)(2,1)}, f32[256,3072]{1,0:T(8,128)}, f32[256,3072]{1,0:T(8,128)}) custom-call(bf16[768,1536]{1,0:T(8,128)(2,1)} %shard_map.488.k1.v1.q_ref, bf16[768,1536]{1,0:T(8,128)(2,1)} %shard_map.488.k1.v1.q_ref, bf16[768,1536]{1,0:T(8,128)(2,1)} %shard_map.487.q_ref.k2.v2, bf16[768,1536]{1,0:T(8,128)(2,1)} %shard_map.488.k1.v1.q_ref, ...), custom_call_target="tpu_custom_call" | custom-call | flops 41070624768 | bytes 6291456 | tf_op jit(solution)/shard_map/pallas_call | solution.py:319
  389.7 50.6 %shard_map.494 = (bf16[256,1536]{1,0:T(8,128)(2,1)}, bf16[256,3072]{1,0:T(8,128)(2,1)}, bf16[256,3072]{1,0:T(8,128)(2,1)}) custom-call(bf16[768,1536]{1,0:T(8,128)(2,1)} %shard_map.487.q_ref.k2.v2, bf16[768,1536]{1,0:T(8,128)(2,1)} %shard_map.488.k1.v1.q_ref, bf16[768,1536]{1,0:T(8,128)(2,1)} %shard_map.487.q_ref.k2.v2, ...), custom_call_target="tpu_custom_call" | custom-call | flops 41070624768 | bytes 6291456 | tf_op jit(solution)/shard_map/pallas_call | solution.py:319
  440.3 12.6 %shard_map.495 = (bf16[2,768,1024]{2,1,0:T(8,128)(2,1)}, f32[768,1024]{1,0:T(8,128)}, f32[12,2,1024]{2,1,0:T(2,128)}) custom-call(bf16[784,1024]{1,0:T(8,128)(2,1)} %collective-permute-done.one, bf16[784,1024]{1,0:T(8,128)(2,1)} %collective-permute-done.1.two, f32[12,6,1024]{2,1,0:T(8,128)} %reshape.525.mod, bf16[256,1536]{1,0:T(8,128)(2,1)} %get-tuple-element.97.dq, ...), custom_call_target="tpu_custom_call" | custom-call | flops 4831838208 | bytes 9437184 | tf_op jit(solution)/shard_map/pallas_call | solution.py:530
  452.9 14.3 %shard_map.496 = (bf16[2,768,1024]{2,1,0:T(8,128)(2,1)}, bf16[1024,768]{1,0:T(8,128)(2,1)}, f32[12,2,1024]{2,1,0:T(2,128)}) custom-call(bf16[784,1024]{1,0:T(8,128)(2,1)} %fusion.2.one, bf16[784,1024]{1,0:T(8,128)(2,1)} %collective-permute-done.18.two, f32[12,6,1024]{2,1,0:T(8,128)} %reshape.525.mod, bf16[256,1536]{1,0:T(8,128)(2,1)} %get-tuple-element.102.dq, ...), custom_call_target="tpu_custom_call" | custom-call | flops 4831838208 | bytes 9437184 | tf_op jit(solution)/shard_map/pallas_call | solution.py:530
  475.7 8.5 %collective-permute-done.25 = f32[2,8,2304]{2,1,0:T(8,128)S(1)} collective-permute-done((f32[2,8,2304]{2,1,0:T(8,128)S(1)}, f32[2,8,2304]{2,1,0:T(8,128)S(1)}, u32[]{:S(2)}, u32[]{:S(2)}) %collective-permute-start.25) | collective-permute-done | bytes 147488 | tf_op jit(solution)/shard_map/ppermute | solution.py:566
  487.4 6.5 all-to-all-start.5
  499.2 12.5 %all-to-all-done.5 = bf16[8,32,1024]{2,1,0:T(8,128)(2,1)} async-done(((bf16[8,32,1024]{2,1,0:T(8,128)(2,1)}), bf16[8,32,1024]{2,1,0:T(8,128)(2,1)}, u32[]{:S(2)}, u32[]{:S(2)}) %all-to-all-start.5) | async-done | bytes 524320 | tf_op jit(solution)/shard_map/all_to_all | solution.py:730
  511.7 10.9 %all-to-all-start.3 = ((bf16[32,32,768]{2,1,0:T(8,128)(2,1)}), bf16[32,32,768]{2,1,0:T(8,128)(2,1)S(1)}, u32[]{:S(2)}, u32[]{:S(2)}) async-start(bf16[32,32,768]{2,1,0:T(8,128)(2,1)} %bitcast.211), calls=%async_computation.3 | async-start | bytes 3145728 | tf_op jit(solution)/shard_map/all_to_all | solution.py:750
  522.6 3.9 slice_bitcast_fusion.1
  531.1 3.3 collective-permute-start.32
  534.6 36.3 %collective-permute-done.30 = f32[12,192]{1,0:T(8,128)S(1)} collective-permute-done((f32[12,192]{1,0:T(8,128)S(1)}, f32[12,192]{1,0:T(8,128)S(1)}, u32[]{:S(2)}, u32[]{:S(2)}) %collective-permute-start.30) | collective-permute-done | bytes 9248 | tf_op jit(solution)/shard_map/ppermute | solution.py:566
  571.1 3.2 fusion.1
  574.3 6.0 collective-permute-start.36
  593.7 20.4 %collective-permute-done.36.three = bf16[768,1024]{1,0:T(8,128)(2,1)} collective-permute-done((bf16[768,1024]{1,0:T(8,128)(2,1)}, bf16[768,1024]{1,0:T(8,128)(2,1)}, u32[]{:S(2)}, u32[]{:S(2)}) %collective-permute-start.36) | collective-permute-done | bytes 1572896 | tf_op jit(solution)/shard_map/ppermute | solution.py:566
  614.2 7.2 %shard_map.497 = f32[12,64,1024]{2,1,0:T(8,128)} custom-call(bf16[12,64,1024]{2,1,0:T(8,128)(2,1)} %bitcast.192, f32[12,6,1024]{2,1,0:T(8,128)} %reshape.525.mod, f32[12,64,1024]{2,1,0:T(8,128)} %get-tuple-element.110.middle_grad, bf16[768,1024]{1,0:T(8,128)(2,1)} %get-tuple-element.157.one, bf16[768,1024]{1,0:T(8,128)(2,1)} %collective-permute-done.34.two, ...), custom_call_target="tpu_custom_call" | custom-call | flops 15728640 | bytes 12582912 | tf_op jit(solution)/shard_map/pallas_call | solution.py:554
  624.6 12.0 %all_to_all.35 = f32[32,8,128]{2,1,0:T(8,128)S(1)} all-to-all(f32[32,8,128]{2,1,0:T(8,128)S(1)} %broadcast_in_dim.43), channel_id=1, replica_groups=mesh['clip'=8,'row'=4] {'clip','row'}, dimensions={0} | all-to-all | bytes 262144 | tf_op jit(solution)/shard_map/all_to_all | solution.py:787
  (316 shorter events, 113.7 us)
Async XLA Ops:
  7.2 256.4 %all-gather.2.cloned.1.call-start = ((), (), s32[]{:S(2)}) async-start(), calls=%async_computation.8 | async-start | bytes 17301504 | tf_op jit(solution)/shard_map/all_gather | solution.py:642
  13.0 23.7 %collective-permute-start.8 = (bf16[12,1024]{1,0:T(8,128)(2,1)S(1)}, bf16[12,1024]{1,0:T(8,128)(2,1)S(1)}, u32[]{:S(2)}, u32[]{:S(2)}) collective-permute-start(bf16[12,1024]{1,0:T(8,128)(2,1)S(1)} %fusion.21), channel_id=1, source_target_pairs={{0,28},{4,24},{8,20},{12,16},{16,12},{20,8},{24,4},{28,0},{1,29},{... | collective-permute-start | bytes 73736 | tf_op jit(solution)/shard_map/ppermute | solution.py:566
  19.1 17.6 %collective-permute-start.7 = (bf16[12,1024]{1,0:T(8,128)(2,1)S(1)}, bf16[12,1024]{1,0:T(8,128)(2,1)S(1)}, u32[]{:S(2)}, u32[]{:S(2)}) collective-permute-start(bf16[12,1024]{1,0:T(8,128)(2,1)S(1)} %fusion.21), channel_id=1, source_target_pairs={{0,24},{4,28},{8,16},{12,20},{16,8},{20,12},{24,0},{28,4},{1,25},{... | collective-permute-start | bytes 73736 | tf_op jit(solution)/shard_map/ppermute | solution.py:566
  19.3 17.4 %collective-permute-start.6 = (bf16[12,1024]{1,0:T(8,128)(2,1)S(1)}, bf16[12,1024]{1,0:T(8,128)(2,1)S(1)}, u32[]{:S(2)}, u32[]{:S(2)}) collective-permute-start(bf16[12,1024]{1,0:T(8,128)(2,1)S(1)} %fusion.21), channel_id=1, source_target_pairs={{0,20},{4,16},{8,28},{12,24},{16,4},{20,0},{24,12},{28,8},{1,21},{... | collective-permute-start | bytes 73736 | tf_op jit(solution)/shard_map/ppermute | solution.py:566
  20.0 16.6 %collective-permute-start.5 = (bf16[12,1024]{1,0:T(8,128)(2,1)S(1)}, bf16[12,1024]{1,0:T(8,128)(2,1)S(1)}, u32[]{:S(2)}, u32[]{:S(2)}) collective-permute-start(bf16[12,1024]{1,0:T(8,128)(2,1)S(1)} %fusion.21), channel_id=1, source_target_pairs={{0,16},{4,20},{8,24},{12,28},{16,0},{20,4},{24,8},{28,12},{1,17},{... | collective-permute-start | bytes 73736 | tf_op jit(solution)/shard_map/ppermute | solution.py:566
  38.8 17.9 %collective-permute-start.15 = (f32[12,192]{1,0:T(8,128)S(1)}, f32[12,192]{1,0:T(8,128)S(1)}, u32[]{:S(2)}, u32[]{:S(2)}) collective-permute-start(f32[12,192]{1,0:T(8,128)S(1)} %get-tuple-element.189), channel_id=1, source_target_pairs={{0,28},{4,24},{8,20},{12,16},{16,12},{20,8},{24,4},{28,0},{1,29},{... | collective-permute-start | bytes 27656 | tf_op jit(solution)/shard_map/ppermute | solution.py:566
  43.8 12.9 %collective-permute-start.14 = (f32[12,192]{1,0:T(8,128)S(1)}, f32[12,192]{1,0:T(8,128)S(1)}, u32[]{:S(2)}, u32[]{:S(2)}) collective-permute-start(f32[12,192]{1,0:T(8,128)S(1)} %get-tuple-element.190), channel_id=1, source_target_pairs={{0,24},{4,28},{8,16},{12,20},{16,8},{20,12},{24,0},{28,4},{1,25},{... | collective-permute-start | bytes 27656 | tf_op jit(solution)/shard_map/ppermute | solution.py:566
  43.8 12.9 %collective-permute-start.13 = (f32[12,192]{1,0:T(8,128)S(1)}, f32[12,192]{1,0:T(8,128)S(1)}, u32[]{:S(2)}, u32[]{:S(2)}) collective-permute-start(f32[12,192]{1,0:T(8,128)S(1)} %get-tuple-element.191), channel_id=1, source_target_pairs={{0,20},{4,16},{8,28},{12,24},{16,4},{20,0},{24,12},{28,8},{1,21},{... | collective-permute-start | bytes 27656 | tf_op jit(solution)/shard_map/ppermute | solution.py:566
  56.8 94.2 %collective-permute-start.18 = (bf16[784,1024]{1,0:T(8,128)(2,1)}, bf16[784,1024]{1,0:T(8,128)(2,1)}, u32[]{:S(2)}, u32[]{:S(2)}) collective-permute-start(bf16[784,1024]{1,0:T(8,128)(2,1)} %fusion.2.one), channel_id=1, source_target_pairs={{0,1},{1,0},{2,3},{3,2},{4,5},{5,4},{6,7},{7,6},{8,9},{9,8},{10,11... | collective-permute-start | bytes 4816904 | tf_op jit(solution)/shard_map/ppermute | solution.py:566
  57.3 87.8 %collective-permute-start = (bf16[784,1024]{1,0:T(8,128)(2,1)}, bf16[784,1024]{1,0:T(8,128)(2,1)}, u32[]{:S(2)}, u32[]{:S(2)}) collective-permute-start(bf16[784,1024]{1,0:T(8,128)(2,1)} %fusion.2.one), channel_id=1, source_target_pairs={{0,2},{1,3},{2,0},{3,1},{4,6},{5,7},{6,4},{7,5},{8,10},{9,11},{10,... | collective-permute-start | bytes 4816904 | tf_op jit(solution)/shard_map/ppermute | solution.py:566
  60.4 91.3 %all-to-all-start = ((bf16[32,32,768]{2,1,0:T(8,128)(2,1)}), bf16[32,32,768]{2,1,0:T(8,128)(2,1)S(1)}, u32[]{:S(2)}, u32[]{:S(2)}) async-start(bf16[32,32,768]{2,1,0:T(8,128)(2,1)} %bitcast.36), calls=%async_computation | async-start | bytes 3145728 | tf_op jit(solution)/shard_map/all_to_all | solution.py:666
  65.8 77.5 %collective-permute-start.17 = (f32[2,8,12,192]{3,2,1,0:T(8,128)S(1)}, f32[2,8,12,192]{3,2,1,0:T(8,128)S(1)}, u32[]{:S(2)}, u32[]{:S(2)}) collective-permute-start(f32[2,8,12,192]{3,2,1,0:T(8,128)S(1)} %pad_maximum_fusion.12), channel_id=1, source_target_pairs={{0,2},{1,3},{2,0},{3,1},{4,6},{5,7},{6,4},{7,5},{8,10},{9,11},{10,... | collective-permute-start | bytes 442376 | tf_op jit(solution)/shard_map/ppermute | solution.py:566
  166.5 47.5 %all-to-all-start.1 = ((bf16[8,32,1024]{2,1,0:T(8,128)(2,1)}), bf16[8,32,1024]{2,1,0:T(8,128)(2,1)S(1)}, u32[]{:S(2)}, u32[]{:S(2)}) async-start(bf16[8,32,1024]{2,1,0:T(8,128)(2,1)} %broadcast_in_dim.41), calls=%async_computation.1 | async-start | bytes 1048576 | tf_op jit(solution)/shard_map/all_to_all | solution.py:702
  212.2 43.9 %collective-permute-start.21 = (bf16[256,768]{1,0:T(8,128)(2,1)S(1)}, bf16[256,768]{1,0:T(8,128)(2,1)}, u32[]{:S(2)}, u32[]{:S(2)}) collective-permute-start(bf16[256,768]{1,0:T(8,128)(2,1)S(1)} %get-tuple-element.158), channel_id=1, source_target_pairs={{0,3},{1,2},{2,1},{3,0},{4,7},{5,6},{6,5},{7,4},{8,11},{9,10},{10,... | collective-permute-start | bytes 1179656 | tf_op jit(solution)/shard_map/ppermute | solution.py:566
  212.6 43.5 %collective-permute-start.20 = (bf16[256,768]{1,0:T(8,128)(2,1)S(1)}, bf16[256,768]{1,0:T(8,128)(2,1)}, u32[]{:S(2)}, u32[]{:S(2)}) collective-permute-start(bf16[256,768]{1,0:T(8,128)(2,1)S(1)} %get-tuple-element.159), channel_id=1, source_target_pairs={{0,2},{1,3},{2,0},{3,1},{4,6},{5,7},{6,4},{7,5},{8,10},{9,11},{10,... | collective-permute-start | bytes 1179656 | tf_op jit(solution)/shard_map/ppermute | solution.py:566
  215.7 38.9 %all-to-all-start.2 = ((bf16[4,8,32,1024]{3,2,1,0:T(8,128)(2,1)}), bf16[4,8,32,1024]{3,2,1,0:T(8,128)(2,1)S(1)}, u32[]{:S(2)}, u32[]{:S(2)}) async-start(bf16[4,8,32,1024]{3,2,1,0:T(8,128)(2,1)} %broadcast_in_dim.42), calls=%async_computation.2 | async-start | bytes 4194304 | tf_op jit(solution)/shard_map/all_to_all | solution.py:705
  219.3 402.1 %reduce-scatter.2.cloned.1.call-start = ((), (), s32[]{:S(2)}) async-start(), calls=%async_computation.9 | async-start | bytes 17301504 | tf_op jit(solution)/shard_map/reduce_scatter | solution.py:722
  330.7 59.0 %collective-permute-start.23 = (bf16[256,768]{1,0:T(8,128)(2,1)S(1)}, bf16[256,768]{1,0:T(8,128)(2,1)}, u32[]{:S(2)}, u32[]{:S(2)}) collective-permute-start(bf16[256,768]{1,0:T(8,128)(2,1)S(1)} %copy-done.30), channel_id=1, source_target_pairs={{0,2},{1,3},{2,0},{3,1},{4,6},{5,7},{6,4},{7,5},{8,10},{9,11},{10,... | collective-permute-start | bytes 1179656 | tf_op jit(solution)/shard_map/ppermute | solution.py:566
  331.2 58.5 %collective-permute-start.24 = (bf16[256,768]{1,0:T(8,128)(2,1)S(1)}, bf16[256,768]{1,0:T(8,128)(2,1)}, u32[]{:S(2)}, u32[]{:S(2)}) collective-permute-start(bf16[256,768]{1,0:T(8,128)(2,1)S(1)} %copy-done.29), channel_id=1, source_target_pairs={{0,3},{1,2},{2,1},{3,0},{4,7},{5,6},{6,5},{7,4},{8,11},{9,10},{10,... | collective-permute-start | bytes 1179656 | tf_op jit(solution)/shard_map/ppermute | solution.py:566
  336.9 147.5 %all-to-all-start.4 = ((bf16[4,8,32,1024]{3,2,1,0:T(8,128)(2,1)}), bf16[4,8,32,1024]{3,2,1,0:T(8,128)(2,1)}, u32[]{:S(2)}, u32[]{:S(2)}) async-start(bf16[4,8,32,1024]{3,2,1,0:T(8,128)(2,1)} %copy.194), calls=%async_computation.4 | async-start | bytes 4194304 | tf_op jit(solution)/shard_map/all_to_all | solution.py:728
  487.4 24.3 %all-to-all-start.5 = ((bf16[8,32,1024]{2,1,0:T(8,128)(2,1)}), bf16[8,32,1024]{2,1,0:T(8,128)(2,1)}, u32[]{:S(2)}, u32[]{:S(2)}) async-start(bf16[8,32,1024]{2,1,0:T(8,128)(2,1)} %reduce_sum.177), calls=%async_computation.5 | async-start | bytes 1048576 | tf_op jit(solution)/shard_map/all_to_all | solution.py:730
  495.2 75.9 %collective-permute-start.35 = (bf16[768,1024]{1,0:T(8,128)(2,1)}, bf16[768,1024]{1,0:T(8,128)(2,1)S(1)}, u32[]{:S(2)}, u32[]{:S(2)}) collective-permute-start(bf16[768,1024]{1,0:T(8,128)(2,1)} %slice_bitcast_fusion), channel_id=1, source_target_pairs={{0,1},{1,0},{2,3},{3,2},{4,5},{5,4},{6,7},{7,6},{8,9},{9,8},{10,11... | collective-permute-start | bytes 4718600 | tf_op jit(solution)/shard_map/ppermute | solution.py:566
  495.7 34.0 %collective-permute-start.27 = (f32[12,192]{1,0:T(8,128)S(1)}, f32[12,192]{1,0:T(8,128)S(1)}, u32[]{:S(2)}, u32[]{:S(2)}) collective-permute-start(f32[12,192]{1,0:T(8,128)S(1)} %squeeze.53), channel_id=1, source_target_pairs={{0,4},{4,0},{8,12},{12,8},{16,20},{20,16},{24,28},{28,24},{1,5},{5... | collective-permute-start | bytes 27656 | tf_op jit(solution)/shard_map/ppermute | solution.py:566
  497.7 33.5 %collective-permute-start.28 = (f32[12,192]{1,0:T(8,128)S(1)}, f32[12,192]{1,0:T(8,128)S(1)}, u32[]{:S(2)}, u32[]{:S(2)}) collective-permute-start(f32[12,192]{1,0:T(8,128)S(1)} %squeeze.54), channel_id=1, source_target_pairs={{0,8},{4,12},{8,0},{12,4},{16,24},{20,28},{24,16},{28,20},{1,9},{5... | collective-permute-start | bytes 27656 | tf_op jit(solution)/shard_map/ppermute | solution.py:566
  499.1 35.3 %collective-permute-start.29 = (f32[12,192]{1,0:T(8,128)S(1)}, f32[12,192]{1,0:T(8,128)S(1)}, u32[]{:S(2)}, u32[]{:S(2)}) collective-permute-start(f32[12,192]{1,0:T(8,128)S(1)} %squeeze.55), channel_id=1, source_target_pairs={{0,12},{4,8},{8,4},{12,0},{16,28},{20,24},{24,20},{28,16},{1,13},{... | collective-permute-start | bytes 27656 | tf_op jit(solution)/shard_map/ppermute | solution.py:566
  511.7 73.5 %all-to-all-start.3 = ((bf16[32,32,768]{2,1,0:T(8,128)(2,1)}), bf16[32,32,768]{2,1,0:T(8,128)(2,1)S(1)}, u32[]{:S(2)}, u32[]{:S(2)}) async-start(bf16[32,32,768]{2,1,0:T(8,128)(2,1)} %bitcast.211), calls=%async_computation.3 | async-start | bytes 3145728 | tf_op jit(solution)/shard_map/all_to_all | solution.py:750
  526.8 44.1 %collective-permute-start.30 = (f32[12,192]{1,0:T(8,128)S(1)}, f32[12,192]{1,0:T(8,128)S(1)}, u32[]{:S(2)}, u32[]{:S(2)}) collective-permute-start(f32[12,192]{1,0:T(8,128)S(1)} %squeeze.56), channel_id=1, source_target_pairs={{0,16},{4,20},{8,24},{12,28},{16,0},{20,4},{24,8},{28,12},{1,17},{... | collective-permute-start | bytes 27656 | tf_op jit(solution)/shard_map/ppermute | solution.py:566
  529.7 41.2 %collective-permute-start.31 = (f32[12,192]{1,0:T(8,128)S(1)}, f32[12,192]{1,0:T(8,128)S(1)}, u32[]{:S(2)}, u32[]{:S(2)}) collective-permute-start(f32[12,192]{1,0:T(8,128)S(1)} %squeeze.57), channel_id=1, source_target_pairs={{0,20},{4,16},{8,28},{12,24},{16,4},{20,0},{24,12},{28,8},{1,21},{... | collective-permute-start | bytes 27656 | tf_op jit(solution)/shard_map/ppermute | solution.py:566
  531.1 39.8 %collective-permute-start.32 = (f32[12,192]{1,0:T(8,128)S(1)}, f32[12,192]{1,0:T(8,128)S(1)}, u32[]{:S(2)}, u32[]{:S(2)}) collective-permute-start(f32[12,192]{1,0:T(8,128)S(1)} %squeeze.58), channel_id=1, source_target_pairs={{0,24},{4,28},{8,16},{12,20},{16,8},{20,12},{24,0},{28,4},{1,25},{... | collective-permute-start | bytes 27656 | tf_op jit(solution)/shard_map/ppermute | solution.py:566
  534.4 36.6 %collective-permute-start.33 = (f32[12,192]{1,0:T(8,128)S(1)}, f32[12,192]{1,0:T(8,128)S(1)}, u32[]{:S(2)}, u32[]{:S(2)}) collective-permute-start(f32[12,192]{1,0:T(8,128)S(1)} %squeeze.59), channel_id=1, source_target_pairs={{0,28},{4,24},{8,20},{12,16},{16,12},{20,8},{24,4},{28,0},{1,29},{... | collective-permute-start | bytes 27656 | tf_op jit(solution)/shard_map/ppermute | solution.py:566
  570.9 22.8 %collective-permute-start.34 = (bf16[768,1024]{1,0:T(8,128)(2,1)}, bf16[768,1024]{1,0:T(8,128)(2,1)}, u32[]{:S(2)}, u32[]{:S(2)}) collective-permute-start(bf16[768,1024]{1,0:T(8,128)(2,1)} %get-tuple-element.156), channel_id=1, source_target_pairs={{0,1},{1,0},{2,3},{3,2},{4,5},{5,4},{6,7},{7,6},{8,9},{9,8},{10,11... | collective-permute-start | bytes 4718600 | tf_op jit(solution)/shard_map/ppermute | solution.py:566
  574.3 39.8 %collective-permute-start.36 = (bf16[768,1024]{1,0:T(8,128)(2,1)}, bf16[768,1024]{1,0:T(8,128)(2,1)}, u32[]{:S(2)}, u32[]{:S(2)}) collective-permute-start(bf16[768,1024]{1,0:T(8,128)(2,1)} %fusion.1), channel_id=1, source_target_pairs={{0,2},{1,3},{2,0},{3,1},{4,6},{5,7},{6,4},{7,5},{8,10},{9,11},{10,... | collective-permute-start | bytes 4718600 | tf_op jit(solution)/shard_map/ppermute | solution.py:566
  (45 other events, 342.4 us)
Sparse Core Ops, SparseCore 0:
  11.5 158.6 all-gather.1
  329.8 240.8 reduce-scatter.1

commit v4 on v3

--- a/solution.py
+++ b/solution.py
@@ -30,6 +30,7 @@
 TT = (((0,), (1,)), ((), ()))
 MIB = 2**20
 VMEM = pltpu.VMEM
+ROW = ("x", "core")
 
 
 def dot(left, right, dims=NN):
@@ -374,28 +375,44 @@
     )(order, *parts, proj, tokens, cotangent, mod)
 
 
-def feed_kernel(
-    order, weights, hidden, branch, tokens, cotangent, att_out, mod, a0, a1, a2, a3, proj,
-    grads, block_out, middle_grad, mod_grad, d0, d1, d2, d3, proj_raw, out_sum, in_sum, att_grad,
-):
+def weight_places(shape):
+    groups, pairs = shape[0], shape[1]
+    if pairs == 1:
+        return [(0, 0)]
+    return [(2 * c + core, x) for c in range(groups // 2) for x in range(pairs) for core in range(2)]
+
+
+def load_weight(weights, kind):
+    return jnp.concatenate(
+        [weights[group, x, kind] for group, x in weight_places(weights.shape)], axis=0
+    )
+
+
+def feed_kernel(weights, hidden, branch, out, into, active_out, wide_out, out_sum, in_sum):
     step = pl.program_id(0)
-    count, width = hidden.shape
-    units = weights.shape[3]
-    widen = weights[:, 0].reshape(width, units)
-    narrow = weights[:, 1].reshape(width, units)
+    widen = load_weight(weights, 0)
+    narrow = load_weight(weights, 1)
     hid, bra = hidden[...], branch[...]
-    wide = dot(hid, widen)
-    active_grad = dot(bra, narrow)
+    units = widen.shape[1]
+    half = units // 2
     factor = math.sqrt(2.0 / math.pi)
-    square = wide * wide
-    bend = jnp.tanh(factor * wide * (1.0 + 0.044715 * square))
-    active = (0.5 * wide * (1.0 + bend)).astype(bf16)
-    slope = 0.5 * (1.0 + bend) + 0.5 * wide * (1.0 - bend * bend) * (
-        factor * (1.0 + 3.0 * 0.044715 * square)
-    )
-    wide_grad = (active_grad * slope).astype(bf16)
-    out_part = dot(active, narrow, NT)
-    in_part = dot(wide_grad, widen, NT)
+    wides = [dot(hid, widen[:, at : at + half]) for at in (0, half)]
+    grads = [dot(bra, narrow[:, at : at + half]) for at in (0, half)]
+    out_part, in_part = None, None
+    for at, wide, grad in zip((0, half), wides, grads):
+        square = wide * wide
+        bend = jnp.tanh(factor * wide * (1.0 + 0.044715 * square))
+        active = (0.5 * wide * (1.0 + bend)).astype(bf16)
+        slope = 0.5 * (1.0 + bend) + 0.5 * wide * (1.0 - bend * bend) * (
+            factor * (1.0 + 3.0 * 0.044715 * square)
+        )
+        wide_grad = (grad * slope).astype(bf16)
+        active_out[:, at : at + half] = active
+        wide_out[:, at : at + half] = wide_grad
+        one = dot(active, narrow[:, at : at + half], NT)
+        two = dot(wide_grad, widen[:, at : at + half], NT)
+        out_part = one if out_part is None else out_part + one
+        in_part = two if in_part is None else in_part + two
 
     @pl.when(step == 0)
     def _():
@@ -407,68 +424,161 @@
         out_sum[...] += out_part
         in_sum[...] += in_part
 
-    shape = (grads.shape[0], grads.shape[2], units)
-    grads[:, 0] = dot(hid, wide_grad, TN).astype(bf16).reshape(shape)
-    grads[:, 1] = dot(bra, active, TN).astype(bf16).reshape(shape)
-
     @pl.when(step == pl.num_programs(0) - 1)
     def _():
-        frames, per_frame, _ = tokens.shape
-        chunk = 2
-        for start in range(0, frames, chunk):
-            some = slice(start, start + chunk)
-            flat = slice(start * per_frame, (start + chunk) * per_frame)
-            cube = (chunk, per_frame, width)
-            here = mod[some]
-            att = att_out[some]
-            middle = tokens[some].astype(f32) + here[:, 2:3] * att
-            normed, inverse = layer_norm(middle)
-            upstream = cotangent[some].astype(f32)
-            branch_out = out_sum[flat, :].reshape(cube)
-            block_out[some] = (middle + here[:, 5:6] * branch_out).astype(bf16)
-            mod_grad[some, 3:4] = jnp.sum(upstream * branch_out, axis=1, keepdims=True)
-            hid_grad = in_sum[flat, :].reshape(cube)
-            mod_grad[some, 1:2] = jnp.sum(hid_grad, axis=1, keepdims=True)
-            mod_grad[some, 2:3] = jnp.sum(hid_grad * normed, axis=1, keepdims=True)
-            mid = upstream + norm_back(normed, inverse, hid_grad * (1.0 + here[:, 4:5]))
-            middle_grad[some] = mid
-            mod_grad[some, 0:1] = jnp.sum(mid * att, axis=1, keepdims=True)
-            att_grad[flat, :] = (here[:, 2:3] * mid).astype(bf16).reshape(chunk * per_frame, width)
-        features = a0.shape[0]
-        grad = att_grad[...]
-        for slot, (part, out) in enumerate(((a0, d0), (a1, d1), (a2, d2), (a3, d3))):
-            place = pl.ds(pl.multiple_of(order[slot] * features, features), features)
-            out[...] = dot(proj[:, place], grad, TT).astype(bf16)
-            proj_raw[place, :] = dot(part[...], grad).astype(bf16)
-
-
-def feed_forward(order, weights, hidden, branch, tokens, cotangent, att_out, mod, parts, proj):
+        out[...] = out_sum[...].astype(out.dtype)
+        into[...] = in_sum[...].astype(into.dtype)
+
+
+def feed_forward(weights, hidden, branch, kind):
     count, width = hidden.shape
-    groups, _, rows, units = weights.shape
+    units = weights.shape[-1]
     block = 512
-    frames = tokens.shape[0]
-    features = parts[0].shape[0]
-    spec = pl.BlockSpec((groups, 2, rows, block), lambda i: (0, 0, 0, i))
+    spec = pl.BlockSpec(weights.shape[:-1] + (block,), lambda i: (0, 0, 0, 0, i))
+    flat = pl.BlockSpec((count, width), lambda i: (0, 0))
+    wide = pl.BlockSpec((count, block), lambda i: (0, i))
     return pl.pallas_call(
         feed_kernel,
         grid=(units // block,),
-        in_specs=[whole(pltpu.SMEM), spec]
-        + [whole()] * 6
-        + [pl.BlockSpec((features, count), lambda i: (0, 0))] * 4
+        in_specs=[spec, flat, flat],
+        out_specs=[flat, flat, wide, wide],
+        out_shape=[jax.ShapeDtypeStruct((count, width), kind)] * 2
+        + [jax.ShapeDtypeStruct((count, units), bf16)] * 2,
+        scratch_shapes=[VMEM((count, width), f32), VMEM((count, width), f32)],
+        compiler_params=params(),
+        cost_estimate=cost(8 * count * width * units, 4 * width * units + 4 * count * units),
+    )(weights, hidden, branch)
+
+
+def feed_weight_kernel(parts, *refs):
+    hidden, branch = refs[:parts], refs[parts : 2 * parts]
+    active, wide = refs[2 * parts : 3 * parts], refs[3 * parts : 4 * parts]
+    grads = refs[-1]
+    for kind, left, right in ((0, hidden, wide), (1, branch, active)):
+        total = None
+        for one, two in zip(left, right):
+            term = dot(one[...], two[...], TN)
+            total = term if total is None else total + term
+        total = total.astype(bf16)
+        rows = grads.shape[3]
+        for at, (group, x) in enumerate(weight_places(grads.shape)):
+            grads[group, x, kind] = total[at * rows : (at + 1) * rows]
+
+
+def feed_weights(shape, hidden, branch, active, wide):
+    width = hidden[0].shape[1]
+    units = active[0].shape[1]
+    block = 512
+
+    def fixed(value):
+        return pl.BlockSpec(value.shape, lambda i: (0, 0))
+
+    def moving(value):
+        return pl.BlockSpec((value.shape[0], block), lambda i: (0, i))
+
+    count = sum(value.shape[0] for value in hidden)
+    return pl.pallas_call(
+        functools.partial(feed_weight_kernel, len(hidden)),
+        grid=(units // block,),
+        in_specs=[fixed(value) for value in (*hidden, *branch)]
+        + [moving(value) for value in (*active, *wide)],
+        out_specs=pl.BlockSpec(shape[:-1] + (block,), lambda i: (0, 0, 0, 0, i)),
+        out_shape=jax.ShapeDtypeStruct(shape, bf16),
+        compiler_params=params(),
+        cost_estimate=cost(4 * count * width * units, 4 * width * units + 4 * count * units),
+    )(*hidden, *branch, *active, *wide)
+
+
+def middle_kernel(
+    order, into, into_far, tokens, cotangent, att_out, mod, a0, a1, a2, a3, proj,
+    middle_grad, mod_grad, d0, d1, d2, d3, proj_raw, raw_sum,
+):
+    step = pl.program_id(0)
+    shape = tokens.shape
+    flat = (shape[0] * shape[1], shape[2])
+    att = att_out[...]
+    middle = tokens[...].astype(f32) + mod[:, 2:3] * att
+    normed, inverse = layer_norm(middle)
+    hid_grad = (into[...] + into_far[...].astype(f32)).reshape(shape)
+    mod_grad[:, 1:2] = jnp.sum(hid_grad, axis=1, keepdims=True)
+    mod_grad[:, 2:3] = jnp.sum(hid_grad * normed, axis=1, keepdims=True)
+    mid = cotangent[...].astype(f32) + norm_back(normed, inverse, hid_grad * (1.0 + mod[:, 4:5]))
+    middle_grad[...] = mid
+    mod_grad[:, 0:1] = jnp.sum(mid * att, axis=1, keepdims=True)
+    grad = (mod[:, 2:3] * mid).astype(bf16).reshape(flat)
+    features = a0.shape[0]
+    for slot, (part, out) in enumerate(((a0, d0), (a1, d1), (a2, d2), (a3, d3))):
+        place = pl.ds(pl.multiple_of(order[slot] * features, features), features)
+        out[...] = dot(proj[:, place], grad, TT).astype(bf16)
+        term = dot(part[...], grad)
+
+        @pl.when(step == 0)
+        def _():
+            raw_sum[place, :] = term
+
+        @pl.when(step > 0)
+        def _():
+            raw_sum[place, :] += term
+
+    @pl.when(step == pl.num_programs(0) - 1)
+    def _():
+        proj_raw[...] = jnp.transpose(raw_sum[...]).astype(bf16)
+
+
+def middle_back(order, into, into_far, tokens, cotangent, att_out, mod, parts, proj):
+    frames, per_frame, width = tokens.shape
+    chunk = 4
+    block = chunk * per_frame
+    features = parts[0].shape[0]
+    cube = pl.BlockSpec((chunk, per_frame, width), lambda i: (i, 0, 0))
+    flat = pl.BlockSpec((block, width), lambda i: (i, 0))
+    turned = pl.BlockSpec((features, block), lambda i: (0, i))
+    return pl.pallas_call(
+        middle_kernel,
+        grid=(frames // chunk,),
+        in_specs=[whole(pltpu.SMEM), flat, flat, cube, cube, cube]
+        + [pl.BlockSpec((chunk, 6, width), lambda i: (i, 0, 0))]
+        + [turned] * 4
         + [whole()],
-        out_specs=[spec] + [whole()] * 8,
+        out_specs=[cube, pl.BlockSpec((chunk, 3, width), lambda i: (i, 0, 0))]
+        + [turned] * 4
+        + [whole()],
         out_shape=[
-            jax.ShapeDtypeStruct(weights.shape, bf16),
+            jax.ShapeDtypeStruct(tokens.shape, f32),
+            jax.ShapeDtypeStruct((frames, 3, width), f32),
+        ]
+        + [jax.ShapeDtypeStruct((features, frames * per_frame), bf16)] * 4
+        + [jax.ShapeDtypeStruct((width, width), bf16)],
+        scratch_shapes=[VMEM((width, width), f32)],
+        compiler_params=params(),
+        cost_estimate=cost(4 * frames * per_frame * width * width, 24 * frames * per_frame * width),
+    )(order, into, into_far, tokens, cotangent, att_out, mod, *parts, proj)
+
+
+def output_kernel(out, out_far, tokens, cotangent, att_out, mod, block_out, mod_grad):
+    branch_out = (out[...] + out_far[...].astype(f32)).reshape(tokens.shape)
+    middle = tokens[...].astype(f32) + mod[:, 2:3] * att_out[...]
+    block_out[...] = (middle + mod[:, 5:6] * branch_out).astype(bf16)
+    mod_grad[...] = jnp.sum(cotangent[...].astype(f32) * branch_out, axis=1, keepdims=True)
+
+
+def block_output(out, out_far, tokens, cotangent, att_out, mod):
+    frames, per_frame, width = tokens.shape
+    chunk = 4
+    cube = pl.BlockSpec((chunk, per_frame, width), lambda i: (i, 0, 0))
+    flat = pl.BlockSpec((chunk * per_frame, width), lambda i: (i, 0))
+    return pl.pallas_call(
+        output_kernel,
+        grid=(frames // chunk,),
+        in_specs=[flat, flat, cube, cube, cube, pl.BlockSpec((chunk, 6, width), lambda i: (i, 0, 0))],
+        out_specs=[cube, pl.BlockSpec((chunk, 1, width), lambda i: (i, 0, 0))],
+        out_shape=[
             jax.ShapeDtypeStruct(tokens.shape, bf16),
-            jax.ShapeDtypeStruct(tokens.shape, f32),
-            jax.ShapeDtypeStruct((frames, 4, width), f32),
-        ]
-        + [jax.ShapeDtypeStruct((features, count), bf16)] * 4
-        + [jax.ShapeDtypeStruct((width, width), bf16)],
-        scratch_shapes=[VMEM((count, width), f32), VMEM((count, width), f32), VMEM((count, width), bf16)],
-        compiler_params=params(62),
-        cost_estimate=cost(12 * count * width * units, 8 * width * units),
-    )(order, weights, hidden, branch, tokens, cotangent, att_out, mod, *parts, proj)
+            jax.ShapeDtypeStruct((frames, 1, width), f32),
+        ],
+        compiler_params=params(),
+        cost_estimate=cost(8 * frames * per_frame * width, 16 * frames * per_frame * width),
+    )(out, out_far, tokens, cotangent, att_out, mod)
 
 
 def first_back_kernel(half, last, one, two, mod, dq, dk, dv, weight, *rest):
@@ -630,20 +740,9 @@
     count = frames * per_frame
     devices = clips * rows
     features = width // rows
-    clip, row = lax.axis_index("clip"), lax.axis_index("row")
-    both = ("clip", "row")
+    clip, far, row = lax.axis_index("clip"), lax.axis_index("x"), lax.axis_index(ROW)
+    both = ("clip",) + ROW
     order = (row ^ jnp.arange(rows)).astype(jnp.int32)
-
-    shard = widen_weight.shape[0]
-    feed_shard = jnp.concatenate(
-        [widen_weight.astype(bf16), narrow_weight.T.astype(bf16)], axis=0
-    )
-    units = feed_shard.shape[1]
-    feed_full = lax.all_gather(feed_shard, both, axis=0, tiled=True)
-    feed_full = feed_full.reshape(devices, 2, shard, units)
-    fused = shard % 16 == 0
-    if not fused:
-        feed_full = feed_full.transpose(1, 0, 2, 3).reshape(1, 2, width, units)
 
     own = tokens.reshape(frames, per_frame, width)
     upstream = cotangent.reshape(frames, per_frame, width)
@@ -656,30 +755,45 @@
     small = jnp.pad(small, ((0, 0), (0, spare * width - count))).reshape(3 * spare, width)
     small = jnp.pad(small, ((0, 16 - 3 * spare), (0, 0)))
     tok0 = jnp.concatenate([own.reshape(count, width), small], axis=0)
-    tok2 = swap(tok0, "row", rows, 2)
-    tok1 = swap(tok0, "row", rows, 1)
-    tok3 = swap(tok2, "row", rows, 1)
-
+    tok2 = swap(tok0, ROW, rows, 2)
+    tok1 = swap(tok0, ROW, rows, 1)
+    tok3 = swap(tok2, ROW, rows, 1)
+
+    shard = widen_weight.shape[0]
     attend_mine = attend_weight.astype(bf16).reshape(shard, 3, rows, features)
-    attend_mine = attend_mine.transpose(2, 0, 1, 3).reshape(1, rows, shard, 3 * features)
-    attend_mine = jnp.broadcast_to(attend_mine, (clips, rows, shard, 3 * features))
-    attend_full = lax.all_to_all(
-        attend_mine.reshape(devices, shard, 3 * features), both, 0, 0, tiled=True
-    )
-    attend_turned = attend_full.reshape(width, 3 * features).T
+    attend_mine = attend_mine.transpose(2, 0, 1, 3).reshape(rows, shard, 3 * features)
+    attend_mine = relative(trade(relative(attend_mine, row), ROW, rows), row)
+    attend_full = lax.all_gather(
+        attend_mine.reshape(rows * shard, 3 * features), "clip", axis=0, tiled=True
+    )
+
+    units = widen_weight.shape[1]
+    feed_mine = jnp.stack([widen_weight.astype(bf16), narrow_weight.T.astype(bf16)])
+    feed_mine = feed_mine.reshape(2, shard, 2, units // 2).transpose(2, 0, 1, 3)
+    feed_mine = relative(trade(relative(feed_mine, far), "x", 2), far)
+    feed_mine, attend_full = lax.optimization_barrier((feed_mine, attend_full))
+    attend_turned = attend_full.T
+    feed_full = lax.all_gather(
+        feed_mine.reshape(4 * shard, units // 2), ("clip", "core"), axis=0, tiled=True
+    )
+    feed_full = feed_full.reshape(2 * clips, 2, 2, shard, units // 2)
+    fused = shard % 16 == 0
+    if not fused:
+        feed_full = feed_full.reshape(clips, 2, 2, 2, shard, units // 2).transpose(3, 0, 2, 1, 4, 5)
+        feed_full = feed_full.reshape(1, 1, 2, width, units // 2)
 
     cond_act = jax.nn.silu(condition[0].astype(f32)).astype(bf16)
-    cond_act, tok0 = lax.optimization_barrier((cond_act, tok0))
-    cond_all = trade([cond_act] * clips, "clip", clips).reshape(clips * frames, width)
+    cond_all = lax.all_to_all(
+        jnp.broadcast_to(cond_act[None], (clips, frames, width)), "clip", 0, 0, tiled=True
+    ).reshape(clips * frames, width)
     mod_mine = dot(cond_all, adaptive_weight.astype(bf16)) + adaptive_offsets.astype(bf16).astype(
         f32
     )
     part = mod_mine.shape[1]
-    mod = trade(mod_mine.reshape(clips, frames, part), "clip", clips)[None]
-    for step in (1, 2):
-        mod = jnp.concatenate([mod, swap(mod, "row", rows, step)], axis=0)
-    mod = relative(mod, row).reshape(rows, clips, frames * part).swapaxes(0, 1)
-    mod = relative(mod, clip).reshape(devices, frames, part)
+    mod_mine = jnp.broadcast_to(
+        mod_mine.reshape(clips, 1, frames, part), (clips, rows, frames, part)
+    )
+    mod = lax.all_to_all(mod_mine.reshape(devices, frames, part), both, 0, 0, tiled=True)
     mod = mod.transpose(1, 0, 2).reshape(frames, 6, width)
 
     small = jnp.concatenate(
@@ -703,46 +817,80 @@
         jnp.broadcast_to(project_mine[None], (clips, shard, width)), "clip", 0, 0, tiled=True
     )
     project_full = lax.all_to_all(
-        jnp.broadcast_to(project_full[None], (rows, clips, shard, width)), "row", 0, 0, tiled=True
+        jnp.broadcast_to(project_full[None], (rows, clips, shard, width)), ROW, 0, 0, tiled=True
     )
     project_full = project_full.transpose(1, 0, 2, 3).reshape(width, width)
+
+    cot_far, qkv_near = lax.optimization_barrier((upstream, qkv_near))
+    cot_far = swap(cot_far, "x", 2, 1)
+    branch_far = (mod[:, 5:6, :] * cot_far.astype(f32)).astype(bf16).reshape(count, width)
 
     out_far, lse_far = attend(qkv_far, qkv_near, qkv_far, bias)
     out_far, qkv_near = lax.optimization_barrier((out_far, qkv_near))
-    part2 = swap(out_far[:, :count], "row", rows, 2)
-    part3 = swap(out_far[:, count:], "row", rows, 3)
+    part2 = swap(out_far[:, :count], ROW, rows, 2)
+    part3 = swap(out_far[:, count:], ROW, rows, 3)
     out_near, lse_near = attend(qkv_near, qkv_near, qkv_far, bias)
-    parts = [out_near, swap(out_near[:, count:], "row", rows, 1), part2, part3]
+    parts = [out_near, swap(out_near[:, count:], ROW, rows, 1), part2, part3]
     att_out, hidden_two, branch_grad = project_out(order, parts, project_full, own, upstream, mod)
-    feed_raw, block_out, middle_grad, mod_late, d0, d1, d2, d3, project_raw = feed_forward(
-        order, feed_full, hidden_two, branch_grad, own, upstream, att_out, mod, parts, project_full
+    half = count // 2
+    hid1 = swap(hidden_two[:half], "x", 2, 1)
+    hid2 = swap(hidden_two[half:], "x", 2, 1)
+    out_own, in_own, act0, wide0 = feed_forward(feed_full, hidden_two, branch_grad, f32)
+    hid1, hid2, out_own = lax.optimization_barrier((hid1, hid2, out_own))
+    out1, in1, act1, wide1 = feed_forward(feed_full, hid1, branch_far[:half], bf16)
+    in1 = swap(in1, "x", 2, 1)
+    hid2, act1 = lax.optimization_barrier((hid2, act1))
+    out2, in2, act2, wide2 = feed_forward(feed_full, hid2, branch_far[half:], bf16)
+    in2 = swap(in2, "x", 2, 1)
+    out1 = swap(out1, "x", 2, 1)
+    out2 = swap(out2, "x", 2, 1)
+    feed_raw = feed_weights(
+        feed_full.shape,
+        (hidden_two, hid1, hid2),
+        (branch_grad, branch_far[:half], branch_far[half:]),
+        (act0, act1, act2),
+        (wide0, wide1, wide2),
     )
     if not fused:
-        feed_raw = feed_raw.reshape(2, devices, shard, units).transpose(1, 0, 2, 3)
+        feed_raw = feed_raw.reshape(2, clips, 2, 2, shard, units // 2).transpose(1, 3, 2, 0, 4, 5)
+    feed_raw, in1, in2 = lax.optimization_barrier((feed_raw, in1, in2))
     feed_sum = lax.psum_scatter(
-        feed_raw.reshape(devices * 2 * shard, units), both, scatter_dimension=0, tiled=True
-    ).astype(f32)
-    widen_sum, narrow_sum = feed_sum[:shard], feed_sum[shard:].T
-
-    project_raw = project_raw.T.reshape(clips, rows, shard, width).transpose(1, 0, 2, 3)
-    project_raw = lax.all_to_all(project_raw, "row", 0, 0, tiled=True)
+        feed_raw.reshape(8 * clips * shard, units // 2),
+        ("clip", "core"),
+        scatter_dimension=0,
+        tiled=True,
+    ).reshape(2, 2, shard, units // 2)
+    feed_sum = relative(trade(relative(feed_sum, far), "x", 2), far).astype(f32)
+    widen_sum, narrow_sum = feed_sum.transpose(1, 2, 0, 3).reshape(2, shard, units)
+    narrow_sum = narrow_sum.T
+    middle_grad, mod_late, d0, d1, d2, d3, project_raw = middle_back(
+        order, in_own, jnp.concatenate([in1, in2], axis=0), own, upstream, att_out, mod, parts, project_full
+    )
+
+    project_raw = project_raw.reshape(clips, rows, shard, width).transpose(1, 0, 2, 3)
+    project_raw = lax.all_to_all(project_raw, ROW, 0, 0, tiled=True)
+
+    turning = (cosine, sine)
+    d2 = swap(d2, ROW, rows, 2)
+    d3 = swap(d3, ROW, rows, 3)
+    d1 = swap(d1, ROW, rows, 1)
+    dq_near, dk, dv = attend_back(
+        qkv_near, qkv_near, qkv_far, bias, out_near, (d0, d1), lse_near, turning, 0
+    )
+    dk, d2, d3, project_raw, out1, out2 = lax.optimization_barrier(
+        (dk, d2, d3, project_raw, out1, out2)
+    )
     project_raw = jnp.sum(project_raw.astype(f32), axis=0).astype(bf16)
     project_raw = lax.all_to_all(project_raw, "clip", 0, 0, tiled=True)
-    project_sum = jnp.sum(project_raw.astype(f32), axis=0).T
-
-    turning = (cosine, sine)
-    d2 = swap(d2, "row", rows, 2)
-    d3 = swap(d3, "row", rows, 3)
-    d1 = swap(d1, "row", rows, 1)
-    dq_near, dk, dv = attend_back(
-        qkv_near, qkv_near, qkv_far, bias, out_near, (d0, d1), lse_near, turning, 0
-    )
-    dk, d2, d3 = lax.optimization_barrier((dk, d2, d3))
+    block_out, mod_gate = block_output(
+        out_own, jnp.concatenate([out1, out2], axis=0), own, upstream, att_out, mod
+    )
     dq_far, dk, dv = attend_back(
         qkv_far, qkv_near, qkv_far, bias, out_far, (d2, d3), lse_far, turning, 1, (dk, dv)
     )
     back_far, raw, mod_early = first_back(tok2, tok3, mod, dq_far, dk, dv, attend_turned, 1)
-    back_far, dq_near = lax.optimization_barrier((back_far, dq_near))
+    back_far, dq_near, project_raw = lax.optimization_barrier((back_far, dq_near, project_raw))
+    project_sum = jnp.sum(project_raw.astype(f32), axis=0).T
     back_near, attend_raw, mod_early = first_back(
         tok0, tok1, mod, dq_near, dk, dv, attend_turned, 0, (raw, mod_early)
     )
@@ -754,23 +902,23 @@
     attend_sum = attend_sum.transpose(1, 2, 0, 3).reshape(shard, 3 * width)
 
     far = (
-        back_far[0].astype(f32) + swap(back_far[1], "row", rows, 1).astype(f32)
+        back_far[0].astype(f32) + swap(back_far[1], ROW, rows, 1).astype(f32)
     ).astype(bf16)
     input_gradient = input_back(
         own,
         mod,
         middle_grad,
-        (back_near[0], swap(back_near[1], "row", rows, 1), swap(far, "row", rows, 2)),
-    )
-
-    mod_grad = jnp.concatenate([mod_early, mod_late], axis=1)
+        (back_near[0], swap(back_near[1], ROW, rows, 1), swap(far, ROW, rows, 2)),
+    )
+
+    mod_grad = jnp.concatenate([mod_early, mod_late, mod_gate], axis=1)
     mod_grad = mod_grad.reshape(frames, clips, rows, part).transpose(1, 2, 0, 3)
     mod_grad = relative(mod_grad.reshape(clips, rows * frames, part), clip)
     mod_grad = mod_grad.reshape(clips, rows, frames * part).swapaxes(0, 1)
     mod_grad = relative(mod_grad, row)
-    mod_grad = mod_grad[:2] + swap(mod_grad[2:], "row", rows, 2)
-    mod_grad = mod_grad[0] + swap(mod_grad[1], "row", rows, 1)
-    mod_grad = trade(mod_grad.reshape(clips, frames, part), "clip", clips)
+    mod_grad = mod_grad[:2] + swap(mod_grad[2:], ROW, rows, 2)
+    mod_grad = mod_grad[0] + swap(mod_grad[1], ROW, rows, 1)
+    mod_grad = relative(trade(mod_grad.reshape(clips, frames, part), "clip", clips), clip)
     mod_grad = mod_grad.reshape(clips * frames, part)
     adaptive_sum = lax.dot_general(
         mod_grad,
@@ -817,15 +965,17 @@
 
 
 def solution(mesh):
-    both = ("clip", "row")
-    token = P("clip", None, "row", None, None)
+    clips, rows = mesh.shape["clip"], mesh.shape["row"]
+    cut = jax.sharding.Mesh(mesh.devices.reshape(clips, 2, rows // 2), ("clip", "x", "core"))
+    both = ("clip",) + ROW
+    token = P("clip", None, ROW, None, None)
     down, across, line = P(both, None), P(None, both), P(both)
     placed = (
         token,
         P("clip", None, None),
         token,
-        P(None, "clip", None, "row", None),
-        P("clip", None, "row", None),
+        P(None, "clip", None, ROW, None),
+        P("clip", None, ROW, None),
         P("clip"),
         across,
         line,
@@ -850,8 +1000,8 @@
     for spec in (across, line, down, across, down, across):
         outs += (spec,) * 5
     return jax.shard_map(
-        functools.partial(local, mesh.shape["clip"], mesh.shape["row"]),
-        mesh=mesh,
+        functools.partial(local, clips, rows),
+        mesh=cut,
         in_specs=placed,
         out_specs=outs,
         check_vma=False,

time: 665 us -> 730 us (1.098)
  waiting for transfers between devices: 173 us -> 217 us
  Pallas kernels: 280 us -> 307 us
  starting transfers between devices: 92.1 us -> 65.7 us
  other arithmetic: 37.9 us -> 47.2 us
  local copies, waits for them, and re-layouts: 38.4 us -> 46.6 us
    all_to_all x2 -> x3, waiting for transfers between devices: 0.01 us -> 54.3 us  [the longest x1 21.5 us: local(): lax.all_to_all(mod_mine.reshape(devices, frames, part), both, 0, 0, tiled...]
    ppermute x37 -> x33, waiting for transfers between devices: 155 us -> 116 us  [swap(): lax.ppermute(value, axis, [(place, place ^ step) for place in range(size)])]
    all_gather x1 -> x2, waiting for transfers between devices: 0.01 us -> 29 us  [the longest x1 29 us: local(): lax.all_gather(attend_mine.reshape(rows * shard, 3 * features), 'clip', a...]
    pallas_call x1 -> x6, Pallas kernels: 65.9 us -> 93 us  [the longest x3 49.6 us: feed_forward(): pl.pallas_call(feed_kernel, grid=(units // block,), in_specs=[spec, flat,...]
    ppermute x37 -> x33, starting transfers between devices: 54 us -> 34.4 us  [swap(): lax.ppermute(value, axis, [(place, place ^ step) for place in range(size)])]
    all_to_all x1, waiting for transfers between devices: 12.5 us -> 0.01 us  [local(): project_raw = lax.all_to_all(project_raw, 'clip', 0, 0, tiled=True)]
    all_to_all x1, waiting for transfers between devices: 5.26 us -> 17.1 us  [local(): lax.all_to_all(jnp.broadcast_to(project_full[None], (rows, clips, shard,...]
  transfers between devices with their start and end apart: 45 -> 43, of which waited for: 11 -> 18; matrix products, arithmetic and copies ran while one was open for 9% -> 10% of each run, Pallas kernels for 33% -> 39%
where the time goes in v4:
time: 730 us; the launch traced here: 719 us
  Pallas kernels  307 us (42%)
  waiting for transfers between devices  217 us (30%)
  starting transfers between devices  65.7 us (9%)
  other arithmetic  47.2 us (6%)
  local copies, waits for them, and re-layouts  46.6 us (6%)
  between operations  21.9 us (3%)
  blocking collectives  11.6 us (2%)
    ppermute x33, waiting for transfers between devices, swap(): lax.ppermute(value, axis, [(place, place ^ step) for place in range(size)])  116 us
    pallas_call x2, Pallas kernels, attend_back(): pl.pallas_call(functools.partial(attend_back_kernel, heads, last), grid=(...  99.1 us
    pallas_call x2, Pallas kernels, attend(): pl.pallas_call(functools.partial(attend_kernel, heads), grid=(count // bl...  55.6 us
    pallas_call x3, Pallas kernels, feed_forward(): pl.pallas_call(feed_kernel, grid=(units // block,), in_specs=[spec, flat,...  49.6 us
    ppermute x33, starting transfers between devices, swap(): lax.ppermute(value, axis, [(place, place ^ step) for place in range(size)])  34.4 us
    all_gather x1, waiting for transfers between devices, local(): lax.all_gather(attend_mine.reshape(rows * shard, 3 * features), 'clip', a...  29 us
    pallas_call x2, Pallas kernels, first_back(): pl.pallas_call(functools.partial(first_back_kernel, half, last), grid=(2...  26.9 us
    pallas_call x1, Pallas kernels, feed_weights(): pl.pallas_call(functools.partial(feed_weight_kernel, len(hidden)), grid=(...  21.7 us
  transfers between devices with their start and end apart: 43, of which 18 were waited for; matrix products, arithmetic and copies ran while one was open for 10% of the time, Pallas kernels for 39%

profile of v4, /device:TPU:0, one launch (start us, length us, event | category | flops | bytes accessed | tf_op | source)
XLA Modules:
  0.0 719.1 jit_solution(2719526514421472719)
XLA Ops:
  23.8 6.7 collective-permute-done.2
  35.2 29.0 %all-gather.3.cloned.1.call-done = bf16[1024,768]{0,1:T(8,128)(2,1)} async-done(((bf16[128,768]{0,1:T(8,128)(2,1)}), bf16[1024,768]{0,1:T(8,128)(2,1)}) %all-gather.3.cloned.1.call-update) | async-done | bytes 1572880 | tf_op jit(solution)/shard_map/all_gather | solution.py:766
  69.3 34.9 %collective-permute-done.one = bf16[784,1024]{1,0:T(8,128)(2,1)} collective-permute-done((bf16[784,1024]{1,0:T(8,128)(2,1)}, bf16[784,1024]{1,0:T(8,128)(2,1)}, u32[]{:S(2)}, u32[]{:S(2)}) %collective-permute-start) | collective-permute-done | bytes 1605664 | tf_op jit(solution)/shard_map/ppermute | solution.py:676
  108.6 17.1 %all-to-all-done = bf16[8,12,1024]{2,1,0:T(8,128)(2,1)S(1)} async-done(((bf16[8,12,1024]{2,1,0:T(8,128)(2,1)}), bf16[8,12,1024]{2,1,0:T(8,128)(2,1)S(1)}, u32[]{:S(2)}, u32[]{:S(2)}) %all-to-all-start) | async-done | bytes 196640 | tf_op jit(solution)/shard_map/all_to_all | solution.py:786
  131.2 21.5 %all-to-all-done.1 = f32[32,12,192]{2,1,0:T(8,128)S(1)} async-done(((f32[32,12,192]{2,1,0:T(8,128)}), f32[32,12,192]{2,1,0:T(8,128)S(1)}, u32[]{:S(2)}, u32[]{:S(2)}) %all-to-all-start.1) | async-done | bytes 294944 | tf_op jit(solution)/shard_map/all_to_all | solution.py:796
  158.3 9.0 %shard_map.488.k1.v1.q_ref = bf16[768,1536]{1,0:T(8,128)(2,1)} custom-call(bf16[784,1024]{1,0:T(8,128)(2,1)} %fusion.2.one, bf16[784,1024]{1,0:T(8,128)(2,1)} %collective-permute-done.6.two, f32[12,6,1024]{2,1,0:T(8,128)} %copy-done.2, bf16[768,1024]{1,0:T(8,128)(2,1)} %bitcast.288, f32[32,3072]{1,0:T(8,128)} %get-tuple-element.235.cosine.cos_all, ...), custom_call_target="tpu_custom_call" | custom-call | flops 2415919104 | bytes 6291456 | tf_op jit(solution)/shard_map/pallas_call | solution.py:120
  171.7 9.1 %shard_map.487.q_ref.k2.v2 = bf16[768,1536]{1,0:T(8,128)(2,1)} custom-call(bf16[784,1024]{1,0:T(8,128)(2,1)} %collective-permute-done.one, bf16[784,1024]{1,0:T(8,128)(2,1)} %collective-permute-done.1.two, f32[12,6,1024]{2,1,0:T(8,128)} %copy-done.2, bf16[768,1024]{1,0:T(8,128)(2,1)} %bitcast.289, f32[32,3072]{1,0:T(8,128)} %get-tuple-element.235.cosine.cos_all, ...), custom_call_target="tpu_custom_call" | custom-call | flops 2415919104 | bytes 6291456 | tf_op jit(solution)/shard_map/pallas_call | solution.py:120
  181.4 27.8 %shard_map.489 = (bf16[256,1536]{1,0:T(8,128)(2,1)}, f32[4,1536]{1,0:T(4,128)}) custom-call(bf16[768,1536]{1,0:T(8,128)(2,1)} %shard_map.487.q_ref.k2.v2, bf16[768,1536]{1,0:T(8,128)(2,1)} %shard_map.488.k1.v1.q_ref, bf16[768,1536]{1,0:T(8,128)(2,1)} %shard_map.487.q_ref.k2.v2, bf16[768,1536]{1,0:T(8,128)(2,1)} %shard_map.488.k1.v1.q_ref, ...), custom_call_target="tpu_custom_call" | custom-call | flops 19327352832 | bytes 3145728 | tf_op jit(solution)/shard_map/pallas_call | solution.py:174
  217.0 27.8 %shard_map.490 = (bf16[256,1536]{1,0:T(8,128)(2,1)}, f32[4,1536]{1,0:T(4,128)}) custom-call(bf16[768,1536]{1,0:T(8,128)(2,1)} %shard_map.488.k1.v1.q_ref, bf16[768,1536]{1,0:T(8,128)(2,1)} %shard_map.488.k1.v1.q_ref, bf16[768,1536]{1,0:T(8,128)(2,1)} %shard_map.487.q_ref.k2.v2, bf16[768,1536]{1,0:T(8,128)(2,1)} %shard_map.488.k1.v1.q_ref, ...), custom_call_target="tpu_custom_call" | custom-call | flops 19327352832 | bytes 3145728 | tf_op jit(solution)/shard_map/pallas_call | solution.py:174
  252.0 17.1 %all-to-all-done.3 = bf16[4,8,32,1024]{3,2,1,0:T(8,128)(2,1)} async-done(((bf16[4,8,32,1024]{3,2,1,0:T(8,128)(2,1)}), bf16[4,8,32,1024]{3,2,1,0:T(8,128)(2,1)}, u32[]{:S(2)}, u32[]{:S(2)}) %all-to-all-start.3) | async-done | bytes 2097184 | tf_op jit(solution)/shard_map/all_to_all | solution.py:819
  277.5 6.5 collective-permute-done.9.a3
  284.7 7.5 %shard_map.491 = (f32[12,64,1024]{2,1,0:T(8,128)}, bf16[768,1024]{1,0:T(8,128)(2,1)}, bf16[768,1024]{1,0:T(8,128)(2,1)}) custom-call(s32[4]{0:T(128)} %iota_xor_fusion.order, bf16[256,1536]{1,0:T(8,128)(2,1)} %get-tuple-element.105.a0.out_ref, bf16[256,768]{1,0:T(8,128)(2,1)} %copy-done.17, bf16[256,768]{1,0:T(8,128)(2,1)} %copy-done.18, ...), custom_call_target="tpu_custom_call" | custom-call | flops 1610612736 | bytes 11010048 | tf_op jit(solution)/shard_map/pallas_call | solution.py:361
  295.8 23.7 %shard_map.492 = (f32[768,1024]{1,0:T(8,128)}, f32[768,1024]{1,0:T(8,128)}, bf16[768,2048]{1,0:T(8,128)(2,1)}, bf16[768,2048]{1,0:T(8,128)(2,1)}) custom-call(bf16[16,2,2,32,2048]{4,3,2,1,0:T(8,128)(2,1)} %bitcast.285, bf16[768,1024]{1,0:T(8,128)(2,1)} %get-tuple-element.108.hidden.refs_0_, bf16[768,1024]{1,0:T(8,128)(2,1)} %get-tuple-element.110.branch.refs_3_), custom_call_target="tpu_custom_call" | custom-call | flops 12884901888 | bytes 14680064 | tf_op jit(solution)/shard_map/pallas_call | solution.py:440
  319.5 11.4 %collective-permute-done.11.hidden.refs_2_ = bf16[384,1024]{1,0:T(8,128)(2,1)S(1)} collective-permute-done((bf16[384,1024]{1,0:T(8,128)(2,1)S(1)}, bf16[384,1024]{1,0:T(8,128)(2,1)S(1)}, u32[]{:S(2)}, u32[]{:S(2)}) %collective-permute-start.11) | collective-permute-done | bytes 786464 | tf_op jit(solution)/shard_map/ppermute | solution.py:676
  330.9 13.1 %shard_map.493 = (bf16[384,1024]{1,0:T(8,128)(2,1)}, bf16[384,1024]{1,0:T(8,128)(2,1)}, bf16[384,2048]{1,0:T(8,128)(2,1)}, bf16[384,2048]{1,0:T(8,128)(2,1)}) custom-call(bf16[16,2,2,32,2048]{4,3,2,1,0:T(8,128)(2,1)} %bitcast.286, bf16[384,1024]{1,0:T(8,128)(2,1)} %copy-done.46, bf16[384,1024]{1,0:T(8,128)(2,1)} %bitcast.266), custom_call_target="tpu_custom_call" | custom-call | flops 6442450944 | bytes 11534336 | tf_op jit(solution)/shard_map/pallas_call | solution.py:440
  345.5 12.8 %shard_map.494 = (bf16[384,1024]{1,0:T(8,128)(2,1)}, bf16[384,1024]{1,0:T(8,128)(2,1)}, bf16[384,2048]{1,0:T(8,128)(2,1)}, bf16[384,2048]{1,0:T(8,128)(2,1)}) custom-call(bf16[16,2,2,32,2048]{4,3,2,1,0:T(8,128)(2,1)} %bitcast.287, bf16[384,1024]{1,0:T(8,128)(2,1)} %copy-done.47, bf16[384,1024]{1,0:T(8,128)(2,1)} %bitcast.264), custom_call_target="tpu_custom_call" | custom-call | flops 6442450944 | bytes 11534336 | tf_op jit(solution)/shard_map/pallas_call | solution.py:440
  358.8 21.7 %shard_map.495 = bf16[16,2,2,32,2048]{4,3,2,1,0:T(8,128)(2,1)} custom-call(bf16[768,1024]{1,0:T(8,128)(2,1)} %get-tuple-element.108.hidden.refs_0_, bf16[384,1024]{1,0:T(8,128)(2,1)} %copy-done.46, bf16[384,1024]{1,0:T(8,128)(2,1)} %copy-done.47, bf16[768,1024]{1,0:T(8,128)(2,1)} %get-tuple-element.110.branch.refs_3_, bf16[384,1024]{1,0:T(8,128)(2,1)} %bitcast.267, ...), custom_call_target="tpu_custom_call" | custom-call | flops 12884901888 | bytes 20971520 | tf_op jit(solution)/shard_map/pallas_call | solution.py:480
  381.8 15.5 %shard_map.496 = (f32[12,64,1024]{2,1,0:T(8,128)}, f32[12,3,1024]{2,1,0:T(4,128)}, bf16[256,768]{1,0:T(8,128)(2,1)}, bf16[256,768]{1,0:T(8,128)(2,1)}, bf16[256,...) custom-call(s32[4]{0:T(128)} %iota_xor_fusion.order, f32[768,1024]{1,0:T(8,128)} %get-tuple-element.113.into, ...), custom_call_target="tpu_custom_call" | custom-call | flops 3221225472 | bytes 18874368 | tf_op jit(solution)/shard_map/pallas_call | solution.py:536
  409.5 48.6 %shard_map.497 = (bf16[256,1536]{1,0:T(8,128)(2,1)}, f32[256,3072]{1,0:T(8,128)}, f32[256,3072]{1,0:T(8,128)}) custom-call(bf16[768,1536]{1,0:T(8,128)(2,1)} %shard_map.488.k1.v1.q_ref, bf16[768,1536]{1,0:T(8,128)(2,1)} %shard_map.488.k1.v1.q_ref, bf16[768,1536]{1,0:T(8,128)(2,1)} %shard_map.487.q_ref.k2.v2, bf16[768,1536]{1,0:T(8,128)(2,1)} %shard_map.488.k1.v1.q_ref, ...), custom_call_target="tpu_custom_call" | custom-call | flops 41070624768 | bytes 6291456 | tf_op jit(solution)/shard_map/pallas_call | solution.py:320
  458.1 15.7 %all-to-all-done.4 = bf16[4,8,32,1024]{3,2,1,0:T(8,128)(2,1)} async-done(((bf16[4,8,32,1024]{3,2,1,0:T(8,128)(2,1)}), bf16[4,8,32,1024]{3,2,1,0:T(8,128)(2,1)}, u32[]{:S(2)}, u32[]{:S(2)}) %all-to-all-start.4) | async-done | bytes 2097184 | tf_op jit(solution)/shard_map/all_to_all | solution.py:871
  476.8 5.9 all-to-all-start.5
  482.7 50.6 %shard_map.499 = (bf16[256,1536]{1,0:T(8,128)(2,1)}, bf16[256,3072]{1,0:T(8,128)(2,1)}, bf16[256,3072]{1,0:T(8,128)(2,1)}) custom-call(bf16[768,1536]{1,0:T(8,128)(2,1)} %shard_map.487.q_ref.k2.v2, bf16[768,1536]{1,0:T(8,128)(2,1)} %shard_map.488.k1.v1.q_ref, bf16[768,1536]{1,0:T(8,128)(2,1)} %shard_map.487.q_ref.k2.v2, ...), custom_call_target="tpu_custom_call" | custom-call | flops 41070624768 | bytes 6291456 | tf_op jit(solution)/shard_map/pallas_call | solution.py:320
  535.9 6.2 shard_map.498
  542.1 12.5 %shard_map.500 = (bf16[2,768,1024]{2,1,0:T(8,128)(2,1)}, f32[768,1024]{1,0:T(8,128)}, f32[12,2,1024]{2,1,0:T(2,128)}) custom-call(bf16[784,1024]{1,0:T(8,128)(2,1)} %collective-permute-done.one, bf16[784,1024]{1,0:T(8,128)(2,1)} %collective-permute-done.1.two, f32[12,6,1024]{2,1,0:T(8,128)} %copy-done.2, bf16[256,1536]{1,0:T(8,128)(2,1)} %get-tuple-element.147.dq, ...), custom_call_target="tpu_custom_call" | custom-call | flops 4831838208 | bytes 9437184 | tf_op jit(solution)/shard_map/pallas_call | solution.py:640
  554.7 14.4 %shard_map.501 = (bf16[2,768,1024]{2,1,0:T(8,128)(2,1)}, bf16[1024,768]{1,0:T(8,128)(2,1)}, f32[12,2,1024]{2,1,0:T(2,128)}) custom-call(bf16[784,1024]{1,0:T(8,128)(2,1)} %fusion.2.one, bf16[784,1024]{1,0:T(8,128)(2,1)} %collective-permute-done.6.two, f32[12,6,1024]{2,1,0:T(8,128)} %copy-done.2, bf16[256,1536]{1,0:T(8,128)(2,1)} %get-tuple-element.153.dq, ...), custom_call_target="tpu_custom_call" | custom-call | flops 4831838208 | bytes 9437184 | tf_op jit(solution)/shard_map/pallas_call | solution.py:640
  578.4 5.2 all-to-all-start.6
  598.3 12.3 %collective-permute-done.23 = f32[12,192]{1,0:T(8,128)S(1)} collective-permute-done((f32[12,192]{1,0:T(8,128)S(1)}, f32[12,192]{1,0:T(8,128)S(1)}, u32[]{:S(2)}, u32[]{:S(2)}) %collective-permute-start.23) | collective-permute-done | bytes 9248 | tf_op jit(solution)/shard_map/ppermute | solution.py:676
  610.7 5.3 collective-permute-start.26
  616.4 6.7 collective-permute-done.25
  650.0 22.8 %collective-permute-done.32.three = bf16[768,1024]{1,0:T(8,128)(2,1)} collective-permute-done((bf16[768,1024]{1,0:T(8,128)(2,1)}, bf16[768,1024]{1,0:T(8,128)(2,1)}, u32[]{:S(2)}, u32[]{:S(2)}) %collective-permute-start.32) | collective-permute-done | bytes 1572896 | tf_op jit(solution)/shard_map/ppermute | solution.py:676
  672.8 7.2 %shard_map.502 = f32[12,64,1024]{2,1,0:T(8,128)} custom-call(bf16[12,64,1024]{2,1,0:T(8,128)(2,1)} %bitcast.221, f32[12,6,1024]{2,1,0:T(8,128)} %copy-done.2, f32[12,64,1024]{2,1,0:T(8,128)} %get-tuple-element.162.middle_grad, bf16[768,1024]{1,0:T(8,128)(2,1)} %get-tuple-element.205.one, bf16[768,1024]{1,0:T(8,128)(2,1)} %collective-permute-done.30.two, ...), custom_call_target="tpu_custom_call" | custom-call | flops 15728640 | bytes 12582912 | tf_op jit(solution)/shard_map/pallas_call | solution.py:664
  687.5 11.6 %all_to_all.40 = f32[32,8,128]{2,1,0:T(8,128)S(1)} all-to-all(f32[32,8,128]{2,1,0:T(8,128)S(1)} %broadcast_in_dim.49), channel_id=1, replica_groups=mesh['clip'=8,'x'=2,'core'=2] {'clip','x','core'}, dimensions={0} | all-to-all | bytes 262144 | tf_op jit(solution)/shard_map/all_to_all | solution.py:935
  (350 shorter events, 160.0 us)
Async XLA Ops:
  7.2 57.0 %all-gather.3.cloned.1.call-start = ((), (), s32[]{:S(2)}) async-start(), calls=%async_computation.9 | async-start | bytes 1769472 | tf_op jit(solution)/shard_map/all_gather | solution.py:766
  17.7 278.1 %all-gather.5.cloned.1.call-start = ((), (), s32[]{:S(2)}) async-start(), calls=%async_computation.10 | async-start | bytes 8912896 | tf_op jit(solution)/shard_map/all_gather | solution.py:776
  67.8 36.4 %collective-permute-start = (bf16[784,1024]{1,0:T(8,128)(2,1)}, bf16[784,1024]{1,0:T(8,128)(2,1)}, u32[]{:S(2)}, u32[]{:S(2)}) collective-permute-start(bf16[784,1024]{1,0:T(8,128)(2,1)} %fusion.2.one), channel_id=1, source_target_pairs={{0,2},{1,3},{2,0},{3,1},{4,6},{5,7},{6,4},{7,5},{8,10},{9,11},{10,... | collective-permute-start | bytes 4816904 | tf_op jit(solution)/shard_map/ppermute | solution.py:676
  69.3 85.4 %collective-permute-start.6 = (bf16[784,1024]{1,0:T(8,128)(2,1)}, bf16[784,1024]{1,0:T(8,128)(2,1)}, u32[]{:S(2)}, u32[]{:S(2)}) collective-permute-start(bf16[784,1024]{1,0:T(8,128)(2,1)} %fusion.2.one), channel_id=1, source_target_pairs={{0,1},{1,0},{2,3},{3,2},{4,5},{5,4},{6,7},{7,6},{8,9},{9,8},{10,11... | collective-permute-start | bytes 4816904 | tf_op jit(solution)/shard_map/ppermute | solution.py:676
  104.1 51.2 %collective-permute-start.1 = (bf16[784,1024]{1,0:T(8,128)(2,1)}, bf16[784,1024]{1,0:T(8,128)(2,1)}, u32[]{:S(2)}, u32[]{:S(2)}) collective-permute-start(bf16[784,1024]{1,0:T(8,128)(2,1)} %collective-permute-done.one), channel_id=1, source_target_pairs={{0,1},{1,0},{2,3},{3,2},{4,5},{5,4},{6,7},{7,6},{8,9},{9,8},{10,11... | collective-permute-start | bytes 4816904 | tf_op jit(solution)/shard_map/ppermute | solution.py:676
  104.9 20.8 %all-to-all-start = ((bf16[8,12,1024]{2,1,0:T(8,128)(2,1)}), bf16[8,12,1024]{2,1,0:T(8,128)(2,1)S(1)}, u32[]{:S(2)}, u32[]{:S(2)}) async-start(bf16[8,12,1024]{2,1,0:T(8,128)(2,1)} %broadcast_in_dim.42), calls=%async_computation | async-start | bytes 524288 | tf_op jit(solution)/shard_map/all_to_all | solution.py:786
  126.9 25.7 %all-to-all-start.1 = ((f32[32,12,192]{2,1,0:T(8,128)}), f32[32,12,192]{2,1,0:T(8,128)S(1)}, u32[]{:S(2)}, u32[]{:S(2)}) async-start(f32[32,12,192]{2,1,0:T(8,128)} %bitcast.3), calls=%async_computation.1 | async-start | bytes 1048576 | tf_op jit(solution)/shard_map/all_to_all | solution.py:796
  168.2 42.6 %all-to-all-start.2 = ((bf16[8,32,1024]{2,1,0:T(8,128)(2,1)}), bf16[8,32,1024]{2,1,0:T(8,128)(2,1)S(1)}, u32[]{:S(2)}, u32[]{:S(2)}) async-start(bf16[8,32,1024]{2,1,0:T(8,128)(2,1)} %broadcast_in_dim.47), calls=%async_computation.2 | async-start | bytes 1048576 | tf_op jit(solution)/shard_map/all_to_all | solution.py:816
  209.3 39.6 %collective-permute-start.12 = (bf16[12,64,1024]{2,1,0:T(8,128)(2,1)S(1)}, bf16[12,64,1024]{2,1,0:T(8,128)(2,1)}, u32[]{:S(2)}, u32[]{:S(2)}) collective-permute-start(bf16[12,64,1024]{2,1,0:T(8,128)(2,1)S(1)} %bitcast.228), channel_id=1, source_target_pairs={{0,2},{2,0},{1,3},{3,1},{4,6},{6,4},{5,7},{7,5},{8,10},{10,8},{9,1... | collective-permute-start | bytes 4718600 | tf_op jit(solution)/shard_map/ppermute | solution.py:676
  212.4 56.8 %all-to-all-start.3 = ((bf16[4,8,32,1024]{3,2,1,0:T(8,128)(2,1)}), bf16[4,8,32,1024]{3,2,1,0:T(8,128)(2,1)}, u32[]{:S(2)}, u32[]{:S(2)}) async-start(bf16[4,8,32,1024]{3,2,1,0:T(8,128)(2,1)} %broadcast_in_dim.48), calls=%async_computation.3 | async-start | bytes 4194304 | tf_op jit(solution)/shard_map/all_to_all | solution.py:819
  245.9 26.5 %collective-permute-start.7 = (bf16[256,768]{1,0:T(8,128)(2,1)S(1)}, bf16[256,768]{1,0:T(8,128)(2,1)S(1)}, u32[]{:S(2)}, u32[]{:S(2)}) collective-permute-start(bf16[256,768]{1,0:T(8,128)(2,1)S(1)} %slice.290), channel_id=1, source_target_pairs={{0,1},{1,0},{2,3},{3,2},{4,5},{5,4},{6,7},{7,6},{8,9},{9,8},{10,11... | collective-permute-start | bytes 1179656 | tf_op jit(solution)/shard_map/ppermute | solution.py:676
  247.2 30.3 %collective-permute-start.8 = (bf16[256,768]{1,0:T(8,128)(2,1)}, bf16[256,768]{1,0:T(8,128)(2,1)S(1)}, u32[]{:S(2)}, u32[]{:S(2)}) collective-permute-start(bf16[256,768]{1,0:T(8,128)(2,1)} %get-tuple-element.213), channel_id=1, source_target_pairs={{0,2},{1,3},{2,0},{3,1},{4,6},{5,7},{6,4},{7,5},{8,10},{9,11},{10,... | collective-permute-start | bytes 1179656 | tf_op jit(solution)/shard_map/ppermute | solution.py:676
  248.9 35.1 %collective-permute-start.9 = (bf16[256,768]{1,0:T(8,128)(2,1)S(1)}, bf16[256,768]{1,0:T(8,128)(2,1)S(1)}, u32[]{:S(2)}, u32[]{:S(2)}) collective-permute-start(bf16[256,768]{1,0:T(8,128)(2,1)S(1)} %get-tuple-element.212), channel_id=1, source_target_pairs={{0,3},{1,2},{2,1},{3,0},{4,7},{5,6},{6,5},{7,4},{8,11},{9,10},{10,... | collective-permute-start | bytes 1179656 | tf_op jit(solution)/shard_map/ppermute | solution.py:676
  293.7 25.8 %collective-permute-start.10 = (bf16[384,1024]{1,0:T(8,128)(2,1)S(1)}, bf16[384,1024]{1,0:T(8,128)(2,1)S(1)}, u32[]{:S(2)}, u32[]{:S(2)}) collective-permute-start(bf16[384,1024]{1,0:T(8,128)(2,1)S(1)} %get-tuple-element.209), channel_id=1, source_target_pairs={{0,2},{2,0},{1,3},{3,1},{4,6},{6,4},{5,7},{7,5},{8,10},{10,8},{9,1... | collective-permute-start | bytes 2359304 | tf_op jit(solution)/shard_map/ppermute | solution.py:676
  295.4 35.5 %collective-permute-start.11 = (bf16[384,1024]{1,0:T(8,128)(2,1)S(1)}, bf16[384,1024]{1,0:T(8,128)(2,1)S(1)}, u32[]{:S(2)}, u32[]{:S(2)}) collective-permute-start(bf16[384,1024]{1,0:T(8,128)(2,1)S(1)} %get-tuple-element.208), channel_id=1, source_target_pairs={{0,2},{2,0},{1,3},{3,1},{4,6},{6,4},{5,7},{7,5},{8,10},{10,8},{9,1... | collective-permute-start | bytes 2359304 | tf_op jit(solution)/shard_map/ppermute | solution.py:676
  344.0 36.5 %collective-permute-start.13 = (bf16[384,1024]{1,0:T(8,128)(2,1)}, bf16[384,1024]{1,0:T(8,128)(2,1)S(1)}, u32[]{:S(2)}, u32[]{:S(2)}) collective-permute-start(bf16[384,1024]{1,0:T(8,128)(2,1)} %get-tuple-element.125), channel_id=1, source_target_pairs={{0,2},{2,0},{1,3},{3,1},{4,6},{6,4},{5,7},{7,5},{8,10},{10,8},{9,1... | collective-permute-start | bytes 2359304 | tf_op jit(solution)/shard_map/ppermute | solution.py:676
  358.3 22.2 %collective-permute-start.14 = (bf16[384,1024]{1,0:T(8,128)(2,1)}, bf16[384,1024]{1,0:T(8,128)(2,1)S(1)}, u32[]{:S(2)}, u32[]{:S(2)}) collective-permute-start(bf16[384,1024]{1,0:T(8,128)(2,1)} %get-tuple-element.126), channel_id=1, source_target_pairs={{0,2},{2,0},{1,3},{3,1},{4,6},{6,4},{5,7},{7,5},{8,10},{10,8},{9,1... | collective-permute-start | bytes 2359304 | tf_op jit(solution)/shard_map/ppermute | solution.py:676
  397.4 60.6 %collective-permute-start.18 = (bf16[384,1024]{1,0:T(8,128)(2,1)}, bf16[384,1024]{1,0:T(8,128)(2,1)S(1)}, u32[]{:S(2)}, u32[]{:S(2)}) collective-permute-start(bf16[384,1024]{1,0:T(8,128)(2,1)} %get-tuple-element.137), channel_id=1, source_target_pairs={{0,2},{2,0},{1,3},{3,1},{4,6},{6,4},{5,7},{7,5},{8,10},{10,8},{9,1... | collective-permute-start | bytes 2359304 | tf_op jit(solution)/shard_map/ppermute | solution.py:676
  399.1 59.0 %collective-permute-start.19 = (bf16[384,1024]{1,0:T(8,128)(2,1)}, bf16[384,1024]{1,0:T(8,128)(2,1)}, u32[]{:S(2)}, u32[]{:S(2)}) collective-permute-start(bf16[384,1024]{1,0:T(8,128)(2,1)} %get-tuple-element.138), channel_id=1, source_target_pairs={{0,2},{2,0},{1,3},{3,1},{4,6},{6,4},{5,7},{7,5},{8,10},{10,8},{9,1... | collective-permute-start | bytes 2359304 | tf_op jit(solution)/shard_map/ppermute | solution.py:676
  399.5 58.6 %collective-permute-start.16 = (bf16[256,768]{1,0:T(8,128)(2,1)}, bf16[256,768]{1,0:T(8,128)(2,1)}, u32[]{:S(2)}, u32[]{:S(2)}) collective-permute-start(bf16[256,768]{1,0:T(8,128)(2,1)} %get-tuple-element.134), channel_id=1, source_target_pairs={{0,2},{1,3},{2,0},{3,1},{4,6},{5,7},{6,4},{7,5},{8,10},{9,11},{10,... | collective-permute-start | bytes 1179656 | tf_op jit(solution)/shard_map/ppermute | solution.py:676
  401.1 57.0 %collective-permute-start.17 = (bf16[256,768]{1,0:T(8,128)(2,1)}, bf16[256,768]{1,0:T(8,128)(2,1)}, u32[]{:S(2)}, u32[]{:S(2)}) collective-permute-start(bf16[256,768]{1,0:T(8,128)(2,1)} %get-tuple-element.135), channel_id=1, source_target_pairs={{0,3},{1,2},{2,1},{3,0},{4,7},{5,6},{6,5},{7,4},{8,11},{9,10},{10,... | collective-permute-start | bytes 1179656 | tf_op jit(solution)/shard_map/ppermute | solution.py:676
  404.3 69.6 %all-to-all-start.4 = ((bf16[4,8,32,1024]{3,2,1,0:T(8,128)(2,1)}), bf16[4,8,32,1024]{3,2,1,0:T(8,128)(2,1)}, u32[]{:S(2)}, u32[]{:S(2)}) async-start(bf16[4,8,32,1024]{3,2,1,0:T(8,128)(2,1)} %bitcast.206), calls=%async_computation.4 | async-start | bytes 4194304 | tf_op jit(solution)/shard_map/all_to_all | solution.py:871
  408.8 227.7 %reduce-scatter.2.cloned.1.call-start = ((), (), s32[]{:S(2)}) async-start(), calls=%async_computation.11 | async-start | bytes 8912896 | tf_op jit(solution)/shard_map/reduce_scatter | solution.py:857
  476.8 77.8 %all-to-all-start.5 = ((bf16[8,32,1024]{2,1,0:T(8,128)(2,1)}), bf16[8,32,1024]{2,1,0:T(8,128)(2,1)S(1)}, u32[]{:S(2)}, u32[]{:S(2)}) async-start(bf16[8,32,1024]{2,1,0:T(8,128)(2,1)} %reduce_sum.102), calls=%async_computation.5 | async-start | bytes 1048576 | tf_op jit(solution)/shard_map/all_to_all | solution.py:884
  578.4 63.1 %all-to-all-start.6 = ((bf16[32,32,768]{2,1,0:T(8,128)(2,1)}), bf16[32,32,768]{2,1,0:T(8,128)(2,1)S(1)}, u32[]{:S(2)}, u32[]{:S(2)}) async-start(bf16[32,32,768]{2,1,0:T(8,128)(2,1)} %bitcast.253), calls=%async_computation.6 | async-start | bytes 3145728 | tf_op jit(solution)/shard_map/all_to_all | solution.py:898
  587.6 62.4 %collective-permute-start.30 = (bf16[768,1024]{1,0:T(8,128)(2,1)}, bf16[768,1024]{1,0:T(8,128)(2,1)}, u32[]{:S(2)}, u32[]{:S(2)}) collective-permute-start(bf16[768,1024]{1,0:T(8,128)(2,1)} %get-tuple-element.204), channel_id=1, source_target_pairs={{0,1},{1,0},{2,3},{3,2},{4,5},{5,4},{6,7},{7,6},{8,9},{9,8},{10,11... | collective-permute-start | bytes 4718600 | tf_op jit(solution)/shard_map/ppermute | solution.py:676
  589.3 42.3 %collective-permute-start.31 = (bf16[768,1024]{1,0:T(8,128)(2,1)}, bf16[768,1024]{1,0:T(8,128)(2,1)}, u32[]{:S(2)}, u32[]{:S(2)}) collective-permute-start(bf16[768,1024]{1,0:T(8,128)(2,1)} %slice_bitcast_fusion), channel_id=1, source_target_pairs={{0,1},{1,0},{2,3},{3,2},{4,5},{5,4},{6,7},{7,6},{8,9},{9,8},{10,11... | collective-permute-start | bytes 4718600 | tf_op jit(solution)/shard_map/ppermute | solution.py:676
  593.5 17.1 %collective-permute-start.23 = (f32[12,192]{1,0:T(8,128)S(1)}, f32[12,192]{1,0:T(8,128)S(1)}, u32[]{:S(2)}, u32[]{:S(2)}) collective-permute-start(f32[12,192]{1,0:T(8,128)S(1)} %squeeze.66), channel_id=1, source_target_pairs={{0,8},{4,12},{8,0},{12,4},{16,24},{20,28},{24,16},{28,20},{1,9},{5... | collective-permute-start | bytes 27656 | tf_op jit(solution)/shard_map/ppermute | solution.py:676
  595.1 20.9 %collective-permute-start.24 = (f32[12,192]{1,0:T(8,128)S(1)}, f32[12,192]{1,0:T(8,128)S(1)}, u32[]{:S(2)}, u32[]{:S(2)}) collective-permute-start(f32[12,192]{1,0:T(8,128)S(1)} %squeeze.67), channel_id=1, source_target_pairs={{0,12},{4,8},{8,4},{12,0},{16,28},{20,24},{24,20},{28,16},{1,13},{... | collective-permute-start | bytes 27656 | tf_op jit(solution)/shard_map/ppermute | solution.py:676
  596.1 27.0 %collective-permute-start.25 = (f32[12,192]{1,0:T(8,128)S(1)}, f32[12,192]{1,0:T(8,128)S(1)}, u32[]{:S(2)}, u32[]{:S(2)}) collective-permute-start(f32[12,192]{1,0:T(8,128)S(1)} %squeeze.68), channel_id=1, source_target_pairs={{0,16},{4,20},{8,24},{12,28},{16,0},{20,4},{24,8},{28,12},{1,17},{... | collective-permute-start | bytes 27656 | tf_op jit(solution)/shard_map/ppermute | solution.py:676
  635.3 37.6 %collective-permute-start.32 = (bf16[768,1024]{1,0:T(8,128)(2,1)}, bf16[768,1024]{1,0:T(8,128)(2,1)}, u32[]{:S(2)}, u32[]{:S(2)}) collective-permute-start(bf16[768,1024]{1,0:T(8,128)(2,1)} %fusion.1), channel_id=1, source_target_pairs={{0,2},{1,3},{2,0},{3,1},{4,6},{5,7},{6,4},{7,5},{8,10},{9,11},{10,... | collective-permute-start | bytes 4718600 | tf_op jit(solution)/shard_map/ppermute | solution.py:676
  639.5 41.0 %collective-permute-start.29 = (bf16[2,32,2048]{2,1,0:T(8,128)(2,1)}, bf16[2,32,2048]{2,1,0:T(8,128)(2,1)S(1)}, u32[]{:S(2)}, u32[]{:S(2)}) collective-permute-start(bf16[2,32,2048]{2,1,0:T(8,128)(2,1)} %get-tuple-element.217), channel_id=1, source_target_pairs={{0,2},{2,0},{1,3},{3,1},{4,6},{6,4},{5,7},{7,5},{8,10},{10,8},{9,1... | collective-permute-start | bytes 786440 | tf_op jit(solution)/shard_map/ppermute | solution.py:676
  (59 other events, 581.8 us)
Sparse Core Ops, SparseCore 0:
  17.8 46.3 all-gather.2
  67.0 85.7 all-gather.4
  413.7 111.5 reduce-scatter.1

commit v5 on v4

--- a/solution.py
+++ b/solution.py
@@ -110,13 +110,13 @@
     ]
 
 
-def project_qkv(one, two, mod, weight, cosine, sine, offset):
-    total, width = cosine.shape[1] // 2, weight.shape[1]
+def project_qkv(one, two, mod, weight, cosine, sine):
+    total, width = cosine.shape[1], weight.shape[1]
     frames, chunk = mod.shape[0], 4
     block = total // 2 // frames * chunk
     half, specs = token_specs(frames, block, width, chunk)
     rows = weight.shape[0]
-    angle = pl.BlockSpec((cosine.shape[0], block), lambda i: (0, i + offset * 2 * half))
+    angle = pl.BlockSpec((cosine.shape[0], block), lambda i: (0, i))
     return pl.pallas_call(
         functools.partial(qkv_kernel, half),
         grid=(2 * half,),
@@ -522,10 +522,18 @@
 
     @pl.when(step == pl.num_programs(0) - 1)
     def _():
-        proj_raw[...] = jnp.transpose(raw_sum[...]).astype(bf16)
-
-
-def middle_back(order, into, into_far, tokens, cotangent, att_out, mod, parts, proj):
+        turned = jnp.transpose(raw_sum[...])
+        groups, owners, rows, _ = proj_raw.shape
+        for group in range(groups):
+            some = [
+                turned[(owner * groups + group) * rows : (owner * groups + group + 1) * rows]
+                for owner in range(owners)
+            ]
+            some = jnp.concatenate(some, axis=0).astype(bf16)
+            proj_raw[group] = some.reshape(proj_raw.shape[1:])
+
+
+def middle_back(order, into, into_far, tokens, cotangent, att_out, mod, parts, proj, owners):
     frames, per_frame, width = tokens.shape
     chunk = 4
     block = chunk * per_frame
@@ -548,7 +556,7 @@
             jax.ShapeDtypeStruct((frames, 3, width), f32),
         ]
         + [jax.ShapeDtypeStruct((features, frames * per_frame), bf16)] * 4
-        + [jax.ShapeDtypeStruct((width, width), bf16)],
+        + [jax.ShapeDtypeStruct(owners + (width // (owners[0] * owners[1]), width), bf16)],
         scratch_shapes=[VMEM((width, width), f32)],
         compiler_params=params(),
         cost_estimate=cost(4 * frames * per_frame * width * width, 24 * frames * per_frame * width),
@@ -767,11 +775,26 @@
         attend_mine.reshape(rows * shard, 3 * features), "clip", axis=0, tiled=True
     )
 
+    cond_act = jax.nn.silu(condition[0].astype(f32)).astype(bf16)
+    cond_act, tok0 = lax.optimization_barrier((cond_act, tok0))
+    cond_all = lax.all_to_all(
+        jnp.broadcast_to(cond_act[None], (clips, frames, width)), "clip", 0, 0, tiled=True
+    ).reshape(clips * frames, width)
+    mod_mine = dot(cond_all, adaptive_weight.astype(bf16)) + adaptive_offsets.astype(bf16).astype(
+        f32
+    )
+    part = mod_mine.shape[1]
+    mod_mine = jnp.broadcast_to(
+        mod_mine.reshape(clips, 1, frames, part), (clips, rows, frames, part)
+    )
+    mod = lax.all_to_all(mod_mine.reshape(devices, frames, part), both, 0, 0, tiled=True)
+    mod = mod.transpose(1, 0, 2).reshape(frames, 6, width)
+
     units = widen_weight.shape[1]
     feed_mine = jnp.stack([widen_weight.astype(bf16), narrow_weight.T.astype(bf16)])
     feed_mine = feed_mine.reshape(2, shard, 2, units // 2).transpose(2, 0, 1, 3)
     feed_mine = relative(trade(relative(feed_mine, far), "x", 2), far)
-    feed_mine, attend_full = lax.optimization_barrier((feed_mine, attend_full))
+    feed_mine, attend_full, mod = lax.optimization_barrier((feed_mine, attend_full, mod))
     attend_turned = attend_full.T
     feed_full = lax.all_gather(
         feed_mine.reshape(4 * shard, units // 2), ("clip", "core"), axis=0, tiled=True
@@ -782,51 +805,49 @@
         feed_full = feed_full.reshape(clips, 2, 2, 2, shard, units // 2).transpose(3, 0, 2, 1, 4, 5)
         feed_full = feed_full.reshape(1, 1, 2, width, units // 2)
 
-    cond_act = jax.nn.silu(condition[0].astype(f32)).astype(bf16)
-    cond_all = lax.all_to_all(
-        jnp.broadcast_to(cond_act[None], (clips, frames, width)), "clip", 0, 0, tiled=True
-    ).reshape(clips * frames, width)
-    mod_mine = dot(cond_all, adaptive_weight.astype(bf16)) + adaptive_offsets.astype(bf16).astype(
-        f32
-    )
-    part = mod_mine.shape[1]
-    mod_mine = jnp.broadcast_to(
-        mod_mine.reshape(clips, 1, frames, part), (clips, rows, frames, part)
-    )
-    mod = lax.all_to_all(mod_mine.reshape(devices, frames, part), both, 0, 0, tiled=True)
-    mod = mod.transpose(1, 0, 2).reshape(frames, 6, width)
-
-    small = jnp.concatenate(
-        [
+    quarter = HEAD_DIM // 4
+    freqs = jnp.exp(-math.log(10000.0) * jnp.arange(quarter, dtype=f32) / quarter)[:, None]
+
+    def places_of(pieces):
+        small = [
             piece[count : count + 3 * spare].reshape(3, spare * width)[:, :count]
-            for piece in (tok0, tok1, tok2, tok3)
-        ],
-        axis=1,
-    ).astype(f32)
-    bias = jnp.where(small[2:3] > 0.5, 0.0, MASKED)
-    quarter = HEAD_DIM // 4
-    freqs = jnp.exp(-math.log(10000.0) * jnp.arange(quarter, dtype=f32) / quarter)
-    angles = jnp.concatenate([freqs[:, None] * small[0:1], freqs[:, None] * small[1:2]], axis=0)
-    cosine, sine = jnp.cos(angles), jnp.sin(angles)
-
-    qkv_near = project_qkv(tok0, tok1, mod, attend_turned, cosine, sine, 0)
-    qkv_far = project_qkv(tok2, tok3, mod, attend_turned, cosine, sine, 1)
-
-    project_mine, qkv_near = lax.optimization_barrier((project_weight.T.astype(bf16), qkv_near))
+            for piece in pieces
+        ]
+        small = jnp.concatenate(small, axis=1).astype(f32)
+        angles = jnp.concatenate([freqs * small[0:1], freqs * small[1:2]], axis=0)
+        return jnp.cos(angles), jnp.sin(angles), jnp.where(small[2:3] > 0.5, 0.0, MASKED)
+
+    cos_near, sin_near, bias_near = places_of((tok0, tok1))
+    cos_far, sin_far, bias_far = places_of((tok2, tok3))
+    near = 2 * count
+
+    qkv_near = project_qkv(tok0, tok1, mod, attend_turned, cos_near, sin_near)
+    qkv_far = project_qkv(tok2, tok3, mod, attend_turned, cos_far, sin_far)
+    cosine = jnp.concatenate([cos_near, cos_far], axis=1)
+    sine = jnp.concatenate([sin_near, sin_far], axis=1)
+    bias = jnp.concatenate([bias_near, bias_far], axis=1)
+
     project_full = lax.all_to_all(
-        jnp.broadcast_to(project_mine[None], (clips, shard, width)), "clip", 0, 0, tiled=True
-    )
+        jnp.broadcast_to(project_weight.T.astype(bf16)[None], (clips, shard, width)),
+        "clip",
+        0,
+        0,
+        tiled=True,
+    )
+    project_full, qkv_far = lax.optimization_barrier((project_full, qkv_far))
     project_full = lax.all_to_all(
         jnp.broadcast_to(project_full[None], (rows, clips, shard, width)), ROW, 0, 0, tiled=True
     )
+
+    cot_far, mod = lax.optimization_barrier((upstream, mod))
+    cot_far = swap(cot_far, "x", 2, 1)
+    out_far, lse_far = attend(qkv_far, qkv_near, qkv_far, bias)
+    out_far, qkv_near, project_full, cot_far = lax.optimization_barrier(
+        (out_far, qkv_near, project_full, cot_far)
+    )
     project_full = project_full.transpose(1, 0, 2, 3).reshape(width, width)
-
-    cot_far, qkv_near = lax.optimization_barrier((upstream, qkv_near))
-    cot_far = swap(cot_far, "x", 2, 1)
     branch_far = (mod[:, 5:6, :] * cot_far.astype(f32)).astype(bf16).reshape(count, width)
 
-    out_far, lse_far = attend(qkv_far, qkv_near, qkv_far, bias)
-    out_far, qkv_near = lax.optimization_barrier((out_far, qkv_near))
     part2 = swap(out_far[:, :count], ROW, rows, 2)
     part3 = swap(out_far[:, count:], ROW, rows, 3)
     out_near, lse_near = attend(qkv_near, qkv_near, qkv_far, bias)
@@ -842,8 +863,6 @@
     hid2, act1 = lax.optimization_barrier((hid2, act1))
     out2, in2, act2, wide2 = feed_forward(feed_full, hid2, branch_far[half:], bf16)
     in2 = swap(in2, "x", 2, 1)
-    out1 = swap(out1, "x", 2, 1)
-    out2 = swap(out2, "x", 2, 1)
     feed_raw = feed_weights(
         feed_full.shape,
         (hidden_two, hid1, hid2),
@@ -860,14 +879,10 @@
         scatter_dimension=0,
         tiled=True,
     ).reshape(2, 2, shard, units // 2)
-    feed_sum = relative(trade(relative(feed_sum, far), "x", 2), far).astype(f32)
-    widen_sum, narrow_sum = feed_sum.transpose(1, 2, 0, 3).reshape(2, shard, units)
-    narrow_sum = narrow_sum.T
     middle_grad, mod_late, d0, d1, d2, d3, project_raw = middle_back(
-        order, in_own, jnp.concatenate([in1, in2], axis=0), own, upstream, att_out, mod, parts, project_full
-    )
-
-    project_raw = project_raw.reshape(clips, rows, shard, width).transpose(1, 0, 2, 3)
+        order, in_own, jnp.concatenate([in1, in2], axis=0), own, upstream, att_out, mod, parts, project_full, (rows, clips)
+    )
+
     project_raw = lax.all_to_all(project_raw, ROW, 0, 0, tiled=True)
 
     turning = (cosine, sine)
@@ -882,44 +897,55 @@
     )
     project_raw = jnp.sum(project_raw.astype(f32), axis=0).astype(bf16)
     project_raw = lax.all_to_all(project_raw, "clip", 0, 0, tiled=True)
+    out1 = swap(out1, "x", 2, 1)
+    out2 = swap(out2, "x", 2, 1)
+    dq_far, dk, dv = attend_back(
+        qkv_far, qkv_near, qkv_far, bias, out_far, (d2, d3), lse_far, turning, 1, (dk, dv)
+    )
+    dq_far, project_raw, out1, out2 = lax.optimization_barrier((dq_far, project_raw, out1, out2))
+    project_sum = jnp.sum(project_raw.astype(f32), axis=0).T
     block_out, mod_gate = block_output(
         out_own, jnp.concatenate([out1, out2], axis=0), own, upstream, att_out, mod
     )
-    dq_far, dk, dv = attend_back(
-        qkv_far, qkv_near, qkv_far, bias, out_far, (d2, d3), lse_far, turning, 1, (dk, dv)
-    )
     back_far, raw, mod_early = first_back(tok2, tok3, mod, dq_far, dk, dv, attend_turned, 1)
-    back_far, dq_near, project_raw = lax.optimization_barrier((back_far, dq_near, project_raw))
-    project_sum = jnp.sum(project_raw.astype(f32), axis=0).T
+    back_far = (
+        back_far[0].astype(f32) + swap(back_far[1], ROW, rows, 1).astype(f32)
+    ).astype(bf16)
+    back_far, dq_near, feed_sum = lax.optimization_barrier((back_far, dq_near, feed_sum))
+    back_far = swap(back_far, ROW, rows, 2)
+    feed_sum = relative(trade(relative(feed_sum, far), "x", 2), far).astype(f32)
+    widen_sum, narrow_sum = feed_sum.transpose(1, 2, 0, 3).reshape(2, shard, units)
+    narrow_sum = narrow_sum.T
+    extra = -(-2 * frames * part // (3 * features))
     back_near, attend_raw, mod_early = first_back(
         tok0, tok1, mod, dq_near, dk, dv, attend_turned, 0, (raw, mod_early)
     )
-
-    attend_raw = lax.all_to_all(
-        attend_raw.reshape(devices, shard, 3 * features), both, 0, 0, tiled=True
-    )
-    attend_sum = jnp.sum(attend_raw.reshape(clips, rows, shard, 3, features).astype(f32), axis=0)
+    back_near = (back_near[0], swap(back_near[1], ROW, rows, 1), back_far)
+
+    mod_grad = jnp.concatenate([mod_early, mod_late, mod_gate], axis=1)
+    mod_grad = mod_grad.reshape(frames, devices, part).transpose(1, 0, 2).reshape(devices, -1)
+    mod_high = mod_grad.astype(bf16)
+    mod_low = (mod_grad - mod_high.astype(f32)).astype(bf16)
+    small = jnp.concatenate([mod_high, mod_low], axis=1)
+    small = jnp.pad(small, ((0, 0), (0, extra * 3 * features - small.shape[1])))
+    attend_raw = jnp.concatenate(
+        [
+            attend_raw.reshape(devices, shard, 3 * features),
+            small.reshape(devices, extra, 3 * features),
+        ],
+        axis=1,
+    )
+    attend_raw = lax.all_to_all(attend_raw, both, 0, 0, tiled=True)
+    input_gradient = input_back(own, mod, middle_grad, back_near)
+    attend_raw, input_gradient = lax.optimization_barrier((attend_raw, input_gradient))
+    small = attend_raw[:, shard : shard + extra].reshape(devices, -1)[:, : 2 * frames * part]
+    small = small.astype(f32).reshape(clips, rows, 2, frames, part)
+    mod_grad = jnp.sum(small, axis=(1, 2)).reshape(clips * frames, part)
+    attend_sum = jnp.sum(
+        attend_raw[:, :shard].reshape(clips, rows, shard, 3, features).astype(f32), axis=0
+    )
     attend_sum = attend_sum.transpose(1, 2, 0, 3).reshape(shard, 3 * width)
 
-    far = (
-        back_far[0].astype(f32) + swap(back_far[1], ROW, rows, 1).astype(f32)
-    ).astype(bf16)
-    input_gradient = input_back(
-        own,
-        mod,
-        middle_grad,
-        (back_near[0], swap(back_near[1], ROW, rows, 1), swap(far, ROW, rows, 2)),
-    )
-
-    mod_grad = jnp.concatenate([mod_early, mod_late, mod_gate], axis=1)
-    mod_grad = mod_grad.reshape(frames, clips, rows, part).transpose(1, 2, 0, 3)
-    mod_grad = relative(mod_grad.reshape(clips, rows * frames, part), clip)
-    mod_grad = mod_grad.reshape(clips, rows, frames * part).swapaxes(0, 1)
-    mod_grad = relative(mod_grad, row)
-    mod_grad = mod_grad[:2] + swap(mod_grad[2:], ROW, rows, 2)
-    mod_grad = mod_grad[0] + swap(mod_grad[1], ROW, rows, 1)
-    mod_grad = relative(trade(mod_grad.reshape(clips, frames, part), "clip", clips), clip)
-    mod_grad = mod_grad.reshape(clips * frames, part)
     adaptive_sum = lax.dot_general(
         mod_grad,
         cond_all.astype(f32),
@@ -931,7 +957,6 @@
 
     reduced = [adaptive_sum, offsets_sum, attend_sum, project_sum, widen_sum, narrow_sum]
     squares = sum((jnp.sum(item * item) for item in reduced))
-    squares, input_gradient = lax.optimization_barrier((squares, input_gradient))
     squares = lax.all_to_all(
         jnp.broadcast_to(squares, (devices, 8, 128)), both, 0, 0, tiled=True
     )

time: 730 us -> 666 us (0.912)
  waiting for transfers between devices: 217 us -> 159 us
  starting transfers between devices: 65.7 us -> 55.4 us
    all_gather x1, waiting for transfers between devices: 29 us -> 3.65 us  [local(): lax.all_gather(attend_mine.reshape(rows * shard, 3 * features), 'clip', a...]
    all_to_all x1, waiting for transfers between devices: 17.1 us -> 0.01 us  [local(): lax.all_to_all(jnp.broadcast_to(project_full[None], (rows, clips, shard,...]
    all_to_all x1, waiting for transfers between devices: 15.7 us -> 0.01 us  [local(): project_raw = lax.all_to_all(project_raw, ROW, 0, 0, tiled=True)]
    ppermute x33 -> x24, starting transfers between devices: 34.4 us -> 21.1 us  [swap(): lax.ppermute(value, axis, [(place, place ^ step) for place in range(size)])]
    all_to_all x2, waiting for transfers between devices: 0.01 us -> 12.9 us  [the longest x1 12.9 us: local(): lax.all_to_all(jnp.broadcast_to(project_weight.T.astype(bf16)[None], (cli...]
    ppermute x33 -> x24, waiting for transfers between devices: 116 us -> 112 us  [swap(): lax.ppermute(value, axis, [(place, place ^ step) for place in range(size)])]
  transfers between devices with their start and end apart: 43 -> 34, of which waited for: 18 -> 8; matrix products, arithmetic and copies ran while one was open for 10% -> 9% of each run, Pallas kernels for 39% -> 41%
where the time goes in v5:
time: 666 us; the launch traced here: 657 us
  Pallas kernels  307 us (46%)
  waiting for transfers between devices  159 us (24%)
  starting transfers between devices  55.4 us (8%)
  other arithmetic  54.5 us (8%)
  local copies, waits for them, and re-layouts  44.8 us (7%)
  between operations  21.7 us (3%)
  blocking collectives  12.6 us (2%)
    ppermute x24, waiting for transfers between devices, swap(): lax.ppermute(value, axis, [(place, place ^ step) for place in range(size)])  112 us
    pallas_call x2, Pallas kernels, attend_back(): pl.pallas_call(functools.partial(attend_back_kernel, heads, last), grid=(...  99 us
    pallas_call x2, Pallas kernels, attend(): pl.pallas_call(functools.partial(attend_kernel, heads), grid=(count // bl...  55.6 us
    pallas_call x3, Pallas kernels, feed_forward(): pl.pallas_call(feed_kernel, grid=(units // block,), in_specs=[spec, flat,...  49.3 us
    pallas_call x2, Pallas kernels, first_back(): pl.pallas_call(functools.partial(first_back_kernel, half, last), grid=(2...  26.5 us
    pallas_call x1, Pallas kernels, feed_weights(): pl.pallas_call(functools.partial(feed_weight_kernel, len(hidden)), grid=(...  21.8 us
    ppermute x24, starting transfers between devices, swap(): lax.ppermute(value, axis, [(place, place ^ step) for place in range(size)])  21.1 us
    all_to_all x1, waiting for transfers between devices, local(): lax.all_to_all(mod_mine.reshape(devices, frames, part), both, 0, 0, tiled...  20.1 us
  transfers between devices with their start and end apart: 34, of which 8 were waited for; matrix products, arithmetic and copies ran while one was open for 9% of the time, Pallas kernels for 41%

profile of v5, /device:TPU:0, one launch (start us, length us, event | category | flops | bytes accessed | tf_op | source)
XLA Modules:
  0.0 657.2 jit_solution(6849097170708784657)
XLA Ops:
  23.9 5.8 all-to-all-start.1
  31.4 11.1 %all-to-all-done.1 = bf16[8,12,1024]{2,1,0:T(8,128)(2,1)S(1)} async-done(((bf16[8,12,1024]{2,1,0:T(8,128)(2,1)}), bf16[8,12,1024]{2,1,0:T(8,128)(2,1)S(1)}, u32[]{:S(2)}, u32[]{:S(2)}) %all-to-all-start.1) | async-done | bytes 196640 | tf_op jit(solution)/shard_map/all_to_all | solution.py:780
  50.1 20.1 %all-to-all-done.2 = f32[32,12,192]{2,1,0:T(8,128)S(1)} async-done(((f32[32,12,192]{2,1,0:T(8,128)}), f32[32,12,192]{2,1,0:T(8,128)S(1)}, u32[]{:S(2)}, u32[]{:S(2)}) %all-to-all-start.2) | async-done | bytes 294944 | tf_op jit(solution)/shard_map/all_to_all | solution.py:790
  70.7 3.7 all-gather.3.cloned.1.call-done
  77.0 35.2 %collective-permute-done.one = bf16[784,1024]{1,0:T(8,128)(2,1)} collective-permute-done((bf16[784,1024]{1,0:T(8,128)(2,1)}, bf16[784,1024]{1,0:T(8,128)(2,1)}, u32[]{:S(2)}, u32[]{:S(2)}) %collective-permute-start) | collective-permute-done | bytes 1605664 | tf_op jit(solution)/shard_map/ppermute | solution.py:684
  113.0 5.3 all-to-all-start
  126.0 9.0 %shard_map.487.q_ref.k2.v2 = bf16[768,1536]{1,0:T(8,128)(2,1)} custom-call(bf16[784,1024]{1,0:T(8,128)(2,1)} %collective-permute-done.one, bf16[784,1024]{1,0:T(8,128)(2,1)} %collective-permute-done.1.two, f32[12,6,1024]{2,1,0:T(8,128)} %copy-done.2, bf16[768,1024]{1,0:T(8,128)(2,1)} %bitcast.189, f32[32,1536]{1,0:T(8,128)} %get-tuple-element.272.cosine, ...), custom_call_target="tpu_custom_call" | custom-call | flops 2415919104 | bytes 6291456 | tf_op jit(solution)/shard_map/pallas_call | solution.py:120
  135.0 12.9 %all-to-all-done = bf16[8,32,1024]{2,1,0:T(8,128)(2,1)S(1)} async-done(((bf16[8,32,1024]{2,1,0:T(8,128)(2,1)}), bf16[8,32,1024]{2,1,0:T(8,128)(2,1)S(1)}, u32[]{:S(2)}, u32[]{:S(2)}) %all-to-all-start) | async-done | bytes 524320 | tf_op jit(solution)/shard_map/all_to_all | solution.py:830
  149.5 4.5 all-to-all-start.3
  154.2 9.2 %shard_map.488.k1.v1.q_ref = bf16[768,1536]{1,0:T(8,128)(2,1)} custom-call(bf16[784,1024]{1,0:T(8,128)(2,1)} %fusion.2.one, bf16[784,1024]{1,0:T(8,128)(2,1)} %collective-permute-done.6.two, f32[12,6,1024]{2,1,0:T(8,128)} %copy-done.2, bf16[768,1024]{1,0:T(8,128)(2,1)} %bitcast.190, f32[32,1536]{1,0:T(8,128)} %get-tuple-element.243.cosine, ...), custom_call_target="tpu_custom_call" | custom-call | flops 2415919104 | bytes 6291456 | tf_op jit(solution)/shard_map/pallas_call | solution.py:120
  164.0 27.7 %shard_map.489 = (bf16[256,1536]{1,0:T(8,128)(2,1)}, f32[4,1536]{1,0:T(4,128)}) custom-call(bf16[768,1536]{1,0:T(8,128)(2,1)} %shard_map.487.q_ref.k2.v2, bf16[768,1536]{1,0:T(8,128)(2,1)} %shard_map.488.k1.v1.q_ref, bf16[768,1536]{1,0:T(8,128)(2,1)} %shard_map.487.q_ref.k2.v2, bf16[768,1536]{1,0:T(8,128)(2,1)} %shard_map.488.k1.v1.q_ref, ...), custom_call_target="tpu_custom_call" | custom-call | flops 19327352832 | bytes 3145728 | tf_op jit(solution)/shard_map/pallas_call | solution.py:174
  195.0 27.9 %shard_map.490 = (bf16[256,1536]{1,0:T(8,128)(2,1)}, f32[4,1536]{1,0:T(4,128)}) custom-call(bf16[768,1536]{1,0:T(8,128)(2,1)} %shard_map.488.k1.v1.q_ref, bf16[768,1536]{1,0:T(8,128)(2,1)} %shard_map.488.k1.v1.q_ref, bf16[768,1536]{1,0:T(8,128)(2,1)} %shard_map.487.q_ref.k2.v2, bf16[768,1536]{1,0:T(8,128)(2,1)} %shard_map.488.k1.v1.q_ref, ...), custom_call_target="tpu_custom_call" | custom-call | flops 19327352832 | bytes 3145728 | tf_op jit(solution)/shard_map/pallas_call | solution.py:174
  231.3 7.5 %shard_map.491 = (f32[12,64,1024]{2,1,0:T(8,128)}, bf16[768,1024]{1,0:T(8,128)(2,1)}, bf16[768,1024]{1,0:T(8,128)(2,1)}) custom-call(s32[4]{0:T(128)} %iota_xor_fusion.order, bf16[256,1536]{1,0:T(8,128)(2,1)} %get-tuple-element.118.a0.out_ref, bf16[256,768]{1,0:T(8,128)(2,1)} %copy-done.24, bf16[256,768]{1,0:T(8,128)(2,1)} %copy-done.23, ...), custom_call_target="tpu_custom_call" | custom-call | flops 1610612736 | bytes 11010048 | tf_op jit(solution)/shard_map/pallas_call | solution.py:361
  242.4 23.7 %shard_map.492 = (f32[768,1024]{1,0:T(8,128)}, f32[768,1024]{1,0:T(8,128)}, bf16[768,2048]{1,0:T(8,128)(2,1)}, bf16[768,2048]{1,0:T(8,128)(2,1)}) custom-call(bf16[16,2,2,32,2048]{4,3,2,1,0:T(8,128)(2,1)} %bitcast.186, bf16[768,1024]{1,0:T(8,128)(2,1)} %get-tuple-element.122.hidden.refs_0_, bf16[768,1024]{1,0:T(8,128)(2,1)} %get-tuple-element.124.branch.refs_3_), custom_call_target="tpu_custom_call" | custom-call | flops 12884901888 | bytes 14680064 | tf_op jit(solution)/shard_map/pallas_call | solution.py:440
  266.1 11.0 %collective-permute-done.11.hidden.refs_1_ = bf16[384,1024]{1,0:T(8,128)(2,1)S(1)} collective-permute-done((bf16[384,1024]{1,0:T(8,128)(2,1)S(1)}, bf16[384,1024]{1,0:T(8,128)(2,1)S(1)}, u32[]{:S(2)}, u32[]{:S(2)}) %collective-permute-start.11) | collective-permute-done | bytes 786464 | tf_op jit(solution)/shard_map/ppermute | solution.py:684
  278.0 12.8 %shard_map.493 = (bf16[384,1024]{1,0:T(8,128)(2,1)}, bf16[384,1024]{1,0:T(8,128)(2,1)}, bf16[384,2048]{1,0:T(8,128)(2,1)}, bf16[384,2048]{1,0:T(8,128)(2,1)}) custom-call(bf16[16,2,2,32,2048]{4,3,2,1,0:T(8,128)(2,1)} %bitcast.187, bf16[384,1024]{1,0:T(8,128)(2,1)} %copy-done.49, bf16[384,1024]{1,0:T(8,128)(2,1)} %bitcast.176), custom_call_target="tpu_custom_call" | custom-call | flops 6442450944 | bytes 11534336 | tf_op jit(solution)/shard_map/pallas_call | solution.py:440
  290.8 12.8 %shard_map.494 = (bf16[384,1024]{1,0:T(8,128)(2,1)}, bf16[384,1024]{1,0:T(8,128)(2,1)}, bf16[384,2048]{1,0:T(8,128)(2,1)}, bf16[384,2048]{1,0:T(8,128)(2,1)}) custom-call(bf16[16,2,2,32,2048]{4,3,2,1,0:T(8,128)(2,1)} %bitcast.188, bf16[384,1024]{1,0:T(8,128)(2,1)} %copy-done.48, bf16[384,1024]{1,0:T(8,128)(2,1)} %bitcast.174), custom_call_target="tpu_custom_call" | custom-call | flops 6442450944 | bytes 11534336 | tf_op jit(solution)/shard_map/pallas_call | solution.py:440
  305.7 21.8 %shard_map.495 = bf16[16,2,2,32,2048]{4,3,2,1,0:T(8,128)(2,1)} custom-call(bf16[768,1024]{1,0:T(8,128)(2,1)} %get-tuple-element.122.hidden.refs_0_, bf16[384,1024]{1,0:T(8,128)(2,1)} %copy-done.49, bf16[384,1024]{1,0:T(8,128)(2,1)} %copy-done.48, bf16[768,1024]{1,0:T(8,128)(2,1)} %get-tuple-element.124.branch.refs_3_, bf16[384,1024]{1,0:T(8,128)(2,1)} %bitcast.177, ...), custom_call_target="tpu_custom_call" | custom-call | flops 12884901888 | bytes 20971520 | tf_op jit(solution)/shard_map/pallas_call | solution.py:480
  327.5 12.3 %collective-permute-done.13 = bf16[384,1024]{1,0:T(8,128)(2,1)S(1)} collective-permute-done((bf16[384,1024]{1,0:T(8,128)(2,1)S(1)}, bf16[384,1024]{1,0:T(8,128)(2,1)S(1)}, u32[]{:S(2)}, u32[]{:S(2)}) %collective-permute-start.13) | collective-permute-done | bytes 786464 | tf_op jit(solution)/shard_map/ppermute | solution.py:684
  341.1 15.6 %shard_map.496 = (f32[12,64,1024]{2,1,0:T(8,128)}, f32[12,3,1024]{2,1,0:T(4,128)}, bf16[256,768]{1,0:T(8,128)(2,1)}, bf16[256,768]{1,0:T(8,128)(2,1)}, bf16[256,...) custom-call(s32[4]{0:T(128)} %iota_xor_fusion.order, ...), custom_call_target="tpu_custom_call" | custom-call | flops 3221225472 | bytes 18874368 | tf_op jit(solution)/shard_map/pallas_call | solution.py:544
  358.4 4.8 all-to-all-start.4
  365.2 48.3 %shard_map.497 = (bf16[256,1536]{1,0:T(8,128)(2,1)}, f32[256,3072]{1,0:T(8,128)}, f32[256,3072]{1,0:T(8,128)}) custom-call(bf16[768,1536]{1,0:T(8,128)(2,1)} %shard_map.488.k1.v1.q_ref, bf16[768,1536]{1,0:T(8,128)(2,1)} %shard_map.488.k1.v1.q_ref, bf16[768,1536]{1,0:T(8,128)(2,1)} %shard_map.487.q_ref.k2.v2, bf16[768,1536]{1,0:T(8,128)(2,1)} %shard_map.488.k1.v1.q_ref, ...), custom_call_target="tpu_custom_call" | custom-call | flops 41070624768 | bytes 6291456 | tf_op jit(solution)/shard_map/pallas_call | solution.py:320
  416.7 4.3 all-to-all-start.5
  423.1 50.7 %shard_map.498 = (bf16[256,1536]{1,0:T(8,128)(2,1)}, bf16[256,3072]{1,0:T(8,128)(2,1)}, bf16[256,3072]{1,0:T(8,128)(2,1)}) custom-call(bf16[768,1536]{1,0:T(8,128)(2,1)} %shard_map.487.q_ref.k2.v2, bf16[768,1536]{1,0:T(8,128)(2,1)} %shard_map.488.k1.v1.q_ref, bf16[768,1536]{1,0:T(8,128)(2,1)} %shard_map.487.q_ref.k2.v2, ...), custom_call_target="tpu_custom_call" | custom-call | flops 41070624768 | bytes 6291456 | tf_op jit(solution)/shard_map/pallas_call | solution.py:320
  473.8 12.5 %shard_map.500 = (bf16[2,768,1024]{2,1,0:T(8,128)(2,1)}, f32[768,1024]{1,0:T(8,128)}, f32[12,2,1024]{2,1,0:T(2,128)}) custom-call(bf16[784,1024]{1,0:T(8,128)(2,1)} %collective-permute-done.one, bf16[784,1024]{1,0:T(8,128)(2,1)} %collective-permute-done.1.two, f32[12,6,1024]{2,1,0:T(8,128)} %copy-done.2, bf16[256,1536]{1,0:T(8,128)(2,1)} %get-tuple-element.165.dq, ...), custom_call_target="tpu_custom_call" | custom-call | flops 4831838208 | bytes 9437184 | tf_op jit(solution)/shard_map/pallas_call | solution.py:648
  491.7 6.3 shard_map.499
  501.3 14.0 %shard_map.501 = (bf16[2,768,1024]{2,1,0:T(8,128)(2,1)}, bf16[1024,768]{1,0:T(8,128)(2,1)}, f32[12,2,1024]{2,1,0:T(2,128)}) custom-call(bf16[784,1024]{1,0:T(8,128)(2,1)} %fusion.2.one, bf16[784,1024]{1,0:T(8,128)(2,1)} %collective-permute-done.6.two, f32[12,6,1024]{2,1,0:T(8,128)} %copy-done.2, bf16[256,1536]{1,0:T(8,128)(2,1)} %get-tuple-element.171.dq, ...), custom_call_target="tpu_custom_call" | custom-call | flops 4831838208 | bytes 9437184 | tf_op jit(solution)/shard_map/pallas_call | solution.py:648
  518.9 6.2 all-to-all-start.6
  535.2 53.1 %collective-permute-done.23 = bf16[2,32,2048]{2,1,0:T(8,128)(2,1)S(1)} collective-permute-done((bf16[2,32,2048]{2,1,0:T(8,128)(2,1)S(1)}, bf16[2,32,2048]{2,1,0:T(8,128)(2,1)S(1)}, u32[]{:S(2)}, u32[]{:S(2)}) %collective-permute-start.23) | collective-permute-done | bytes 262176 | tf_op jit(solution)/shard_map/ppermute | solution.py:684
  595.0 7.2 %shard_map.502 = f32[12,64,1024]{2,1,0:T(8,128)} custom-call(bf16[12,64,1024]{2,1,0:T(8,128)(2,1)} %bitcast.143, f32[12,6,1024]{2,1,0:T(8,128)} %copy-done.2, f32[12,64,1024]{2,1,0:T(8,128)} %get-tuple-element.178.middle_grad, bf16[768,1024]{1,0:T(8,128)(2,1)} %get-tuple-element.221.one, bf16[768,1024]{1,0:T(8,128)(2,1)} %collective-permute-done.21.two, ...), custom_call_target="tpu_custom_call" | custom-call | flops 15728640 | bytes 12582912 | tf_op jit(solution)/shard_map/pallas_call | solution.py:672
  610.8 3.5 reshape.425
  623.4 12.6 %all_to_all.40 = f32[32,8,128]{2,1,0:T(8,128)S(1)} all-to-all(f32[32,8,128]{2,1,0:T(8,128)S(1)} %broadcast_in_dim.47), channel_id=1, replica_groups=mesh['clip'=8,'x'=2,'core'=2] {'clip','x','core'}, dimensions={0} | all-to-all | bytes 262144 | tf_op jit(solution)/shard_map/all_to_all | solution.py:960
  (300 shorter events, 122.0 us)
Async XLA Ops:
  7.2 67.2 %all-gather.3.cloned.1.call-start = ((), (), s32[]{:S(2)}) async-start(), calls=%async_computation.9 | async-start | bytes 1769472 | tf_op jit(solution)/shard_map/all_gather | solution.py:774
  9.5 6.9 %collective-permute-start.5 = (bf16[32,768]{1,0:T(8,128)(2,1)S(1)}, bf16[32,768]{1,0:T(8,128)(2,1)S(1)}, u32[]{:S(2)}, u32[]{:S(2)}) collective-permute-start(bf16[32,768]{1,0:T(8,128)(2,1)S(1)} %get-tuple-element.253), channel_id=1, source_target_pairs={{0,3},{1,2},{2,1},{3,0},{4,7},{5,6},{6,5},{7,4},{8,11},{9,10},{10,... | collective-permute-start | bytes 147464 | tf_op jit(solution)/shard_map/ppermute | solution.py:684
  18.8 11.0 %collective-permute-start.2 = (bf16[2,32,2048]{2,1,0:T(8,128)(2,1)S(1)}, bf16[2,32,2048]{2,1,0:T(8,128)(2,1)S(1)}, u32[]{:S(2)}, u32[]{:S(2)}) collective-permute-start(bf16[2,32,2048]{2,1,0:T(8,128)(2,1)S(1)} %bitcast.178), channel_id=1, source_target_pairs={{0,2},{2,0},{1,3},{3,1},{4,6},{6,4},{5,7},{7,5},{8,10},{10,8},{9,1... | collective-permute-start | bytes 786440 | tf_op jit(solution)/shard_map/ppermute | solution.py:684
  23.9 18.6 %all-to-all-start.1 = ((bf16[8,12,1024]{2,1,0:T(8,128)(2,1)}), bf16[8,12,1024]{2,1,0:T(8,128)(2,1)S(1)}, u32[]{:S(2)}, u32[]{:S(2)}) async-start(bf16[8,12,1024]{2,1,0:T(8,128)(2,1)} %broadcast_in_dim.41), calls=%async_computation.1 | async-start | bytes 524288 | tf_op jit(solution)/shard_map/all_to_all | solution.py:780
  43.7 26.5 %all-to-all-start.2 = ((f32[32,12,192]{2,1,0:T(8,128)}), f32[32,12,192]{2,1,0:T(8,128)S(1)}, u32[]{:S(2)}, u32[]{:S(2)}) async-start(f32[32,12,192]{2,1,0:T(8,128)} %bitcast.34), calls=%async_computation.2 | async-start | bytes 1048576 | tf_op jit(solution)/shard_map/all_to_all | solution.py:790
  46.4 196.0 %all-gather.5.cloned.1.call-start = ((), (), s32[]{:S(2)}) async-start(), calls=%async_computation.10 | async-start | bytes 8912896 | tf_op jit(solution)/shard_map/all_gather | solution.py:799
  75.4 36.8 %collective-permute-start = (bf16[784,1024]{1,0:T(8,128)(2,1)}, bf16[784,1024]{1,0:T(8,128)(2,1)}, u32[]{:S(2)}, u32[]{:S(2)}) collective-permute-start(bf16[784,1024]{1,0:T(8,128)(2,1)} %fusion.2.one), channel_id=1, source_target_pairs={{0,2},{1,3},{2,0},{3,1},{4,6},{5,7},{6,4},{7,5},{8,10},{9,11},{10,... | collective-permute-start | bytes 4816904 | tf_op jit(solution)/shard_map/ppermute | solution.py:684
  77.0 43.3 %collective-permute-start.6 = (bf16[784,1024]{1,0:T(8,128)(2,1)}, bf16[784,1024]{1,0:T(8,128)(2,1)}, u32[]{:S(2)}, u32[]{:S(2)}) collective-permute-start(bf16[784,1024]{1,0:T(8,128)(2,1)} %fusion.2.one), channel_id=1, source_target_pairs={{0,1},{1,0},{2,3},{3,2},{4,5},{5,4},{6,7},{7,6},{8,9},{9,8},{10,11... | collective-permute-start | bytes 4816904 | tf_op jit(solution)/shard_map/ppermute | solution.py:684
  112.2 10.8 %collective-permute-start.1 = (bf16[784,1024]{1,0:T(8,128)(2,1)}, bf16[784,1024]{1,0:T(8,128)(2,1)}, u32[]{:S(2)}, u32[]{:S(2)}) collective-permute-start(bf16[784,1024]{1,0:T(8,128)(2,1)} %collective-permute-done.one), channel_id=1, source_target_pairs={{0,1},{1,0},{2,3},{3,2},{4,5},{5,4},{6,7},{7,6},{8,9},{9,8},{10,11... | collective-permute-start | bytes 4816904 | tf_op jit(solution)/shard_map/ppermute | solution.py:684
  113.0 34.9 %all-to-all-start = ((bf16[8,32,1024]{2,1,0:T(8,128)(2,1)}), bf16[8,32,1024]{2,1,0:T(8,128)(2,1)S(1)}, u32[]{:S(2)}, u32[]{:S(2)}) async-start(bf16[8,32,1024]{2,1,0:T(8,128)(2,1)} %broadcast_in_dim.40), calls=%async_computation | async-start | bytes 1048576 | tf_op jit(solution)/shard_map/all_to_all | solution.py:830
  121.2 70.6 %collective-permute-start.7 = (bf16[12,64,1024]{2,1,0:T(8,128)(2,1)S(1)}, bf16[12,64,1024]{2,1,0:T(8,128)(2,1)}, u32[]{:S(2)}, u32[]{:S(2)}) collective-permute-start(bf16[12,64,1024]{2,1,0:T(8,128)(2,1)S(1)} %bitcast.150), channel_id=1, source_target_pairs={{0,2},{2,0},{1,3},{3,1},{4,6},{6,4},{5,7},{7,5},{8,10},{10,8},{9,1... | collective-permute-start | bytes 4718600 | tf_op jit(solution)/shard_map/ppermute | solution.py:684
  149.5 42.3 %all-to-all-start.3 = ((bf16[4,8,32,1024]{3,2,1,0:T(8,128)(2,1)}), bf16[4,8,32,1024]{3,2,1,0:T(8,128)(2,1)}, u32[]{:S(2)}, u32[]{:S(2)}) async-start(bf16[4,8,32,1024]{3,2,1,0:T(8,128)(2,1)} %broadcast_in_dim.46), calls=%async_computation.3 | async-start | bytes 4194304 | tf_op jit(solution)/shard_map/all_to_all | solution.py:838
  153.9 347.4 %reduce-scatter.2.cloned.1.call-start = ((), (), s32[]{:S(2)}) async-start(), calls=%async_computation.11 | async-start | bytes 8912896 | tf_op jit(solution)/shard_map/reduce_scatter | solution.py:876
  192.9 37.4 %collective-permute-start.10 = (bf16[256,768]{1,0:T(8,128)(2,1)S(1)}, bf16[256,768]{1,0:T(8,128)(2,1)S(1)}, u32[]{:S(2)}, u32[]{:S(2)}) collective-permute-start(bf16[256,768]{1,0:T(8,128)(2,1)S(1)} %get-tuple-element.228), channel_id=1, source_target_pairs={{0,3},{1,2},{2,1},{3,0},{4,7},{5,6},{6,5},{7,4},{8,11},{9,10},{10,... | collective-permute-start | bytes 1179656 | tf_op jit(solution)/shard_map/ppermute | solution.py:684
  194.5 35.8 %collective-permute-start.9 = (bf16[256,768]{1,0:T(8,128)(2,1)S(1)}, bf16[256,768]{1,0:T(8,128)(2,1)S(1)}, u32[]{:S(2)}, u32[]{:S(2)}) collective-permute-start(bf16[256,768]{1,0:T(8,128)(2,1)S(1)} %get-tuple-element.229), channel_id=1, source_target_pairs={{0,2},{1,3},{2,0},{3,1},{4,6},{5,7},{6,4},{7,5},{8,10},{9,11},{10,... | collective-permute-start | bytes 1179656 | tf_op jit(solution)/shard_map/ppermute | solution.py:684
  223.9 6.4 collective-permute-start.8
  240.3 25.8 %collective-permute-start.12 = (bf16[384,1024]{1,0:T(8,128)(2,1)S(1)}, bf16[384,1024]{1,0:T(8,128)(2,1)S(1)}, u32[]{:S(2)}, u32[]{:S(2)}) collective-permute-start(bf16[384,1024]{1,0:T(8,128)(2,1)S(1)} %get-tuple-element.224), channel_id=1, source_target_pairs={{0,2},{2,0},{1,3},{3,1},{4,6},{6,4},{5,7},{7,5},{8,10},{10,8},{9,1... | collective-permute-start | bytes 2359304 | tf_op jit(solution)/shard_map/ppermute | solution.py:684
  242.1 35.0 %collective-permute-start.11 = (bf16[384,1024]{1,0:T(8,128)(2,1)S(1)}, bf16[384,1024]{1,0:T(8,128)(2,1)S(1)}, u32[]{:S(2)}, u32[]{:S(2)}) collective-permute-start(bf16[384,1024]{1,0:T(8,128)(2,1)S(1)} %get-tuple-element.225), channel_id=1, source_target_pairs={{0,2},{2,0},{1,3},{3,1},{4,6},{6,4},{5,7},{7,5},{8,10},{10,8},{9,1... | collective-permute-start | bytes 2359304 | tf_op jit(solution)/shard_map/ppermute | solution.py:684
  303.6 23.9 %collective-permute-start.14 = (bf16[384,1024]{1,0:T(8,128)(2,1)}, bf16[384,1024]{1,0:T(8,128)(2,1)S(1)}, u32[]{:S(2)}, u32[]{:S(2)}) collective-permute-start(bf16[384,1024]{1,0:T(8,128)(2,1)} %get-tuple-element.140), channel_id=1, source_target_pairs={{0,2},{2,0},{1,3},{3,1},{4,6},{6,4},{5,7},{7,5},{8,10},{10,8},{9,1... | collective-permute-start | bytes 2359304 | tf_op jit(solution)/shard_map/ppermute | solution.py:684
  305.2 34.6 %collective-permute-start.13 = (bf16[384,1024]{1,0:T(8,128)(2,1)S(1)}, bf16[384,1024]{1,0:T(8,128)(2,1)S(1)}, u32[]{:S(2)}, u32[]{:S(2)}) collective-permute-start(bf16[384,1024]{1,0:T(8,128)(2,1)S(1)} %copy-done.50), channel_id=1, source_target_pairs={{0,2},{2,0},{1,3},{3,1},{4,6},{6,4},{5,7},{7,5},{8,10},{10,8},{9,1... | collective-permute-start | bytes 2359304 | tf_op jit(solution)/shard_map/ppermute | solution.py:684
  356.8 8.5 %collective-permute-start.15 = (bf16[256,768]{1,0:T(8,128)(2,1)}, bf16[256,768]{1,0:T(8,128)(2,1)}, u32[]{:S(2)}, u32[]{:S(2)}) collective-permute-start(bf16[256,768]{1,0:T(8,128)(2,1)} %get-tuple-element.145), channel_id=1, source_target_pairs={{0,1},{1,0},{2,3},{3,2},{4,5},{5,4},{6,7},{7,6},{8,9},{9,8},{10,11... | collective-permute-start | bytes 1179656 | tf_op jit(solution)/shard_map/ppermute | solution.py:684
  358.4 55.2 %all-to-all-start.4 = ((bf16[4,8,32,1024]{3,2,1,0:T(8,128)(2,1)}), bf16[4,8,32,1024]{3,2,1,0:T(8,128)(2,1)}, u32[]{:S(2)}, u32[]{:S(2)}) async-start(bf16[4,8,32,1024]{3,2,1,0:T(8,128)(2,1)} %get-tuple-element.150), calls=%async_computation.4 | async-start | bytes 4194304 | tf_op jit(solution)/shard_map/all_to_all | solution.py:886
  363.2 50.4 %collective-permute-start.16 = (bf16[256,768]{1,0:T(8,128)(2,1)}, bf16[256,768]{1,0:T(8,128)(2,1)S(1)}, u32[]{:S(2)}, u32[]{:S(2)}) collective-permute-start(bf16[256,768]{1,0:T(8,128)(2,1)} %get-tuple-element.148), channel_id=1, source_target_pairs={{0,2},{1,3},{2,0},{3,1},{4,6},{5,7},{6,4},{7,5},{8,10},{9,11},{10,... | collective-permute-start | bytes 1179656 | tf_op jit(solution)/shard_map/ppermute | solution.py:684
  365.2 48.3 %collective-permute-start.17 = (bf16[256,768]{1,0:T(8,128)(2,1)}, bf16[256,768]{1,0:T(8,128)(2,1)S(1)}, u32[]{:S(2)}, u32[]{:S(2)}) collective-permute-start(bf16[256,768]{1,0:T(8,128)(2,1)} %get-tuple-element.149), channel_id=1, source_target_pairs={{0,3},{1,2},{2,1},{3,0},{4,7},{5,6},{6,5},{7,4},{8,11},{9,10},{10,... | collective-permute-start | bytes 1179656 | tf_op jit(solution)/shard_map/ppermute | solution.py:684
  416.7 57.1 %all-to-all-start.5 = ((bf16[8,32,1024]{2,1,0:T(8,128)(2,1)}), bf16[8,32,1024]{2,1,0:T(8,128)(2,1)S(1)}, u32[]{:S(2)}, u32[]{:S(2)}) async-start(bf16[8,32,1024]{2,1,0:T(8,128)(2,1)} %reduce_sum.118), calls=%async_computation.5 | async-start | bytes 1048576 | tf_op jit(solution)/shard_map/all_to_all | solution.py:899
  421.0 52.8 %collective-permute-start.18 = (bf16[384,1024]{1,0:T(8,128)(2,1)}, bf16[384,1024]{1,0:T(8,128)(2,1)}, u32[]{:S(2)}, u32[]{:S(2)}) collective-permute-start(bf16[384,1024]{1,0:T(8,128)(2,1)} %get-tuple-element.160), channel_id=1, source_target_pairs={{0,2},{2,0},{1,3},{3,1},{4,6},{6,4},{5,7},{7,5},{8,10},{10,8},{9,1... | collective-permute-start | bytes 2359304 | tf_op jit(solution)/shard_map/ppermute | solution.py:684
  422.5 51.3 %collective-permute-start.19 = (bf16[384,1024]{1,0:T(8,128)(2,1)}, bf16[384,1024]{1,0:T(8,128)(2,1)}, u32[]{:S(2)}, u32[]{:S(2)}) collective-permute-start(bf16[384,1024]{1,0:T(8,128)(2,1)} %get-tuple-element.161), channel_id=1, source_target_pairs={{0,2},{2,0},{1,3},{3,1},{4,6},{6,4},{5,7},{7,5},{8,10},{10,8},{9,1... | collective-permute-start | bytes 2359304 | tf_op jit(solution)/shard_map/ppermute | solution.py:684
  489.1 9.0 %collective-permute-start.20 = (bf16[768,1024]{1,0:T(8,128)(2,1)}, bf16[768,1024]{1,0:T(8,128)(2,1)}, u32[]{:S(2)}, u32[]{:S(2)}) collective-permute-start(bf16[768,1024]{1,0:T(8,128)(2,1)} %slice_bitcast_fusion.2), channel_id=1, source_target_pairs={{0,1},{1,0},{2,3},{3,2},{4,5},{5,4},{6,7},{7,6},{8,9},{9,8},{10,11... | collective-permute-start | bytes 4718600 | tf_op jit(solution)/shard_map/ppermute | solution.py:684
  518.9 83.4 %all-to-all-start.6 = ((bf16[32,38,768]{2,1,0:T(8,128)(2,1)}), bf16[32,38,768]{2,1,0:T(8,128)(2,1)S(1)}, u32[]{:S(2)}, u32[]{:S(2)}) async-start(bf16[32,38,768]{2,1,0:T(8,128)(2,1)} %pad_maximum_fusion), calls=%async_computation.7 | async-start | bytes 3932160 | tf_op jit(solution)/shard_map/all_to_all | solution.py:938
  526.5 68.5 %collective-permute-start.22 = (bf16[768,1024]{1,0:T(8,128)(2,1)S(1)}, bf16[768,1024]{1,0:T(8,128)(2,1)}, u32[]{:S(2)}, u32[]{:S(2)}) collective-permute-start(bf16[768,1024]{1,0:T(8,128)(2,1)S(1)} %copy-done.18), channel_id=1, source_target_pairs={{0,2},{1,3},{2,0},{3,1},{4,6},{5,7},{6,4},{7,5},{8,10},{9,11},{10,... | collective-permute-start | bytes 4718600 | tf_op jit(solution)/shard_map/ppermute | solution.py:684
  531.7 63.3 %collective-permute-start.21 = (bf16[768,1024]{1,0:T(8,128)(2,1)S(1)}, bf16[768,1024]{1,0:T(8,128)(2,1)}, u32[]{:S(2)}, u32[]{:S(2)}) collective-permute-start(bf16[768,1024]{1,0:T(8,128)(2,1)S(1)} %get-tuple-element.220), channel_id=1, source_target_pairs={{0,1},{1,0},{2,3},{3,2},{4,5},{5,4},{6,7},{7,6},{8,9},{9,8},{10,11... | collective-permute-start | bytes 4718600 | tf_op jit(solution)/shard_map/ppermute | solution.py:684
  534.2 54.1 %collective-permute-start.23 = (bf16[2,32,2048]{2,1,0:T(8,128)(2,1)S(1)}, bf16[2,32,2048]{2,1,0:T(8,128)(2,1)S(1)}, u32[]{:S(2)}, u32[]{:S(2)}) collective-permute-start(bf16[2,32,2048]{2,1,0:T(8,128)(2,1)S(1)} %bitcast.180), channel_id=1, source_target_pairs={{0,2},{2,0},{1,3},{3,1},{4,6},{6,4},{5,7},{7,5},{8,10},{10,8},{9,1... | collective-permute-start | bytes 786440 | tf_op jit(solution)/shard_map/ppermute | solution.py:684
  (55 other events, 472.1 us)
Sparse Core Ops, SparseCore 0:
  18.0 56.3 all-gather.2
  77.1 84.3 all-gather.4
  340.0 113.6 reduce-scatter.1

commit v6 on v5

--- a/solution.py
+++ b/solution.py
@@ -157,7 +157,7 @@
         probs = jnp.exp2(logits - peak).astype(bf16)
         mixed = dot(v_wide[head], probs)
         norm = mixed[HEAD_DIM : HEAD_DIM + 1]
-        out[head * HEAD_DIM : (head + 1) * HEAD_DIM, :] = (mixed[:HEAD_DIM] / norm).astype(bf16)
+        out[0, head * HEAD_DIM : (head + 1) * HEAD_DIM, :] = (mixed[:HEAD_DIM] / norm).astype(bf16)
         lse[head : head + 1, :] = peak + jnp.log2(norm)
         logits = later
 
@@ -166,7 +166,7 @@
     rows, count = queries.shape[0] // 3, queries.shape[1]
     total = bias.shape[1]
     heads = rows // HEAD_DIM
-    block = 512 if count % 512 == 0 else 128
+    block = count // 2
 
     def piece(index):
         return pl.BlockSpec((rows, count), lambda i: (index, 0))
@@ -183,11 +183,11 @@
             pl.BlockSpec((1, total), lambda i: (0, 0)),
         ],
         out_specs=[
-            pl.BlockSpec((rows, block), lambda i: (0, i)),
+            pl.BlockSpec((1, rows, block), lambda i: (i, 0, 0)),
             pl.BlockSpec((heads, block), lambda i: (0, i)),
         ],
         out_shape=[
-            jax.ShapeDtypeStruct((rows, count), bf16),
+            jax.ShapeDtypeStruct((2, rows, block), bf16),
             jax.ShapeDtypeStruct((heads, count), f32),
         ],
         scratch_shapes=[
@@ -243,7 +243,7 @@
             axis=0,
         )
         grad = grad_all[rows, :]
-        mean = jnp.sum(grad.astype(f32) * out_ref[rows, :].astype(f32), axis=0, keepdims=True)
+        mean = jnp.sum(grad.astype(f32) * out_ref[0, rows, :].astype(f32), axis=0, keepdims=True)
         one, two, three = split3(-mean)
         grad_wide = jnp.concatenate([grad, one, two, three, jnp.zeros((61, block), bf16)], axis=0)
         return dot(wide, k_wide[head], TN), dot(grad_wide, v_wide[head], TN)
@@ -297,7 +297,7 @@
         piece(2),
         piece(2),
         pl.BlockSpec((1, total), lambda i: (0, 0)),
-        moving,
+        pl.BlockSpec((1, rows, block), lambda i: (i // half, 0, lax.rem(i, half))),
         pl.BlockSpec((rows, block), lambda i: (0, jnp.minimum(i, half - 1))),
         pl.BlockSpec((rows, block), lambda i: (0, jnp.maximum(i - half, 0))),
         pl.BlockSpec((heads, block), lambda i: (0, i)),
@@ -333,10 +333,10 @@
     )(*operands)
 
 
-def project_kernel(order, a0, a1, a2, a3, proj, tokens, cotangent, mod, att_out, hidden, branch):
-    features = a0.shape[0]
+def project_kernel(order, a0, a1, a2, a3, proj, tokens, cotangent, mod, att_out, hid1, hid2, branch):
+    features = a1.shape[0]
     mixed = None
-    for slot, part in enumerate((a0, a1, a2, a3)):
+    for slot, part in enumerate((a0.at[0], a1, a2, a3)):
         columns = proj[:, pl.ds(pl.multiple_of(order[slot] * features, features), features)]
         term = dot(part[...], columns, TT)
         mixed = term if mixed is None else mixed + term
@@ -347,28 +347,47 @@
     normed, _ = layer_norm(middle)
     hidden_two = normed * (1.0 + mod[:, 4:5, :]) + mod[:, 3:4, :]
     flat = (shape[0] * shape[1], shape[2])
-    hidden[...] = hidden_two.astype(bf16).reshape(flat)
+    hidden_two = hidden_two.astype(bf16).reshape(flat)
+    first = pl.program_id(0) < pl.num_programs(0) // 2
+
+    @pl.when(first)
+    def _():
+        hid1[...] = hidden_two
+
+    @pl.when(jnp.logical_not(first))
+    def _():
+        hid2[...] = hidden_two
+
     branch[...] = (mod[:, 5:6, :] * cotangent[...].astype(f32)).astype(bf16).reshape(flat)
 
 
 def project_out(order, parts, proj, tokens, cotangent, mod):
     frames, per_frame, width = tokens.shape
-    chunk = 4
+    chunk = 2
+    half = frames // chunk // 2
     block = chunk * per_frame
-    features = parts[0].shape[0]
+    features = parts[1].shape[0]
     cube = pl.BlockSpec((chunk, per_frame, width), lambda i: (i, 0, 0))
     flat = pl.BlockSpec((block, width), lambda i: (i, 0))
+    count = frames * per_frame
     return pl.pallas_call(
         project_kernel,
         grid=(frames // chunk,),
         in_specs=[whole(pltpu.SMEM)]
-        + [pl.BlockSpec((features, block), lambda i: (0, i))] * 4
+        + [pl.BlockSpec((1, features, block), lambda i: (0, 0, i))]
+        + [pl.BlockSpec((features, block), lambda i: (0, i))] * 3
         + [whole(), cube, cube, pl.BlockSpec((chunk, 6, width), lambda i: (i, 0, 0))],
-        out_specs=[cube, flat, flat],
+        out_specs=[
+            cube,
+            pl.BlockSpec((block, width), lambda i: (jnp.minimum(i, half - 1), 0)),
+            pl.BlockSpec((block, width), lambda i: (jnp.maximum(i - half, 0), 0)),
+            flat,
+        ],
         out_shape=[
             jax.ShapeDtypeStruct(tokens.shape, f32),
-            jax.ShapeDtypeStruct((frames * per_frame, width), bf16),
-            jax.ShapeDtypeStruct((frames * per_frame, width), bf16),
+            jax.ShapeDtypeStruct((count // 2, width), bf16),
+            jax.ShapeDtypeStruct((count // 2, width), bf16),
+            jax.ShapeDtypeStruct((count, width), bf16),
         ],
         compiler_params=params(),
         cost_estimate=cost(2 * frames * per_frame * width * width, 14 * frames * per_frame * width),
@@ -388,7 +407,9 @@
     )
 
 
-def feed_kernel(weights, hidden, branch, out, into, active_out, wide_out, out_sum, in_sum):
+def feed_kernel(
+    weights, hidden, branch, cotangent, out, into, active_out, wide_out, gate, out_sum, in_sum
+):
     step = pl.program_id(0)
     widen = load_weight(weights, 0)
     narrow = load_weight(weights, 1)
@@ -426,28 +447,38 @@
 
     @pl.when(step == pl.num_programs(0) - 1)
     def _():
-        out[...] = out_sum[...].astype(out.dtype)
+        total = out_sum[...]
+        out[...] = total.astype(out.dtype)
         into[...] = in_sum[...].astype(into.dtype)
-
-
-def feed_forward(weights, hidden, branch, kind):
+        shape = cotangent.shape
+        gate[...] = jnp.sum(cotangent[...].astype(f32) * total.reshape(shape), axis=1, keepdims=True)
+
+
+def feed_forward(weights, hidden, branch, cotangent, part, kind):
     count, width = hidden.shape
     units = weights.shape[-1]
     block = 512
+    frames, per_frame = count // cotangent.shape[1], cotangent.shape[1]
     spec = pl.BlockSpec(weights.shape[:-1] + (block,), lambda i: (0, 0, 0, 0, i))
     flat = pl.BlockSpec((count, width), lambda i: (0, 0))
     wide = pl.BlockSpec((count, block), lambda i: (0, i))
     return pl.pallas_call(
         feed_kernel,
         grid=(units // block,),
-        in_specs=[spec, flat, flat],
-        out_specs=[flat, flat, wide, wide],
+        in_specs=[
+            spec,
+            flat,
+            pl.BlockSpec((count, width), lambda i: (part, 0)),
+            pl.BlockSpec((frames, per_frame, width), lambda i: (part, 0, 0)),
+        ],
+        out_specs=[flat, flat, wide, wide, pl.BlockSpec((frames, 1, width), lambda i: (0, 0, 0))],
         out_shape=[jax.ShapeDtypeStruct((count, width), kind)] * 2
-        + [jax.ShapeDtypeStruct((count, units), bf16)] * 2,
+        + [jax.ShapeDtypeStruct((count, units), bf16)] * 2
+        + [jax.ShapeDtypeStruct((frames, 1, width), f32)],
         scratch_shapes=[VMEM((count, width), f32), VMEM((count, width), f32)],
         compiler_params=params(),
         cost_estimate=cost(8 * count * width * units, 4 * width * units + 4 * count * units),
-    )(weights, hidden, branch)
+    )(weights, hidden, branch, cotangent)
 
 
 def feed_weight_kernel(parts, *refs):
@@ -470,17 +501,20 @@
     units = active[0].shape[1]
     block = 512
 
-    def fixed(value):
-        return pl.BlockSpec(value.shape, lambda i: (0, 0))
+    deep = hidden[0].shape[0]
+
+    def fixed(part):
+        return pl.BlockSpec((deep, width), lambda i: (part, 0))
 
     def moving(value):
         return pl.BlockSpec((value.shape[0], block), lambda i: (0, i))
 
-    count = sum(value.shape[0] for value in hidden)
+    count = deep * len(hidden)
     return pl.pallas_call(
         functools.partial(feed_weight_kernel, len(hidden)),
         grid=(units // block,),
-        in_specs=[fixed(value) for value in (*hidden, *branch)]
+        in_specs=[fixed(0)] * len(hidden)
+        + [fixed(index % 2) for index in range(len(branch))]
         + [moving(value) for value in (*active, *wide)],
         out_specs=pl.BlockSpec(shape[:-1] + (block,), lambda i: (0, 0, 0, 0, i)),
         out_shape=jax.ShapeDtypeStruct(shape, bf16),
@@ -490,7 +524,7 @@
 
 
 def middle_kernel(
-    order, into, into_far, tokens, cotangent, att_out, mod, a0, a1, a2, a3, proj,
+    order, into1, into2, far1, far2, tokens, cotangent, att_out, mod, a0, a1, a2, a3, proj,
     middle_grad, mod_grad, d0, d1, d2, d3, proj_raw, raw_sum,
 ):
     step = pl.program_id(0)
@@ -499,15 +533,18 @@
     att = att_out[...]
     middle = tokens[...].astype(f32) + mod[:, 2:3] * att
     normed, inverse = layer_norm(middle)
-    hid_grad = (into[...] + into_far[...].astype(f32)).reshape(shape)
+    first = step < pl.num_programs(0) // 2
+    hid_grad = jnp.where(
+        first, into1[...] + far1[...].astype(f32), into2[...] + far2[...].astype(f32)
+    ).reshape(shape)
     mod_grad[:, 1:2] = jnp.sum(hid_grad, axis=1, keepdims=True)
     mod_grad[:, 2:3] = jnp.sum(hid_grad * normed, axis=1, keepdims=True)
     mid = cotangent[...].astype(f32) + norm_back(normed, inverse, hid_grad * (1.0 + mod[:, 4:5]))
     middle_grad[...] = mid
     mod_grad[:, 0:1] = jnp.sum(mid * att, axis=1, keepdims=True)
     grad = (mod[:, 2:3] * mid).astype(bf16).reshape(flat)
-    features = a0.shape[0]
-    for slot, (part, out) in enumerate(((a0, d0), (a1, d1), (a2, d2), (a3, d3))):
+    features = a1.shape[0]
+    for slot, (part, out) in enumerate(((a0.at[0], d0), (a1, d1), (a2, d2), (a3, d3))):
         place = pl.ds(pl.multiple_of(order[slot] * features, features), features)
         out[...] = dot(proj[:, place], grad, TT).astype(bf16)
         term = dot(part[...], grad)
@@ -533,20 +570,23 @@
             proj_raw[group] = some.reshape(proj_raw.shape[1:])
 
 
-def middle_back(order, into, into_far, tokens, cotangent, att_out, mod, parts, proj, owners):
+def middle_back(order, into, tokens, cotangent, att_out, mod, parts, proj, owners):
     frames, per_frame, width = tokens.shape
-    chunk = 4
+    chunk = 2
+    half = frames // chunk // 2
     block = chunk * per_frame
-    features = parts[0].shape[0]
+    features = parts[1].shape[0]
     cube = pl.BlockSpec((chunk, per_frame, width), lambda i: (i, 0, 0))
-    flat = pl.BlockSpec((block, width), lambda i: (i, 0))
+    one = pl.BlockSpec((block, width), lambda i: (jnp.minimum(i, half - 1), 0))
+    two = pl.BlockSpec((block, width), lambda i: (jnp.maximum(i - half, 0), 0))
     turned = pl.BlockSpec((features, block), lambda i: (0, i))
     return pl.pallas_call(
         middle_kernel,
         grid=(frames // chunk,),
-        in_specs=[whole(pltpu.SMEM), flat, flat, cube, cube, cube]
+        in_specs=[whole(pltpu.SMEM), one, two, one, two, cube, cube, cube]
         + [pl.BlockSpec((chunk, 6, width), lambda i: (i, 0, 0))]
-        + [turned] * 4
+        + [pl.BlockSpec((1, features, block), lambda i: (0, 0, i))]
+        + [turned] * 3
         + [whole()],
         out_specs=[cube, pl.BlockSpec((chunk, 3, width), lambda i: (i, 0, 0))]
         + [turned] * 4
@@ -560,33 +600,36 @@
         scratch_shapes=[VMEM((width, width), f32)],
         compiler_params=params(),
         cost_estimate=cost(4 * frames * per_frame * width * width, 24 * frames * per_frame * width),
-    )(order, into, into_far, tokens, cotangent, att_out, mod, *parts, proj)
-
-
-def output_kernel(out, out_far, tokens, cotangent, att_out, mod, block_out, mod_grad):
-    branch_out = (out[...] + out_far[...].astype(f32)).reshape(tokens.shape)
+    )(order, *into, tokens, cotangent, att_out, mod, *parts, proj)
+
+
+def output_kernel(one, two, far1, far2, tokens, att_out, mod, block_out):
+    first = pl.program_id(0) < pl.num_programs(0) // 2
+    branch_out = jnp.where(
+        first, one[...] + far1[...].astype(f32), two[...] + far2[...].astype(f32)
+    ).reshape(tokens.shape)
     middle = tokens[...].astype(f32) + mod[:, 2:3] * att_out[...]
     block_out[...] = (middle + mod[:, 5:6] * branch_out).astype(bf16)
-    mod_grad[...] = jnp.sum(cotangent[...].astype(f32) * branch_out, axis=1, keepdims=True)
-
-
-def block_output(out, out_far, tokens, cotangent, att_out, mod):
+
+
+def block_output(parts, tokens, att_out, mod):
     frames, per_frame, width = tokens.shape
-    chunk = 4
+    chunk = 2
+    half = frames // chunk // 2
+    block = chunk * per_frame
     cube = pl.BlockSpec((chunk, per_frame, width), lambda i: (i, 0, 0))
-    flat = pl.BlockSpec((chunk * per_frame, width), lambda i: (i, 0))
+    one = pl.BlockSpec((block, width), lambda i: (jnp.minimum(i, half - 1), 0))
+    two = pl.BlockSpec((block, width), lambda i: (jnp.maximum(i - half, 0), 0))
     return pl.pallas_call(
         output_kernel,
         grid=(frames // chunk,),
-        in_specs=[flat, flat, cube, cube, cube, pl.BlockSpec((chunk, 6, width), lambda i: (i, 0, 0))],
-        out_specs=[cube, pl.BlockSpec((chunk, 1, width), lambda i: (i, 0, 0))],
-        out_shape=[
-            jax.ShapeDtypeStruct(tokens.shape, bf16),
-            jax.ShapeDtypeStruct((frames, 1, width), f32),
-        ],
+        in_specs=[one, two, one, two, cube, cube]
+        + [pl.BlockSpec((chunk, 6, width), lambda i: (i, 0, 0))],
+        out_specs=cube,
+        out_shape=jax.ShapeDtypeStruct(tokens.shape, bf16),
         compiler_params=params(),
         cost_estimate=cost(8 * frames * per_frame * width, 16 * frames * per_frame * width),
-    )(out, out_far, tokens, cotangent, att_out, mod)
+    )(*parts, tokens, att_out, mod)
 
 
 def first_back_kernel(half, last, one, two, mod, dq, dk, dv, weight, *rest):
@@ -678,6 +721,23 @@
         compiler_params=params(),
         cost_estimate=cost(20 * frames * per_frame * width, 16 * frames * per_frame * width),
     )(tokens, mod, middle_grad, *parts)
+
+
+def total_kernel(pieces, out):
+    out[...] = jnp.sum(pieces[...].astype(f32), axis=0)
+
+
+def total_over(pieces):
+    count, owners, rows, columns = pieces.shape
+    return pl.pallas_call(
+        total_kernel,
+        grid=(owners,),
+        in_specs=[pl.BlockSpec((count, 1, rows, columns), lambda i: (0, i, 0, 0))],
+        out_specs=pl.BlockSpec((1, rows, columns), lambda i: (i, 0, 0)),
+        out_shape=jax.ShapeDtypeStruct((owners, rows, columns), f32),
+        compiler_params=params(),
+        cost_estimate=cost(pieces.size, 3 * pieces.size),
+    )(pieces)
 
 
 def swap(value, axis, size, step):
@@ -748,7 +808,8 @@
     count = frames * per_frame
     devices = clips * rows
     features = width // rows
-    clip, far, row = lax.axis_index("clip"), lax.axis_index("x"), lax.axis_index(ROW)
+    clip, far, core = lax.axis_index("clip"), lax.axis_index("x"), lax.axis_index("core")
+    row = lax.axis_index(ROW)
     both = ("clip",) + ROW
     order = (row ^ jnp.arange(rows)).astype(jnp.int32)
 
@@ -763,9 +824,8 @@
     small = jnp.pad(small, ((0, 0), (0, spare * width - count))).reshape(3 * spare, width)
     small = jnp.pad(small, ((0, 16 - 3 * spare), (0, 0)))
     tok0 = jnp.concatenate([own.reshape(count, width), small], axis=0)
-    tok2 = swap(tok0, ROW, rows, 2)
     tok1 = swap(tok0, ROW, rows, 1)
-    tok3 = swap(tok2, ROW, rows, 1)
+    tok2_one = swap(tok0[: count // 2], "x", 2, 1)
 
     shard = widen_weight.shape[0]
     attend_mine = attend_weight.astype(bf16).reshape(shard, 3, rows, features)
@@ -777,6 +837,8 @@
 
     cond_act = jax.nn.silu(condition[0].astype(f32)).astype(bf16)
     cond_act, tok0 = lax.optimization_barrier((cond_act, tok0))
+    project_mine = project_weight.T.astype(bf16)
+    project_mine = relative(jnp.stack([project_mine, swap(project_mine, "x", 2, 1)]), far)
     cond_all = lax.all_to_all(
         jnp.broadcast_to(cond_act[None], (clips, frames, width)), "clip", 0, 0, tiled=True
     ).reshape(clips * frames, width)
@@ -784,6 +846,8 @@
         f32
     )
     part = mod_mine.shape[1]
+    tok2_two, mod_mine, tok2_one = lax.optimization_barrier((tok0[count // 2 :], mod_mine, tok2_one))
+    tok2_two = swap(tok2_two, "x", 2, 1)
     mod_mine = jnp.broadcast_to(
         mod_mine.reshape(clips, 1, frames, part), (clips, rows, frames, part)
     )
@@ -794,7 +858,11 @@
     feed_mine = jnp.stack([widen_weight.astype(bf16), narrow_weight.T.astype(bf16)])
     feed_mine = feed_mine.reshape(2, shard, 2, units // 2).transpose(2, 0, 1, 3)
     feed_mine = relative(trade(relative(feed_mine, far), "x", 2), far)
-    feed_mine, attend_full, mod = lax.optimization_barrier((feed_mine, attend_full, mod))
+    feed_mine, attend_full, mod, tok2_two = lax.optimization_barrier(
+        (feed_mine, attend_full, mod, tok2_two)
+    )
+    tok2 = jnp.concatenate([tok2_one, tok2_two], axis=0)
+    tok3 = swap(tok2, ROW, rows, 1)
     attend_turned = attend_full.T
     feed_full = lax.all_gather(
         feed_mine.reshape(4 * shard, units // 2), ("clip", "core"), axis=0, tiled=True
@@ -818,25 +886,16 @@
         return jnp.cos(angles), jnp.sin(angles), jnp.where(small[2:3] > 0.5, 0.0, MASKED)
 
     cos_near, sin_near, bias_near = places_of((tok0, tok1))
+    qkv_near = project_qkv(tok0, tok1, mod, attend_turned, cos_near, sin_near)
+    qkv_near, tok3 = lax.optimization_barrier((qkv_near, tok3))
     cos_far, sin_far, bias_far = places_of((tok2, tok3))
-    near = 2 * count
-
-    qkv_near = project_qkv(tok0, tok1, mod, attend_turned, cos_near, sin_near)
     qkv_far = project_qkv(tok2, tok3, mod, attend_turned, cos_far, sin_far)
     cosine = jnp.concatenate([cos_near, cos_far], axis=1)
     sine = jnp.concatenate([sin_near, sin_far], axis=1)
     bias = jnp.concatenate([bias_near, bias_far], axis=1)
 
     project_full = lax.all_to_all(
-        jnp.broadcast_to(project_weight.T.astype(bf16)[None], (clips, shard, width)),
-        "clip",
-        0,
-        0,
-        tiled=True,
-    )
-    project_full, qkv_far = lax.optimization_barrier((project_full, qkv_far))
-    project_full = lax.all_to_all(
-        jnp.broadcast_to(project_full[None], (rows, clips, shard, width)), ROW, 0, 0, tiled=True
+        jnp.broadcast_to(project_mine[None], (clips, 2, shard, width)), "clip", 0, 0, tiled=True
     )
 
     cot_far, mod = lax.optimization_barrier((upstream, mod))
@@ -845,34 +904,39 @@
     out_far, qkv_near, project_full, cot_far = lax.optimization_barrier(
         (out_far, qkv_near, project_full, cot_far)
     )
-    project_full = project_full.transpose(1, 0, 2, 3).reshape(width, width)
+    project_near = swap(project_full, "core", 2, 1)
+    part2 = swap(out_far[0], ROW, rows, 2)
+    part3 = swap(out_far[1], ROW, rows, 3)
+    out_near, lse_near = attend(qkv_near, qkv_near, qkv_far, bias)
+    out_near, project_near = lax.optimization_barrier((out_near, project_near))
+    part1 = swap(out_near[1], ROW, rows, 1)
+    project_full = relative(jnp.stack([project_full, project_near]), core)
+    project_full = project_full.transpose(1, 2, 0, 3, 4).reshape(width, width)
     branch_far = (mod[:, 5:6, :] * cot_far.astype(f32)).astype(bf16).reshape(count, width)
-
-    part2 = swap(out_far[:, :count], ROW, rows, 2)
-    part3 = swap(out_far[:, count:], ROW, rows, 3)
-    out_near, lse_near = attend(qkv_near, qkv_near, qkv_far, bias)
-    parts = [out_near, swap(out_near[:, count:], ROW, rows, 1), part2, part3]
-    att_out, hidden_two, branch_grad = project_out(order, parts, project_full, own, upstream, mod)
-    half = count // 2
-    hid1 = swap(hidden_two[:half], "x", 2, 1)
-    hid2 = swap(hidden_two[half:], "x", 2, 1)
-    out_own, in_own, act0, wide0 = feed_forward(feed_full, hidden_two, branch_grad, f32)
-    hid1, hid2, out_own = lax.optimization_barrier((hid1, hid2, out_own))
-    out1, in1, act1, wide1 = feed_forward(feed_full, hid1, branch_far[:half], bf16)
-    in1 = swap(in1, "x", 2, 1)
-    hid2, act1 = lax.optimization_barrier((hid2, act1))
-    out2, in2, act2, wide2 = feed_forward(feed_full, hid2, branch_far[half:], bf16)
-    in2 = swap(in2, "x", 2, 1)
+    parts = [out_near, part1, part2, part3]
+    att_out, hid1, hid2, branch = project_out(order, parts, project_full, own, upstream, mod)
+
+    far1 = swap(hid1, "x", 2, 1)
+    out1, in1, act1, wide1, gate1 = feed_forward(feed_full, hid1, branch, upstream, 0, f32)
+    far2, out1 = lax.optimization_barrier((hid2, out1))
+    far2 = swap(far2, "x", 2, 1)
+    out2, in2, act2, wide2, gate2 = feed_forward(feed_full, hid2, branch, upstream, 1, f32)
+    far1, out2 = lax.optimization_barrier((far1, out2))
+    out3, in3, act3, wide3, gate3 = feed_forward(feed_full, far1, branch_far, cot_far, 0, bf16)
+    in3 = swap(in3, "x", 2, 1)
+    far2, act3 = lax.optimization_barrier((far2, act3))
+    out4, in4, act4, wide4, gate4 = feed_forward(feed_full, far2, branch_far, cot_far, 1, bf16)
+    in4 = swap(in4, "x", 2, 1)
     feed_raw = feed_weights(
         feed_full.shape,
-        (hidden_two, hid1, hid2),
-        (branch_grad, branch_far[:half], branch_far[half:]),
-        (act0, act1, act2),
-        (wide0, wide1, wide2),
+        (hid1, hid2, far1, far2),
+        (branch, branch, branch_far, branch_far),
+        (act1, act2, act3, act4),
+        (wide1, wide2, wide3, wide4),
     )
     if not fused:
         feed_raw = feed_raw.reshape(2, clips, 2, 2, shard, units // 2).transpose(1, 3, 2, 0, 4, 5)
-    feed_raw, in1, in2 = lax.optimization_barrier((feed_raw, in1, in2))
+    feed_raw, in3, in4 = lax.optimization_barrier((feed_raw, in3, in4))
     feed_sum = lax.psum_scatter(
         feed_raw.reshape(8 * clips * shard, units // 2),
         ("clip", "core"),
@@ -880,8 +944,9 @@
         tiled=True,
     ).reshape(2, 2, shard, units // 2)
     middle_grad, mod_late, d0, d1, d2, d3, project_raw = middle_back(
-        order, in_own, jnp.concatenate([in1, in2], axis=0), own, upstream, att_out, mod, parts, project_full, (rows, clips)
-    )
+        order, (in1, in2, in3, in4), own, upstream, att_out, mod, parts, project_full, (rows, clips)
+    )
+    mod_gate = jnp.concatenate([gate1 + gate3, gate2 + gate4], axis=0)
 
     project_raw = lax.all_to_all(project_raw, ROW, 0, 0, tiled=True)
 
@@ -892,27 +957,25 @@
     dq_near, dk, dv = attend_back(
         qkv_near, qkv_near, qkv_far, bias, out_near, (d0, d1), lse_near, turning, 0
     )
-    dk, d2, d3, project_raw, out1, out2 = lax.optimization_barrier(
-        (dk, d2, d3, project_raw, out1, out2)
+    dk, d2, d3, project_raw, out3, out4 = lax.optimization_barrier(
+        (dk, d2, d3, project_raw, out3, out4)
     )
     project_raw = jnp.sum(project_raw.astype(f32), axis=0).astype(bf16)
     project_raw = lax.all_to_all(project_raw, "clip", 0, 0, tiled=True)
-    out1 = swap(out1, "x", 2, 1)
-    out2 = swap(out2, "x", 2, 1)
+    out3 = swap(out3, "x", 2, 1)
+    out4 = swap(out4, "x", 2, 1)
     dq_far, dk, dv = attend_back(
         qkv_far, qkv_near, qkv_far, bias, out_far, (d2, d3), lse_far, turning, 1, (dk, dv)
     )
-    dq_far, project_raw, out1, out2 = lax.optimization_barrier((dq_far, project_raw, out1, out2))
+    dq_far, project_raw, out3, out4 = lax.optimization_barrier((dq_far, project_raw, out3, out4))
     project_sum = jnp.sum(project_raw.astype(f32), axis=0).T
-    block_out, mod_gate = block_output(
-        out_own, jnp.concatenate([out1, out2], axis=0), own, upstream, att_out, mod
-    )
     back_far, raw, mod_early = first_back(tok2, tok3, mod, dq_far, dk, dv, attend_turned, 1)
     back_far = (
         back_far[0].astype(f32) + swap(back_far[1], ROW, rows, 1).astype(f32)
     ).astype(bf16)
     back_far, dq_near, feed_sum = lax.optimization_barrier((back_far, dq_near, feed_sum))
-    back_far = swap(back_far, ROW, rows, 2)
+    back_far = lax.all_gather(back_far, "x", axis=0)
+    back_far = lax.dynamic_index_in_dim(back_far, 1 - far, 0, keepdims=False)
     feed_sum = relative(trade(relative(feed_sum, far), "x", 2), far).astype(f32)
     widen_sum, narrow_sum = feed_sum.transpose(1, 2, 0, 3).reshape(2, shard, units)
     narrow_sum = narrow_sum.T
@@ -936,14 +999,16 @@
         axis=1,
     )
     attend_raw = lax.all_to_all(attend_raw, both, 0, 0, tiled=True)
+    block_out = block_output((out1, out2, out3, out4), own, att_out, mod)
     input_gradient = input_back(own, mod, middle_grad, back_near)
-    attend_raw, input_gradient = lax.optimization_barrier((attend_raw, input_gradient))
+    attend_raw, input_gradient, block_out = lax.optimization_barrier(
+        (attend_raw, input_gradient, block_out)
+    )
     small = attend_raw[:, shard : shard + extra].reshape(devices, -1)[:, : 2 * frames * part]
     small = small.astype(f32).reshape(clips, rows, 2, frames, part)
     mod_grad = jnp.sum(small, axis=(1, 2)).reshape(clips * frames, part)
-    attend_sum = jnp.sum(
-        attend_raw[:, :shard].reshape(clips, rows, shard, 3, features).astype(f32), axis=0
-    )
+    attend_sum = total_over(attend_raw.reshape(clips, rows, shard + extra, 3 * features))
+    attend_sum = attend_sum[:, :shard].reshape(rows, shard, 3, features)
     attend_sum = attend_sum.transpose(1, 2, 0, 3).reshape(shard, 3 * width)
 
     adaptive_sum = lax.dot_general(

time: 666 us -> 594 us (0.89)
  waiting for transfers between devices: 159 us -> 78.3 us
  Pallas kernels: 307 us -> 327 us
    ppermute x24 -> x26, waiting for transfers between devices: 112 us -> 24.1 us  [swap(): lax.ppermute(value, axis, [(place, place ^ step) for place in range(size)])]
    all_gather x0 -> x1, waiting for transfers between devices: none -> 28.8 us  [local(): back_far = lax.all_gather(back_far, 'x', axis=0)]
    all_to_all x2 -> x1, waiting for transfers between devices: 12.9 us -> 0.01 us  [local(): lax.all_to_all(jnp.broadcast_to(project_mine[None], (clips, 2, shard, wid...]
    all_to_all x1, waiting for transfers between devices: 11.1 us -> 0.01 us  [local(): lax.all_to_all(jnp.broadcast_to(cond_act[None], (clips, frames, width)),...]
    pallas_call x3 -> x4, Pallas kernels: 49.3 us -> 54.1 us  [feed_forward(): pl.pallas_call(feed_kernel, grid=(units // block,), in_specs=[spec, flat,...]
    ppermute x24 -> x26, starting transfers between devices: 21.1 us -> 22 us  [swap(): lax.ppermute(value, axis, [(place, place ^ step) for place in range(size)])]
  transfers between devices with their start and end apart: 34 -> 36, of which waited for: 8 -> 6; matrix products, arithmetic and copies ran while one was open for 9% -> 10% of each run, Pallas kernels for 41% -> 53%
where the time goes in v6:
time: 594 us; the launch traced here: 585 us
  Pallas kernels  327 us (55%)
  waiting for transfers between devices  78.3 us (13%)
  starting transfers between devices  55.1 us (9%)
  other arithmetic  49.5 us (8%)
  local copies, waits for them, and re-layouts  38.9 us (7%)
  between operations  22.1 us (4%)
  blocking collectives  12.3 us (2%)
    pallas_call x2, Pallas kernels, attend_back(): pl.pallas_call(functools.partial(attend_back_kernel, heads, last), grid=(...  99.5 us
    pallas_call x2, Pallas kernels, attend(): pl.pallas_call(functools.partial(attend_kernel, heads), grid=(count // bl...  55 us
    pallas_call x4, Pallas kernels, feed_forward(): pl.pallas_call(feed_kernel, grid=(units // block,), in_specs=[spec, flat,...  54.1 us
    all_gather x1, waiting for transfers between devices, local(): back_far = lax.all_gather(back_far, 'x', axis=0)  28.8 us
    pallas_call x2, Pallas kernels, first_back(): pl.pallas_call(functools.partial(first_back_kernel, half, last), grid=(2...  26.7 us
    ppermute x26, waiting for transfers between devices, swap(): lax.ppermute(value, axis, [(place, place ^ step) for place in range(size)])  24.1 us
    pallas_call x1, Pallas kernels, feed_weights(): pl.pallas_call(functools.partial(feed_weight_kernel, len(hidden)), grid=(...  23.8 us
    ppermute x26, starting transfers between devices, swap(): lax.ppermute(value, axis, [(place, place ^ step) for place in range(size)])  22 us
  transfers between devices with their start and end apart: 36, of which 6 were waited for; matrix products, arithmetic and copies ran while one was open for 10% of the time, Pallas kernels for 53%

profile of v6, /device:TPU:0, one launch (start us, length us, event | category | flops | bytes accessed | tf_op | source)
XLA Modules:
  0.0 584.9 jit_solution(17874061008750820221)
XLA Ops:
  18.7 5.8 all-to-all-start
  33.4 5.9 %collective-permute-done.1 = bf16[2,32,2048]{2,1,0:T(8,128)(2,1)S(1)} collective-permute-done((bf16[2,32,2048]{2,1,0:T(8,128)(2,1)S(1)}, bf16[2,32,2048]{2,1,0:T(8,128)(2,1)S(1)}, u32[]{:S(2)}, u32[]{:S(2)}) %collective-permute-start.1) | collective-permute-done | bytes 262176 | tf_op jit(solution)/shard_map/ppermute | solution.py:744
  43.6 5.0 all-to-all-start.1
  51.9 19.1 %all-to-all-done.1 = f32[32,12,192]{2,1,0:T(8,128)S(1)} async-done(((f32[32,12,192]{2,1,0:T(8,128)}), f32[32,12,192]{2,1,0:T(8,128)S(1)}, u32[]{:S(2)}, u32[]{:S(2)}) %all-to-all-start.1) | async-done | bytes 294944 | tf_op jit(solution)/shard_map/all_to_all | solution.py:854
  71.6 6.3 %all-gather.5.cloned.1.call-done = bf16[1024,768]{0,1:T(8,128)(2,1)} async-done(((bf16[128,768]{0,1:T(8,128)(2,1)}), bf16[1024,768]{0,1:T(8,128)(2,1)}) %all-gather.5.cloned.1.call-update) | async-done | bytes 1572880 | tf_op jit(solution)/shard_map/all_gather | solution.py:834
  86.3 5.1 all-to-all-start.2
  95.1 9.0 %shard_map.487.k1.v1.q_ref = bf16[768,1536]{1,0:T(8,128)(2,1)} custom-call(bf16[784,1024]{1,0:T(8,128)(2,1)} %fusion.2.one, bf16[784,1024]{1,0:T(8,128)(2,1)} %collective-permute-done.two, f32[12,6,1024]{2,1,0:T(8,128)} %copy-done.2, bf16[768,1024]{1,0:T(8,128)(2,1)} %bitcast.233, f32[32,1536]{1,0:T(8,128)} %get-tuple-element.273.cosine, ...), custom_call_target="tpu_custom_call" | custom-call | flops 2415919104 | bytes 6291456 | tf_op jit(solution)/shard_map/pallas_call | solution.py:120
  107.1 9.0 %shard_map.488.q_ref.k2.v2 = bf16[768,1536]{1,0:T(8,128)(2,1)} custom-call(bf16[784,1024]{1,0:T(8,128)(2,1)} %constant_dynamic-update-slice_fusion.one, bf16[784,1024]{1,0:T(8,128)(2,1)} %collective-permute-done.7.two, f32[12,6,1024]{2,1,0:T(8,128)} %copy-done.2, bf16[768,1024]{1,0:T(8,128)(2,1)} %bitcast.234, f32[32,1536]{1,0:T(8,128)} %get-tuple-element.271.cosine, ...), custom_call_target="tpu_custom_call" | custom-call | flops 2415919104 | bytes 6291456 | tf_op jit(solution)/shard_map/pallas_call | solution.py:120
  116.0 27.3 %shard_map.489 = (bf16[2,256,768]{2,1,0:T(8,128)(2,1)}, f32[4,1536]{1,0:T(4,128)}) custom-call(bf16[768,1536]{1,0:T(8,128)(2,1)} %shard_map.488.q_ref.k2.v2, bf16[768,1536]{1,0:T(8,128)(2,1)} %shard_map.487.k1.v1.q_ref, bf16[768,1536]{1,0:T(8,128)(2,1)} %shard_map.488.q_ref.k2.v2, bf16[768,1536]{1,0:T(8,128)(2,1)} %shard_map.487.k1.v1.q_ref, ...), custom_call_target="tpu_custom_call" | custom-call | flops 19327352832 | bytes 3145728 | tf_op jit(solution)/shard_map/pallas_call | solution.py:174
  147.1 27.7 %shard_map.490 = (bf16[2,256,768]{2,1,0:T(8,128)(2,1)}, f32[4,1536]{1,0:T(4,128)}) custom-call(bf16[768,1536]{1,0:T(8,128)(2,1)} %shard_map.487.k1.v1.q_ref, bf16[768,1536]{1,0:T(8,128)(2,1)} %shard_map.487.k1.v1.q_ref, bf16[768,1536]{1,0:T(8,128)(2,1)} %shard_map.488.q_ref.k2.v2, bf16[768,1536]{1,0:T(8,128)(2,1)} %shard_map.487.k1.v1.q_ref, ...), custom_call_target="tpu_custom_call" | custom-call | flops 19327352832 | bytes 3145728 | tf_op jit(solution)/shard_map/pallas_call | solution.py:174
  182.1 10.7 %shard_map.491 = (f32[12,64,1024]{2,1,0:T(8,128)}, bf16[384,1024]{1,0:T(8,128)(2,1)}, bf16[384,1024]{1,0:T(8,128)(2,1)}, bf16[768,1024]{1,0:T(8,128)(2,1)}) custom-call(s32[4]{0:T(128)} %iota_xor_fusion.order, bf16[2,256,768]{2,1,0:T(8,128)(2,1)} %get-tuple-element.141.a0.out_ref, bf16[256,768]{1,0:T(8,128)(2,1)} %copy-done.24, bf16[256,768]{1,0:T(8,128)(2,1)} %copy-done.23, ...), custom_call_target="tpu_custom_call" | custom-call | flops 1610612736 | bytes 11010048 | tf_op jit(solution)/shard_map/pallas_call | solution.py:373
  194.2 13.8 %shard_map.492 = (f32[384,1024]{1,0:T(8,128)}, f32[384,1024]{1,0:T(8,128)}, bf16[384,2048]{1,0:T(8,128)(2,1)}, bf16[384,2048]{1,0:T(8,128)(2,1)}, f32[6,1,1024]{2,1,0:T(1,128)}) custom-call(bf16[16,2,2,32,2048]{4,3,2,1,0:T(8,128)(2,1)} %bitcast.229, bf16[384,1024]{1,0:T(8,128)(2,1)} %get-tuple-element.144.hidden.refs_0_, ...), custom_call_target="tpu_custom_call" | custom-call | flops 6442450944 | bytes 11534336 | tf_op jit(solution)/shard_map/pallas_call | solution.py:465
  208.7 13.7 %shard_map.493 = (f32[384,1024]{1,0:T(8,128)}, f32[384,1024]{1,0:T(8,128)}, bf16[384,2048]{1,0:T(8,128)(2,1)}, bf16[384,2048]{1,0:T(8,128)(2,1)}, f32[6,1,1024]{2,1,0:T(1,128)}) custom-call(bf16[16,2,2,32,2048]{4,3,2,1,0:T(8,128)(2,1)} %bitcast.230, bf16[384,1024]{1,0:T(8,128)(2,1)} %get-tuple-element.152.hidden.refs_1_, ...), custom_call_target="tpu_custom_call" | custom-call | flops 6442450944 | bytes 11534336 | tf_op jit(solution)/shard_map/pallas_call | solution.py:465
  223.3 13.2 %shard_map.494 = (bf16[384,1024]{1,0:T(8,128)(2,1)}, bf16[384,1024]{1,0:T(8,128)(2,1)}, bf16[384,2048]{1,0:T(8,128)(2,1)}, bf16[384,2048]{1,0:T(8,128)(2,1)}, f32[6,1,1024]{2,1,0:T(1,128)}) custom-call(bf16[16,2,2,32,2048]{4,3,2,1,0:T(8,128)(2,1)} %bitcast.231, bf16[384,1024]{1,0:T(8,128)(2,1)} %copy-done.52, bf16[768,1024]{1,0:T(8,128)(2,1)} %bitcast.210, ...), custom_call_target="tpu_custom_call" | custom-call | flops 6442450944 | bytes 11534336 | tf_op jit(solution)/shard_map/pallas_call | solution.py:465
  238.8 13.4 %shard_map.495 = (bf16[384,1024]{1,0:T(8,128)(2,1)}, bf16[384,1024]{1,0:T(8,128)(2,1)}, bf16[384,2048]{1,0:T(8,128)(2,1)}, bf16[384,2048]{1,0:T(8,128)(2,1)}, f32[6,1,1024]{2,1,0:T(1,128)}) custom-call(bf16[16,2,2,32,2048]{4,3,2,1,0:T(8,128)(2,1)} %bitcast.232, bf16[384,1024]{1,0:T(8,128)(2,1)} %copy-done.53, bf16[768,1024]{1,0:T(8,128)(2,1)} %bitcast.211, ...), custom_call_target="tpu_custom_call" | custom-call | flops 6442450944 | bytes 11534336 | tf_op jit(solution)/shard_map/pallas_call | solution.py:465
  252.8 23.8 %shard_map.496 = bf16[16,2,2,32,2048]{4,3,2,1,0:T(8,128)(2,1)} custom-call(bf16[384,1024]{1,0:T(8,128)(2,1)} %get-tuple-element.144.hidden.refs_0_, bf16[384,1024]{1,0:T(8,128)(2,1)} %get-tuple-element.152.hidden.refs_1_, bf16[384,1024]{1,0:T(8,128)(2,1)} %copy-done.52, bf16[384,1024]{1,0:T(8,128)(2,1)} %copy-done.53, ...), custom_call_target="tpu_custom_call" | custom-call | flops 12884901888 | bytes 20971520 | tf_op jit(solution)/shard_map/pallas_call | solution.py:513
  277.8 21.8 %shard_map.497 = (f32[12,64,1024]{2,1,0:T(8,128)}, f32[12,3,1024]{2,1,0:T(4,128)}, bf16[256,768]{1,0:T(8,128)(2,1)}, bf16[256,768]{1,0:T(8,128)(2,1)}, bf16[256,...) custom-call(s32[4]{0:T(128)} %iota_xor_fusion.order, ...), custom_call_target="tpu_custom_call" | custom-call | flops 3221225472 | bytes 18874368 | tf_op jit(solution)/shard_map/pallas_call | solution.py:583
  300.6 4.8 all-to-all-start.3
  307.6 48.9 %shard_map.498 = (bf16[256,1536]{1,0:T(8,128)(2,1)}, f32[256,3072]{1,0:T(8,128)}, f32[256,3072]{1,0:T(8,128)}) custom-call(bf16[768,1536]{1,0:T(8,128)(2,1)} %shard_map.487.k1.v1.q_ref, bf16[768,1536]{1,0:T(8,128)(2,1)} %shard_map.487.k1.v1.q_ref, bf16[768,1536]{1,0:T(8,128)(2,1)} %shard_map.488.q_ref.k2.v2, bf16[768,1536]{1,0:T(8,128)(2,1)} %shard_map.487.k1.v1.q_ref, ...), custom_call_target="tpu_custom_call" | custom-call | flops 41070624768 | bytes 6291456 | tf_op jit(solution)/shard_map/pallas_call | solution.py:320
  356.6 3.1 reduce_sum.109
  359.7 6.0 %all-to-all-start.4 = ((bf16[8,32,1024]{2,1,0:T(8,128)(2,1)}), bf16[8,32,1024]{2,1,0:T(8,128)(2,1)S(1)}, u32[]{:S(2)}, u32[]{:S(2)}) async-start(bf16[8,32,1024]{2,1,0:T(8,128)(2,1)} %reduce_sum.109), calls=%async_computation.4 | async-start | bytes 1048576 | tf_op jit(solution)/shard_map/all_to_all | solution.py:964
  367.8 50.6 %shard_map.499 = (bf16[256,1536]{1,0:T(8,128)(2,1)}, bf16[256,3072]{1,0:T(8,128)(2,1)}, bf16[256,3072]{1,0:T(8,128)(2,1)}) custom-call(bf16[768,1536]{1,0:T(8,128)(2,1)} %shard_map.488.q_ref.k2.v2, bf16[768,1536]{1,0:T(8,128)(2,1)} %shard_map.487.k1.v1.q_ref, bf16[768,1536]{1,0:T(8,128)(2,1)} %shard_map.488.q_ref.k2.v2, ...), custom_call_target="tpu_custom_call" | custom-call | flops 41070624768 | bytes 6291456 | tf_op jit(solution)/shard_map/pallas_call | solution.py:320
  418.4 12.5 %shard_map.500 = (bf16[2,768,1024]{2,1,0:T(8,128)(2,1)}, f32[768,1024]{1,0:T(8,128)}, f32[12,2,1024]{2,1,0:T(2,128)}) custom-call(bf16[784,1024]{1,0:T(8,128)(2,1)} %constant_dynamic-update-slice_fusion.one, bf16[784,1024]{1,0:T(8,128)(2,1)} %collective-permute-done.7.two, f32[12,6,1024]{2,1,0:T(8,128)} %copy-done.2, ...), custom_call_target="tpu_custom_call" | custom-call | flops 4831838208 | bytes 9437184 | tf_op jit(solution)/shard_map/pallas_call | solution.py:691
  432.8 3.3 collective-permute-done.23
  438.0 14.1 %shard_map.501 = (bf16[2,768,1024]{2,1,0:T(8,128)(2,1)}, bf16[1024,768]{1,0:T(8,128)(2,1)}, f32[12,2,1024]{2,1,0:T(2,128)}) custom-call(bf16[784,1024]{1,0:T(8,128)(2,1)} %fusion.2.one, bf16[784,1024]{1,0:T(8,128)(2,1)} %collective-permute-done.two, f32[12,6,1024]{2,1,0:T(8,128)} %copy-done.2, bf16[256,1536]{1,0:T(8,128)(2,1)} %get-tuple-element.193.dq, ...), custom_call_target="tpu_custom_call" | custom-call | flops 4831838208 | bytes 9437184 | tf_op jit(solution)/shard_map/pallas_call | solution.py:691
  455.8 6.0 %all-to-all-start.5 = ((bf16[32,38,768]{2,1,0:T(8,128)(2,1)}), bf16[32,38,768]{2,1,0:T(8,128)(2,1)S(1)}, u32[]{:S(2)}, u32[]{:S(2)}) async-start(bf16[32,38,768]{2,1,0:T(8,128)(2,1)} %pad_maximum_fusion.2), calls=%async_computation.6 | async-start | bytes 3932160 | tf_op jit(solution)/shard_map/all_to_all | solution.py:1001
  461.9 6.7 %shard_map.503 = bf16[12,64,1024]{2,1,0:T(8,128)(2,1)} custom-call(f32[384,1024]{1,0:T(8,128)} %get-tuple-element.206.one, f32[384,1024]{1,0:T(8,128)} %get-tuple-element.207.two, bf16[384,1024]{1,0:T(8,128)(2,1)} %collective-permute-done.21.far1, bf16[384,1024]{1,0:T(8,128)(2,1)} %collective-permute-done.22.far2, bf16[12,64,1024]{2,1,0:T(8,128)(2,1)} %bitcast.174, ...), custom_call_target="tpu_custom_call" | custom-call | flops 6291456 | bytes 12582912 | tf_op jit(solution)/shard_map/pallas_call | solution.py:623
  476.6 14.8 %collective-permute-done.25 = bf16[2,32,2048]{2,1,0:T(8,128)(2,1)S(1)} collective-permute-done((bf16[2,32,2048]{2,1,0:T(8,128)(2,1)S(1)}, bf16[2,32,2048]{2,1,0:T(8,128)(2,1)S(1)}, u32[]{:S(2)}, u32[]{:S(2)}) %collective-permute-start.25) | collective-permute-done | bytes 262176 | tf_op jit(solution)/shard_map/ppermute | solution.py:744
  497.0 28.8 %all-gather.9.cloned.1.call-done = bf16[1536,1024]{1,0:T(8,128)(2,1)} async-done(((bf16[768,1024]{1,0:T(8,128)(2,1)}), bf16[1536,1024]{1,0:T(8,128)(2,1)}) %all-gather.9.cloned.1.call-update) | async-done | bytes 3145744 | tf_op jit(solution)/shard_map/all_gather | solution.py:977
  528.4 7.2 %shard_map.502 = f32[12,64,1024]{2,1,0:T(8,128)} custom-call(bf16[12,64,1024]{2,1,0:T(8,128)(2,1)} %bitcast.175, f32[12,6,1024]{2,1,0:T(8,128)} %copy-done.2, f32[12,64,1024]{2,1,0:T(8,128)} %get-tuple-element.203.middle_grad, bf16[768,1024]{1,0:T(8,128)(2,1)} %get-tuple-element.251.one, bf16[768,1024]{1,0:T(8,128)(2,1)} %collective-permute-done.24.two, ...), custom_call_target="tpu_custom_call" | custom-call | flops 15728640 | bytes 12582912 | tf_op jit(solution)/shard_map/pallas_call | solution.py:715
  537.5 3.8 shard_map.504
  549.9 12.3 %all_to_all.35 = f32[32,8,128]{2,1,0:T(8,128)S(1)} all-to-all(f32[32,8,128]{2,1,0:T(8,128)S(1)} %broadcast_in_dim.39), channel_id=1, replica_groups=mesh['clip'=8,'x'=2,'core'=2] {'clip','x','core'}, dimensions={0} | all-to-all | bytes 262144 | tf_op jit(solution)/shard_map/all_to_all | solution.py:1025
  (319 shorter events, 109.2 us)
Async XLA Ops:
  9.5 15.5 %collective-permute-start.4 = (bf16[32,768]{1,0:T(8,128)(2,1)S(1)}, bf16[32,768]{1,0:T(8,128)(2,1)S(1)}, u32[]{:S(2)}, u32[]{:S(2)}) collective-permute-start(bf16[32,768]{1,0:T(8,128)(2,1)S(1)} %get-tuple-element.281), channel_id=1, source_target_pairs={{0,3},{1,2},{2,1},{3,0},{4,7},{5,6},{6,5},{7,4},{8,11},{9,10},{10,... | collective-permute-start | bytes 147464 | tf_op jit(solution)/shard_map/ppermute | solution.py:744
  11.9 13.1 %collective-permute-start.3 = (bf16[32,768]{1,0:T(8,128)(2,1)S(1)}, bf16[32,768]{1,0:T(8,128)(2,1)S(1)}, u32[]{:S(2)}, u32[]{:S(2)}) collective-permute-start(bf16[32,768]{1,0:T(8,128)(2,1)S(1)} %get-tuple-element.282), channel_id=1, source_target_pairs={{0,2},{1,3},{2,0},{3,1},{4,6},{5,7},{6,4},{7,5},{8,10},{9,11},{10,... | collective-permute-start | bytes 147464 | tf_op jit(solution)/shard_map/ppermute | solution.py:744
  12.6 12.5 %collective-permute-start.2 = (bf16[32,768]{1,0:T(8,128)(2,1)S(1)}, bf16[32,768]{1,0:T(8,128)(2,1)S(1)}, u32[]{:S(2)}, u32[]{:S(2)}) collective-permute-start(bf16[32,768]{1,0:T(8,128)(2,1)S(1)} %get-tuple-element.283), channel_id=1, source_target_pairs={{0,1},{1,0},{2,3},{3,2},{4,5},{5,4},{6,7},{7,6},{8,9},{9,8},{10,11... | collective-permute-start | bytes 147464 | tf_op jit(solution)/shard_map/ppermute | solution.py:744
  13.5 26.5 %collective-permute-start.5 = (bf16[384,1024]{1,0:T(8,128)(2,1)}, bf16[384,1024]{1,0:T(8,128)(2,1)}, u32[]{:S(2)}, u32[]{:S(2)}) collective-permute-start(bf16[384,1024]{1,0:T(8,128)(2,1)} %bitcast.34), channel_id=1, source_target_pairs={{0,2},{2,0},{1,3},{3,1},{4,6},{6,4},{5,7},{7,5},{8,10},{10,8},{9,1... | collective-permute-start | bytes 2359304 | tf_op jit(solution)/shard_map/ppermute | solution.py:744
  18.7 21.0 %all-to-all-start = ((bf16[8,12,1024]{2,1,0:T(8,128)(2,1)}), bf16[8,12,1024]{2,1,0:T(8,128)(2,1)S(1)}, u32[]{:S(2)}, u32[]{:S(2)}) async-start(bf16[8,12,1024]{2,1,0:T(8,128)(2,1)} %broadcast_in_dim.33), calls=%async_computation | async-start | bytes 524288 | tf_op jit(solution)/shard_map/all_to_all | solution.py:842
  24.5 53.3 %all-gather.5.cloned.1.call-start = ((), (), s32[]{:S(2)}) async-start(), calls=%async_computation.8 | async-start | bytes 1769472 | tf_op jit(solution)/shard_map/all_gather | solution.py:834
  30.7 8.6 %collective-permute-start.1 = (bf16[2,32,2048]{2,1,0:T(8,128)(2,1)S(1)}, bf16[2,32,2048]{2,1,0:T(8,128)(2,1)S(1)}, u32[]{:S(2)}, u32[]{:S(2)}) collective-permute-start(bf16[2,32,2048]{2,1,0:T(8,128)(2,1)S(1)} %bitcast.221), channel_id=1, source_target_pairs={{0,2},{2,0},{1,3},{3,1},{4,6},{6,4},{5,7},{7,5},{8,10},{10,8},{9,1... | collective-permute-start | bytes 786440 | tf_op jit(solution)/shard_map/ppermute | solution.py:744
  40.1 31.5 %collective-permute-start.6 = (bf16[400,1024]{1,0:T(8,128)(2,1)}, bf16[400,1024]{1,0:T(8,128)(2,1)S(1)}, u32[]{:S(2)}, u32[]{:S(2)}) collective-permute-start(bf16[400,1024]{1,0:T(8,128)(2,1)} %slice.203), channel_id=1, source_target_pairs={{0,2},{2,0},{1,3},{3,1},{4,6},{6,4},{5,7},{7,5},{8,10},{10,8},{9,1... | collective-permute-start | bytes 2457608 | tf_op jit(solution)/shard_map/ppermute | solution.py:744
  43.6 27.5 %all-to-all-start.1 = ((f32[32,12,192]{2,1,0:T(8,128)}), f32[32,12,192]{2,1,0:T(8,128)S(1)}, u32[]{:S(2)}, u32[]{:S(2)}) async-start(f32[32,12,192]{2,1,0:T(8,128)} %bitcast.35), calls=%async_computation.1 | async-start | bytes 1048576 | tf_op jit(solution)/shard_map/all_to_all | solution.py:854
  48.6 145.6 %all-gather.7.cloned.1.call-start = ((), (), s32[]{:S(2)}) async-start(), calls=%async_computation.9 | async-start | bytes 8912896 | tf_op jit(solution)/shard_map/all_gather | solution.py:867
  78.8 12.7 %collective-permute-start = (bf16[784,1024]{1,0:T(8,128)(2,1)}, bf16[784,1024]{1,0:T(8,128)(2,1)}, u32[]{:S(2)}, u32[]{:S(2)}) collective-permute-start(bf16[784,1024]{1,0:T(8,128)(2,1)} %fusion.2.one), channel_id=1, source_target_pairs={{0,1},{1,0},{2,3},{3,2},{4,5},{5,4},{6,7},{7,6},{8,9},{9,8},{10,11... | collective-permute-start | bytes 4816904 | tf_op jit(solution)/shard_map/ppermute | solution.py:744
  83.7 20.5 %collective-permute-start.7 = (bf16[784,1024]{1,0:T(8,128)(2,1)}, bf16[784,1024]{1,0:T(8,128)(2,1)}, u32[]{:S(2)}, u32[]{:S(2)}) collective-permute-start(bf16[784,1024]{1,0:T(8,128)(2,1)} %constant_dynamic-update-slice_fusion.one), channel_id=1, source_target_pairs={{0,1},{1,0},{2,3},{3,2},{4,5},{5,4},{6,7},{7,6},{8,9},{9,8},{10,11... | collective-permute-start | bytes 4816904 | tf_op jit(solution)/shard_map/ppermute | solution.py:744
  86.3 57.0 %all-to-all-start.2 = ((bf16[8,2,32,1024]{3,2,1,0:T(8,128)(2,1)}), bf16[8,2,32,1024]{3,2,1,0:T(8,128)(2,1)S(1)}, u32[]{:S(2)}, u32[]{:S(2)}) async-start(bf16[8,2,32,1024]{3,2,1,0:T(8,128)(2,1)} %broadcast_in_dim.38), calls=%async_computation.2 | async-start | bytes 2097152 | tf_op jit(solution)/shard_map/all_to_all | solution.py:897
  91.4 346.6 %reduce-scatter.2.cloned.1.call-start = ((), (), s32[]{:S(2)}) async-start(), calls=%async_computation.10 | async-start | bytes 8912896 | tf_op jit(solution)/shard_map/reduce_scatter | solution.py:940
  94.6 48.8 %collective-permute-start.9 = (bf16[12,64,1024]{2,1,0:T(8,128)(2,1)S(1)}, bf16[12,64,1024]{2,1,0:T(8,128)(2,1)}, u32[]{:S(2)}, u32[]{:S(2)}) collective-permute-start(bf16[12,64,1024]{2,1,0:T(8,128)(2,1)S(1)} %bitcast.187), channel_id=1, source_target_pairs={{0,2},{2,0},{1,3},{3,1},{4,6},{6,4},{5,7},{7,5},{8,10},{10,8},{9,1... | collective-permute-start | bytes 4718600 | tf_op jit(solution)/shard_map/ppermute | solution.py:744
  145.2 35.8 %collective-permute-start.13 = (bf16[256,768]{1,0:T(8,128)(2,1)}, bf16[256,768]{1,0:T(8,128)(2,1)S(1)}, u32[]{:S(2)}, u32[]{:S(2)}) collective-permute-start(bf16[256,768]{1,0:T(8,128)(2,1)} %get-tuple-element.256), channel_id=1, source_target_pairs={{0,3},{1,2},{2,1},{3,0},{4,7},{5,6},{6,5},{7,4},{8,11},{9,10},{10,... | collective-permute-start | bytes 1179656 | tf_op jit(solution)/shard_map/ppermute | solution.py:744
  146.2 34.9 %collective-permute-start.12 = (bf16[256,768]{1,0:T(8,128)(2,1)S(1)}, bf16[256,768]{1,0:T(8,128)(2,1)S(1)}, u32[]{:S(2)}, u32[]{:S(2)}) collective-permute-start(bf16[256,768]{1,0:T(8,128)(2,1)S(1)} %get-tuple-element.257), channel_id=1, source_target_pairs={{0,2},{1,3},{2,0},{3,1},{4,6},{5,7},{6,4},{7,5},{8,10},{9,11},{10,... | collective-permute-start | bytes 1179656 | tf_op jit(solution)/shard_map/ppermute | solution.py:744
  146.8 31.0 %collective-permute-start.10 = (bf16[8,2,32,1024]{3,2,1,0:T(8,128)(2,1)S(1)}, bf16[8,2,32,1024]{3,2,1,0:T(8,128)(2,1)S(1)}, u32[]{:S(2)}, u32[]{:S(2)}) collective-permute-start(bf16[8,2,32,1024]{3,2,1,0:T(8,128)(2,1)S(1)} %all-to-all-done.2), channel_id=1, source_target_pairs={{0,1},{1,0},{2,3},{3,2},{4,5},{5,4},{6,7},{7,6},{8,9},{9,8},{10,11... | collective-permute-start | bytes 3145736 | tf_op jit(solution)/shard_map/ppermute | solution.py:744
  192.8 29.6 %collective-permute-start.14 = (bf16[384,1024]{1,0:T(8,128)(2,1)}, bf16[384,1024]{1,0:T(8,128)(2,1)S(1)}, u32[]{:S(2)}, u32[]{:S(2)}) collective-permute-start(bf16[384,1024]{1,0:T(8,128)(2,1)} %get-tuple-element.144.hidden.refs_0_), channel_id=1, source_target_pairs={{0,2},{2,0},{1,3},{3,1},{4,6},{6,4},{5,7},{7,5},{8,10},{10,8},{9,1... | collective-permute-start | bytes 2359304 | tf_op jit(solution)/shard_map/ppermute | solution.py:744
  208.0 29.9 %collective-permute-start.15 = (bf16[384,1024]{1,0:T(8,128)(2,1)S(1)}, bf16[384,1024]{1,0:T(8,128)(2,1)S(1)}, u32[]{:S(2)}, u32[]{:S(2)}) collective-permute-start(bf16[384,1024]{1,0:T(8,128)(2,1)S(1)} %copy-done.51), channel_id=1, source_target_pairs={{0,2},{2,0},{1,3},{3,1},{4,6},{6,4},{5,7},{7,5},{8,10},{10,8},{9,1... | collective-permute-start | bytes 2359304 | tf_op jit(solution)/shard_map/ppermute | solution.py:744
  236.5 40.1 %collective-permute-start.16 = (bf16[384,1024]{1,0:T(8,128)(2,1)}, bf16[384,1024]{1,0:T(8,128)(2,1)S(1)}, u32[]{:S(2)}, u32[]{:S(2)}) collective-permute-start(bf16[384,1024]{1,0:T(8,128)(2,1)} %get-tuple-element.164), channel_id=1, source_target_pairs={{0,2},{2,0},{1,3},{3,1},{4,6},{6,4},{5,7},{7,5},{8,10},{10,8},{9,1... | collective-permute-start | bytes 2359304 | tf_op jit(solution)/shard_map/ppermute | solution.py:744
  252.2 24.5 %collective-permute-start.17 = (bf16[384,1024]{1,0:T(8,128)(2,1)}, bf16[384,1024]{1,0:T(8,128)(2,1)S(1)}, u32[]{:S(2)}, u32[]{:S(2)}) collective-permute-start(bf16[384,1024]{1,0:T(8,128)(2,1)} %get-tuple-element.165), channel_id=1, source_target_pairs={{0,2},{2,0},{1,3},{3,1},{4,6},{6,4},{5,7},{7,5},{8,10},{10,8},{9,1... | collective-permute-start | bytes 2359304 | tf_op jit(solution)/shard_map/ppermute | solution.py:744
  300.6 55.9 %all-to-all-start.3 = ((bf16[4,8,32,1024]{3,2,1,0:T(8,128)(2,1)}), bf16[4,8,32,1024]{3,2,1,0:T(8,128)(2,1)}, u32[]{:S(2)}, u32[]{:S(2)}) async-start(bf16[4,8,32,1024]{3,2,1,0:T(8,128)(2,1)} %get-tuple-element.175), calls=%async_computation.3 | async-start | bytes 4194304 | tf_op jit(solution)/shard_map/all_to_all | solution.py:951
  305.5 51.0 %collective-permute-start.19 = (bf16[256,768]{1,0:T(8,128)(2,1)}, bf16[256,768]{1,0:T(8,128)(2,1)S(1)}, u32[]{:S(2)}, u32[]{:S(2)}) collective-permute-start(bf16[256,768]{1,0:T(8,128)(2,1)} %get-tuple-element.173), channel_id=1, source_target_pairs={{0,2},{1,3},{2,0},{3,1},{4,6},{5,7},{6,4},{7,5},{8,10},{9,11},{10,... | collective-permute-start | bytes 1179656 | tf_op jit(solution)/shard_map/ppermute | solution.py:744
  307.5 49.0 %collective-permute-start.20 = (bf16[256,768]{1,0:T(8,128)(2,1)}, bf16[256,768]{1,0:T(8,128)(2,1)S(1)}, u32[]{:S(2)}, u32[]{:S(2)}) collective-permute-start(bf16[256,768]{1,0:T(8,128)(2,1)} %get-tuple-element.174), channel_id=1, source_target_pairs={{0,3},{1,2},{2,1},{3,0},{4,7},{5,6},{6,5},{7,4},{8,11},{9,10},{10,... | collective-permute-start | bytes 1179656 | tf_op jit(solution)/shard_map/ppermute | solution.py:744
  359.7 58.7 %all-to-all-start.4 = ((bf16[8,32,1024]{2,1,0:T(8,128)(2,1)}), bf16[8,32,1024]{2,1,0:T(8,128)(2,1)S(1)}, u32[]{:S(2)}, u32[]{:S(2)}) async-start(bf16[8,32,1024]{2,1,0:T(8,128)(2,1)} %reduce_sum.109), calls=%async_computation.4 | async-start | bytes 1048576 | tf_op jit(solution)/shard_map/all_to_all | solution.py:964
  365.7 52.7 %collective-permute-start.21 = (bf16[384,1024]{1,0:T(8,128)(2,1)}, bf16[384,1024]{1,0:T(8,128)(2,1)}, u32[]{:S(2)}, u32[]{:S(2)}) collective-permute-start(bf16[384,1024]{1,0:T(8,128)(2,1)} %get-tuple-element.185), channel_id=1, source_target_pairs={{0,2},{2,0},{1,3},{3,1},{4,6},{6,4},{5,7},{7,5},{8,10},{10,8},{9,1... | collective-permute-start | bytes 2359304 | tf_op jit(solution)/shard_map/ppermute | solution.py:744
  367.3 51.1 %collective-permute-start.22 = (bf16[384,1024]{1,0:T(8,128)(2,1)}, bf16[384,1024]{1,0:T(8,128)(2,1)}, u32[]{:S(2)}, u32[]{:S(2)}) collective-permute-start(bf16[384,1024]{1,0:T(8,128)(2,1)} %get-tuple-element.186), channel_id=1, source_target_pairs={{0,2},{2,0},{1,3},{3,1},{4,6},{6,4},{5,7},{7,5},{8,10},{10,8},{9,1... | collective-permute-start | bytes 2359304 | tf_op jit(solution)/shard_map/ppermute | solution.py:744
  455.8 79.9 %all-to-all-start.5 = ((bf16[32,38,768]{2,1,0:T(8,128)(2,1)}), bf16[32,38,768]{2,1,0:T(8,128)(2,1)S(1)}, u32[]{:S(2)}, u32[]{:S(2)}) async-start(bf16[32,38,768]{2,1,0:T(8,128)(2,1)} %pad_maximum_fusion.2), calls=%async_computation.6 | async-start | bytes 3932160 | tf_op jit(solution)/shard_map/all_to_all | solution.py:1001
  461.9 63.9 %all-gather.9.cloned.1.call-start = ((), (), s32[]{:S(2)}) async-start(), calls=%async_computation.11 | async-start | bytes 4718592 | tf_op jit(solution)/shard_map/all_gather | solution.py:977
  472.0 19.3 %collective-permute-start.25 = (bf16[2,32,2048]{2,1,0:T(8,128)(2,1)S(1)}, bf16[2,32,2048]{2,1,0:T(8,128)(2,1)S(1)}, u32[]{:S(2)}, u32[]{:S(2)}) collective-permute-start(bf16[2,32,2048]{2,1,0:T(8,128)(2,1)S(1)} %bitcast.219), channel_id=1, source_target_pairs={{0,2},{2,0},{1,3},{3,1},{4,6},{6,4},{5,7},{7,5},{8,10},{10,8},{9,1... | collective-permute-start | bytes 786440 | tf_op jit(solution)/shard_map/ppermute | solution.py:744
  475.8 52.6 %collective-permute-start.24 = (bf16[768,1024]{1,0:T(8,128)(2,1)}, bf16[768,1024]{1,0:T(8,128)(2,1)}, u32[]{:S(2)}, u32[]{:S(2)}) collective-permute-start(bf16[768,1024]{1,0:T(8,128)(2,1)} %get-tuple-element.250), channel_id=1, source_target_pairs={{0,1},{1,0},{2,3},{3,2},{4,5},{5,4},{6,7},{7,6},{8,9},{9,8},{10,11... | collective-permute-start | bytes 4718600 | tf_op jit(solution)/shard_map/ppermute | solution.py:744
  (60 other events, 414.1 us)
Sparse Core Ops, SparseCore 0:
  27.9 49.8 all-gather.4
  80.6 94.9 all-gather.6
  276.8 117.6 reduce-scatter.1
  468.8 56.9 all-gather.8

commit v7 on v6

--- a/solution.py
+++ b/solution.py
@@ -84,13 +84,25 @@
     return jnp.concatenate(out, axis=0)
 
 
-def qkv_kernel(half, one, two, mod, weight, cosine, sine, out):
-    step = pl.program_id(0)
-    values = jnp.where(step < half, one[...].astype(f32), two[...].astype(f32))
+def hold_piece(pieces, held):
+    for index, piece in enumerate(pieces):
+
+        @pl.when(pl.program_id(0) == index)
+        def _(piece=piece):
+            held[...] = piece[...]
+
+    return held[...].astype(f32)
+
+
+def modulated(values, mod):
     count, width = values.shape
     normed, _ = layer_norm(values.reshape(mod.shape[0], -1, width))
     hidden = normed * (1.0 + mod[:, 1:2, :]) + mod[:, 0:1, :]
-    hidden = hidden.astype(bf16).reshape(count, width)
+    return normed, hidden.astype(bf16).reshape(count, width)
+
+
+def qkv_kernel(one, two, three, four, mod, weight, cosine, sine, out, held):
+    _, hidden = modulated(hold_piece((one, two, three, four), held), mod)
     projected = dot(weight[...], hidden, NT)
     third = projected.shape[0] // 3
     cos, sin = cosine[...], sine[...]
@@ -101,31 +113,31 @@
     out[2 * third :, :] = projected[2 * third :].astype(bf16)
 
 
-def token_specs(frames, block, width, chunk):
-    half = frames // chunk
-    return half, [
-        pl.BlockSpec((block, width), lambda i: (jnp.minimum(i, half - 1), 0)),
-        pl.BlockSpec((block, width), lambda i: (jnp.maximum(i - half, 0), 0)),
-        pl.BlockSpec((chunk, 6, width), lambda i: (lax.rem(i, half), 0, 0)),
+def token_specs(pieces, frames, block, width):
+    def piece_spec(index):
+        return pl.BlockSpec((block, width), lambda i: (index, 0))
+
+    return [piece_spec(index) for _, index in pieces] + [
+        pl.BlockSpec((frames // 2, 6, width), lambda i: (lax.rem(i, 2), 0, 0))
     ]
 
 
-def project_qkv(one, two, mod, weight, cosine, sine):
+def project_qkv(pieces, mod, weight, cosine, sine):
     total, width = cosine.shape[1], weight.shape[1]
-    frames, chunk = mod.shape[0], 4
-    block = total // 2 // frames * chunk
-    half, specs = token_specs(frames, block, width, chunk)
+    block = total // 4
+    specs = token_specs(pieces, mod.shape[0], block, width)
     rows = weight.shape[0]
     angle = pl.BlockSpec((cosine.shape[0], block), lambda i: (0, i))
     return pl.pallas_call(
-        functools.partial(qkv_kernel, half),
-        grid=(2 * half,),
+        qkv_kernel,
+        grid=(4,),
         in_specs=specs + [whole(), angle, angle],
         out_specs=pl.BlockSpec((rows, block), lambda i: (0, i)),
         out_shape=jax.ShapeDtypeStruct((rows, total), bf16),
+        scratch_shapes=[VMEM((block, width), bf16)],
         compiler_params=params(),
         cost_estimate=cost(2 * rows * total * width, 4 * total * width),
-    )(one, two, mod, weight, cosine, sine)
+    )(*[piece for piece, _ in pieces], mod, weight, cosine, sine)
 
 
 def attend_kernel(heads, q_ref, k1, k2, v1, v2, bias, out, lse, k_wide, v_wide):
@@ -333,12 +345,19 @@
     )(*operands)
 
 
-def project_kernel(order, a0, a1, a2, a3, proj, tokens, cotangent, mod, att_out, hid1, hid2, branch):
+def project_kernel(
+    order, a0, a1, a2, a3, weight, tokens, cotangent, mod, att_out, hid1, hid2, branch, proj
+):
     features = a1.shape[0]
+
+    @pl.when(pl.program_id(0) == 0)
+    def _():
+        proj[...] = jnp.transpose(weight[...])
+
     mixed = None
     for slot, part in enumerate((a0.at[0], a1, a2, a3)):
-        columns = proj[:, pl.ds(pl.multiple_of(order[slot] * features, features), features)]
-        term = dot(part[...], columns, TT)
+        place = pl.ds(pl.multiple_of(order[slot] * features, features), features)
+        term = dot(part[...], proj[place, :], TN)
         mixed = term if mixed is None else mixed + term
     shape = tokens.shape
     mixed = mixed.reshape(shape)
@@ -363,8 +382,8 @@
 
 def project_out(order, parts, proj, tokens, cotangent, mod):
     frames, per_frame, width = tokens.shape
-    chunk = 2
-    half = frames // chunk // 2
+    chunk = frames // 2
+    half = 1
     block = chunk * per_frame
     features = parts[1].shape[0]
     cube = pl.BlockSpec((chunk, per_frame, width), lambda i: (i, 0, 0))
@@ -382,12 +401,14 @@
             pl.BlockSpec((block, width), lambda i: (jnp.minimum(i, half - 1), 0)),
             pl.BlockSpec((block, width), lambda i: (jnp.maximum(i - half, 0), 0)),
             flat,
+            whole(),
         ],
         out_shape=[
             jax.ShapeDtypeStruct(tokens.shape, f32),
             jax.ShapeDtypeStruct((count // 2, width), bf16),
             jax.ShapeDtypeStruct((count // 2, width), bf16),
             jax.ShapeDtypeStruct((count, width), bf16),
+            jax.ShapeDtypeStruct((width, width), bf16),
         ],
         compiler_params=params(),
         cost_estimate=cost(2 * frames * per_frame * width * width, 14 * frames * per_frame * width),
@@ -484,12 +505,15 @@
 def feed_weight_kernel(parts, *refs):
     hidden, branch = refs[:parts], refs[parts : 2 * parts]
     active, wide = refs[2 * parts : 3 * parts], refs[3 * parts : 4 * parts]
-    grads = refs[-1]
-    for kind, left, right in ((0, hidden, wide), (1, branch, active)):
-        total = None
-        for one, two in zip(left, right):
-            term = dot(one[...], two[...], TN)
-            total = term if total is None else total + term
+    grads, turned = refs[-2:]
+
+    @pl.when(pl.program_id(0) == 0)
+    def _():
+        turned[0] = jnp.transpose(jnp.concatenate([value[...] for value in hidden], axis=0))
+        turned[1] = jnp.transpose(jnp.concatenate([value[...] for value in branch], axis=0))
+
+    for kind, right in ((0, wide), (1, active)):
+        total = dot(turned[kind], jnp.concatenate([value[...] for value in right], axis=0))
         total = total.astype(bf16)
         rows = grads.shape[3]
         for at, (group, x) in enumerate(weight_places(grads.shape)):
@@ -518,6 +542,7 @@
         + [moving(value) for value in (*active, *wide)],
         out_specs=pl.BlockSpec(shape[:-1] + (block,), lambda i: (0, 0, 0, 0, i)),
         out_shape=jax.ShapeDtypeStruct(shape, bf16),
+        scratch_shapes=[VMEM((2, width, count), bf16)],
         compiler_params=params(),
         cost_estimate=cost(4 * count * width * units, 4 * width * units + 4 * count * units),
     )(*hidden, *branch, *active, *wide)
@@ -546,7 +571,7 @@
     features = a1.shape[0]
     for slot, (part, out) in enumerate(((a0.at[0], d0), (a1, d1), (a2, d2), (a3, d3))):
         place = pl.ds(pl.multiple_of(order[slot] * features, features), features)
-        out[...] = dot(proj[:, place], grad, TT).astype(bf16)
+        out[...] = dot(proj[place, :], grad, NT).astype(bf16)
         term = dot(part[...], grad)
 
         @pl.when(step == 0)
@@ -559,21 +584,13 @@
 
     @pl.when(step == pl.num_programs(0) - 1)
     def _():
-        turned = jnp.transpose(raw_sum[...])
-        groups, owners, rows, _ = proj_raw.shape
-        for group in range(groups):
-            some = [
-                turned[(owner * groups + group) * rows : (owner * groups + group + 1) * rows]
-                for owner in range(owners)
-            ]
-            some = jnp.concatenate(some, axis=0).astype(bf16)
-            proj_raw[group] = some.reshape(proj_raw.shape[1:])
-
-
-def middle_back(order, into, tokens, cotangent, att_out, mod, parts, proj, owners):
+        proj_raw[...] = jnp.transpose(raw_sum[...]).astype(bf16)
+
+
+def middle_back(order, into, tokens, cotangent, att_out, mod, parts, proj):
     frames, per_frame, width = tokens.shape
-    chunk = 2
-    half = frames // chunk // 2
+    chunk = frames // 2
+    half = 1
     block = chunk * per_frame
     features = parts[1].shape[0]
     cube = pl.BlockSpec((chunk, per_frame, width), lambda i: (i, 0, 0))
@@ -596,7 +613,7 @@
             jax.ShapeDtypeStruct((frames, 3, width), f32),
         ]
         + [jax.ShapeDtypeStruct((features, frames * per_frame), bf16)] * 4
-        + [jax.ShapeDtypeStruct(owners + (width // (owners[0] * owners[1]), width), bf16)],
+        + [jax.ShapeDtypeStruct((width, width), bf16)],
         scratch_shapes=[VMEM((width, width), f32)],
         compiler_params=params(),
         cost_estimate=cost(4 * frames * per_frame * width * width, 24 * frames * per_frame * width),
@@ -614,8 +631,8 @@
 
 def block_output(parts, tokens, att_out, mod):
     frames, per_frame, width = tokens.shape
-    chunk = 2
-    half = frames // chunk // 2
+    chunk = frames // 2
+    half = 1
     block = chunk * per_frame
     cube = pl.BlockSpec((chunk, per_frame, width), lambda i: (i, 0, 0))
     one = pl.BlockSpec((block, width), lambda i: (jnp.minimum(i, half - 1), 0))
@@ -632,11 +649,11 @@
     )(*parts, tokens, att_out, mod)
 
 
-def first_back_kernel(half, last, one, two, mod, dq, dk, dv, weight, *rest):
+def first_back_kernel(last, one, two, three, four, mod, dq, dk, dv, weight, *rest):
     if last:
-        raw_in, mod_in, grads, raw, mod_grad, total = rest
+        raw_in, mod_in, grads, raw, mod_grad, total, held = rest
     else:
-        grads, total, mod_grad = rest
+        grads, total, mod_grad, held = rest
     step = pl.program_id(0)
     chunk = mod.shape[0]
 
@@ -645,18 +662,14 @@
         total[...] = raw_in[...] if last else jnp.zeros_like(total)
         mod_grad[...] = mod_in[...] if last else jnp.zeros_like(mod_grad)
 
-    values = jnp.where(step < half, one[...].astype(f32), two[...].astype(f32))
-    count, width = values.shape
-    shape = (chunk, count // chunk, width)
-    normed, _ = layer_norm(values.reshape(shape))
-    hidden = normed * (1.0 + mod[:, 1:2, :]) + mod[:, 0:1, :]
-    hidden = hidden.astype(bf16).reshape(count, width)
+    normed, hidden = modulated(hold_piece((one, two, three, four), held), mod)
+    shape = normed.shape
     pieces = jnp.concatenate([dq[...], dk[...], dv[...]], axis=0)
     total[...] += dot(pieces, hidden)
     back = dot(pieces, weight[...], TN)
     grads[...] = back.astype(bf16).reshape(grads.shape)
     back = back.reshape(shape)
-    place = pl.ds(lax.rem(step, half) * chunk, chunk)
+    place = pl.ds(lax.rem(step, 2) * chunk, chunk)
     mod_grad[place, 0:1] += jnp.sum(back, axis=1, keepdims=True)
     mod_grad[place, 1:2] += jnp.sum(back * normed, axis=1, keepdims=True)
 
@@ -667,30 +680,30 @@
             raw[...] = jnp.transpose(total[...]).astype(bf16)
 
 
-def first_back(one, two, mod, dq, dk, dv, weight, offset, sums=None):
+def first_back(pieces, mod, dq, dk, dv, weight, offset, sums=None):
     rows, count = dq.shape
     frames, width = mod.shape[0], weight.shape[1]
-    chunk, tokens = 4, count // 2 // frames
-    block = chunk * tokens
-    half, specs = token_specs(frames, block, width, chunk)
+    block = count // 4
+    specs = token_specs(pieces, frames, block, width)
     last = sums is not None
-    moved = pl.BlockSpec((rows, block), lambda i: (0, i + offset * 2 * half))
+    moved = pl.BlockSpec((rows, block), lambda i: (0, i + offset * 4))
     in_specs = specs + [pl.BlockSpec((rows, block), lambda i: (0, i)), moved, moved, whole()]
-    operands = [one, two, mod, dq, dk, dv, weight]
-    grads = jax.ShapeDtypeStruct((2, frames * tokens, width), bf16)
-    grads_spec = pl.BlockSpec((1, block, width), lambda i: (i // half, lax.rem(i, half), 0))
+    operands = [piece for piece, _ in pieces] + [mod, dq, dk, dv, weight]
+    grads = jax.ShapeDtypeStruct((2, count // 2, width), bf16)
+    grads_spec = pl.BlockSpec((1, block, width), lambda i: (i // 2, lax.rem(i, 2), 0))
+    held = VMEM((block, width), bf16)
     mods = jax.ShapeDtypeStruct((frames, 2, width), f32)
     if last:
         in_specs += [whole(), whole()]
         operands += list(sums)
         out_shape = [grads, jax.ShapeDtypeStruct((width, 3 * rows), bf16), mods]
-        scratch = [VMEM((3 * rows, width), f32)]
+        scratch = [VMEM((3 * rows, width), f32), held]
     else:
         out_shape = [grads, jax.ShapeDtypeStruct((3 * rows, width), f32), mods]
-        scratch = []
+        scratch = [held]
     return pl.pallas_call(
-        functools.partial(first_back_kernel, half, last),
-        grid=(2 * half,),
+        functools.partial(first_back_kernel, last),
+        grid=(4,),
         in_specs=in_specs,
         out_specs=[grads_spec, whole(), whole()],
         out_shape=out_shape,
@@ -826,6 +839,7 @@
     tok0 = jnp.concatenate([own.reshape(count, width), small], axis=0)
     tok1 = swap(tok0, ROW, rows, 1)
     tok2_one = swap(tok0[: count // 2], "x", 2, 1)
+    tok3_one = swap(tok2_one, "core", 2, 1)
 
     shard = widen_weight.shape[0]
     attend_mine = attend_weight.astype(bf16).reshape(shard, 3, rows, features)
@@ -861,8 +875,7 @@
     feed_mine, attend_full, mod, tok2_two = lax.optimization_barrier(
         (feed_mine, attend_full, mod, tok2_two)
     )
-    tok2 = jnp.concatenate([tok2_one, tok2_two], axis=0)
-    tok3 = swap(tok2, ROW, rows, 1)
+    tok3_two = swap(tok2_two, "core", 2, 1)
     attend_turned = attend_full.T
     feed_full = lax.all_gather(
         feed_mine.reshape(4 * shard, units // 2), ("clip", "core"), axis=0, tiled=True
@@ -878,18 +891,21 @@
 
     def places_of(pieces):
         small = [
-            piece[count : count + 3 * spare].reshape(3, spare * width)[:, :count]
-            for piece in pieces
+            piece[-16 : 3 * spare - 16].reshape(3, spare * width)[:, :count] for piece in pieces
         ]
         small = jnp.concatenate(small, axis=1).astype(f32)
         angles = jnp.concatenate([freqs * small[0:1], freqs * small[1:2]], axis=0)
         return jnp.cos(angles), jnp.sin(angles), jnp.where(small[2:3] > 0.5, 0.0, MASKED)
 
     cos_near, sin_near, bias_near = places_of((tok0, tok1))
-    qkv_near = project_qkv(tok0, tok1, mod, attend_turned, cos_near, sin_near)
-    qkv_near, tok3 = lax.optimization_barrier((qkv_near, tok3))
-    cos_far, sin_far, bias_far = places_of((tok2, tok3))
-    qkv_far = project_qkv(tok2, tok3, mod, attend_turned, cos_far, sin_far)
+    near = ((tok0, 0), (tok0, 1), (tok1, 0), (tok1, 1))
+    qkv_near = project_qkv(near, mod, attend_turned, cos_near, sin_near)
+    qkv_near, tok2_one, tok2_two, tok3_one, tok3_two, project_mine = lax.optimization_barrier(
+        (qkv_near, tok2_one, tok2_two, tok3_one, tok3_two, project_mine)
+    )
+    cos_far, sin_far, bias_far = places_of((tok2_two, tok3_two))
+    across = ((tok2_one, 0), (tok2_two, 0), (tok3_one, 0), (tok3_two, 0))
+    qkv_far = project_qkv(across, mod, attend_turned, cos_far, sin_far)
     cosine = jnp.concatenate([cos_near, cos_far], axis=1)
     sine = jnp.concatenate([sin_near, sin_far], axis=1)
     bias = jnp.concatenate([bias_near, bias_far], axis=1)
@@ -914,7 +930,7 @@
     project_full = project_full.transpose(1, 2, 0, 3, 4).reshape(width, width)
     branch_far = (mod[:, 5:6, :] * cot_far.astype(f32)).astype(bf16).reshape(count, width)
     parts = [out_near, part1, part2, part3]
-    att_out, hid1, hid2, branch = project_out(order, parts, project_full, own, upstream, mod)
+    att_out, hid1, hid2, branch, project_turned = project_out(order, parts, project_full, own, upstream, mod)
 
     far1 = swap(hid1, "x", 2, 1)
     out1, in1, act1, wide1, gate1 = feed_forward(feed_full, hid1, branch, upstream, 0, f32)
@@ -944,11 +960,13 @@
         tiled=True,
     ).reshape(2, 2, shard, units // 2)
     middle_grad, mod_late, d0, d1, d2, d3, project_raw = middle_back(
-        order, (in1, in2, in3, in4), own, upstream, att_out, mod, parts, project_full, (rows, clips)
+        order, (in1, in2, in3, in4), own, upstream, att_out, mod, parts, project_turned
     )
     mod_gate = jnp.concatenate([gate1 + gate3, gate2 + gate4], axis=0)
 
-    project_raw = lax.all_to_all(project_raw, ROW, 0, 0, tiled=True)
+    project_raw = lax.all_to_all(
+        project_raw.reshape(devices, shard, width), both, 0, 0, tiled=True
+    )
 
     turning = (cosine, sine)
     d2 = swap(d2, ROW, rows, 2)
@@ -957,33 +975,31 @@
     dq_near, dk, dv = attend_back(
         qkv_near, qkv_near, qkv_far, bias, out_near, (d0, d1), lse_near, turning, 0
     )
-    dk, d2, d3, project_raw, out3, out4 = lax.optimization_barrier(
-        (dk, d2, d3, project_raw, out3, out4)
-    )
-    project_raw = jnp.sum(project_raw.astype(f32), axis=0).astype(bf16)
-    project_raw = lax.all_to_all(project_raw, "clip", 0, 0, tiled=True)
+    dk, d2, d3, out3, out4 = lax.optimization_barrier((dk, d2, d3, out3, out4))
     out3 = swap(out3, "x", 2, 1)
     out4 = swap(out4, "x", 2, 1)
     dq_far, dk, dv = attend_back(
         qkv_far, qkv_near, qkv_far, bias, out_far, (d2, d3), lse_far, turning, 1, (dk, dv)
     )
-    dq_far, project_raw, out3, out4 = lax.optimization_barrier((dq_far, project_raw, out3, out4))
-    project_sum = jnp.sum(project_raw.astype(f32), axis=0).T
-    back_far, raw, mod_early = first_back(tok2, tok3, mod, dq_far, dk, dv, attend_turned, 1)
+    dq_far, project_raw, out3, out4, feed_sum = lax.optimization_barrier(
+        (dq_far, project_raw, out3, out4, feed_sum)
+    )
+    feed_sum = trade(relative(feed_sum, far), "x", 2)
+    back_far, raw, mod_early = first_back(across, mod, dq_far, dk, dv, attend_turned, 1)
     back_far = (
         back_far[0].astype(f32) + swap(back_far[1], ROW, rows, 1).astype(f32)
     ).astype(bf16)
     back_far, dq_near, feed_sum = lax.optimization_barrier((back_far, dq_near, feed_sum))
     back_far = lax.all_gather(back_far, "x", axis=0)
     back_far = lax.dynamic_index_in_dim(back_far, 1 - far, 0, keepdims=False)
-    feed_sum = relative(trade(relative(feed_sum, far), "x", 2), far).astype(f32)
+    feed_sum = relative(feed_sum, far).astype(f32)
     widen_sum, narrow_sum = feed_sum.transpose(1, 2, 0, 3).reshape(2, shard, units)
     narrow_sum = narrow_sum.T
     extra = -(-2 * frames * part // (3 * features))
     back_near, attend_raw, mod_early = first_back(
-        tok0, tok1, mod, dq_near, dk, dv, attend_turned, 0, (raw, mod_early)
-    )
-    back_near = (back_near[0], swap(back_near[1], ROW, rows, 1), back_far)
+        near, mod, dq_near, dk, dv, attend_turned, 0, (raw, mod_early)
+    )
+    back_near = (back_near[0], swap(back_near[1], ROW, rows, 1))
 
     mod_grad = jnp.concatenate([mod_early, mod_late, mod_gate], axis=1)
     mod_grad = mod_grad.reshape(frames, devices, part).transpose(1, 0, 2).reshape(devices, -1)
@@ -999,10 +1015,12 @@
         axis=1,
     )
     attend_raw = lax.all_to_all(attend_raw, both, 0, 0, tiled=True)
+    out3, back_far, project_raw = lax.optimization_barrier((out3, back_far, project_raw))
+    project_sum = total_over(project_raw.reshape(devices, 1, shard, width))[0].T
     block_out = block_output((out1, out2, out3, out4), own, att_out, mod)
-    input_gradient = input_back(own, mod, middle_grad, back_near)
-    attend_raw, input_gradient, block_out = lax.optimization_barrier(
-        (attend_raw, input_gradient, block_out)
+    input_gradient = input_back(own, mod, middle_grad, back_near + (back_far,))
+    attend_raw, input_gradient, block_out, project_sum = lax.optimization_barrier(
+        (attend_raw, input_gradient, block_out, project_sum)
     )
     small = attend_raw[:, shard : shard + extra].reshape(devices, -1)[:, : 2 * frames * part]
     small = small.astype(f32).reshape(clips, rows, 2, frames, part)

time: 594 us -> 607 us (1.022)
  waiting for transfers between devices: 78.3 us -> 107 us
  starting transfers between devices: 55.1 us -> 47.8 us
    all_gather x1, waiting for transfers between devices: 28.8 us -> 50.4 us  [local(): back_far = lax.all_gather(back_far, 'x', axis=0)]
    reduce_scatter x1, waiting for transfers between devices: 0.01 us -> 12.4 us  [local(): lax.psum_scatter(feed_raw.reshape(8 * clips * shard, units // 2), ('clip'...]
    ppermute x26 -> x27, waiting for transfers between devices: 24.1 us -> 16.8 us  [swap(): lax.ppermute(value, axis, [(place, place ^ step) for place in range(size)])]
    all_to_all x2 -> x1, starting transfers between devices: 10.8 us -> 4.02 us  [local(): lax.all_to_all(project_raw.reshape(devices, shard, width), both, 0, 0, ti...]
    ppermute x26 -> x27, starting transfers between devices: 22 us -> 22.9 us  [swap(): lax.ppermute(value, axis, [(place, place ^ step) for place in range(size)])]
  transfers between devices with their start and end apart: 36 -> 36, of which waited for: 6 -> 8; matrix products, arithmetic and copies ran while one was open for 10% -> 8% of each run, Pallas kernels for 53% -> 49%
where the time goes in v7:
time: 607 us; the launch traced here: 598 us
  Pallas kernels  322 us (53%)
  waiting for transfers between devices  107 us (18%)
  starting transfers between devices  47.8 us (8%)
  other arithmetic  45.8 us (8%)
  local copies, waits for them, and re-layouts  38.2 us (6%)
  between operations  22.1 us (4%)
  blocking collectives  12.5 us (2%)
    pallas_call x2, Pallas kernels, attend_back(): pl.pallas_call(functools.partial(attend_back_kernel, heads, last), grid=(...  99.2 us
    pallas_call x2, Pallas kernels, attend(): pl.pallas_call(functools.partial(attend_kernel, heads), grid=(count // bl...  54.9 us
    pallas_call x4, Pallas kernels, feed_forward(): pl.pallas_call(feed_kernel, grid=(units // block,), in_specs=[spec, flat,...  54.3 us
    all_gather x1, waiting for transfers between devices, local(): back_far = lax.all_gather(back_far, 'x', axis=0)  50.4 us
    pallas_call x2, Pallas kernels, first_back(): pl.pallas_call(functools.partial(first_back_kernel, last), grid=(4,), in_...  27.7 us
    ppermute x27, starting transfers between devices, swap(): lax.ppermute(value, axis, [(place, place ^ step) for place in range(size)])  22.9 us
    pallas_call x1, Pallas kernels, feed_weights(): pl.pallas_call(functools.partial(feed_weight_kernel, len(hidden)), grid=(...  21 us
    all_to_all x1, waiting for transfers between devices, local(): lax.all_to_all(mod_mine.reshape(devices, frames, part), both, 0, 0, tiled...  20.5 us
  transfers between devices with their start and end apart: 36, of which 8 were waited for; matrix products, arithmetic and copies ran while one was open for 8% of the time, Pallas kernels for 49%

profile of v7, /device:TPU:0, one launch (start us, length us, event | category | flops | bytes accessed | tf_op | source)
XLA Modules:
  0.0 598.5 jit_solution(4563262277519359663)
XLA Ops:
  17.4 5.8 all-to-all-start
  32.0 7.3 %collective-permute-done.1 = bf16[2,32,2048]{2,1,0:T(8,128)(2,1)S(1)} collective-permute-done((bf16[2,32,2048]{2,1,0:T(8,128)(2,1)S(1)}, bf16[2,32,2048]{2,1,0:T(8,128)(2,1)S(1)}, u32[]{:S(2)}, u32[]{:S(2)}) %collective-permute-start.1) | collective-permute-done | bytes 262176 | tf_op jit(solution)/shard_map/ppermute | solution.py:757
  46.1 5.1 all-to-all-start.1
  54.6 20.5 %all-to-all-done.1 = f32[32,12,192]{2,1,0:T(8,128)} async-done(((f32[32,12,192]{2,1,0:T(8,128)}), f32[32,12,192]{2,1,0:T(8,128)}, u32[]{:S(2)}, u32[]{:S(2)}) %all-to-all-start.1) | async-done | bytes 294944 | tf_op jit(solution)/shard_map/all_to_all | solution.py:868
  89.4 9.6 %shard_map.487.k1.v1.q_ref = bf16[768,1536]{1,0:T(8,128)(2,1)} custom-call(bf16[784,1024]{1,0:T(8,128)(2,1)} %copy-done.1, bf16[784,1024]{1,0:T(8,128)(2,1)} %copy-done.1, bf16[784,1024]{1,0:T(8,128)(2,1)} %collective-permute-done.three.four, bf16[784,1024]{1,0:T(8,128)(2,1)} %collective-permute-done.three.four, f32[12,6,1024]{2,1,0:T(8,128)} %copy-done.2, ...), custom_call_target="tpu_custom_call" | custom-call | flops 2415919104 | bytes 6291456 | tf_op jit(solution)/shard_map/pallas_call | solution.py:131
  101.1 5.0 all-to-all-start.2
  108.4 9.2 %shard_map.488.q_ref.k2.v2 = bf16[768,1536]{1,0:T(8,128)(2,1)} custom-call(bf16[384,1024]{1,0:T(8,128)(2,1)} %collective-permute-done.5.one, bf16[400,1024]{1,0:T(8,128)(2,1)} %collective-permute-done.6.two, bf16[384,1024]{1,0:T(8,128)(2,1)} %collective-permute-done.7.three, bf16[400,1024]{1,0:T(8,128)(2,1)} %copy-done.52, f32[12,6,1024]{2,1,0:T(8,128)} %copy-done.2, ...), custom_call_target="tpu_custom_call" | custom-call | flops 2415919104 | bytes 6291456 | tf_op jit(solution)/shard_map/pallas_call | solution.py:131
  117.6 27.3 %shard_map.489 = (bf16[2,256,768]{2,1,0:T(8,128)(2,1)}, f32[4,1536]{1,0:T(4,128)}) custom-call(bf16[768,1536]{1,0:T(8,128)(2,1)} %shard_map.488.q_ref.k2.v2, bf16[768,1536]{1,0:T(8,128)(2,1)} %shard_map.487.k1.v1.q_ref, bf16[768,1536]{1,0:T(8,128)(2,1)} %shard_map.488.q_ref.k2.v2, bf16[768,1536]{1,0:T(8,128)(2,1)} %shard_map.487.k1.v1.q_ref, ...), custom_call_target="tpu_custom_call" | custom-call | flops 19327352832 | bytes 3145728 | tf_op jit(solution)/shard_map/pallas_call | solution.py:186
  144.9 4.2 all-to-all-done.2
  152.8 27.6 %shard_map.490 = (bf16[2,256,768]{2,1,0:T(8,128)(2,1)}, f32[4,1536]{1,0:T(4,128)}) custom-call(bf16[768,1536]{1,0:T(8,128)(2,1)} %shard_map.487.k1.v1.q_ref, bf16[768,1536]{1,0:T(8,128)(2,1)} %shard_map.487.k1.v1.q_ref, bf16[768,1536]{1,0:T(8,128)(2,1)} %shard_map.488.q_ref.k2.v2, bf16[768,1536]{1,0:T(8,128)(2,1)} %shard_map.487.k1.v1.q_ref, ...), custom_call_target="tpu_custom_call" | custom-call | flops 19327352832 | bytes 3145728 | tf_op jit(solution)/shard_map/pallas_call | solution.py:186
  180.5 3.1 multiply_convert_fusion
  187.6 9.5 %shard_map.491 = (f32[12,64,1024]{2,1,0:T(8,128)}, bf16[384,1024]{1,0:T(8,128)(2,1)}, bf16[384,1024]{1,0:T(8,128)(2,1)}, bf16[768,1024]{1,0:T(8,128)(2,1)}, bf16[1024,1024]{1,0:T(8,128)(2,1)}) custom-call(s32[4]{0:T(128)} %iota_xor_fusion.order, bf16[2,256,768]{2,1,0:T(8,128)(2,1)} %get-tuple-element.154.a0.out_ref, bf16[256,768]{1,0:T(8,128)(2,1)} %copy-done.23, ...), custom_call_target="tpu_custom_call" | custom-call | flops 1610612736 | bytes 11010048 | tf_op jit(solution)/shard_map/pallas_call | solution.py:392
  198.5 13.9 %shard_map.492 = (f32[384,1024]{1,0:T(8,128)}, f32[384,1024]{1,0:T(8,128)}, bf16[384,2048]{1,0:T(8,128)(2,1)}, bf16[384,2048]{1,0:T(8,128)(2,1)}, f32[6,1,1024]{2,1,0:T(1,128)}) custom-call(bf16[16,2,2,32,2048]{4,3,2,1,0:T(8,128)(2,1)} %bitcast.232, bf16[384,1024]{1,0:T(8,128)(2,1)} %get-tuple-element.157.hidden.refs_0_, ...), custom_call_target="tpu_custom_call" | custom-call | flops 6442450944 | bytes 11534336 | tf_op jit(solution)/shard_map/pallas_call | solution.py:486
  213.0 13.8 %shard_map.493 = (f32[384,1024]{1,0:T(8,128)}, f32[384,1024]{1,0:T(8,128)}, bf16[384,2048]{1,0:T(8,128)(2,1)}, bf16[384,2048]{1,0:T(8,128)(2,1)}, f32[6,1,1024]{2,1,0:T(1,128)}) custom-call(bf16[16,2,2,32,2048]{4,3,2,1,0:T(8,128)(2,1)} %bitcast.233, bf16[384,1024]{1,0:T(8,128)(2,1)} %get-tuple-element.165.hidden.refs_1_, ...), custom_call_target="tpu_custom_call" | custom-call | flops 6442450944 | bytes 11534336 | tf_op jit(solution)/shard_map/pallas_call | solution.py:486
  227.7 13.2 %shard_map.494 = (bf16[384,1024]{1,0:T(8,128)(2,1)}, bf16[384,1024]{1,0:T(8,128)(2,1)}, bf16[384,2048]{1,0:T(8,128)(2,1)}, bf16[384,2048]{1,0:T(8,128)(2,1)}, f32[6,1,1024]{2,1,0:T(1,128)}) custom-call(bf16[16,2,2,32,2048]{4,3,2,1,0:T(8,128)(2,1)} %bitcast.234, bf16[384,1024]{1,0:T(8,128)(2,1)} %copy-done.54, bf16[768,1024]{1,0:T(8,128)(2,1)} %bitcast.207, ...), custom_call_target="tpu_custom_call" | custom-call | flops 6442450944 | bytes 11534336 | tf_op jit(solution)/shard_map/pallas_call | solution.py:486
  243.1 13.5 %shard_map.495 = (bf16[384,1024]{1,0:T(8,128)(2,1)}, bf16[384,1024]{1,0:T(8,128)(2,1)}, bf16[384,2048]{1,0:T(8,128)(2,1)}, bf16[384,2048]{1,0:T(8,128)(2,1)}, f32[6,1,1024]{2,1,0:T(1,128)}) custom-call(bf16[16,2,2,32,2048]{4,3,2,1,0:T(8,128)(2,1)} %bitcast.235, bf16[384,1024]{1,0:T(8,128)(2,1)} %copy-done.55, bf16[768,1024]{1,0:T(8,128)(2,1)} %bitcast.208, ...), custom_call_target="tpu_custom_call" | custom-call | flops 6442450944 | bytes 11534336 | tf_op jit(solution)/shard_map/pallas_call | solution.py:486
  257.3 21.0 %shard_map.496 = bf16[16,2,2,32,2048]{4,3,2,1,0:T(8,128)(2,1)} custom-call(bf16[384,1024]{1,0:T(8,128)(2,1)} %get-tuple-element.157.hidden.refs_0_, bf16[384,1024]{1,0:T(8,128)(2,1)} %get-tuple-element.165.hidden.refs_1_, bf16[384,1024]{1,0:T(8,128)(2,1)} %copy-done.54, bf16[384,1024]{1,0:T(8,128)(2,1)} %copy-done.55, ...), custom_call_target="tpu_custom_call" | custom-call | flops 12884901888 | bytes 20971520 | tf_op jit(solution)/shard_map/pallas_call | solution.py:537
  279.5 17.6 %shard_map.497 = (f32[12,64,1024]{2,1,0:T(8,128)}, f32[12,3,1024]{2,1,0:T(4,128)}, bf16[256,768]{1,0:T(8,128)(2,1)}, bf16[256,768]{1,0:T(8,128)(2,1)}, bf16[256,...) custom-call(s32[4]{0:T(128)} %iota_xor_fusion.order, f32[384,1024]{1,0:T(8,128)} %get-tuple-element.159.into1, ...), custom_call_target="tpu_custom_call" | custom-call | flops 3221225472 | bytes 18874368 | tf_op jit(solution)/shard_map/pallas_call | solution.py:600
  298.2 4.0 all-to-all-start.3
  304.0 48.5 %shard_map.498 = (bf16[256,1536]{1,0:T(8,128)(2,1)}, f32[256,3072]{1,0:T(8,128)}, f32[256,3072]{1,0:T(8,128)}) custom-call(bf16[768,1536]{1,0:T(8,128)(2,1)} %shard_map.487.k1.v1.q_ref, bf16[768,1536]{1,0:T(8,128)(2,1)} %shard_map.487.k1.v1.q_ref, bf16[768,1536]{1,0:T(8,128)(2,1)} %shard_map.488.q_ref.k2.v2, bf16[768,1536]{1,0:T(8,128)(2,1)} %shard_map.487.k1.v1.q_ref, ...), custom_call_target="tpu_custom_call" | custom-call | flops 41070624768 | bytes 6291456 | tf_op jit(solution)/shard_map/pallas_call | solution.py:332
  354.7 50.7 %shard_map.499 = (bf16[256,1536]{1,0:T(8,128)(2,1)}, bf16[256,3072]{1,0:T(8,128)(2,1)}, bf16[256,3072]{1,0:T(8,128)(2,1)}) custom-call(bf16[768,1536]{1,0:T(8,128)(2,1)} %shard_map.488.q_ref.k2.v2, bf16[768,1536]{1,0:T(8,128)(2,1)} %shard_map.487.k1.v1.q_ref, bf16[768,1536]{1,0:T(8,128)(2,1)} %shard_map.488.q_ref.k2.v2, ...), custom_call_target="tpu_custom_call" | custom-call | flops 41070624768 | bytes 6291456 | tf_op jit(solution)/shard_map/pallas_call | solution.py:332
  405.4 12.4 %reduce-scatter.2.cloned.1.call-done = bf16[128,2048]{1,0:T(8,128)(2,1)} async-done(((bf16[2048,2048]{1,0:T(8,128)(2,1)}), bf16[128,2048]{1,0:T(8,128)(2,1)}) %reduce-scatter.2.cloned.1.call-update) | async-done | bytes 524304 | tf_op jit(solution)/shard_map/reduce_scatter | solution.py:956
  417.8 13.1 %shard_map.500 = (bf16[2,768,1024]{2,1,0:T(8,128)(2,1)}, f32[768,1024]{1,0:T(8,128)}, f32[12,2,1024]{2,1,0:T(2,128)}) custom-call(bf16[384,1024]{1,0:T(8,128)(2,1)} %collective-permute-done.5.one, bf16[400,1024]{1,0:T(8,128)(2,1)} %collective-permute-done.6.two, bf16[384,1024]{1,0:T(8,128)(2,1)} %collective-permute-done.7.three, ...), custom_call_target="tpu_custom_call" | custom-call | flops 4831838208 | bytes 9437184 | tf_op jit(solution)/shard_map/pallas_call | solution.py:704
  437.6 7.2 %collective-permute-done.25 = bf16[2,32,2048]{2,1,0:T(8,128)(2,1)S(1)} collective-permute-done((bf16[2,32,2048]{2,1,0:T(8,128)(2,1)S(1)}, bf16[2,32,2048]{2,1,0:T(8,128)(2,1)S(1)}, u32[]{:S(2)}, u32[]{:S(2)}) %collective-permute-start.25) | collective-permute-done | bytes 262176 | tf_op jit(solution)/shard_map/ppermute | solution.py:757
  448.3 14.6 %shard_map.501 = (bf16[2,768,1024]{2,1,0:T(8,128)(2,1)}, bf16[1024,768]{1,0:T(8,128)(2,1)}, f32[12,2,1024]{2,1,0:T(2,128)}) custom-call(bf16[784,1024]{1,0:T(8,128)(2,1)} %copy-done.1, bf16[784,1024]{1,0:T(8,128)(2,1)} %copy-done.1, bf16[784,1024]{1,0:T(8,128)(2,1)} %collective-permute-done.three.four, bf16[784,1024]{1,0:T(8,128)(2,1)} %collective-permute-done.three.four, ...), custom_call_target="tpu_custom_call" | custom-call | flops 4831838208 | bytes 9437184 | tf_op jit(solution)/shard_map/pallas_call | solution.py:704
  466.4 4.3 all-to-all-start.4
  471.4 3.9 slice_bitcast_fusion
  478.7 50.4 %all-gather.9.cloned.1.call-done = bf16[1536,1024]{1,0:T(8,128)(2,1)} async-done(((bf16[768,1024]{1,0:T(8,128)(2,1)}), bf16[1536,1024]{1,0:T(8,128)(2,1)}) %all-gather.9.cloned.1.call-update) | async-done | bytes 3145744 | tf_op jit(solution)/shard_map/all_gather | solution.py:993
  534.3 5.2 shard_map.503
  539.5 7.3 %shard_map.502 = f32[12,64,1024]{2,1,0:T(8,128)} custom-call(bf16[12,64,1024]{2,1,0:T(8,128)(2,1)} %bitcast.176, f32[12,6,1024]{2,1,0:T(8,128)} %copy-done.2, f32[12,64,1024]{2,1,0:T(8,128)} %get-tuple-element.217.middle_grad, bf16[768,1024]{1,0:T(8,128)(2,1)} %get-tuple-element.269.one, bf16[768,1024]{1,0:T(8,128)(2,1)} %collective-permute-done.26.two, ...), custom_call_target="tpu_custom_call" | custom-call | flops 15728640 | bytes 12582912 | tf_op jit(solution)/shard_map/pallas_call | solution.py:728
  549.3 3.5 shard_map.505
  562.4 12.5 %all_to_all.30 = f32[32,8,128]{2,1,0:T(8,128)S(1)} all-to-all(f32[32,8,128]{2,1,0:T(8,128)S(1)} %broadcast_in_dim.40), channel_id=1, replica_groups=mesh['clip'=8,'x'=2,'core'=2] {'clip','x','core'}, dimensions={0} | all-to-all | bytes 262144 | tf_op jit(solution)/shard_map/all_to_all | solution.py:1043
  (320 shorter events, 111.6 us)
Async XLA Ops:
  9.5 15.3 %collective-permute-start.4 = (bf16[32,768]{1,0:T(8,128)(2,1)S(1)}, bf16[32,768]{1,0:T(8,128)(2,1)S(1)}, u32[]{:S(2)}, u32[]{:S(2)}) collective-permute-start(bf16[32,768]{1,0:T(8,128)(2,1)S(1)} %get-tuple-element.299), channel_id=1, source_target_pairs={{0,3},{1,2},{2,1},{3,0},{4,7},{5,6},{6,5},{7,4},{8,11},{9,10},{10,... | collective-permute-start | bytes 147464 | tf_op jit(solution)/shard_map/ppermute | solution.py:757
  11.9 12.9 %collective-permute-start.3 = (bf16[32,768]{1,0:T(8,128)(2,1)S(1)}, bf16[32,768]{1,0:T(8,128)(2,1)S(1)}, u32[]{:S(2)}, u32[]{:S(2)}) collective-permute-start(bf16[32,768]{1,0:T(8,128)(2,1)S(1)} %get-tuple-element.300), channel_id=1, source_target_pairs={{0,2},{1,3},{2,0},{3,1},{4,6},{5,7},{6,4},{7,5},{8,10},{9,11},{10,... | collective-permute-start | bytes 147464 | tf_op jit(solution)/shard_map/ppermute | solution.py:757
  12.6 12.3 %collective-permute-start.2 = (bf16[32,768]{1,0:T(8,128)(2,1)S(1)}, bf16[32,768]{1,0:T(8,128)(2,1)S(1)}, u32[]{:S(2)}, u32[]{:S(2)}) collective-permute-start(bf16[32,768]{1,0:T(8,128)(2,1)S(1)} %get-tuple-element.301), channel_id=1, source_target_pairs={{0,1},{1,0},{2,3},{3,2},{4,5},{5,4},{6,7},{7,6},{8,9},{9,8},{10,11... | collective-permute-start | bytes 147464 | tf_op jit(solution)/shard_map/ppermute | solution.py:757
  13.5 29.0 %collective-permute-start.5 = (bf16[384,1024]{1,0:T(8,128)(2,1)}, bf16[384,1024]{1,0:T(8,128)(2,1)}, u32[]{:S(2)}, u32[]{:S(2)}) collective-permute-start(bf16[384,1024]{1,0:T(8,128)(2,1)} %bitcast.34), channel_id=1, source_target_pairs={{0,2},{2,0},{1,3},{3,1},{4,6},{6,4},{5,7},{7,5},{8,10},{10,8},{9,1... | collective-permute-start | bytes 2359304 | tf_op jit(solution)/shard_map/ppermute | solution.py:757
  17.4 22.3 %all-to-all-start = ((bf16[8,12,1024]{2,1,0:T(8,128)(2,1)}), bf16[8,12,1024]{2,1,0:T(8,128)(2,1)}, u32[]{:S(2)}, u32[]{:S(2)}) async-start(bf16[8,12,1024]{2,1,0:T(8,128)(2,1)} %broadcast_in_dim.34), calls=%async_computation | async-start | bytes 524288 | tf_op jit(solution)/shard_map/all_to_all | solution.py:856
  23.3 55.8 %all-gather.5.cloned.1.call-start = ((), (), s32[]{:S(2)}) async-start(), calls=%async_computation.7 | async-start | bytes 1769472 | tf_op jit(solution)/shard_map/all_gather | solution.py:848
  30.5 8.8 %collective-permute-start.1 = (bf16[2,32,2048]{2,1,0:T(8,128)(2,1)S(1)}, bf16[2,32,2048]{2,1,0:T(8,128)(2,1)S(1)}, u32[]{:S(2)}, u32[]{:S(2)}) collective-permute-start(bf16[2,32,2048]{2,1,0:T(8,128)(2,1)S(1)} %bitcast.224), channel_id=1, source_target_pairs={{0,2},{2,0},{1,3},{3,1},{4,6},{6,4},{5,7},{7,5},{8,10},{10,8},{9,1... | collective-permute-start | bytes 786440 | tf_op jit(solution)/shard_map/ppermute | solution.py:757
  42.6 34.0 %collective-permute-start.6 = (bf16[400,1024]{1,0:T(8,128)(2,1)}, bf16[400,1024]{1,0:T(8,128)(2,1)}, u32[]{:S(2)}, u32[]{:S(2)}) collective-permute-start(bf16[400,1024]{1,0:T(8,128)(2,1)} %slice.203), channel_id=1, source_target_pairs={{0,2},{2,0},{1,3},{3,1},{4,6},{6,4},{5,7},{7,5},{8,10},{10,8},{9,1... | collective-permute-start | bytes 2457608 | tf_op jit(solution)/shard_map/ppermute | solution.py:757
  46.1 28.9 %all-to-all-start.1 = ((f32[32,12,192]{2,1,0:T(8,128)}), f32[32,12,192]{2,1,0:T(8,128)}, u32[]{:S(2)}, u32[]{:S(2)}) async-start(f32[32,12,192]{2,1,0:T(8,128)} %bitcast.203), calls=%async_computation.1 | async-start | bytes 1048576 | tf_op jit(solution)/shard_map/all_to_all | solution.py:868
  51.3 147.2 %all-gather.7.cloned.1.call-start = ((), (), s32[]{:S(2)}) async-start(), calls=%async_computation.8 | async-start | bytes 8912896 | tf_op jit(solution)/shard_map/all_gather | solution.py:880
  84.8 14.3 %collective-permute-start.7 = (bf16[384,1024]{1,0:T(8,128)(2,1)}, bf16[384,1024]{1,0:T(8,128)(2,1)}, u32[]{:S(2)}, u32[]{:S(2)}) collective-permute-start(bf16[384,1024]{1,0:T(8,128)(2,1)} %collective-permute-done.5.one), channel_id=1, source_target_pairs={{0,1},{1,0},{2,3},{3,2},{4,5},{5,4},{6,7},{7,6},{8,9},{9,8},{10,11... | collective-permute-start | bytes 2359304 | tf_op jit(solution)/shard_map/ppermute | solution.py:757
  85.6 13.5 %collective-permute-start.8 = (bf16[400,1024]{1,0:T(8,128)(2,1)}, bf16[400,1024]{1,0:T(8,128)(2,1)S(1)}, u32[]{:S(2)}, u32[]{:S(2)}) collective-permute-start(bf16[400,1024]{1,0:T(8,128)(2,1)} %collective-permute-done.6.two), channel_id=1, source_target_pairs={{0,1},{1,0},{2,3},{3,2},{4,5},{5,4},{6,7},{7,6},{8,9},{9,8},{10,11... | collective-permute-start | bytes 2457608 | tf_op jit(solution)/shard_map/ppermute | solution.py:757
  87.8 57.1 %collective-permute-start.10 = (bf16[12,64,1024]{2,1,0:T(8,128)(2,1)}, bf16[12,64,1024]{2,1,0:T(8,128)(2,1)}, u32[]{:S(2)}, u32[]{:S(2)}) collective-permute-start(bf16[12,64,1024]{2,1,0:T(8,128)(2,1)} %bitcast.4.cotangent), channel_id=1, source_target_pairs={{0,2},{2,0},{1,3},{3,1},{4,6},{6,4},{5,7},{7,5},{8,10},{10,8},{9,1... | collective-permute-start | bytes 4718600 | tf_op jit(solution)/shard_map/ppermute | solution.py:757
  101.1 47.9 %all-to-all-start.2 = ((bf16[8,2,32,1024]{3,2,1,0:T(8,128)(2,1)}), bf16[8,2,32,1024]{3,2,1,0:T(8,128)(2,1)S(1)}, u32[]{:S(2)}, u32[]{:S(2)}) async-start(bf16[8,2,32,1024]{3,2,1,0:T(8,128)(2,1)} %broadcast_in_dim.39), calls=%async_computation.2 | async-start | bytes 2097152 | tf_op jit(solution)/shard_map/all_to_all | solution.py:913
  106.1 311.7 %reduce-scatter.2.cloned.1.call-start = ((), (), s32[]{:S(2)}) async-start(), calls=%async_computation.9 | async-start | bytes 8912896 | tf_op jit(solution)/shard_map/reduce_scatter | solution.py:956
  151.0 35.6 %collective-permute-start.14 = (bf16[256,768]{1,0:T(8,128)(2,1)}, bf16[256,768]{1,0:T(8,128)(2,1)S(1)}, u32[]{:S(2)}, u32[]{:S(2)}) collective-permute-start(bf16[256,768]{1,0:T(8,128)(2,1)} %get-tuple-element.274), channel_id=1, source_target_pairs={{0,3},{1,2},{2,1},{3,0},{4,7},{5,6},{6,5},{7,4},{8,11},{9,10},{10,... | collective-permute-start | bytes 1179656 | tf_op jit(solution)/shard_map/ppermute | solution.py:757
  151.1 35.4 %collective-permute-start.13 = (bf16[256,768]{1,0:T(8,128)(2,1)S(1)}, bf16[256,768]{1,0:T(8,128)(2,1)S(1)}, u32[]{:S(2)}, u32[]{:S(2)}) collective-permute-start(bf16[256,768]{1,0:T(8,128)(2,1)S(1)} %get-tuple-element.275), channel_id=1, source_target_pairs={{0,2},{1,3},{2,0},{3,1},{4,6},{5,7},{6,4},{7,5},{8,10},{9,11},{10,... | collective-permute-start | bytes 1179656 | tf_op jit(solution)/shard_map/ppermute | solution.py:757
  152.3 31.2 %collective-permute-start.11 = (bf16[8,2,32,1024]{3,2,1,0:T(8,128)(2,1)S(1)}, bf16[8,2,32,1024]{3,2,1,0:T(8,128)(2,1)S(1)}, u32[]{:S(2)}, u32[]{:S(2)}) collective-permute-start(bf16[8,2,32,1024]{3,2,1,0:T(8,128)(2,1)S(1)} %all-to-all-done.2), channel_id=1, source_target_pairs={{0,1},{1,0},{2,3},{3,2},{4,5},{5,4},{6,7},{7,6},{8,9},{9,8},{10,11... | collective-permute-start | bytes 3145736 | tf_op jit(solution)/shard_map/ppermute | solution.py:757
  197.1 29.8 %collective-permute-start.15 = (bf16[384,1024]{1,0:T(8,128)(2,1)}, bf16[384,1024]{1,0:T(8,128)(2,1)S(1)}, u32[]{:S(2)}, u32[]{:S(2)}) collective-permute-start(bf16[384,1024]{1,0:T(8,128)(2,1)} %get-tuple-element.157.hidden.refs_0_), channel_id=1, source_target_pairs={{0,2},{2,0},{1,3},{3,1},{4,6},{6,4},{5,7},{7,5},{8,10},{10,8},{9,1... | collective-permute-start | bytes 2359304 | tf_op jit(solution)/shard_map/ppermute | solution.py:757
  212.3 29.9 %collective-permute-start.16 = (bf16[384,1024]{1,0:T(8,128)(2,1)S(1)}, bf16[384,1024]{1,0:T(8,128)(2,1)S(1)}, u32[]{:S(2)}, u32[]{:S(2)}) collective-permute-start(bf16[384,1024]{1,0:T(8,128)(2,1)S(1)} %copy-done.53), channel_id=1, source_target_pairs={{0,2},{2,0},{1,3},{3,1},{4,6},{6,4},{5,7},{7,5},{8,10},{10,8},{9,1... | collective-permute-start | bytes 2359304 | tf_op jit(solution)/shard_map/ppermute | solution.py:757
  240.9 37.4 %collective-permute-start.17 = (bf16[384,1024]{1,0:T(8,128)(2,1)}, bf16[384,1024]{1,0:T(8,128)(2,1)S(1)}, u32[]{:S(2)}, u32[]{:S(2)}) collective-permute-start(bf16[384,1024]{1,0:T(8,128)(2,1)} %get-tuple-element.177), channel_id=1, source_target_pairs={{0,2},{2,0},{1,3},{3,1},{4,6},{6,4},{5,7},{7,5},{8,10},{10,8},{9,1... | collective-permute-start | bytes 2359304 | tf_op jit(solution)/shard_map/ppermute | solution.py:757
  256.6 21.7 %collective-permute-start.18 = (bf16[384,1024]{1,0:T(8,128)(2,1)}, bf16[384,1024]{1,0:T(8,128)(2,1)S(1)}, u32[]{:S(2)}, u32[]{:S(2)}) collective-permute-start(bf16[384,1024]{1,0:T(8,128)(2,1)} %get-tuple-element.178), channel_id=1, source_target_pairs={{0,2},{2,0},{1,3},{3,1},{4,6},{6,4},{5,7},{7,5},{8,10},{10,8},{9,1... | collective-permute-start | bytes 2359304 | tf_op jit(solution)/shard_map/ppermute | solution.py:757
  298.2 107.2 %all-to-all-start.3 = ((bf16[32,32,1024]{2,1,0:T(8,128)(2,1)}), bf16[32,32,1024]{2,1,0:T(8,128)(2,1)}, u32[]{:S(2)}, u32[]{:S(2)}) async-start(bf16[32,32,1024]{2,1,0:T(8,128)(2,1)} %bitcast.204), calls=%async_computation.3 | async-start | bytes 4194304 | tf_op jit(solution)/shard_map/all_to_all | solution.py:967
  302.2 50.3 %collective-permute-start.20 = (bf16[256,768]{1,0:T(8,128)(2,1)S(1)}, bf16[256,768]{1,0:T(8,128)(2,1)}, u32[]{:S(2)}, u32[]{:S(2)}) collective-permute-start(bf16[256,768]{1,0:T(8,128)(2,1)S(1)} %copy-done.57), channel_id=1, source_target_pairs={{0,2},{1,3},{2,0},{3,1},{4,6},{5,7},{6,4},{7,5},{8,10},{9,11},{10,... | collective-permute-start | bytes 1179656 | tf_op jit(solution)/shard_map/ppermute | solution.py:757
  304.0 48.5 %collective-permute-start.21 = (bf16[256,768]{1,0:T(8,128)(2,1)S(1)}, bf16[256,768]{1,0:T(8,128)(2,1)}, u32[]{:S(2)}, u32[]{:S(2)}) collective-permute-start(bf16[256,768]{1,0:T(8,128)(2,1)S(1)} %copy-done.56), channel_id=1, source_target_pairs={{0,3},{1,2},{2,1},{3,0},{4,7},{5,6},{6,5},{7,4},{8,11},{9,10},{10,... | collective-permute-start | bytes 1179656 | tf_op jit(solution)/shard_map/ppermute | solution.py:757
  352.6 52.8 %collective-permute-start.22 = (bf16[384,1024]{1,0:T(8,128)(2,1)}, bf16[384,1024]{1,0:T(8,128)(2,1)S(1)}, u32[]{:S(2)}, u32[]{:S(2)}) collective-permute-start(bf16[384,1024]{1,0:T(8,128)(2,1)} %get-tuple-element.198), channel_id=1, source_target_pairs={{0,2},{2,0},{1,3},{3,1},{4,6},{6,4},{5,7},{7,5},{8,10},{10,8},{9,1... | collective-permute-start | bytes 2359304 | tf_op jit(solution)/shard_map/ppermute | solution.py:757
  354.1 51.3 %collective-permute-start.23 = (bf16[384,1024]{1,0:T(8,128)(2,1)}, bf16[384,1024]{1,0:T(8,128)(2,1)}, u32[]{:S(2)}, u32[]{:S(2)}) collective-permute-start(bf16[384,1024]{1,0:T(8,128)(2,1)} %get-tuple-element.199), channel_id=1, source_target_pairs={{0,2},{2,0},{1,3},{3,1},{4,6},{6,4},{5,7},{7,5},{8,10},{10,8},{9,1... | collective-permute-start | bytes 2359304 | tf_op jit(solution)/shard_map/ppermute | solution.py:757
  432.5 13.9 %collective-permute-start.24 = (bf16[768,1024]{1,0:T(8,128)(2,1)S(1)}, bf16[768,1024]{1,0:T(8,128)(2,1)S(1)}, u32[]{:S(2)}, u32[]{:S(2)}) collective-permute-start(bf16[768,1024]{1,0:T(8,128)(2,1)S(1)} %slice_bitcast_fusion.2), channel_id=1, source_target_pairs={{0,1},{1,0},{2,3},{3,2},{4,5},{5,4},{6,7},{7,6},{8,9},{9,8},{10,11... | collective-permute-start | bytes 4718600 | tf_op jit(solution)/shard_map/ppermute | solution.py:757
  436.0 8.8 %collective-permute-start.25 = (bf16[2,32,2048]{2,1,0:T(8,128)(2,1)S(1)}, bf16[2,32,2048]{2,1,0:T(8,128)(2,1)S(1)}, u32[]{:S(2)}, u32[]{:S(2)}) collective-permute-start(bf16[2,32,2048]{2,1,0:T(8,128)(2,1)S(1)} %bitcast.222), channel_id=1, source_target_pairs={{0,2},{2,0},{1,3},{3,1},{4,6},{6,4},{5,7},{7,5},{8,10},{10,8},{9,1... | collective-permute-start | bytes 786440 | tf_op jit(solution)/shard_map/ppermute | solution.py:757
  466.4 80.4 %all-to-all-start.4 = ((bf16[32,38,768]{2,1,0:T(8,128)(2,1)}), bf16[32,38,768]{2,1,0:T(8,128)(2,1)S(1)}, u32[]{:S(2)}, u32[]{:S(2)}) async-start(bf16[32,38,768]{2,1,0:T(8,128)(2,1)} %pad_maximum_fusion.2), calls=%async_computation.5 | async-start | bytes 3932160 | tf_op jit(solution)/shard_map/all_to_all | solution.py:1017
  470.8 58.3 %all-gather.9.cloned.1.call-start = ((), (), s32[]{:S(2)}) async-start(), calls=%async_computation.10 | async-start | bytes 4718592 | tf_op jit(solution)/shard_map/all_gather | solution.py:993
  475.3 64.3 %collective-permute-start.26 = (bf16[768,1024]{1,0:T(8,128)(2,1)}, bf16[768,1024]{1,0:T(8,128)(2,1)}, u32[]{:S(2)}, u32[]{:S(2)}) collective-permute-start(bf16[768,1024]{1,0:T(8,128)(2,1)} %get-tuple-element.268), channel_id=1, source_target_pairs={{0,1},{1,0},{2,3},{3,2},{4,5},{5,4},{6,7},{7,6},{8,9},{9,8},{10,11... | collective-permute-start | bytes 4718600 | tf_op jit(solution)/shard_map/ppermute | solution.py:757
  (62 other events, 426.9 us)
Sparse Core Ops, SparseCore 0:
  26.7 52.2 all-gather.4
  81.8 88.1 all-gather.6
  278.5 139.2 reduce-scatter.1
  472.9 56.2 all-gather.8

commit v8 on v7

--- a/solution.py
+++ b/solution.py
@@ -346,13 +346,21 @@
 
 
 def project_kernel(
-    order, a0, a1, a2, a3, weight, tokens, cotangent, mod, att_out, hid1, hid2, branch, proj
+    order, a0, a1, a2, a3, mine, other, tokens, cotangent, cot_far, mod,
+    att_out, hid1, hid2, branch, branch_far, proj,
 ):
     features = a1.shape[0]
 
     @pl.when(pl.program_id(0) == 0)
     def _():
-        proj[...] = jnp.transpose(weight[...])
+        low = order[4] == 0
+        clips, pairs, shard, width = mine.shape
+        rows = []
+        for clip in range(clips):
+            for pair in range(pairs):
+                one, two = mine[clip, pair].astype(f32), other[clip, pair].astype(f32)
+                rows += [jnp.where(low, one, two), jnp.where(low, two, one)]
+        proj[...] = jnp.transpose(jnp.concatenate(rows, axis=0)).astype(bf16)
 
     mixed = None
     for slot, part in enumerate((a0.at[0], a1, a2, a3)):
@@ -378,9 +386,10 @@
         hid2[...] = hidden_two
 
     branch[...] = (mod[:, 5:6, :] * cotangent[...].astype(f32)).astype(bf16).reshape(flat)
-
-
-def project_out(order, parts, proj, tokens, cotangent, mod):
+    branch_far[...] = (mod[:, 5:6, :] * cot_far[...].astype(f32)).astype(bf16).reshape(flat)
+
+
+def project_out(order, parts, weight, tokens, cotangent, cot_far, mod):
     frames, per_frame, width = tokens.shape
     chunk = frames // 2
     half = 1
@@ -395,11 +404,13 @@
         in_specs=[whole(pltpu.SMEM)]
         + [pl.BlockSpec((1, features, block), lambda i: (0, 0, i))]
         + [pl.BlockSpec((features, block), lambda i: (0, i))] * 3
-        + [whole(), cube, cube, pl.BlockSpec((chunk, 6, width), lambda i: (i, 0, 0))],
+        + [whole(), whole(), cube, cube, cube]
+        + [pl.BlockSpec((chunk, 6, width), lambda i: (i, 0, 0))],
         out_specs=[
             cube,
             pl.BlockSpec((block, width), lambda i: (jnp.minimum(i, half - 1), 0)),
             pl.BlockSpec((block, width), lambda i: (jnp.maximum(i - half, 0), 0)),
+            flat,
             flat,
             whole(),
         ],
@@ -408,11 +419,12 @@
             jax.ShapeDtypeStruct((count // 2, width), bf16),
             jax.ShapeDtypeStruct((count // 2, width), bf16),
             jax.ShapeDtypeStruct((count, width), bf16),
+            jax.ShapeDtypeStruct((count, width), bf16),
             jax.ShapeDtypeStruct((width, width), bf16),
         ],
         compiler_params=params(),
         cost_estimate=cost(2 * frames * per_frame * width * width, 14 * frames * per_frame * width),
-    )(order, *parts, proj, tokens, cotangent, mod)
+    )(order, *parts, *weight, tokens, cotangent, cot_far, mod)
 
 
 def weight_places(shape):
@@ -713,22 +725,29 @@
     )(*operands)
 
 
-def input_kernel(tokens, mod, middle_grad, one, two, three, out):
+def input_kernel(tokens, mod, middle_grad, one, two, far1, far2, out):
     normed, inverse = layer_norm(tokens[...].astype(f32))
-    grad = one[...].astype(f32) + two[...].astype(f32) + three[...].astype(f32)
+    first = pl.program_id(0) < pl.num_programs(0) // 2
+    grad = jnp.where(first, far1[...].astype(f32), far2[...].astype(f32))
+    grad = grad + one[...].astype(f32) + two[...].astype(f32)
     grad = grad.reshape(tokens.shape) * (1.0 + mod[:, 1:2, :])
     out[...] = middle_grad[...] + norm_back(normed, inverse, grad)
 
 
 def input_back(tokens, mod, middle_grad, parts):
     frames, per_frame, width = tokens.shape
-    chunk = 4
+    chunk = 2
+    half = frames // chunk // 2
+    block = chunk * per_frame
     cube = pl.BlockSpec((chunk, per_frame, width), lambda i: (i, 0, 0))
-    flat = pl.BlockSpec((chunk * per_frame, width), lambda i: (i, 0))
+    flat = pl.BlockSpec((block, width), lambda i: (i, 0))
+    one = pl.BlockSpec((block, width), lambda i: (jnp.minimum(i, half - 1), 0))
+    two = pl.BlockSpec((block, width), lambda i: (jnp.maximum(i - half, 0), 0))
     return pl.pallas_call(
         input_kernel,
         grid=(frames // chunk,),
-        in_specs=[cube, pl.BlockSpec((chunk, 6, width), lambda i: (i, 0, 0)), cube, flat, flat, flat],
+        in_specs=[cube, pl.BlockSpec((chunk, 6, width), lambda i: (i, 0, 0)), cube]
+        + [flat, flat, one, two],
         out_specs=cube,
         out_shape=jax.ShapeDtypeStruct(tokens.shape, f32),
         compiler_params=params(),
@@ -820,11 +839,12 @@
     per_frame = patch_rows * grid_cols
     count = frames * per_frame
     devices = clips * rows
+    half = count // 2
     features = width // rows
     clip, far, core = lax.axis_index("clip"), lax.axis_index("x"), lax.axis_index("core")
     row = lax.axis_index(ROW)
     both = ("clip",) + ROW
-    order = (row ^ jnp.arange(rows)).astype(jnp.int32)
+    order = jnp.append(row ^ jnp.arange(rows), core).astype(jnp.int32)
 
     own = tokens.reshape(frames, per_frame, width)
     upstream = cotangent.reshape(frames, per_frame, width)
@@ -926,11 +946,10 @@
     out_near, lse_near = attend(qkv_near, qkv_near, qkv_far, bias)
     out_near, project_near = lax.optimization_barrier((out_near, project_near))
     part1 = swap(out_near[1], ROW, rows, 1)
-    project_full = relative(jnp.stack([project_full, project_near]), core)
-    project_full = project_full.transpose(1, 2, 0, 3, 4).reshape(width, width)
-    branch_far = (mod[:, 5:6, :] * cot_far.astype(f32)).astype(bf16).reshape(count, width)
     parts = [out_near, part1, part2, part3]
-    att_out, hid1, hid2, branch, project_turned = project_out(order, parts, project_full, own, upstream, mod)
+    att_out, hid1, hid2, branch, branch_far, project_turned = project_out(
+        order, parts, (project_full, project_near), own, upstream, cot_far, mod
+    )
 
     far1 = swap(hid1, "x", 2, 1)
     out1, in1, act1, wide1, gate1 = feed_forward(feed_full, hid1, branch, upstream, 0, f32)
@@ -981,24 +1000,25 @@
     dq_far, dk, dv = attend_back(
         qkv_far, qkv_near, qkv_far, bias, out_far, (d2, d3), lse_far, turning, 1, (dk, dv)
     )
-    dq_far, project_raw, out3, out4, feed_sum = lax.optimization_barrier(
-        (dq_far, project_raw, out3, out4, feed_sum)
-    )
-    feed_sum = trade(relative(feed_sum, far), "x", 2)
+    dq_far, project_raw, out3, out4 = lax.optimization_barrier((dq_far, project_raw, out3, out4))
+    project_sum = total_over(project_raw.reshape(devices, 1, shard, width))[0].T
     back_far, raw, mod_early = first_back(across, mod, dq_far, dk, dv, attend_turned, 1)
     back_far = (
         back_far[0].astype(f32) + swap(back_far[1], ROW, rows, 1).astype(f32)
     ).astype(bf16)
-    back_far, dq_near, feed_sum = lax.optimization_barrier((back_far, dq_near, feed_sum))
-    back_far = lax.all_gather(back_far, "x", axis=0)
-    back_far = lax.dynamic_index_in_dim(back_far, 1 - far, 0, keepdims=False)
-    feed_sum = relative(feed_sum, far).astype(f32)
-    widen_sum, narrow_sum = feed_sum.transpose(1, 2, 0, 3).reshape(2, shard, units)
-    narrow_sum = narrow_sum.T
+    back_far, dq_near = lax.optimization_barrier((back_far, dq_near))
+    far_one = swap(back_far[:half], "x", 2, 1)
     extra = -(-2 * frames * part // (3 * features))
     back_near, attend_raw, mod_early = first_back(
         near, mod, dq_near, dk, dv, attend_turned, 0, (raw, mod_early)
     )
+    attend_raw, far_one, feed_sum, far_two = lax.optimization_barrier(
+        (attend_raw, far_one, feed_sum, back_far[half:])
+    )
+    far_two = swap(far_two, "x", 2, 1)
+    feed_sum = relative(trade(relative(feed_sum, far), "x", 2), far).astype(f32)
+    widen_sum, narrow_sum = feed_sum.transpose(1, 2, 0, 3).reshape(2, shard, units)
+    narrow_sum = narrow_sum.T
     back_near = (back_near[0], swap(back_near[1], ROW, rows, 1))
 
     mod_grad = jnp.concatenate([mod_early, mod_late, mod_gate], axis=1)
@@ -1015,10 +1035,9 @@
         axis=1,
     )
     attend_raw = lax.all_to_all(attend_raw, both, 0, 0, tiled=True)
-    out3, back_far, project_raw = lax.optimization_barrier((out3, back_far, project_raw))
-    project_sum = total_over(project_raw.reshape(devices, 1, shard, width))[0].T
+    out3, far_two = lax.optimization_barrier((out3, far_two))
     block_out = block_output((out1, out2, out3, out4), own, att_out, mod)
-    input_gradient = input_back(own, mod, middle_grad, back_near + (back_far,))
+    input_gradient = input_back(own, mod, middle_grad, back_near + (far_one, far_two))
     attend_raw, input_gradient, block_out, project_sum = lax.optimization_barrier(
         (attend_raw, input_gradient, block_out, project_sum)
     )

time: 607 us -> 569 us (0.937)
  waiting for transfers between devices: 107 us -> 70.5 us
    all_gather x1 -> x0, waiting for transfers between devices: 50.4 us -> none  [local(): back_far = lax.all_gather(back_far, 'x', axis=0)]
    ppermute x27 -> x29, waiting for transfers between devices: 16.8 us -> 44.2 us  [swap(): lax.ppermute(value, axis, [(place, place ^ step) for place in range(size)])]
    reduce_scatter x1, waiting for transfers between devices: 12.4 us -> 0.01 us  [local(): lax.psum_scatter(feed_raw.reshape(8 * clips * shard, units // 2), ('clip'...]
    ppermute x27 -> x29, starting transfers between devices: 22.9 us -> 25.1 us  [swap(): lax.ppermute(value, axis, [(place, place ^ step) for place in range(size)])]
  transfers between devices with their start and end apart: 36 -> 37, of which waited for: 8 -> 10; matrix products, arithmetic and copies ran while one was open for 8% -> 9% of each run, Pallas kernels for 49% -> 57%
where the time goes in v8:
time: 569 us; the launch traced here: 560 us
  Pallas kernels  324 us (57%)
  waiting for transfers between devices  70.5 us (12%)
  starting transfers between devices  50.9 us (9%)
  other arithmetic  39.8 us (7%)
  local copies, waits for them, and re-layouts  38.7 us (7%)
  between operations  21.8 us (4%)
  blocking collectives  12.4 us (2%)
    pallas_call x2, Pallas kernels, attend_back(): pl.pallas_call(functools.partial(attend_back_kernel, heads, last), grid=(...  99.4 us
    pallas_call x2, Pallas kernels, attend(): pl.pallas_call(functools.partial(attend_kernel, heads), grid=(count // bl...  54.9 us
    pallas_call x4, Pallas kernels, feed_forward(): pl.pallas_call(feed_kernel, grid=(units // block,), in_specs=[spec, flat,...  54.4 us
    ppermute x29, waiting for transfers between devices, swap(): lax.ppermute(value, axis, [(place, place ^ step) for place in range(size)])  44.2 us
    pallas_call x2, Pallas kernels, first_back(): pl.pallas_call(functools.partial(first_back_kernel, last), grid=(4,), in_...  27.9 us
    ppermute x29, starting transfers between devices, swap(): lax.ppermute(value, axis, [(place, place ^ step) for place in range(size)])  25.1 us
    pallas_call x1, Pallas kernels, feed_weights(): pl.pallas_call(functools.partial(feed_weight_kernel, len(hidden)), grid=(...  21 us
    all_to_all x1, waiting for transfers between devices, local(): lax.all_to_all(mod_mine.reshape(devices, frames, part), both, 0, 0, tiled...  20.5 us
  transfers between devices with their start and end apart: 37, of which 10 were waited for; matrix products, arithmetic and copies ran while one was open for 9% of the time, Pallas kernels for 57%

profile of v8, /device:TPU:0, one launch (start us, length us, event | category | flops | bytes accessed | tf_op | source)
XLA Modules:
  0.0 560.3 jit_solution(5902859197937974888)
XLA Ops:
  18.0 5.8 %all-to-all-start = ((bf16[8,12,1024]{2,1,0:T(8,128)(2,1)}), bf16[8,12,1024]{2,1,0:T(8,128)(2,1)S(1)}, u32[]{:S(2)}, u32[]{:S(2)}) async-start(bf16[8,12,1024]{2,1,0:T(8,128)(2,1)} %broadcast_in_dim.34), calls=%async_computation | async-start | bytes 524288 | tf_op jit(solution)/shard_map/all_to_all | solution.py:876
  33.4 6.4 %collective-permute-done.1 = bf16[2,32,2048]{2,1,0:T(8,128)(2,1)S(1)} collective-permute-done((bf16[2,32,2048]{2,1,0:T(8,128)(2,1)S(1)}, bf16[2,32,2048]{2,1,0:T(8,128)(2,1)S(1)}, u32[]{:S(2)}, u32[]{:S(2)}) %collective-permute-start.1) | collective-permute-done | bytes 262176 | tf_op jit(solution)/shard_map/ppermute | solution.py:776
  46.9 5.1 all-to-all-start.1
  55.3 20.5 %all-to-all-done.1 = f32[32,12,192]{2,1,0:T(8,128)} async-done(((f32[32,12,192]{2,1,0:T(8,128)}), f32[32,12,192]{2,1,0:T(8,128)}, u32[]{:S(2)}, u32[]{:S(2)}) %all-to-all-start.1) | async-done | bytes 294944 | tf_op jit(solution)/shard_map/all_to_all | solution.py:888
  82.6 2.8 collective-permute-done.9
  89.3 9.6 %shard_map.487.k1.v1.q_ref = bf16[768,1536]{1,0:T(8,128)(2,1)} custom-call(bf16[784,1024]{1,0:T(8,128)(2,1)} %copy-done.1, bf16[784,1024]{1,0:T(8,128)(2,1)} %copy-done.1, bf16[784,1024]{1,0:T(8,128)(2,1)} %copy-done.3, bf16[784,1024]{1,0:T(8,128)(2,1)} %copy-done.3, f32[12,6,1024]{2,1,0:T(8,128)} %reshape.439.mod, bf16[768,1024]{1,0:T(8,128)(2,1)} %bitcast.187, ...), custom_call_target="tpu_custom_call" | custom-call | flops 2415919104 | bytes 6291456 | tf_op jit(solution)/shard_map/pallas_call | solution.py:131
  101.4 5.2 all-to-all-start.2
  108.9 9.2 %shard_map.488.q_ref.k2.v2 = bf16[768,1536]{1,0:T(8,128)(2,1)} custom-call(bf16[384,1024]{1,0:T(8,128)(2,1)} %collective-permute-done.5.one, bf16[400,1024]{1,0:T(8,128)(2,1)} %collective-permute-done.6.two, bf16[384,1024]{1,0:T(8,128)(2,1)} %collective-permute-done.7.three, bf16[400,1024]{1,0:T(8,128)(2,1)} %collective-permute-done.8.four, ...), custom_call_target="tpu_custom_call" | custom-call | flops 2415919104 | bytes 6291456 | tf_op jit(solution)/shard_map/pallas_call | solution.py:131
  118.1 27.5 %shard_map.489 = (bf16[2,256,768]{2,1,0:T(8,128)(2,1)}, f32[4,1536]{1,0:T(4,128)}) custom-call(bf16[768,1536]{1,0:T(8,128)(2,1)} %shard_map.488.q_ref.k2.v2, bf16[768,1536]{1,0:T(8,128)(2,1)} %shard_map.487.k1.v1.q_ref, bf16[768,1536]{1,0:T(8,128)(2,1)} %shard_map.488.q_ref.k2.v2, bf16[768,1536]{1,0:T(8,128)(2,1)} %shard_map.487.k1.v1.q_ref, ...), custom_call_target="tpu_custom_call" | custom-call | flops 19327352832 | bytes 3145728 | tf_op jit(solution)/shard_map/pallas_call | solution.py:186
  145.6 4.1 all-to-all-done.2.mine
  153.8 27.4 %shard_map.490 = (bf16[2,256,768]{2,1,0:T(8,128)(2,1)}, f32[4,1536]{1,0:T(4,128)}) custom-call(bf16[768,1536]{1,0:T(8,128)(2,1)} %shard_map.487.k1.v1.q_ref, bf16[768,1536]{1,0:T(8,128)(2,1)} %shard_map.487.k1.v1.q_ref, bf16[768,1536]{1,0:T(8,128)(2,1)} %shard_map.488.q_ref.k2.v2, bf16[768,1536]{1,0:T(8,128)(2,1)} %shard_map.487.k1.v1.q_ref, ...), custom_call_target="tpu_custom_call" | custom-call | flops 19327352832 | bytes 3145728 | tf_op jit(solution)/shard_map/pallas_call | solution.py:186
  184.9 10.2 %shard_map.491 = (f32[12,64,1024]{2,1,0:T(8,128)}, bf16[384,1024]{1,0:T(8,128)(2,1)}, bf16[384,1024]{1,0:T(8,128)(2,1)}, bf16[768,1024]{1,0:T(8,128)(2,1)}, bf16...) custom-call(s32[5]{0:T(128)} %pad_add_fusion.order, bf16[2,256,768]{2,1,0:T(8,128)(2,1)} %get-tuple-element.156.a0.out_ref, ...), custom_call_target="tpu_custom_call" | custom-call | flops 1610612736 | bytes 11010048 | tf_op jit(solution)/shard_map/pallas_call | solution.py:401
  196.6 13.8 %shard_map.492 = (f32[384,1024]{1,0:T(8,128)}, f32[384,1024]{1,0:T(8,128)}, bf16[384,2048]{1,0:T(8,128)(2,1)}, bf16[384,2048]{1,0:T(8,128)(2,1)}, f32[6,1,1024]{2,1,0:T(1,128)}) custom-call(bf16[16,2,2,32,2048]{4,3,2,1,0:T(8,128)(2,1)} %bitcast.202, bf16[384,1024]{1,0:T(8,128)(2,1)} %get-tuple-element.160.hidden.refs_0_, ...), custom_call_target="tpu_custom_call" | custom-call | flops 6442450944 | bytes 11534336 | tf_op jit(solution)/shard_map/pallas_call | solution.py:498
  211.0 13.7 %shard_map.493 = (f32[384,1024]{1,0:T(8,128)}, f32[384,1024]{1,0:T(8,128)}, bf16[384,2048]{1,0:T(8,128)(2,1)}, bf16[384,2048]{1,0:T(8,128)(2,1)}, f32[6,1,1024]{2,1,0:T(1,128)}) custom-call(bf16[16,2,2,32,2048]{4,3,2,1,0:T(8,128)(2,1)} %bitcast.203, bf16[384,1024]{1,0:T(8,128)(2,1)} %get-tuple-element.168.hidden.refs_1_, ...), custom_call_target="tpu_custom_call" | custom-call | flops 6442450944 | bytes 11534336 | tf_op jit(solution)/shard_map/pallas_call | solution.py:498
  225.6 13.3 %shard_map.494 = (bf16[384,1024]{1,0:T(8,128)(2,1)}, bf16[384,1024]{1,0:T(8,128)(2,1)}, bf16[384,2048]{1,0:T(8,128)(2,1)}, bf16[384,2048]{1,0:T(8,128)(2,1)}, f32[6,1,1024]{2,1,0:T(1,128)}) custom-call(bf16[16,2,2,32,2048]{4,3,2,1,0:T(8,128)(2,1)} %bitcast.204, bf16[384,1024]{1,0:T(8,128)(2,1)} %copy-done.52, ...), custom_call_target="tpu_custom_call" | custom-call | flops 6442450944 | bytes 11534336 | tf_op jit(solution)/shard_map/pallas_call | solution.py:498
  241.3 13.6 %shard_map.495 = (bf16[384,1024]{1,0:T(8,128)(2,1)}, bf16[384,1024]{1,0:T(8,128)(2,1)}, bf16[384,2048]{1,0:T(8,128)(2,1)}, bf16[384,2048]{1,0:T(8,128)(2,1)}, f32[6,1,1024]{2,1,0:T(1,128)}) custom-call(bf16[16,2,2,32,2048]{4,3,2,1,0:T(8,128)(2,1)} %bitcast.205, bf16[384,1024]{1,0:T(8,128)(2,1)} %copy-done.53, ...), custom_call_target="tpu_custom_call" | custom-call | flops 6442450944 | bytes 11534336 | tf_op jit(solution)/shard_map/pallas_call | solution.py:498
  255.4 21.0 %shard_map.496 = bf16[16,2,2,32,2048]{4,3,2,1,0:T(8,128)(2,1)} custom-call(bf16[384,1024]{1,0:T(8,128)(2,1)} %get-tuple-element.160.hidden.refs_0_, bf16[384,1024]{1,0:T(8,128)(2,1)} %get-tuple-element.168.hidden.refs_1_, bf16[384,1024]{1,0:T(8,128)(2,1)} %copy-done.52, bf16[384,1024]{1,0:T(8,128)(2,1)} %copy-done.53, ...), custom_call_target="tpu_custom_call" | custom-call | flops 12884901888 | bytes 20971520 | tf_op jit(solution)/shard_map/pallas_call | solution.py:549
  277.6 17.6 %shard_map.497 = (f32[12,64,1024]{2,1,0:T(8,128)}, f32[12,3,1024]{2,1,0:T(4,128)}, bf16[256,768]{1,0:T(8,128)(2,1)}, bf16[256,768]{1,0:T(8,128)(2,1)}, bf16[256,...) custom-call(s32[5]{0:T(128)} %pad_add_fusion.order, f32[384,1024]{1,0:T(8,128)} %get-tuple-element.162.into1, ...), custom_call_target="tpu_custom_call" | custom-call | flops 3221225472 | bytes 18874368 | tf_op jit(solution)/shard_map/pallas_call | solution.py:612
  296.3 3.8 all-to-all-start.3
  302.0 48.4 %shard_map.498 = (bf16[256,1536]{1,0:T(8,128)(2,1)}, f32[256,3072]{1,0:T(8,128)}, f32[256,3072]{1,0:T(8,128)}) custom-call(bf16[768,1536]{1,0:T(8,128)(2,1)} %shard_map.487.k1.v1.q_ref, bf16[768,1536]{1,0:T(8,128)(2,1)} %shard_map.487.k1.v1.q_ref, bf16[768,1536]{1,0:T(8,128)(2,1)} %shard_map.488.q_ref.k2.v2, bf16[768,1536]{1,0:T(8,128)(2,1)} %shard_map.487.k1.v1.q_ref, ...), custom_call_target="tpu_custom_call" | custom-call | flops 41070624768 | bytes 6291456 | tf_op jit(solution)/shard_map/pallas_call | solution.py:332
  352.6 50.9 %shard_map.499 = (bf16[256,1536]{1,0:T(8,128)(2,1)}, bf16[256,3072]{1,0:T(8,128)(2,1)}, bf16[256,3072]{1,0:T(8,128)(2,1)}) custom-call(bf16[768,1536]{1,0:T(8,128)(2,1)} %shard_map.488.q_ref.k2.v2, bf16[768,1536]{1,0:T(8,128)(2,1)} %shard_map.487.k1.v1.q_ref, bf16[768,1536]{1,0:T(8,128)(2,1)} %shard_map.488.q_ref.k2.v2, ...), custom_call_target="tpu_custom_call" | custom-call | flops 41070624768 | bytes 6291456 | tf_op jit(solution)/shard_map/pallas_call | solution.py:332
  403.6 13.3 %shard_map.500 = (bf16[2,768,1024]{2,1,0:T(8,128)(2,1)}, f32[768,1024]{1,0:T(8,128)}, f32[12,2,1024]{2,1,0:T(2,128)}) custom-call(bf16[384,1024]{1,0:T(8,128)(2,1)} %collective-permute-done.5.one, bf16[400,1024]{1,0:T(8,128)(2,1)} %collective-permute-done.6.two, bf16[384,1024]{1,0:T(8,128)(2,1)} %collective-permute-done.7.three, ...), custom_call_target="tpu_custom_call" | custom-call | flops 4831838208 | bytes 9437184 | tf_op jit(solution)/shard_map/pallas_call | solution.py:716
  418.9 3.3 collective-permute-done.24
  425.6 14.6 %shard_map.501 = (bf16[2,768,1024]{2,1,0:T(8,128)(2,1)}, bf16[1024,768]{1,0:T(8,128)(2,1)}, f32[12,2,1024]{2,1,0:T(2,128)}) custom-call(bf16[784,1024]{1,0:T(8,128)(2,1)} %copy-done.1, bf16[784,1024]{1,0:T(8,128)(2,1)} %copy-done.1, bf16[784,1024]{1,0:T(8,128)(2,1)} %copy-done.3, bf16[784,1024]{1,0:T(8,128)(2,1)} %copy-done.3, f32[12,6,1024]{2,1,0:T(8,128)} %reshape.439.mod, ...), custom_call_target="tpu_custom_call" | custom-call | flops 4831838208 | bytes 9437184 | tf_op jit(solution)/shard_map/pallas_call | solution.py:716
  445.4 5.5 all-to-all-start.4
  451.0 3.9 slice_bitcast_fusion
  463.1 13.5 %collective-permute-done.28 = bf16[2,32,2048]{2,1,0:T(8,128)(2,1)S(1)} collective-permute-done((bf16[2,32,2048]{2,1,0:T(8,128)(2,1)S(1)}, bf16[2,32,2048]{2,1,0:T(8,128)(2,1)S(1)}, u32[]{:S(2)}, u32[]{:S(2)}) %collective-permute-start.28) | collective-permute-done | bytes 262176 | tf_op jit(solution)/shard_map/ppermute | solution.py:776
  482.2 15.4 %collective-permute-done.27.far2 = bf16[384,1024]{1,0:T(8,128)(2,1)} collective-permute-done((bf16[384,1024]{1,0:T(8,128)(2,1)}, bf16[384,1024]{1,0:T(8,128)(2,1)}, u32[]{:S(2)}, u32[]{:S(2)}) %collective-permute-start.27) | collective-permute-done | bytes 786464 | tf_op jit(solution)/shard_map/ppermute | solution.py:776
  497.7 5.2 shard_map.503
  502.8 7.9 %shard_map.502 = f32[12,64,1024]{2,1,0:T(8,128)} custom-call(bf16[12,64,1024]{2,1,0:T(8,128)(2,1)} %bitcast.156, f32[12,6,1024]{2,1,0:T(8,128)} %reshape.439.mod, f32[12,64,1024]{2,1,0:T(8,128)} %get-tuple-element.221.middle_grad, bf16[768,1024]{1,0:T(8,128)(2,1)} %get-tuple-element.273.one, bf16[768,1024]{1,0:T(8,128)(2,1)} %collective-permute-done.26.two, ...), custom_call_target="tpu_custom_call" | custom-call | flops 15728640 | bytes 12582912 | tf_op jit(solution)/shard_map/pallas_call | solution.py:746
  513.1 3.7 shard_map.505
  525.4 12.4 %all_to_all.30 = f32[32,8,128]{2,1,0:T(8,128)S(1)} all-to-all(f32[32,8,128]{2,1,0:T(8,128)S(1)} %broadcast_in_dim.40), channel_id=1, replica_groups=mesh['clip'=8,'x'=2,'core'=2] {'clip','x','core'}, dimensions={0} | all-to-all | bytes 262144 | tf_op jit(solution)/shard_map/all_to_all | solution.py:1062
  (312 shorter events, 109.8 us)
Async XLA Ops:
  10.1 15.3 %collective-permute-start.4 = (bf16[32,768]{1,0:T(8,128)(2,1)}, bf16[32,768]{1,0:T(8,128)(2,1)}, u32[]{:S(2)}, u32[]{:S(2)}) collective-permute-start(bf16[32,768]{1,0:T(8,128)(2,1)} %get-tuple-element.303), channel_id=1, source_target_pairs={{0,3},{1,2},{2,1},{3,0},{4,7},{5,6},{6,5},{7,4},{8,11},{9,10},{10,... | collective-permute-start | bytes 147464 | tf_op jit(solution)/shard_map/ppermute | solution.py:776
  12.5 12.9 %collective-permute-start.3 = (bf16[32,768]{1,0:T(8,128)(2,1)}, bf16[32,768]{1,0:T(8,128)(2,1)}, u32[]{:S(2)}, u32[]{:S(2)}) collective-permute-start(bf16[32,768]{1,0:T(8,128)(2,1)} %get-tuple-element.304), channel_id=1, source_target_pairs={{0,2},{1,3},{2,0},{3,1},{4,6},{5,7},{6,4},{7,5},{8,10},{9,11},{10,... | collective-permute-start | bytes 147464 | tf_op jit(solution)/shard_map/ppermute | solution.py:776
  13.1 12.3 %collective-permute-start.2 = (bf16[32,768]{1,0:T(8,128)(2,1)S(1)}, bf16[32,768]{1,0:T(8,128)(2,1)}, u32[]{:S(2)}, u32[]{:S(2)}) collective-permute-start(bf16[32,768]{1,0:T(8,128)(2,1)S(1)} %get-tuple-element.305), channel_id=1, source_target_pairs={{0,1},{1,0},{2,3},{3,2},{4,5},{5,4},{6,7},{7,6},{8,9},{9,8},{10,11... | collective-permute-start | bytes 147464 | tf_op jit(solution)/shard_map/ppermute | solution.py:776
  14.1 27.7 %collective-permute-start.5 = (bf16[384,1024]{1,0:T(8,128)(2,1)}, bf16[384,1024]{1,0:T(8,128)(2,1)}, u32[]{:S(2)}, u32[]{:S(2)}) collective-permute-start(bf16[384,1024]{1,0:T(8,128)(2,1)} %bitcast.34), channel_id=1, source_target_pairs={{0,2},{2,0},{1,3},{3,1},{4,6},{6,4},{5,7},{7,5},{8,10},{10,8},{9,1... | collective-permute-start | bytes 2359304 | tf_op jit(solution)/shard_map/ppermute | solution.py:776
  18.0 22.2 %all-to-all-start = ((bf16[8,12,1024]{2,1,0:T(8,128)(2,1)}), bf16[8,12,1024]{2,1,0:T(8,128)(2,1)S(1)}, u32[]{:S(2)}, u32[]{:S(2)}) async-start(bf16[8,12,1024]{2,1,0:T(8,128)(2,1)} %broadcast_in_dim.34), calls=%async_computation | async-start | bytes 524288 | tf_op jit(solution)/shard_map/all_to_all | solution.py:876
  23.8 56.0 %all-gather.3.cloned.1.call-start = ((), (), s32[]{:S(2)}) async-start(), calls=%async_computation.7 | async-start | bytes 1769472 | tf_op jit(solution)/shard_map/all_gather | solution.py:868
  31.9 8.0 %collective-permute-start.1 = (bf16[2,32,2048]{2,1,0:T(8,128)(2,1)S(1)}, bf16[2,32,2048]{2,1,0:T(8,128)(2,1)S(1)}, u32[]{:S(2)}, u32[]{:S(2)}) collective-permute-start(bf16[2,32,2048]{2,1,0:T(8,128)(2,1)S(1)} %bitcast.198), channel_id=1, source_target_pairs={{0,2},{2,0},{1,3},{3,1},{4,6},{6,4},{5,7},{7,5},{8,10},{10,8},{9,1... | collective-permute-start | bytes 786440 | tf_op jit(solution)/shard_map/ppermute | solution.py:776
  41.8 36.3 %collective-permute-start.6 = (bf16[400,1024]{1,0:T(8,128)(2,1)}, bf16[400,1024]{1,0:T(8,128)(2,1)}, u32[]{:S(2)}, u32[]{:S(2)}) collective-permute-start(bf16[400,1024]{1,0:T(8,128)(2,1)} %slice.200), channel_id=1, source_target_pairs={{0,2},{2,0},{1,3},{3,1},{4,6},{6,4},{5,7},{7,5},{8,10},{10,8},{9,1... | collective-permute-start | bytes 2457608 | tf_op jit(solution)/shard_map/ppermute | solution.py:776
  46.9 28.9 %all-to-all-start.1 = ((f32[32,12,192]{2,1,0:T(8,128)}), f32[32,12,192]{2,1,0:T(8,128)}, u32[]{:S(2)}, u32[]{:S(2)}) async-start(f32[32,12,192]{2,1,0:T(8,128)} %bitcast.182), calls=%async_computation.1 | async-start | bytes 1048576 | tf_op jit(solution)/shard_map/all_to_all | solution.py:888
  52.0 144.7 %all-gather.5.cloned.1.call-start = ((), (), s32[]{:S(2)}) async-start(), calls=%async_computation.8 | async-start | bytes 8912896 | tf_op jit(solution)/shard_map/all_gather | solution.py:900
  85.5 13.4 %collective-permute-start.7 = (bf16[384,1024]{1,0:T(8,128)(2,1)}, bf16[384,1024]{1,0:T(8,128)(2,1)}, u32[]{:S(2)}, u32[]{:S(2)}) collective-permute-start(bf16[384,1024]{1,0:T(8,128)(2,1)} %collective-permute-done.5.one), channel_id=1, source_target_pairs={{0,1},{1,0},{2,3},{3,2},{4,5},{5,4},{6,7},{7,6},{8,9},{9,8},{10,11... | collective-permute-start | bytes 2359304 | tf_op jit(solution)/shard_map/ppermute | solution.py:776
  85.7 13.3 %collective-permute-start.8 = (bf16[400,1024]{1,0:T(8,128)(2,1)}, bf16[400,1024]{1,0:T(8,128)(2,1)}, u32[]{:S(2)}, u32[]{:S(2)}) collective-permute-start(bf16[400,1024]{1,0:T(8,128)(2,1)} %collective-permute-done.6.two), channel_id=1, source_target_pairs={{0,1},{1,0},{2,3},{3,2},{4,5},{5,4},{6,7},{7,6},{8,9},{9,8},{10,11... | collective-permute-start | bytes 2457608 | tf_op jit(solution)/shard_map/ppermute | solution.py:776
  87.7 57.9 %collective-permute-start.10 = (bf16[12,64,1024]{2,1,0:T(8,128)(2,1)}, bf16[12,64,1024]{2,1,0:T(8,128)(2,1)S(1)}, u32[]{:S(2)}, u32[]{:S(2)}) collective-permute-start(bf16[12,64,1024]{2,1,0:T(8,128)(2,1)} %bitcast.160), channel_id=1, source_target_pairs={{0,2},{2,0},{1,3},{3,1},{4,6},{6,4},{5,7},{7,5},{8,10},{10,8},{9,1... | collective-permute-start | bytes 4718600 | tf_op jit(solution)/shard_map/ppermute | solution.py:776
  101.4 48.2 %all-to-all-start.2 = ((bf16[8,2,32,1024]{3,2,1,0:T(8,128)(2,1)}), bf16[8,2,32,1024]{3,2,1,0:T(8,128)(2,1)S(1)}, u32[]{:S(2)}, u32[]{:S(2)}) async-start(bf16[8,2,32,1024]{3,2,1,0:T(8,128)(2,1)} %broadcast_in_dim.39), calls=%async_computation.2 | async-start | bytes 2097152 | tf_op jit(solution)/shard_map/all_to_all | solution.py:933
  106.7 337.3 %reduce-scatter.2.cloned.1.call-start = ((), (), s32[]{:S(2)}) async-start(), calls=%async_computation.9 | async-start | bytes 8912896 | tf_op jit(solution)/shard_map/reduce_scatter | solution.py:975
  152.0 31.2 %collective-permute-start.14 = (bf16[256,768]{1,0:T(8,128)(2,1)}, bf16[256,768]{1,0:T(8,128)(2,1)S(1)}, u32[]{:S(2)}, u32[]{:S(2)}) collective-permute-start(bf16[256,768]{1,0:T(8,128)(2,1)} %get-tuple-element.278), channel_id=1, source_target_pairs={{0,3},{1,2},{2,1},{3,0},{4,7},{5,6},{6,5},{7,4},{8,11},{9,10},{10,... | collective-permute-start | bytes 1179656 | tf_op jit(solution)/shard_map/ppermute | solution.py:776
  152.3 30.8 %collective-permute-start.13 = (bf16[256,768]{1,0:T(8,128)(2,1)S(1)}, bf16[256,768]{1,0:T(8,128)(2,1)S(1)}, u32[]{:S(2)}, u32[]{:S(2)}) collective-permute-start(bf16[256,768]{1,0:T(8,128)(2,1)S(1)} %get-tuple-element.279), channel_id=1, source_target_pairs={{0,2},{1,3},{2,0},{3,1},{4,6},{5,7},{6,4},{7,5},{8,10},{9,11},{10,... | collective-permute-start | bytes 1179656 | tf_op jit(solution)/shard_map/ppermute | solution.py:776
  153.5 27.8 %collective-permute-start.11 = (bf16[8,2,32,1024]{3,2,1,0:T(8,128)(2,1)S(1)}, bf16[8,2,32,1024]{3,2,1,0:T(8,128)(2,1)}, u32[]{:S(2)}, u32[]{:S(2)}) collective-permute-start(bf16[8,2,32,1024]{3,2,1,0:T(8,128)(2,1)S(1)} %all-to-all-done.2.mine), channel_id=1, source_target_pairs={{0,1},{1,0},{2,3},{3,2},{4,5},{5,4},{6,7},{7,6},{8,9},{9,8},{10,11... | collective-permute-start | bytes 3145736 | tf_op jit(solution)/shard_map/ppermute | solution.py:776
  195.1 29.7 %collective-permute-start.15 = (bf16[384,1024]{1,0:T(8,128)(2,1)}, bf16[384,1024]{1,0:T(8,128)(2,1)S(1)}, u32[]{:S(2)}, u32[]{:S(2)}) collective-permute-start(bf16[384,1024]{1,0:T(8,128)(2,1)} %get-tuple-element.160.hidden.refs_0_), channel_id=1, source_target_pairs={{0,2},{2,0},{1,3},{3,1},{4,6},{6,4},{5,7},{7,5},{8,10},{10,8},{9,1... | collective-permute-start | bytes 2359304 | tf_op jit(solution)/shard_map/ppermute | solution.py:776
  210.4 30.0 %collective-permute-start.16 = (bf16[384,1024]{1,0:T(8,128)(2,1)S(1)}, bf16[384,1024]{1,0:T(8,128)(2,1)S(1)}, u32[]{:S(2)}, u32[]{:S(2)}) collective-permute-start(bf16[384,1024]{1,0:T(8,128)(2,1)S(1)} %copy-done.51), channel_id=1, source_target_pairs={{0,2},{2,0},{1,3},{3,1},{4,6},{6,4},{5,7},{7,5},{8,10},{10,8},{9,1... | collective-permute-start | bytes 2359304 | tf_op jit(solution)/shard_map/ppermute | solution.py:776
  238.9 37.5 %collective-permute-start.17 = (bf16[384,1024]{1,0:T(8,128)(2,1)}, bf16[384,1024]{1,0:T(8,128)(2,1)S(1)}, u32[]{:S(2)}, u32[]{:S(2)}) collective-permute-start(bf16[384,1024]{1,0:T(8,128)(2,1)} %get-tuple-element.180), channel_id=1, source_target_pairs={{0,2},{2,0},{1,3},{3,1},{4,6},{6,4},{5,7},{7,5},{8,10},{10,8},{9,1... | collective-permute-start | bytes 2359304 | tf_op jit(solution)/shard_map/ppermute | solution.py:776
  254.9 21.6 %collective-permute-start.18 = (bf16[384,1024]{1,0:T(8,128)(2,1)}, bf16[384,1024]{1,0:T(8,128)(2,1)S(1)}, u32[]{:S(2)}, u32[]{:S(2)}) collective-permute-start(bf16[384,1024]{1,0:T(8,128)(2,1)} %get-tuple-element.181), channel_id=1, source_target_pairs={{0,2},{2,0},{1,3},{3,1},{4,6},{6,4},{5,7},{7,5},{8,10},{10,8},{9,1... | collective-permute-start | bytes 2359304 | tf_op jit(solution)/shard_map/ppermute | solution.py:776
  296.3 107.3 %all-to-all-start.3 = ((bf16[32,32,1024]{2,1,0:T(8,128)(2,1)}), bf16[32,32,1024]{2,1,0:T(8,128)(2,1)}, u32[]{:S(2)}, u32[]{:S(2)}) async-start(bf16[32,32,1024]{2,1,0:T(8,128)(2,1)} %bitcast.183), calls=%async_computation.3 | async-start | bytes 4194304 | tf_op jit(solution)/shard_map/all_to_all | solution.py:986
  300.1 50.4 %collective-permute-start.20 = (bf16[256,768]{1,0:T(8,128)(2,1)S(1)}, bf16[256,768]{1,0:T(8,128)(2,1)}, u32[]{:S(2)}, u32[]{:S(2)}) collective-permute-start(bf16[256,768]{1,0:T(8,128)(2,1)S(1)} %copy-done.55), channel_id=1, source_target_pairs={{0,2},{1,3},{2,0},{3,1},{4,6},{5,7},{6,4},{7,5},{8,10},{9,11},{10,... | collective-permute-start | bytes 1179656 | tf_op jit(solution)/shard_map/ppermute | solution.py:776
  302.0 48.5 %collective-permute-start.21 = (bf16[256,768]{1,0:T(8,128)(2,1)S(1)}, bf16[256,768]{1,0:T(8,128)(2,1)}, u32[]{:S(2)}, u32[]{:S(2)}) collective-permute-start(bf16[256,768]{1,0:T(8,128)(2,1)S(1)} %copy-done.54), channel_id=1, source_target_pairs={{0,3},{1,2},{2,1},{3,0},{4,7},{5,6},{6,5},{7,4},{8,11},{9,10},{10,... | collective-permute-start | bytes 1179656 | tf_op jit(solution)/shard_map/ppermute | solution.py:776
  350.5 53.0 %collective-permute-start.22 = (bf16[384,1024]{1,0:T(8,128)(2,1)}, bf16[384,1024]{1,0:T(8,128)(2,1)S(1)}, u32[]{:S(2)}, u32[]{:S(2)}) collective-permute-start(bf16[384,1024]{1,0:T(8,128)(2,1)} %get-tuple-element.201), channel_id=1, source_target_pairs={{0,2},{2,0},{1,3},{3,1},{4,6},{6,4},{5,7},{7,5},{8,10},{10,8},{9,1... | collective-permute-start | bytes 2359304 | tf_op jit(solution)/shard_map/ppermute | solution.py:776
  352.0 51.5 %collective-permute-start.23 = (bf16[384,1024]{1,0:T(8,128)(2,1)}, bf16[384,1024]{1,0:T(8,128)(2,1)}, u32[]{:S(2)}, u32[]{:S(2)}) collective-permute-start(bf16[384,1024]{1,0:T(8,128)(2,1)} %get-tuple-element.202), channel_id=1, source_target_pairs={{0,2},{2,0},{1,3},{3,1},{4,6},{6,4},{5,7},{7,5},{8,10},{10,8},{9,1... | collective-permute-start | bytes 2359304 | tf_op jit(solution)/shard_map/ppermute | solution.py:776
  424.1 19.8 %collective-permute-start.25 = (bf16[384,1024]{1,0:T(8,128)(2,1)}, bf16[384,1024]{1,0:T(8,128)(2,1)S(1)}, u32[]{:S(2)}, u32[]{:S(2)}) collective-permute-start(bf16[384,1024]{1,0:T(8,128)(2,1)} %get-tuple-element.275), channel_id=1, source_target_pairs={{0,2},{2,0},{1,3},{3,1},{4,6},{6,4},{5,7},{7,5},{8,10},{10,8},{9,1... | collective-permute-start | bytes 2359304 | tf_op jit(solution)/shard_map/ppermute | solution.py:776
  445.4 65.3 %all-to-all-start.4 = ((bf16[32,38,768]{2,1,0:T(8,128)(2,1)}), bf16[32,38,768]{2,1,0:T(8,128)(2,1)S(1)}, u32[]{:S(2)}, u32[]{:S(2)}) async-start(bf16[32,38,768]{2,1,0:T(8,128)(2,1)} %pad_maximum_fusion), calls=%async_computation.5 | async-start | bytes 3932160 | tf_op jit(solution)/shard_map/all_to_all | solution.py:1037
  454.9 48.0 %collective-permute-start.26 = (bf16[768,1024]{1,0:T(8,128)(2,1)}, bf16[768,1024]{1,0:T(8,128)(2,1)}, u32[]{:S(2)}, u32[]{:S(2)}) collective-permute-start(bf16[768,1024]{1,0:T(8,128)(2,1)} %get-tuple-element.272), channel_id=1, source_target_pairs={{0,1},{1,0},{2,3},{3,2},{4,5},{5,4},{6,7},{7,6},{8,9},{9,8},{10,11... | collective-permute-start | bytes 4718600 | tf_op jit(solution)/shard_map/ppermute | solution.py:776
  458.5 18.1 %collective-permute-start.28 = (bf16[2,32,2048]{2,1,0:T(8,128)(2,1)S(1)}, bf16[2,32,2048]{2,1,0:T(8,128)(2,1)S(1)}, u32[]{:S(2)}, u32[]{:S(2)}) collective-permute-start(bf16[2,32,2048]{2,1,0:T(8,128)(2,1)S(1)} %bitcast.196), channel_id=1, source_target_pairs={{0,2},{2,0},{1,3},{3,1},{4,6},{6,4},{5,7},{7,5},{8,10},{10,8},{9,1... | collective-permute-start | bytes 786440 | tf_op jit(solution)/shard_map/ppermute | solution.py:776
  462.7 34.9 %collective-permute-start.27 = (bf16[384,1024]{1,0:T(8,128)(2,1)}, bf16[384,1024]{1,0:T(8,128)(2,1)}, u32[]{:S(2)}, u32[]{:S(2)}) collective-permute-start(bf16[384,1024]{1,0:T(8,128)(2,1)} %get-tuple-element.225), channel_id=1, source_target_pairs={{0,2},{2,0},{1,3},{3,1},{4,6},{6,4},{5,7},{7,5},{8,10},{10,8},{9,1... | collective-permute-start | bytes 2359304 | tf_op jit(solution)/shard_map/ppermute | solution.py:776
  (61 other events, 433.9 us)
Sparse Core Ops, SparseCore 0:
  27.8 51.9 all-gather.2
  82.5 88.0 all-gather.4
  276.6 139.1 reduce-scatter.1

commit v9 on v8

--- a/solution.py
+++ b/solution.py
@@ -663,9 +663,9 @@
 
 def first_back_kernel(last, one, two, three, four, mod, dq, dk, dv, weight, *rest):
     if last:
-        raw_in, mod_in, grads, raw, mod_grad, total, held = rest
+        raw_in, mod_in, grad1, grad2, raw, mod_grad, total, held = rest
     else:
-        grads, total, mod_grad, held = rest
+        grad1, grad2, total, mod_grad, held = rest
     step = pl.program_id(0)
     chunk = mod.shape[0]
 
@@ -679,7 +679,16 @@
     pieces = jnp.concatenate([dq[...], dk[...], dv[...]], axis=0)
     total[...] += dot(pieces, hidden)
     back = dot(pieces, weight[...], TN)
-    grads[...] = back.astype(bf16).reshape(grads.shape)
+    low = back.astype(bf16)
+
+    @pl.when(step < 2)
+    def _():
+        grad1[...] = low
+
+    @pl.when(step >= 2)
+    def _():
+        grad2[...] = low
+
     back = back.reshape(shape)
     place = pl.ds(lax.rem(step, 2) * chunk, chunk)
     mod_grad[place, 0:1] += jnp.sum(back, axis=1, keepdims=True)
@@ -701,23 +710,26 @@
     moved = pl.BlockSpec((rows, block), lambda i: (0, i + offset * 4))
     in_specs = specs + [pl.BlockSpec((rows, block), lambda i: (0, i)), moved, moved, whole()]
     operands = [piece for piece, _ in pieces] + [mod, dq, dk, dv, weight]
-    grads = jax.ShapeDtypeStruct((2, count // 2, width), bf16)
-    grads_spec = pl.BlockSpec((1, block, width), lambda i: (i // 2, lax.rem(i, 2), 0))
+    grads = jax.ShapeDtypeStruct((count // 2, width), bf16)
+    grads_specs = [
+        pl.BlockSpec((block, width), lambda i: (jnp.minimum(i, 1), 0)),
+        pl.BlockSpec((block, width), lambda i: (jnp.maximum(i - 2, 0), 0)),
+    ]
     held = VMEM((block, width), bf16)
     mods = jax.ShapeDtypeStruct((frames, 2, width), f32)
     if last:
         in_specs += [whole(), whole()]
         operands += list(sums)
-        out_shape = [grads, jax.ShapeDtypeStruct((width, 3 * rows), bf16), mods]
+        out_shape = [grads, grads, jax.ShapeDtypeStruct((width, 3 * rows), bf16), mods]
         scratch = [VMEM((3 * rows, width), f32), held]
     else:
-        out_shape = [grads, jax.ShapeDtypeStruct((3 * rows, width), f32), mods]
+        out_shape = [grads, grads, jax.ShapeDtypeStruct((3 * rows, width), f32), mods]
         scratch = [held]
     return pl.pallas_call(
         functools.partial(first_back_kernel, last),
         grid=(4,),
         in_specs=in_specs,
-        out_specs=[grads_spec, whole(), whole()],
+        out_specs=grads_specs + [whole(), whole()],
         out_shape=out_shape,
         scratch_shapes=scratch,
         compiler_params=params(),
@@ -763,9 +775,8 @@
     count, owners, rows, columns = pieces.shape
     return pl.pallas_call(
         total_kernel,
-        grid=(owners,),
-        in_specs=[pl.BlockSpec((count, 1, rows, columns), lambda i: (0, i, 0, 0))],
-        out_specs=pl.BlockSpec((1, rows, columns), lambda i: (i, 0, 0)),
+        in_specs=[whole()],
+        out_specs=whole(),
         out_shape=jax.ShapeDtypeStruct((owners, rows, columns), f32),
         compiler_params=params(),
         cost_estimate=cost(pieces.size, 3 * pieces.size),
@@ -865,14 +876,12 @@
     attend_mine = attend_weight.astype(bf16).reshape(shard, 3, rows, features)
     attend_mine = attend_mine.transpose(2, 0, 1, 3).reshape(rows, shard, 3 * features)
     attend_mine = relative(trade(relative(attend_mine, row), ROW, rows), row)
+
+    cond_act = jax.nn.silu(condition[0].astype(f32)).astype(bf16)
+    cond_act, tok0, attend_mine = lax.optimization_barrier((cond_act, tok0, attend_mine))
     attend_full = lax.all_gather(
         attend_mine.reshape(rows * shard, 3 * features), "clip", axis=0, tiled=True
     )
-
-    cond_act = jax.nn.silu(condition[0].astype(f32)).astype(bf16)
-    cond_act, tok0 = lax.optimization_barrier((cond_act, tok0))
-    project_mine = project_weight.T.astype(bf16)
-    project_mine = relative(jnp.stack([project_mine, swap(project_mine, "x", 2, 1)]), far)
     cond_all = lax.all_to_all(
         jnp.broadcast_to(cond_act[None], (clips, frames, width)), "clip", 0, 0, tiled=True
     ).reshape(clips * frames, width)
@@ -880,7 +889,11 @@
         f32
     )
     part = mod_mine.shape[1]
-    tok2_two, mod_mine, tok2_one = lax.optimization_barrier((tok0[count // 2 :], mod_mine, tok2_one))
+    tok2_two, mod_mine, tok2_one, project_mine, feed_wide, feed_narrow = lax.optimization_barrier(
+        (tok0[count // 2 :], mod_mine, tok2_one, project_weight, widen_weight, narrow_weight)
+    )
+    project_mine = project_mine.T.astype(bf16)
+    project_mine = relative(jnp.stack([project_mine, swap(project_mine, "x", 2, 1)]), far)
     tok2_two = swap(tok2_two, "x", 2, 1)
     mod_mine = jnp.broadcast_to(
         mod_mine.reshape(clips, 1, frames, part), (clips, rows, frames, part)
@@ -889,7 +902,7 @@
     mod = mod.transpose(1, 0, 2).reshape(frames, 6, width)
 
     units = widen_weight.shape[1]
-    feed_mine = jnp.stack([widen_weight.astype(bf16), narrow_weight.T.astype(bf16)])
+    feed_mine = jnp.stack([feed_wide.astype(bf16), feed_narrow.T.astype(bf16)])
     feed_mine = feed_mine.reshape(2, shard, 2, units // 2).transpose(2, 0, 1, 3)
     feed_mine = relative(trade(relative(feed_mine, far), "x", 2), far)
     feed_mine, attend_full, mod, tok2_two = lax.optimization_barrier(
@@ -918,28 +931,24 @@
         return jnp.cos(angles), jnp.sin(angles), jnp.where(small[2:3] > 0.5, 0.0, MASKED)
 
     cos_near, sin_near, bias_near = places_of((tok0, tok1))
+    cos_far, sin_far, bias_far = places_of((tok2_two, tok3_two))
+    project_full = lax.all_to_all(
+        jnp.broadcast_to(project_mine[None], (clips, 2, shard, width)), "clip", 0, 0, tiled=True
+    )
+
     near = ((tok0, 0), (tok0, 1), (tok1, 0), (tok1, 1))
     qkv_near = project_qkv(near, mod, attend_turned, cos_near, sin_near)
-    qkv_near, tok2_one, tok2_two, tok3_one, tok3_two, project_mine = lax.optimization_barrier(
-        (qkv_near, tok2_one, tok2_two, tok3_one, tok3_two, project_mine)
-    )
-    cos_far, sin_far, bias_far = places_of((tok2_two, tok3_two))
+    qkv_near, project_full = lax.optimization_barrier((qkv_near, project_full))
     across = ((tok2_one, 0), (tok2_two, 0), (tok3_one, 0), (tok3_two, 0))
     qkv_far = project_qkv(across, mod, attend_turned, cos_far, sin_far)
     cosine = jnp.concatenate([cos_near, cos_far], axis=1)
     sine = jnp.concatenate([sin_near, sin_far], axis=1)
     bias = jnp.concatenate([bias_near, bias_far], axis=1)
 
-    project_full = lax.all_to_all(
-        jnp.broadcast_to(project_mine[None], (clips, 2, shard, width)), "clip", 0, 0, tiled=True
-    )
-
     cot_far, mod = lax.optimization_barrier((upstream, mod))
     cot_far = swap(cot_far, "x", 2, 1)
     out_far, lse_far = attend(qkv_far, qkv_near, qkv_far, bias)
-    out_far, qkv_near, project_full, cot_far = lax.optimization_barrier(
-        (out_far, qkv_near, project_full, cot_far)
-    )
+    out_far, qkv_near, cot_far = lax.optimization_barrier((out_far, qkv_near, cot_far))
     project_near = swap(project_full, "core", 2, 1)
     part2 = swap(out_far[0], ROW, rows, 2)
     part3 = swap(out_far[1], ROW, rows, 3)
@@ -1002,24 +1011,26 @@
     )
     dq_far, project_raw, out3, out4 = lax.optimization_barrier((dq_far, project_raw, out3, out4))
     project_sum = total_over(project_raw.reshape(devices, 1, shard, width))[0].T
-    back_far, raw, mod_early = first_back(across, mod, dq_far, dk, dv, attend_turned, 1)
-    back_far = (
-        back_far[0].astype(f32) + swap(back_far[1], ROW, rows, 1).astype(f32)
-    ).astype(bf16)
-    back_far, dq_near = lax.optimization_barrier((back_far, dq_near))
-    far_one = swap(back_far[:half], "x", 2, 1)
+    back1, back2, raw, mod_early = first_back(across, mod, dq_far, dk, dv, attend_turned, 1)
+    back2 = swap(back2, ROW, rows, 1)
+    far_one, far_two = [
+        (back1[at : at + half].astype(f32) + back2[at : at + half].astype(f32)).astype(bf16)
+        for at in (0, half)
+    ]
+    far_one, far_two, dq_near = lax.optimization_barrier((far_one, far_two, dq_near))
+    far_one = swap(far_one, "x", 2, 1)
     extra = -(-2 * frames * part // (3 * features))
-    back_near, attend_raw, mod_early = first_back(
+    back1, back2, attend_raw, mod_early = first_back(
         near, mod, dq_near, dk, dv, attend_turned, 0, (raw, mod_early)
     )
     attend_raw, far_one, feed_sum, far_two = lax.optimization_barrier(
-        (attend_raw, far_one, feed_sum, back_far[half:])
+        (attend_raw, far_one, feed_sum, far_two)
     )
     far_two = swap(far_two, "x", 2, 1)
     feed_sum = relative(trade(relative(feed_sum, far), "x", 2), far).astype(f32)
     widen_sum, narrow_sum = feed_sum.transpose(1, 2, 0, 3).reshape(2, shard, units)
     narrow_sum = narrow_sum.T
-    back_near = (back_near[0], swap(back_near[1], ROW, rows, 1))
+    back_near = (back1, swap(back2, ROW, rows, 1))
 
     mod_grad = jnp.concatenate([mod_early, mod_late, mod_gate], axis=1)
     mod_grad = mod_grad.reshape(frames, devices, part).transpose(1, 0, 2).reshape(devices, -1)
@@ -1035,7 +1046,6 @@
         axis=1,
     )
     attend_raw = lax.all_to_all(attend_raw, both, 0, 0, tiled=True)
-    out3, far_two = lax.optimization_barrier((out3, far_two))
     block_out = block_output((out1, out2, out3, out4), own, att_out, mod)
     input_gradient = input_back(own, mod, middle_grad, back_near + (far_one, far_two))
     attend_raw, input_gradient, block_out, project_sum = lax.optimization_barrier(

time: 569 us -> 586 us (1.030)
  waiting for transfers between devices: 70.5 us -> 93.3 us
  local copies, waits for them, and re-layouts: 38.7 us -> 29.6 us
    all_to_all x1, waiting for transfers between devices: 4.06 us -> 28 us  [local(): lax.all_to_all(jnp.broadcast_to(project_mine[None], (clips, 2, shard, wid...]
    all_to_all x1, waiting for transfers between devices: 0.01 us -> 7.06 us  [local(): lax.all_to_all(jnp.broadcast_to(cond_act[None], (clips, frames, width)),...]
  transfers between devices with their start and end apart: 37 -> 37, of which waited for: 10 -> 12; matrix products, arithmetic and copies ran while one was open for 9% -> 8% of each run, Pallas kernels for 57% -> 56%
where the time goes in v9:
time: 586 us; the launch traced here: 579 us
  Pallas kernels  325 us (55%)
  waiting for transfers between devices  93.3 us (16%)
  starting transfers between devices  52.1 us (9%)
  other arithmetic  42.3 us (7%)
  local copies, waits for them, and re-layouts  29.6 us (5%)
  between operations  21.8 us (4%)
  blocking collectives  12.6 us (2%)
    pallas_call x2, Pallas kernels, attend_back(): pl.pallas_call(functools.partial(attend_back_kernel, heads, last), grid=(...  99.4 us
    pallas_call x2, Pallas kernels, attend(): pl.pallas_call(functools.partial(attend_kernel, heads), grid=(count // bl...  54.9 us
    pallas_call x4, Pallas kernels, feed_forward(): pl.pallas_call(feed_kernel, grid=(units // block,), in_specs=[spec, flat,...  54.4 us
    ppermute x29, waiting for transfers between devices, swap(): lax.ppermute(value, axis, [(place, place ^ step) for place in range(size)])  39.2 us
    pallas_call x2, Pallas kernels, first_back(): pl.pallas_call(functools.partial(first_back_kernel, last), grid=(4,), in_...  31 us
    all_to_all x1, waiting for transfers between devices, local(): lax.all_to_all(jnp.broadcast_to(project_mine[None], (clips, 2, shard, wid...  28 us
    ppermute x29, starting transfers between devices, swap(): lax.ppermute(value, axis, [(place, place ^ step) for place in range(size)])  26.2 us
    pallas_call x1, Pallas kernels, feed_weights(): pl.pallas_call(functools.partial(feed_weight_kernel, len(hidden)), grid=(...  21 us
  transfers between devices with their start and end apart: 37, of which 12 were waited for; matrix products, arithmetic and copies ran while one was open for 8% of the time, Pallas kernels for 56%

profile of v9, /device:TPU:0, one launch (start us, length us, event | category | flops | bytes accessed | tf_op | source)
XLA Modules:
  0.0 578.5 jit_solution(13969899045094563987)
XLA Ops:
  17.9 6.0 %all-to-all-start = ((bf16[8,12,1024]{2,1,0:T(8,128)(2,1)}), bf16[8,12,1024]{2,1,0:T(8,128)(2,1)S(1)}, u32[]{:S(2)}, u32[]{:S(2)}) async-start(bf16[8,12,1024]{2,1,0:T(8,128)(2,1)} %broadcast_in_dim.33), calls=%async_computation | async-start | bytes 524288 | tf_op jit(solution)/shard_map/all_to_all | solution.py:885
  25.7 7.1 %all-to-all-done = bf16[8,12,1024]{2,1,0:T(8,128)(2,1)S(1)} async-done(((bf16[8,12,1024]{2,1,0:T(8,128)(2,1)}), bf16[8,12,1024]{2,1,0:T(8,128)(2,1)S(1)}, u32[]{:S(2)}, u32[]{:S(2)}) %all-to-all-start) | async-done | bytes 196640 | tf_op jit(solution)/shard_map/all_to_all | solution.py:885
  41.8 5.0 all-to-all-start.1
  53.6 14.9 %all-to-all-done.1 = f32[32,12,192]{2,1,0:T(8,128)S(1)} async-done(((f32[32,12,192]{2,1,0:T(8,128)}), f32[32,12,192]{2,1,0:T(8,128)S(1)}, u32[]{:S(2)}, u32[]{:S(2)}) %all-to-all-start.1) | async-done | bytes 294944 | tf_op jit(solution)/shard_map/all_to_all | solution.py:901
  69.7 3.2 collective-permute-done.6.two
  72.9 4.1 all-gather.3.cloned.1.call-done
  83.9 4.7 all-to-all-start.2
  94.2 9.3 %shard_map.488.k1.v1.q_ref = bf16[768,1536]{1,0:T(8,128)(2,1)} custom-call(bf16[784,1024]{1,0:T(8,128)(2,1)} %copy-done.1, bf16[784,1024]{1,0:T(8,128)(2,1)} %copy-done.1, bf16[784,1024]{1,0:T(8,128)(2,1)} %copy-done.3, bf16[784,1024]{1,0:T(8,128)(2,1)} %copy-done.3, f32[12,6,1024]{2,1,0:T(8,128)} %reshape.461.mod, bf16[768,1024]{1,0:T(8,128)(2,1)} %bitcast.181, ...), custom_call_target="tpu_custom_call" | custom-call | flops 2415919104 | bytes 6291456 | tf_op jit(solution)/shard_map/pallas_call | solution.py:131
  103.5 28.0 %all-to-all-done.2.mine = bf16[8,2,32,1024]{3,2,1,0:T(8,128)(2,1)} async-done(((bf16[8,2,32,1024]{3,2,1,0:T(8,128)(2,1)}), bf16[8,2,32,1024]{3,2,1,0:T(8,128)(2,1)}, u32[]{:S(2)}, u32[]{:S(2)}) %all-to-all-start.2) | async-done | bytes 1048608 | tf_op jit(solution)/shard_map/all_to_all | solution.py:935
  133.8 9.2 %shard_map.487.q_ref.k2.v2 = bf16[768,1536]{1,0:T(8,128)(2,1)} custom-call(bf16[384,1024]{1,0:T(8,128)(2,1)} %collective-permute-done.4.one, bf16[400,1024]{1,0:T(8,128)(2,1)} %collective-permute-done.6.two, bf16[384,1024]{1,0:T(8,128)(2,1)} %collective-permute-done.7.three, bf16[400,1024]{1,0:T(8,128)(2,1)} %collective-permute-done.8.four, ...), custom_call_target="tpu_custom_call" | custom-call | flops 2415919104 | bytes 6291456 | tf_op jit(solution)/shard_map/pallas_call | solution.py:131
  143.7 27.5 %shard_map.489 = (bf16[2,256,768]{2,1,0:T(8,128)(2,1)}, f32[4,1536]{1,0:T(4,128)}) custom-call(bf16[768,1536]{1,0:T(8,128)(2,1)} %shard_map.487.q_ref.k2.v2, bf16[768,1536]{1,0:T(8,128)(2,1)} %shard_map.488.k1.v1.q_ref, bf16[768,1536]{1,0:T(8,128)(2,1)} %shard_map.487.q_ref.k2.v2, bf16[768,1536]{1,0:T(8,128)(2,1)} %shard_map.488.k1.v1.q_ref, ...), custom_call_target="tpu_custom_call" | custom-call | flops 19327352832 | bytes 3145728 | tf_op jit(solution)/shard_map/pallas_call | solution.py:186
  175.8 27.4 %shard_map.490 = (bf16[2,256,768]{2,1,0:T(8,128)(2,1)}, f32[4,1536]{1,0:T(4,128)}) custom-call(bf16[768,1536]{1,0:T(8,128)(2,1)} %shard_map.488.k1.v1.q_ref, bf16[768,1536]{1,0:T(8,128)(2,1)} %shard_map.488.k1.v1.q_ref, bf16[768,1536]{1,0:T(8,128)(2,1)} %shard_map.487.q_ref.k2.v2, bf16[768,1536]{1,0:T(8,128)(2,1)} %shard_map.488.k1.v1.q_ref, ...), custom_call_target="tpu_custom_call" | custom-call | flops 19327352832 | bytes 3145728 | tf_op jit(solution)/shard_map/pallas_call | solution.py:186
  207.1 10.2 %shard_map.491 = (f32[12,64,1024]{2,1,0:T(8,128)}, bf16[384,1024]{1,0:T(8,128)(2,1)}, bf16[384,1024]{1,0:T(8,128)(2,1)}, bf16[768,1024]{1,0:T(8,128)(2,1)}, bf16...) custom-call(s32[5]{0:T(128)} %pad_add_fusion.order, bf16[2,256,768]{2,1,0:T(8,128)(2,1)} %get-tuple-element.155.a0.out_ref, ...), custom_call_target="tpu_custom_call" | custom-call | flops 1610612736 | bytes 11010048 | tf_op jit(solution)/shard_map/pallas_call | solution.py:401
  218.9 13.8 %shard_map.492 = (f32[384,1024]{1,0:T(8,128)}, f32[384,1024]{1,0:T(8,128)}, bf16[384,2048]{1,0:T(8,128)(2,1)}, bf16[384,2048]{1,0:T(8,128)(2,1)}, f32[6,1,1024]{2,1,0:T(1,128)}) custom-call(bf16[16,2,2,32,2048]{4,3,2,1,0:T(8,128)(2,1)} %bitcast.201, bf16[384,1024]{1,0:T(8,128)(2,1)} %get-tuple-element.159.hidden.refs_0_, ...), custom_call_target="tpu_custom_call" | custom-call | flops 6442450944 | bytes 11534336 | tf_op jit(solution)/shard_map/pallas_call | solution.py:498
  233.3 13.8 %shard_map.493 = (f32[384,1024]{1,0:T(8,128)}, f32[384,1024]{1,0:T(8,128)}, bf16[384,2048]{1,0:T(8,128)(2,1)}, bf16[384,2048]{1,0:T(8,128)(2,1)}, f32[6,1,1024]{2,1,0:T(1,128)}) custom-call(bf16[16,2,2,32,2048]{4,3,2,1,0:T(8,128)(2,1)} %bitcast.202, bf16[384,1024]{1,0:T(8,128)(2,1)} %get-tuple-element.167.hidden.refs_1_, ...), custom_call_target="tpu_custom_call" | custom-call | flops 6442450944 | bytes 11534336 | tf_op jit(solution)/shard_map/pallas_call | solution.py:498
  247.9 13.3 %shard_map.494 = (bf16[384,1024]{1,0:T(8,128)(2,1)}, bf16[384,1024]{1,0:T(8,128)(2,1)}, bf16[384,2048]{1,0:T(8,128)(2,1)}, bf16[384,2048]{1,0:T(8,128)(2,1)}, f32[6,1,1024]{2,1,0:T(1,128)}) custom-call(bf16[16,2,2,32,2048]{4,3,2,1,0:T(8,128)(2,1)} %bitcast.203, bf16[384,1024]{1,0:T(8,128)(2,1)} %copy-done.52, ...), custom_call_target="tpu_custom_call" | custom-call | flops 6442450944 | bytes 11534336 | tf_op jit(solution)/shard_map/pallas_call | solution.py:498
  263.6 13.6 %shard_map.495 = (bf16[384,1024]{1,0:T(8,128)(2,1)}, bf16[384,1024]{1,0:T(8,128)(2,1)}, bf16[384,2048]{1,0:T(8,128)(2,1)}, bf16[384,2048]{1,0:T(8,128)(2,1)}, f32[6,1,1024]{2,1,0:T(1,128)}) custom-call(bf16[16,2,2,32,2048]{4,3,2,1,0:T(8,128)(2,1)} %bitcast.204, bf16[384,1024]{1,0:T(8,128)(2,1)} %copy-done.53, ...), custom_call_target="tpu_custom_call" | custom-call | flops 6442450944 | bytes 11534336 | tf_op jit(solution)/shard_map/pallas_call | solution.py:498
  277.7 21.0 %shard_map.496 = bf16[16,2,2,32,2048]{4,3,2,1,0:T(8,128)(2,1)} custom-call(bf16[384,1024]{1,0:T(8,128)(2,1)} %get-tuple-element.159.hidden.refs_0_, bf16[384,1024]{1,0:T(8,128)(2,1)} %get-tuple-element.167.hidden.refs_1_, bf16[384,1024]{1,0:T(8,128)(2,1)} %copy-done.52, bf16[384,1024]{1,0:T(8,128)(2,1)} %copy-done.53, ...), custom_call_target="tpu_custom_call" | custom-call | flops 12884901888 | bytes 20971520 | tf_op jit(solution)/shard_map/pallas_call | solution.py:549
  299.9 17.6 %shard_map.497 = (f32[12,64,1024]{2,1,0:T(8,128)}, f32[12,3,1024]{2,1,0:T(4,128)}, bf16[256,768]{1,0:T(8,128)(2,1)}, bf16[256,768]{1,0:T(8,128)(2,1)}, bf16[256,...) custom-call(s32[5]{0:T(128)} %pad_add_fusion.order, f32[384,1024]{1,0:T(8,128)} %get-tuple-element.161.into1, ...), custom_call_target="tpu_custom_call" | custom-call | flops 3221225472 | bytes 18874368 | tf_op jit(solution)/shard_map/pallas_call | solution.py:612
  318.5 4.4 all-to-all-start.3
  324.9 48.4 %shard_map.498 = (bf16[256,1536]{1,0:T(8,128)(2,1)}, f32[256,3072]{1,0:T(8,128)}, f32[256,3072]{1,0:T(8,128)}) custom-call(bf16[768,1536]{1,0:T(8,128)(2,1)} %shard_map.488.k1.v1.q_ref, bf16[768,1536]{1,0:T(8,128)(2,1)} %shard_map.488.k1.v1.q_ref, bf16[768,1536]{1,0:T(8,128)(2,1)} %shard_map.487.q_ref.k2.v2, bf16[768,1536]{1,0:T(8,128)(2,1)} %shard_map.488.k1.v1.q_ref, ...), custom_call_target="tpu_custom_call" | custom-call | flops 41070624768 | bytes 6291456 | tf_op jit(solution)/shard_map/pallas_call | solution.py:332
  375.5 51.0 %shard_map.499 = (bf16[256,1536]{1,0:T(8,128)(2,1)}, bf16[256,3072]{1,0:T(8,128)(2,1)}, bf16[256,3072]{1,0:T(8,128)(2,1)}) custom-call(bf16[768,1536]{1,0:T(8,128)(2,1)} %shard_map.487.q_ref.k2.v2, bf16[768,1536]{1,0:T(8,128)(2,1)} %shard_map.488.k1.v1.q_ref, bf16[768,1536]{1,0:T(8,128)(2,1)} %shard_map.487.q_ref.k2.v2, ...), custom_call_target="tpu_custom_call" | custom-call | flops 41070624768 | bytes 6291456 | tf_op jit(solution)/shard_map/pallas_call | solution.py:332
  426.5 15.1 %shard_map.500 = (bf16[768,1024]{1,0:T(8,128)(2,1)}, bf16[768,1024]{1,0:T(8,128)(2,1)}, f32[768,1024]{1,0:T(8,128)}, f32[12,2,1024]{2,1,0:T(2,128)}) custom-call(bf16[384,1024]{1,0:T(8,128)(2,1)} %collective-permute-done.4.one, bf16[400,1024]{1,0:T(8,128)(2,1)} %collective-permute-done.6.two, bf16[384,1024]{1,0:T(8,128)(2,1)} %collective-permute-done.7.three, ...), custom_call_target="tpu_custom_call" | custom-call | flops 4831838208 | bytes 9437184 | tf_op jit(solution)/shard_map/pallas_call | solution.py:728
  441.8 3.5 collective-permute-done.24
  445.3 3.2 add_convert_fusion
  450.0 15.9 %shard_map.501 = (bf16[768,1024]{1,0:T(8,128)(2,1)}, bf16[768,1024]{1,0:T(8,128)(2,1)}, bf16[1024,768]{1,0:T(8,128)(2,1)}, f32[12,2,1024]{2,1,0:T(2,128)}) custom-call(bf16[784,1024]{1,0:T(8,128)(2,1)} %copy-done.1, bf16[784,1024]{1,0:T(8,128)(2,1)} %copy-done.1, bf16[784,1024]{1,0:T(8,128)(2,1)} %copy-done.3, bf16[784,1024]{1,0:T(8,128)(2,1)} %copy-done.3, ...), custom_call_target="tpu_custom_call" | custom-call | flops 4831838208 | bytes 9437184 | tf_op jit(solution)/shard_map/pallas_call | solution.py:728
  469.9 5.4 all-to-all-start.4
  483.3 5.2 shard_map.503
  488.8 12.4 %collective-permute-done.28 = bf16[2,32,2048]{2,1,0:T(8,128)(2,1)S(1)} collective-permute-done((bf16[2,32,2048]{2,1,0:T(8,128)(2,1)S(1)}, bf16[2,32,2048]{2,1,0:T(8,128)(2,1)S(1)}, u32[]{:S(2)}, u32[]{:S(2)}) %collective-permute-start.28) | collective-permute-done | bytes 262176 | tf_op jit(solution)/shard_map/ppermute | solution.py:787
  506.8 15.0 %collective-permute-done.27.far2 = bf16[384,1024]{1,0:T(8,128)(2,1)} collective-permute-done((bf16[384,1024]{1,0:T(8,128)(2,1)}, bf16[384,1024]{1,0:T(8,128)(2,1)}, u32[]{:S(2)}, u32[]{:S(2)}) %collective-permute-start.27) | collective-permute-done | bytes 786464 | tf_op jit(solution)/shard_map/ppermute | solution.py:787
  521.8 8.1 %shard_map.502 = f32[12,64,1024]{2,1,0:T(8,128)} custom-call(bf16[12,64,1024]{2,1,0:T(8,128)(2,1)} %bitcast.151, f32[12,6,1024]{2,1,0:T(8,128)} %reshape.461.mod, f32[12,64,1024]{2,1,0:T(8,128)} %get-tuple-element.222.middle_grad, bf16[768,1024]{1,0:T(8,128)(2,1)} %get-tuple-element.223.one, bf16[768,1024]{1,0:T(8,128)(2,1)} %collective-permute-done.26.two, ...), custom_call_target="tpu_custom_call" | custom-call | flops 15728640 | bytes 12582912 | tf_op jit(solution)/shard_map/pallas_call | solution.py:758
  543.4 12.6 %all_to_all.30 = f32[32,8,128]{2,1,0:T(8,128)S(1)} all-to-all(f32[32,8,128]{2,1,0:T(8,128)S(1)} %broadcast_in_dim.39), channel_id=1, replica_groups=mesh['clip'=8,'x'=2,'core'=2] {'clip','x','core'}, dimensions={0} | all-to-all | bytes 262144 | tf_op jit(solution)/shard_map/all_to_all | solution.py:1072
  (306 shorter events, 107.0 us)
Async XLA Ops:
  9.5 7.2 %collective-permute-start.2 = (bf16[32,768]{1,0:T(8,128)(2,1)S(1)}, bf16[32,768]{1,0:T(8,128)(2,1)S(1)}, u32[]{:S(2)}, u32[]{:S(2)}) collective-permute-start(bf16[32,768]{1,0:T(8,128)(2,1)S(1)} %get-tuple-element.301), channel_id=1, source_target_pairs={{0,3},{1,2},{2,1},{3,0},{4,7},{5,6},{6,5},{7,4},{8,11},{9,10},{10,... | collective-permute-start | bytes 147464 | tf_op jit(solution)/shard_map/ppermute | solution.py:787
  13.5 20.2 %collective-permute-start.4 = (bf16[384,1024]{1,0:T(8,128)(2,1)}, bf16[384,1024]{1,0:T(8,128)(2,1)}, u32[]{:S(2)}, u32[]{:S(2)}) collective-permute-start(bf16[384,1024]{1,0:T(8,128)(2,1)} %bitcast.22), channel_id=1, source_target_pairs={{0,2},{2,0},{1,3},{3,1},{4,6},{6,4},{5,7},{7,5},{8,10},{10,8},{9,1... | collective-permute-start | bytes 2359304 | tf_op jit(solution)/shard_map/ppermute | solution.py:787
  17.9 14.9 %all-to-all-start = ((bf16[8,12,1024]{2,1,0:T(8,128)(2,1)}), bf16[8,12,1024]{2,1,0:T(8,128)(2,1)S(1)}, u32[]{:S(2)}, u32[]{:S(2)}) async-start(bf16[8,12,1024]{2,1,0:T(8,128)(2,1)} %broadcast_in_dim.33), calls=%async_computation | async-start | bytes 524288 | tf_op jit(solution)/shard_map/all_to_all | solution.py:885
  23.9 53.2 %all-gather.3.cloned.1.call-start = ((), (), s32[]{:S(2)}) async-start(), calls=%async_computation.7 | async-start | bytes 1769472 | tf_op jit(solution)/shard_map/all_gather | solution.py:882
  39.5 9.4 %collective-permute-start.5 = (bf16[2,32,2048]{2,1,0:T(8,128)(2,1)S(1)}, bf16[2,32,2048]{2,1,0:T(8,128)(2,1)S(1)}, u32[]{:S(2)}, u32[]{:S(2)}) collective-permute-start(bf16[2,32,2048]{2,1,0:T(8,128)(2,1)S(1)} %bitcast.189), channel_id=1, source_target_pairs={{0,2},{2,0},{1,3},{3,1},{4,6},{6,4},{5,7},{7,5},{8,10},{10,8},{9,1... | collective-permute-start | bytes 786440 | tf_op jit(solution)/shard_map/ppermute | solution.py:787
  41.8 26.7 %all-to-all-start.1 = ((f32[32,12,192]{2,1,0:T(8,128)}), f32[32,12,192]{2,1,0:T(8,128)S(1)}, u32[]{:S(2)}, u32[]{:S(2)}) async-start(f32[32,12,192]{2,1,0:T(8,128)} %bitcast.35), calls=%async_computation.1 | async-start | bytes 1048576 | tf_op jit(solution)/shard_map/all_to_all | solution.py:901
  46.8 172.1 %all-gather.5.cloned.1.call-start = ((), (), s32[]{:S(2)}) async-start(), calls=%async_computation.8 | async-start | bytes 8912896 | tf_op jit(solution)/shard_map/all_gather | solution.py:913
  47.0 25.9 %collective-permute-start.6 = (bf16[400,1024]{1,0:T(8,128)(2,1)}, bf16[400,1024]{1,0:T(8,128)(2,1)}, u32[]{:S(2)}, u32[]{:S(2)}) collective-permute-start(bf16[400,1024]{1,0:T(8,128)(2,1)} %slice.187), channel_id=1, source_target_pairs={{0,2},{2,0},{1,3},{3,1},{4,6},{6,4},{5,7},{7,5},{8,10},{10,8},{9,1... | collective-permute-start | bytes 2457608 | tf_op jit(solution)/shard_map/ppermute | solution.py:787
  78.0 11.0 %collective-permute-start.3 = (bf16[784,1024]{1,0:T(8,128)(2,1)S(1)}, bf16[784,1024]{1,0:T(8,128)(2,1)S(1)}, u32[]{:S(2)}, u32[]{:S(2)}) collective-permute-start(bf16[784,1024]{1,0:T(8,128)(2,1)S(1)} %fusion.1.one.two), channel_id=1, source_target_pairs={{0,1},{1,0},{2,3},{3,2},{4,5},{5,4},{6,7},{7,6},{8,9},{9,8},{10,11... | collective-permute-start | bytes 4816904 | tf_op jit(solution)/shard_map/ppermute | solution.py:787
  82.7 8.6 %collective-permute-start.8 = (bf16[400,1024]{1,0:T(8,128)(2,1)}, bf16[400,1024]{1,0:T(8,128)(2,1)}, u32[]{:S(2)}, u32[]{:S(2)}) collective-permute-start(bf16[400,1024]{1,0:T(8,128)(2,1)} %collective-permute-done.6.two), channel_id=1, source_target_pairs={{0,1},{1,0},{2,3},{3,2},{4,5},{5,4},{6,7},{7,6},{8,9},{9,8},{10,11... | collective-permute-start | bytes 2457608 | tf_op jit(solution)/shard_map/ppermute | solution.py:787
  83.9 47.6 %all-to-all-start.2 = ((bf16[8,2,32,1024]{3,2,1,0:T(8,128)(2,1)}), bf16[8,2,32,1024]{3,2,1,0:T(8,128)(2,1)}, u32[]{:S(2)}, u32[]{:S(2)}) async-start(bf16[8,2,32,1024]{3,2,1,0:T(8,128)(2,1)} %broadcast_in_dim.36), calls=%async_computation.2 | async-start | bytes 2097152 | tf_op jit(solution)/shard_map/all_to_all | solution.py:935
  88.7 379.7 %reduce-scatter.2.cloned.1.call-start = ((), (), s32[]{:S(2)}) async-start(), calls=%async_computation.9 | async-start | bytes 8912896 | tf_op jit(solution)/shard_map/reduce_scatter | solution.py:984
  88.7 45.1 %collective-permute-start.7 = (bf16[384,1024]{1,0:T(8,128)(2,1)}, bf16[384,1024]{1,0:T(8,128)(2,1)}, u32[]{:S(2)}, u32[]{:S(2)}) collective-permute-start(bf16[384,1024]{1,0:T(8,128)(2,1)} %collective-permute-done.4.one), channel_id=1, source_target_pairs={{0,1},{1,0},{2,3},{3,2},{4,5},{5,4},{6,7},{7,6},{8,9},{9,8},{10,11... | collective-permute-start | bytes 2359304 | tf_op jit(solution)/shard_map/ppermute | solution.py:787
  89.8 81.3 %collective-permute-start.10 = (bf16[12,64,1024]{2,1,0:T(8,128)(2,1)}, bf16[12,64,1024]{2,1,0:T(8,128)(2,1)S(1)}, u32[]{:S(2)}, u32[]{:S(2)}) collective-permute-start(bf16[12,64,1024]{2,1,0:T(8,128)(2,1)} %bitcast.155), channel_id=1, source_target_pairs={{0,2},{2,0},{1,3},{3,1},{4,6},{6,4},{5,7},{7,5},{8,10},{10,8},{9,1... | collective-permute-start | bytes 4718600 | tf_op jit(solution)/shard_map/ppermute | solution.py:787
  131.5 71.7 %collective-permute-start.11 = (bf16[8,2,32,1024]{3,2,1,0:T(8,128)(2,1)}, bf16[8,2,32,1024]{3,2,1,0:T(8,128)(2,1)S(1)}, u32[]{:S(2)}, u32[]{:S(2)}) collective-permute-start(bf16[8,2,32,1024]{3,2,1,0:T(8,128)(2,1)} %all-to-all-done.2.mine), channel_id=1, source_target_pairs={{0,1},{1,0},{2,3},{3,2},{4,5},{5,4},{6,7},{7,6},{8,9},{9,8},{10,11... | collective-permute-start | bytes 3145736 | tf_op jit(solution)/shard_map/ppermute | solution.py:787
  173.7 31.6 %collective-permute-start.14 = (bf16[256,768]{1,0:T(8,128)(2,1)}, bf16[256,768]{1,0:T(8,128)(2,1)S(1)}, u32[]{:S(2)}, u32[]{:S(2)}) collective-permute-start(bf16[256,768]{1,0:T(8,128)(2,1)} %get-tuple-element.276), channel_id=1, source_target_pairs={{0,3},{1,2},{2,1},{3,0},{4,7},{5,6},{6,5},{7,4},{8,11},{9,10},{10,... | collective-permute-start | bytes 1179656 | tf_op jit(solution)/shard_map/ppermute | solution.py:787
  175.3 30.0 %collective-permute-start.13 = (bf16[256,768]{1,0:T(8,128)(2,1)S(1)}, bf16[256,768]{1,0:T(8,128)(2,1)S(1)}, u32[]{:S(2)}, u32[]{:S(2)}) collective-permute-start(bf16[256,768]{1,0:T(8,128)(2,1)S(1)} %get-tuple-element.277), channel_id=1, source_target_pairs={{0,2},{1,3},{2,0},{3,1},{4,6},{5,7},{6,4},{7,5},{8,10},{9,11},{10,... | collective-permute-start | bytes 1179656 | tf_op jit(solution)/shard_map/ppermute | solution.py:787
  217.3 29.7 %collective-permute-start.15 = (bf16[384,1024]{1,0:T(8,128)(2,1)}, bf16[384,1024]{1,0:T(8,128)(2,1)S(1)}, u32[]{:S(2)}, u32[]{:S(2)}) collective-permute-start(bf16[384,1024]{1,0:T(8,128)(2,1)} %get-tuple-element.159.hidden.refs_0_), channel_id=1, source_target_pairs={{0,2},{2,0},{1,3},{3,1},{4,6},{6,4},{5,7},{7,5},{8,10},{10,8},{9,1... | collective-permute-start | bytes 2359304 | tf_op jit(solution)/shard_map/ppermute | solution.py:787
  232.7 30.0 %collective-permute-start.16 = (bf16[384,1024]{1,0:T(8,128)(2,1)S(1)}, bf16[384,1024]{1,0:T(8,128)(2,1)S(1)}, u32[]{:S(2)}, u32[]{:S(2)}) collective-permute-start(bf16[384,1024]{1,0:T(8,128)(2,1)S(1)} %copy-done.51), channel_id=1, source_target_pairs={{0,2},{2,0},{1,3},{3,1},{4,6},{6,4},{5,7},{7,5},{8,10},{10,8},{9,1... | collective-permute-start | bytes 2359304 | tf_op jit(solution)/shard_map/ppermute | solution.py:787
  261.2 37.5 %collective-permute-start.17 = (bf16[384,1024]{1,0:T(8,128)(2,1)}, bf16[384,1024]{1,0:T(8,128)(2,1)S(1)}, u32[]{:S(2)}, u32[]{:S(2)}) collective-permute-start(bf16[384,1024]{1,0:T(8,128)(2,1)} %get-tuple-element.179), channel_id=1, source_target_pairs={{0,2},{2,0},{1,3},{3,1},{4,6},{6,4},{5,7},{7,5},{8,10},{10,8},{9,1... | collective-permute-start | bytes 2359304 | tf_op jit(solution)/shard_map/ppermute | solution.py:787
  277.2 21.6 %collective-permute-start.18 = (bf16[384,1024]{1,0:T(8,128)(2,1)}, bf16[384,1024]{1,0:T(8,128)(2,1)S(1)}, u32[]{:S(2)}, u32[]{:S(2)}) collective-permute-start(bf16[384,1024]{1,0:T(8,128)(2,1)} %get-tuple-element.180), channel_id=1, source_target_pairs={{0,2},{2,0},{1,3},{3,1},{4,6},{6,4},{5,7},{7,5},{8,10},{10,8},{9,1... | collective-permute-start | bytes 2359304 | tf_op jit(solution)/shard_map/ppermute | solution.py:787
  317.4 7.5 %collective-permute-start.19 = (bf16[256,768]{1,0:T(8,128)(2,1)}, bf16[256,768]{1,0:T(8,128)(2,1)}, u32[]{:S(2)}, u32[]{:S(2)}) collective-permute-start(bf16[256,768]{1,0:T(8,128)(2,1)} %get-tuple-element.186), channel_id=1, source_target_pairs={{0,1},{1,0},{2,3},{3,2},{4,5},{5,4},{6,7},{7,6},{8,9},{9,8},{10,11... | collective-permute-start | bytes 1179656 | tf_op jit(solution)/shard_map/ppermute | solution.py:787
  318.5 108.0 %all-to-all-start.3 = ((bf16[32,32,1024]{2,1,0:T(8,128)(2,1)}), bf16[32,32,1024]{2,1,0:T(8,128)(2,1)}, u32[]{:S(2)}, u32[]{:S(2)}) async-start(bf16[32,32,1024]{2,1,0:T(8,128)(2,1)} %bitcast.175), calls=%async_computation.3 | async-start | bytes 4194304 | tf_op jit(solution)/shard_map/all_to_all | solution.py:995
  323.0 50.4 %collective-permute-start.20 = (bf16[256,768]{1,0:T(8,128)(2,1)S(1)}, bf16[256,768]{1,0:T(8,128)(2,1)}, u32[]{:S(2)}, u32[]{:S(2)}) collective-permute-start(bf16[256,768]{1,0:T(8,128)(2,1)S(1)} %copy-done.55), channel_id=1, source_target_pairs={{0,2},{1,3},{2,0},{3,1},{4,6},{5,7},{6,4},{7,5},{8,10},{9,11},{10,... | collective-permute-start | bytes 1179656 | tf_op jit(solution)/shard_map/ppermute | solution.py:787
  324.9 48.5 %collective-permute-start.21 = (bf16[256,768]{1,0:T(8,128)(2,1)S(1)}, bf16[256,768]{1,0:T(8,128)(2,1)}, u32[]{:S(2)}, u32[]{:S(2)}) collective-permute-start(bf16[256,768]{1,0:T(8,128)(2,1)S(1)} %copy-done.54), channel_id=1, source_target_pairs={{0,3},{1,2},{2,1},{3,0},{4,7},{5,6},{6,5},{7,4},{8,11},{9,10},{10,... | collective-permute-start | bytes 1179656 | tf_op jit(solution)/shard_map/ppermute | solution.py:787
  373.4 53.1 %collective-permute-start.22 = (bf16[384,1024]{1,0:T(8,128)(2,1)}, bf16[384,1024]{1,0:T(8,128)(2,1)S(1)}, u32[]{:S(2)}, u32[]{:S(2)}) collective-permute-start(bf16[384,1024]{1,0:T(8,128)(2,1)} %get-tuple-element.200), channel_id=1, source_target_pairs={{0,2},{2,0},{1,3},{3,1},{4,6},{6,4},{5,7},{7,5},{8,10},{10,8},{9,1... | collective-permute-start | bytes 2359304 | tf_op jit(solution)/shard_map/ppermute | solution.py:787
  374.9 51.5 %collective-permute-start.23 = (bf16[384,1024]{1,0:T(8,128)(2,1)}, bf16[384,1024]{1,0:T(8,128)(2,1)}, u32[]{:S(2)}, u32[]{:S(2)}) collective-permute-start(bf16[384,1024]{1,0:T(8,128)(2,1)} %get-tuple-element.201), channel_id=1, source_target_pairs={{0,2},{2,0},{1,3},{3,1},{4,6},{6,4},{5,7},{7,5},{8,10},{10,8},{9,1... | collective-permute-start | bytes 2359304 | tf_op jit(solution)/shard_map/ppermute | solution.py:787
  448.5 19.8 %collective-permute-start.25 = (bf16[384,1024]{1,0:T(8,128)(2,1)}, bf16[384,1024]{1,0:T(8,128)(2,1)S(1)}, u32[]{:S(2)}, u32[]{:S(2)}) collective-permute-start(bf16[384,1024]{1,0:T(8,128)(2,1)} %get-tuple-element.212), channel_id=1, source_target_pairs={{0,2},{2,0},{1,3},{3,1},{4,6},{6,4},{5,7},{7,5},{8,10},{10,8},{9,1... | collective-permute-start | bytes 2359304 | tf_op jit(solution)/shard_map/ppermute | solution.py:787
  469.9 60.0 %all-to-all-start.4 = ((bf16[32,38,768]{2,1,0:T(8,128)(2,1)}), bf16[32,38,768]{2,1,0:T(8,128)(2,1)S(1)}, u32[]{:S(2)}, u32[]{:S(2)}) async-start(bf16[32,38,768]{2,1,0:T(8,128)(2,1)} %pad_maximum_fusion), calls=%async_computation.5 | async-start | bytes 3932160 | tf_op jit(solution)/shard_map/all_to_all | solution.py:1048
  475.3 31.5 %collective-permute-start.26 = (bf16[768,1024]{1,0:T(8,128)(2,1)}, bf16[768,1024]{1,0:T(8,128)(2,1)}, u32[]{:S(2)}, u32[]{:S(2)}) collective-permute-start(bf16[768,1024]{1,0:T(8,128)(2,1)} %get-tuple-element.224), channel_id=1, source_target_pairs={{0,1},{1,0},{2,3},{3,2},{4,5},{5,4},{6,7},{7,6},{8,9},{9,8},{10,11... | collective-permute-start | bytes 4718600 | tf_op jit(solution)/shard_map/ppermute | solution.py:787
  479.0 22.2 %collective-permute-start.28 = (bf16[2,32,2048]{2,1,0:T(8,128)(2,1)S(1)}, bf16[2,32,2048]{2,1,0:T(8,128)(2,1)S(1)}, u32[]{:S(2)}, u32[]{:S(2)}) collective-permute-start(bf16[2,32,2048]{2,1,0:T(8,128)(2,1)S(1)} %bitcast.191), channel_id=1, source_target_pairs={{0,2},{2,0},{1,3},{3,1},{4,6},{6,4},{5,7},{7,5},{8,10},{10,8},{9,1... | collective-permute-start | bytes 786440 | tf_op jit(solution)/shard_map/ppermute | solution.py:787
  488.4 33.4 %collective-permute-start.27 = (bf16[384,1024]{1,0:T(8,128)(2,1)}, bf16[384,1024]{1,0:T(8,128)(2,1)}, u32[]{:S(2)}, u32[]{:S(2)}) collective-permute-start(bf16[384,1024]{1,0:T(8,128)(2,1)} %get-tuple-element.226), channel_id=1, source_target_pairs={{0,2},{2,0},{1,3},{3,1},{4,6},{6,4},{5,7},{7,5},{8,10},{10,8},{9,1... | collective-permute-start | bytes 2359304 | tf_op jit(solution)/shard_map/ppermute | solution.py:787
  (61 other events, 470.2 us)
Sparse Core Ops, SparseCore 0:
  27.3 49.6 all-gather.2
  79.8 94.5 all-gather.4
  298.9 139.7 reduce-scatter.1

commit v10 on v9

--- a/solution.py
+++ b/solution.py
@@ -663,9 +663,9 @@
 
 def first_back_kernel(last, one, two, three, four, mod, dq, dk, dv, weight, *rest):
     if last:
-        raw_in, mod_in, grad1, grad2, raw, mod_grad, total, held = rest
+        raw_in, mod_in, grads, raw, mod_grad, total, held = rest
     else:
-        grad1, grad2, total, mod_grad, held = rest
+        grads, total, mod_grad, held = rest
     step = pl.program_id(0)
     chunk = mod.shape[0]
 
@@ -679,16 +679,7 @@
     pieces = jnp.concatenate([dq[...], dk[...], dv[...]], axis=0)
     total[...] += dot(pieces, hidden)
     back = dot(pieces, weight[...], TN)
-    low = back.astype(bf16)
-
-    @pl.when(step < 2)
-    def _():
-        grad1[...] = low
-
-    @pl.when(step >= 2)
-    def _():
-        grad2[...] = low
-
+    grads[...] = back.astype(bf16).reshape(grads.shape)
     back = back.reshape(shape)
     place = pl.ds(lax.rem(step, 2) * chunk, chunk)
     mod_grad[place, 0:1] += jnp.sum(back, axis=1, keepdims=True)
@@ -710,26 +701,23 @@
     moved = pl.BlockSpec((rows, block), lambda i: (0, i + offset * 4))
     in_specs = specs + [pl.BlockSpec((rows, block), lambda i: (0, i)), moved, moved, whole()]
     operands = [piece for piece, _ in pieces] + [mod, dq, dk, dv, weight]
-    grads = jax.ShapeDtypeStruct((count // 2, width), bf16)
-    grads_specs = [
-        pl.BlockSpec((block, width), lambda i: (jnp.minimum(i, 1), 0)),
-        pl.BlockSpec((block, width), lambda i: (jnp.maximum(i - 2, 0), 0)),
-    ]
+    grads = jax.ShapeDtypeStruct((2, count // 2, width), bf16)
+    grads_spec = pl.BlockSpec((1, block, width), lambda i: (i // 2, lax.rem(i, 2), 0))
     held = VMEM((block, width), bf16)
     mods = jax.ShapeDtypeStruct((frames, 2, width), f32)
     if last:
         in_specs += [whole(), whole()]
         operands += list(sums)
-        out_shape = [grads, grads, jax.ShapeDtypeStruct((width, 3 * rows), bf16), mods]
+        out_shape = [grads, jax.ShapeDtypeStruct((width, 3 * rows), bf16), mods]
         scratch = [VMEM((3 * rows, width), f32), held]
     else:
-        out_shape = [grads, grads, jax.ShapeDtypeStruct((3 * rows, width), f32), mods]
+        out_shape = [grads, jax.ShapeDtypeStruct((3 * rows, width), f32), mods]
         scratch = [held]
     return pl.pallas_call(
         functools.partial(first_back_kernel, last),
         grid=(4,),
         in_specs=in_specs,
-        out_specs=grads_specs + [whole(), whole()],
+        out_specs=[grads_spec, whole(), whole()],
         out_shape=out_shape,
         scratch_shapes=scratch,
         compiler_params=params(),
@@ -741,7 +729,7 @@
     normed, inverse = layer_norm(tokens[...].astype(f32))
     first = pl.program_id(0) < pl.num_programs(0) // 2
     grad = jnp.where(first, far1[...].astype(f32), far2[...].astype(f32))
-    grad = grad + one[...].astype(f32) + two[...].astype(f32)
+    grad = grad + one[0].astype(f32) + two[...].astype(f32)
     grad = grad.reshape(tokens.shape) * (1.0 + mod[:, 1:2, :])
     out[...] = middle_grad[...] + norm_back(normed, inverse, grad)
 
@@ -759,7 +747,7 @@
         input_kernel,
         grid=(frames // chunk,),
         in_specs=[cube, pl.BlockSpec((chunk, 6, width), lambda i: (i, 0, 0)), cube]
-        + [flat, flat, one, two],
+        + [pl.BlockSpec((1, block, width), lambda i: (0, i, 0)), flat, one, two],
         out_specs=cube,
         out_shape=jax.ShapeDtypeStruct(tokens.shape, f32),
         compiler_params=params(),
@@ -878,7 +866,9 @@
     attend_mine = relative(trade(relative(attend_mine, row), ROW, rows), row)
 
     cond_act = jax.nn.silu(condition[0].astype(f32)).astype(bf16)
-    cond_act, tok0, attend_mine = lax.optimization_barrier((cond_act, tok0, attend_mine))
+    cond_act, tok0, attend_mine, tok1 = lax.optimization_barrier(
+        (cond_act, tok0, attend_mine, tok1)
+    )
     attend_full = lax.all_gather(
         attend_mine.reshape(rows * shard, 3 * features), "clip", axis=0, tiled=True
     )
@@ -932,14 +922,13 @@
 
     cos_near, sin_near, bias_near = places_of((tok0, tok1))
     cos_far, sin_far, bias_far = places_of((tok2_two, tok3_two))
+    near = ((tok0, 0), (tok0, 1), (tok1, 0), (tok1, 1))
+    qkv_near = project_qkv(near, mod, attend_turned, cos_near, sin_near)
+    across = ((tok2_one, 0), (tok2_two, 0), (tok3_one, 0), (tok3_two, 0))
+    project_mine, qkv_near = lax.optimization_barrier((project_mine, qkv_near))
     project_full = lax.all_to_all(
         jnp.broadcast_to(project_mine[None], (clips, 2, shard, width)), "clip", 0, 0, tiled=True
     )
-
-    near = ((tok0, 0), (tok0, 1), (tok1, 0), (tok1, 1))
-    qkv_near = project_qkv(near, mod, attend_turned, cos_near, sin_near)
-    qkv_near, project_full = lax.optimization_barrier((qkv_near, project_full))
-    across = ((tok2_one, 0), (tok2_two, 0), (tok3_one, 0), (tok3_two, 0))
     qkv_far = project_qkv(across, mod, attend_turned, cos_far, sin_far)
     cosine = jnp.concatenate([cos_near, cos_far], axis=1)
     sine = jnp.concatenate([sin_near, sin_far], axis=1)
@@ -948,7 +937,9 @@
     cot_far, mod = lax.optimization_barrier((upstream, mod))
     cot_far = swap(cot_far, "x", 2, 1)
     out_far, lse_far = attend(qkv_far, qkv_near, qkv_far, bias)
-    out_far, qkv_near, cot_far = lax.optimization_barrier((out_far, qkv_near, cot_far))
+    out_far, qkv_near, cot_far, project_full = lax.optimization_barrier(
+        (out_far, qkv_near, cot_far, project_full)
+    )
     project_near = swap(project_full, "core", 2, 1)
     part2 = swap(out_far[0], ROW, rows, 2)
     part3 = swap(out_far[1], ROW, rows, 3)
@@ -1011,16 +1002,16 @@
     )
     dq_far, project_raw, out3, out4 = lax.optimization_barrier((dq_far, project_raw, out3, out4))
     project_sum = total_over(project_raw.reshape(devices, 1, shard, width))[0].T
-    back1, back2, raw, mod_early = first_back(across, mod, dq_far, dk, dv, attend_turned, 1)
-    back2 = swap(back2, ROW, rows, 1)
+    back, raw, mod_early = first_back(across, mod, dq_far, dk, dv, attend_turned, 1)
+    other = swap(back[1], ROW, rows, 1)
     far_one, far_two = [
-        (back1[at : at + half].astype(f32) + back2[at : at + half].astype(f32)).astype(bf16)
+        (back[0, at : at + half].astype(f32) + other[at : at + half].astype(f32)).astype(bf16)
         for at in (0, half)
     ]
     far_one, far_two, dq_near = lax.optimization_barrier((far_one, far_two, dq_near))
     far_one = swap(far_one, "x", 2, 1)
     extra = -(-2 * frames * part // (3 * features))
-    back1, back2, attend_raw, mod_early = first_back(
+    back, attend_raw, mod_early = first_back(
         near, mod, dq_near, dk, dv, attend_turned, 0, (raw, mod_early)
     )
     attend_raw, far_one, feed_sum, far_two = lax.optimization_barrier(
@@ -1030,7 +1021,7 @@
     feed_sum = relative(trade(relative(feed_sum, far), "x", 2), far).astype(f32)
     widen_sum, narrow_sum = feed_sum.transpose(1, 2, 0, 3).reshape(2, shard, units)
     narrow_sum = narrow_sum.T
-    back_near = (back1, swap(back2, ROW, rows, 1))
+    back_near = (back, swap(back[1], ROW, rows, 1))
 
     mod_grad = jnp.concatenate([mod_early, mod_late, mod_gate], axis=1)
     mod_grad = mod_grad.reshape(frames, devices, part).transpose(1, 0, 2).reshape(devices, -1)
@@ -1047,10 +1038,10 @@
     )
     attend_raw = lax.all_to_all(attend_raw, both, 0, 0, tiled=True)
     block_out = block_output((out1, out2, out3, out4), own, att_out, mod)
+    attend_raw, far_two, block_out, project_sum = lax.optimization_barrier(
+        (attend_raw, far_two, block_out, project_sum)
+    )
     input_gradient = input_back(own, mod, middle_grad, back_near + (far_one, far_two))
-    attend_raw, input_gradient, block_out, project_sum = lax.optimization_barrier(
-        (attend_raw, input_gradient, block_out, project_sum)
-    )
     small = attend_raw[:, shard : shard + extra].reshape(devices, -1)[:, : 2 * frames * part]
     small = small.astype(f32).reshape(clips, rows, 2, frames, part)
     mod_grad = jnp.sum(small, axis=(1, 2)).reshape(clips * frames, part)

time: 586 us -> 571 us (0.974)
  waiting for transfers between devices: 93.3 us -> 63.1 us
  local copies, waits for them, and re-layouts: 29.6 us -> 48.1 us
  blocking collectives: 12.6 us -> 0 us
  other arithmetic: 42.3 us -> 49.5 us
    all_to_all x1, waiting for transfers between devices: 28 us -> 3.87 us  [local(): lax.all_to_all(jnp.broadcast_to(project_mine[None], (clips, 2, shard, wid...]
    all_to_all x1 -> x0, blocking collectives: 12.6 us -> none  [local(): lax.all_to_all(jnp.broadcast_to(squares, (devices, 8, 128)), both, 0, 0,...]
  transfers between devices with their start and end apart: 37 -> 38, of which waited for: 12 -> 11; matrix products, arithmetic and copies ran while one was open for 8% -> 14% of each run, Pallas kernels for 56% -> 57%
where the time goes in v10:
time: 571 us; the launch traced here: 563 us
  Pallas kernels  322 us (56%)
  waiting for transfers between devices  63.1 us (11%)
  starting transfers between devices  54.9 us (10%)
  other arithmetic  49.5 us (9%)
  local copies, waits for them, and re-layouts  48.1 us (8%)
  between operations  21.7 us (4%)
    pallas_call x2, Pallas kernels, attend_back(): pl.pallas_call(functools.partial(attend_back_kernel, heads, last), grid=(...  99.4 us
    pallas_call x2, Pallas kernels, attend(): pl.pallas_call(functools.partial(attend_kernel, heads), grid=(count // bl...  54.9 us
    pallas_call x4, Pallas kernels, feed_forward(): pl.pallas_call(feed_kernel, grid=(units // block,), in_specs=[spec, flat,...  54.4 us
    ppermute x29, waiting for transfers between devices, swap(): lax.ppermute(value, axis, [(place, place ^ step) for place in range(size)])  36.5 us
    pallas_call x2, Pallas kernels, first_back(): pl.pallas_call(functools.partial(first_back_kernel, last), grid=(4,), in_...  27.8 us
    ppermute x29, starting transfers between devices, swap(): lax.ppermute(value, axis, [(place, place ^ step) for place in range(size)])  26.2 us
    pallas_call x1, Pallas kernels, feed_weights(): pl.pallas_call(functools.partial(feed_weight_kernel, len(hidden)), grid=(...  21 us
    pallas_call x2, Pallas kernels, project_qkv(): pl.pallas_call(qkv_kernel, grid=(4,), in_specs=specs + [whole(), angle, a...  18.5 us
  transfers between devices with their start and end apart: 38, of which 11 were waited for; matrix products, arithmetic and copies ran while one was open for 14% of the time, Pallas kernels for 57%

profile of v10, /device:TPU:0, one launch (start us, length us, event | category | flops | bytes accessed | tf_op | source)
XLA Modules:
  0.0 562.8 jit_solution(3778630625552645007)
XLA Ops:
  19.9 2.6 collective-permute-start.2
  28.4 5.8 %all-to-all-start = ((bf16[8,12,1024]{2,1,0:T(8,128)(2,1)}), bf16[8,12,1024]{2,1,0:T(8,128)(2,1)S(1)}, u32[]{:S(2)}, u32[]{:S(2)}) async-start(bf16[8,12,1024]{2,1,0:T(8,128)(2,1)} %broadcast_in_dim.34), calls=%async_computation | async-start | bytes 524288 | tf_op jit(solution)/shard_map/all_to_all | solution.py:875
  37.0 5.6 %all-to-all-done = bf16[8,12,1024]{2,1,0:T(8,128)(2,1)S(1)} async-done(((bf16[8,12,1024]{2,1,0:T(8,128)(2,1)}), bf16[8,12,1024]{2,1,0:T(8,128)(2,1)S(1)}, u32[]{:S(2)}, u32[]{:S(2)}) %all-to-all-start) | async-done | bytes 196640 | tf_op jit(solution)/shard_map/all_to_all | solution.py:875
  60.4 3.6 all-to-all-start.1
  70.3 3.0 broadcast_select_fusion.2
  73.2 16.8 %all-to-all-done.1 = f32[32,12,192]{2,1,0:T(8,128)} async-done(((f32[32,12,192]{2,1,0:T(8,128)}), f32[32,12,192]{2,1,0:T(8,128)}, u32[]{:S(2)}, u32[]{:S(2)}) %all-to-all-start.1) | async-done | bytes 294944 | tf_op jit(solution)/shard_map/all_to_all | solution.py:891
  98.2 2.9 collective-permute-done.9
  104.8 9.3 %shard_map.488.k1.v1.q_ref = bf16[768,1536]{1,0:T(8,128)(2,1)} custom-call(bf16[784,1024]{1,0:T(8,128)(2,1)} %copy-done.1, bf16[784,1024]{1,0:T(8,128)(2,1)} %copy-done.1, bf16[784,1024]{1,0:T(8,128)(2,1)} %copy-done.4, bf16[784,1024]{1,0:T(8,128)(2,1)} %copy-done.4, f32[12,6,1024]{2,1,0:T(8,128)} %reshape.442.mod, bf16[768,1024]{1,0:T(8,128)(2,1)} %bitcast.191, ...), custom_call_target="tpu_custom_call" | custom-call | flops 2415919104 | bytes 6291456 | tf_op jit(solution)/shard_map/pallas_call | solution.py:131
  115.2 4.8 all-to-all-start.2
  122.1 9.2 %shard_map.487.q_ref.k2.v2 = bf16[768,1536]{1,0:T(8,128)(2,1)} custom-call(bf16[384,1024]{1,0:T(8,128)(2,1)} %collective-permute-done.4.one, bf16[400,1024]{1,0:T(8,128)(2,1)} %collective-permute-done.6.two, bf16[384,1024]{1,0:T(8,128)(2,1)} %collective-permute-done.7.three, bf16[400,1024]{1,0:T(8,128)(2,1)} %copy-done.56, f32[12,6,1024]{2,1,0:T(8,128)} %reshape.442.mod, ...), custom_call_target="tpu_custom_call" | custom-call | flops 2415919104 | bytes 6291456 | tf_op jit(solution)/shard_map/pallas_call | solution.py:131
  131.3 27.5 %shard_map.489 = (bf16[2,256,768]{2,1,0:T(8,128)(2,1)}, f32[4,1536]{1,0:T(4,128)}) custom-call(bf16[768,1536]{1,0:T(8,128)(2,1)} %shard_map.487.q_ref.k2.v2, bf16[768,1536]{1,0:T(8,128)(2,1)} %shard_map.488.k1.v1.q_ref, bf16[768,1536]{1,0:T(8,128)(2,1)} %shard_map.487.q_ref.k2.v2, bf16[768,1536]{1,0:T(8,128)(2,1)} %shard_map.488.k1.v1.q_ref, ...), custom_call_target="tpu_custom_call" | custom-call | flops 19327352832 | bytes 3145728 | tf_op jit(solution)/shard_map/pallas_call | solution.py:186
  158.8 3.9 all-to-all-done.2.mine
  166.8 27.4 %shard_map.490 = (bf16[2,256,768]{2,1,0:T(8,128)(2,1)}, f32[4,1536]{1,0:T(4,128)}) custom-call(bf16[768,1536]{1,0:T(8,128)(2,1)} %shard_map.488.k1.v1.q_ref, bf16[768,1536]{1,0:T(8,128)(2,1)} %shard_map.488.k1.v1.q_ref, bf16[768,1536]{1,0:T(8,128)(2,1)} %shard_map.487.q_ref.k2.v2, bf16[768,1536]{1,0:T(8,128)(2,1)} %shard_map.488.k1.v1.q_ref, ...), custom_call_target="tpu_custom_call" | custom-call | flops 19327352832 | bytes 3145728 | tf_op jit(solution)/shard_map/pallas_call | solution.py:186
  197.9 10.2 %shard_map.491 = (f32[12,64,1024]{2,1,0:T(8,128)}, bf16[384,1024]{1,0:T(8,128)(2,1)}, bf16[384,1024]{1,0:T(8,128)(2,1)}, bf16[768,1024]{1,0:T(8,128)(2,1)}, bf16...) custom-call(s32[5]{0:T(128)} %pad_add_fusion.order, bf16[2,256,768]{2,1,0:T(8,128)(2,1)} %get-tuple-element.157.a0.out_ref, ...), custom_call_target="tpu_custom_call" | custom-call | flops 1610612736 | bytes 11010048 | tf_op jit(solution)/shard_map/pallas_call | solution.py:401
  209.8 13.8 %shard_map.492 = (f32[384,1024]{1,0:T(8,128)}, f32[384,1024]{1,0:T(8,128)}, bf16[384,2048]{1,0:T(8,128)(2,1)}, bf16[384,2048]{1,0:T(8,128)(2,1)}, f32[6,1,1024]{2,1,0:T(1,128)}) custom-call(bf16[16,2,2,32,2048]{4,3,2,1,0:T(8,128)(2,1)} %bitcast.209, bf16[384,1024]{1,0:T(8,128)(2,1)} %get-tuple-element.161.hidden.refs_0_, ...), custom_call_target="tpu_custom_call" | custom-call | flops 6442450944 | bytes 11534336 | tf_op jit(solution)/shard_map/pallas_call | solution.py:498
  224.0 13.7 %shard_map.493 = (f32[384,1024]{1,0:T(8,128)}, f32[384,1024]{1,0:T(8,128)}, bf16[384,2048]{1,0:T(8,128)(2,1)}, bf16[384,2048]{1,0:T(8,128)(2,1)}, f32[6,1,1024]{2,1,0:T(1,128)}) custom-call(bf16[16,2,2,32,2048]{4,3,2,1,0:T(8,128)(2,1)} %bitcast.210, bf16[384,1024]{1,0:T(8,128)(2,1)} %get-tuple-element.169.hidden.refs_1_, ...), custom_call_target="tpu_custom_call" | custom-call | flops 6442450944 | bytes 11534336 | tf_op jit(solution)/shard_map/pallas_call | solution.py:498
  238.6 13.3 %shard_map.494 = (bf16[384,1024]{1,0:T(8,128)(2,1)}, bf16[384,1024]{1,0:T(8,128)(2,1)}, bf16[384,2048]{1,0:T(8,128)(2,1)}, bf16[384,2048]{1,0:T(8,128)(2,1)}, f32[6,1,1024]{2,1,0:T(1,128)}) custom-call(bf16[16,2,2,32,2048]{4,3,2,1,0:T(8,128)(2,1)} %bitcast.211, bf16[384,1024]{1,0:T(8,128)(2,1)} %copy-done.58, ...), custom_call_target="tpu_custom_call" | custom-call | flops 6442450944 | bytes 11534336 | tf_op jit(solution)/shard_map/pallas_call | solution.py:498
  254.4 13.6 %shard_map.495 = (bf16[384,1024]{1,0:T(8,128)(2,1)}, bf16[384,1024]{1,0:T(8,128)(2,1)}, bf16[384,2048]{1,0:T(8,128)(2,1)}, bf16[384,2048]{1,0:T(8,128)(2,1)}, f32[6,1,1024]{2,1,0:T(1,128)}) custom-call(bf16[16,2,2,32,2048]{4,3,2,1,0:T(8,128)(2,1)} %bitcast.212, bf16[384,1024]{1,0:T(8,128)(2,1)} %copy-done.59, ...), custom_call_target="tpu_custom_call" | custom-call | flops 6442450944 | bytes 11534336 | tf_op jit(solution)/shard_map/pallas_call | solution.py:498
  268.5 21.0 %shard_map.496 = bf16[16,2,2,32,2048]{4,3,2,1,0:T(8,128)(2,1)} custom-call(bf16[384,1024]{1,0:T(8,128)(2,1)} %get-tuple-element.161.hidden.refs_0_, bf16[384,1024]{1,0:T(8,128)(2,1)} %get-tuple-element.169.hidden.refs_1_, bf16[384,1024]{1,0:T(8,128)(2,1)} %copy-done.58, bf16[384,1024]{1,0:T(8,128)(2,1)} %copy-done.59, ...), custom_call_target="tpu_custom_call" | custom-call | flops 12884901888 | bytes 20971520 | tf_op jit(solution)/shard_map/pallas_call | solution.py:549
  290.6 17.6 %shard_map.497 = (f32[12,64,1024]{2,1,0:T(8,128)}, f32[12,3,1024]{2,1,0:T(4,128)}, bf16[256,768]{1,0:T(8,128)(2,1)}, bf16[256,768]{1,0:T(8,128)(2,1)}, bf16[256,...) custom-call(s32[5]{0:T(128)} %pad_add_fusion.order, f32[384,1024]{1,0:T(8,128)} %get-tuple-element.163.into1, ...), custom_call_target="tpu_custom_call" | custom-call | flops 3221225472 | bytes 18874368 | tf_op jit(solution)/shard_map/pallas_call | solution.py:612
  309.3 3.9 all-to-all-start.3
  315.2 48.4 %shard_map.498 = (bf16[256,1536]{1,0:T(8,128)(2,1)}, f32[256,3072]{1,0:T(8,128)}, f32[256,3072]{1,0:T(8,128)}) custom-call(bf16[768,1536]{1,0:T(8,128)(2,1)} %shard_map.488.k1.v1.q_ref, bf16[768,1536]{1,0:T(8,128)(2,1)} %shard_map.488.k1.v1.q_ref, bf16[768,1536]{1,0:T(8,128)(2,1)} %shard_map.487.q_ref.k2.v2, bf16[768,1536]{1,0:T(8,128)(2,1)} %shard_map.488.k1.v1.q_ref, ...), custom_call_target="tpu_custom_call" | custom-call | flops 41070624768 | bytes 6291456 | tf_op jit(solution)/shard_map/pallas_call | solution.py:332
  365.7 51.0 %shard_map.499 = (bf16[256,1536]{1,0:T(8,128)(2,1)}, bf16[256,3072]{1,0:T(8,128)(2,1)}, bf16[256,3072]{1,0:T(8,128)(2,1)}) custom-call(bf16[768,1536]{1,0:T(8,128)(2,1)} %shard_map.487.q_ref.k2.v2, bf16[768,1536]{1,0:T(8,128)(2,1)} %shard_map.488.k1.v1.q_ref, bf16[768,1536]{1,0:T(8,128)(2,1)} %shard_map.487.q_ref.k2.v2, ...), custom_call_target="tpu_custom_call" | custom-call | flops 41070624768 | bytes 6291456 | tf_op jit(solution)/shard_map/pallas_call | solution.py:332
  416.8 13.2 %shard_map.500 = (bf16[2,768,1024]{2,1,0:T(8,128)(2,1)}, f32[768,1024]{1,0:T(8,128)}, f32[12,2,1024]{2,1,0:T(2,128)}) custom-call(bf16[384,1024]{1,0:T(8,128)(2,1)} %collective-permute-done.4.one, bf16[400,1024]{1,0:T(8,128)(2,1)} %collective-permute-done.6.two, bf16[384,1024]{1,0:T(8,128)(2,1)} %collective-permute-done.7.three, ...), custom_call_target="tpu_custom_call" | custom-call | flops 4831838208 | bytes 9437184 | tf_op jit(solution)/shard_map/pallas_call | solution.py:716
  431.9 3.3 collective-permute-done.24
  438.5 14.6 %shard_map.501 = (bf16[2,768,1024]{2,1,0:T(8,128)(2,1)}, bf16[1024,768]{1,0:T(8,128)(2,1)}, f32[12,2,1024]{2,1,0:T(2,128)}) custom-call(bf16[784,1024]{1,0:T(8,128)(2,1)} %copy-done.1, bf16[784,1024]{1,0:T(8,128)(2,1)} %copy-done.1, bf16[784,1024]{1,0:T(8,128)(2,1)} %copy-done.4, bf16[784,1024]{1,0:T(8,128)(2,1)} %copy-done.4, f32[12,6,1024]{2,1,0:T(8,128)} %reshape.442.mod, ...), custom_call_target="tpu_custom_call" | custom-call | flops 4831838208 | bytes 9437184 | tf_op jit(solution)/shard_map/pallas_call | solution.py:716
  458.4 5.7 %all-to-all-start.4 = ((bf16[32,38,768]{2,1,0:T(8,128)(2,1)}), bf16[32,38,768]{2,1,0:T(8,128)(2,1)S(1)}, u32[]{:S(2)}, u32[]{:S(2)}) async-start(bf16[32,38,768]{2,1,0:T(8,128)(2,1)} %pad_maximum_fusion), calls=%async_computation.5 | async-start | bytes 3932160 | tf_op jit(solution)/shard_map/all_to_all | solution.py:1039
  466.6 5.3 shard_map.502
  478.6 11.4 %collective-permute-done.28 = bf16[2,32,2048]{2,1,0:T(8,128)(2,1)S(1)} collective-permute-done((bf16[2,32,2048]{2,1,0:T(8,128)(2,1)S(1)}, bf16[2,32,2048]{2,1,0:T(8,128)(2,1)S(1)}, u32[]{:S(2)}, u32[]{:S(2)}) %collective-permute-start.28) | collective-permute-done | bytes 262176 | tf_op jit(solution)/shard_map/ppermute | solution.py:775
  495.7 15.3 %collective-permute-done.26.far2 = bf16[384,1024]{1,0:T(8,128)(2,1)} collective-permute-done((bf16[384,1024]{1,0:T(8,128)(2,1)S(1)}, bf16[384,1024]{1,0:T(8,128)(2,1)}, u32[]{:S(2)}, u32[]{:S(2)}) %collective-permute-start.26) | collective-permute-done | bytes 786464 | tf_op jit(solution)/shard_map/ppermute | solution.py:775
  527.6 4.6 all-to-all-start.5
  532.2 7.9 %shard_map.504 = f32[12,64,1024]{2,1,0:T(8,128)} custom-call(bf16[12,64,1024]{2,1,0:T(8,128)(2,1)} %bitcast.162, f32[12,6,1024]{2,1,0:T(8,128)} %reshape.442.mod, f32[12,64,1024]{2,1,0:T(8,128)} %get-tuple-element.230.middle_grad, bf16[2,768,1024]{2,1,0:T(8,128)(2,1)} %get-tuple-element.231.one, bf16[768,1024]{1,0:T(8,128)(2,1)} %collective-permute-done.27.two, ...), custom_call_target="tpu_custom_call" | custom-call | flops 15728640 | bytes 12582912 | tf_op jit(solution)/shard_map/pallas_call | solution.py:746
  (321 shorter events, 131.1 us)
Async XLA Ops:
  11.5 16.1 %collective-permute-start.3 = (bf16[784,1024]{1,0:T(8,128)(2,1)S(1)}, bf16[784,1024]{1,0:T(8,128)(2,1)S(1)}, u32[]{:S(2)}, u32[]{:S(2)}) collective-permute-start(bf16[784,1024]{1,0:T(8,128)(2,1)S(1)} %fusion.1.one.two), channel_id=1, source_target_pairs={{0,1},{1,0},{2,3},{3,2},{4,5},{5,4},{6,7},{7,6},{8,9},{9,8},{10,11... | collective-permute-start | bytes 4816904 | tf_op jit(solution)/shard_map/ppermute | solution.py:775
  23.8 21.8 %collective-permute-start.4 = (bf16[384,1024]{1,0:T(8,128)(2,1)}, bf16[384,1024]{1,0:T(8,128)(2,1)}, u32[]{:S(2)}, u32[]{:S(2)}) collective-permute-start(bf16[384,1024]{1,0:T(8,128)(2,1)} %bitcast.22), channel_id=1, source_target_pairs={{0,2},{2,0},{1,3},{3,1},{4,6},{6,4},{5,7},{7,5},{8,10},{10,8},{9,1... | collective-permute-start | bytes 2359304 | tf_op jit(solution)/shard_map/ppermute | solution.py:775
  28.4 14.3 %all-to-all-start = ((bf16[8,12,1024]{2,1,0:T(8,128)(2,1)}), bf16[8,12,1024]{2,1,0:T(8,128)(2,1)S(1)}, u32[]{:S(2)}, u32[]{:S(2)}) async-start(bf16[8,12,1024]{2,1,0:T(8,128)(2,1)} %broadcast_in_dim.34), calls=%async_computation | async-start | bytes 524288 | tf_op jit(solution)/shard_map/all_to_all | solution.py:875
  34.2 59.8 %all-gather.3.cloned.1.call-start = ((), (), s32[]{:S(2)}) async-start(), calls=%async_computation.7 | async-start | bytes 1769472 | tf_op jit(solution)/shard_map/all_gather | solution.py:872
  57.8 8.1 %collective-permute-start.5 = (bf16[2,32,2048]{2,1,0:T(8,128)(2,1)}, bf16[2,32,2048]{2,1,0:T(8,128)(2,1)}, u32[]{:S(2)}, u32[]{:S(2)}) collective-permute-start(bf16[2,32,2048]{2,1,0:T(8,128)(2,1)} %bitcast.155), channel_id=1, source_target_pairs={{0,2},{2,0},{1,3},{3,1},{4,6},{6,4},{5,7},{7,5},{8,10},{10,8},{9,1... | collective-permute-start | bytes 786440 | tf_op jit(solution)/shard_map/ppermute | solution.py:775
  60.4 29.6 %all-to-all-start.1 = ((f32[32,12,192]{2,1,0:T(8,128)}), f32[32,12,192]{2,1,0:T(8,128)}, u32[]{:S(2)}, u32[]{:S(2)}) async-start(f32[32,12,192]{2,1,0:T(8,128)} %bitcast.184), calls=%async_computation.1 | async-start | bytes 1048576 | tf_op jit(solution)/shard_map/all_to_all | solution.py:891
  63.9 145.8 %all-gather.5.cloned.1.call-start = ((), (), s32[]{:S(2)}) async-start(), calls=%async_computation.8 | async-start | bytes 8912896 | tf_op jit(solution)/shard_map/all_gather | solution.py:903
  64.2 29.9 %collective-permute-start.6 = (bf16[400,1024]{1,0:T(8,128)(2,1)}, bf16[400,1024]{1,0:T(8,128)(2,1)}, u32[]{:S(2)}, u32[]{:S(2)}) collective-permute-start(bf16[400,1024]{1,0:T(8,128)(2,1)} %slice.193), channel_id=1, source_target_pairs={{0,2},{2,0},{1,3},{3,1},{4,6},{6,4},{5,7},{7,5},{8,10},{10,8},{9,1... | collective-permute-start | bytes 2457608 | tf_op jit(solution)/shard_map/ppermute | solution.py:775
  96.1 7.1 %collective-permute-start.8 = (bf16[400,1024]{1,0:T(8,128)(2,1)}, bf16[400,1024]{1,0:T(8,128)(2,1)S(1)}, u32[]{:S(2)}, u32[]{:S(2)}) collective-permute-start(bf16[400,1024]{1,0:T(8,128)(2,1)} %collective-permute-done.6.two), channel_id=1, source_target_pairs={{0,1},{1,0},{2,3},{3,2},{4,5},{5,4},{6,7},{7,6},{8,9},{9,8},{10,11... | collective-permute-start | bytes 2457608 | tf_op jit(solution)/shard_map/ppermute | solution.py:775
  96.2 25.9 %collective-permute-start.7 = (bf16[384,1024]{1,0:T(8,128)(2,1)}, bf16[384,1024]{1,0:T(8,128)(2,1)}, u32[]{:S(2)}, u32[]{:S(2)}) collective-permute-start(bf16[384,1024]{1,0:T(8,128)(2,1)} %collective-permute-done.4.one), channel_id=1, source_target_pairs={{0,1},{1,0},{2,3},{3,2},{4,5},{5,4},{6,7},{7,6},{8,9},{9,8},{10,11... | collective-permute-start | bytes 2359304 | tf_op jit(solution)/shard_map/ppermute | solution.py:775
  101.9 56.9 %collective-permute-start.10 = (bf16[12,64,1024]{2,1,0:T(8,128)(2,1)}, bf16[12,64,1024]{2,1,0:T(8,128)(2,1)S(1)}, u32[]{:S(2)}, u32[]{:S(2)}) collective-permute-start(bf16[12,64,1024]{2,1,0:T(8,128)(2,1)} %bitcast.165), channel_id=1, source_target_pairs={{0,2},{2,0},{1,3},{3,1},{4,6},{6,4},{5,7},{7,5},{8,10},{10,8},{9,1... | collective-permute-start | bytes 4718600 | tf_op jit(solution)/shard_map/ppermute | solution.py:775
  115.2 47.5 %all-to-all-start.2 = ((bf16[8,2,32,1024]{3,2,1,0:T(8,128)(2,1)}), bf16[8,2,32,1024]{3,2,1,0:T(8,128)(2,1)S(1)}, u32[]{:S(2)}, u32[]{:S(2)}) async-start(bf16[8,2,32,1024]{3,2,1,0:T(8,128)(2,1)} %broadcast_in_dim.39), calls=%async_computation.2 | async-start | bytes 2097152 | tf_op jit(solution)/shard_map/all_to_all | solution.py:929
  120.0 336.8 %reduce-scatter.2.cloned.1.call-start = ((), (), s32[]{:S(2)}) async-start(), calls=%async_computation.9 | async-start | bytes 8912896 | tf_op jit(solution)/shard_map/reduce_scatter | solution.py:975
  165.0 31.3 %collective-permute-start.14 = (bf16[256,768]{1,0:T(8,128)(2,1)}, bf16[256,768]{1,0:T(8,128)(2,1)S(1)}, u32[]{:S(2)}, u32[]{:S(2)}) collective-permute-start(bf16[256,768]{1,0:T(8,128)(2,1)} %get-tuple-element.276), channel_id=1, source_target_pairs={{0,3},{1,2},{2,1},{3,0},{4,7},{5,6},{6,5},{7,4},{8,11},{9,10},{10,... | collective-permute-start | bytes 1179656 | tf_op jit(solution)/shard_map/ppermute | solution.py:775
  165.0 31.3 %collective-permute-start.13 = (bf16[256,768]{1,0:T(8,128)(2,1)S(1)}, bf16[256,768]{1,0:T(8,128)(2,1)S(1)}, u32[]{:S(2)}, u32[]{:S(2)}) collective-permute-start(bf16[256,768]{1,0:T(8,128)(2,1)S(1)} %get-tuple-element.277), channel_id=1, source_target_pairs={{0,2},{1,3},{2,0},{3,1},{4,6},{5,7},{6,4},{7,5},{8,10},{9,11},{10,... | collective-permute-start | bytes 1179656 | tf_op jit(solution)/shard_map/ppermute | solution.py:775
  166.6 27.7 %collective-permute-start.11 = (bf16[8,2,32,1024]{3,2,1,0:T(8,128)(2,1)S(1)}, bf16[8,2,32,1024]{3,2,1,0:T(8,128)(2,1)}, u32[]{:S(2)}, u32[]{:S(2)}) collective-permute-start(bf16[8,2,32,1024]{3,2,1,0:T(8,128)(2,1)S(1)} %all-to-all-done.2.mine), channel_id=1, source_target_pairs={{0,1},{1,0},{2,3},{3,2},{4,5},{5,4},{6,7},{7,6},{8,9},{9,8},{10,11... | collective-permute-start | bytes 3145736 | tf_op jit(solution)/shard_map/ppermute | solution.py:775
  208.1 29.7 %collective-permute-start.15 = (bf16[384,1024]{1,0:T(8,128)(2,1)}, bf16[384,1024]{1,0:T(8,128)(2,1)S(1)}, u32[]{:S(2)}, u32[]{:S(2)}) collective-permute-start(bf16[384,1024]{1,0:T(8,128)(2,1)} %get-tuple-element.161.hidden.refs_0_), channel_id=1, source_target_pairs={{0,2},{2,0},{1,3},{3,1},{4,6},{6,4},{5,7},{7,5},{8,10},{10,8},{9,1... | collective-permute-start | bytes 2359304 | tf_op jit(solution)/shard_map/ppermute | solution.py:775
  223.5 30.0 %collective-permute-start.16 = (bf16[384,1024]{1,0:T(8,128)(2,1)S(1)}, bf16[384,1024]{1,0:T(8,128)(2,1)S(1)}, u32[]{:S(2)}, u32[]{:S(2)}) collective-permute-start(bf16[384,1024]{1,0:T(8,128)(2,1)S(1)} %copy-done.57), channel_id=1, source_target_pairs={{0,2},{2,0},{1,3},{3,1},{4,6},{6,4},{5,7},{7,5},{8,10},{10,8},{9,1... | collective-permute-start | bytes 2359304 | tf_op jit(solution)/shard_map/ppermute | solution.py:775
  251.9 37.5 %collective-permute-start.17 = (bf16[384,1024]{1,0:T(8,128)(2,1)}, bf16[384,1024]{1,0:T(8,128)(2,1)S(1)}, u32[]{:S(2)}, u32[]{:S(2)}) collective-permute-start(bf16[384,1024]{1,0:T(8,128)(2,1)} %get-tuple-element.181), channel_id=1, source_target_pairs={{0,2},{2,0},{1,3},{3,1},{4,6},{6,4},{5,7},{7,5},{8,10},{10,8},{9,1... | collective-permute-start | bytes 2359304 | tf_op jit(solution)/shard_map/ppermute | solution.py:775
  268.0 21.5 %collective-permute-start.18 = (bf16[384,1024]{1,0:T(8,128)(2,1)}, bf16[384,1024]{1,0:T(8,128)(2,1)S(1)}, u32[]{:S(2)}, u32[]{:S(2)}) collective-permute-start(bf16[384,1024]{1,0:T(8,128)(2,1)} %get-tuple-element.182), channel_id=1, source_target_pairs={{0,2},{2,0},{1,3},{3,1},{4,6},{6,4},{5,7},{7,5},{8,10},{10,8},{9,1... | collective-permute-start | bytes 2359304 | tf_op jit(solution)/shard_map/ppermute | solution.py:775
  308.3 6.9 %collective-permute-start.19 = (bf16[256,768]{1,0:T(8,128)(2,1)}, bf16[256,768]{1,0:T(8,128)(2,1)}, u32[]{:S(2)}, u32[]{:S(2)}) collective-permute-start(bf16[256,768]{1,0:T(8,128)(2,1)} %get-tuple-element.188), channel_id=1, source_target_pairs={{0,1},{1,0},{2,3},{3,2},{4,5},{5,4},{6,7},{7,6},{8,9},{9,8},{10,11... | collective-permute-start | bytes 1179656 | tf_op jit(solution)/shard_map/ppermute | solution.py:775
  309.3 107.4 %all-to-all-start.3 = ((bf16[32,32,1024]{2,1,0:T(8,128)(2,1)}), bf16[32,32,1024]{2,1,0:T(8,128)(2,1)}, u32[]{:S(2)}, u32[]{:S(2)}) async-start(bf16[32,32,1024]{2,1,0:T(8,128)(2,1)} %bitcast.185), calls=%async_computation.3 | async-start | bytes 4194304 | tf_op jit(solution)/shard_map/all_to_all | solution.py:986
  313.2 50.4 %collective-permute-start.20 = (bf16[256,768]{1,0:T(8,128)(2,1)S(1)}, bf16[256,768]{1,0:T(8,128)(2,1)}, u32[]{:S(2)}, u32[]{:S(2)}) collective-permute-start(bf16[256,768]{1,0:T(8,128)(2,1)S(1)} %copy-done.61), channel_id=1, source_target_pairs={{0,2},{1,3},{2,0},{3,1},{4,6},{5,7},{6,4},{7,5},{8,10},{9,11},{10,... | collective-permute-start | bytes 1179656 | tf_op jit(solution)/shard_map/ppermute | solution.py:775
  315.2 48.5 %collective-permute-start.21 = (bf16[256,768]{1,0:T(8,128)(2,1)S(1)}, bf16[256,768]{1,0:T(8,128)(2,1)}, u32[]{:S(2)}, u32[]{:S(2)}) collective-permute-start(bf16[256,768]{1,0:T(8,128)(2,1)S(1)} %copy-done.60), channel_id=1, source_target_pairs={{0,3},{1,2},{2,1},{3,0},{4,7},{5,6},{6,5},{7,4},{8,11},{9,10},{10,... | collective-permute-start | bytes 1179656 | tf_op jit(solution)/shard_map/ppermute | solution.py:775
  363.7 53.1 %collective-permute-start.22 = (bf16[384,1024]{1,0:T(8,128)(2,1)}, bf16[384,1024]{1,0:T(8,128)(2,1)S(1)}, u32[]{:S(2)}, u32[]{:S(2)}) collective-permute-start(bf16[384,1024]{1,0:T(8,128)(2,1)} %get-tuple-element.202), channel_id=1, source_target_pairs={{0,2},{2,0},{1,3},{3,1},{4,6},{6,4},{5,7},{7,5},{8,10},{10,8},{9,1... | collective-permute-start | bytes 2359304 | tf_op jit(solution)/shard_map/ppermute | solution.py:775
  365.2 51.5 %collective-permute-start.23 = (bf16[384,1024]{1,0:T(8,128)(2,1)}, bf16[384,1024]{1,0:T(8,128)(2,1)}, u32[]{:S(2)}, u32[]{:S(2)}) collective-permute-start(bf16[384,1024]{1,0:T(8,128)(2,1)} %get-tuple-element.203), channel_id=1, source_target_pairs={{0,2},{2,0},{1,3},{3,1},{4,6},{6,4},{5,7},{7,5},{8,10},{10,8},{9,1... | collective-permute-start | bytes 2359304 | tf_op jit(solution)/shard_map/ppermute | solution.py:775
  437.0 19.8 %collective-permute-start.25 = (bf16[384,1024]{1,0:T(8,128)(2,1)}, bf16[384,1024]{1,0:T(8,128)(2,1)S(1)}, u32[]{:S(2)}, u32[]{:S(2)}) collective-permute-start(bf16[384,1024]{1,0:T(8,128)(2,1)} %get-tuple-element.213), channel_id=1, source_target_pairs={{0,2},{2,0},{1,3},{3,1},{4,6},{6,4},{5,7},{7,5},{8,10},{10,8},{9,1... | collective-permute-start | bytes 2359304 | tf_op jit(solution)/shard_map/ppermute | solution.py:775
  458.4 52.6 %all-to-all-start.4 = ((bf16[32,38,768]{2,1,0:T(8,128)(2,1)}), bf16[32,38,768]{2,1,0:T(8,128)(2,1)S(1)}, u32[]{:S(2)}, u32[]{:S(2)}) async-start(bf16[32,38,768]{2,1,0:T(8,128)(2,1)} %pad_maximum_fusion), calls=%async_computation.5 | async-start | bytes 3932160 | tf_op jit(solution)/shard_map/all_to_all | solution.py:1039
  475.2 14.8 %collective-permute-start.28 = (bf16[2,32,2048]{2,1,0:T(8,128)(2,1)S(1)}, bf16[2,32,2048]{2,1,0:T(8,128)(2,1)S(1)}, u32[]{:S(2)}, u32[]{:S(2)}) collective-permute-start(bf16[2,32,2048]{2,1,0:T(8,128)(2,1)S(1)} %bitcast.199), channel_id=1, source_target_pairs={{0,2},{2,0},{1,3},{3,1},{4,6},{6,4},{5,7},{7,5},{8,10},{10,8},{9,1... | collective-permute-start | bytes 786440 | tf_op jit(solution)/shard_map/ppermute | solution.py:775
  478.4 53.7 %collective-permute-start.27 = (bf16[768,1024]{1,0:T(8,128)(2,1)}, bf16[768,1024]{1,0:T(8,128)(2,1)}, u32[]{:S(2)}, u32[]{:S(2)}) collective-permute-start(bf16[768,1024]{1,0:T(8,128)(2,1)} %slice_bitcast_fusion), channel_id=1, source_target_pairs={{0,1},{1,0},{2,3},{3,2},{4,5},{5,4},{6,7},{7,6},{8,9},{9,8},{10,11... | collective-permute-start | bytes 4718600 | tf_op jit(solution)/shard_map/ppermute | solution.py:775
  478.4 32.5 %collective-permute-start.26 = (bf16[384,1024]{1,0:T(8,128)(2,1)S(1)}, bf16[384,1024]{1,0:T(8,128)(2,1)}, u32[]{:S(2)}, u32[]{:S(2)}) collective-permute-start(bf16[384,1024]{1,0:T(8,128)(2,1)S(1)} %copy-done.33), channel_id=1, source_target_pairs={{0,2},{2,0},{1,3},{3,1},{4,6},{6,4},{5,7},{7,5},{8,10},{10,8},{9,1... | collective-permute-start | bytes 2359304 | tf_op jit(solution)/shard_map/ppermute | solution.py:775
  527.6 12.8 %all-to-all-start.5 = ((f32[32,8,128]{2,1,0:T(8,128)}), f32[32,8,128]{2,1,0:T(8,128)S(1)}, u32[]{:S(2)}, u32[]{:S(2)}) async-start(f32[32,8,128]{2,1,0:T(8,128)} %broadcast_in_dim.40), calls=%async_computation.6 | async-start | bytes 262144 | tf_op jit(solution)/shard_map/all_to_all | solution.py:1063
  (68 other events, 530.0 us)
Sparse Core Ops, SparseCore 0:
  37.7 54.4 all-gather.2
  96.2 87.0 all-gather.4
  289.6 139.2 reduce-scatter.1

commit v11 on v10

--- a/solution.py
+++ b/solution.py
@@ -865,10 +865,8 @@
     attend_mine = attend_mine.transpose(2, 0, 1, 3).reshape(rows, shard, 3 * features)
     attend_mine = relative(trade(relative(attend_mine, row), ROW, rows), row)
 
+    condition, tok0, attend_mine = lax.optimization_barrier((condition, tok0, attend_mine))
     cond_act = jax.nn.silu(condition[0].astype(f32)).astype(bf16)
-    cond_act, tok0, attend_mine, tok1 = lax.optimization_barrier(
-        (cond_act, tok0, attend_mine, tok1)
-    )
     attend_full = lax.all_gather(
         attend_mine.reshape(rows * shard, 3 * features), "clip", axis=0, tiled=True
     )
@@ -879,16 +877,17 @@
         f32
     )
     part = mod_mine.shape[1]
-    tok2_two, mod_mine, tok2_one, project_mine, feed_wide, feed_narrow = lax.optimization_barrier(
-        (tok0[count // 2 :], mod_mine, tok2_one, project_weight, widen_weight, narrow_weight)
-    )
-    project_mine = project_mine.T.astype(bf16)
-    project_mine = relative(jnp.stack([project_mine, swap(project_mine, "x", 2, 1)]), far)
+    tok2_two, mod_mine, tok2_one = lax.optimization_barrier((tok0[count // 2 :], mod_mine, tok2_one))
     tok2_two = swap(tok2_two, "x", 2, 1)
     mod_mine = jnp.broadcast_to(
         mod_mine.reshape(clips, 1, frames, part), (clips, rows, frames, part)
     )
     mod = lax.all_to_all(mod_mine.reshape(devices, frames, part), both, 0, 0, tiled=True)
+    mod, project_mine, feed_wide, feed_narrow = lax.optimization_barrier(
+        (mod, project_weight, widen_weight, narrow_weight)
+    )
+    project_mine = project_mine.T.astype(bf16)
+    project_mine = relative(jnp.stack([project_mine, swap(project_mine, "x", 2, 1)]), far)
     mod = mod.transpose(1, 0, 2).reshape(frames, 6, width)
 
     units = widen_weight.shape[1]

time: 571 us -> 562 us (0.984)
  waiting for transfers between devices: 63.1 us -> 81.4 us
  local copies, waits for them, and re-layouts: 48.1 us -> 35.1 us
  other arithmetic: 49.5 us -> 42 us
    ppermute x29, waiting for transfers between devices: 36.5 us -> 51.5 us  [swap(): lax.ppermute(value, axis, [(place, place ^ step) for place in range(size)])]
  transfers between devices with their start and end apart: 38 -> 38, of which waited for: 11 -> 13; matrix products, arithmetic and copies ran while one was open for 14% -> 10% of each run, Pallas kernels for 57% -> 58%
where the time goes in v11:
time: 562 us; the launch traced here: 558 us
  Pallas kernels  322 us (57%)
  waiting for transfers between devices  81.4 us (14%)
  starting transfers between devices  54.3 us (10%)
  other arithmetic  42 us (7%)
  local copies, waits for them, and re-layouts  35.1 us (6%)
  between operations  21.9 us (4%)
    pallas_call x2, Pallas kernels, attend_back(): pl.pallas_call(functools.partial(attend_back_kernel, heads, last), grid=(...  99.4 us
    pallas_call x2, Pallas kernels, attend(): pl.pallas_call(functools.partial(attend_kernel, heads), grid=(count // bl...  54.6 us
    pallas_call x4, Pallas kernels, feed_forward(): pl.pallas_call(feed_kernel, grid=(units // block,), in_specs=[spec, flat,...  54.2 us
    ppermute x29, waiting for transfers between devices, swap(): lax.ppermute(value, axis, [(place, place ^ step) for place in range(size)])  51.5 us
    pallas_call x2, Pallas kernels, first_back(): pl.pallas_call(functools.partial(first_back_kernel, last), grid=(4,), in_...  27.8 us
    ppermute x29, starting transfers between devices, swap(): lax.ppermute(value, axis, [(place, place ^ step) for place in range(size)])  24.5 us
    pallas_call x1, Pallas kernels, feed_weights(): pl.pallas_call(functools.partial(feed_weight_kernel, len(hidden)), grid=(...  21 us
    pallas_call x2, Pallas kernels, project_qkv(): pl.pallas_call(qkv_kernel, grid=(4,), in_specs=specs + [whole(), angle, a...  18.5 us
  transfers between devices with their start and end apart: 38, of which 13 were waited for; matrix products, arithmetic and copies ran while one was open for 10% of the time, Pallas kernels for 58%

profile of v11, /device:TPU:0, one launch (start us, length us, event | category | flops | bytes accessed | tf_op | source)
XLA Modules:
  0.0 557.9 jit_solution(8729582308321571629)
XLA Ops:
  18.6 5.8 %all-to-all-start = ((bf16[8,12,1024]{2,1,0:T(8,128)(2,1)}), bf16[8,12,1024]{2,1,0:T(8,128)(2,1)S(1)}, u32[]{:S(2)}, u32[]{:S(2)}) async-start(bf16[8,12,1024]{2,1,0:T(8,128)(2,1)} %broadcast_in_dim.37), calls=%async_computation | async-start | bytes 524288 | tf_op jit(solution)/shard_map/all_to_all | solution.py:873
  25.4 8.0 %all-to-all-done = bf16[8,12,1024]{2,1,0:T(8,128)(2,1)S(1)} async-done(((bf16[8,12,1024]{2,1,0:T(8,128)(2,1)}), bf16[8,12,1024]{2,1,0:T(8,128)(2,1)S(1)}, u32[]{:S(2)}, u32[]{:S(2)}) %all-to-all-start) | async-done | bytes 196640 | tf_op jit(solution)/shard_map/all_to_all | solution.py:873
  34.6 5.9 %all-to-all-start.1 = ((f32[32,12,192]{2,1,0:T(8,128)}), f32[32,12,192]{2,1,0:T(8,128)}, u32[]{:S(2)}, u32[]{:S(2)}) async-start(f32[32,12,192]{2,1,0:T(8,128)} %bitcast.183), calls=%async_computation.1 | async-start | bytes 1048576 | tf_op jit(solution)/shard_map/all_to_all | solution.py:885
  41.7 14.4 %all-to-all-done.1 = f32[32,12,192]{2,1,0:T(8,128)} async-done(((f32[32,12,192]{2,1,0:T(8,128)}), f32[32,12,192]{2,1,0:T(8,128)}, u32[]{:S(2)}, u32[]{:S(2)}) %all-to-all-start.1) | async-done | bytes 294944 | tf_op jit(solution)/shard_map/all_to_all | solution.py:885
  65.7 5.2 collective-permute-done.5
  76.5 10.8 %collective-permute-done.6.two = bf16[400,1024]{1,0:T(8,128)(2,1)} collective-permute-done((bf16[400,1024]{1,0:T(8,128)(2,1)S(1)}, bf16[400,1024]{1,0:T(8,128)(2,1)}, u32[]{:S(2)}, u32[]{:S(2)}) %collective-permute-start.6) | collective-permute-done | bytes 819232 | tf_op jit(solution)/shard_map/ppermute | solution.py:775
  87.4 3.1 all-gather.3.cloned.1.call-done
  101.7 9.3 %shard_map.488.k1.v1.q_ref = bf16[768,1536]{1,0:T(8,128)(2,1)} custom-call(bf16[784,1024]{1,0:T(8,128)(2,1)} %copy-done.1, bf16[784,1024]{1,0:T(8,128)(2,1)} %copy-done.1, bf16[784,1024]{1,0:T(8,128)(2,1)} %copy-done.4, bf16[784,1024]{1,0:T(8,128)(2,1)} %copy-done.4, f32[12,6,1024]{2,1,0:T(8,128)} %reshape.439.mod, bf16[768,1024]{1,0:T(8,128)(2,1)} %bitcast.190, ...), custom_call_target="tpu_custom_call" | custom-call | flops 2415919104 | bytes 6291456 | tf_op jit(solution)/shard_map/pallas_call | solution.py:131
  112.1 3.6 all-to-all-start.2
  117.7 9.2 %shard_map.487.q_ref.k2.v2 = bf16[768,1536]{1,0:T(8,128)(2,1)} custom-call(bf16[384,1024]{1,0:T(8,128)(2,1)} %collective-permute-done.4.one, bf16[400,1024]{1,0:T(8,128)(2,1)} %collective-permute-done.6.two, bf16[384,1024]{1,0:T(8,128)(2,1)} %collective-permute-done.7.three, bf16[400,1024]{1,0:T(8,128)(2,1)} %copy-done.57, f32[12,6,1024]{2,1,0:T(8,128)} %reshape.439.mod, ...), custom_call_target="tpu_custom_call" | custom-call | flops 2415919104 | bytes 6291456 | tf_op jit(solution)/shard_map/pallas_call | solution.py:131
  127.0 27.1 %shard_map.489 = (bf16[2,256,768]{2,1,0:T(8,128)(2,1)}, f32[4,1536]{1,0:T(4,128)}) custom-call(bf16[768,1536]{1,0:T(8,128)(2,1)} %shard_map.487.q_ref.k2.v2, bf16[768,1536]{1,0:T(8,128)(2,1)} %shard_map.488.k1.v1.q_ref, bf16[768,1536]{1,0:T(8,128)(2,1)} %shard_map.487.q_ref.k2.v2, bf16[768,1536]{1,0:T(8,128)(2,1)} %shard_map.488.k1.v1.q_ref, ...), custom_call_target="tpu_custom_call" | custom-call | flops 19327352832 | bytes 3145728 | tf_op jit(solution)/shard_map/pallas_call | solution.py:186
  154.1 4.1 all-to-all-done.2.mine
  161.6 27.5 %shard_map.490 = (bf16[2,256,768]{2,1,0:T(8,128)(2,1)}, f32[4,1536]{1,0:T(4,128)}) custom-call(bf16[768,1536]{1,0:T(8,128)(2,1)} %shard_map.488.k1.v1.q_ref, bf16[768,1536]{1,0:T(8,128)(2,1)} %shard_map.488.k1.v1.q_ref, bf16[768,1536]{1,0:T(8,128)(2,1)} %shard_map.487.q_ref.k2.v2, bf16[768,1536]{1,0:T(8,128)(2,1)} %shard_map.488.k1.v1.q_ref, ...), custom_call_target="tpu_custom_call" | custom-call | flops 19327352832 | bytes 3145728 | tf_op jit(solution)/shard_map/pallas_call | solution.py:186
  193.0 10.2 %shard_map.491 = (f32[12,64,1024]{2,1,0:T(8,128)}, bf16[384,1024]{1,0:T(8,128)(2,1)}, bf16[384,1024]{1,0:T(8,128)(2,1)}, bf16[768,1024]{1,0:T(8,128)(2,1)}, bf16...) custom-call(s32[5]{0:T(128)} %pad_add_fusion.order, bf16[2,256,768]{2,1,0:T(8,128)(2,1)} %get-tuple-element.157.a0.out_ref, ...), custom_call_target="tpu_custom_call" | custom-call | flops 1610612736 | bytes 11010048 | tf_op jit(solution)/shard_map/pallas_call | solution.py:401
  204.5 13.8 %shard_map.492 = (f32[384,1024]{1,0:T(8,128)}, f32[384,1024]{1,0:T(8,128)}, bf16[384,2048]{1,0:T(8,128)(2,1)}, bf16[384,2048]{1,0:T(8,128)(2,1)}, f32[6,1,1024]{2,1,0:T(1,128)}) custom-call(bf16[16,2,2,32,2048]{4,3,2,1,0:T(8,128)(2,1)} %bitcast.208, bf16[384,1024]{1,0:T(8,128)(2,1)} %get-tuple-element.161.hidden.refs_0_, ...), custom_call_target="tpu_custom_call" | custom-call | flops 6442450944 | bytes 11534336 | tf_op jit(solution)/shard_map/pallas_call | solution.py:498
  219.2 13.7 %shard_map.493 = (f32[384,1024]{1,0:T(8,128)}, f32[384,1024]{1,0:T(8,128)}, bf16[384,2048]{1,0:T(8,128)(2,1)}, bf16[384,2048]{1,0:T(8,128)(2,1)}, f32[6,1,1024]{2,1,0:T(1,128)}) custom-call(bf16[16,2,2,32,2048]{4,3,2,1,0:T(8,128)(2,1)} %bitcast.209, bf16[384,1024]{1,0:T(8,128)(2,1)} %get-tuple-element.169.hidden.refs_1_, ...), custom_call_target="tpu_custom_call" | custom-call | flops 6442450944 | bytes 11534336 | tf_op jit(solution)/shard_map/pallas_call | solution.py:498
  233.8 13.2 %shard_map.494 = (bf16[384,1024]{1,0:T(8,128)(2,1)}, bf16[384,1024]{1,0:T(8,128)(2,1)}, bf16[384,2048]{1,0:T(8,128)(2,1)}, bf16[384,2048]{1,0:T(8,128)(2,1)}, f32[6,1,1024]{2,1,0:T(1,128)}) custom-call(bf16[16,2,2,32,2048]{4,3,2,1,0:T(8,128)(2,1)} %bitcast.210, bf16[384,1024]{1,0:T(8,128)(2,1)} %copy-done.59, ...), custom_call_target="tpu_custom_call" | custom-call | flops 6442450944 | bytes 11534336 | tf_op jit(solution)/shard_map/pallas_call | solution.py:498
  249.1 13.6 %shard_map.495 = (bf16[384,1024]{1,0:T(8,128)(2,1)}, bf16[384,1024]{1,0:T(8,128)(2,1)}, bf16[384,2048]{1,0:T(8,128)(2,1)}, bf16[384,2048]{1,0:T(8,128)(2,1)}, f32[6,1,1024]{2,1,0:T(1,128)}) custom-call(bf16[16,2,2,32,2048]{4,3,2,1,0:T(8,128)(2,1)} %bitcast.211, bf16[384,1024]{1,0:T(8,128)(2,1)} %copy-done.60, ...), custom_call_target="tpu_custom_call" | custom-call | flops 6442450944 | bytes 11534336 | tf_op jit(solution)/shard_map/pallas_call | solution.py:498
  263.6 21.0 %shard_map.496 = bf16[16,2,2,32,2048]{4,3,2,1,0:T(8,128)(2,1)} custom-call(bf16[384,1024]{1,0:T(8,128)(2,1)} %get-tuple-element.161.hidden.refs_0_, bf16[384,1024]{1,0:T(8,128)(2,1)} %get-tuple-element.169.hidden.refs_1_, bf16[384,1024]{1,0:T(8,128)(2,1)} %copy-done.59, bf16[384,1024]{1,0:T(8,128)(2,1)} %copy-done.60, ...), custom_call_target="tpu_custom_call" | custom-call | flops 12884901888 | bytes 20971520 | tf_op jit(solution)/shard_map/pallas_call | solution.py:549
  285.8 17.6 %shard_map.497 = (f32[12,64,1024]{2,1,0:T(8,128)}, f32[12,3,1024]{2,1,0:T(4,128)}, bf16[256,768]{1,0:T(8,128)(2,1)}, bf16[256,768]{1,0:T(8,128)(2,1)}, bf16[256,...) custom-call(s32[5]{0:T(128)} %pad_add_fusion.order, f32[384,1024]{1,0:T(8,128)} %get-tuple-element.163.into1, ...), custom_call_target="tpu_custom_call" | custom-call | flops 3221225472 | bytes 18874368 | tf_op jit(solution)/shard_map/pallas_call | solution.py:612
  304.5 3.8 all-to-all-start.3
  310.1 48.4 %shard_map.498 = (bf16[256,1536]{1,0:T(8,128)(2,1)}, f32[256,3072]{1,0:T(8,128)}, f32[256,3072]{1,0:T(8,128)}) custom-call(bf16[768,1536]{1,0:T(8,128)(2,1)} %shard_map.488.k1.v1.q_ref, bf16[768,1536]{1,0:T(8,128)(2,1)} %shard_map.488.k1.v1.q_ref, bf16[768,1536]{1,0:T(8,128)(2,1)} %shard_map.487.q_ref.k2.v2, bf16[768,1536]{1,0:T(8,128)(2,1)} %shard_map.488.k1.v1.q_ref, ...), custom_call_target="tpu_custom_call" | custom-call | flops 41070624768 | bytes 6291456 | tf_op jit(solution)/shard_map/pallas_call | solution.py:332
  360.7 51.0 %shard_map.499 = (bf16[256,1536]{1,0:T(8,128)(2,1)}, bf16[256,3072]{1,0:T(8,128)(2,1)}, bf16[256,3072]{1,0:T(8,128)(2,1)}) custom-call(bf16[768,1536]{1,0:T(8,128)(2,1)} %shard_map.487.q_ref.k2.v2, bf16[768,1536]{1,0:T(8,128)(2,1)} %shard_map.488.k1.v1.q_ref, bf16[768,1536]{1,0:T(8,128)(2,1)} %shard_map.487.q_ref.k2.v2, ...), custom_call_target="tpu_custom_call" | custom-call | flops 41070624768 | bytes 6291456 | tf_op jit(solution)/shard_map/pallas_call | solution.py:332
  411.7 13.2 %shard_map.500 = (bf16[2,768,1024]{2,1,0:T(8,128)(2,1)}, f32[768,1024]{1,0:T(8,128)}, f32[12,2,1024]{2,1,0:T(2,128)}) custom-call(bf16[384,1024]{1,0:T(8,128)(2,1)} %collective-permute-done.4.one, bf16[400,1024]{1,0:T(8,128)(2,1)} %collective-permute-done.6.two, bf16[384,1024]{1,0:T(8,128)(2,1)} %collective-permute-done.7.three, ...), custom_call_target="tpu_custom_call" | custom-call | flops 4831838208 | bytes 9437184 | tf_op jit(solution)/shard_map/pallas_call | solution.py:716
  426.8 3.3 collective-permute-done.24
  433.4 14.6 %shard_map.501 = (bf16[2,768,1024]{2,1,0:T(8,128)(2,1)}, bf16[1024,768]{1,0:T(8,128)(2,1)}, f32[12,2,1024]{2,1,0:T(2,128)}) custom-call(bf16[784,1024]{1,0:T(8,128)(2,1)} %copy-done.1, bf16[784,1024]{1,0:T(8,128)(2,1)} %copy-done.1, bf16[784,1024]{1,0:T(8,128)(2,1)} %copy-done.4, bf16[784,1024]{1,0:T(8,128)(2,1)} %copy-done.4, f32[12,6,1024]{2,1,0:T(8,128)} %reshape.439.mod, ...), custom_call_target="tpu_custom_call" | custom-call | flops 4831838208 | bytes 9437184 | tf_op jit(solution)/shard_map/pallas_call | solution.py:716
  453.3 5.8 %all-to-all-start.4 = ((bf16[32,38,768]{2,1,0:T(8,128)(2,1)}), bf16[32,38,768]{2,1,0:T(8,128)(2,1)S(1)}, u32[]{:S(2)}, u32[]{:S(2)}) async-start(bf16[32,38,768]{2,1,0:T(8,128)(2,1)} %pad_maximum_fusion), calls=%async_computation.5 | async-start | bytes 3932160 | tf_op jit(solution)/shard_map/all_to_all | solution.py:1038
  461.6 5.3 shard_map.502
  473.7 11.3 %collective-permute-done.28 = bf16[2,32,2048]{2,1,0:T(8,128)(2,1)S(1)} collective-permute-done((bf16[2,32,2048]{2,1,0:T(8,128)(2,1)S(1)}, bf16[2,32,2048]{2,1,0:T(8,128)(2,1)S(1)}, u32[]{:S(2)}, u32[]{:S(2)}) %collective-permute-start.28) | collective-permute-done | bytes 262176 | tf_op jit(solution)/shard_map/ppermute | solution.py:775
  490.7 15.3 %collective-permute-done.26.far2 = bf16[384,1024]{1,0:T(8,128)(2,1)} collective-permute-done((bf16[384,1024]{1,0:T(8,128)(2,1)S(1)}, bf16[384,1024]{1,0:T(8,128)(2,1)}, u32[]{:S(2)}, u32[]{:S(2)}) %collective-permute-start.26) | collective-permute-done | bytes 786464 | tf_op jit(solution)/shard_map/ppermute | solution.py:775
  522.6 4.6 all-to-all-start.5
  527.2 7.9 %shard_map.504 = f32[12,64,1024]{2,1,0:T(8,128)} custom-call(bf16[12,64,1024]{2,1,0:T(8,128)(2,1)} %bitcast.160, f32[12,6,1024]{2,1,0:T(8,128)} %reshape.439.mod, f32[12,64,1024]{2,1,0:T(8,128)} %get-tuple-element.230.middle_grad, bf16[2,768,1024]{2,1,0:T(8,128)(2,1)} %get-tuple-element.231.one, bf16[768,1024]{1,0:T(8,128)(2,1)} %collective-permute-done.27.two, ...), custom_call_target="tpu_custom_call" | custom-call | flops 15728640 | bytes 12582912 | tf_op jit(solution)/shard_map/pallas_call | solution.py:746
  (323 shorter events, 114.6 us)
Async XLA Ops:
  9.5 7.2 %collective-permute-start.2 = (bf16[32,768]{1,0:T(8,128)(2,1)S(1)}, bf16[32,768]{1,0:T(8,128)(2,1)S(1)}, u32[]{:S(2)}, u32[]{:S(2)}) collective-permute-start(bf16[32,768]{1,0:T(8,128)(2,1)S(1)} %get-tuple-element.301), channel_id=1, source_target_pairs={{0,3},{1,2},{2,1},{3,0},{4,7},{5,6},{6,5},{7,4},{8,11},{9,10},{10,... | collective-permute-start | bytes 147464 | tf_op jit(solution)/shard_map/ppermute | solution.py:775
  13.5 20.2 %collective-permute-start.4 = (bf16[384,1024]{1,0:T(8,128)(2,1)}, bf16[384,1024]{1,0:T(8,128)(2,1)}, u32[]{:S(2)}, u32[]{:S(2)}) collective-permute-start(bf16[384,1024]{1,0:T(8,128)(2,1)} %bitcast.21), channel_id=1, source_target_pairs={{0,2},{2,0},{1,3},{3,1},{4,6},{6,4},{5,7},{7,5},{8,10},{10,8},{9,1... | collective-permute-start | bytes 2359304 | tf_op jit(solution)/shard_map/ppermute | solution.py:775
  18.6 14.8 %all-to-all-start = ((bf16[8,12,1024]{2,1,0:T(8,128)(2,1)}), bf16[8,12,1024]{2,1,0:T(8,128)(2,1)S(1)}, u32[]{:S(2)}, u32[]{:S(2)}) async-start(bf16[8,12,1024]{2,1,0:T(8,128)(2,1)} %broadcast_in_dim.37), calls=%async_computation | async-start | bytes 524288 | tf_op jit(solution)/shard_map/all_to_all | solution.py:873
  34.6 21.4 %all-to-all-start.1 = ((f32[32,12,192]{2,1,0:T(8,128)}), f32[32,12,192]{2,1,0:T(8,128)}, u32[]{:S(2)}, u32[]{:S(2)}) async-start(f32[32,12,192]{2,1,0:T(8,128)} %bitcast.183), calls=%async_computation.1 | async-start | bytes 1048576 | tf_op jit(solution)/shard_map/all_to_all | solution.py:885
  40.5 50.0 %all-gather.3.cloned.1.call-start = ((), (), s32[]{:S(2)}) async-start(), calls=%async_computation.7 | async-start | bytes 1769472 | tf_op jit(solution)/shard_map/all_gather | solution.py:870
  41.4 163.0 %all-gather.5.cloned.1.call-start = ((), (), s32[]{:S(2)}) async-start(), calls=%async_computation.8 | async-start | bytes 8912896 | tf_op jit(solution)/shard_map/all_gather | solution.py:902
  61.4 9.5 %collective-permute-start.5 = (bf16[2,32,2048]{2,1,0:T(8,128)(2,1)}, bf16[2,32,2048]{2,1,0:T(8,128)(2,1)}, u32[]{:S(2)}, u32[]{:S(2)}) collective-permute-start(bf16[2,32,2048]{2,1,0:T(8,128)(2,1)} %bitcast.154), channel_id=1, source_target_pairs={{0,2},{2,0},{1,3},{3,1},{4,6},{6,4},{5,7},{7,5},{8,10},{10,8},{9,1... | collective-permute-start | bytes 786440 | tf_op jit(solution)/shard_map/ppermute | solution.py:775
  62.3 25.1 %collective-permute-start.6 = (bf16[400,1024]{1,0:T(8,128)(2,1)S(1)}, bf16[400,1024]{1,0:T(8,128)(2,1)}, u32[]{:S(2)}, u32[]{:S(2)}) collective-permute-start(bf16[400,1024]{1,0:T(8,128)(2,1)S(1)} %copy-done.29), channel_id=1, source_target_pairs={{0,2},{2,0},{1,3},{3,1},{4,6},{6,4},{5,7},{7,5},{8,10},{10,8},{9,1... | collective-permute-start | bytes 2457608 | tf_op jit(solution)/shard_map/ppermute | solution.py:775
  91.5 8.1 %collective-permute-start.8 = (bf16[400,1024]{1,0:T(8,128)(2,1)}, bf16[400,1024]{1,0:T(8,128)(2,1)S(1)}, u32[]{:S(2)}, u32[]{:S(2)}) collective-permute-start(bf16[400,1024]{1,0:T(8,128)(2,1)} %collective-permute-done.6.two), channel_id=1, source_target_pairs={{0,1},{1,0},{2,3},{3,2},{4,5},{5,4},{6,7},{7,6},{8,9},{9,8},{10,11... | collective-permute-start | bytes 2457608 | tf_op jit(solution)/shard_map/ppermute | solution.py:775
  94.5 23.2 %collective-permute-start.7 = (bf16[384,1024]{1,0:T(8,128)(2,1)}, bf16[384,1024]{1,0:T(8,128)(2,1)}, u32[]{:S(2)}, u32[]{:S(2)}) collective-permute-start(bf16[384,1024]{1,0:T(8,128)(2,1)} %collective-permute-done.4.one), channel_id=1, source_target_pairs={{0,1},{1,0},{2,3},{3,2},{4,5},{5,4},{6,7},{7,6},{8,9},{9,8},{10,11... | collective-permute-start | bytes 2359304 | tf_op jit(solution)/shard_map/ppermute | solution.py:775
  98.2 55.9 %collective-permute-start.10 = (bf16[12,64,1024]{2,1,0:T(8,128)(2,1)}, bf16[12,64,1024]{2,1,0:T(8,128)(2,1)}, u32[]{:S(2)}, u32[]{:S(2)}) collective-permute-start(bf16[12,64,1024]{2,1,0:T(8,128)(2,1)} %bitcast.164), channel_id=1, source_target_pairs={{0,2},{2,0},{1,3},{3,1},{4,6},{6,4},{5,7},{7,5},{8,10},{10,8},{9,1... | collective-permute-start | bytes 4718600 | tf_op jit(solution)/shard_map/ppermute | solution.py:775
  112.1 46.1 %all-to-all-start.2 = ((bf16[8,2,32,1024]{3,2,1,0:T(8,128)(2,1)}), bf16[8,2,32,1024]{3,2,1,0:T(8,128)(2,1)S(1)}, u32[]{:S(2)}, u32[]{:S(2)}) async-start(bf16[8,2,32,1024]{3,2,1,0:T(8,128)(2,1)} %broadcast_in_dim.42), calls=%async_computation.2 | async-start | bytes 2097152 | tf_op jit(solution)/shard_map/all_to_all | solution.py:928
  115.6 336.1 %reduce-scatter.2.cloned.1.call-start = ((), (), s32[]{:S(2)}) async-start(), calls=%async_computation.9 | async-start | bytes 8912896 | tf_op jit(solution)/shard_map/reduce_scatter | solution.py:974
  159.7 31.5 %collective-permute-start.14 = (bf16[256,768]{1,0:T(8,128)(2,1)S(1)}, bf16[256,768]{1,0:T(8,128)(2,1)S(1)}, u32[]{:S(2)}, u32[]{:S(2)}) collective-permute-start(bf16[256,768]{1,0:T(8,128)(2,1)S(1)} %get-tuple-element.276), channel_id=1, source_target_pairs={{0,3},{1,2},{2,1},{3,0},{4,7},{5,6},{6,5},{7,4},{8,11},{9,10},{10,... | collective-permute-start | bytes 1179656 | tf_op jit(solution)/shard_map/ppermute | solution.py:775
  159.8 31.4 %collective-permute-start.13 = (bf16[256,768]{1,0:T(8,128)(2,1)S(1)}, bf16[256,768]{1,0:T(8,128)(2,1)S(1)}, u32[]{:S(2)}, u32[]{:S(2)}) collective-permute-start(bf16[256,768]{1,0:T(8,128)(2,1)S(1)} %get-tuple-element.277), channel_id=1, source_target_pairs={{0,2},{1,3},{2,0},{3,1},{4,6},{5,7},{6,4},{7,5},{8,10},{9,11},{10,... | collective-permute-start | bytes 1179656 | tf_op jit(solution)/shard_map/ppermute | solution.py:775
  161.0 28.2 %collective-permute-start.11 = (bf16[8,2,32,1024]{3,2,1,0:T(8,128)(2,1)S(1)}, bf16[8,2,32,1024]{3,2,1,0:T(8,128)(2,1)S(1)}, u32[]{:S(2)}, u32[]{:S(2)}) collective-permute-start(bf16[8,2,32,1024]{3,2,1,0:T(8,128)(2,1)S(1)} %all-to-all-done.2.mine), channel_id=1, source_target_pairs={{0,1},{1,0},{2,3},{3,2},{4,5},{5,4},{6,7},{7,6},{8,9},{9,8},{10,11... | collective-permute-start | bytes 3145736 | tf_op jit(solution)/shard_map/ppermute | solution.py:775
  203.3 29.6 %collective-permute-start.15 = (bf16[384,1024]{1,0:T(8,128)(2,1)}, bf16[384,1024]{1,0:T(8,128)(2,1)S(1)}, u32[]{:S(2)}, u32[]{:S(2)}) collective-permute-start(bf16[384,1024]{1,0:T(8,128)(2,1)} %get-tuple-element.161.hidden.refs_0_), channel_id=1, source_target_pairs={{0,2},{2,0},{1,3},{3,1},{4,6},{6,4},{5,7},{7,5},{8,10},{10,8},{9,1... | collective-permute-start | bytes 2359304 | tf_op jit(solution)/shard_map/ppermute | solution.py:775
  218.3 29.9 %collective-permute-start.16 = (bf16[384,1024]{1,0:T(8,128)(2,1)S(1)}, bf16[384,1024]{1,0:T(8,128)(2,1)S(1)}, u32[]{:S(2)}, u32[]{:S(2)}) collective-permute-start(bf16[384,1024]{1,0:T(8,128)(2,1)S(1)} %copy-done.58), channel_id=1, source_target_pairs={{0,2},{2,0},{1,3},{3,1},{4,6},{6,4},{5,7},{7,5},{8,10},{10,8},{9,1... | collective-permute-start | bytes 2359304 | tf_op jit(solution)/shard_map/ppermute | solution.py:775
  247.0 37.6 %collective-permute-start.17 = (bf16[384,1024]{1,0:T(8,128)(2,1)}, bf16[384,1024]{1,0:T(8,128)(2,1)S(1)}, u32[]{:S(2)}, u32[]{:S(2)}) collective-permute-start(bf16[384,1024]{1,0:T(8,128)(2,1)} %get-tuple-element.181), channel_id=1, source_target_pairs={{0,2},{2,0},{1,3},{3,1},{4,6},{6,4},{5,7},{7,5},{8,10},{10,8},{9,1... | collective-permute-start | bytes 2359304 | tf_op jit(solution)/shard_map/ppermute | solution.py:775
  262.7 22.0 %collective-permute-start.18 = (bf16[384,1024]{1,0:T(8,128)(2,1)}, bf16[384,1024]{1,0:T(8,128)(2,1)S(1)}, u32[]{:S(2)}, u32[]{:S(2)}) collective-permute-start(bf16[384,1024]{1,0:T(8,128)(2,1)} %get-tuple-element.182), channel_id=1, source_target_pairs={{0,2},{2,0},{1,3},{3,1},{4,6},{6,4},{5,7},{7,5},{8,10},{10,8},{9,1... | collective-permute-start | bytes 2359304 | tf_op jit(solution)/shard_map/ppermute | solution.py:775
  303.4 6.7 %collective-permute-start.19 = (bf16[256,768]{1,0:T(8,128)(2,1)}, bf16[256,768]{1,0:T(8,128)(2,1)}, u32[]{:S(2)}, u32[]{:S(2)}) collective-permute-start(bf16[256,768]{1,0:T(8,128)(2,1)} %get-tuple-element.188), channel_id=1, source_target_pairs={{0,1},{1,0},{2,3},{3,2},{4,5},{5,4},{6,7},{7,6},{8,9},{9,8},{10,11... | collective-permute-start | bytes 1179656 | tf_op jit(solution)/shard_map/ppermute | solution.py:775
  304.5 107.2 %all-to-all-start.3 = ((bf16[32,32,1024]{2,1,0:T(8,128)(2,1)}), bf16[32,32,1024]{2,1,0:T(8,128)(2,1)}, u32[]{:S(2)}, u32[]{:S(2)}) async-start(bf16[32,32,1024]{2,1,0:T(8,128)(2,1)} %bitcast.184), calls=%async_computation.3 | async-start | bytes 4194304 | tf_op jit(solution)/shard_map/all_to_all | solution.py:985
  308.3 50.3 %collective-permute-start.20 = (bf16[256,768]{1,0:T(8,128)(2,1)S(1)}, bf16[256,768]{1,0:T(8,128)(2,1)}, u32[]{:S(2)}, u32[]{:S(2)}) collective-permute-start(bf16[256,768]{1,0:T(8,128)(2,1)S(1)} %copy-done.62), channel_id=1, source_target_pairs={{0,2},{1,3},{2,0},{3,1},{4,6},{5,7},{6,4},{7,5},{8,10},{9,11},{10,... | collective-permute-start | bytes 1179656 | tf_op jit(solution)/shard_map/ppermute | solution.py:775
  310.1 48.5 %collective-permute-start.21 = (bf16[256,768]{1,0:T(8,128)(2,1)S(1)}, bf16[256,768]{1,0:T(8,128)(2,1)}, u32[]{:S(2)}, u32[]{:S(2)}) collective-permute-start(bf16[256,768]{1,0:T(8,128)(2,1)S(1)} %copy-done.61), channel_id=1, source_target_pairs={{0,3},{1,2},{2,1},{3,0},{4,7},{5,6},{6,5},{7,4},{8,11},{9,10},{10,... | collective-permute-start | bytes 1179656 | tf_op jit(solution)/shard_map/ppermute | solution.py:775
  358.6 53.1 %collective-permute-start.22 = (bf16[384,1024]{1,0:T(8,128)(2,1)}, bf16[384,1024]{1,0:T(8,128)(2,1)S(1)}, u32[]{:S(2)}, u32[]{:S(2)}) collective-permute-start(bf16[384,1024]{1,0:T(8,128)(2,1)} %get-tuple-element.202), channel_id=1, source_target_pairs={{0,2},{2,0},{1,3},{3,1},{4,6},{6,4},{5,7},{7,5},{8,10},{10,8},{9,1... | collective-permute-start | bytes 2359304 | tf_op jit(solution)/shard_map/ppermute | solution.py:775
  360.1 51.6 %collective-permute-start.23 = (bf16[384,1024]{1,0:T(8,128)(2,1)}, bf16[384,1024]{1,0:T(8,128)(2,1)}, u32[]{:S(2)}, u32[]{:S(2)}) collective-permute-start(bf16[384,1024]{1,0:T(8,128)(2,1)} %get-tuple-element.203), channel_id=1, source_target_pairs={{0,2},{2,0},{1,3},{3,1},{4,6},{6,4},{5,7},{7,5},{8,10},{10,8},{9,1... | collective-permute-start | bytes 2359304 | tf_op jit(solution)/shard_map/ppermute | solution.py:775
  432.0 19.8 %collective-permute-start.25 = (bf16[384,1024]{1,0:T(8,128)(2,1)}, bf16[384,1024]{1,0:T(8,128)(2,1)S(1)}, u32[]{:S(2)}, u32[]{:S(2)}) collective-permute-start(bf16[384,1024]{1,0:T(8,128)(2,1)} %get-tuple-element.213), channel_id=1, source_target_pairs={{0,2},{2,0},{1,3},{3,1},{4,6},{6,4},{5,7},{7,5},{8,10},{10,8},{9,1... | collective-permute-start | bytes 2359304 | tf_op jit(solution)/shard_map/ppermute | solution.py:775
  453.3 52.7 %all-to-all-start.4 = ((bf16[32,38,768]{2,1,0:T(8,128)(2,1)}), bf16[32,38,768]{2,1,0:T(8,128)(2,1)S(1)}, u32[]{:S(2)}, u32[]{:S(2)}) async-start(bf16[32,38,768]{2,1,0:T(8,128)(2,1)} %pad_maximum_fusion), calls=%async_computation.5 | async-start | bytes 3932160 | tf_op jit(solution)/shard_map/all_to_all | solution.py:1038
  470.2 14.8 %collective-permute-start.28 = (bf16[2,32,2048]{2,1,0:T(8,128)(2,1)S(1)}, bf16[2,32,2048]{2,1,0:T(8,128)(2,1)S(1)}, u32[]{:S(2)}, u32[]{:S(2)}) collective-permute-start(bf16[2,32,2048]{2,1,0:T(8,128)(2,1)S(1)} %bitcast.198), channel_id=1, source_target_pairs={{0,2},{2,0},{1,3},{3,1},{4,6},{6,4},{5,7},{7,5},{8,10},{10,8},{9,1... | collective-permute-start | bytes 786440 | tf_op jit(solution)/shard_map/ppermute | solution.py:775
  473.5 53.7 %collective-permute-start.27 = (bf16[768,1024]{1,0:T(8,128)(2,1)}, bf16[768,1024]{1,0:T(8,128)(2,1)}, u32[]{:S(2)}, u32[]{:S(2)}) collective-permute-start(bf16[768,1024]{1,0:T(8,128)(2,1)} %slice_bitcast_fusion), channel_id=1, source_target_pairs={{0,1},{1,0},{2,3},{3,2},{4,5},{5,4},{6,7},{7,6},{8,9},{9,8},{10,11... | collective-permute-start | bytes 4718600 | tf_op jit(solution)/shard_map/ppermute | solution.py:775
  473.5 32.5 %collective-permute-start.26 = (bf16[384,1024]{1,0:T(8,128)(2,1)S(1)}, bf16[384,1024]{1,0:T(8,128)(2,1)}, u32[]{:S(2)}, u32[]{:S(2)}) collective-permute-start(bf16[384,1024]{1,0:T(8,128)(2,1)S(1)} %copy-done.34), channel_id=1, source_target_pairs={{0,2},{2,0},{1,3},{3,1},{4,6},{6,4},{5,7},{7,5},{8,10},{10,8},{9,1... | collective-permute-start | bytes 2359304 | tf_op jit(solution)/shard_map/ppermute | solution.py:775
  522.6 12.8 %all-to-all-start.5 = ((f32[32,8,128]{2,1,0:T(8,128)}), f32[32,8,128]{2,1,0:T(8,128)S(1)}, u32[]{:S(2)}, u32[]{:S(2)}) async-start(f32[32,8,128]{2,1,0:T(8,128)} %broadcast_in_dim.43), calls=%async_computation.6 | async-start | bytes 262144 | tf_op jit(solution)/shard_map/all_to_all | solution.py:1062
  (69 other events, 480.5 us)
Sparse Core Ops, SparseCore 0:
  44.0 46.4 all-gather.2
  93.2 85.5 all-gather.4
  284.8 139.0 reduce-scatter.1

commit v12 on v11

--- a/solution.py
+++ b/solution.py
@@ -865,8 +865,10 @@
     attend_mine = attend_mine.transpose(2, 0, 1, 3).reshape(rows, shard, 3 * features)
     attend_mine = relative(trade(relative(attend_mine, row), ROW, rows), row)
 
-    condition, tok0, attend_mine = lax.optimization_barrier((condition, tok0, attend_mine))
     cond_act = jax.nn.silu(condition[0].astype(f32)).astype(bf16)
+    cond_act, tok0 = lax.optimization_barrier((cond_act, tok0))
+    project_mine = project_weight.T.astype(bf16)
+    project_mine = relative(jnp.stack([project_mine, swap(project_mine, "x", 2, 1)]), far)
     attend_full = lax.all_gather(
         attend_mine.reshape(rows * shard, 3 * features), "clip", axis=0, tiled=True
     )
@@ -883,15 +885,10 @@
         mod_mine.reshape(clips, 1, frames, part), (clips, rows, frames, part)
     )
     mod = lax.all_to_all(mod_mine.reshape(devices, frames, part), both, 0, 0, tiled=True)
-    mod, project_mine, feed_wide, feed_narrow = lax.optimization_barrier(
-        (mod, project_weight, widen_weight, narrow_weight)
-    )
-    project_mine = project_mine.T.astype(bf16)
-    project_mine = relative(jnp.stack([project_mine, swap(project_mine, "x", 2, 1)]), far)
     mod = mod.transpose(1, 0, 2).reshape(frames, 6, width)
 
     units = widen_weight.shape[1]
-    feed_mine = jnp.stack([feed_wide.astype(bf16), feed_narrow.T.astype(bf16)])
+    feed_mine = jnp.stack([widen_weight.astype(bf16), narrow_weight.T.astype(bf16)])
     feed_mine = feed_mine.reshape(2, shard, 2, units // 2).transpose(2, 0, 1, 3)
     feed_mine = relative(trade(relative(feed_mine, far), "x", 2), far)
     feed_mine, attend_full, mod, tok2_two = lax.optimization_barrier(

time: 562 us -> 559 us (level)
  waiting for transfers between devices: 81.4 us -> 69.3 us
    ppermute x29, waiting for transfers between devices: 51.5 us -> 41.7 us  [swap(): lax.ppermute(value, axis, [(place, place ^ step) for place in range(size)])]
    all_to_all x1, waiting for transfers between devices: 7.96 us -> 0.01 us  [local(): lax.all_to_all(jnp.broadcast_to(cond_act[None], (clips, frames, width)),...]
    all_to_all x1, waiting for transfers between devices: 14.4 us -> 20.5 us  [local(): lax.all_to_all(mod_mine.reshape(devices, frames, part), both, 0, 0, tiled...]
  transfers between devices with their start and end apart: 38 -> 38, of which waited for: 13 -> 11; matrix products, arithmetic and copies ran while one was open for 10% -> 11% of each run, Pallas kernels for 58% -> 59%
where the time goes in v12:
time: 559 us; the launch traced here: 550 us
  Pallas kernels  322 us (58%)
  waiting for transfers between devices  69.3 us (12%)
  starting transfers between devices  55.5 us (10%)
  other arithmetic  42.4 us (8%)
  local copies, waits for them, and re-layouts  35.8 us (6%)
  between operations  21.8 us (4%)
    pallas_call x2, Pallas kernels, attend_back(): pl.pallas_call(functools.partial(attend_back_kernel, heads, last), grid=(...  99.4 us
    pallas_call x2, Pallas kernels, attend(): pl.pallas_call(functools.partial(attend_kernel, heads), grid=(count // bl...  54.9 us
    pallas_call x4, Pallas kernels, feed_forward(): pl.pallas_call(feed_kernel, grid=(units // block,), in_specs=[spec, flat,...  54.3 us
    ppermute x29, waiting for transfers between devices, swap(): lax.ppermute(value, axis, [(place, place ^ step) for place in range(size)])  41.7 us
    pallas_call x2, Pallas kernels, first_back(): pl.pallas_call(functools.partial(first_back_kernel, last), grid=(4,), in_...  27.8 us
    ppermute x29, starting transfers between devices, swap(): lax.ppermute(value, axis, [(place, place ^ step) for place in range(size)])  24.9 us
    pallas_call x1, Pallas kernels, feed_weights(): pl.pallas_call(functools.partial(feed_weight_kernel, len(hidden)), grid=(...  21 us
    all_to_all x1, waiting for transfers between devices, local(): lax.all_to_all(mod_mine.reshape(devices, frames, part), both, 0, 0, tiled...  20.5 us
  transfers between devices with their start and end apart: 38, of which 11 were waited for; matrix products, arithmetic and copies ran while one was open for 11% of the time, Pallas kernels for 59%

profile of v12, /device:TPU:0, one launch (start us, length us, event | category | flops | bytes accessed | tf_op | source)
XLA Modules:
  0.0 549.8 jit_solution(8713670873135313907)
XLA Ops:
  18.0 5.8 %all-to-all-start = ((bf16[8,12,1024]{2,1,0:T(8,128)(2,1)}), bf16[8,12,1024]{2,1,0:T(8,128)(2,1)S(1)}, u32[]{:S(2)}, u32[]{:S(2)}) async-start(bf16[8,12,1024]{2,1,0:T(8,128)(2,1)} %broadcast_in_dim.34), calls=%async_computation | async-start | bytes 524288 | tf_op jit(solution)/shard_map/all_to_all | solution.py:875
  33.4 6.4 %collective-permute-done.1 = bf16[2,32,2048]{2,1,0:T(8,128)(2,1)S(1)} collective-permute-done((bf16[2,32,2048]{2,1,0:T(8,128)(2,1)S(1)}, bf16[2,32,2048]{2,1,0:T(8,128)(2,1)S(1)}, u32[]{:S(2)}, u32[]{:S(2)}) %collective-permute-start.1) | collective-permute-done | bytes 262176 | tf_op jit(solution)/shard_map/ppermute | solution.py:775
  46.9 5.1 all-to-all-start.1
  55.3 20.5 %all-to-all-done.1 = f32[32,12,192]{2,1,0:T(8,128)} async-done(((f32[32,12,192]{2,1,0:T(8,128)}), f32[32,12,192]{2,1,0:T(8,128)}, u32[]{:S(2)}, u32[]{:S(2)}) %all-to-all-start.1) | async-done | bytes 294944 | tf_op jit(solution)/shard_map/all_to_all | solution.py:887
  83.1 2.6 collective-permute-done.9
  89.9 9.5 %shard_map.488.k1.v1.q_ref = bf16[768,1536]{1,0:T(8,128)(2,1)} custom-call(bf16[784,1024]{1,0:T(8,128)(2,1)} %copy-done.1, bf16[784,1024]{1,0:T(8,128)(2,1)} %copy-done.1, bf16[784,1024]{1,0:T(8,128)(2,1)} %copy-done.4, bf16[784,1024]{1,0:T(8,128)(2,1)} %copy-done.4, f32[12,6,1024]{2,1,0:T(8,128)} %reshape.441.mod, bf16[768,1024]{1,0:T(8,128)(2,1)} %bitcast.188, ...), custom_call_target="tpu_custom_call" | custom-call | flops 2415919104 | bytes 6291456 | tf_op jit(solution)/shard_map/pallas_call | solution.py:131
  100.6 5.1 all-to-all-start.2
  107.8 9.2 %shard_map.487.q_ref.k2.v2 = bf16[768,1536]{1,0:T(8,128)(2,1)} custom-call(bf16[384,1024]{1,0:T(8,128)(2,1)} %collective-permute-done.5.one, bf16[400,1024]{1,0:T(8,128)(2,1)} %collective-permute-done.6.two, bf16[384,1024]{1,0:T(8,128)(2,1)} %collective-permute-done.7.three, bf16[400,1024]{1,0:T(8,128)(2,1)} %copy-done.53, f32[12,6,1024]{2,1,0:T(8,128)} %reshape.441.mod, ...), custom_call_target="tpu_custom_call" | custom-call | flops 2415919104 | bytes 6291456 | tf_op jit(solution)/shard_map/pallas_call | solution.py:131
  117.0 27.5 %shard_map.489 = (bf16[2,256,768]{2,1,0:T(8,128)(2,1)}, f32[4,1536]{1,0:T(4,128)}) custom-call(bf16[768,1536]{1,0:T(8,128)(2,1)} %shard_map.487.q_ref.k2.v2, bf16[768,1536]{1,0:T(8,128)(2,1)} %shard_map.488.k1.v1.q_ref, bf16[768,1536]{1,0:T(8,128)(2,1)} %shard_map.487.q_ref.k2.v2, bf16[768,1536]{1,0:T(8,128)(2,1)} %shard_map.488.k1.v1.q_ref, ...), custom_call_target="tpu_custom_call" | custom-call | flops 19327352832 | bytes 3145728 | tf_op jit(solution)/shard_map/pallas_call | solution.py:186
  144.5 5.1 all-to-all-done.2.mine
  153.8 27.4 %shard_map.490 = (bf16[2,256,768]{2,1,0:T(8,128)(2,1)}, f32[4,1536]{1,0:T(4,128)}) custom-call(bf16[768,1536]{1,0:T(8,128)(2,1)} %shard_map.488.k1.v1.q_ref, bf16[768,1536]{1,0:T(8,128)(2,1)} %shard_map.488.k1.v1.q_ref, bf16[768,1536]{1,0:T(8,128)(2,1)} %shard_map.487.q_ref.k2.v2, bf16[768,1536]{1,0:T(8,128)(2,1)} %shard_map.488.k1.v1.q_ref, ...), custom_call_target="tpu_custom_call" | custom-call | flops 19327352832 | bytes 3145728 | tf_op jit(solution)/shard_map/pallas_call | solution.py:186
  184.8 10.2 %shard_map.491 = (f32[12,64,1024]{2,1,0:T(8,128)}, bf16[384,1024]{1,0:T(8,128)(2,1)}, bf16[384,1024]{1,0:T(8,128)(2,1)}, bf16[768,1024]{1,0:T(8,128)(2,1)}, bf16...) custom-call(s32[5]{0:T(128)} %pad_add_fusion.order, bf16[2,256,768]{2,1,0:T(8,128)(2,1)} %get-tuple-element.147.a0.out_ref, ...), custom_call_target="tpu_custom_call" | custom-call | flops 1610612736 | bytes 11010048 | tf_op jit(solution)/shard_map/pallas_call | solution.py:401
  196.6 13.8 %shard_map.492 = (f32[384,1024]{1,0:T(8,128)}, f32[384,1024]{1,0:T(8,128)}, bf16[384,2048]{1,0:T(8,128)(2,1)}, bf16[384,2048]{1,0:T(8,128)(2,1)}, f32[6,1,1024]{2,1,0:T(1,128)}) custom-call(bf16[16,2,2,32,2048]{4,3,2,1,0:T(8,128)(2,1)} %bitcast.203, bf16[384,1024]{1,0:T(8,128)(2,1)} %get-tuple-element.151.hidden.refs_0_, ...), custom_call_target="tpu_custom_call" | custom-call | flops 6442450944 | bytes 11534336 | tf_op jit(solution)/shard_map/pallas_call | solution.py:498
  211.0 13.7 %shard_map.493 = (f32[384,1024]{1,0:T(8,128)}, f32[384,1024]{1,0:T(8,128)}, bf16[384,2048]{1,0:T(8,128)(2,1)}, bf16[384,2048]{1,0:T(8,128)(2,1)}, f32[6,1,1024]{2,1,0:T(1,128)}) custom-call(bf16[16,2,2,32,2048]{4,3,2,1,0:T(8,128)(2,1)} %bitcast.204, bf16[384,1024]{1,0:T(8,128)(2,1)} %get-tuple-element.159.hidden.refs_1_, ...), custom_call_target="tpu_custom_call" | custom-call | flops 6442450944 | bytes 11534336 | tf_op jit(solution)/shard_map/pallas_call | solution.py:498
  225.6 13.2 %shard_map.494 = (bf16[384,1024]{1,0:T(8,128)(2,1)}, bf16[384,1024]{1,0:T(8,128)(2,1)}, bf16[384,2048]{1,0:T(8,128)(2,1)}, bf16[384,2048]{1,0:T(8,128)(2,1)}, f32[6,1,1024]{2,1,0:T(1,128)}) custom-call(bf16[16,2,2,32,2048]{4,3,2,1,0:T(8,128)(2,1)} %bitcast.205, bf16[384,1024]{1,0:T(8,128)(2,1)} %copy-done.55, ...), custom_call_target="tpu_custom_call" | custom-call | flops 6442450944 | bytes 11534336 | tf_op jit(solution)/shard_map/pallas_call | solution.py:498
  241.3 13.6 %shard_map.495 = (bf16[384,1024]{1,0:T(8,128)(2,1)}, bf16[384,1024]{1,0:T(8,128)(2,1)}, bf16[384,2048]{1,0:T(8,128)(2,1)}, bf16[384,2048]{1,0:T(8,128)(2,1)}, f32[6,1,1024]{2,1,0:T(1,128)}) custom-call(bf16[16,2,2,32,2048]{4,3,2,1,0:T(8,128)(2,1)} %bitcast.206, bf16[384,1024]{1,0:T(8,128)(2,1)} %copy-done.56, ...), custom_call_target="tpu_custom_call" | custom-call | flops 6442450944 | bytes 11534336 | tf_op jit(solution)/shard_map/pallas_call | solution.py:498
  255.4 21.0 %shard_map.496 = bf16[16,2,2,32,2048]{4,3,2,1,0:T(8,128)(2,1)} custom-call(bf16[384,1024]{1,0:T(8,128)(2,1)} %get-tuple-element.151.hidden.refs_0_, bf16[384,1024]{1,0:T(8,128)(2,1)} %get-tuple-element.159.hidden.refs_1_, bf16[384,1024]{1,0:T(8,128)(2,1)} %copy-done.55, bf16[384,1024]{1,0:T(8,128)(2,1)} %copy-done.56, ...), custom_call_target="tpu_custom_call" | custom-call | flops 12884901888 | bytes 20971520 | tf_op jit(solution)/shard_map/pallas_call | solution.py:549
  277.6 17.6 %shard_map.497 = (f32[12,64,1024]{2,1,0:T(8,128)}, f32[12,3,1024]{2,1,0:T(4,128)}, bf16[256,768]{1,0:T(8,128)(2,1)}, bf16[256,768]{1,0:T(8,128)(2,1)}, bf16[256,...) custom-call(s32[5]{0:T(128)} %pad_add_fusion.order, f32[384,1024]{1,0:T(8,128)} %get-tuple-element.153.into1, ...), custom_call_target="tpu_custom_call" | custom-call | flops 3221225472 | bytes 18874368 | tf_op jit(solution)/shard_map/pallas_call | solution.py:612
  296.3 3.8 all-to-all-start.3
  301.9 48.4 %shard_map.498 = (bf16[256,1536]{1,0:T(8,128)(2,1)}, f32[256,3072]{1,0:T(8,128)}, f32[256,3072]{1,0:T(8,128)}) custom-call(bf16[768,1536]{1,0:T(8,128)(2,1)} %shard_map.488.k1.v1.q_ref, bf16[768,1536]{1,0:T(8,128)(2,1)} %shard_map.488.k1.v1.q_ref, bf16[768,1536]{1,0:T(8,128)(2,1)} %shard_map.487.q_ref.k2.v2, bf16[768,1536]{1,0:T(8,128)(2,1)} %shard_map.488.k1.v1.q_ref, ...), custom_call_target="tpu_custom_call" | custom-call | flops 41070624768 | bytes 6291456 | tf_op jit(solution)/shard_map/pallas_call | solution.py:332
  352.5 51.0 %shard_map.499 = (bf16[256,1536]{1,0:T(8,128)(2,1)}, bf16[256,3072]{1,0:T(8,128)(2,1)}, bf16[256,3072]{1,0:T(8,128)(2,1)}) custom-call(bf16[768,1536]{1,0:T(8,128)(2,1)} %shard_map.487.q_ref.k2.v2, bf16[768,1536]{1,0:T(8,128)(2,1)} %shard_map.488.k1.v1.q_ref, bf16[768,1536]{1,0:T(8,128)(2,1)} %shard_map.487.q_ref.k2.v2, ...), custom_call_target="tpu_custom_call" | custom-call | flops 41070624768 | bytes 6291456 | tf_op jit(solution)/shard_map/pallas_call | solution.py:332
  403.5 13.2 %shard_map.500 = (bf16[2,768,1024]{2,1,0:T(8,128)(2,1)}, f32[768,1024]{1,0:T(8,128)}, f32[12,2,1024]{2,1,0:T(2,128)}) custom-call(bf16[384,1024]{1,0:T(8,128)(2,1)} %collective-permute-done.5.one, bf16[400,1024]{1,0:T(8,128)(2,1)} %collective-permute-done.6.two, bf16[384,1024]{1,0:T(8,128)(2,1)} %collective-permute-done.7.three, ...), custom_call_target="tpu_custom_call" | custom-call | flops 4831838208 | bytes 9437184 | tf_op jit(solution)/shard_map/pallas_call | solution.py:716
  418.6 3.3 collective-permute-done.24
  425.3 14.6 %shard_map.501 = (bf16[2,768,1024]{2,1,0:T(8,128)(2,1)}, bf16[1024,768]{1,0:T(8,128)(2,1)}, f32[12,2,1024]{2,1,0:T(2,128)}) custom-call(bf16[784,1024]{1,0:T(8,128)(2,1)} %copy-done.1, bf16[784,1024]{1,0:T(8,128)(2,1)} %copy-done.1, bf16[784,1024]{1,0:T(8,128)(2,1)} %copy-done.4, bf16[784,1024]{1,0:T(8,128)(2,1)} %copy-done.4, f32[12,6,1024]{2,1,0:T(8,128)} %reshape.441.mod, ...), custom_call_target="tpu_custom_call" | custom-call | flops 4831838208 | bytes 9437184 | tf_op jit(solution)/shard_map/pallas_call | solution.py:716
  445.1 5.8 %all-to-all-start.4 = ((bf16[32,38,768]{2,1,0:T(8,128)(2,1)}), bf16[32,38,768]{2,1,0:T(8,128)(2,1)S(1)}, u32[]{:S(2)}, u32[]{:S(2)}) async-start(bf16[32,38,768]{2,1,0:T(8,128)(2,1)} %pad_maximum_fusion), calls=%async_computation.5 | async-start | bytes 3932160 | tf_op jit(solution)/shard_map/all_to_all | solution.py:1035
  453.5 5.3 shard_map.502
  465.5 11.3 %collective-permute-done.28 = bf16[2,32,2048]{2,1,0:T(8,128)(2,1)S(1)} collective-permute-done((bf16[2,32,2048]{2,1,0:T(8,128)(2,1)S(1)}, bf16[2,32,2048]{2,1,0:T(8,128)(2,1)S(1)}, u32[]{:S(2)}, u32[]{:S(2)}) %collective-permute-start.28) | collective-permute-done | bytes 262176 | tf_op jit(solution)/shard_map/ppermute | solution.py:775
  482.5 15.3 %collective-permute-done.26.far2 = bf16[384,1024]{1,0:T(8,128)(2,1)} collective-permute-done((bf16[384,1024]{1,0:T(8,128)(2,1)S(1)}, bf16[384,1024]{1,0:T(8,128)(2,1)}, u32[]{:S(2)}, u32[]{:S(2)}) %collective-permute-start.26) | collective-permute-done | bytes 786464 | tf_op jit(solution)/shard_map/ppermute | solution.py:775
  499.1 2.6 reshape.462
  506.3 2.6 shard_map.505
  514.5 4.6 all-to-all-start.5
  519.1 7.9 %shard_map.504 = f32[12,64,1024]{2,1,0:T(8,128)} custom-call(bf16[12,64,1024]{2,1,0:T(8,128)(2,1)} %bitcast.157, f32[12,6,1024]{2,1,0:T(8,128)} %reshape.441.mod, f32[12,64,1024]{2,1,0:T(8,128)} %get-tuple-element.220.middle_grad, bf16[2,768,1024]{2,1,0:T(8,128)(2,1)} %get-tuple-element.221.one, bf16[768,1024]{1,0:T(8,128)(2,1)} %collective-permute-done.27.two, ...), custom_call_target="tpu_custom_call" | custom-call | flops 15728640 | bytes 12582912 | tf_op jit(solution)/shard_map/pallas_call | solution.py:746
  (317 shorter events, 110.8 us)
Async XLA Ops:
  10.1 15.3 %collective-permute-start.4 = (bf16[32,768]{1,0:T(8,128)(2,1)}, bf16[32,768]{1,0:T(8,128)(2,1)}, u32[]{:S(2)}, u32[]{:S(2)}) collective-permute-start(bf16[32,768]{1,0:T(8,128)(2,1)} %get-tuple-element.291), channel_id=1, source_target_pairs={{0,3},{1,2},{2,1},{3,0},{4,7},{5,6},{6,5},{7,4},{8,11},{9,10},{10,... | collective-permute-start | bytes 147464 | tf_op jit(solution)/shard_map/ppermute | solution.py:775
  12.5 12.9 %collective-permute-start.3 = (bf16[32,768]{1,0:T(8,128)(2,1)}, bf16[32,768]{1,0:T(8,128)(2,1)}, u32[]{:S(2)}, u32[]{:S(2)}) collective-permute-start(bf16[32,768]{1,0:T(8,128)(2,1)} %get-tuple-element.292), channel_id=1, source_target_pairs={{0,2},{1,3},{2,0},{3,1},{4,6},{5,7},{6,4},{7,5},{8,10},{9,11},{10,... | collective-permute-start | bytes 147464 | tf_op jit(solution)/shard_map/ppermute | solution.py:775
  13.1 12.3 %collective-permute-start.2 = (bf16[32,768]{1,0:T(8,128)(2,1)S(1)}, bf16[32,768]{1,0:T(8,128)(2,1)}, u32[]{:S(2)}, u32[]{:S(2)}) collective-permute-start(bf16[32,768]{1,0:T(8,128)(2,1)S(1)} %get-tuple-element.293), channel_id=1, source_target_pairs={{0,1},{1,0},{2,3},{3,2},{4,5},{5,4},{6,7},{7,6},{8,9},{9,8},{10,11... | collective-permute-start | bytes 147464 | tf_op jit(solution)/shard_map/ppermute | solution.py:775
  14.1 27.7 %collective-permute-start.5 = (bf16[384,1024]{1,0:T(8,128)(2,1)}, bf16[384,1024]{1,0:T(8,128)(2,1)}, u32[]{:S(2)}, u32[]{:S(2)}) collective-permute-start(bf16[384,1024]{1,0:T(8,128)(2,1)} %bitcast.34), channel_id=1, source_target_pairs={{0,2},{2,0},{1,3},{3,1},{4,6},{6,4},{5,7},{7,5},{8,10},{10,8},{9,1... | collective-permute-start | bytes 2359304 | tf_op jit(solution)/shard_map/ppermute | solution.py:775
  18.0 22.2 %all-to-all-start = ((bf16[8,12,1024]{2,1,0:T(8,128)(2,1)}), bf16[8,12,1024]{2,1,0:T(8,128)(2,1)S(1)}, u32[]{:S(2)}, u32[]{:S(2)}) async-start(bf16[8,12,1024]{2,1,0:T(8,128)(2,1)} %broadcast_in_dim.34), calls=%async_computation | async-start | bytes 524288 | tf_op jit(solution)/shard_map/all_to_all | solution.py:875
  23.8 56.0 %all-gather.3.cloned.1.call-start = ((), (), s32[]{:S(2)}) async-start(), calls=%async_computation.7 | async-start | bytes 1769472 | tf_op jit(solution)/shard_map/all_gather | solution.py:872
  31.9 8.0 %collective-permute-start.1 = (bf16[2,32,2048]{2,1,0:T(8,128)(2,1)S(1)}, bf16[2,32,2048]{2,1,0:T(8,128)(2,1)S(1)}, u32[]{:S(2)}, u32[]{:S(2)}) collective-permute-start(bf16[2,32,2048]{2,1,0:T(8,128)(2,1)S(1)} %bitcast.199), channel_id=1, source_target_pairs={{0,2},{2,0},{1,3},{3,1},{4,6},{6,4},{5,7},{7,5},{8,10},{10,8},{9,1... | collective-permute-start | bytes 786440 | tf_op jit(solution)/shard_map/ppermute | solution.py:775
  41.8 36.3 %collective-permute-start.6 = (bf16[400,1024]{1,0:T(8,128)(2,1)}, bf16[400,1024]{1,0:T(8,128)(2,1)}, u32[]{:S(2)}, u32[]{:S(2)}) collective-permute-start(bf16[400,1024]{1,0:T(8,128)(2,1)} %slice.200), channel_id=1, source_target_pairs={{0,2},{2,0},{1,3},{3,1},{4,6},{6,4},{5,7},{7,5},{8,10},{10,8},{9,1... | collective-permute-start | bytes 2457608 | tf_op jit(solution)/shard_map/ppermute | solution.py:775
  46.9 28.9 %all-to-all-start.1 = ((f32[32,12,192]{2,1,0:T(8,128)}), f32[32,12,192]{2,1,0:T(8,128)}, u32[]{:S(2)}, u32[]{:S(2)}) async-start(f32[32,12,192]{2,1,0:T(8,128)} %bitcast.183), calls=%async_computation.1 | async-start | bytes 1048576 | tf_op jit(solution)/shard_map/all_to_all | solution.py:887
  52.0 144.6 %all-gather.5.cloned.1.call-start = ((), (), s32[]{:S(2)}) async-start(), calls=%async_computation.8 | async-start | bytes 8912896 | tf_op jit(solution)/shard_map/all_gather | solution.py:899
  85.8 22.0 %collective-permute-start.7 = (bf16[384,1024]{1,0:T(8,128)(2,1)}, bf16[384,1024]{1,0:T(8,128)(2,1)}, u32[]{:S(2)}, u32[]{:S(2)}) collective-permute-start(bf16[384,1024]{1,0:T(8,128)(2,1)} %collective-permute-done.5.one), channel_id=1, source_target_pairs={{0,1},{1,0},{2,3},{3,2},{4,5},{5,4},{6,7},{7,6},{8,9},{9,8},{10,11... | collective-permute-start | bytes 2359304 | tf_op jit(solution)/shard_map/ppermute | solution.py:775
  86.7 57.8 %collective-permute-start.10 = (bf16[12,64,1024]{2,1,0:T(8,128)(2,1)}, bf16[12,64,1024]{2,1,0:T(8,128)(2,1)S(1)}, u32[]{:S(2)}, u32[]{:S(2)}) collective-permute-start(bf16[12,64,1024]{2,1,0:T(8,128)(2,1)} %bitcast.161), channel_id=1, source_target_pairs={{0,2},{2,0},{1,3},{3,1},{4,6},{6,4},{5,7},{7,5},{8,10},{10,8},{9,1... | collective-permute-start | bytes 4718600 | tf_op jit(solution)/shard_map/ppermute | solution.py:775
  100.6 49.1 %all-to-all-start.2 = ((bf16[8,2,32,1024]{3,2,1,0:T(8,128)(2,1)}), bf16[8,2,32,1024]{3,2,1,0:T(8,128)(2,1)S(1)}, u32[]{:S(2)}, u32[]{:S(2)}) async-start(bf16[8,2,32,1024]{3,2,1,0:T(8,128)(2,1)} %broadcast_in_dim.39), calls=%async_computation.2 | async-start | bytes 2097152 | tf_op jit(solution)/shard_map/all_to_all | solution.py:925
  105.7 337.9 %reduce-scatter.2.cloned.1.call-start = ((), (), s32[]{:S(2)}) async-start(), calls=%async_computation.9 | async-start | bytes 8912896 | tf_op jit(solution)/shard_map/reduce_scatter | solution.py:971
  151.9 31.2 %collective-permute-start.14 = (bf16[256,768]{1,0:T(8,128)(2,1)}, bf16[256,768]{1,0:T(8,128)(2,1)S(1)}, u32[]{:S(2)}, u32[]{:S(2)}) collective-permute-start(bf16[256,768]{1,0:T(8,128)(2,1)} %get-tuple-element.266), channel_id=1, source_target_pairs={{0,3},{1,2},{2,1},{3,0},{4,7},{5,6},{6,5},{7,4},{8,11},{9,10},{10,... | collective-permute-start | bytes 1179656 | tf_op jit(solution)/shard_map/ppermute | solution.py:775
  152.6 30.5 %collective-permute-start.13 = (bf16[256,768]{1,0:T(8,128)(2,1)S(1)}, bf16[256,768]{1,0:T(8,128)(2,1)S(1)}, u32[]{:S(2)}, u32[]{:S(2)}) collective-permute-start(bf16[256,768]{1,0:T(8,128)(2,1)S(1)} %get-tuple-element.267), channel_id=1, source_target_pairs={{0,2},{1,3},{2,0},{3,1},{4,6},{5,7},{6,4},{7,5},{8,10},{9,11},{10,... | collective-permute-start | bytes 1179656 | tf_op jit(solution)/shard_map/ppermute | solution.py:775
  153.5 27.8 %collective-permute-start.11 = (bf16[8,2,32,1024]{3,2,1,0:T(8,128)(2,1)S(1)}, bf16[8,2,32,1024]{3,2,1,0:T(8,128)(2,1)}, u32[]{:S(2)}, u32[]{:S(2)}) collective-permute-start(bf16[8,2,32,1024]{3,2,1,0:T(8,128)(2,1)S(1)} %all-to-all-done.2.mine), channel_id=1, source_target_pairs={{0,1},{1,0},{2,3},{3,2},{4,5},{5,4},{6,7},{7,6},{8,9},{9,8},{10,11... | collective-permute-start | bytes 3145736 | tf_op jit(solution)/shard_map/ppermute | solution.py:775
  195.0 29.7 %collective-permute-start.15 = (bf16[384,1024]{1,0:T(8,128)(2,1)}, bf16[384,1024]{1,0:T(8,128)(2,1)S(1)}, u32[]{:S(2)}, u32[]{:S(2)}) collective-permute-start(bf16[384,1024]{1,0:T(8,128)(2,1)} %get-tuple-element.151.hidden.refs_0_), channel_id=1, source_target_pairs={{0,2},{2,0},{1,3},{3,1},{4,6},{6,4},{5,7},{7,5},{8,10},{10,8},{9,1... | collective-permute-start | bytes 2359304 | tf_op jit(solution)/shard_map/ppermute | solution.py:775
  210.4 30.0 %collective-permute-start.16 = (bf16[384,1024]{1,0:T(8,128)(2,1)S(1)}, bf16[384,1024]{1,0:T(8,128)(2,1)S(1)}, u32[]{:S(2)}, u32[]{:S(2)}) collective-permute-start(bf16[384,1024]{1,0:T(8,128)(2,1)S(1)} %copy-done.54), channel_id=1, source_target_pairs={{0,2},{2,0},{1,3},{3,1},{4,6},{6,4},{5,7},{7,5},{8,10},{10,8},{9,1... | collective-permute-start | bytes 2359304 | tf_op jit(solution)/shard_map/ppermute | solution.py:775
  238.8 37.6 %collective-permute-start.17 = (bf16[384,1024]{1,0:T(8,128)(2,1)}, bf16[384,1024]{1,0:T(8,128)(2,1)S(1)}, u32[]{:S(2)}, u32[]{:S(2)}) collective-permute-start(bf16[384,1024]{1,0:T(8,128)(2,1)} %get-tuple-element.171), channel_id=1, source_target_pairs={{0,2},{2,0},{1,3},{3,1},{4,6},{6,4},{5,7},{7,5},{8,10},{10,8},{9,1... | collective-permute-start | bytes 2359304 | tf_op jit(solution)/shard_map/ppermute | solution.py:775
  254.9 21.6 %collective-permute-start.18 = (bf16[384,1024]{1,0:T(8,128)(2,1)}, bf16[384,1024]{1,0:T(8,128)(2,1)S(1)}, u32[]{:S(2)}, u32[]{:S(2)}) collective-permute-start(bf16[384,1024]{1,0:T(8,128)(2,1)} %get-tuple-element.172), channel_id=1, source_target_pairs={{0,2},{2,0},{1,3},{3,1},{4,6},{6,4},{5,7},{7,5},{8,10},{10,8},{9,1... | collective-permute-start | bytes 2359304 | tf_op jit(solution)/shard_map/ppermute | solution.py:775
  296.3 107.2 %all-to-all-start.3 = ((bf16[32,32,1024]{2,1,0:T(8,128)(2,1)}), bf16[32,32,1024]{2,1,0:T(8,128)(2,1)}, u32[]{:S(2)}, u32[]{:S(2)}) async-start(bf16[32,32,1024]{2,1,0:T(8,128)(2,1)} %bitcast.184), calls=%async_computation.3 | async-start | bytes 4194304 | tf_op jit(solution)/shard_map/all_to_all | solution.py:982
  300.1 50.3 %collective-permute-start.20 = (bf16[256,768]{1,0:T(8,128)(2,1)S(1)}, bf16[256,768]{1,0:T(8,128)(2,1)}, u32[]{:S(2)}, u32[]{:S(2)}) collective-permute-start(bf16[256,768]{1,0:T(8,128)(2,1)S(1)} %copy-done.58), channel_id=1, source_target_pairs={{0,2},{1,3},{2,0},{3,1},{4,6},{5,7},{6,4},{7,5},{8,10},{9,11},{10,... | collective-permute-start | bytes 1179656 | tf_op jit(solution)/shard_map/ppermute | solution.py:775
  301.9 48.5 %collective-permute-start.21 = (bf16[256,768]{1,0:T(8,128)(2,1)S(1)}, bf16[256,768]{1,0:T(8,128)(2,1)}, u32[]{:S(2)}, u32[]{:S(2)}) collective-permute-start(bf16[256,768]{1,0:T(8,128)(2,1)S(1)} %copy-done.57), channel_id=1, source_target_pairs={{0,3},{1,2},{2,1},{3,0},{4,7},{5,6},{6,5},{7,4},{8,11},{9,10},{10,... | collective-permute-start | bytes 1179656 | tf_op jit(solution)/shard_map/ppermute | solution.py:775
  350.4 53.1 %collective-permute-start.22 = (bf16[384,1024]{1,0:T(8,128)(2,1)}, bf16[384,1024]{1,0:T(8,128)(2,1)S(1)}, u32[]{:S(2)}, u32[]{:S(2)}) collective-permute-start(bf16[384,1024]{1,0:T(8,128)(2,1)} %get-tuple-element.192), channel_id=1, source_target_pairs={{0,2},{2,0},{1,3},{3,1},{4,6},{6,4},{5,7},{7,5},{8,10},{10,8},{9,1... | collective-permute-start | bytes 2359304 | tf_op jit(solution)/shard_map/ppermute | solution.py:775
  351.9 51.6 %collective-permute-start.23 = (bf16[384,1024]{1,0:T(8,128)(2,1)}, bf16[384,1024]{1,0:T(8,128)(2,1)}, u32[]{:S(2)}, u32[]{:S(2)}) collective-permute-start(bf16[384,1024]{1,0:T(8,128)(2,1)} %get-tuple-element.193), channel_id=1, source_target_pairs={{0,2},{2,0},{1,3},{3,1},{4,6},{6,4},{5,7},{7,5},{8,10},{10,8},{9,1... | collective-permute-start | bytes 2359304 | tf_op jit(solution)/shard_map/ppermute | solution.py:775
  423.8 19.8 %collective-permute-start.25 = (bf16[384,1024]{1,0:T(8,128)(2,1)}, bf16[384,1024]{1,0:T(8,128)(2,1)S(1)}, u32[]{:S(2)}, u32[]{:S(2)}) collective-permute-start(bf16[384,1024]{1,0:T(8,128)(2,1)} %get-tuple-element.203), channel_id=1, source_target_pairs={{0,2},{2,0},{1,3},{3,1},{4,6},{6,4},{5,7},{7,5},{8,10},{10,8},{9,1... | collective-permute-start | bytes 2359304 | tf_op jit(solution)/shard_map/ppermute | solution.py:775
  445.1 52.7 %all-to-all-start.4 = ((bf16[32,38,768]{2,1,0:T(8,128)(2,1)}), bf16[32,38,768]{2,1,0:T(8,128)(2,1)S(1)}, u32[]{:S(2)}, u32[]{:S(2)}) async-start(bf16[32,38,768]{2,1,0:T(8,128)(2,1)} %pad_maximum_fusion), calls=%async_computation.5 | async-start | bytes 3932160 | tf_op jit(solution)/shard_map/all_to_all | solution.py:1035
  462.1 14.8 %collective-permute-start.28 = (bf16[2,32,2048]{2,1,0:T(8,128)(2,1)S(1)}, bf16[2,32,2048]{2,1,0:T(8,128)(2,1)S(1)}, u32[]{:S(2)}, u32[]{:S(2)}) collective-permute-start(bf16[2,32,2048]{2,1,0:T(8,128)(2,1)S(1)} %bitcast.197), channel_id=1, source_target_pairs={{0,2},{2,0},{1,3},{3,1},{4,6},{6,4},{5,7},{7,5},{8,10},{10,8},{9,1... | collective-permute-start | bytes 786440 | tf_op jit(solution)/shard_map/ppermute | solution.py:775
  465.3 53.8 %collective-permute-start.27 = (bf16[768,1024]{1,0:T(8,128)(2,1)}, bf16[768,1024]{1,0:T(8,128)(2,1)}, u32[]{:S(2)}, u32[]{:S(2)}) collective-permute-start(bf16[768,1024]{1,0:T(8,128)(2,1)} %slice_bitcast_fusion), channel_id=1, source_target_pairs={{0,1},{1,0},{2,3},{3,2},{4,5},{5,4},{6,7},{7,6},{8,9},{9,8},{10,11... | collective-permute-start | bytes 4718600 | tf_op jit(solution)/shard_map/ppermute | solution.py:775
  465.3 32.5 %collective-permute-start.26 = (bf16[384,1024]{1,0:T(8,128)(2,1)S(1)}, bf16[384,1024]{1,0:T(8,128)(2,1)}, u32[]{:S(2)}, u32[]{:S(2)}) collective-permute-start(bf16[384,1024]{1,0:T(8,128)(2,1)S(1)} %copy-done.31), channel_id=1, source_target_pairs={{0,2},{2,0},{1,3},{3,1},{4,6},{6,4},{5,7},{7,5},{8,10},{10,8},{9,1... | collective-permute-start | bytes 2359304 | tf_op jit(solution)/shard_map/ppermute | solution.py:775
  514.5 12.8 %all-to-all-start.5 = ((f32[32,8,128]{2,1,0:T(8,128)}), f32[32,8,128]{2,1,0:T(8,128)S(1)}, u32[]{:S(2)}, u32[]{:S(2)}) async-start(f32[32,8,128]{2,1,0:T(8,128)} %broadcast_in_dim.40), calls=%async_computation.6 | async-start | bytes 262144 | tf_op jit(solution)/shard_map/all_to_all | solution.py:1059
  (65 other events, 453.8 us)
Sparse Core Ops, SparseCore 0:
  27.8 51.9 all-gather.2
  82.5 88.0 all-gather.4
  276.6 139.0 reduce-scatter.1

commit v13 on v12

--- a/solution.py
+++ b/solution.py
@@ -84,14 +84,29 @@
     return jnp.concatenate(out, axis=0)
 
 
-def hold_piece(pieces, held):
-    for index, piece in enumerate(pieces):
-
-        @pl.when(pl.program_id(0) == index)
-        def _(piece=piece):
-            held[...] = piece[...]
-
-    return held[...].astype(f32)
+def hold_piece(places, pieces, held, arrived):
+    rows = held.shape[1]
+
+    def copy(index):
+        source = pieces[index].at[pl.ds(places[index] * rows, rows)]
+        return pltpu.make_async_copy(source, held.at[index % 2], arrived.at[index % 2])
+
+    step = pl.program_id(0)
+    for index in range(len(pieces)):
+
+        @pl.when(step == index)
+        def _(index=index):
+            if index == 0:
+                copy(0).start()
+            if index + 1 < len(pieces):
+                copy(index + 1).start()
+            copy(index).wait()
+
+    return held[lax.rem(step, 2)].astype(f32)
+
+
+def hold_scratch(block, width):
+    return [VMEM((2, block, width), bf16), pltpu.SemaphoreType.DMA((2,))]
 
 
 def modulated(values, mod):
@@ -101,8 +116,9 @@
     return normed, hidden.astype(bf16).reshape(count, width)
 
 
-def qkv_kernel(one, two, three, four, mod, weight, cosine, sine, out, held):
-    _, hidden = modulated(hold_piece((one, two, three, four), held), mod)
+def qkv_kernel(places, *refs):
+    pieces, (mod, weight, cosine, sine, out, held, arrived) = refs[: len(places)], refs[len(places) :]
+    _, hidden = modulated(hold_piece(places, pieces, held, arrived), mod)
     projected = dot(weight[...], hidden, NT)
     third = projected.shape[0] // 3
     cos, sin = cosine[...], sine[...]
@@ -114,33 +130,30 @@
 
 
 def token_specs(pieces, frames, block, width):
-    def piece_spec(index):
-        return pl.BlockSpec((block, width), lambda i: (index, 0))
-
-    return [piece_spec(index) for _, index in pieces] + [
+    return [whole(pl.ANY)] * len(pieces) + [
         pl.BlockSpec((frames // 2, 6, width), lambda i: (lax.rem(i, 2), 0, 0))
     ]
 
 
 def project_qkv(pieces, mod, weight, cosine, sine):
     total, width = cosine.shape[1], weight.shape[1]
-    block = total // 4
+    block = total // len(pieces)
     specs = token_specs(pieces, mod.shape[0], block, width)
     rows = weight.shape[0]
     angle = pl.BlockSpec((cosine.shape[0], block), lambda i: (0, i))
     return pl.pallas_call(
-        qkv_kernel,
-        grid=(4,),
+        functools.partial(qkv_kernel, [place for _, place in pieces]),
+        grid=(len(pieces),),
         in_specs=specs + [whole(), angle, angle],
         out_specs=pl.BlockSpec((rows, block), lambda i: (0, i)),
         out_shape=jax.ShapeDtypeStruct((rows, total), bf16),
-        scratch_shapes=[VMEM((block, width), bf16)],
+        scratch_shapes=hold_scratch(block, width),
         compiler_params=params(),
         cost_estimate=cost(2 * rows * total * width, 4 * total * width),
     )(*[piece for piece, _ in pieces], mod, weight, cosine, sine)
 
 
-def attend_kernel(heads, q_ref, k1, k2, v1, v2, bias, out, lse, k_wide, v_wide):
+def attend_kernel(heads, q_ref, k_ref, v_ref, bias, out, lse, k_wide, v_wide):
     total = bias.shape[1]
     block = q_ref.shape[1]
 
@@ -148,8 +161,7 @@
     def _():
         for head in range(heads):
             rows = slice(head * HEAD_DIM, (head + 1) * HEAD_DIM)
-            keys = jnp.concatenate([k1[rows, :], k2[rows, :]], axis=1)
-            vals = jnp.concatenate([v1[rows, :], v2[rows, :]], axis=1)
+            keys, vals = k_ref[rows, :], v_ref[rows, :]
             wide = jnp.concatenate([keys, keys, bias[...].astype(bf16), jnp.zeros((127, total), bf16)], axis=0)
             k_wide[head] = jnp.transpose(wide)
             v_wide[head] = jnp.concatenate([vals, jnp.ones((HEAD_DIM, total), bf16)], axis=0)
@@ -174,23 +186,21 @@
         logits = later
 
 
-def attend(queries, ours, theirs, bias):
-    rows, count = queries.shape[0] // 3, queries.shape[1]
-    total = bias.shape[1]
+def attend(qkv, part, bias):
+    rows, total = qkv.shape[0] // 3, qkv.shape[1]
+    count = total // 2
     heads = rows // HEAD_DIM
     block = count // 2
 
     def piece(index):
-        return pl.BlockSpec((rows, count), lambda i: (index, 0))
+        return pl.BlockSpec((rows, total), lambda i: (index, 0))
 
     return pl.pallas_call(
         functools.partial(attend_kernel, heads),
         grid=(count // block,),
         in_specs=[
-            pl.BlockSpec((rows, block), lambda i: (0, i)),
+            pl.BlockSpec((rows, block), lambda i: (0, i + 2 * part)),
             piece(1),
-            piece(1),
-            piece(2),
             piece(2),
             pl.BlockSpec((1, total), lambda i: (0, 0)),
         ],
@@ -208,11 +218,11 @@
         ],
         compiler_params=params(),
         cost_estimate=cost(16 * total * count * rows, 4 * rows * total, heads * count * total),
-    )(queries, ours, theirs, ours, theirs, bias)
+    )(qkv, qkv, qkv, bias)
 
 
 def attend_back_kernel(
-    heads, last, q_ref, k1, k2, v1, v2, bias, out_ref, grad1, grad2, lse, cosine, sine, cos_all, sin_all,
+    heads, last, q_ref, k_ref, v_ref, bias, out_ref, grad1, grad2, lse, cosine, sine, cos_all, sin_all,
     *rest,
 ):
     if last:
@@ -230,8 +240,7 @@
     def _():
         for head in range(heads):
             rows = slice(head * HEAD_DIM, (head + 1) * HEAD_DIM)
-            keys = jnp.concatenate([k1[rows, :], k2[rows, :]], axis=1)
-            vals = jnp.concatenate([v1[rows, :], v2[rows, :]], axis=1)
+            keys, vals = k_ref[rows, :], v_ref[rows, :]
             k_wide[head] = jnp.concatenate(
                 [keys, keys, bias[...].astype(bf16), jnp.ones((15, total), bf16), jnp.zeros((112, total), bf16)],
                 axis=0,
@@ -286,9 +295,9 @@
             dv[...] = dv_sum[...].astype(bf16)
 
 
-def attend_back(queries, ours, theirs, bias, out, grads, lse, angles, offset, sums=None):
-    rows, count = queries.shape[0] // 3, queries.shape[1]
-    total = bias.shape[1]
+def attend_back(qkv, bias, out, grads, lse, angles, offset, sums=None):
+    rows, total = qkv.shape[0] // 3, qkv.shape[1]
+    count = total // 2
     heads = rows // HEAD_DIM
     block = 256 if count % 256 == 0 else 128
     steps = count // block
@@ -297,16 +306,14 @@
     cosine, sine = angles
 
     def piece(index):
-        return pl.BlockSpec((rows, count), lambda i: (index, 0))
+        return pl.BlockSpec((rows, total), lambda i: (index, 0))
 
     moving = pl.BlockSpec((rows, block), lambda i: (0, i))
     fixed = pl.BlockSpec((rows, total), lambda i: (0, 0))
     angle = pl.BlockSpec((cosine.shape[0], block), lambda i: (0, i + offset * steps))
     in_specs = [
-        moving,
+        pl.BlockSpec((rows, block), lambda i: (0, i + offset * steps)),
         piece(1),
-        piece(1),
-        piece(2),
         piece(2),
         pl.BlockSpec((1, total), lambda i: (0, 0)),
         pl.BlockSpec((1, rows, block), lambda i: (i // half, 0, lax.rem(i, half))),
@@ -318,7 +325,7 @@
         whole(),
         whole(),
     ]
-    operands = [queries, ours, theirs, ours, theirs, bias, out, *grads, lse, cosine, sine, cosine, sine]
+    operands = [qkv, qkv, qkv, bias, out, *grads, lse, cosine, sine, cosine, sine]
     kind = f32
     scratch = [
         VMEM((heads, 256, total), bf16),
@@ -661,11 +668,12 @@
     )(*parts, tokens, att_out, mod)
 
 
-def first_back_kernel(last, one, two, three, four, mod, dq, dk, dv, weight, *rest):
+def first_back_kernel(last, places, *refs):
+    pieces, (mod, dq, dk, dv, weight, *rest) = refs[: len(places)], refs[len(places) :]
     if last:
-        raw_in, mod_in, grads, raw, mod_grad, total, held = rest
+        raw_in, mod_in, grads, raw, mod_grad, total, held, arrived = rest
     else:
-        grads, total, mod_grad, held = rest
+        grads, total, mod_grad, held, arrived = rest
     step = pl.program_id(0)
     chunk = mod.shape[0]
 
@@ -674,7 +682,7 @@
         total[...] = raw_in[...] if last else jnp.zeros_like(total)
         mod_grad[...] = mod_in[...] if last else jnp.zeros_like(mod_grad)
 
-    normed, hidden = modulated(hold_piece((one, two, three, four), held), mod)
+    normed, hidden = modulated(hold_piece(places, pieces, held, arrived), mod)
     shape = normed.shape
     pieces = jnp.concatenate([dq[...], dk[...], dv[...]], axis=0)
     total[...] += dot(pieces, hidden)
@@ -703,18 +711,18 @@
     operands = [piece for piece, _ in pieces] + [mod, dq, dk, dv, weight]
     grads = jax.ShapeDtypeStruct((2, count // 2, width), bf16)
     grads_spec = pl.BlockSpec((1, block, width), lambda i: (i // 2, lax.rem(i, 2), 0))
-    held = VMEM((block, width), bf16)
+    held = hold_scratch(block, width)
     mods = jax.ShapeDtypeStruct((frames, 2, width), f32)
     if last:
         in_specs += [whole(), whole()]
         operands += list(sums)
         out_shape = [grads, jax.ShapeDtypeStruct((width, 3 * rows), bf16), mods]
-        scratch = [VMEM((3 * rows, width), f32), held]
+        scratch = [VMEM((3 * rows, width), f32)] + held
     else:
         out_shape = [grads, jax.ShapeDtypeStruct((3 * rows, width), f32), mods]
-        scratch = [held]
+        scratch = held
     return pl.pallas_call(
-        functools.partial(first_back_kernel, last),
+        functools.partial(first_back_kernel, last, [place for _, place in pieces]),
         grid=(4,),
         in_specs=in_specs,
         out_specs=[grads_spec, whole(), whole()],
@@ -916,30 +924,25 @@
         angles = jnp.concatenate([freqs * small[0:1], freqs * small[1:2]], axis=0)
         return jnp.cos(angles), jnp.sin(angles), jnp.where(small[2:3] > 0.5, 0.0, MASKED)
 
-    cos_near, sin_near, bias_near = places_of((tok0, tok1))
-    cos_far, sin_far, bias_far = places_of((tok2_two, tok3_two))
+    cosine, sine, bias = places_of((tok0, tok1, tok2_two, tok3_two))
     near = ((tok0, 0), (tok0, 1), (tok1, 0), (tok1, 1))
-    qkv_near = project_qkv(near, mod, attend_turned, cos_near, sin_near)
     across = ((tok2_one, 0), (tok2_two, 0), (tok3_one, 0), (tok3_two, 0))
-    project_mine, qkv_near = lax.optimization_barrier((project_mine, qkv_near))
+    qkv = project_qkv(near + across, mod, attend_turned, cosine, sine)
+
     project_full = lax.all_to_all(
         jnp.broadcast_to(project_mine[None], (clips, 2, shard, width)), "clip", 0, 0, tiled=True
     )
-    qkv_far = project_qkv(across, mod, attend_turned, cos_far, sin_far)
-    cosine = jnp.concatenate([cos_near, cos_far], axis=1)
-    sine = jnp.concatenate([sin_near, sin_far], axis=1)
-    bias = jnp.concatenate([bias_near, bias_far], axis=1)
 
     cot_far, mod = lax.optimization_barrier((upstream, mod))
     cot_far = swap(cot_far, "x", 2, 1)
-    out_far, lse_far = attend(qkv_far, qkv_near, qkv_far, bias)
-    out_far, qkv_near, cot_far, project_full = lax.optimization_barrier(
-        (out_far, qkv_near, cot_far, project_full)
+    out_far, lse_far = attend(qkv, 1, bias)
+    out_far, qkv, cot_far, project_full = lax.optimization_barrier(
+        (out_far, qkv, cot_far, project_full)
     )
     project_near = swap(project_full, "core", 2, 1)
     part2 = swap(out_far[0], ROW, rows, 2)
     part3 = swap(out_far[1], ROW, rows, 3)
-    out_near, lse_near = attend(qkv_near, qkv_near, qkv_far, bias)
+    out_near, lse_near = attend(qkv, 0, bias)
     out_near, project_near = lax.optimization_barrier((out_near, project_near))
     part1 = swap(out_near[1], ROW, rows, 1)
     parts = [out_near, part1, part2, part3]
@@ -988,13 +991,13 @@
     d3 = swap(d3, ROW, rows, 3)
     d1 = swap(d1, ROW, rows, 1)
     dq_near, dk, dv = attend_back(
-        qkv_near, qkv_near, qkv_far, bias, out_near, (d0, d1), lse_near, turning, 0
+        qkv, bias, out_near, (d0, d1), lse_near, turning, 0
     )
     dk, d2, d3, out3, out4 = lax.optimization_barrier((dk, d2, d3, out3, out4))
     out3 = swap(out3, "x", 2, 1)
     out4 = swap(out4, "x", 2, 1)
     dq_far, dk, dv = attend_back(
-        qkv_far, qkv_near, qkv_far, bias, out_far, (d2, d3), lse_far, turning, 1, (dk, dv)
+        qkv, bias, out_far, (d2, d3), lse_far, turning, 1, (dk, dv)
     )
     dq_far, project_raw, out3, out4 = lax.optimization_barrier((dq_far, project_raw, out3, out4))
     project_sum = total_over(project_raw.reshape(devices, 1, shard, width))[0].T
@@ -1006,7 +1009,7 @@
     ]
     far_one, far_two, dq_near = lax.optimization_barrier((far_one, far_two, dq_near))
     far_one = swap(far_one, "x", 2, 1)
-    extra = -(-2 * frames * part // (3 * features))
+    extra = -(-frames * part // (3 * features))
     back, attend_raw, mod_early = first_back(
         near, mod, dq_near, dk, dv, attend_turned, 0, (raw, mod_early)
     )
@@ -1021,9 +1024,7 @@
 
     mod_grad = jnp.concatenate([mod_early, mod_late, mod_gate], axis=1)
     mod_grad = mod_grad.reshape(frames, devices, part).transpose(1, 0, 2).reshape(devices, -1)
-    mod_high = mod_grad.astype(bf16)
-    mod_low = (mod_grad - mod_high.astype(f32)).astype(bf16)
-    small = jnp.concatenate([mod_high, mod_low], axis=1)
+    small = mod_grad.astype(bf16)
     small = jnp.pad(small, ((0, 0), (0, extra * 3 * features - small.shape[1])))
     attend_raw = jnp.concatenate(
         [
@@ -1038,9 +1039,9 @@
         (attend_raw, far_two, block_out, project_sum)
     )
     input_gradient = input_back(own, mod, middle_grad, back_near + (far_one, far_two))
-    small = attend_raw[:, shard : shard + extra].reshape(devices, -1)[:, : 2 * frames * part]
-    small = small.astype(f32).reshape(clips, rows, 2, frames, part)
-    mod_grad = jnp.sum(small, axis=(1, 2)).reshape(clips * frames, part)
+    small = attend_raw[:, shard : shard + extra].reshape(devices, -1)[:, : frames * part]
+    small = small.astype(f32).reshape(clips, rows, frames, part)
+    mod_grad = jnp.sum(small, axis=1).reshape(clips * frames, part)
     attend_sum = total_over(attend_raw.reshape(clips, rows, shard + extra, 3 * features))
     attend_sum = attend_sum[:, :shard].reshape(rows, shard, 3, features)
     attend_sum = attend_sum.transpose(1, 2, 0, 3).reshape(shard, 3 * width)

time: 559 us -> 547 us (0.979)
    pallas_call x4 -> x3, Pallas kernels: 46.6 us -> 42.4 us  [the longest x2 27.4 us: first_back(): pl.pallas_call(functools.partial(first_back_kernel, last, [place for _, p...]
  transfers between devices with their start and end apart: 38 -> 38, of which waited for: 11 -> 10; matrix products, arithmetic and copies ran while one was open for 11% -> 10% of each run, Pallas kernels for 59% -> 59%
where the time goes in v13:
time: 547 us; the launch traced here: 538 us
  Pallas kernels  318 us (58%)
  waiting for transfers between devices  65.9 us (12%)
  starting transfers between devices  58.1 us (11%)
  other arithmetic  38.4 us (7%)
  local copies, waits for them, and re-layouts  34 us (6%)
  between operations  21.9 us (4%)
    pallas_call x2, Pallas kernels, attend_back(): pl.pallas_call(functools.partial(attend_back_kernel, heads, last), grid=(...  99.3 us
    pallas_call x2, Pallas kernels, attend(): pl.pallas_call(functools.partial(attend_kernel, heads), grid=(count // bl...  55 us
    pallas_call x4, Pallas kernels, feed_forward(): pl.pallas_call(feed_kernel, grid=(units // block,), in_specs=[spec, flat,...  54.2 us
    ppermute x29, waiting for transfers between devices, swap(): lax.ppermute(value, axis, [(place, place ^ step) for place in range(size)])  41.2 us
    pallas_call x2, Pallas kernels, first_back(): pl.pallas_call(functools.partial(first_back_kernel, last, [place for _, p...  27.4 us
    ppermute x29, starting transfers between devices, swap(): lax.ppermute(value, axis, [(place, place ^ step) for place in range(size)])  25.3 us
    pallas_call x1, Pallas kernels, feed_weights(): pl.pallas_call(functools.partial(feed_weight_kernel, len(hidden)), grid=(...  21 us
    all_to_all x1, waiting for transfers between devices, local(): lax.all_to_all(mod_mine.reshape(devices, frames, part), both, 0, 0, tiled...  18.8 us
  transfers between devices with their start and end apart: 38, of which 10 were waited for; matrix products, arithmetic and copies ran while one was open for 10% of the time, Pallas kernels for 59%

profile of v13, /device:TPU:0, one launch (start us, length us, event | category | flops | bytes accessed | tf_op | source)
XLA Modules:
  0.0 538.4 jit_solution(5294233611372244606)
XLA Ops:
  9.5 2.4 collective-permute-start.4
  18.7 5.8 %all-to-all-start = ((bf16[8,12,1024]{2,1,0:T(8,128)(2,1)}), bf16[8,12,1024]{2,1,0:T(8,128)(2,1)S(1)}, u32[]{:S(2)}, u32[]{:S(2)}) async-start(bf16[8,12,1024]{2,1,0:T(8,128)(2,1)} %broadcast_in_dim.31), calls=%async_computation | async-start | bytes 524288 | tf_op jit(solution)/shard_map/all_to_all | solution.py:883
  32.5 6.8 %collective-permute-done.1 = bf16[2,32,2048]{2,1,0:T(8,128)(2,1)S(1)} collective-permute-done((bf16[2,32,2048]{2,1,0:T(8,128)(2,1)S(1)}, bf16[2,32,2048]{2,1,0:T(8,128)(2,1)S(1)}, u32[]{:S(2)}, u32[]{:S(2)}) %collective-permute-start.1) | collective-permute-done | bytes 262176 | tf_op jit(solution)/shard_map/ppermute | solution.py:783
  43.6 5.0 all-to-all-start.1
  49.9 2.3 broadcast_select_fusion.2
  52.3 18.8 %all-to-all-done.1 = f32[32,12,192]{2,1,0:T(8,128)S(1)} async-done(((f32[32,12,192]{2,1,0:T(8,128)}), f32[32,12,192]{2,1,0:T(8,128)S(1)}, u32[]{:S(2)}, u32[]{:S(2)}) %all-to-all-start.1) | async-done | bytes 294944 | tf_op jit(solution)/shard_map/all_to_all | solution.py:895
  72.3 5.6 %all-gather.3.cloned.1.call-done = bf16[1024,768]{0,1:T(8,128)(2,1)} async-done(((bf16[128,768]{0,1:T(8,128)(2,1)}), bf16[1024,768]{0,1:T(8,128)(2,1)}) %all-gather.3.cloned.1.call-update) | async-done | bytes 1572880 | tf_op jit(solution)/shard_map/all_gather | solution.py:880
  84.9 5.2 all-to-all-start.2
  95.5 15.0 %shard_map.487.q_ref.k_ref.v_ref = bf16[768,3072]{1,0:T(8,128)(2,1)} custom-call(bf16[784,1024]{1,0:T(8,128)(2,1)} %fusion.1.refs_0_.refs_1_, bf16[784,1024]{1,0:T(8,128)(2,1)} %fusion.1.refs_0_.refs_1_, bf16[784,1024]{1,0:T(8,128)(2,1)} %collective-permute-done.refs_2_.refs_3_, bf16[784,1024]{1,0:T(8,128)(2,1)} %collective-permute-done.refs_2_.refs_3_, ...), custom_call_target="tpu_custom_call" | custom-call | flops 4831838208 | bytes 12582912 | tf_op jit(solution)/shard_map/pallas_call | solution.py:144
  111.1 27.5 %shard_map.488 = (bf16[2,256,768]{2,1,0:T(8,128)(2,1)}, f32[4,1536]{1,0:T(4,128)}) custom-call(bf16[768,3072]{1,0:T(8,128)(2,1)} %shard_map.487.q_ref.k_ref.v_ref, bf16[768,3072]{1,0:T(8,128)(2,1)} %shard_map.487.q_ref.k_ref.v_ref, bf16[768,3072]{1,0:T(8,128)(2,1)} %shard_map.487.q_ref.k_ref.v_ref, f32[1,3072]{1,0:T(1,128)} %compare_select_fusion.bias), custom_call_target="tpu_custom_call" | custom-call | flops 19327352832 | bytes 3145728 | tf_op jit(solution)/shard_map/pallas_call | solution.py:198
  142.1 27.5 %shard_map.489 = (bf16[2,256,768]{2,1,0:T(8,128)(2,1)}, f32[4,1536]{1,0:T(4,128)}) custom-call(bf16[768,3072]{1,0:T(8,128)(2,1)} %shard_map.487.q_ref.k_ref.v_ref, bf16[768,3072]{1,0:T(8,128)(2,1)} %shard_map.487.q_ref.k_ref.v_ref, bf16[768,3072]{1,0:T(8,128)(2,1)} %shard_map.487.q_ref.k_ref.v_ref, f32[1,3072]{1,0:T(1,128)} %compare_select_fusion.bias), custom_call_target="tpu_custom_call" | custom-call | flops 19327352832 | bytes 3145728 | tf_op jit(solution)/shard_map/pallas_call | solution.py:198
  173.7 10.3 %shard_map.490 = (f32[12,64,1024]{2,1,0:T(8,128)}, bf16[384,1024]{1,0:T(8,128)(2,1)}, bf16[384,1024]{1,0:T(8,128)(2,1)}, bf16[768,1024]{1,0:T(8,128)(2,1)}, bf16...) custom-call(s32[5]{0:T(128)} %pad_add_fusion.order, bf16[2,256,768]{2,1,0:T(8,128)(2,1)} %get-tuple-element.143.a0.out_ref, ...), custom_call_target="tpu_custom_call" | custom-call | flops 1610612736 | bytes 11010048 | tf_op jit(solution)/shard_map/pallas_call | solution.py:408
  184.6 13.8 %shard_map.491 = (f32[384,1024]{1,0:T(8,128)}, f32[384,1024]{1,0:T(8,128)}, bf16[384,2048]{1,0:T(8,128)(2,1)}, bf16[384,2048]{1,0:T(8,128)(2,1)}, f32[6,1,1024]{2,1,0:T(1,128)}) custom-call(bf16[16,2,2,32,2048]{4,3,2,1,0:T(8,128)(2,1)} %bitcast.206, bf16[384,1024]{1,0:T(8,128)(2,1)} %get-tuple-element.147.hidden.refs_0_, ...), custom_call_target="tpu_custom_call" | custom-call | flops 6442450944 | bytes 11534336 | tf_op jit(solution)/shard_map/pallas_call | solution.py:505
  199.9 13.8 %shard_map.492 = (f32[384,1024]{1,0:T(8,128)}, f32[384,1024]{1,0:T(8,128)}, bf16[384,2048]{1,0:T(8,128)(2,1)}, bf16[384,2048]{1,0:T(8,128)(2,1)}, f32[6,1,1024]{2,1,0:T(1,128)}) custom-call(bf16[16,2,2,32,2048]{4,3,2,1,0:T(8,128)(2,1)} %bitcast.207, bf16[384,1024]{1,0:T(8,128)(2,1)} %get-tuple-element.155.hidden.refs_1_, ...), custom_call_target="tpu_custom_call" | custom-call | flops 6442450944 | bytes 11534336 | tf_op jit(solution)/shard_map/pallas_call | solution.py:505
  214.6 13.2 %shard_map.493 = (bf16[384,1024]{1,0:T(8,128)(2,1)}, bf16[384,1024]{1,0:T(8,128)(2,1)}, bf16[384,2048]{1,0:T(8,128)(2,1)}, bf16[384,2048]{1,0:T(8,128)(2,1)}, f32[6,1,1024]{2,1,0:T(1,128)}) custom-call(bf16[16,2,2,32,2048]{4,3,2,1,0:T(8,128)(2,1)} %bitcast.208, bf16[384,1024]{1,0:T(8,128)(2,1)} %copy-done.57, ...), custom_call_target="tpu_custom_call" | custom-call | flops 6442450944 | bytes 11534336 | tf_op jit(solution)/shard_map/pallas_call | solution.py:505
  229.3 13.4 %shard_map.494 = (bf16[384,1024]{1,0:T(8,128)(2,1)}, bf16[384,1024]{1,0:T(8,128)(2,1)}, bf16[384,2048]{1,0:T(8,128)(2,1)}, bf16[384,2048]{1,0:T(8,128)(2,1)}, f32[6,1,1024]{2,1,0:T(1,128)}) custom-call(bf16[16,2,2,32,2048]{4,3,2,1,0:T(8,128)(2,1)} %bitcast.209, bf16[384,1024]{1,0:T(8,128)(2,1)} %copy-done.58, ...), custom_call_target="tpu_custom_call" | custom-call | flops 6442450944 | bytes 11534336 | tf_op jit(solution)/shard_map/pallas_call | solution.py:505
  244.2 21.0 %shard_map.495 = bf16[16,2,2,32,2048]{4,3,2,1,0:T(8,128)(2,1)} custom-call(bf16[384,1024]{1,0:T(8,128)(2,1)} %get-tuple-element.147.hidden.refs_0_, bf16[384,1024]{1,0:T(8,128)(2,1)} %get-tuple-element.155.hidden.refs_1_, bf16[384,1024]{1,0:T(8,128)(2,1)} %copy-done.57, bf16[384,1024]{1,0:T(8,128)(2,1)} %copy-done.58, ...), custom_call_target="tpu_custom_call" | custom-call | flops 12884901888 | bytes 20971520 | tf_op jit(solution)/shard_map/pallas_call | solution.py:556
  266.4 17.2 %shard_map.496 = (f32[12,64,1024]{2,1,0:T(8,128)}, f32[12,3,1024]{2,1,0:T(4,128)}, bf16[256,768]{1,0:T(8,128)(2,1)}, bf16[256,768]{1,0:T(8,128)(2,1)}, bf16[256,...) custom-call(s32[5]{0:T(128)} %pad_add_fusion.order, f32[384,1024]{1,0:T(8,128)} %get-tuple-element.149.into1, ...), custom_call_target="tpu_custom_call" | custom-call | flops 3221225472 | bytes 18874368 | tf_op jit(solution)/shard_map/pallas_call | solution.py:619
  283.7 5.7 %all-to-all-start.3 = ((bf16[32,32,1024]{2,1,0:T(8,128)(2,1)}), bf16[32,32,1024]{2,1,0:T(8,128)(2,1)}, u32[]{:S(2)}, u32[]{:S(2)}) async-start(bf16[32,32,1024]{2,1,0:T(8,128)(2,1)} %bitcast.185), calls=%async_computation.3 | async-start | bytes 4194304 | tf_op jit(solution)/shard_map/all_to_all | solution.py:985
  291.4 48.4 %shard_map.497 = (bf16[256,1536]{1,0:T(8,128)(2,1)}, f32[256,3072]{1,0:T(8,128)}, f32[256,3072]{1,0:T(8,128)}) custom-call(bf16[768,3072]{1,0:T(8,128)(2,1)} %shard_map.487.q_ref.k_ref.v_ref, bf16[768,3072]{1,0:T(8,128)(2,1)} %shard_map.487.q_ref.k_ref.v_ref, bf16[768,3072]{1,0:T(8,128)(2,1)} %shard_map.487.q_ref.k_ref.v_ref, ...), custom_call_target="tpu_custom_call" | custom-call | flops 41070624768 | bytes 6291456 | tf_op jit(solution)/shard_map/pallas_call | solution.py:339
  341.8 51.0 %shard_map.498 = (bf16[256,1536]{1,0:T(8,128)(2,1)}, bf16[256,3072]{1,0:T(8,128)(2,1)}, bf16[256,3072]{1,0:T(8,128)(2,1)}) custom-call(bf16[768,3072]{1,0:T(8,128)(2,1)} %shard_map.487.q_ref.k_ref.v_ref, bf16[768,3072]{1,0:T(8,128)(2,1)} %shard_map.487.q_ref.k_ref.v_ref, bf16[768,3072]{1,0:T(8,128)(2,1)} %shard_map.487.q_ref.k_ref.v_ref, ...), custom_call_target="tpu_custom_call" | custom-call | flops 41070624768 | bytes 6291456 | tf_op jit(solution)/shard_map/pallas_call | solution.py:339
  392.8 13.0 %shard_map.499 = (bf16[2,768,1024]{2,1,0:T(8,128)(2,1)}, f32[768,1024]{1,0:T(8,128)}, f32[12,2,1024]{2,1,0:T(2,128)}) custom-call(bf16[384,1024]{1,0:T(8,128)(2,1)} %collective-permute-done.5.refs_4_.refs_0_, bf16[400,1024]{1,0:T(8,128)(2,1)} %collective-permute-done.6.refs_5_.refs_1_, bf16[384,1024]{1,0:T(8,128)(2,1)} %collective-permute-done.7.refs_6_.refs_2_, ...), custom_call_target="tpu_custom_call" | custom-call | flops 4831838208 | bytes 9437184 | tf_op jit(solution)/shard_map/pallas_call | solution.py:724
  407.7 3.3 collective-permute-done.24
  414.5 14.4 %shard_map.500 = (bf16[2,768,1024]{2,1,0:T(8,128)(2,1)}, bf16[1024,768]{1,0:T(8,128)(2,1)}, f32[12,2,1024]{2,1,0:T(2,128)}) custom-call(bf16[784,1024]{1,0:T(8,128)(2,1)} %fusion.1.refs_0_.refs_1_, bf16[784,1024]{1,0:T(8,128)(2,1)} %fusion.1.refs_0_.refs_1_, bf16[784,1024]{1,0:T(8,128)(2,1)} %collective-permute-done.refs_2_.refs_3_, ...), custom_call_target="tpu_custom_call" | custom-call | flops 4831838208 | bytes 9437184 | tf_op jit(solution)/shard_map/pallas_call | solution.py:724
  434.2 5.7 %all-to-all-start.4 = ((bf16[32,35,768]{2,1,0:T(8,128)(2,1)}), bf16[32,35,768]{2,1,0:T(8,128)(2,1)S(1)}, u32[]{:S(2)}, u32[]{:S(2)}) async-start(bf16[32,35,768]{2,1,0:T(8,128)(2,1)} %pad_maximum_fusion), calls=%async_computation.5 | async-start | bytes 3932160 | tf_op jit(solution)/shard_map/all_to_all | solution.py:1036
  439.9 2.5 shard_map.502
  442.5 5.3 shard_map.501
  454.5 11.4 %collective-permute-done.28 = bf16[2,32,2048]{2,1,0:T(8,128)(2,1)S(1)} collective-permute-done((bf16[2,32,2048]{2,1,0:T(8,128)(2,1)S(1)}, bf16[2,32,2048]{2,1,0:T(8,128)(2,1)S(1)}, u32[]{:S(2)}, u32[]{:S(2)}) %collective-permute-start.28) | collective-permute-done | bytes 262176 | tf_op jit(solution)/shard_map/ppermute | solution.py:783
  471.6 15.2 %collective-permute-done.26.far2 = bf16[384,1024]{1,0:T(8,128)(2,1)} collective-permute-done((bf16[384,1024]{1,0:T(8,128)(2,1)S(1)}, bf16[384,1024]{1,0:T(8,128)(2,1)}, u32[]{:S(2)}, u32[]{:S(2)}) %collective-permute-start.26) | collective-permute-done | bytes 786464 | tf_op jit(solution)/shard_map/ppermute | solution.py:783
  495.2 2.6 shard_map.504
  503.4 4.8 all-to-all-start.5
  508.2 7.9 %shard_map.503 = f32[12,64,1024]{2,1,0:T(8,128)} custom-call(bf16[12,64,1024]{2,1,0:T(8,128)(2,1)} %bitcast.159, f32[12,6,1024]{2,1,0:T(8,128)} %reshape.459.refs_8_.mod.refs_4_, f32[12,64,1024]{2,1,0:T(8,128)} %get-tuple-element.216.middle_grad, bf16[2,768,1024]{2,1,0:T(8,128)(2,1)} %get-tuple-element.217.one, ...), custom_call_target="tpu_custom_call" | custom-call | flops 15728640 | bytes 12582912 | tf_op jit(solution)/shard_map/pallas_call | solution.py:754
  (318 shorter events, 100.7 us)
Async XLA Ops:
  9.5 15.6 %collective-permute-start.4 = (bf16[32,768]{1,0:T(8,128)(2,1)S(1)}, bf16[32,768]{1,0:T(8,128)(2,1)S(1)}, u32[]{:S(2)}, u32[]{:S(2)}) collective-permute-start(bf16[32,768]{1,0:T(8,128)(2,1)S(1)} %get-tuple-element.279), channel_id=1, source_target_pairs={{0,3},{1,2},{2,1},{3,0},{4,7},{5,6},{6,5},{7,4},{8,11},{9,10},{10,... | collective-permute-start | bytes 147464 | tf_op jit(solution)/shard_map/ppermute | solution.py:783
  11.9 13.1 %collective-permute-start.3 = (bf16[32,768]{1,0:T(8,128)(2,1)S(1)}, bf16[32,768]{1,0:T(8,128)(2,1)S(1)}, u32[]{:S(2)}, u32[]{:S(2)}) collective-permute-start(bf16[32,768]{1,0:T(8,128)(2,1)S(1)} %get-tuple-element.280), channel_id=1, source_target_pairs={{0,2},{1,3},{2,0},{3,1},{4,6},{5,7},{6,4},{7,5},{8,10},{9,11},{10,... | collective-permute-start | bytes 147464 | tf_op jit(solution)/shard_map/ppermute | solution.py:783
  12.6 12.5 %collective-permute-start.2 = (bf16[32,768]{1,0:T(8,128)(2,1)S(1)}, bf16[32,768]{1,0:T(8,128)(2,1)S(1)}, u32[]{:S(2)}, u32[]{:S(2)}) collective-permute-start(bf16[32,768]{1,0:T(8,128)(2,1)S(1)} %get-tuple-element.281), channel_id=1, source_target_pairs={{0,1},{1,0},{2,3},{3,2},{4,5},{5,4},{6,7},{7,6},{8,9},{9,8},{10,11... | collective-permute-start | bytes 147464 | tf_op jit(solution)/shard_map/ppermute | solution.py:783
  13.5 26.5 %collective-permute-start.5 = (bf16[384,1024]{1,0:T(8,128)(2,1)}, bf16[384,1024]{1,0:T(8,128)(2,1)}, u32[]{:S(2)}, u32[]{:S(2)}) collective-permute-start(bf16[384,1024]{1,0:T(8,128)(2,1)} %bitcast.34), channel_id=1, source_target_pairs={{0,2},{2,0},{1,3},{3,1},{4,6},{6,4},{5,7},{7,5},{8,10},{10,8},{9,1... | collective-permute-start | bytes 2359304 | tf_op jit(solution)/shard_map/ppermute | solution.py:783
  18.7 21.0 %all-to-all-start = ((bf16[8,12,1024]{2,1,0:T(8,128)(2,1)}), bf16[8,12,1024]{2,1,0:T(8,128)(2,1)S(1)}, u32[]{:S(2)}, u32[]{:S(2)}) async-start(bf16[8,12,1024]{2,1,0:T(8,128)(2,1)} %broadcast_in_dim.31), calls=%async_computation | async-start | bytes 524288 | tf_op jit(solution)/shard_map/all_to_all | solution.py:883
  24.5 53.3 %all-gather.3.cloned.1.call-start = ((), (), s32[]{:S(2)}) async-start(), calls=%async_computation.7 | async-start | bytes 1769472 | tf_op jit(solution)/shard_map/all_gather | solution.py:880
  40.1 32.2 %collective-permute-start.6 = (bf16[400,1024]{1,0:T(8,128)(2,1)S(1)}, bf16[400,1024]{1,0:T(8,128)(2,1)}, u32[]{:S(2)}, u32[]{:S(2)}) collective-permute-start(bf16[400,1024]{1,0:T(8,128)(2,1)S(1)} %slice.191), channel_id=1, source_target_pairs={{0,2},{2,0},{1,3},{3,1},{4,6},{6,4},{5,7},{7,5},{8,10},{10,8},{9,1... | collective-permute-start | bytes 2457608 | tf_op jit(solution)/shard_map/ppermute | solution.py:783
  43.6 27.4 %all-to-all-start.1 = ((f32[32,12,192]{2,1,0:T(8,128)}), f32[32,12,192]{2,1,0:T(8,128)S(1)}, u32[]{:S(2)}, u32[]{:S(2)}) async-start(f32[32,12,192]{2,1,0:T(8,128)} %bitcast.35), calls=%async_computation.1 | async-start | bytes 1048576 | tf_op jit(solution)/shard_map/all_to_all | solution.py:895
  48.6 136.0 %all-gather.5.cloned.1.call-start = ((), (), s32[]{:S(2)}) async-start(), calls=%async_computation.8 | async-start | bytes 8912896 | tf_op jit(solution)/shard_map/all_gather | solution.py:907
  78.8 11.4 %collective-permute-start = (bf16[784,1024]{1,0:T(8,128)(2,1)}, bf16[784,1024]{1,0:T(8,128)(2,1)}, u32[]{:S(2)}, u32[]{:S(2)}) collective-permute-start(bf16[784,1024]{1,0:T(8,128)(2,1)} %fusion.1.refs_0_.refs_1_), channel_id=1, source_target_pairs={{0,1},{1,0},{2,3},{3,2},{4,5},{5,4},{6,7},{7,6},{8,9},{9,8},{10,11... | collective-permute-start | bytes 4816904 | tf_op jit(solution)/shard_map/ppermute | solution.py:783
  78.9 14.3 %collective-permute-start.8 = (bf16[400,1024]{1,0:T(8,128)(2,1)}, bf16[400,1024]{1,0:T(8,128)(2,1)S(1)}, u32[]{:S(2)}, u32[]{:S(2)}) collective-permute-start(bf16[400,1024]{1,0:T(8,128)(2,1)} %collective-permute-done.6.refs_5_.refs_1_), channel_id=1, source_target_pairs={{0,1},{1,0},{2,3},{3,2},{4,5},{5,4},{6,7},{7,6},{8,9},{9,8},{10,11... | collective-permute-start | bytes 2457608 | tf_op jit(solution)/shard_map/ppermute | solution.py:783
  84.9 53.7 %all-to-all-start.2 = ((bf16[8,2,32,1024]{3,2,1,0:T(8,128)(2,1)}), bf16[8,2,32,1024]{3,2,1,0:T(8,128)(2,1)S(1)}, u32[]{:S(2)}, u32[]{:S(2)}) async-start(bf16[8,2,32,1024]{3,2,1,0:T(8,128)(2,1)} %broadcast_in_dim.36), calls=%async_computation.2 | async-start | bytes 2097152 | tf_op jit(solution)/shard_map/all_to_all | solution.py:932
  90.1 342.5 %reduce-scatter.2.cloned.1.call-start = ((), (), s32[]{:S(2)}) async-start(), calls=%async_computation.9 | async-start | bytes 8912896 | tf_op jit(solution)/shard_map/reduce_scatter | solution.py:974
  91.7 46.9 %collective-permute-start.9 = (bf16[12,64,1024]{2,1,0:T(8,128)(2,1)S(1)}, bf16[12,64,1024]{2,1,0:T(8,128)(2,1)}, u32[]{:S(2)}, u32[]{:S(2)}) collective-permute-start(bf16[12,64,1024]{2,1,0:T(8,128)(2,1)S(1)} %bitcast.167), channel_id=1, source_target_pairs={{0,2},{2,0},{1,3},{3,1},{4,6},{6,4},{5,7},{7,5},{8,10},{10,8},{9,1... | collective-permute-start | bytes 4718600 | tf_op jit(solution)/shard_map/ppermute | solution.py:783
  140.2 31.9 %collective-permute-start.14 = (bf16[256,768]{1,0:T(8,128)(2,1)S(1)}, bf16[256,768]{1,0:T(8,128)(2,1)S(1)}, u32[]{:S(2)}, u32[]{:S(2)}) collective-permute-start(bf16[256,768]{1,0:T(8,128)(2,1)S(1)} %get-tuple-element.256), channel_id=1, source_target_pairs={{0,3},{1,2},{2,1},{3,0},{4,7},{5,6},{6,5},{7,4},{8,11},{9,10},{10,... | collective-permute-start | bytes 1179656 | tf_op jit(solution)/shard_map/ppermute | solution.py:783
  140.6 31.6 %collective-permute-start.13 = (bf16[256,768]{1,0:T(8,128)(2,1)S(1)}, bf16[256,768]{1,0:T(8,128)(2,1)S(1)}, u32[]{:S(2)}, u32[]{:S(2)}) collective-permute-start(bf16[256,768]{1,0:T(8,128)(2,1)S(1)} %get-tuple-element.257), channel_id=1, source_target_pairs={{0,2},{1,3},{2,0},{3,1},{4,6},{5,7},{6,4},{7,5},{8,10},{9,11},{10,... | collective-permute-start | bytes 1179656 | tf_op jit(solution)/shard_map/ppermute | solution.py:783
  142.1 27.6 %collective-permute-start.11 = (bf16[8,2,32,1024]{3,2,1,0:T(8,128)(2,1)S(1)}, bf16[8,2,32,1024]{3,2,1,0:T(8,128)(2,1)S(1)}, u32[]{:S(2)}, u32[]{:S(2)}) collective-permute-start(bf16[8,2,32,1024]{3,2,1,0:T(8,128)(2,1)S(1)} %all-to-all-done.2.mine), channel_id=1, source_target_pairs={{0,1},{1,0},{2,3},{3,2},{4,5},{5,4},{6,7},{7,6},{8,9},{9,8},{10,11... | collective-permute-start | bytes 3145736 | tf_op jit(solution)/shard_map/ppermute | solution.py:783
  184.0 29.7 %collective-permute-start.15 = (bf16[384,1024]{1,0:T(8,128)(2,1)}, bf16[384,1024]{1,0:T(8,128)(2,1)S(1)}, u32[]{:S(2)}, u32[]{:S(2)}) collective-permute-start(bf16[384,1024]{1,0:T(8,128)(2,1)} %get-tuple-element.147.hidden.refs_0_), channel_id=1, source_target_pairs={{0,2},{2,0},{1,3},{3,1},{4,6},{6,4},{5,7},{7,5},{8,10},{10,8},{9,1... | collective-permute-start | bytes 2359304 | tf_op jit(solution)/shard_map/ppermute | solution.py:783
  198.4 30.0 %collective-permute-start.16 = (bf16[384,1024]{1,0:T(8,128)(2,1)S(1)}, bf16[384,1024]{1,0:T(8,128)(2,1)S(1)}, u32[]{:S(2)}, u32[]{:S(2)}) collective-permute-start(bf16[384,1024]{1,0:T(8,128)(2,1)S(1)} %copy-done.56), channel_id=1, source_target_pairs={{0,2},{2,0},{1,3},{3,1},{4,6},{6,4},{5,7},{7,5},{8,10},{10,8},{9,1... | collective-permute-start | bytes 2359304 | tf_op jit(solution)/shard_map/ppermute | solution.py:783
  227.8 37.4 %collective-permute-start.17 = (bf16[384,1024]{1,0:T(8,128)(2,1)}, bf16[384,1024]{1,0:T(8,128)(2,1)S(1)}, u32[]{:S(2)}, u32[]{:S(2)}) collective-permute-start(bf16[384,1024]{1,0:T(8,128)(2,1)} %get-tuple-element.167), channel_id=1, source_target_pairs={{0,2},{2,0},{1,3},{3,1},{4,6},{6,4},{5,7},{7,5},{8,10},{10,8},{9,1... | collective-permute-start | bytes 2359304 | tf_op jit(solution)/shard_map/ppermute | solution.py:783
  242.7 22.5 %collective-permute-start.18 = (bf16[384,1024]{1,0:T(8,128)(2,1)}, bf16[384,1024]{1,0:T(8,128)(2,1)S(1)}, u32[]{:S(2)}, u32[]{:S(2)}) collective-permute-start(bf16[384,1024]{1,0:T(8,128)(2,1)} %get-tuple-element.168), channel_id=1, source_target_pairs={{0,2},{2,0},{1,3},{3,1},{4,6},{6,4},{5,7},{7,5},{8,10},{10,8},{9,1... | collective-permute-start | bytes 2359304 | tf_op jit(solution)/shard_map/ppermute | solution.py:783
  283.7 109.1 %all-to-all-start.3 = ((bf16[32,32,1024]{2,1,0:T(8,128)(2,1)}), bf16[32,32,1024]{2,1,0:T(8,128)(2,1)}, u32[]{:S(2)}, u32[]{:S(2)}) async-start(bf16[32,32,1024]{2,1,0:T(8,128)(2,1)} %bitcast.185), calls=%async_computation.3 | async-start | bytes 4194304 | tf_op jit(solution)/shard_map/all_to_all | solution.py:985
  289.4 50.3 %collective-permute-start.20 = (bf16[256,768]{1,0:T(8,128)(2,1)S(1)}, bf16[256,768]{1,0:T(8,128)(2,1)}, u32[]{:S(2)}, u32[]{:S(2)}) collective-permute-start(bf16[256,768]{1,0:T(8,128)(2,1)S(1)} %copy-done.60), channel_id=1, source_target_pairs={{0,2},{1,3},{2,0},{3,1},{4,6},{5,7},{6,4},{7,5},{8,10},{9,11},{10,... | collective-permute-start | bytes 1179656 | tf_op jit(solution)/shard_map/ppermute | solution.py:783
  291.3 48.4 %collective-permute-start.21 = (bf16[256,768]{1,0:T(8,128)(2,1)S(1)}, bf16[256,768]{1,0:T(8,128)(2,1)}, u32[]{:S(2)}, u32[]{:S(2)}) collective-permute-start(bf16[256,768]{1,0:T(8,128)(2,1)S(1)} %copy-done.59), channel_id=1, source_target_pairs={{0,3},{1,2},{2,1},{3,0},{4,7},{5,6},{6,5},{7,4},{8,11},{9,10},{10,... | collective-permute-start | bytes 1179656 | tf_op jit(solution)/shard_map/ppermute | solution.py:783
  339.8 53.0 %collective-permute-start.22 = (bf16[384,1024]{1,0:T(8,128)(2,1)}, bf16[384,1024]{1,0:T(8,128)(2,1)S(1)}, u32[]{:S(2)}, u32[]{:S(2)}) collective-permute-start(bf16[384,1024]{1,0:T(8,128)(2,1)} %get-tuple-element.188), channel_id=1, source_target_pairs={{0,2},{2,0},{1,3},{3,1},{4,6},{6,4},{5,7},{7,5},{8,10},{10,8},{9,1... | collective-permute-start | bytes 2359304 | tf_op jit(solution)/shard_map/ppermute | solution.py:783
  341.3 51.5 %collective-permute-start.23 = (bf16[384,1024]{1,0:T(8,128)(2,1)}, bf16[384,1024]{1,0:T(8,128)(2,1)}, u32[]{:S(2)}, u32[]{:S(2)}) collective-permute-start(bf16[384,1024]{1,0:T(8,128)(2,1)} %get-tuple-element.189), channel_id=1, source_target_pairs={{0,2},{2,0},{1,3},{3,1},{4,6},{6,4},{5,7},{7,5},{8,10},{10,8},{9,1... | collective-permute-start | bytes 2359304 | tf_op jit(solution)/shard_map/ppermute | solution.py:783
  412.9 19.8 %collective-permute-start.25 = (bf16[384,1024]{1,0:T(8,128)(2,1)}, bf16[384,1024]{1,0:T(8,128)(2,1)S(1)}, u32[]{:S(2)}, u32[]{:S(2)}) collective-permute-start(bf16[384,1024]{1,0:T(8,128)(2,1)} %get-tuple-element.199), channel_id=1, source_target_pairs={{0,2},{2,0},{1,3},{3,1},{4,6},{6,4},{5,7},{7,5},{8,10},{10,8},{9,1... | collective-permute-start | bytes 2359304 | tf_op jit(solution)/shard_map/ppermute | solution.py:783
  434.2 52.6 %all-to-all-start.4 = ((bf16[32,35,768]{2,1,0:T(8,128)(2,1)}), bf16[32,35,768]{2,1,0:T(8,128)(2,1)S(1)}, u32[]{:S(2)}, u32[]{:S(2)}) async-start(bf16[32,35,768]{2,1,0:T(8,128)(2,1)} %pad_maximum_fusion), calls=%async_computation.5 | async-start | bytes 3932160 | tf_op jit(solution)/shard_map/all_to_all | solution.py:1036
  451.1 14.8 %collective-permute-start.28 = (bf16[2,32,2048]{2,1,0:T(8,128)(2,1)S(1)}, bf16[2,32,2048]{2,1,0:T(8,128)(2,1)S(1)}, u32[]{:S(2)}, u32[]{:S(2)}) collective-permute-start(bf16[2,32,2048]{2,1,0:T(8,128)(2,1)S(1)} %bitcast.195), channel_id=1, source_target_pairs={{0,2},{2,0},{1,3},{3,1},{4,6},{6,4},{5,7},{7,5},{8,10},{10,8},{9,1... | collective-permute-start | bytes 786440 | tf_op jit(solution)/shard_map/ppermute | solution.py:783
  454.3 53.9 %collective-permute-start.27 = (bf16[768,1024]{1,0:T(8,128)(2,1)}, bf16[768,1024]{1,0:T(8,128)(2,1)}, u32[]{:S(2)}, u32[]{:S(2)}) collective-permute-start(bf16[768,1024]{1,0:T(8,128)(2,1)} %slice_bitcast_fusion), channel_id=1, source_target_pairs={{0,1},{1,0},{2,3},{3,2},{4,5},{5,4},{6,7},{7,6},{8,9},{9,8},{10,11... | collective-permute-start | bytes 4718600 | tf_op jit(solution)/shard_map/ppermute | solution.py:783
  454.3 32.5 %collective-permute-start.26 = (bf16[384,1024]{1,0:T(8,128)(2,1)S(1)}, bf16[384,1024]{1,0:T(8,128)(2,1)}, u32[]{:S(2)}, u32[]{:S(2)}) collective-permute-start(bf16[384,1024]{1,0:T(8,128)(2,1)S(1)} %copy-done.31), channel_id=1, source_target_pairs={{0,2},{2,0},{1,3},{3,1},{4,6},{6,4},{5,7},{7,5},{8,10},{10,8},{9,1... | collective-permute-start | bytes 2359304 | tf_op jit(solution)/shard_map/ppermute | solution.py:783
  503.4 13.0 %all-to-all-start.5 = ((f32[32,8,128]{2,1,0:T(8,128)}), f32[32,8,128]{2,1,0:T(8,128)S(1)}, u32[]{:S(2)}, u32[]{:S(2)}) async-start(f32[32,8,128]{2,1,0:T(8,128)} %broadcast_in_dim.37), calls=%async_computation.6 | async-start | bytes 262144 | tf_op jit(solution)/shard_map/all_to_all | solution.py:1060
  (67 other events, 325.2 us)
Sparse Core Ops, SparseCore 0:
  28.0 49.8 all-gather.2
  80.6 94.5 all-gather.4
  265.4 139.6 reduce-scatter.1

commit v14 on v13

--- a/solution.py
+++ b/solution.py
@@ -365,7 +365,8 @@
         rows = []
         for clip in range(clips):
             for pair in range(pairs):
-                one, two = mine[clip, pair].astype(f32), other[clip, pair].astype(f32)
+                kind = bf16 if shard % 16 == 0 else f32
+                one, two = mine[clip, pair].astype(kind), other[clip, pair].astype(kind)
                 rows += [jnp.where(low, one, two), jnp.where(low, two, one)]
         proj[...] = jnp.transpose(jnp.concatenate(rows, axis=0)).astype(bf16)
 
@@ -603,7 +604,7 @@
 
     @pl.when(step == pl.num_programs(0) - 1)
     def _():
-        proj_raw[...] = jnp.transpose(raw_sum[...]).astype(bf16)
+        proj_raw[...] = jnp.transpose(raw_sum[...].astype(bf16))
 
 
 def middle_back(order, into, tokens, cotangent, att_out, mod, parts, proj):
@@ -697,7 +698,7 @@
 
         @pl.when(step == pl.num_programs(0) - 1)
         def _():
-            raw[...] = jnp.transpose(total[...]).astype(bf16)
+            raw[...] = jnp.transpose(total[...].astype(bf16))
 
 
 def first_back(pieces, mod, dq, dk, dv, weight, offset, sums=None):
@@ -893,12 +894,14 @@
         mod_mine.reshape(clips, 1, frames, part), (clips, rows, frames, part)
     )
     mod = lax.all_to_all(mod_mine.reshape(devices, frames, part), both, 0, 0, tiled=True)
-    mod = mod.transpose(1, 0, 2).reshape(frames, 6, width)
 
     units = widen_weight.shape[1]
     feed_mine = jnp.stack([widen_weight.astype(bf16), narrow_weight.T.astype(bf16)])
     feed_mine = feed_mine.reshape(2, shard, 2, units // 2).transpose(2, 0, 1, 3)
-    feed_mine = relative(trade(relative(feed_mine, far), "x", 2), far)
+    feed_mine = trade(relative(feed_mine, far), "x", 2)
+    feed_mine, mod = lax.optimization_barrier((feed_mine, mod))
+    feed_mine = relative(feed_mine, far)
+    mod = mod.transpose(1, 0, 2).reshape(frames, 6, width)
     feed_mine, attend_full, mod, tok2_two = lax.optimization_barrier(
         (feed_mine, attend_full, mod, tok2_two)
     )
@@ -1058,7 +1061,7 @@
     reduced = [adaptive_sum, offsets_sum, attend_sum, project_sum, widen_sum, narrow_sum]
     squares = sum((jnp.sum(item * item) for item in reduced))
     squares = lax.all_to_all(
-        jnp.broadcast_to(squares, (devices, 8, 128)), both, 0, 0, tiled=True
+        jnp.broadcast_to(squares, (devices, 1, 128)), both, 0, 0, tiled=True
     )
     gradient_norm = jnp.sqrt(jnp.sum(squares[:, 0, 0]))
     factor = clip_limit / jnp.maximum(gradient_norm, clip_limit)

time: 547 us -> 544 us (level)
    ppermute x29, waiting for transfers between devices: 41.2 us -> 56.4 us  [swap(): lax.ppermute(value, axis, [(place, place ^ step) for place in range(size)])]
    all_to_all x1, waiting for transfers between devices: 18.8 us -> 4.11 us  [local(): lax.all_to_all(mod_mine.reshape(devices, frames, part), both, 0, 0, tiled...]
  transfers between devices with their start and end apart: 38 -> 38, of which waited for: 10 -> 11; matrix products, arithmetic and copies ran while one was open for 10% -> 10% of each run, Pallas kernels for 59% -> 59%
where the time goes in v14:
time: 544 us; the launch traced here: 537 us
  Pallas kernels  318 us (58%)
  waiting for transfers between devices  66.3 us (12%)
  starting transfers between devices  57.2 us (11%)
  other arithmetic  37.5 us (7%)
  local copies, waits for them, and re-layouts  33.9 us (6%)
  between operations  21.9 us (4%)
    pallas_call x2, Pallas kernels, attend_back(): pl.pallas_call(functools.partial(attend_back_kernel, heads, last), grid=(...  99.3 us
    ppermute x29, waiting for transfers between devices, swap(): lax.ppermute(value, axis, [(place, place ^ step) for place in range(size)])  56.4 us
    pallas_call x2, Pallas kernels, attend(): pl.pallas_call(functools.partial(attend_kernel, heads), grid=(count // bl...  55 us
    pallas_call x4, Pallas kernels, feed_forward(): pl.pallas_call(feed_kernel, grid=(units // block,), in_specs=[spec, flat,...  54.2 us
    pallas_call x2, Pallas kernels, first_back(): pl.pallas_call(functools.partial(first_back_kernel, last, [place for _, p...  27.4 us
    ppermute x29, starting transfers between devices, swap(): lax.ppermute(value, axis, [(place, place ^ step) for place in range(size)])  26.2 us
    pallas_call x1, Pallas kernels, feed_weights(): pl.pallas_call(functools.partial(feed_weight_kernel, len(hidden)), grid=(...  21 us
    pallas_call x1, Pallas kernels, middle_back(): pl.pallas_call(middle_kernel, grid=(frames // chunk,), in_specs=[whole(pl...  17.4 us
  transfers between devices with their start and end apart: 38, of which 11 were waited for; matrix products, arithmetic and copies ran while one was open for 10% of the time, Pallas kernels for 59%

profile of v14, /device:TPU:0, one launch (start us, length us, event | category | flops | bytes accessed | tf_op | source)
XLA Modules:
  0.0 536.9 jit_solution(8512525681544256005)
XLA Ops:
  9.5 2.4 collective-permute-start.5
  18.7 5.8 %all-to-all-start = ((bf16[8,12,1024]{2,1,0:T(8,128)(2,1)}), bf16[8,12,1024]{2,1,0:T(8,128)(2,1)S(1)}, u32[]{:S(2)}, u32[]{:S(2)}) async-start(bf16[8,12,1024]{2,1,0:T(8,128)(2,1)} %broadcast_in_dim.31), calls=%async_computation | async-start | bytes 524288 | tf_op jit(solution)/shard_map/all_to_all | solution.py:884
  34.7 5.7 %all-to-all-start.1 = ((f32[32,12,192]{2,1,0:T(8,128)}), f32[32,12,192]{2,1,0:T(8,128)S(1)}, u32[]{:S(2)}, u32[]{:S(2)}) async-start(f32[32,12,192]{2,1,0:T(8,128)} %bitcast.14), calls=%async_computation.1 | async-start | bytes 1048576 | tf_op jit(solution)/shard_map/all_to_all | solution.py:896
  43.7 9.4 %collective-permute-done.1 = bf16[2,32,2048]{2,1,0:T(8,128)(2,1)S(1)} collective-permute-done((bf16[2,32,2048]{2,1,0:T(8,128)(2,1)S(1)}, bf16[2,32,2048]{2,1,0:T(8,128)(2,1)S(1)}, u32[]{:S(2)}, u32[]{:S(2)}) %collective-permute-start.1) | collective-permute-done | bytes 262176 | tf_op jit(solution)/shard_map/ppermute | solution.py:784
  56.1 4.1 all-to-all-done.1
  63.6 11.8 %collective-permute-done.6.refs_5_.refs_1_ = bf16[400,1024]{1,0:T(8,128)(2,1)} collective-permute-done((bf16[400,1024]{1,0:T(8,128)(2,1)S(1)}, bf16[400,1024]{1,0:T(8,128)(2,1)}, u32[]{:S(2)}, u32[]{:S(2)}) %collective-permute-start.6) | collective-permute-done | bytes 819232 | tf_op jit(solution)/shard_map/ppermute | solution.py:784
  75.4 3.3 all-gather.3.cloned.1.call-done
  85.8 3.6 all-to-all-start.2
  94.7 15.0 %shard_map.487.q_ref.k_ref.v_ref = bf16[768,3072]{1,0:T(8,128)(2,1)} custom-call(bf16[784,1024]{1,0:T(8,128)(2,1)} %fusion.1.refs_0_.refs_1_, bf16[784,1024]{1,0:T(8,128)(2,1)} %fusion.1.refs_0_.refs_1_, bf16[784,1024]{1,0:T(8,128)(2,1)} %collective-permute-done.refs_2_.refs_3_, bf16[784,1024]{1,0:T(8,128)(2,1)} %collective-permute-done.refs_2_.refs_3_, ...), custom_call_target="tpu_custom_call" | custom-call | flops 4831838208 | bytes 12582912 | tf_op jit(solution)/shard_map/pallas_call | solution.py:144
  110.3 27.5 %shard_map.488 = (bf16[2,256,768]{2,1,0:T(8,128)(2,1)}, f32[4,1536]{1,0:T(4,128)}) custom-call(bf16[768,3072]{1,0:T(8,128)(2,1)} %shard_map.487.q_ref.k_ref.v_ref, bf16[768,3072]{1,0:T(8,128)(2,1)} %shard_map.487.q_ref.k_ref.v_ref, bf16[768,3072]{1,0:T(8,128)(2,1)} %shard_map.487.q_ref.k_ref.v_ref, f32[1,3072]{1,0:T(1,128)} %compare_select_fusion.bias), custom_call_target="tpu_custom_call" | custom-call | flops 19327352832 | bytes 3145728 | tf_op jit(solution)/shard_map/pallas_call | solution.py:198
  141.4 27.5 %shard_map.489 = (bf16[2,256,768]{2,1,0:T(8,128)(2,1)}, f32[4,1536]{1,0:T(4,128)}) custom-call(bf16[768,3072]{1,0:T(8,128)(2,1)} %shard_map.487.q_ref.k_ref.v_ref, bf16[768,3072]{1,0:T(8,128)(2,1)} %shard_map.487.q_ref.k_ref.v_ref, bf16[768,3072]{1,0:T(8,128)(2,1)} %shard_map.487.q_ref.k_ref.v_ref, f32[1,3072]{1,0:T(1,128)} %compare_select_fusion.bias), custom_call_target="tpu_custom_call" | custom-call | flops 19327352832 | bytes 3145728 | tf_op jit(solution)/shard_map/pallas_call | solution.py:198
  173.4 10.2 %shard_map.490 = (f32[12,64,1024]{2,1,0:T(8,128)}, bf16[384,1024]{1,0:T(8,128)(2,1)}, bf16[384,1024]{1,0:T(8,128)(2,1)}, bf16[768,1024]{1,0:T(8,128)(2,1)}, bf16...) custom-call(s32[5]{0:T(128)} %pad_add_fusion.order, bf16[2,256,768]{2,1,0:T(8,128)(2,1)} %get-tuple-element.147.a0.out_ref, ...), custom_call_target="tpu_custom_call" | custom-call | flops 1610612736 | bytes 11010048 | tf_op jit(solution)/shard_map/pallas_call | solution.py:409
  183.8 13.8 %shard_map.491 = (f32[384,1024]{1,0:T(8,128)}, f32[384,1024]{1,0:T(8,128)}, bf16[384,2048]{1,0:T(8,128)(2,1)}, bf16[384,2048]{1,0:T(8,128)(2,1)}, f32[6,1,1024]{2,1,0:T(1,128)}) custom-call(bf16[16,2,2,32,2048]{4,3,2,1,0:T(8,128)(2,1)} %bitcast.206, bf16[384,1024]{1,0:T(8,128)(2,1)} %get-tuple-element.151.hidden.refs_0_, ...), custom_call_target="tpu_custom_call" | custom-call | flops 6442450944 | bytes 11534336 | tf_op jit(solution)/shard_map/pallas_call | solution.py:506
  199.5 13.8 %shard_map.492 = (f32[384,1024]{1,0:T(8,128)}, f32[384,1024]{1,0:T(8,128)}, bf16[384,2048]{1,0:T(8,128)(2,1)}, bf16[384,2048]{1,0:T(8,128)(2,1)}, f32[6,1,1024]{2,1,0:T(1,128)}) custom-call(bf16[16,2,2,32,2048]{4,3,2,1,0:T(8,128)(2,1)} %bitcast.207, bf16[384,1024]{1,0:T(8,128)(2,1)} %get-tuple-element.159.hidden.refs_1_, ...), custom_call_target="tpu_custom_call" | custom-call | flops 6442450944 | bytes 11534336 | tf_op jit(solution)/shard_map/pallas_call | solution.py:506
  214.1 13.2 %shard_map.493 = (bf16[384,1024]{1,0:T(8,128)(2,1)}, bf16[384,1024]{1,0:T(8,128)(2,1)}, bf16[384,2048]{1,0:T(8,128)(2,1)}, bf16[384,2048]{1,0:T(8,128)(2,1)}, f32[6,1,1024]{2,1,0:T(1,128)}) custom-call(bf16[16,2,2,32,2048]{4,3,2,1,0:T(8,128)(2,1)} %bitcast.208, bf16[384,1024]{1,0:T(8,128)(2,1)} %copy-done.57, ...), custom_call_target="tpu_custom_call" | custom-call | flops 6442450944 | bytes 11534336 | tf_op jit(solution)/shard_map/pallas_call | solution.py:506
  228.5 13.4 %shard_map.494 = (bf16[384,1024]{1,0:T(8,128)(2,1)}, bf16[384,1024]{1,0:T(8,128)(2,1)}, bf16[384,2048]{1,0:T(8,128)(2,1)}, bf16[384,2048]{1,0:T(8,128)(2,1)}, f32[6,1,1024]{2,1,0:T(1,128)}) custom-call(bf16[16,2,2,32,2048]{4,3,2,1,0:T(8,128)(2,1)} %bitcast.209, bf16[384,1024]{1,0:T(8,128)(2,1)} %copy-done.58, ...), custom_call_target="tpu_custom_call" | custom-call | flops 6442450944 | bytes 11534336 | tf_op jit(solution)/shard_map/pallas_call | solution.py:506
  243.8 21.0 %shard_map.495 = bf16[16,2,2,32,2048]{4,3,2,1,0:T(8,128)(2,1)} custom-call(bf16[384,1024]{1,0:T(8,128)(2,1)} %get-tuple-element.151.hidden.refs_0_, bf16[384,1024]{1,0:T(8,128)(2,1)} %get-tuple-element.159.hidden.refs_1_, bf16[384,1024]{1,0:T(8,128)(2,1)} %copy-done.57, bf16[384,1024]{1,0:T(8,128)(2,1)} %copy-done.58, ...), custom_call_target="tpu_custom_call" | custom-call | flops 12884901888 | bytes 20971520 | tf_op jit(solution)/shard_map/pallas_call | solution.py:557
  266.0 17.4 %shard_map.496 = (f32[12,64,1024]{2,1,0:T(8,128)}, f32[12,3,1024]{2,1,0:T(4,128)}, bf16[256,768]{1,0:T(8,128)(2,1)}, bf16[256,768]{1,0:T(8,128)(2,1)}, bf16[256,...) custom-call(s32[5]{0:T(128)} %pad_add_fusion.order, f32[384,1024]{1,0:T(8,128)} %get-tuple-element.153.into1, ...), custom_call_target="tpu_custom_call" | custom-call | flops 3221225472 | bytes 18874368 | tf_op jit(solution)/shard_map/pallas_call | solution.py:620
  283.5 4.7 all-to-all-start.3
  290.1 48.4 %shard_map.497 = (bf16[256,1536]{1,0:T(8,128)(2,1)}, f32[256,3072]{1,0:T(8,128)}, f32[256,3072]{1,0:T(8,128)}) custom-call(bf16[768,3072]{1,0:T(8,128)(2,1)} %shard_map.487.q_ref.k_ref.v_ref, bf16[768,3072]{1,0:T(8,128)(2,1)} %shard_map.487.q_ref.k_ref.v_ref, bf16[768,3072]{1,0:T(8,128)(2,1)} %shard_map.487.q_ref.k_ref.v_ref, ...), custom_call_target="tpu_custom_call" | custom-call | flops 41070624768 | bytes 6291456 | tf_op jit(solution)/shard_map/pallas_call | solution.py:339
  340.6 51.0 %shard_map.498 = (bf16[256,1536]{1,0:T(8,128)(2,1)}, bf16[256,3072]{1,0:T(8,128)(2,1)}, bf16[256,3072]{1,0:T(8,128)(2,1)}) custom-call(bf16[768,3072]{1,0:T(8,128)(2,1)} %shard_map.487.q_ref.k_ref.v_ref, bf16[768,3072]{1,0:T(8,128)(2,1)} %shard_map.487.q_ref.k_ref.v_ref, bf16[768,3072]{1,0:T(8,128)(2,1)} %shard_map.487.q_ref.k_ref.v_ref, ...), custom_call_target="tpu_custom_call" | custom-call | flops 41070624768 | bytes 6291456 | tf_op jit(solution)/shard_map/pallas_call | solution.py:339
  391.6 13.0 %shard_map.499 = (bf16[2,768,1024]{2,1,0:T(8,128)(2,1)}, f32[768,1024]{1,0:T(8,128)}, f32[12,2,1024]{2,1,0:T(2,128)}) custom-call(bf16[384,1024]{1,0:T(8,128)(2,1)} %collective-permute-done.2.refs_4_.refs_0_, bf16[400,1024]{1,0:T(8,128)(2,1)} %collective-permute-done.6.refs_5_.refs_1_, bf16[384,1024]{1,0:T(8,128)(2,1)} %collective-permute-done.7.refs_6_.refs_2_, ...), custom_call_target="tpu_custom_call" | custom-call | flops 4831838208 | bytes 9437184 | tf_op jit(solution)/shard_map/pallas_call | solution.py:725
  406.5 3.3 collective-permute-done.24
  413.2 14.4 %shard_map.500 = (bf16[2,768,1024]{2,1,0:T(8,128)(2,1)}, bf16[1024,768]{1,0:T(8,128)(2,1)}, f32[12,2,1024]{2,1,0:T(2,128)}) custom-call(bf16[784,1024]{1,0:T(8,128)(2,1)} %fusion.1.refs_0_.refs_1_, bf16[784,1024]{1,0:T(8,128)(2,1)} %fusion.1.refs_0_.refs_1_, bf16[784,1024]{1,0:T(8,128)(2,1)} %collective-permute-done.refs_2_.refs_3_, ...), custom_call_target="tpu_custom_call" | custom-call | flops 4831838208 | bytes 9437184 | tf_op jit(solution)/shard_map/pallas_call | solution.py:725
  433.0 5.7 %all-to-all-start.4 = ((bf16[32,35,768]{2,1,0:T(8,128)(2,1)}), bf16[32,35,768]{2,1,0:T(8,128)(2,1)S(1)}, u32[]{:S(2)}, u32[]{:S(2)}) async-start(bf16[32,35,768]{2,1,0:T(8,128)(2,1)} %pad_maximum_fusion), calls=%async_computation.5 | async-start | bytes 3932160 | tf_op jit(solution)/shard_map/all_to_all | solution.py:1039
  438.7 2.5 shard_map.502
  441.2 5.3 shard_map.501
  453.3 11.4 %collective-permute-done.28 = bf16[2,32,2048]{2,1,0:T(8,128)(2,1)S(1)} collective-permute-done((bf16[2,32,2048]{2,1,0:T(8,128)(2,1)S(1)}, bf16[2,32,2048]{2,1,0:T(8,128)(2,1)S(1)}, u32[]{:S(2)}, u32[]{:S(2)}) %collective-permute-start.28) | collective-permute-done | bytes 262176 | tf_op jit(solution)/shard_map/ppermute | solution.py:784
  470.3 15.2 %collective-permute-done.26.far2 = bf16[384,1024]{1,0:T(8,128)(2,1)} collective-permute-done((bf16[384,1024]{1,0:T(8,128)(2,1)S(1)}, bf16[384,1024]{1,0:T(8,128)(2,1)}, u32[]{:S(2)}, u32[]{:S(2)}) %collective-permute-start.26) | collective-permute-done | bytes 786464 | tf_op jit(solution)/shard_map/ppermute | solution.py:784
  493.9 2.6 shard_map.504
  502.1 4.8 all-to-all-start.5
  506.9 7.9 %shard_map.503 = f32[12,64,1024]{2,1,0:T(8,128)} custom-call(bf16[12,64,1024]{2,1,0:T(8,128)(2,1)} %bitcast.158, f32[12,6,1024]{2,1,0:T(8,128)} %reshape.444.refs_8_.mod.refs_4_, f32[12,64,1024]{2,1,0:T(8,128)} %get-tuple-element.220.middle_grad, bf16[2,768,1024]{2,1,0:T(8,128)(2,1)} %get-tuple-element.221.one, ...), custom_call_target="tpu_custom_call" | custom-call | flops 15728640 | bytes 12582912 | tf_op jit(solution)/shard_map/pallas_call | solution.py:755
  (318 shorter events, 105.9 us)
Async XLA Ops:
  9.5 16.5 %collective-permute-start.5 = (bf16[32,768]{1,0:T(8,128)(2,1)S(1)}, bf16[32,768]{1,0:T(8,128)(2,1)S(1)}, u32[]{:S(2)}, u32[]{:S(2)}) collective-permute-start(bf16[32,768]{1,0:T(8,128)(2,1)S(1)} %get-tuple-element.283), channel_id=1, source_target_pairs={{0,3},{1,2},{2,1},{3,0},{4,7},{5,6},{6,5},{7,4},{8,11},{9,10},{10,... | collective-permute-start | bytes 147464 | tf_op jit(solution)/shard_map/ppermute | solution.py:784
  11.9 14.0 %collective-permute-start.4 = (bf16[32,768]{1,0:T(8,128)(2,1)S(1)}, bf16[32,768]{1,0:T(8,128)(2,1)S(1)}, u32[]{:S(2)}, u32[]{:S(2)}) collective-permute-start(bf16[32,768]{1,0:T(8,128)(2,1)S(1)} %get-tuple-element.284), channel_id=1, source_target_pairs={{0,2},{1,3},{2,0},{3,1},{4,6},{5,7},{6,4},{7,5},{8,10},{9,11},{10,... | collective-permute-start | bytes 147464 | tf_op jit(solution)/shard_map/ppermute | solution.py:784
  12.6 13.4 %collective-permute-start.3 = (bf16[32,768]{1,0:T(8,128)(2,1)S(1)}, bf16[32,768]{1,0:T(8,128)(2,1)S(1)}, u32[]{:S(2)}, u32[]{:S(2)}) collective-permute-start(bf16[32,768]{1,0:T(8,128)(2,1)S(1)} %get-tuple-element.285), channel_id=1, source_target_pairs={{0,1},{1,0},{2,3},{3,2},{4,5},{5,4},{6,7},{7,6},{8,9},{9,8},{10,11... | collective-permute-start | bytes 147464 | tf_op jit(solution)/shard_map/ppermute | solution.py:784
  13.5 20.2 %collective-permute-start.2 = (bf16[384,1024]{1,0:T(8,128)(2,1)}, bf16[384,1024]{1,0:T(8,128)(2,1)}, u32[]{:S(2)}, u32[]{:S(2)}) collective-permute-start(bf16[384,1024]{1,0:T(8,128)(2,1)} %bitcast.13), channel_id=1, source_target_pairs={{0,2},{2,0},{1,3},{3,1},{4,6},{6,4},{5,7},{7,5},{8,10},{10,8},{9,1... | collective-permute-start | bytes 2359304 | tf_op jit(solution)/shard_map/ppermute | solution.py:784
  18.7 14.8 %all-to-all-start = ((bf16[8,12,1024]{2,1,0:T(8,128)(2,1)}), bf16[8,12,1024]{2,1,0:T(8,128)(2,1)S(1)}, u32[]{:S(2)}, u32[]{:S(2)}) async-start(bf16[8,12,1024]{2,1,0:T(8,128)(2,1)} %broadcast_in_dim.31), calls=%async_computation | async-start | bytes 524288 | tf_op jit(solution)/shard_map/all_to_all | solution.py:884
  24.5 54.2 %all-gather.3.cloned.1.call-start = ((), (), s32[]{:S(2)}) async-start(), calls=%async_computation.7 | async-start | bytes 1769472 | tf_op jit(solution)/shard_map/all_gather | solution.py:881
  34.7 25.6 %all-to-all-start.1 = ((f32[32,12,192]{2,1,0:T(8,128)}), f32[32,12,192]{2,1,0:T(8,128)S(1)}, u32[]{:S(2)}, u32[]{:S(2)}) async-start(f32[32,12,192]{2,1,0:T(8,128)} %bitcast.14), calls=%async_computation.1 | async-start | bytes 1048576 | tf_op jit(solution)/shard_map/all_to_all | solution.py:896
  40.4 143.4 %all-gather.5.cloned.1.call-start = ((), (), s32[]{:S(2)}) async-start(), calls=%async_computation.8 | async-start | bytes 8912896 | tf_op jit(solution)/shard_map/all_gather | solution.py:910
  41.9 11.2 %collective-permute-start.1 = (bf16[2,32,2048]{2,1,0:T(8,128)(2,1)S(1)}, bf16[2,32,2048]{2,1,0:T(8,128)(2,1)S(1)}, u32[]{:S(2)}, u32[]{:S(2)}) collective-permute-start(bf16[2,32,2048]{2,1,0:T(8,128)(2,1)S(1)} %bitcast.197), channel_id=1, source_target_pairs={{0,2},{2,0},{1,3},{3,1},{4,6},{6,4},{5,7},{7,5},{8,10},{10,8},{9,1... | collective-permute-start | bytes 786440 | tf_op jit(solution)/shard_map/ppermute | solution.py:784
  54.7 20.7 %collective-permute-start.6 = (bf16[400,1024]{1,0:T(8,128)(2,1)S(1)}, bf16[400,1024]{1,0:T(8,128)(2,1)}, u32[]{:S(2)}, u32[]{:S(2)}) collective-permute-start(bf16[400,1024]{1,0:T(8,128)(2,1)S(1)} %slice.177), channel_id=1, source_target_pairs={{0,2},{2,0},{1,3},{3,1},{4,6},{6,4},{5,7},{7,5},{8,10},{10,8},{9,1... | collective-permute-start | bytes 2457608 | tf_op jit(solution)/shard_map/ppermute | solution.py:784
  79.8 12.6 %collective-permute-start.8 = (bf16[400,1024]{1,0:T(8,128)(2,1)}, bf16[400,1024]{1,0:T(8,128)(2,1)S(1)}, u32[]{:S(2)}, u32[]{:S(2)}) collective-permute-start(bf16[400,1024]{1,0:T(8,128)(2,1)} %collective-permute-done.6.refs_5_.refs_1_), channel_id=1, source_target_pairs={{0,1},{1,0},{2,3},{3,2},{4,5},{5,4},{6,7},{7,6},{8,9},{9,8},{10,11... | collective-permute-start | bytes 2457608 | tf_op jit(solution)/shard_map/ppermute | solution.py:784
  85.8 52.0 %all-to-all-start.2 = ((bf16[8,2,32,1024]{3,2,1,0:T(8,128)(2,1)}), bf16[8,2,32,1024]{3,2,1,0:T(8,128)(2,1)S(1)}, u32[]{:S(2)}, u32[]{:S(2)}) async-start(bf16[8,2,32,1024]{3,2,1,0:T(8,128)(2,1)} %broadcast_in_dim.36), calls=%async_computation.2 | async-start | bytes 2097152 | tf_op jit(solution)/shard_map/all_to_all | solution.py:935
  89.4 342.1 %reduce-scatter.2.cloned.1.call-start = ((), (), s32[]{:S(2)}) async-start(), calls=%async_computation.9 | async-start | bytes 8912896 | tf_op jit(solution)/shard_map/reduce_scatter | solution.py:977
  90.9 46.9 %collective-permute-start.9 = (bf16[12,64,1024]{2,1,0:T(8,128)(2,1)S(1)}, bf16[12,64,1024]{2,1,0:T(8,128)(2,1)}, u32[]{:S(2)}, u32[]{:S(2)}) collective-permute-start(bf16[12,64,1024]{2,1,0:T(8,128)(2,1)S(1)} %bitcast.167), channel_id=1, source_target_pairs={{0,2},{2,0},{1,3},{3,1},{4,6},{6,4},{5,7},{7,5},{8,10},{10,8},{9,1... | collective-permute-start | bytes 4718600 | tf_op jit(solution)/shard_map/ppermute | solution.py:784
  139.4 31.9 %collective-permute-start.14 = (bf16[256,768]{1,0:T(8,128)(2,1)S(1)}, bf16[256,768]{1,0:T(8,128)(2,1)S(1)}, u32[]{:S(2)}, u32[]{:S(2)}) collective-permute-start(bf16[256,768]{1,0:T(8,128)(2,1)S(1)} %get-tuple-element.260), channel_id=1, source_target_pairs={{0,3},{1,2},{2,1},{3,0},{4,7},{5,6},{6,5},{7,4},{8,11},{9,10},{10,... | collective-permute-start | bytes 1179656 | tf_op jit(solution)/shard_map/ppermute | solution.py:784
  139.9 31.5 %collective-permute-start.13 = (bf16[256,768]{1,0:T(8,128)(2,1)S(1)}, bf16[256,768]{1,0:T(8,128)(2,1)S(1)}, u32[]{:S(2)}, u32[]{:S(2)}) collective-permute-start(bf16[256,768]{1,0:T(8,128)(2,1)S(1)} %get-tuple-element.261), channel_id=1, source_target_pairs={{0,2},{1,3},{2,0},{3,1},{4,6},{5,7},{6,4},{7,5},{8,10},{9,11},{10,... | collective-permute-start | bytes 1179656 | tf_op jit(solution)/shard_map/ppermute | solution.py:784
  141.3 27.6 %collective-permute-start.11 = (bf16[8,2,32,1024]{3,2,1,0:T(8,128)(2,1)S(1)}, bf16[8,2,32,1024]{3,2,1,0:T(8,128)(2,1)S(1)}, u32[]{:S(2)}, u32[]{:S(2)}) collective-permute-start(bf16[8,2,32,1024]{3,2,1,0:T(8,128)(2,1)S(1)} %all-to-all-done.2.mine), channel_id=1, source_target_pairs={{0,1},{1,0},{2,3},{3,2},{4,5},{5,4},{6,7},{7,6},{8,9},{9,8},{10,11... | collective-permute-start | bytes 3145736 | tf_op jit(solution)/shard_map/ppermute | solution.py:784
  183.5 29.7 %collective-permute-start.15 = (bf16[384,1024]{1,0:T(8,128)(2,1)}, bf16[384,1024]{1,0:T(8,128)(2,1)S(1)}, u32[]{:S(2)}, u32[]{:S(2)}) collective-permute-start(bf16[384,1024]{1,0:T(8,128)(2,1)} %get-tuple-element.151.hidden.refs_0_), channel_id=1, source_target_pairs={{0,2},{2,0},{1,3},{3,1},{4,6},{6,4},{5,7},{7,5},{8,10},{10,8},{9,1... | collective-permute-start | bytes 2359304 | tf_op jit(solution)/shard_map/ppermute | solution.py:784
  197.6 30.0 %collective-permute-start.16 = (bf16[384,1024]{1,0:T(8,128)(2,1)S(1)}, bf16[384,1024]{1,0:T(8,128)(2,1)S(1)}, u32[]{:S(2)}, u32[]{:S(2)}) collective-permute-start(bf16[384,1024]{1,0:T(8,128)(2,1)S(1)} %copy-done.56), channel_id=1, source_target_pairs={{0,2},{2,0},{1,3},{3,1},{4,6},{6,4},{5,7},{7,5},{8,10},{10,8},{9,1... | collective-permute-start | bytes 2359304 | tf_op jit(solution)/shard_map/ppermute | solution.py:784
  227.4 37.4 %collective-permute-start.17 = (bf16[384,1024]{1,0:T(8,128)(2,1)}, bf16[384,1024]{1,0:T(8,128)(2,1)S(1)}, u32[]{:S(2)}, u32[]{:S(2)}) collective-permute-start(bf16[384,1024]{1,0:T(8,128)(2,1)} %get-tuple-element.171), channel_id=1, source_target_pairs={{0,2},{2,0},{1,3},{3,1},{4,6},{6,4},{5,7},{7,5},{8,10},{10,8},{9,1... | collective-permute-start | bytes 2359304 | tf_op jit(solution)/shard_map/ppermute | solution.py:784
  241.9 22.9 %collective-permute-start.18 = (bf16[384,1024]{1,0:T(8,128)(2,1)}, bf16[384,1024]{1,0:T(8,128)(2,1)S(1)}, u32[]{:S(2)}, u32[]{:S(2)}) collective-permute-start(bf16[384,1024]{1,0:T(8,128)(2,1)} %get-tuple-element.172), channel_id=1, source_target_pairs={{0,2},{2,0},{1,3},{3,1},{4,6},{6,4},{5,7},{7,5},{8,10},{10,8},{9,1... | collective-permute-start | bytes 2359304 | tf_op jit(solution)/shard_map/ppermute | solution.py:784
  283.5 108.1 %all-to-all-start.3 = ((bf16[32,32,1024]{2,1,0:T(8,128)(2,1)}), bf16[32,32,1024]{2,1,0:T(8,128)(2,1)}, u32[]{:S(2)}, u32[]{:S(2)}) async-start(bf16[32,32,1024]{2,1,0:T(8,128)(2,1)} %bitcast.185), calls=%async_computation.3 | async-start | bytes 4194304 | tf_op jit(solution)/shard_map/all_to_all | solution.py:988
  288.1 50.3 %collective-permute-start.20 = (bf16[256,768]{1,0:T(8,128)(2,1)S(1)}, bf16[256,768]{1,0:T(8,128)(2,1)}, u32[]{:S(2)}, u32[]{:S(2)}) collective-permute-start(bf16[256,768]{1,0:T(8,128)(2,1)S(1)} %copy-done.60), channel_id=1, source_target_pairs={{0,2},{1,3},{2,0},{3,1},{4,6},{5,7},{6,4},{7,5},{8,10},{9,11},{10,... | collective-permute-start | bytes 1179656 | tf_op jit(solution)/shard_map/ppermute | solution.py:784
  290.1 48.4 %collective-permute-start.21 = (bf16[256,768]{1,0:T(8,128)(2,1)S(1)}, bf16[256,768]{1,0:T(8,128)(2,1)}, u32[]{:S(2)}, u32[]{:S(2)}) collective-permute-start(bf16[256,768]{1,0:T(8,128)(2,1)S(1)} %copy-done.59), channel_id=1, source_target_pairs={{0,3},{1,2},{2,1},{3,0},{4,7},{5,6},{6,5},{7,4},{8,11},{9,10},{10,... | collective-permute-start | bytes 1179656 | tf_op jit(solution)/shard_map/ppermute | solution.py:784
  338.5 53.0 %collective-permute-start.22 = (bf16[384,1024]{1,0:T(8,128)(2,1)}, bf16[384,1024]{1,0:T(8,128)(2,1)S(1)}, u32[]{:S(2)}, u32[]{:S(2)}) collective-permute-start(bf16[384,1024]{1,0:T(8,128)(2,1)} %get-tuple-element.192), channel_id=1, source_target_pairs={{0,2},{2,0},{1,3},{3,1},{4,6},{6,4},{5,7},{7,5},{8,10},{10,8},{9,1... | collective-permute-start | bytes 2359304 | tf_op jit(solution)/shard_map/ppermute | solution.py:784
  340.0 51.5 %collective-permute-start.23 = (bf16[384,1024]{1,0:T(8,128)(2,1)}, bf16[384,1024]{1,0:T(8,128)(2,1)}, u32[]{:S(2)}, u32[]{:S(2)}) collective-permute-start(bf16[384,1024]{1,0:T(8,128)(2,1)} %get-tuple-element.193), channel_id=1, source_target_pairs={{0,2},{2,0},{1,3},{3,1},{4,6},{6,4},{5,7},{7,5},{8,10},{10,8},{9,1... | collective-permute-start | bytes 2359304 | tf_op jit(solution)/shard_map/ppermute | solution.py:784
  411.6 19.8 %collective-permute-start.25 = (bf16[384,1024]{1,0:T(8,128)(2,1)}, bf16[384,1024]{1,0:T(8,128)(2,1)S(1)}, u32[]{:S(2)}, u32[]{:S(2)}) collective-permute-start(bf16[384,1024]{1,0:T(8,128)(2,1)} %get-tuple-element.203), channel_id=1, source_target_pairs={{0,2},{2,0},{1,3},{3,1},{4,6},{6,4},{5,7},{7,5},{8,10},{10,8},{9,1... | collective-permute-start | bytes 2359304 | tf_op jit(solution)/shard_map/ppermute | solution.py:784
  433.0 52.6 %all-to-all-start.4 = ((bf16[32,35,768]{2,1,0:T(8,128)(2,1)}), bf16[32,35,768]{2,1,0:T(8,128)(2,1)S(1)}, u32[]{:S(2)}, u32[]{:S(2)}) async-start(bf16[32,35,768]{2,1,0:T(8,128)(2,1)} %pad_maximum_fusion), calls=%async_computation.5 | async-start | bytes 3932160 | tf_op jit(solution)/shard_map/all_to_all | solution.py:1039
  449.8 14.8 %collective-permute-start.28 = (bf16[2,32,2048]{2,1,0:T(8,128)(2,1)S(1)}, bf16[2,32,2048]{2,1,0:T(8,128)(2,1)S(1)}, u32[]{:S(2)}, u32[]{:S(2)}) collective-permute-start(bf16[2,32,2048]{2,1,0:T(8,128)(2,1)S(1)} %bitcast.195), channel_id=1, source_target_pairs={{0,2},{2,0},{1,3},{3,1},{4,6},{6,4},{5,7},{7,5},{8,10},{10,8},{9,1... | collective-permute-start | bytes 786440 | tf_op jit(solution)/shard_map/ppermute | solution.py:784
  453.0 53.8 %collective-permute-start.27 = (bf16[768,1024]{1,0:T(8,128)(2,1)}, bf16[768,1024]{1,0:T(8,128)(2,1)}, u32[]{:S(2)}, u32[]{:S(2)}) collective-permute-start(bf16[768,1024]{1,0:T(8,128)(2,1)} %slice_bitcast_fusion), channel_id=1, source_target_pairs={{0,1},{1,0},{2,3},{3,2},{4,5},{5,4},{6,7},{7,6},{8,9},{9,8},{10,11... | collective-permute-start | bytes 4718600 | tf_op jit(solution)/shard_map/ppermute | solution.py:784
  453.0 32.5 %collective-permute-start.26 = (bf16[384,1024]{1,0:T(8,128)(2,1)S(1)}, bf16[384,1024]{1,0:T(8,128)(2,1)}, u32[]{:S(2)}, u32[]{:S(2)}) collective-permute-start(bf16[384,1024]{1,0:T(8,128)(2,1)S(1)} %copy-done.31), channel_id=1, source_target_pairs={{0,2},{2,0},{1,3},{3,1},{4,6},{6,4},{5,7},{7,5},{8,10},{10,8},{9,1... | collective-permute-start | bytes 2359304 | tf_op jit(solution)/shard_map/ppermute | solution.py:784
  502.1 12.8 %all-to-all-start.5 = ((f32[32,1,128]{2,1,0:T(1,128)}), f32[32,1,128]{2,1,0:T(1,128)S(1)}, u32[]{:S(2)}, u32[]{:S(2)}) async-start(f32[32,1,128]{2,1,0:T(1,128)} %broadcast_in_dim.37), calls=%async_computation.6 | async-start | bytes 32768 | tf_op jit(solution)/shard_map/all_to_all | solution.py:1063
  (67 other events, 323.9 us)
Sparse Core Ops, SparseCore 0:
  28.0 50.7 all-gather.2
  81.4 92.4 all-gather.4
  265.0 138.8 reduce-scatter.1

commit v15 on v14

--- a/solution.py
+++ b/solution.py
@@ -900,10 +900,14 @@
     feed_mine = feed_mine.reshape(2, shard, 2, units // 2).transpose(2, 0, 1, 3)
     feed_mine = trade(relative(feed_mine, far), "x", 2)
     feed_mine, mod = lax.optimization_barrier((feed_mine, mod))
+    project_mine, mod = lax.optimization_barrier((project_mine, mod))
+    project_full = lax.all_to_all(
+        jnp.broadcast_to(project_mine[None], (clips, 2, shard, width)), "clip", 0, 0, tiled=True
+    )
     feed_mine = relative(feed_mine, far)
     mod = mod.transpose(1, 0, 2).reshape(frames, 6, width)
-    feed_mine, attend_full, mod, tok2_two = lax.optimization_barrier(
-        (feed_mine, attend_full, mod, tok2_two)
+    feed_mine, attend_full, mod, tok2_two, project_full = lax.optimization_barrier(
+        (feed_mine, attend_full, mod, tok2_two, project_full)
     )
     tok3_two = swap(tok2_two, "core", 2, 1)
     attend_turned = attend_full.T
@@ -932,16 +936,10 @@
     across = ((tok2_one, 0), (tok2_two, 0), (tok3_one, 0), (tok3_two, 0))
     qkv = project_qkv(near + across, mod, attend_turned, cosine, sine)
 
-    project_full = lax.all_to_all(
-        jnp.broadcast_to(project_mine[None], (clips, 2, shard, width)), "clip", 0, 0, tiled=True
-    )
-
     cot_far, mod = lax.optimization_barrier((upstream, mod))
     cot_far = swap(cot_far, "x", 2, 1)
     out_far, lse_far = attend(qkv, 1, bias)
-    out_far, qkv, cot_far, project_full = lax.optimization_barrier(
-        (out_far, qkv, cot_far, project_full)
-    )
+    out_far, qkv, cot_far = lax.optimization_barrier((out_far, qkv, cot_far))
     project_near = swap(project_full, "core", 2, 1)
     part2 = swap(out_far[0], ROW, rows, 2)
     part3 = swap(out_far[1], ROW, rows, 3)
@@ -1042,9 +1040,9 @@
         (attend_raw, far_two, block_out, project_sum)
     )
     input_gradient = input_back(own, mod, middle_grad, back_near + (far_one, far_two))
-    small = attend_raw[:, shard : shard + extra].reshape(devices, -1)[:, : frames * part]
-    small = small.astype(f32).reshape(clips, rows, frames, part)
-    mod_grad = jnp.sum(small, axis=1).reshape(clips * frames, part)
+    small = attend_raw[:, shard : shard + extra].astype(f32)
+    small = jnp.sum(small.reshape(clips, rows, extra, 3 * features), axis=1)
+    mod_grad = small.reshape(clips, -1)[:, : frames * part].reshape(clips * frames, part)
     attend_sum = total_over(attend_raw.reshape(clips, rows, shard + extra, 3 * features))
     attend_sum = attend_sum[:, :shard].reshape(rows, shard, 3, features)
     attend_sum = attend_sum.transpose(1, 2, 0, 3).reshape(shard, 3 * width)

time: 544 us -> 579 us (1.064)
  waiting for transfers between devices: 66.3 us -> 88.5 us
  Pallas kernels: 318 us -> 326 us
    all_to_all x1, waiting for transfers between devices: 4.11 us -> 19.4 us  [local(): lax.all_to_all(mod_mine.reshape(devices, frames, part), both, 0, 0, tiled...]
    pallas_call x2, Pallas kernels: 55 us -> 63 us  [attend(): pl.pallas_call(functools.partial(attend_kernel, heads), grid=(count // bl...]
    ppermute x29, waiting for transfers between devices: 56.4 us -> 62.5 us  [swap(): lax.ppermute(value, axis, [(place, place ^ step) for place in range(size)])]
  transfers between devices with their start and end apart: 38 -> 38, of which waited for: 11 -> 11; matrix products, arithmetic and copies ran while one was open for 10% -> 10% of each run, Pallas kernels for 59% -> 57%
where the time goes in v15:
time: 579 us; the launch traced here: 570 us
  Pallas kernels  326 us (56%)
  waiting for transfers between devices  88.5 us (15%)
  starting transfers between devices  54.8 us (9%)
  other arithmetic  40.5 us (7%)
  local copies, waits for them, and re-layouts  35.7 us (6%)
  between operations  21.8 us (4%)
    pallas_call x2, Pallas kernels, attend_back(): pl.pallas_call(functools.partial(attend_back_kernel, heads, last), grid=(...  99.1 us
    pallas_call x2, Pallas kernels, attend(): pl.pallas_call(functools.partial(attend_kernel, heads), grid=(count // bl...  63 us
    ppermute x29, waiting for transfers between devices, swap(): lax.ppermute(value, axis, [(place, place ^ step) for place in range(size)])  62.5 us
    pallas_call x4, Pallas kernels, feed_forward(): pl.pallas_call(feed_kernel, grid=(units // block,), in_specs=[spec, flat,...  54.5 us
    pallas_call x2, Pallas kernels, first_back(): pl.pallas_call(functools.partial(first_back_kernel, last, [place for _, p...  27.4 us
    ppermute x29, starting transfers between devices, swap(): lax.ppermute(value, axis, [(place, place ^ step) for place in range(size)])  24.2 us
    pallas_call x1, Pallas kernels, feed_weights(): pl.pallas_call(functools.partial(feed_weight_kernel, len(hidden)), grid=(...  21 us
    all_to_all x1, waiting for transfers between devices, local(): lax.all_to_all(mod_mine.reshape(devices, frames, part), both, 0, 0, tiled...  19.4 us
  transfers between devices with their start and end apart: 38, of which 11 were waited for; matrix products, arithmetic and copies ran while one was open for 10% of the time, Pallas kernels for 57%

profile of v15, /device:TPU:0, one launch (start us, length us, event | category | flops | bytes accessed | tf_op | source)
XLA Modules:
  0.0 569.7 jit_solution(13826509161212340646)
XLA Ops:
  8.8 2.9 collective-permute-start.6
  25.1 6.1 %all-to-all-start = ((bf16[8,12,1024]{2,1,0:T(8,128)(2,1)}), bf16[8,12,1024]{2,1,0:T(8,128)(2,1)S(1)}, u32[]{:S(2)}, u32[]{:S(2)}) async-start(bf16[8,12,1024]{2,1,0:T(8,128)(2,1)} %broadcast_in_dim.32), calls=%async_computation | async-start | bytes 524288 | tf_op jit(solution)/shard_map/all_to_all | solution.py:884
  40.5 13.1 %collective-permute-done.2.refs_4_.refs_0_ = bf16[384,1024]{1,0:T(8,128)(2,1)S(1)} collective-permute-done((bf16[384,1024]{1,0:T(8,128)(2,1)}, bf16[384,1024]{1,0:T(8,128)(2,1)S(1)}, u32[]{:S(2)}, u32[]{:S(2)}) %collective-permute-start.2) | collective-permute-done | bytes 786464 | tf_op jit(solution)/shard_map/ppermute | solution.py:784
  54.5 5.5 all-to-all-start.1
  63.5 19.4 %all-to-all-done.1 = f32[32,12,192]{2,1,0:T(8,128)S(1)} async-done(((f32[32,12,192]{2,1,0:T(8,128)}), f32[32,12,192]{2,1,0:T(8,128)S(1)}, u32[]{:S(2)}, u32[]{:S(2)}) %all-to-all-start.1) | async-done | bytes 294944 | tf_op jit(solution)/shard_map/all_to_all | solution.py:896
  84.0 4.2 all-to-all-start.2
  94.1 14.3 %collective-permute-done.7.refs_5_.refs_1_ = bf16[400,1024]{1,0:T(8,128)(2,1)} collective-permute-done((bf16[400,1024]{1,0:T(8,128)(2,1)}, bf16[400,1024]{1,0:T(8,128)(2,1)}, u32[]{:S(2)}, u32[]{:S(2)}) %collective-permute-start.7) | collective-permute-done | bytes 819232 | tf_op jit(solution)/shard_map/ppermute | solution.py:784
  108.4 5.5 all-to-all-done.2.mine
  126.2 15.0 %shard_map.487.q_ref.k_ref.v_ref = bf16[768,3072]{1,0:T(8,128)(2,1)} custom-call(bf16[784,1024]{1,0:T(8,128)(2,1)} %copy-done.5, bf16[784,1024]{1,0:T(8,128)(2,1)} %copy-done.5, bf16[784,1024]{1,0:T(8,128)(2,1)} %copy-done.56, bf16[784,1024]{1,0:T(8,128)(2,1)} %copy-done.56, bf16[384,1024]{1,0:T(8,128)(2,1)} %copy-done.57, ...), custom_call_target="tpu_custom_call" | custom-call | flops 4831838208 | bytes 12582912 | tf_op jit(solution)/shard_map/pallas_call | solution.py:144
  141.2 35.7 %shard_map.488 = (bf16[2,256,768]{2,1,0:T(8,128)(2,1)}, f32[4,1536]{1,0:T(4,128)}) custom-call(bf16[768,3072]{1,0:T(8,128)(2,1)} %shard_map.487.q_ref.k_ref.v_ref, bf16[768,3072]{1,0:T(8,128)(2,1)} %shard_map.487.q_ref.k_ref.v_ref, bf16[768,3072]{1,0:T(8,128)(2,1)} %shard_map.487.q_ref.k_ref.v_ref, f32[1,3072]{1,0:T(1,128)} %compare_select_fusion.bias), custom_call_target="tpu_custom_call" | custom-call | flops 19327352832 | bytes 3145728 | tf_op jit(solution)/shard_map/pallas_call | solution.py:198
  179.9 27.3 %shard_map.489 = (bf16[2,256,768]{2,1,0:T(8,128)(2,1)}, f32[4,1536]{1,0:T(4,128)}) custom-call(bf16[768,3072]{1,0:T(8,128)(2,1)} %shard_map.487.q_ref.k_ref.v_ref, bf16[768,3072]{1,0:T(8,128)(2,1)} %shard_map.487.q_ref.k_ref.v_ref, bf16[768,3072]{1,0:T(8,128)(2,1)} %shard_map.487.q_ref.k_ref.v_ref, f32[1,3072]{1,0:T(1,128)} %compare_select_fusion.bias), custom_call_target="tpu_custom_call" | custom-call | flops 19327352832 | bytes 3145728 | tf_op jit(solution)/shard_map/pallas_call | solution.py:198
  210.7 10.2 %shard_map.490 = (f32[12,64,1024]{2,1,0:T(8,128)}, bf16[384,1024]{1,0:T(8,128)(2,1)}, bf16[384,1024]{1,0:T(8,128)(2,1)}, bf16[768,1024]{1,0:T(8,128)(2,1)}, bf16...) custom-call(s32[5]{0:T(128)} %pad_add_fusion.order, bf16[2,256,768]{2,1,0:T(8,128)(2,1)} %get-tuple-element.151.a0.out_ref, ...), custom_call_target="tpu_custom_call" | custom-call | flops 1610612736 | bytes 11010048 | tf_op jit(solution)/shard_map/pallas_call | solution.py:409
  221.6 13.8 %shard_map.491 = (f32[384,1024]{1,0:T(8,128)}, f32[384,1024]{1,0:T(8,128)}, bf16[384,2048]{1,0:T(8,128)(2,1)}, bf16[384,2048]{1,0:T(8,128)(2,1)}, f32[6,1,1024]{2,1,0:T(1,128)}) custom-call(bf16[16,2,2,32,2048]{4,3,2,1,0:T(8,128)(2,1)} %bitcast.200, bf16[384,1024]{1,0:T(8,128)(2,1)} %get-tuple-element.155.hidden.refs_0_, ...), custom_call_target="tpu_custom_call" | custom-call | flops 6442450944 | bytes 11534336 | tf_op jit(solution)/shard_map/pallas_call | solution.py:506
  236.8 13.8 %shard_map.492 = (f32[384,1024]{1,0:T(8,128)}, f32[384,1024]{1,0:T(8,128)}, bf16[384,2048]{1,0:T(8,128)(2,1)}, bf16[384,2048]{1,0:T(8,128)(2,1)}, f32[6,1,1024]{2,1,0:T(1,128)}) custom-call(bf16[16,2,2,32,2048]{4,3,2,1,0:T(8,128)(2,1)} %bitcast.201, bf16[384,1024]{1,0:T(8,128)(2,1)} %get-tuple-element.163.hidden.refs_1_, ...), custom_call_target="tpu_custom_call" | custom-call | flops 6442450944 | bytes 11534336 | tf_op jit(solution)/shard_map/pallas_call | solution.py:506
  251.5 13.3 %shard_map.493 = (bf16[384,1024]{1,0:T(8,128)(2,1)}, bf16[384,1024]{1,0:T(8,128)(2,1)}, bf16[384,2048]{1,0:T(8,128)(2,1)}, bf16[384,2048]{1,0:T(8,128)(2,1)}, f32[6,1,1024]{2,1,0:T(1,128)}) custom-call(bf16[16,2,2,32,2048]{4,3,2,1,0:T(8,128)(2,1)} %bitcast.202, bf16[384,1024]{1,0:T(8,128)(2,1)} %copy-done.60, ...), custom_call_target="tpu_custom_call" | custom-call | flops 6442450944 | bytes 11534336 | tf_op jit(solution)/shard_map/pallas_call | solution.py:506
  266.3 13.7 %shard_map.494 = (bf16[384,1024]{1,0:T(8,128)(2,1)}, bf16[384,1024]{1,0:T(8,128)(2,1)}, bf16[384,2048]{1,0:T(8,128)(2,1)}, bf16[384,2048]{1,0:T(8,128)(2,1)}, f32[6,1,1024]{2,1,0:T(1,128)}) custom-call(bf16[16,2,2,32,2048]{4,3,2,1,0:T(8,128)(2,1)} %bitcast.203, bf16[384,1024]{1,0:T(8,128)(2,1)} %copy-done.61, ...), custom_call_target="tpu_custom_call" | custom-call | flops 6442450944 | bytes 11534336 | tf_op jit(solution)/shard_map/pallas_call | solution.py:506
  281.4 21.0 %shard_map.495 = bf16[16,2,2,32,2048]{4,3,2,1,0:T(8,128)(2,1)} custom-call(bf16[384,1024]{1,0:T(8,128)(2,1)} %get-tuple-element.155.hidden.refs_0_, bf16[384,1024]{1,0:T(8,128)(2,1)} %get-tuple-element.163.hidden.refs_1_, bf16[384,1024]{1,0:T(8,128)(2,1)} %copy-done.60, bf16[384,1024]{1,0:T(8,128)(2,1)} %copy-done.61, ...), custom_call_target="tpu_custom_call" | custom-call | flops 12884901888 | bytes 20971520 | tf_op jit(solution)/shard_map/pallas_call | solution.py:557
  303.6 17.6 %shard_map.496 = (f32[12,64,1024]{2,1,0:T(8,128)}, f32[12,3,1024]{2,1,0:T(4,128)}, bf16[256,768]{1,0:T(8,128)(2,1)}, bf16[256,768]{1,0:T(8,128)(2,1)}, bf16[256,...) custom-call(s32[5]{0:T(128)} %pad_add_fusion.order, f32[384,1024]{1,0:T(8,128)} %get-tuple-element.157.into1, ...), custom_call_target="tpu_custom_call" | custom-call | flops 3221225472 | bytes 18874368 | tf_op jit(solution)/shard_map/pallas_call | solution.py:620
  321.3 3.8 all-to-all-start.3
  327.0 48.3 %shard_map.497 = (bf16[256,1536]{1,0:T(8,128)(2,1)}, f32[256,3072]{1,0:T(8,128)}, f32[256,3072]{1,0:T(8,128)}) custom-call(bf16[768,3072]{1,0:T(8,128)(2,1)} %shard_map.487.q_ref.k_ref.v_ref, bf16[768,3072]{1,0:T(8,128)(2,1)} %shard_map.487.q_ref.k_ref.v_ref, bf16[768,3072]{1,0:T(8,128)(2,1)} %shard_map.487.q_ref.k_ref.v_ref, ...), custom_call_target="tpu_custom_call" | custom-call | flops 41070624768 | bytes 6291456 | tf_op jit(solution)/shard_map/pallas_call | solution.py:339
  377.4 50.9 %shard_map.498 = (bf16[256,1536]{1,0:T(8,128)(2,1)}, bf16[256,3072]{1,0:T(8,128)(2,1)}, bf16[256,3072]{1,0:T(8,128)(2,1)}) custom-call(bf16[768,3072]{1,0:T(8,128)(2,1)} %shard_map.487.q_ref.k_ref.v_ref, bf16[768,3072]{1,0:T(8,128)(2,1)} %shard_map.487.q_ref.k_ref.v_ref, bf16[768,3072]{1,0:T(8,128)(2,1)} %shard_map.487.q_ref.k_ref.v_ref, ...), custom_call_target="tpu_custom_call" | custom-call | flops 41070624768 | bytes 6291456 | tf_op jit(solution)/shard_map/pallas_call | solution.py:339
  428.3 13.0 %shard_map.499 = (bf16[2,768,1024]{2,1,0:T(8,128)(2,1)}, f32[768,1024]{1,0:T(8,128)}, f32[12,2,1024]{2,1,0:T(2,128)}) custom-call(bf16[384,1024]{1,0:T(8,128)(2,1)} %copy-done.57, bf16[400,1024]{1,0:T(8,128)(2,1)} %collective-permute-done.7.refs_5_.refs_1_, bf16[384,1024]{1,0:T(8,128)(2,1)} %copy-done.58, bf16[400,1024]{1,0:T(8,128)(2,1)} %copy-done.55, ...), custom_call_target="tpu_custom_call" | custom-call | flops 4831838208 | bytes 9437184 | tf_op jit(solution)/shard_map/pallas_call | solution.py:725
  443.2 3.3 collective-permute-done.24
  449.9 14.4 %shard_map.500 = (bf16[2,768,1024]{2,1,0:T(8,128)(2,1)}, bf16[1024,768]{1,0:T(8,128)(2,1)}, f32[12,2,1024]{2,1,0:T(2,128)}) custom-call(bf16[784,1024]{1,0:T(8,128)(2,1)} %copy-done.5, bf16[784,1024]{1,0:T(8,128)(2,1)} %copy-done.5, bf16[784,1024]{1,0:T(8,128)(2,1)} %copy-done.56, bf16[784,1024]{1,0:T(8,128)(2,1)} %copy-done.56, ...), custom_call_target="tpu_custom_call" | custom-call | flops 4831838208 | bytes 9437184 | tf_op jit(solution)/shard_map/pallas_call | solution.py:725
  469.7 5.8 %all-to-all-start.4 = ((bf16[32,35,768]{2,1,0:T(8,128)(2,1)}), bf16[32,35,768]{2,1,0:T(8,128)(2,1)S(1)}, u32[]{:S(2)}, u32[]{:S(2)}) async-start(bf16[32,35,768]{2,1,0:T(8,128)(2,1)} %pad_maximum_fusion), calls=%async_computation.5 | async-start | bytes 3932160 | tf_op jit(solution)/shard_map/all_to_all | solution.py:1037
  475.5 2.5 shard_map.502
  478.0 5.3 shard_map.501
  490.1 11.4 %collective-permute-done.28 = bf16[2,32,2048]{2,1,0:T(8,128)(2,1)S(1)} collective-permute-done((bf16[2,32,2048]{2,1,0:T(8,128)(2,1)S(1)}, bf16[2,32,2048]{2,1,0:T(8,128)(2,1)S(1)}, u32[]{:S(2)}, u32[]{:S(2)}) %collective-permute-start.28) | collective-permute-done | bytes 262176 | tf_op jit(solution)/shard_map/ppermute | solution.py:784
  507.1 15.3 %collective-permute-done.26.far2 = bf16[384,1024]{1,0:T(8,128)(2,1)} collective-permute-done((bf16[384,1024]{1,0:T(8,128)(2,1)S(1)}, bf16[384,1024]{1,0:T(8,128)(2,1)}, u32[]{:S(2)}, u32[]{:S(2)}) %collective-permute-start.26) | collective-permute-done | bytes 786464 | tf_op jit(solution)/shard_map/ppermute | solution.py:784
  526.8 2.6 shard_map.504
  534.9 4.8 all-to-all-start.5
  539.8 7.9 %shard_map.503 = f32[12,64,1024]{2,1,0:T(8,128)} custom-call(bf16[12,64,1024]{2,1,0:T(8,128)(2,1)} %bitcast.159, f32[12,6,1024]{2,1,0:T(8,128)} %reshape.421.refs_8_.mod.refs_4_, f32[12,64,1024]{2,1,0:T(8,128)} %get-tuple-element.224.middle_grad, bf16[2,768,1024]{2,1,0:T(8,128)(2,1)} %get-tuple-element.225.one, ...), custom_call_target="tpu_custom_call" | custom-call | flops 15728640 | bytes 12582912 | tf_op jit(solution)/shard_map/pallas_call | solution.py:755
  (321 shorter events, 106.5 us)
Async XLA Ops:
  8.8 29.4 %collective-permute-start.6 = (bf16[32,1024]{1,0:T(8,128)(2,1)}, bf16[32,1024]{1,0:T(8,128)(2,1)}, u32[]{:S(2)}, u32[]{:S(2)}) collective-permute-start(bf16[32,1024]{1,0:T(8,128)(2,1)} %get-tuple-element.299), channel_id=1, source_target_pairs={{0,2},{2,0},{1,3},{3,1},{4,6},{6,4},{5,7},{7,5},{8,10},{10,8},{9,1... | collective-permute-start | bytes 196616 | tf_op jit(solution)/shard_map/ppermute | solution.py:784
  14.6 19.8 %collective-permute-start.5 = (bf16[32,768]{1,0:T(8,128)(2,1)}, bf16[32,768]{1,0:T(8,128)(2,1)}, u32[]{:S(2)}, u32[]{:S(2)}) collective-permute-start(bf16[32,768]{1,0:T(8,128)(2,1)} %get-tuple-element.287), channel_id=1, source_target_pairs={{0,3},{1,2},{2,1},{3,0},{4,7},{5,6},{6,5},{7,4},{8,11},{9,10},{10,... | collective-permute-start | bytes 147464 | tf_op jit(solution)/shard_map/ppermute | solution.py:784
  14.6 21.3 %collective-permute-start.4 = (bf16[32,768]{1,0:T(8,128)(2,1)}, bf16[32,768]{1,0:T(8,128)(2,1)}, u32[]{:S(2)}, u32[]{:S(2)}) collective-permute-start(bf16[32,768]{1,0:T(8,128)(2,1)} %get-tuple-element.288), channel_id=1, source_target_pairs={{0,2},{1,3},{2,0},{3,1},{4,6},{5,7},{6,4},{7,5},{8,10},{9,11},{10,... | collective-permute-start | bytes 147464 | tf_op jit(solution)/shard_map/ppermute | solution.py:784
  15.8 20.1 %collective-permute-start.3 = (bf16[32,768]{1,0:T(8,128)(2,1)}, bf16[32,768]{1,0:T(8,128)(2,1)}, u32[]{:S(2)}, u32[]{:S(2)}) collective-permute-start(bf16[32,768]{1,0:T(8,128)(2,1)} %get-tuple-element.289), channel_id=1, source_target_pairs={{0,1},{1,0},{2,3},{3,2},{4,5},{5,4},{6,7},{7,6},{8,9},{9,8},{10,11... | collective-permute-start | bytes 147464 | tf_op jit(solution)/shard_map/ppermute | solution.py:784
  22.6 38.3 %collective-permute-start.1 = (bf16[2,32,2048]{2,1,0:T(8,128)(2,1)}, bf16[2,32,2048]{2,1,0:T(8,128)(2,1)}, u32[]{:S(2)}, u32[]{:S(2)}) collective-permute-start(bf16[2,32,2048]{2,1,0:T(8,128)(2,1)} %bitcast.152), channel_id=1, source_target_pairs={{0,2},{2,0},{1,3},{3,1},{4,6},{6,4},{5,7},{7,5},{8,10},{10,8},{9,1... | collective-permute-start | bytes 786440 | tf_op jit(solution)/shard_map/ppermute | solution.py:784
  25.1 15.1 %all-to-all-start = ((bf16[8,12,1024]{2,1,0:T(8,128)(2,1)}), bf16[8,12,1024]{2,1,0:T(8,128)(2,1)S(1)}, u32[]{:S(2)}, u32[]{:S(2)}) async-start(bf16[8,12,1024]{2,1,0:T(8,128)(2,1)} %broadcast_in_dim.32), calls=%async_computation | async-start | bytes 524288 | tf_op jit(solution)/shard_map/all_to_all | solution.py:884
  31.2 77.2 %all-gather.3.cloned.1.call-start = ((), (), s32[]{:S(2)}) async-start(), calls=%async_computation.7 | async-start | bytes 1769472 | tf_op jit(solution)/shard_map/all_gather | solution.py:881
  34.3 19.3 %collective-permute-start.2 = (bf16[384,1024]{1,0:T(8,128)(2,1)}, bf16[384,1024]{1,0:T(8,128)(2,1)S(1)}, u32[]{:S(2)}, u32[]{:S(2)}) collective-permute-start(bf16[384,1024]{1,0:T(8,128)(2,1)} %bitcast.13), channel_id=1, source_target_pairs={{0,2},{2,0},{1,3},{3,1},{4,6},{6,4},{5,7},{7,5},{8,10},{10,8},{9,1... | collective-permute-start | bytes 2359304 | tf_op jit(solution)/shard_map/ppermute | solution.py:784
  54.5 28.4 %all-to-all-start.1 = ((f32[32,12,192]{2,1,0:T(8,128)}), f32[32,12,192]{2,1,0:T(8,128)S(1)}, u32[]{:S(2)}, u32[]{:S(2)}) async-start(f32[32,12,192]{2,1,0:T(8,128)} %bitcast.14), calls=%async_computation.1 | async-start | bytes 1048576 | tf_op jit(solution)/shard_map/all_to_all | solution.py:896
  84.0 29.9 %all-to-all-start.2 = ((bf16[8,2,32,1024]{3,2,1,0:T(8,128)(2,1)}), bf16[8,2,32,1024]{3,2,1,0:T(8,128)(2,1)S(1)}, u32[]{:S(2)}, u32[]{:S(2)}) async-start(bf16[8,2,32,1024]{3,2,1,0:T(8,128)(2,1)} %broadcast_in_dim.35), calls=%async_computation.2 | async-start | bytes 2097152 | tf_op jit(solution)/shard_map/all_to_all | solution.py:904
  88.2 133.4 %all-gather.5.cloned.1.call-start = ((), (), s32[]{:S(2)}) async-start(), calls=%async_computation.8 | async-start | bytes 8912896 | tf_op jit(solution)/shard_map/all_gather | solution.py:914
  88.5 19.9 %collective-permute-start.7 = (bf16[400,1024]{1,0:T(8,128)(2,1)}, bf16[400,1024]{1,0:T(8,128)(2,1)}, u32[]{:S(2)}, u32[]{:S(2)}) collective-permute-start(bf16[400,1024]{1,0:T(8,128)(2,1)} %slice.177), channel_id=1, source_target_pairs={{0,2},{2,0},{1,3},{3,1},{4,6},{6,4},{5,7},{7,5},{8,10},{10,8},{9,1... | collective-permute-start | bytes 2457608 | tf_op jit(solution)/shard_map/ppermute | solution.py:784
  116.2 351.9 %reduce-scatter.2.cloned.1.call-start = ((), (), s32[]{:S(2)}) async-start(), calls=%async_computation.9 | async-start | bytes 8912896 | tf_op jit(solution)/shard_map/reduce_scatter | solution.py:975
  120.8 86.4 %collective-permute-start.11 = (bf16[8,2,32,1024]{3,2,1,0:T(8,128)(2,1)S(1)}, bf16[8,2,32,1024]{3,2,1,0:T(8,128)(2,1)}, u32[]{:S(2)}, u32[]{:S(2)}) collective-permute-start(bf16[8,2,32,1024]{3,2,1,0:T(8,128)(2,1)S(1)} %all-to-all-done.2.mine), channel_id=1, source_target_pairs={{0,1},{1,0},{2,3},{3,2},{4,5},{5,4},{6,7},{7,6},{8,9},{9,8},{10,11... | collective-permute-start | bytes 3145736 | tf_op jit(solution)/shard_map/ppermute | solution.py:784
  120.9 56.0 %collective-permute-start.10 = (bf16[12,64,1024]{2,1,0:T(8,128)(2,1)S(1)}, bf16[12,64,1024]{2,1,0:T(8,128)(2,1)}, u32[]{:S(2)}, u32[]{:S(2)}) collective-permute-start(bf16[12,64,1024]{2,1,0:T(8,128)(2,1)S(1)} %bitcast.168), channel_id=1, source_target_pairs={{0,2},{2,0},{1,3},{3,1},{4,6},{6,4},{5,7},{7,5},{8,10},{10,8},{9,1... | collective-permute-start | bytes 4718600 | tf_op jit(solution)/shard_map/ppermute | solution.py:784
  178.1 31.0 %collective-permute-start.14 = (bf16[256,768]{1,0:T(8,128)(2,1)S(1)}, bf16[256,768]{1,0:T(8,128)(2,1)S(1)}, u32[]{:S(2)}, u32[]{:S(2)}) collective-permute-start(bf16[256,768]{1,0:T(8,128)(2,1)S(1)} %get-tuple-element.264), channel_id=1, source_target_pairs={{0,3},{1,2},{2,1},{3,0},{4,7},{5,6},{6,5},{7,4},{8,11},{9,10},{10,... | collective-permute-start | bytes 1179656 | tf_op jit(solution)/shard_map/ppermute | solution.py:784
  178.4 30.6 %collective-permute-start.13 = (bf16[256,768]{1,0:T(8,128)(2,1)S(1)}, bf16[256,768]{1,0:T(8,128)(2,1)S(1)}, u32[]{:S(2)}, u32[]{:S(2)}) collective-permute-start(bf16[256,768]{1,0:T(8,128)(2,1)S(1)} %get-tuple-element.265), channel_id=1, source_target_pairs={{0,2},{1,3},{2,0},{3,1},{4,6},{5,7},{6,4},{7,5},{8,10},{9,11},{10,... | collective-permute-start | bytes 1179656 | tf_op jit(solution)/shard_map/ppermute | solution.py:784
  220.9 29.7 %collective-permute-start.15 = (bf16[384,1024]{1,0:T(8,128)(2,1)}, bf16[384,1024]{1,0:T(8,128)(2,1)S(1)}, u32[]{:S(2)}, u32[]{:S(2)}) collective-permute-start(bf16[384,1024]{1,0:T(8,128)(2,1)} %get-tuple-element.155.hidden.refs_0_), channel_id=1, source_target_pairs={{0,2},{2,0},{1,3},{3,1},{4,6},{6,4},{5,7},{7,5},{8,10},{10,8},{9,1... | collective-permute-start | bytes 2359304 | tf_op jit(solution)/shard_map/ppermute | solution.py:784
  235.4 30.0 %collective-permute-start.16 = (bf16[384,1024]{1,0:T(8,128)(2,1)S(1)}, bf16[384,1024]{1,0:T(8,128)(2,1)S(1)}, u32[]{:S(2)}, u32[]{:S(2)}) collective-permute-start(bf16[384,1024]{1,0:T(8,128)(2,1)S(1)} %copy-done.59), channel_id=1, source_target_pairs={{0,2},{2,0},{1,3},{3,1},{4,6},{6,4},{5,7},{7,5},{8,10},{10,8},{9,1... | collective-permute-start | bytes 2359304 | tf_op jit(solution)/shard_map/ppermute | solution.py:784
  264.8 37.6 %collective-permute-start.17 = (bf16[384,1024]{1,0:T(8,128)(2,1)}, bf16[384,1024]{1,0:T(8,128)(2,1)S(1)}, u32[]{:S(2)}, u32[]{:S(2)}) collective-permute-start(bf16[384,1024]{1,0:T(8,128)(2,1)} %get-tuple-element.175), channel_id=1, source_target_pairs={{0,2},{2,0},{1,3},{3,1},{4,6},{6,4},{5,7},{7,5},{8,10},{10,8},{9,1... | collective-permute-start | bytes 2359304 | tf_op jit(solution)/shard_map/ppermute | solution.py:784
  280.0 22.5 %collective-permute-start.18 = (bf16[384,1024]{1,0:T(8,128)(2,1)}, bf16[384,1024]{1,0:T(8,128)(2,1)S(1)}, u32[]{:S(2)}, u32[]{:S(2)}) collective-permute-start(bf16[384,1024]{1,0:T(8,128)(2,1)} %get-tuple-element.176), channel_id=1, source_target_pairs={{0,2},{2,0},{1,3},{3,1},{4,6},{6,4},{5,7},{7,5},{8,10},{10,8},{9,1... | collective-permute-start | bytes 2359304 | tf_op jit(solution)/shard_map/ppermute | solution.py:784
  321.3 107.0 %all-to-all-start.3 = ((bf16[32,32,1024]{2,1,0:T(8,128)(2,1)}), bf16[32,32,1024]{2,1,0:T(8,128)(2,1)}, u32[]{:S(2)}, u32[]{:S(2)}) async-start(bf16[32,32,1024]{2,1,0:T(8,128)(2,1)} %bitcast.186), calls=%async_computation.3 | async-start | bytes 4194304 | tf_op jit(solution)/shard_map/all_to_all | solution.py:986
  325.1 50.1 %collective-permute-start.20 = (bf16[256,768]{1,0:T(8,128)(2,1)S(1)}, bf16[256,768]{1,0:T(8,128)(2,1)}, u32[]{:S(2)}, u32[]{:S(2)}) collective-permute-start(bf16[256,768]{1,0:T(8,128)(2,1)S(1)} %copy-done.63), channel_id=1, source_target_pairs={{0,2},{1,3},{2,0},{3,1},{4,6},{5,7},{6,4},{7,5},{8,10},{9,11},{10,... | collective-permute-start | bytes 1179656 | tf_op jit(solution)/shard_map/ppermute | solution.py:784
  327.0 48.3 %collective-permute-start.21 = (bf16[256,768]{1,0:T(8,128)(2,1)S(1)}, bf16[256,768]{1,0:T(8,128)(2,1)}, u32[]{:S(2)}, u32[]{:S(2)}) collective-permute-start(bf16[256,768]{1,0:T(8,128)(2,1)S(1)} %copy-done.62), channel_id=1, source_target_pairs={{0,3},{1,2},{2,1},{3,0},{4,7},{5,6},{6,5},{7,4},{8,11},{9,10},{10,... | collective-permute-start | bytes 1179656 | tf_op jit(solution)/shard_map/ppermute | solution.py:784
  375.3 53.0 %collective-permute-start.22 = (bf16[384,1024]{1,0:T(8,128)(2,1)}, bf16[384,1024]{1,0:T(8,128)(2,1)S(1)}, u32[]{:S(2)}, u32[]{:S(2)}) collective-permute-start(bf16[384,1024]{1,0:T(8,128)(2,1)} %get-tuple-element.196), channel_id=1, source_target_pairs={{0,2},{2,0},{1,3},{3,1},{4,6},{6,4},{5,7},{7,5},{8,10},{10,8},{9,1... | collective-permute-start | bytes 2359304 | tf_op jit(solution)/shard_map/ppermute | solution.py:784
  376.8 51.5 %collective-permute-start.23 = (bf16[384,1024]{1,0:T(8,128)(2,1)}, bf16[384,1024]{1,0:T(8,128)(2,1)}, u32[]{:S(2)}, u32[]{:S(2)}) collective-permute-start(bf16[384,1024]{1,0:T(8,128)(2,1)} %get-tuple-element.197), channel_id=1, source_target_pairs={{0,2},{2,0},{1,3},{3,1},{4,6},{6,4},{5,7},{7,5},{8,10},{10,8},{9,1... | collective-permute-start | bytes 2359304 | tf_op jit(solution)/shard_map/ppermute | solution.py:784
  448.3 19.8 %collective-permute-start.25 = (bf16[384,1024]{1,0:T(8,128)(2,1)}, bf16[384,1024]{1,0:T(8,128)(2,1)S(1)}, u32[]{:S(2)}, u32[]{:S(2)}) collective-permute-start(bf16[384,1024]{1,0:T(8,128)(2,1)} %get-tuple-element.207), channel_id=1, source_target_pairs={{0,2},{2,0},{1,3},{3,1},{4,6},{6,4},{5,7},{7,5},{8,10},{10,8},{9,1... | collective-permute-start | bytes 2359304 | tf_op jit(solution)/shard_map/ppermute | solution.py:784
  469.7 52.7 %all-to-all-start.4 = ((bf16[32,35,768]{2,1,0:T(8,128)(2,1)}), bf16[32,35,768]{2,1,0:T(8,128)(2,1)S(1)}, u32[]{:S(2)}, u32[]{:S(2)}) async-start(bf16[32,35,768]{2,1,0:T(8,128)(2,1)} %pad_maximum_fusion), calls=%async_computation.5 | async-start | bytes 3932160 | tf_op jit(solution)/shard_map/all_to_all | solution.py:1037
  486.6 14.8 %collective-permute-start.28 = (bf16[2,32,2048]{2,1,0:T(8,128)(2,1)S(1)}, bf16[2,32,2048]{2,1,0:T(8,128)(2,1)S(1)}, u32[]{:S(2)}, u32[]{:S(2)}) collective-permute-start(bf16[2,32,2048]{2,1,0:T(8,128)(2,1)S(1)} %bitcast.196), channel_id=1, source_target_pairs={{0,2},{2,0},{1,3},{3,1},{4,6},{6,4},{5,7},{7,5},{8,10},{10,8},{9,1... | collective-permute-start | bytes 786440 | tf_op jit(solution)/shard_map/ppermute | solution.py:784
  489.8 49.9 %collective-permute-start.27 = (bf16[768,1024]{1,0:T(8,128)(2,1)}, bf16[768,1024]{1,0:T(8,128)(2,1)}, u32[]{:S(2)}, u32[]{:S(2)}) collective-permute-start(bf16[768,1024]{1,0:T(8,128)(2,1)} %slice_bitcast_fusion), channel_id=1, source_target_pairs={{0,1},{1,0},{2,3},{3,2},{4,5},{5,4},{6,7},{7,6},{8,9},{9,8},{10,11... | collective-permute-start | bytes 4718600 | tf_op jit(solution)/shard_map/ppermute | solution.py:784
  489.8 32.5 %collective-permute-start.26 = (bf16[384,1024]{1,0:T(8,128)(2,1)S(1)}, bf16[384,1024]{1,0:T(8,128)(2,1)}, u32[]{:S(2)}, u32[]{:S(2)}) collective-permute-start(bf16[384,1024]{1,0:T(8,128)(2,1)S(1)} %copy-done.32), channel_id=1, source_target_pairs={{0,2},{2,0},{1,3},{3,1},{4,6},{6,4},{5,7},{7,5},{8,10},{10,8},{9,1... | collective-permute-start | bytes 2359304 | tf_op jit(solution)/shard_map/ppermute | solution.py:784
  534.9 12.8 %all-to-all-start.5 = ((f32[32,1,128]{2,1,0:T(1,128)}), f32[32,1,128]{2,1,0:T(1,128)S(1)}, u32[]{:S(2)}, u32[]{:S(2)}) async-start(f32[32,1,128]{2,1,0:T(1,128)} %broadcast_in_dim.38), calls=%async_computation.6 | async-start | bytes 32768 | tf_op jit(solution)/shard_map/all_to_all | solution.py:1061
  (70 other events, 329.6 us)
Sparse Core Ops, SparseCore 0:
  38.2 50.4 all-gather.2
  116.3 73.7 all-gather.4
  302.6 138.1 reduce-scatter.1

commit v16 on v14

--- a/solution.py
+++ b/solution.py
@@ -1042,9 +1042,9 @@
         (attend_raw, far_two, block_out, project_sum)
     )
     input_gradient = input_back(own, mod, middle_grad, back_near + (far_one, far_two))
-    small = attend_raw[:, shard : shard + extra].reshape(devices, -1)[:, : frames * part]
-    small = small.astype(f32).reshape(clips, rows, frames, part)
-    mod_grad = jnp.sum(small, axis=1).reshape(clips * frames, part)
+    small = attend_raw[:, shard : shard + extra].astype(f32)
+    small = jnp.sum(small.reshape(clips, rows, extra, 3 * features), axis=1)
+    mod_grad = small.reshape(clips, -1)[:, : frames * part].reshape(clips * frames, part)
     attend_sum = total_over(attend_raw.reshape(clips, rows, shard + extra, 3 * features))
     attend_sum = attend_sum[:, :shard].reshape(rows, shard, 3, features)
     attend_sum = attend_sum.transpose(1, 2, 0, 3).reshape(shard, 3 * width)

time: 544 us -> 540 us (level)
  transfers between devices with their start and end apart: 38 -> 38, of which waited for: 11 -> 11; matrix products, arithmetic and copies ran while one was open for 10% -> 9% of each run, Pallas kernels for 59% -> 60%
where the time goes in v16:
time: 540 us; the launch traced here: 533 us
  Pallas kernels  318 us (59%)
  waiting for transfers between devices  66.3 us (12%)
  starting transfers between devices  57.3 us (11%)
  other arithmetic  35.5 us (7%)
  local copies, waits for them, and re-layouts  31.9 us (6%)
  between operations  21.9 us (4%)
    pallas_call x2, Pallas kernels, attend_back(): pl.pallas_call(functools.partial(attend_back_kernel, heads, last), grid=(...  99.3 us
    ppermute x29, waiting for transfers between devices, swap(): lax.ppermute(value, axis, [(place, place ^ step) for place in range(size)])  56.3 us
    pallas_call x2, Pallas kernels, attend(): pl.pallas_call(functools.partial(attend_kernel, heads), grid=(count // bl...  55 us
    pallas_call x4, Pallas kernels, feed_forward(): pl.pallas_call(feed_kernel, grid=(units // block,), in_specs=[spec, flat,...  54.1 us
    pallas_call x2, Pallas kernels, first_back(): pl.pallas_call(functools.partial(first_back_kernel, last, [place for _, p...  27.4 us
    ppermute x29, starting transfers between devices, swap(): lax.ppermute(value, axis, [(place, place ^ step) for place in range(size)])  26.3 us
    pallas_call x1, Pallas kernels, feed_weights(): pl.pallas_call(functools.partial(feed_weight_kernel, len(hidden)), grid=(...  21 us
    pallas_call x1, Pallas kernels, middle_back(): pl.pallas_call(middle_kernel, grid=(frames // chunk,), in_specs=[whole(pl...  17.3 us
  transfers between devices with their start and end apart: 38, of which 11 were waited for; matrix products, arithmetic and copies ran while one was open for 9% of the time, Pallas kernels for 60%

profile of v16, /device:TPU:0, one launch (start us, length us, event | category | flops | bytes accessed | tf_op | source)
XLA Modules:
  0.0 532.8 jit_solution(3905302115936324945)
XLA Ops:
  9.5 2.4 collective-permute-start.5
  18.7 5.8 %all-to-all-start = ((bf16[8,12,1024]{2,1,0:T(8,128)(2,1)}), bf16[8,12,1024]{2,1,0:T(8,128)(2,1)S(1)}, u32[]{:S(2)}, u32[]{:S(2)}) async-start(bf16[8,12,1024]{2,1,0:T(8,128)(2,1)} %broadcast_in_dim.31), calls=%async_computation | async-start | bytes 524288 | tf_op jit(solution)/shard_map/all_to_all | solution.py:884
  34.7 5.7 %all-to-all-start.1 = ((f32[32,12,192]{2,1,0:T(8,128)}), f32[32,12,192]{2,1,0:T(8,128)S(1)}, u32[]{:S(2)}, u32[]{:S(2)}) async-start(f32[32,12,192]{2,1,0:T(8,128)} %bitcast.14), calls=%async_computation.1 | async-start | bytes 1048576 | tf_op jit(solution)/shard_map/all_to_all | solution.py:896
  43.7 9.4 %collective-permute-done.1 = bf16[2,32,2048]{2,1,0:T(8,128)(2,1)S(1)} collective-permute-done((bf16[2,32,2048]{2,1,0:T(8,128)(2,1)S(1)}, bf16[2,32,2048]{2,1,0:T(8,128)(2,1)S(1)}, u32[]{:S(2)}, u32[]{:S(2)}) %collective-permute-start.1) | collective-permute-done | bytes 262176 | tf_op jit(solution)/shard_map/ppermute | solution.py:784
  56.1 4.1 all-to-all-done.1
  63.6 11.8 %collective-permute-done.6.refs_5_.refs_1_ = bf16[400,1024]{1,0:T(8,128)(2,1)} collective-permute-done((bf16[400,1024]{1,0:T(8,128)(2,1)S(1)}, bf16[400,1024]{1,0:T(8,128)(2,1)}, u32[]{:S(2)}, u32[]{:S(2)}) %collective-permute-start.6) | collective-permute-done | bytes 819232 | tf_op jit(solution)/shard_map/ppermute | solution.py:784
  75.4 3.4 all-gather.3.cloned.1.call-done
  85.8 3.6 all-to-all-start.2
  94.7 15.0 %shard_map.487.q_ref.k_ref.v_ref = bf16[768,3072]{1,0:T(8,128)(2,1)} custom-call(bf16[784,1024]{1,0:T(8,128)(2,1)} %fusion.1.refs_0_.refs_1_, bf16[784,1024]{1,0:T(8,128)(2,1)} %fusion.1.refs_0_.refs_1_, bf16[784,1024]{1,0:T(8,128)(2,1)} %collective-permute-done.refs_2_.refs_3_, bf16[784,1024]{1,0:T(8,128)(2,1)} %collective-permute-done.refs_2_.refs_3_, ...), custom_call_target="tpu_custom_call" | custom-call | flops 4831838208 | bytes 12582912 | tf_op jit(solution)/shard_map/pallas_call | solution.py:144
  110.3 27.5 %shard_map.488 = (bf16[2,256,768]{2,1,0:T(8,128)(2,1)}, f32[4,1536]{1,0:T(4,128)}) custom-call(bf16[768,3072]{1,0:T(8,128)(2,1)} %shard_map.487.q_ref.k_ref.v_ref, bf16[768,3072]{1,0:T(8,128)(2,1)} %shard_map.487.q_ref.k_ref.v_ref, bf16[768,3072]{1,0:T(8,128)(2,1)} %shard_map.487.q_ref.k_ref.v_ref, f32[1,3072]{1,0:T(1,128)} %compare_select_fusion.bias), custom_call_target="tpu_custom_call" | custom-call | flops 19327352832 | bytes 3145728 | tf_op jit(solution)/shard_map/pallas_call | solution.py:198
  141.4 27.5 %shard_map.489 = (bf16[2,256,768]{2,1,0:T(8,128)(2,1)}, f32[4,1536]{1,0:T(4,128)}) custom-call(bf16[768,3072]{1,0:T(8,128)(2,1)} %shard_map.487.q_ref.k_ref.v_ref, bf16[768,3072]{1,0:T(8,128)(2,1)} %shard_map.487.q_ref.k_ref.v_ref, bf16[768,3072]{1,0:T(8,128)(2,1)} %shard_map.487.q_ref.k_ref.v_ref, f32[1,3072]{1,0:T(1,128)} %compare_select_fusion.bias), custom_call_target="tpu_custom_call" | custom-call | flops 19327352832 | bytes 3145728 | tf_op jit(solution)/shard_map/pallas_call | solution.py:198
  173.4 10.2 %shard_map.490 = (f32[12,64,1024]{2,1,0:T(8,128)}, bf16[384,1024]{1,0:T(8,128)(2,1)}, bf16[384,1024]{1,0:T(8,128)(2,1)}, bf16[768,1024]{1,0:T(8,128)(2,1)}, bf16...) custom-call(s32[5]{0:T(128)} %pad_add_fusion.order, bf16[2,256,768]{2,1,0:T(8,128)(2,1)} %get-tuple-element.147.a0.out_ref, ...), custom_call_target="tpu_custom_call" | custom-call | flops 1610612736 | bytes 11010048 | tf_op jit(solution)/shard_map/pallas_call | solution.py:409
  183.8 13.8 %shard_map.491 = (f32[384,1024]{1,0:T(8,128)}, f32[384,1024]{1,0:T(8,128)}, bf16[384,2048]{1,0:T(8,128)(2,1)}, bf16[384,2048]{1,0:T(8,128)(2,1)}, f32[6,1,1024]{2,1,0:T(1,128)}) custom-call(bf16[16,2,2,32,2048]{4,3,2,1,0:T(8,128)(2,1)} %bitcast.207, bf16[384,1024]{1,0:T(8,128)(2,1)} %get-tuple-element.151.hidden.refs_0_, ...), custom_call_target="tpu_custom_call" | custom-call | flops 6442450944 | bytes 11534336 | tf_op jit(solution)/shard_map/pallas_call | solution.py:506
  199.5 13.7 %shard_map.492 = (f32[384,1024]{1,0:T(8,128)}, f32[384,1024]{1,0:T(8,128)}, bf16[384,2048]{1,0:T(8,128)(2,1)}, bf16[384,2048]{1,0:T(8,128)(2,1)}, f32[6,1,1024]{2,1,0:T(1,128)}) custom-call(bf16[16,2,2,32,2048]{4,3,2,1,0:T(8,128)(2,1)} %bitcast.208, bf16[384,1024]{1,0:T(8,128)(2,1)} %get-tuple-element.159.hidden.refs_1_, ...), custom_call_target="tpu_custom_call" | custom-call | flops 6442450944 | bytes 11534336 | tf_op jit(solution)/shard_map/pallas_call | solution.py:506
  214.0 13.2 %shard_map.493 = (bf16[384,1024]{1,0:T(8,128)(2,1)}, bf16[384,1024]{1,0:T(8,128)(2,1)}, bf16[384,2048]{1,0:T(8,128)(2,1)}, bf16[384,2048]{1,0:T(8,128)(2,1)}, f32[6,1,1024]{2,1,0:T(1,128)}) custom-call(bf16[16,2,2,32,2048]{4,3,2,1,0:T(8,128)(2,1)} %bitcast.209, bf16[384,1024]{1,0:T(8,128)(2,1)} %copy-done.57, ...), custom_call_target="tpu_custom_call" | custom-call | flops 6442450944 | bytes 11534336 | tf_op jit(solution)/shard_map/pallas_call | solution.py:506
  228.4 13.4 %shard_map.494 = (bf16[384,1024]{1,0:T(8,128)(2,1)}, bf16[384,1024]{1,0:T(8,128)(2,1)}, bf16[384,2048]{1,0:T(8,128)(2,1)}, bf16[384,2048]{1,0:T(8,128)(2,1)}, f32[6,1,1024]{2,1,0:T(1,128)}) custom-call(bf16[16,2,2,32,2048]{4,3,2,1,0:T(8,128)(2,1)} %bitcast.210, bf16[384,1024]{1,0:T(8,128)(2,1)} %copy-done.58, ...), custom_call_target="tpu_custom_call" | custom-call | flops 6442450944 | bytes 11534336 | tf_op jit(solution)/shard_map/pallas_call | solution.py:506
  243.6 21.0 %shard_map.495 = bf16[16,2,2,32,2048]{4,3,2,1,0:T(8,128)(2,1)} custom-call(bf16[384,1024]{1,0:T(8,128)(2,1)} %get-tuple-element.151.hidden.refs_0_, bf16[384,1024]{1,0:T(8,128)(2,1)} %get-tuple-element.159.hidden.refs_1_, bf16[384,1024]{1,0:T(8,128)(2,1)} %copy-done.57, bf16[384,1024]{1,0:T(8,128)(2,1)} %copy-done.58, ...), custom_call_target="tpu_custom_call" | custom-call | flops 12884901888 | bytes 20971520 | tf_op jit(solution)/shard_map/pallas_call | solution.py:557
  265.8 17.3 %shard_map.496 = (f32[12,64,1024]{2,1,0:T(8,128)}, f32[12,3,1024]{2,1,0:T(4,128)}, bf16[256,768]{1,0:T(8,128)(2,1)}, bf16[256,768]{1,0:T(8,128)(2,1)}, bf16[256,...) custom-call(s32[5]{0:T(128)} %pad_add_fusion.order, f32[384,1024]{1,0:T(8,128)} %get-tuple-element.153.into1, ...), custom_call_target="tpu_custom_call" | custom-call | flops 3221225472 | bytes 18874368 | tf_op jit(solution)/shard_map/pallas_call | solution.py:620
  283.2 4.7 all-to-all-start.3
  289.9 48.4 %shard_map.497 = (bf16[256,1536]{1,0:T(8,128)(2,1)}, f32[256,3072]{1,0:T(8,128)}, f32[256,3072]{1,0:T(8,128)}) custom-call(bf16[768,3072]{1,0:T(8,128)(2,1)} %shard_map.487.q_ref.k_ref.v_ref, bf16[768,3072]{1,0:T(8,128)(2,1)} %shard_map.487.q_ref.k_ref.v_ref, bf16[768,3072]{1,0:T(8,128)(2,1)} %shard_map.487.q_ref.k_ref.v_ref, ...), custom_call_target="tpu_custom_call" | custom-call | flops 41070624768 | bytes 6291456 | tf_op jit(solution)/shard_map/pallas_call | solution.py:339
  340.4 51.0 %shard_map.498 = (bf16[256,1536]{1,0:T(8,128)(2,1)}, bf16[256,3072]{1,0:T(8,128)(2,1)}, bf16[256,3072]{1,0:T(8,128)(2,1)}) custom-call(bf16[768,3072]{1,0:T(8,128)(2,1)} %shard_map.487.q_ref.k_ref.v_ref, bf16[768,3072]{1,0:T(8,128)(2,1)} %shard_map.487.q_ref.k_ref.v_ref, bf16[768,3072]{1,0:T(8,128)(2,1)} %shard_map.487.q_ref.k_ref.v_ref, ...), custom_call_target="tpu_custom_call" | custom-call | flops 41070624768 | bytes 6291456 | tf_op jit(solution)/shard_map/pallas_call | solution.py:339
  391.4 13.0 %shard_map.499 = (bf16[2,768,1024]{2,1,0:T(8,128)(2,1)}, f32[768,1024]{1,0:T(8,128)}, f32[12,2,1024]{2,1,0:T(2,128)}) custom-call(bf16[384,1024]{1,0:T(8,128)(2,1)} %collective-permute-done.2.refs_4_.refs_0_, bf16[400,1024]{1,0:T(8,128)(2,1)} %collective-permute-done.6.refs_5_.refs_1_, bf16[384,1024]{1,0:T(8,128)(2,1)} %collective-permute-done.7.refs_6_.refs_2_, ...), custom_call_target="tpu_custom_call" | custom-call | flops 4831838208 | bytes 9437184 | tf_op jit(solution)/shard_map/pallas_call | solution.py:725
  406.3 3.3 collective-permute-done.24
  413.1 14.4 %shard_map.500 = (bf16[2,768,1024]{2,1,0:T(8,128)(2,1)}, bf16[1024,768]{1,0:T(8,128)(2,1)}, f32[12,2,1024]{2,1,0:T(2,128)}) custom-call(bf16[784,1024]{1,0:T(8,128)(2,1)} %fusion.1.refs_0_.refs_1_, bf16[784,1024]{1,0:T(8,128)(2,1)} %fusion.1.refs_0_.refs_1_, bf16[784,1024]{1,0:T(8,128)(2,1)} %collective-permute-done.refs_2_.refs_3_, ...), custom_call_target="tpu_custom_call" | custom-call | flops 4831838208 | bytes 9437184 | tf_op jit(solution)/shard_map/pallas_call | solution.py:725
  432.8 5.7 %all-to-all-start.4 = ((bf16[32,35,768]{2,1,0:T(8,128)(2,1)}), bf16[32,35,768]{2,1,0:T(8,128)(2,1)S(1)}, u32[]{:S(2)}, u32[]{:S(2)}) async-start(bf16[32,35,768]{2,1,0:T(8,128)(2,1)} %pad_maximum_fusion), calls=%async_computation.5 | async-start | bytes 3932160 | tf_op jit(solution)/shard_map/all_to_all | solution.py:1039
  438.5 2.5 shard_map.502
  441.0 5.3 shard_map.501
  453.1 11.4 %collective-permute-done.28 = bf16[2,32,2048]{2,1,0:T(8,128)(2,1)S(1)} collective-permute-done((bf16[2,32,2048]{2,1,0:T(8,128)(2,1)S(1)}, bf16[2,32,2048]{2,1,0:T(8,128)(2,1)S(1)}, u32[]{:S(2)}, u32[]{:S(2)}) %collective-permute-start.28) | collective-permute-done | bytes 262176 | tf_op jit(solution)/shard_map/ppermute | solution.py:784
  470.1 15.3 %collective-permute-done.26.far2 = bf16[384,1024]{1,0:T(8,128)(2,1)} collective-permute-done((bf16[384,1024]{1,0:T(8,128)(2,1)S(1)}, bf16[384,1024]{1,0:T(8,128)(2,1)}, u32[]{:S(2)}, u32[]{:S(2)}) %collective-permute-start.26) | collective-permute-done | bytes 786464 | tf_op jit(solution)/shard_map/ppermute | solution.py:784
  489.8 2.6 shard_map.504
  498.0 4.8 all-to-all-start.5
  502.8 7.9 %shard_map.503 = f32[12,64,1024]{2,1,0:T(8,128)} custom-call(bf16[12,64,1024]{2,1,0:T(8,128)(2,1)} %bitcast.159, f32[12,6,1024]{2,1,0:T(8,128)} %reshape.443.refs_8_.mod.refs_4_, f32[12,64,1024]{2,1,0:T(8,128)} %get-tuple-element.220.middle_grad, bf16[2,768,1024]{2,1,0:T(8,128)(2,1)} %get-tuple-element.221.one, ...), custom_call_target="tpu_custom_call" | custom-call | flops 15728640 | bytes 12582912 | tf_op jit(solution)/shard_map/pallas_call | solution.py:755
  (315 shorter events, 101.9 us)
Async XLA Ops:
  9.5 16.4 %collective-permute-start.5 = (bf16[32,768]{1,0:T(8,128)(2,1)S(1)}, bf16[32,768]{1,0:T(8,128)(2,1)S(1)}, u32[]{:S(2)}, u32[]{:S(2)}) collective-permute-start(bf16[32,768]{1,0:T(8,128)(2,1)S(1)} %get-tuple-element.283), channel_id=1, source_target_pairs={{0,3},{1,2},{2,1},{3,0},{4,7},{5,6},{6,5},{7,4},{8,11},{9,10},{10,... | collective-permute-start | bytes 147464 | tf_op jit(solution)/shard_map/ppermute | solution.py:784
  11.9 14.0 %collective-permute-start.4 = (bf16[32,768]{1,0:T(8,128)(2,1)S(1)}, bf16[32,768]{1,0:T(8,128)(2,1)S(1)}, u32[]{:S(2)}, u32[]{:S(2)}) collective-permute-start(bf16[32,768]{1,0:T(8,128)(2,1)S(1)} %get-tuple-element.284), channel_id=1, source_target_pairs={{0,2},{1,3},{2,0},{3,1},{4,6},{5,7},{6,4},{7,5},{8,10},{9,11},{10,... | collective-permute-start | bytes 147464 | tf_op jit(solution)/shard_map/ppermute | solution.py:784
  12.6 13.4 %collective-permute-start.3 = (bf16[32,768]{1,0:T(8,128)(2,1)S(1)}, bf16[32,768]{1,0:T(8,128)(2,1)S(1)}, u32[]{:S(2)}, u32[]{:S(2)}) collective-permute-start(bf16[32,768]{1,0:T(8,128)(2,1)S(1)} %get-tuple-element.285), channel_id=1, source_target_pairs={{0,1},{1,0},{2,3},{3,2},{4,5},{5,4},{6,7},{7,6},{8,9},{9,8},{10,11... | collective-permute-start | bytes 147464 | tf_op jit(solution)/shard_map/ppermute | solution.py:784
  13.5 20.2 %collective-permute-start.2 = (bf16[384,1024]{1,0:T(8,128)(2,1)}, bf16[384,1024]{1,0:T(8,128)(2,1)}, u32[]{:S(2)}, u32[]{:S(2)}) collective-permute-start(bf16[384,1024]{1,0:T(8,128)(2,1)} %bitcast.13), channel_id=1, source_target_pairs={{0,2},{2,0},{1,3},{3,1},{4,6},{6,4},{5,7},{7,5},{8,10},{10,8},{9,1... | collective-permute-start | bytes 2359304 | tf_op jit(solution)/shard_map/ppermute | solution.py:784
  18.7 14.8 %all-to-all-start = ((bf16[8,12,1024]{2,1,0:T(8,128)(2,1)}), bf16[8,12,1024]{2,1,0:T(8,128)(2,1)S(1)}, u32[]{:S(2)}, u32[]{:S(2)}) async-start(bf16[8,12,1024]{2,1,0:T(8,128)(2,1)} %broadcast_in_dim.31), calls=%async_computation | async-start | bytes 524288 | tf_op jit(solution)/shard_map/all_to_all | solution.py:884
  24.5 54.2 %all-gather.3.cloned.1.call-start = ((), (), s32[]{:S(2)}) async-start(), calls=%async_computation.7 | async-start | bytes 1769472 | tf_op jit(solution)/shard_map/all_gather | solution.py:881
  34.7 25.6 %all-to-all-start.1 = ((f32[32,12,192]{2,1,0:T(8,128)}), f32[32,12,192]{2,1,0:T(8,128)S(1)}, u32[]{:S(2)}, u32[]{:S(2)}) async-start(f32[32,12,192]{2,1,0:T(8,128)} %bitcast.14), calls=%async_computation.1 | async-start | bytes 1048576 | tf_op jit(solution)/shard_map/all_to_all | solution.py:896
  40.4 143.4 %all-gather.5.cloned.1.call-start = ((), (), s32[]{:S(2)}) async-start(), calls=%async_computation.8 | async-start | bytes 8912896 | tf_op jit(solution)/shard_map/all_gather | solution.py:910
  41.9 11.2 %collective-permute-start.1 = (bf16[2,32,2048]{2,1,0:T(8,128)(2,1)S(1)}, bf16[2,32,2048]{2,1,0:T(8,128)(2,1)S(1)}, u32[]{:S(2)}, u32[]{:S(2)}) collective-permute-start(bf16[2,32,2048]{2,1,0:T(8,128)(2,1)S(1)} %bitcast.198), channel_id=1, source_target_pairs={{0,2},{2,0},{1,3},{3,1},{4,6},{6,4},{5,7},{7,5},{8,10},{10,8},{9,1... | collective-permute-start | bytes 786440 | tf_op jit(solution)/shard_map/ppermute | solution.py:784
  54.7 20.7 %collective-permute-start.6 = (bf16[400,1024]{1,0:T(8,128)(2,1)S(1)}, bf16[400,1024]{1,0:T(8,128)(2,1)}, u32[]{:S(2)}, u32[]{:S(2)}) collective-permute-start(bf16[400,1024]{1,0:T(8,128)(2,1)S(1)} %slice.177), channel_id=1, source_target_pairs={{0,2},{2,0},{1,3},{3,1},{4,6},{6,4},{5,7},{7,5},{8,10},{10,8},{9,1... | collective-permute-start | bytes 2457608 | tf_op jit(solution)/shard_map/ppermute | solution.py:784
  79.8 12.6 %collective-permute-start.8 = (bf16[400,1024]{1,0:T(8,128)(2,1)}, bf16[400,1024]{1,0:T(8,128)(2,1)S(1)}, u32[]{:S(2)}, u32[]{:S(2)}) collective-permute-start(bf16[400,1024]{1,0:T(8,128)(2,1)} %collective-permute-done.6.refs_5_.refs_1_), channel_id=1, source_target_pairs={{0,1},{1,0},{2,3},{3,2},{4,5},{5,4},{6,7},{7,6},{8,9},{9,8},{10,11... | collective-permute-start | bytes 2457608 | tf_op jit(solution)/shard_map/ppermute | solution.py:784
  85.8 52.0 %all-to-all-start.2 = ((bf16[8,2,32,1024]{3,2,1,0:T(8,128)(2,1)}), bf16[8,2,32,1024]{3,2,1,0:T(8,128)(2,1)S(1)}, u32[]{:S(2)}, u32[]{:S(2)}) async-start(bf16[8,2,32,1024]{3,2,1,0:T(8,128)(2,1)} %broadcast_in_dim.36), calls=%async_computation.2 | async-start | bytes 2097152 | tf_op jit(solution)/shard_map/all_to_all | solution.py:935
  89.4 341.9 %reduce-scatter.2.cloned.1.call-start = ((), (), s32[]{:S(2)}) async-start(), calls=%async_computation.9 | async-start | bytes 8912896 | tf_op jit(solution)/shard_map/reduce_scatter | solution.py:977
  90.9 46.9 %collective-permute-start.9 = (bf16[12,64,1024]{2,1,0:T(8,128)(2,1)S(1)}, bf16[12,64,1024]{2,1,0:T(8,128)(2,1)}, u32[]{:S(2)}, u32[]{:S(2)}) collective-permute-start(bf16[12,64,1024]{2,1,0:T(8,128)(2,1)S(1)} %bitcast.168), channel_id=1, source_target_pairs={{0,2},{2,0},{1,3},{3,1},{4,6},{6,4},{5,7},{7,5},{8,10},{10,8},{9,1... | collective-permute-start | bytes 4718600 | tf_op jit(solution)/shard_map/ppermute | solution.py:784
  139.4 31.9 %collective-permute-start.14 = (bf16[256,768]{1,0:T(8,128)(2,1)S(1)}, bf16[256,768]{1,0:T(8,128)(2,1)S(1)}, u32[]{:S(2)}, u32[]{:S(2)}) collective-permute-start(bf16[256,768]{1,0:T(8,128)(2,1)S(1)} %get-tuple-element.260), channel_id=1, source_target_pairs={{0,3},{1,2},{2,1},{3,0},{4,7},{5,6},{6,5},{7,4},{8,11},{9,10},{10,... | collective-permute-start | bytes 1179656 | tf_op jit(solution)/shard_map/ppermute | solution.py:784
  139.9 31.5 %collective-permute-start.13 = (bf16[256,768]{1,0:T(8,128)(2,1)S(1)}, bf16[256,768]{1,0:T(8,128)(2,1)S(1)}, u32[]{:S(2)}, u32[]{:S(2)}) collective-permute-start(bf16[256,768]{1,0:T(8,128)(2,1)S(1)} %get-tuple-element.261), channel_id=1, source_target_pairs={{0,2},{1,3},{2,0},{3,1},{4,6},{5,7},{6,4},{7,5},{8,10},{9,11},{10,... | collective-permute-start | bytes 1179656 | tf_op jit(solution)/shard_map/ppermute | solution.py:784
  141.3 27.6 %collective-permute-start.11 = (bf16[8,2,32,1024]{3,2,1,0:T(8,128)(2,1)S(1)}, bf16[8,2,32,1024]{3,2,1,0:T(8,128)(2,1)S(1)}, u32[]{:S(2)}, u32[]{:S(2)}) collective-permute-start(bf16[8,2,32,1024]{3,2,1,0:T(8,128)(2,1)S(1)} %all-to-all-done.2.mine), channel_id=1, source_target_pairs={{0,1},{1,0},{2,3},{3,2},{4,5},{5,4},{6,7},{7,6},{8,9},{9,8},{10,11... | collective-permute-start | bytes 3145736 | tf_op jit(solution)/shard_map/ppermute | solution.py:784
  183.5 29.6 %collective-permute-start.15 = (bf16[384,1024]{1,0:T(8,128)(2,1)}, bf16[384,1024]{1,0:T(8,128)(2,1)S(1)}, u32[]{:S(2)}, u32[]{:S(2)}) collective-permute-start(bf16[384,1024]{1,0:T(8,128)(2,1)} %get-tuple-element.151.hidden.refs_0_), channel_id=1, source_target_pairs={{0,2},{2,0},{1,3},{3,1},{4,6},{6,4},{5,7},{7,5},{8,10},{10,8},{9,1... | collective-permute-start | bytes 2359304 | tf_op jit(solution)/shard_map/ppermute | solution.py:784
  197.6 29.9 %collective-permute-start.16 = (bf16[384,1024]{1,0:T(8,128)(2,1)S(1)}, bf16[384,1024]{1,0:T(8,128)(2,1)S(1)}, u32[]{:S(2)}, u32[]{:S(2)}) collective-permute-start(bf16[384,1024]{1,0:T(8,128)(2,1)S(1)} %copy-done.56), channel_id=1, source_target_pairs={{0,2},{2,0},{1,3},{3,1},{4,6},{6,4},{5,7},{7,5},{8,10},{10,8},{9,1... | collective-permute-start | bytes 2359304 | tf_op jit(solution)/shard_map/ppermute | solution.py:784
  227.2 37.4 %collective-permute-start.17 = (bf16[384,1024]{1,0:T(8,128)(2,1)}, bf16[384,1024]{1,0:T(8,128)(2,1)S(1)}, u32[]{:S(2)}, u32[]{:S(2)}) collective-permute-start(bf16[384,1024]{1,0:T(8,128)(2,1)} %get-tuple-element.171), channel_id=1, source_target_pairs={{0,2},{2,0},{1,3},{3,1},{4,6},{6,4},{5,7},{7,5},{8,10},{10,8},{9,1... | collective-permute-start | bytes 2359304 | tf_op jit(solution)/shard_map/ppermute | solution.py:784
  241.8 22.9 %collective-permute-start.18 = (bf16[384,1024]{1,0:T(8,128)(2,1)}, bf16[384,1024]{1,0:T(8,128)(2,1)S(1)}, u32[]{:S(2)}, u32[]{:S(2)}) collective-permute-start(bf16[384,1024]{1,0:T(8,128)(2,1)} %get-tuple-element.172), channel_id=1, source_target_pairs={{0,2},{2,0},{1,3},{3,1},{4,6},{6,4},{5,7},{7,5},{8,10},{10,8},{9,1... | collective-permute-start | bytes 2359304 | tf_op jit(solution)/shard_map/ppermute | solution.py:784
  283.2 108.2 %all-to-all-start.3 = ((bf16[32,32,1024]{2,1,0:T(8,128)(2,1)}), bf16[32,32,1024]{2,1,0:T(8,128)(2,1)}, u32[]{:S(2)}, u32[]{:S(2)}) async-start(bf16[32,32,1024]{2,1,0:T(8,128)(2,1)} %bitcast.186), calls=%async_computation.3 | async-start | bytes 4194304 | tf_op jit(solution)/shard_map/all_to_all | solution.py:988
  288.0 50.3 %collective-permute-start.20 = (bf16[256,768]{1,0:T(8,128)(2,1)S(1)}, bf16[256,768]{1,0:T(8,128)(2,1)}, u32[]{:S(2)}, u32[]{:S(2)}) collective-permute-start(bf16[256,768]{1,0:T(8,128)(2,1)S(1)} %copy-done.60), channel_id=1, source_target_pairs={{0,2},{1,3},{2,0},{3,1},{4,6},{5,7},{6,4},{7,5},{8,10},{9,11},{10,... | collective-permute-start | bytes 1179656 | tf_op jit(solution)/shard_map/ppermute | solution.py:784
  289.9 48.4 %collective-permute-start.21 = (bf16[256,768]{1,0:T(8,128)(2,1)S(1)}, bf16[256,768]{1,0:T(8,128)(2,1)}, u32[]{:S(2)}, u32[]{:S(2)}) collective-permute-start(bf16[256,768]{1,0:T(8,128)(2,1)S(1)} %copy-done.59), channel_id=1, source_target_pairs={{0,3},{1,2},{2,1},{3,0},{4,7},{5,6},{6,5},{7,4},{8,11},{9,10},{10,... | collective-permute-start | bytes 1179656 | tf_op jit(solution)/shard_map/ppermute | solution.py:784
  338.3 53.1 %collective-permute-start.22 = (bf16[384,1024]{1,0:T(8,128)(2,1)}, bf16[384,1024]{1,0:T(8,128)(2,1)S(1)}, u32[]{:S(2)}, u32[]{:S(2)}) collective-permute-start(bf16[384,1024]{1,0:T(8,128)(2,1)} %get-tuple-element.192), channel_id=1, source_target_pairs={{0,2},{2,0},{1,3},{3,1},{4,6},{6,4},{5,7},{7,5},{8,10},{10,8},{9,1... | collective-permute-start | bytes 2359304 | tf_op jit(solution)/shard_map/ppermute | solution.py:784
  339.9 51.5 %collective-permute-start.23 = (bf16[384,1024]{1,0:T(8,128)(2,1)}, bf16[384,1024]{1,0:T(8,128)(2,1)}, u32[]{:S(2)}, u32[]{:S(2)}) collective-permute-start(bf16[384,1024]{1,0:T(8,128)(2,1)} %get-tuple-element.193), channel_id=1, source_target_pairs={{0,2},{2,0},{1,3},{3,1},{4,6},{6,4},{5,7},{7,5},{8,10},{10,8},{9,1... | collective-permute-start | bytes 2359304 | tf_op jit(solution)/shard_map/ppermute | solution.py:784
  411.5 19.8 %collective-permute-start.25 = (bf16[384,1024]{1,0:T(8,128)(2,1)}, bf16[384,1024]{1,0:T(8,128)(2,1)S(1)}, u32[]{:S(2)}, u32[]{:S(2)}) collective-permute-start(bf16[384,1024]{1,0:T(8,128)(2,1)} %get-tuple-element.203), channel_id=1, source_target_pairs={{0,2},{2,0},{1,3},{3,1},{4,6},{6,4},{5,7},{7,5},{8,10},{10,8},{9,1... | collective-permute-start | bytes 2359304 | tf_op jit(solution)/shard_map/ppermute | solution.py:784
  432.8 52.6 %all-to-all-start.4 = ((bf16[32,35,768]{2,1,0:T(8,128)(2,1)}), bf16[32,35,768]{2,1,0:T(8,128)(2,1)S(1)}, u32[]{:S(2)}, u32[]{:S(2)}) async-start(bf16[32,35,768]{2,1,0:T(8,128)(2,1)} %pad_maximum_fusion), calls=%async_computation.5 | async-start | bytes 3932160 | tf_op jit(solution)/shard_map/all_to_all | solution.py:1039
  449.6 14.8 %collective-permute-start.28 = (bf16[2,32,2048]{2,1,0:T(8,128)(2,1)S(1)}, bf16[2,32,2048]{2,1,0:T(8,128)(2,1)S(1)}, u32[]{:S(2)}, u32[]{:S(2)}) collective-permute-start(bf16[2,32,2048]{2,1,0:T(8,128)(2,1)S(1)} %bitcast.196), channel_id=1, source_target_pairs={{0,2},{2,0},{1,3},{3,1},{4,6},{6,4},{5,7},{7,5},{8,10},{10,8},{9,1... | collective-permute-start | bytes 786440 | tf_op jit(solution)/shard_map/ppermute | solution.py:784
  452.9 49.9 %collective-permute-start.27 = (bf16[768,1024]{1,0:T(8,128)(2,1)}, bf16[768,1024]{1,0:T(8,128)(2,1)}, u32[]{:S(2)}, u32[]{:S(2)}) collective-permute-start(bf16[768,1024]{1,0:T(8,128)(2,1)} %slice_bitcast_fusion), channel_id=1, source_target_pairs={{0,1},{1,0},{2,3},{3,2},{4,5},{5,4},{6,7},{7,6},{8,9},{9,8},{10,11... | collective-permute-start | bytes 4718600 | tf_op jit(solution)/shard_map/ppermute | solution.py:784
  452.9 32.5 %collective-permute-start.26 = (bf16[384,1024]{1,0:T(8,128)(2,1)S(1)}, bf16[384,1024]{1,0:T(8,128)(2,1)}, u32[]{:S(2)}, u32[]{:S(2)}) collective-permute-start(bf16[384,1024]{1,0:T(8,128)(2,1)S(1)} %copy-done.31), channel_id=1, source_target_pairs={{0,2},{2,0},{1,3},{3,1},{4,6},{6,4},{5,7},{7,5},{8,10},{10,8},{9,1... | collective-permute-start | bytes 2359304 | tf_op jit(solution)/shard_map/ppermute | solution.py:784
  498.0 12.8 %all-to-all-start.5 = ((f32[32,1,128]{2,1,0:T(1,128)}), f32[32,1,128]{2,1,0:T(1,128)S(1)}, u32[]{:S(2)}, u32[]{:S(2)}) async-start(f32[32,1,128]{2,1,0:T(1,128)} %broadcast_in_dim.37), calls=%async_computation.6 | async-start | bytes 32768 | tf_op jit(solution)/shard_map/all_to_all | solution.py:1063
  (67 other events, 317.5 us)
Sparse Core Ops, SparseCore 0:
  28.0 50.7 all-gather.2
  81.4 92.4 all-gather.4
  264.8 138.8 reduce-scatter.1
